TPU v7x, 32 devices: a whole 2x2x4 slice. The times are simulated.
32 devices in a mesh: tm: 4 (over z), height: 4 (over y, x), width: 2 (over core).
Axes of the slice: x: 2, y: 2, z: 4, core: 2. Of those that a mesh axis runs over, the one named last changes fastest.
Arguments:
- latent: bfloat16 [128, 8, 16, 512], P(None, 'tm', 'height', 'width'), may hold values from -64 to 64
- exponents: int32 [32], replicated, may hold values from -1 to 1
- cotangent: bfloat16 [128, 8, 16, 512], P(None, 'tm', 'height', 'width'), may hold values from -6 to 6
- conv_first: bfloat16 [128, 3456], replicated, may hold values from -0.109375 to 0.109375
- conv_second: bfloat16 [128, 3456], replicated, may hold values from -0.109375 to 0.109375
- gain_first: float32 [128], replicated, may hold values from 0.1 to 1.9
- shift_first: float32 [128], replicated, may hold values from -2.5 to 2.5
- gain_second: float32 [128], replicated, may hold values from 0.1 to 1.9
- shift_second: float32 [128], replicated, may hold values from -2.5 to 2.5
Outputs:
- decoded_grad: float32 [128, 8, 16, 512], P(None, 'tm', 'height', 'width')
- conv_first_grad: float32 [128, 3456], replicated
- conv_second_grad: float32 [128, 3456], replicated
All inputs are finite; a program needn't handle non-finite values.
Results may differ from a plain program's by a relative error of at most 0.005.
Values may be sent and summed in bfloat16 or wider, within the bound.
No kernel may reach another device: no remote copies, remote signals or barrier semaphores. Data moves between devices by JAX's collectives and lax.ppermute only.
A program may use at most 128 MiB of HBM per device.

v0:
```python
import jax
import jax.numpy as jnp
from jax import lax
from jax.sharding import PartitionSpec as P

epsilon = 1e-05


def padded_2(cells, sides, width):
    for axis, dim in sides:
        count = lax.axis_size(axis)
        ends = count - 1
        head = lax.slice_in_dim(cells, 0, width, axis=dim)
        tail = lax.slice_in_dim(cells, cells.shape[dim] - width, cells.shape[dim], axis=dim)
        cells = jnp.concatenate(
            [
                lax.ppermute(tail, axis, [(i, (i + 1) % count) for i in range(ends)]),
                cells,
                lax.ppermute(head, axis, [((i + 1) % count, i) for i in range(ends)]),
            ],
            axis=dim,
        )
    return cells


def from_behind(value, axis, steps):
    count = lax.axis_size(axis)
    initial, last = (max(0, -steps), min(count, count - steps))
    return lax.ppermute(value, axis, [(source, source + steps) for source in range(initial, last)])


def group_terms(values, groups):
    return jnp.sum(values.reshape(groups, -1), axis=1)


def per_channel(stat, channels):
    return jnp.repeat(stat, channels // stat.shape[0])[:, None, None, None]


def channel(vector):
    return vector[:, None, None, None]


def across(terms):
    return lax.psum(terms, ("tm", "height", "width"))


def group_stats(values, groups, count):
    channels = values.shape[0]
    (sums,) = across((group_terms(values, groups),))
    mean_value = sums / count
    centered = values - per_channel(mean_value, channels)
    (squares,) = across((group_terms(centered * centered, groups),))
    variance = squares / count
    inverse = 1.0 / jnp.sqrt(variance + epsilon)
    return (centered * per_channel(inverse, channels), inverse)


def silu_slope(pre):
    sigmoid_value = jax.nn.sigmoid(pre)
    return sigmoid_value * (1.0 + pre * (1.0 - sigmoid_value))


def norm_backward(grad, pre, normed, gain, inverse, groups, count):
    channels = grad.shape[0]
    scaled = grad * silu_slope(pre) * channel(gain)
    first_sum, second_sum = across(
        (group_terms(scaled, groups), group_terms(scaled * normed, groups))
    )
    return per_channel(inverse, channels) * (
        scaled
        - per_channel(first_sum / count, channels)
        - normed * per_channel(second_sum / count, channels)
    )


def rimmed(timed):
    return padded_2(timed, (("height", 2), ("width", 3)), 1)


def extend_past(values):
    before = from_behind(values, "tm", 1)
    return rimmed(jnp.concatenate([before, values], axis=1))


def extend_future(values):
    after = from_behind(values, "tm", -1)
    return rimmed(jnp.concatenate([values, after], axis=1))


def tap_stack(padded, first, top, col_taps, frame_count, row_count, col_count):
    pieces = [
        padded[:, first : first + frame_count, top : top + row_count, col_tap : col_tap + col_count]
        for col_tap in col_taps
    ]
    return jnp.concatenate(pieces, axis=0).reshape(len(col_taps) * padded.shape[0], -1)


def forward_conv(padded, weight, frame_count, row_count, col_count):
    channels = weight.shape[0]
    accum = jnp.zeros((channels, frame_count * row_count * col_count), jnp.float32)
    for depth_tap in range(3):
        for row_tap in range(3):
            start_col = (depth_tap * 3 + row_tap) * 3 * channels
            stacked = tap_stack(
                padded, depth_tap, row_tap, (0, 1, 2), frame_count, row_count, col_count
            )
            accum = accum + jnp.dot(
                weight[:, start_col : start_col + 3 * channels],
                stacked,
                preferred_element_type=jnp.float32,
            )
    return accum.reshape(channels, frame_count, row_count, col_count)


def transposed_conv(padded, weight, frame_count, row_count, col_count):
    channels = weight.shape[0]
    accum = jnp.zeros((channels, frame_count * row_count * col_count), jnp.float32)
    for depth_tap in range(3):
        for row_tap in range(3):
            start_col = (depth_tap * 3 + row_tap) * 3 * channels
            w_block = (
                weight[:, start_col : start_col + 3 * channels]
                .reshape(channels, 3, channels)
                .transpose(2, 1, 0)
                .reshape(channels, 3 * channels)
            )
            stacked = tap_stack(
                padded, 2 - depth_tap, 2 - row_tap, (2, 1, 0), frame_count, row_count, col_count
            )
            accum = accum + jnp.dot(w_block, stacked, preferred_element_type=jnp.float32)
    return accum.reshape(channels, frame_count, row_count, col_count)


def weight_terms(padded, grad, frame_count, row_count, col_count):
    channels = grad.shape[0]
    flat_grad = grad.reshape(channels, -1)
    pieces = []
    for depth_tap in range(3):
        for row_tap in range(3):
            stacked = tap_stack(
                padded, depth_tap, row_tap, (0, 1, 2), frame_count, row_count, col_count
            )
            pieces.append(
                lax.dot_general(
                    flat_grad, stacked, (((1,), (1,)), ((), ())), preferred_element_type=jnp.float32
                )
            )
    return jnp.concatenate(pieces, axis=1)


def reduce_weights(terms):
    result = lax.psum(terms, ("tm", "height", "width"))
    return result


def shards(
    latent,
    exponents,
    cotangent,
    conv_first,
    conv_second,
    gain_first,
    shift_first,
    gain_second,
    shift_second,
):
    channels, frame_count, row_count, col_count = latent.shape
    groups = exponents.shape[0]
    count = float(
        channels
        // groups
        * frame_count
        * row_count
        * col_count
        * lax.axis_size("tm")
        * lax.axis_size("height")
        * lax.axis_size("width")
    )
    decoded = latent.astype(jnp.float32) * per_channel(
        jnp.exp2(exponents.astype(jnp.float32)), channels
    )
    normed_first, inverse_first = group_stats(decoded, groups, count)
    pre_first = normed_first * channel(gain_first) + channel(shift_first)
    act_first = jax.nn.silu(pre_first).astype(jnp.bfloat16)
    padded_first = extend_past(act_first)
    hidden = forward_conv(padded_first, conv_first, frame_count, row_count, col_count)
    normed_second, inverse_second = group_stats(hidden, groups, count)
    pre_second = normed_second * channel(gain_second) + channel(shift_second)
    act_second = jax.nn.silu(pre_second).astype(jnp.bfloat16)
    padded_second = extend_past(act_second)
    padded_cotangent = extend_future(cotangent)
    grad_second = transposed_conv(padded_cotangent, conv_second, frame_count, row_count, col_count)
    conv_second_grad = reduce_weights(
        weight_terms(padded_second, cotangent, frame_count, row_count, col_count)
    )
    hidden_grad = norm_backward(
        grad_second, pre_second, normed_second, gain_second, inverse_second, groups, count
    ).astype(jnp.bfloat16)
    padded_hidden = extend_future(hidden_grad)
    grad_first = transposed_conv(padded_hidden, conv_first, frame_count, row_count, col_count)
    conv_first_grad = reduce_weights(
        weight_terms(padded_first, hidden_grad, frame_count, row_count, col_count)
    )
    decoded_grad = cotangent.astype(jnp.float32) + norm_backward(
        grad_first, pre_first, normed_first, gain_first, inverse_first, groups, count
    )
    return (decoded_grad, conv_first_grad, conv_second_grad)


def solution(mesh):
    placed = (
        P(None, "tm", "height", "width"),
        P(),
        P(None, "tm", "height", "width"),
        P(),
        P(),
        P(),
        P(),
        P(),
        P(),
    )
    return jax.shard_map(
        shards,
        mesh=mesh,
        in_specs=placed,
        out_specs=(P(None, "tm", "height", "width"), P(), P()),
        check_vma=False,
    )
```

profile of v0, /device:TPU:1, one launch (start us, length us, event | category | flops | bytes accessed | tf_op | source)
XLA Modules:
  0.0 645.5 jit_solution(1552945713985232665)
XLA Ops:
  11.2 40.6 %psum.70 = f32[32]{0:T(128)S(1)} all-reduce(f32[32]{0:T(128)S(1)} %reduce_sum.97), channel_id=1, replica_groups=mesh['tm'=4,'height'=4,'width'=2] {'tm','height','width'}, use_global_device_ids=true, to_apply=%region_2.0 | all-reduce | flops 32 | bytes 256 | tf_op jit(solution)/shard_map/psum | solution.py:45
  53.9 41.3 %psum.71 = f32[32]{0:T(128)S(1)} all-reduce(f32[32]{0:T(128)S(1)} %reduce_sum.100), channel_id=1, replica_groups=mesh['tm'=4,'height'=4,'width'=2] {'tm','height','width'}, use_global_device_ids=true, to_apply=%region_5.6 | all-reduce | flops 32 | bytes 256 | tf_op jit(solution)/shard_map/psum | solution.py:45
  96.2 3.1 collective-permute-start
  112.5 4.7 collective-permute-start.6
  120.3 4.7 collective-permute-start.1
  140.3 4.4 collective-permute-start.8
  151.6 3.2 collective-permute-start.4
  159.4 3.5 maximum_maximum_fusion
  162.9 4.5 fusion.160
  182.3 3.4 pad_maximum_fusion.15
  193.6 2.9 fusion.143
  215.1 2.6 maximum_maximum_fusion.5
  217.7 39.5 %psum.72 = f32[32]{0:T(128)S(1)} all-reduce(f32[32]{0:T(128)S(1)} %copy-done.129), channel_id=1, replica_groups=mesh['tm'=4,'height'=4,'width'=2] {'tm','height','width'}, use_global_device_ids=true, to_apply=%region_8.9 | all-reduce | flops 32 | bytes 256 | tf_op jit(solution)/shard_map/psum | solution.py:45
  261.5 3.5 fusion.173
  265.0 39.7 %psum.73 = f32[32]{0:T(128)S(1)} all-reduce(f32[32]{0:T(128)S(1)} %copy-done.128), channel_id=1, replica_groups=mesh['tm'=4,'height'=4,'width'=2] {'tm','height','width'}, use_global_device_ids=true, to_apply=%region_11.12 | all-reduce | flops 32 | bytes 256 | tf_op jit(solution)/shard_map/psum | solution.py:45
  326.9 40.4 %all-reduce.1 = (f32[32]{0:T(128)S(1)}, f32[32]{0:T(128)S(1)}) all-reduce(f32[32]{0:T(128)S(1)} %reduce_sum.145, f32[32]{0:T(128)S(1)} %reduce_sum.115), channel_id=1, replica_groups=mesh['tm'=4,'height'=4,'width'=2] {'tm','height','width'}, use_global_device_ids=true, to_apply=%region_17.18 | all-reduce | flops 64 | bytes 512 | tf_op jit(solution)/shard_map/psum | solution.py:45
  368.9 2.7 multiply_convert_fusion
  373.7 4.2 collective-permute-start.15
  387.4 2.9 collective-permute-start.16
  394.0 4.0 collective-permute-start.11
  406.8 9.2 %collective-permute-start.19 = (bf16[128,4,6,1]{0,1,3,2:T(4,128)(2,1)}, bf16[128,4,6,1]{0,1,3,2:T(4,128)(2,1)}, u32[]{:S(2)}, u32[]{:S(2)}) collective-permute-start(bf16[128,4,6,1]{0,1,3,2:T(4,128)(2,1)} %copy.269), channel_id=1, source_target_pairs={{1,0},{3,2},{5,4},{7,6},{9,8},{11,10},{13,12},{15,14},{17,16},{19,... | collective-permute-start | bytes 18440 | tf_op jit(solution)/shard_map/ppermute | solution.py:19
  429.7 4.6 maximum_maximum_fusion.2
  436.5 3.6 fusion.157
  441.8 4.6 pad_maximum_fusion.1
  446.4 3.2 fusion.158
  468.5 2.7 copy.252
  471.2 3.6 pad_maximum_fusion.32
  474.8 2.7 copy.250
  482.5 2.7 fusion.103
  515.4 41.0 %all-reduce = (f32[32]{0:T(128)S(1)}, f32[32]{0:T(128)S(1)}) all-reduce(f32[32]{0:T(128)S(1)} %reduce_sum.151, f32[32]{0:T(128)S(1)} %reduce_sum.148), channel_id=1, replica_groups=mesh['tm'=4,'height'=4,'width'=2] {'tm','height','width'}, use_global_device_ids=true, to_apply=%region_23.24 | all-reduce | flops 64 | bytes 512 | tf_op jit(solution)/shard_map/psum | solution.py:45
  558.9 75.3 %all-reduce.5.cloned.1.call-done = (f32[128,3456]{1,0:T(8,128)}, f32[128,3456]{0,1:T(8,128)}) async-done(((f32[128,3456]{1,0:T(8,128)}, f32[128,3456]{0,1:T(8,128)}), (f32[128,3456]{1,0:T(8,128)}, f32[128,3456]{0,1:T(8,128)})) %all-reduce.5.cloned.1.call-update) | async-done | bytes 3538960 | tf_op jit(solution)/shard_map/psum | solution.py:153
  634.2 2.8 copy.281
  (507 shorter events, 217.3 us)
Async XLA Ops:
  7.2 44.9 %copy-start = (bf16[128,2,4,256]{3,2,1,0:T(4,128)(2,1)S(1)}, bf16[128,2,4,256]{3,2,1,0:T(4,128)(2,1)}, u32[]{:S(2)}) copy-start(bf16[128,2,4,256]{3,2,1,0:T(4,128)(2,1)} %param.9) | copy-start | bytes 1572868
  7.2 88.2 %copy-start.123 = (f32[128]{0:T(128)S(1)}, f32[128]{0:T(128)}, u32[]{:S(2)}) copy-start(f32[128]{0:T(128)} %param.14) | copy-start | bytes 1540
  7.2 88.2 %copy-start.121 = (f32[128]{0:T(128)S(1)}, f32[128]{0:T(128)}, u32[]{:S(2)}) copy-start(f32[128]{0:T(128)} %param.15) | copy-start | bytes 1540
  7.2 627.0 %all-reduce.5.cloned.1.call-start = ((), (), s32[]{:S(2)}) async-start(), calls=%async_computation | async-start | bytes 7077888 | tf_op jit(solution)/shard_map/psum | solution.py:153
  8.1 88.0 %copy-start.114 = (f32[128]{0:T(128)}, f32[128]{0:T(128)S(1)}, u32[]{:S(2)}) copy-start(f32[128]{0:T(128)S(1)} %mul.184) | copy-start | bytes 1540
  8.1 91.1 %copy-start.75 = (bf16[128,3456]{1,0:T(8,128)(2,1)S(1)}, bf16[128,3456]{1,0:T(8,128)(2,1)}, u32[]{:S(2)}) copy-start(bf16[128,3456]{1,0:T(8,128)(2,1)} %param.13) | copy-start | bytes 2654212
  52.0 44.2 %copy-start.116 = (f32[128]{0:T(128)}, f32[128]{0:T(128)S(1)}, u32[]{:S(2)}) copy-start(f32[128]{0:T(128)S(1)} %sub.72) | copy-start | bytes 1540
  52.6 59.0 %collective-permute-start.5 = (bf16[128,2,4,256]{0,3,2,1:T(8,128)(2,1)S(1)}, bf16[128,2,4,256]{0,3,2,1:T(8,128)(2,1)S(1)}, u32[]{:S(2)}, u32[]{:S(2)}) collective-permute-start(bf16[128,2,4,256]{0,3,2,1:T(8,128)(2,1)S(1)} %copy.212), channel_id=1, source_target_pairs={{8,0},{16,8},{24,16},{9,1},{17,9},{25,17},{10,2},{18,10},{26,18},{... | collective-permute-start | bytes 1572872 | tf_op jit(solution)/shard_map/ppermute | solution.py:29
  96.2 23.2 %collective-permute-start = (bf16[128,2,4,256]{3,0,2,1:T(8,128)(2,1)S(1)}, bf16[128,2,4,256]{3,0,2,1:T(8,128)(2,1)S(1)}, u32[]{:S(2)}, u32[]{:S(2)}) collective-permute-start(bf16[128,2,4,256]{3,0,2,1:T(8,128)(2,1)S(1)} %multiply_convert_fusion.2), channel_id=1, source_target_pairs={{0,8},{8,16},{16,24},{1,9},{9,17},{17,25},{2,10},{10,18},{18,26},{... | collective-permute-start | bytes 1572872 | tf_op jit(solution)/shard_map/ppermute | solution.py:29
  111.6 14.6 %copy-start.25 = (bf16[128,3456]{1,0:T(8,128)(2,1)S(1)}, bf16[128,3456]{1,0:T(8,128)(2,1)}, u32[]{:S(2)}) copy-start(bf16[128,3456]{1,0:T(8,128)(2,1)} %param.12) | copy-start | bytes 2654212
  112.5 25.4 %collective-permute-start.6 = (bf16[128,4,1,256]{3,0,2,1:T(8,128)(2,1)}, bf16[128,4,1,256]{3,0,2,1:T(8,128)(2,1)}, u32[]{:S(2)}, u32[]{:S(2)}) collective-permute-start(bf16[128,4,1,256]{3,0,2,1:T(8,128)(2,1)} %copy.213), channel_id=1, source_target_pairs={{0,2},{2,4},{4,6},{1,3},{3,5},{5,7},{8,10},{10,12},{12,14},{9,11},... | collective-permute-start | bytes 786440 | tf_op jit(solution)/shard_map/ppermute | solution.py:17
  118.1 21.0 %collective-permute-start.7 = (bf16[128,4,1,256]{3,0,2,1:T(8,128)(2,1)}, bf16[128,4,1,256]{3,0,2,1:T(8,128)(2,1)}, u32[]{:S(2)}, u32[]{:S(2)}) collective-permute-start(bf16[128,4,1,256]{3,0,2,1:T(8,128)(2,1)} %copy.214), channel_id=1, source_target_pairs={{2,0},{4,2},{6,4},{3,1},{5,3},{7,5},{10,8},{12,10},{14,12},{11,9},... | collective-permute-start | bytes 786440 | tf_op jit(solution)/shard_map/ppermute | solution.py:19
  119.4 40.0 %copy-start.2 = (bf16[128,2,4,256]{3,0,2,1:T(8,128)(2,1)}, bf16[128,2,4,256]{3,0,2,1:T(8,128)(2,1)S(1)}, u32[]{:S(2)}) copy-start(bf16[128,2,4,256]{3,0,2,1:T(8,128)(2,1)S(1)} %collective-permute-done) | copy-start | bytes 1572868
  120.3 25.7 %collective-permute-start.1 = (bf16[128,4,1,256]{3,0,2,1:T(8,128)(2,1)}, bf16[128,4,1,256]{3,0,2,1:T(8,128)(2,1)}, u32[]{:S(2)}, u32[]{:S(2)}) collective-permute-start(bf16[128,4,1,256]{3,0,2,1:T(8,128)(2,1)} %get-tuple-element.150), channel_id=1, source_target_pairs={{0,2},{2,4},{4,6},{1,3},{3,5},{5,7},{8,10},{10,12},{12,14},{9,11},... | collective-permute-start | bytes 786440 | tf_op jit(solution)/shard_map/ppermute | solution.py:17
  125.0 21.0 %collective-permute-start.2 = (bf16[128,4,1,256]{3,0,2,1:T(8,128)(2,1)}, bf16[128,4,1,256]{3,0,2,1:T(8,128)(2,1)}, u32[]{:S(2)}, u32[]{:S(2)}) collective-permute-start(bf16[128,4,1,256]{3,0,2,1:T(8,128)(2,1)} %get-tuple-element.151), channel_id=1, source_target_pairs={{2,0},{4,2},{6,4},{3,1},{5,3},{7,5},{10,8},{12,10},{14,12},{11,9},... | collective-permute-start | bytes 786440 | tf_op jit(solution)/shard_map/ppermute | solution.py:19
  140.3 165.1 %collective-permute-start.8 = (bf16[128,4,6,1]{0,1,3,2:T(4,128)(2,1)S(1)}, bf16[128,4,6,1]{0,1,3,2:T(4,128)(2,1)S(1)}, u32[]{:S(2)}, u32[]{:S(2)}) collective-permute-start(bf16[128,4,6,1]{0,1,3,2:T(4,128)(2,1)S(1)} %copy.217), channel_id=1, source_target_pairs={{1,0},{3,2},{5,4},{7,6},{9,8},{11,10},{13,12},{15,14},{17,16},{19,... | collective-permute-start | bytes 18440 | tf_op jit(solution)/shard_map/ppermute | solution.py:19
  144.7 160.7 %collective-permute-start.9 = (bf16[128,4,6,1]{0,1,3,2:T(4,128)(2,1)S(1)}, bf16[128,4,6,1]{0,1,3,2:T(4,128)(2,1)S(1)}, u32[]{:S(2)}, u32[]{:S(2)}) collective-permute-start(bf16[128,4,6,1]{0,1,3,2:T(4,128)(2,1)S(1)} %copy.220), channel_id=1, source_target_pairs={{0,1},{2,3},{4,5},{6,7},{8,9},{10,11},{12,13},{14,15},{16,17},{18,... | collective-permute-start | bytes 18440 | tf_op jit(solution)/shard_map/ppermute | solution.py:17
  150.0 7.7 %collective-permute-start.3 = (bf16[128,4,6,1]{0,1,3,2:T(4,128)(2,1)S(1)}, bf16[128,4,6,1]{0,1,3,2:T(4,128)(2,1)S(1)}, u32[]{:S(2)}, u32[]{:S(2)}) collective-permute-start(bf16[128,4,6,1]{0,1,3,2:T(4,128)(2,1)S(1)} %copy.189), channel_id=1, source_target_pairs={{0,1},{2,3},{4,5},{6,7},{8,9},{10,11},{12,13},{14,15},{16,17},{18,... | collective-permute-start | bytes 18440 | tf_op jit(solution)/shard_map/ppermute | solution.py:17
  151.6 6.6 %collective-permute-start.4 = (bf16[128,4,6,1]{0,1,3,2:T(4,128)(2,1)S(1)}, bf16[128,4,6,1]{0,1,3,2:T(4,128)(2,1)S(1)}, u32[]{:S(2)}, u32[]{:S(2)}) collective-permute-start(bf16[128,4,6,1]{0,1,3,2:T(4,128)(2,1)S(1)} %copy.191), channel_id=1, source_target_pairs={{1,0},{3,2},{5,4},{7,6},{9,8},{11,10},{13,12},{15,14},{17,16},{19,... | collective-permute-start | bytes 18440 | tf_op jit(solution)/shard_map/ppermute | solution.py:19
  371.6 30.1 %copy-start.4 = (bf16[128,2,4,256]{3,0,2,1:T(8,128)(2,1)}, bf16[128,2,4,256]{3,0,2,1:T(8,128)(2,1)S(1)}, u32[]{:S(2)}) copy-start(bf16[128,2,4,256]{3,0,2,1:T(8,128)(2,1)S(1)} %get-tuple-element.138) | copy-start | bytes 1572868
  372.3 20.0 %collective-permute-start.10 = (bf16[128,2,4,256]{3,0,2,1:T(8,128)(2,1)S(1)}, bf16[128,2,4,256]{3,0,2,1:T(8,128)(2,1)S(1)}, u32[]{:S(2)}, u32[]{:S(2)}) collective-permute-start(bf16[128,2,4,256]{3,0,2,1:T(8,128)(2,1)S(1)} %get-tuple-element.139), channel_id=1, source_target_pairs={{8,0},{16,8},{24,16},{9,1},{17,9},{25,17},{10,2},{18,10},{26,18},{... | collective-permute-start | bytes 1572872 | tf_op jit(solution)/shard_map/ppermute | solution.py:29
  373.7 13.7 %collective-permute-start.15 = (bf16[128,2,4,256]{3,0,2,1:T(8,128)(2,1)S(1)}, bf16[128,2,4,256]{3,0,2,1:T(8,128)(2,1)S(1)}, u32[]{:S(2)}, u32[]{:S(2)}) collective-permute-start(bf16[128,2,4,256]{3,0,2,1:T(8,128)(2,1)S(1)} %get-tuple-element.138), channel_id=1, source_target_pairs={{0,8},{8,16},{16,24},{1,9},{9,17},{17,25},{2,10},{10,18},{18,26},{... | collective-permute-start | bytes 1572872 | tf_op jit(solution)/shard_map/ppermute | solution.py:29
  387.4 14.3 %copy-start.9 = (bf16[128,2,4,256]{3,0,2,1:T(8,128)(2,1)}, bf16[128,2,4,256]{3,0,2,1:T(8,128)(2,1)S(1)}, u32[]{:S(2)}) copy-start(bf16[128,2,4,256]{3,0,2,1:T(8,128)(2,1)S(1)} %collective-permute-done.15) | copy-start | bytes 1572868
  387.4 11.9 %collective-permute-start.16 = (bf16[128,4,1,256]{3,0,2,1:T(8,128)(2,1)S(1)}, bf16[128,4,1,256]{3,0,2,1:T(8,128)(2,1)S(1)}, u32[]{:S(2)}, u32[]{:S(2)}) collective-permute-start(bf16[128,4,1,256]{3,0,2,1:T(8,128)(2,1)S(1)} %get-tuple-element.142), channel_id=1, source_target_pairs={{0,2},{2,4},{4,6},{1,3},{3,5},{5,7},{8,10},{10,12},{12,14},{9,11},... | collective-permute-start | bytes 786440 | tf_op jit(solution)/shard_map/ppermute | solution.py:17
  390.3 9.9 %collective-permute-start.17 = (bf16[128,4,1,256]{3,0,2,1:T(8,128)(2,1)S(1)}, bf16[128,4,1,256]{3,0,2,1:T(8,128)(2,1)S(1)}, u32[]{:S(2)}, u32[]{:S(2)}) collective-permute-start(bf16[128,4,1,256]{3,0,2,1:T(8,128)(2,1)S(1)} %get-tuple-element.143), channel_id=1, source_target_pairs={{2,0},{4,2},{6,4},{3,1},{5,3},{7,5},{10,8},{12,10},{14,12},{11,9},... | collective-permute-start | bytes 786440 | tf_op jit(solution)/shard_map/ppermute | solution.py:19
  394.0 23.2 %collective-permute-start.11 = (bf16[128,4,1,256]{3,0,2,1:T(8,128)(2,1)}, bf16[128,4,1,256]{3,0,2,1:T(8,128)(2,1)S(1)}, u32[]{:S(2)}, u32[]{:S(2)}) collective-permute-start(bf16[128,4,1,256]{3,0,2,1:T(8,128)(2,1)} %get-tuple-element.146), channel_id=1, source_target_pairs={{0,2},{2,4},{4,6},{1,3},{3,5},{5,7},{8,10},{10,12},{12,14},{9,11},... | collective-permute-start | bytes 786440 | tf_op jit(solution)/shard_map/ppermute | solution.py:17
  398.0 19.2 %collective-permute-start.12 = (bf16[128,4,1,256]{3,0,2,1:T(8,128)(2,1)}, bf16[128,4,1,256]{3,0,2,1:T(8,128)(2,1)S(1)}, u32[]{:S(2)}, u32[]{:S(2)}) collective-permute-start(bf16[128,4,1,256]{3,0,2,1:T(8,128)(2,1)} %get-tuple-element.147), channel_id=1, source_target_pairs={{2,0},{4,2},{6,4},{3,1},{5,3},{7,5},{10,8},{12,10},{14,12},{11,9},... | collective-permute-start | bytes 786440 | tf_op jit(solution)/shard_map/ppermute | solution.py:19
  404.6 22.7 %collective-permute-start.18 = (bf16[128,4,6,1]{0,1,3,2:T(4,128)(2,1)S(1)}, bf16[128,4,6,1]{0,1,3,2:T(4,128)(2,1)S(1)}, u32[]{:S(2)}, u32[]{:S(2)}) collective-permute-start(bf16[128,4,6,1]{0,1,3,2:T(4,128)(2,1)S(1)} %copy.267), channel_id=1, source_target_pairs={{0,1},{2,3},{4,5},{6,7},{8,9},{10,11},{12,13},{14,15},{16,17},{18,... | collective-permute-start | bytes 18440 | tf_op jit(solution)/shard_map/ppermute | solution.py:17
  406.8 21.0 %collective-permute-start.19 = (bf16[128,4,6,1]{0,1,3,2:T(4,128)(2,1)}, bf16[128,4,6,1]{0,1,3,2:T(4,128)(2,1)}, u32[]{:S(2)}, u32[]{:S(2)}) collective-permute-start(bf16[128,4,6,1]{0,1,3,2:T(4,128)(2,1)} %copy.269), channel_id=1, source_target_pairs={{1,0},{3,2},{5,4},{7,6},{9,8},{11,10},{13,12},{15,14},{17,16},{19,... | collective-permute-start | bytes 18440 | tf_op jit(solution)/shard_map/ppermute | solution.py:19
  421.9 18.3 %collective-permute-start.13 = (bf16[128,4,6,1]{0,1,3,2:T(4,128)(2,1)S(1)}, bf16[128,4,6,1]{0,1,3,2:T(4,128)(2,1)S(1)}, u32[]{:S(2)}, u32[]{:S(2)}) collective-permute-start(bf16[128,4,6,1]{0,1,3,2:T(4,128)(2,1)S(1)} %copy.244), channel_id=1, source_target_pairs={{1,0},{3,2},{5,4},{7,6},{9,8},{11,10},{13,12},{15,14},{17,16},{19,... | collective-permute-start | bytes 18440 | tf_op jit(solution)/shard_map/ppermute | solution.py:19
  424.6 16.0 %collective-permute-start.14 = (bf16[128,4,6,1]{0,1,3,2:T(4,128)(2,1)S(1)}, bf16[128,4,6,1]{0,1,3,2:T(4,128)(2,1)S(1)}, u32[]{:S(2)}, u32[]{:S(2)}) collective-permute-start(bf16[128,4,6,1]{0,1,3,2:T(4,128)(2,1)S(1)} %copy.246), channel_id=1, source_target_pairs={{0,1},{2,3},{4,5},{6,7},{8,9},{10,11},{12,13},{14,15},{16,17},{18,... | collective-permute-start | bytes 18440 | tf_op jit(solution)/shard_map/ppermute | solution.py:17
  512.8 43.9 %copy-start.70 = (bf16[128,2,4,256]{3,2,1,0:T(4,128)(2,1)S(1)}, bf16[128,2,4,256]{3,2,1,0:T(4,128)(2,1)}, u32[]{:S(2)}) copy-start(bf16[128,2,4,256]{3,2,1,0:T(4,128)(2,1)} %param.11) | copy-start | bytes 1572868
  (119 other events, 246.9 us)
Sparse Core Ops, SparseCore 0:
  496.0 138.1 all-reduce.4
where the time goes:
time: 657 us; the launch traced here: 646 us
  blocking collectives  242 us (37%)
  local copies, waits for them, and re-layouts  147 us (22%)
  waiting for transfers between devices  78.7 us (12%)
  other arithmetic  63.5 us (10%)
  starting transfers between devices  54.9 us (8%)
  matrix products  42.9 us (7%)
  between operations  16.3 us (2%)
    psum x6, blocking collectives, across(): return lax.psum(terms, ('tm', 'height', 'width'))  242 us
    psum x1, waiting for transfers between devices, reduce_weights(): result = lax.psum(terms, ('tm', 'height', 'width'))  75.3 us
    unnamed x283, local copies, waits for them, and re-layouts  37.6 us
    concatenate x18, local copies, waits for them, and re-layouts, tap_stack(): jnp.concatenate(pieces, axis=0).reshape(len(col_taps) * padded.shape[0], -1)  36.9 us
    concatenate x21, other arithmetic, tap_stack(): jnp.concatenate(pieces, axis=0).reshape(len(col_taps) * padded.shape[0], -1)  28.1 us
    slice x12, local copies, waits for them, and re-layouts, tap_stack(): padded[:, first:first + frame_count, top:top + row_count, col_tap:col_tap...  27.9 us
    ppermute x8, starting transfers between devices, padded_2(): lax.ppermute(head, axis, [((i + 1) % count, i) for i in range(ends)])  23.3 us
    ppermute x8, starting transfers between devices, padded_2(): lax.ppermute(tail, axis, [(i, (i + 1) % count) for i in range(ends)])  21.6 us
  transfers between devices with their start and end apart: 21, of which 3 were waited for; matrix products, arithmetic and copies ran while one was open for 23% of the time, Pallas kernels for 0%

commit v1 on v0

v1 whole, which is shorter than its diff:
```python
import functools

import jax
import jax.numpy as jnp
from jax import lax
from jax.experimental import pallas as pl
from jax.experimental.pallas import tpu as pltpu
from jax.sharding import PartitionSpec as P

epsilon = 1e-05
F32 = jnp.float32
BF16 = jnp.bfloat16
GROUP = 4
VMEM = pl.BlockSpec(memory_space=pltpu.VMEM)
SMEM = pl.BlockSpec(memory_space=pltpu.SMEM)


def call(body, outs, specs, args, scratch=(), flops=0, transcendentals=0, limit=48):
    moved = sum(a.size * a.dtype.itemsize for a in args)
    moved += sum(o.size * o.dtype.itemsize for o in outs)
    return pl.pallas_call(
        body,
        out_shape=tuple(outs),
        in_specs=specs,
        out_specs=tuple(VMEM for _ in outs),
        scratch_shapes=scratch,
        compiler_params=pltpu.CompilerParams(vmem_limit_bytes=limit << 20),
        cost_estimate=pl.CostEstimate(
            flops=flops, bytes_accessed=moved, transcendentals=transcendentals
        ),
    )(*args)


def shape(dims, dtype):
    return jax.ShapeDtypeStruct(dims, dtype)


def group_sums(acc):
    rows = acc.shape[0]
    row = lax.broadcasted_iota(jnp.int32, acc.shape, 0)
    step = 1
    while step < GROUP:
        up = pltpu.roll(acc, rows - step, axis=0)
        down = pltpu.roll(acc, step, axis=0)
        acc = acc + jnp.where((row & step) == 0, up, down)
        step *= 2
    return jnp.sum(acc, axis=1, keepdims=True)


def lanes_of(plane):
    total = plane[:, :128]
    for start in range(128, plane.shape[1], 128):
        total = total + plane[:, start : start + 128]
    return total


def as_rows(first, second):
    channels = first.shape[0]
    lane = lax.broadcasted_iota(jnp.int32, (channels, 128), 1)
    both = jnp.where(lane == 0, first, jnp.where(lane == 1, second, 0.0))
    return jnp.transpose(both)[:8]


def local_stats(planes, count):
    acc = None
    for plane in planes:
        part = lanes_of(plane())
        acc = part if acc is None else acc + part
    mean = group_sums(acc) / count
    acc = None
    for plane in planes:
        off = plane() - mean
        part = lanes_of(off * off)
        acc = part if acc is None else acc + part
    return as_rows(mean, group_sums(acc))


def columns_of(rows):
    return jnp.transpose(rows)


def sigmoid(value):
    return 0.5 + 0.5 * jnp.tanh(0.5 * value)


def stats_kernel(planes_ref, par_ref, out_ref):
    rows, frames, _, cols = planes_ref.shape
    scale = columns_of(par_ref[...])[:, 0:1]
    planes = [
        functools.partial(lambda r, t: planes_ref[r, t].astype(F32) * scale, r, t)
        for r in range(rows)
        for t in range(frames)
    ]
    out_ref[...] = local_stats(planes, float(GROUP * rows * frames * cols))


def source(own, other, top, bottom, other_first):
    def at(row, frame):
        if row == 0:
            return top, (frame,)
        if row == own.shape[0] + 1:
            return bottom, (frame,)
        if (frame < 2) == other_first:
            return other, (row - 1, frame % 2)
        return own, (row - 1, frame % 2)

    return at


def edges_kernel(flag_ref, own, other, top, bottom, out_ref, *, other_first):
    at = source(own, other, top, bottom, other_first)
    is_first = flag_ref[3] == 0
    channels = own.shape[2]
    lane = lax.broadcasted_iota(jnp.int32, (channels, 128), 1)
    acc = jnp.zeros((channels, 128), F32)
    for row in range(own.shape[0] + 2):
        for frame in range(4):
            ref, index = at(row, frame)
            plane = ref[index]
            last = pltpu.roll(plane[:, -128:].astype(F32), 1, axis=1)
            edge = jnp.where(is_first, last, plane[:, :128].astype(F32))
            number = 4 * row + frame
            moved = pltpu.roll(edge, number, axis=1) if number else edge
            acc = jnp.where(lane == number, moved, acc)
    out_ref[...] = acc.astype(BF16)


def fill_stack(stack, row, frame, plane, edge, on_left, on_right):
    channels, cols = plane.shape
    lane = lax.broadcasted_iota(jnp.int32, (channels, cols), 1)
    number = 4 * row + frame
    column = edge[:, number : number + 1]
    left = jnp.where(lane == 0, column * on_left, pltpu.roll(plane, 1, axis=1))
    right = jnp.where(lane == cols - 1, column * on_right, pltpu.roll(plane, cols - 1, axis=1))
    stack[row, frame, 0:channels] = left.astype(BF16)
    stack[row, frame, channels : 2 * channels] = plane.astype(BF16)
    stack[row, frame, 2 * channels : 3 * channels] = right.astype(BF16)


def sides(flag_ref):
    on_left = (flag_ref[3] != 0).astype(F32)
    on_right = (flag_ref[3] == 0).astype(F32)
    return on_left, on_right


def conv_rows(stack, weight, row):
    three = stack[row : row + 3].reshape(weight.shape[1], stack.shape[3])
    return jnp.dot(weight[...], three, preferred_element_type=F32)


def norm_columns(par_ref, st_ref, count, gain_row):
    par = par_ref[...]
    stats = st_ref[...]
    mean = stats[0:1]
    inverse = 1.0 / jnp.sqrt(stats[1:2] / count + epsilon)
    gain = par[gain_row : gain_row + 1]
    shift = par[gain_row + 1 : gain_row + 2]
    rows = jnp.concatenate([mean, inverse, gain, shift, par[0:1], stats[2:5]], axis=0)
    cols = columns_of(rows)
    return [cols[:, i : i + 1] for i in range(5)]


def conv_first_kernel(
    flag_ref, own, past, top, bottom, edge_ref, par_ref, st_ref, weight, hidden_ref, st_out, stack_ref, *, count
):
    rows, frames, channels, cols = own.shape
    at = source(own, past, top, bottom, True)
    mean, inverse, gain, shift, scale = norm_columns(par_ref, st_ref, count, 1)

    def act(latent):
        pre = (latent.astype(F32) * scale - mean) * inverse * gain + shift
        return pre * sigmoid(pre)

    has_past = flag_ref[0].astype(F32)
    has_top = flag_ref[1].astype(F32)
    has_bottom = flag_ref[2].astype(F32)
    on_left, on_right = sides(flag_ref)
    lane = lax.broadcasted_iota(jnp.int32, (channels, 128), 1)
    edge = act(edge_ref[...])
    edge = edge * jnp.where((lane & 3) < 2, has_past, 1.0)
    edge = edge * jnp.where(lane < 4, has_top, 1.0)
    edge = edge * jnp.where(lane >= 4 * (rows + 1), has_bottom, 1.0)
    for row in range(rows + 2):
        for frame in range(4):
            ref, index = at(row, frame)
            plane = act(ref[index])
            factor = None
            if frame < 2:
                factor = has_past
            if row in (0, rows + 1):
                beside = has_top if row == 0 else has_bottom
                factor = beside if factor is None else factor * beside
            if factor is not None:
                plane = plane * factor
            fill_stack(stack_ref, row, frame, plane, edge, on_left, on_right)
    for row in range(rows):
        out = conv_rows(stack_ref, weight, row)
        for frame in range(frames):
            hidden_ref[row, frame] = out[frame * channels : (frame + 1) * channels]
    planes = [
        functools.partial(lambda r, t: hidden_ref[r, t], r, t) for r in range(rows) for t in range(frames)
    ]
    st_out[...] = local_stats(planes, float(GROUP * rows * frames * cols))


def conv_back_kernel(flag_ref, own, future, top, bottom, edge_ref, weight, grad_ref, stack_ref):
    rows, frames, channels, cols = own.shape
    at = source(own, future, top, bottom, False)
    on_left, on_right = sides(flag_ref)
    edge = edge_ref[...].astype(F32)
    for row in range(rows + 2):
        for frame in range(4):
            ref, index = at(row, frame)
            fill_stack(stack_ref, row, frame, ref[index].astype(F32), edge, on_left, on_right)
    for row in range(rows):
        out = conv_rows(stack_ref, weight, row)
        for frame in range(frames):
            grad_ref[row, frame] = out[frame * channels : (frame + 1) * channels]


def norm_second_kernel(hidden, grad, par_ref, st_ref, act_ref, scaled_ref, sums_ref, *, count):
    rows, frames, channels, cols = hidden.shape
    mean, inverse, gain, shift, _ = norm_columns(par_ref, st_ref, count, 3)
    first = jnp.zeros((channels, 128), F32)
    second = jnp.zeros((channels, 128), F32)
    for row in range(rows):
        for frame in range(frames):
            normed = (hidden[row, frame] - mean) * inverse
            pre = normed * gain + shift
            sig = sigmoid(pre)
            act = pre * sig
            act_ref[row, frame] = act.astype(BF16)
            scaled = grad[row, frame] * (sig + act * (1.0 - sig)) * gain
            scaled_ref[row, frame] = scaled
            first = first + lanes_of(scaled)
            second = second + lanes_of(scaled * normed)
    sums_ref[...] = as_rows(group_sums(first), group_sums(second))


def hidden_grad_kernel(hidden, scaled, par_ref, st_ref, sums_ref, out_ref, *, count):
    rows, frames, channels, cols = hidden.shape
    mean, inverse, _, _, _ = norm_columns(par_ref, st_ref, count, 3)
    means = columns_of(sums_ref[...] / count)
    first, second = means[:, 0:1], means[:, 1:2]
    for row in range(rows):
        for frame in range(frames):
            normed = (hidden[row, frame] - mean) * inverse
            out_ref[row, frame] = (inverse * (scaled[row, frame] - first - normed * second)).astype(BF16)


def weight_second_kernel(stack_ref, act_ref, out_ref, right_ref):
    rows, frames, channels, cols = act_ref.shape
    for row in range(rows):
        right_ref[row * cols : (row + 1) * cols] = jnp.transpose(
            act_ref[row].reshape(frames * channels, cols)
        )
    right = right_ref[...]
    for down in range(3):
        parts = []
        for frame in range(4):
            left = jnp.concatenate([stack_ref[down + row, frame] for row in range(rows)], axis=1)
            parts.append(jnp.dot(left, right, preferred_element_type=F32))
        for kt in range(3):
            term = parts[2 - kt][:, :channels] + parts[3 - kt][:, channels:]
            for across in range(3):
                tap = 9 * kt + 3 * (2 - down) + (2 - across)
                out_ref[:, tap * channels : (tap + 1) * channels] = term[
                    across * channels : (across + 1) * channels
                ]


def weight_first_kernel(stack_ref, grad_ref, out_ref, right_ref):
    rows, frames, channels, cols = grad_ref.shape
    for row in range(rows):
        right_ref[row * cols : (row + 1) * cols] = jnp.transpose(
            grad_ref[row].reshape(frames * channels, cols)
        )
    right = right_ref[...]
    for down in range(3):
        parts = []
        for frame in range(4):
            left = jnp.concatenate([stack_ref[down + row, frame] for row in range(rows)], axis=1)
            parts.append(jnp.dot(left, right, preferred_element_type=F32))
        for kt in range(3):
            term = parts[kt][:, :channels] + parts[kt + 1][:, channels:]
            for across in range(3):
                tap = 9 * kt + 3 * down + across
                out_ref[:, tap * channels : (tap + 1) * channels] = jnp.transpose(
                    term[across * channels : (across + 1) * channels]
                )


def first_grad_kernel(
    flag_ref, own, future, top, bottom, edge_ref, weight, latent, par_ref, st_ref, scaled_ref, sums_ref, stack_ref,
    *, count
):
    rows, frames, channels, cols = own.shape
    at = source(own, future, top, bottom, False)
    on_left, on_right = sides(flag_ref)
    edge = edge_ref[...].astype(F32)
    mean, inverse, gain, shift, scale = norm_columns(par_ref, st_ref, count, 1)
    for row in range(rows + 2):
        for frame in range(4):
            ref, index = at(row, frame)
            fill_stack(stack_ref, row, frame, ref[index].astype(F32), edge, on_left, on_right)
    first = jnp.zeros((channels, 128), F32)
    second = jnp.zeros((channels, 128), F32)
    for row in range(rows):
        out = conv_rows(stack_ref, weight, row)
        for frame in range(frames):
            grad = out[frame * channels : (frame + 1) * channels]
            normed = (latent[row, frame].astype(F32) * scale - mean) * inverse
            pre = normed * gain + shift
            sig = sigmoid(pre)
            scaled = grad * (sig + pre * sig * (1.0 - sig)) * gain
            scaled_ref[row, frame] = scaled
            first = first + lanes_of(scaled)
            second = second + lanes_of(scaled * normed)
    sums_ref[...] = as_rows(group_sums(first), group_sums(second))


def decoded_grad_kernel(scaled, latent, cotangent, par_ref, st_ref, sums_ref, out_ref, *, count):
    rows, frames, channels, cols = latent.shape
    mean, inverse, _, _, scale = norm_columns(par_ref, st_ref, count, 1)
    means = columns_of(sums_ref[...] / count)
    first, second = means[:, 0:1], means[:, 1:2]
    for row in range(rows):
        for frame in range(frames):
            normed = (latent[row, frame].astype(F32) * scale - mean) * inverse
            out_ref[row, frame] = cotangent[row, frame].astype(F32) + inverse * (
                scaled[row, frame] - first - normed * second
            )


def weight_forward_kernel(weight, out_ref):
    channels = weight.shape[0]
    wide = 3 * channels
    for t in range(2):
        for kr in range(3):
            for f in range(4):
                kt = f - t
                here = slice((kr * 4 + f) * wide, (kr * 4 + f + 1) * wide)
                if 0 <= kt < 3:
                    tap = 3 * kt + kr
                    block = weight[:, tap * wide : (tap + 1) * wide]
                else:
                    block = jnp.zeros((channels, wide), BF16)
                out_ref[t * channels : (t + 1) * channels, here] = block


def weight_back_kernel(weight, out_ref):
    channels = weight.shape[0]
    for down in range(3):
        for across in range(3):
            blocks = [
                jnp.transpose(
                    weight[
                        :,
                        (9 * kt + 3 * (2 - down) + 2 - across) * channels : (9 * kt + 3 * (2 - down) + 3 - across)
                        * channels,
                    ]
                )
                for kt in range(3)
            ]
            for t in range(2):
                for f in range(4):
                    kt = t + 2 - f
                    start = ((down * 4 + f) * 3 + across) * channels
                    block = blocks[kt] if 0 <= kt < 3 else jnp.zeros((channels, channels), BF16)
                    out_ref[t * channels : (t + 1) * channels, start : start + channels] = block


def shifted(value, axis, steps):
    count = lax.axis_size(axis)
    initial, last = max(0, -steps), min(count, count - steps)
    return lax.ppermute(value, axis, [(source, source + steps) for source in range(initial, last)])


def rounds():
    for axis in ("width", "height", "tm"):
        step = 1
        while step < lax.axis_size(axis):
            yield axis, [(i, i ^ step) for i in range(lax.axis_size(axis))]
            step *= 2


def all_sum(value):
    for axis, pairs in rounds():
        value = value + lax.ppermute(value, axis, pairs)
    return value


def all_stats(value, count):
    for axis, pairs in rounds():
        other = lax.ppermute(value, axis, pairs)
        gap = value[0:1] - other[0:1]
        value = jnp.concatenate(
            [
                0.5 * (value[0:1] + other[0:1]),
                value[1:2] + other[1:2] + gap * gap * (0.5 * count),
                jnp.zeros_like(value[2:]),
            ],
            axis=0,
        )
        count = 2.0 * count
    return value


def reduce_weights(term, after):
    stages = (
        lambda v: lax.psum_scatter(v, "width", scatter_dimension=0, tiled=True),
        lambda v: lax.psum_scatter(v, "tm", scatter_dimension=0, tiled=True),
        lambda v: lax.psum(v, "height"),
        lambda v: lax.all_gather(v, "tm", axis=0, tiled=True),
        lambda v: lax.all_gather(v, "width", axis=0, tiled=True),
    )
    results = []
    for number, stage in enumerate(stages):
        if after:
            term, _ = lax.optimization_barrier((term, after[number]))
        term = stage(term)
        results.append(term)
    return term, results


def extended(flags, own, steps):
    other = shifted(own, "tm", steps)
    pair = (other, own) if steps > 0 else (own, other)
    top = shifted(jnp.concatenate([part[-1] for part in pair], axis=0), "height", 1)
    bottom = shifted(jnp.concatenate([part[0] for part in pair], axis=0), "height", -1)
    channels = own.shape[2]
    (edge,) = call(
        functools.partial(edges_kernel, other_first=steps > 0),
        [shape((channels, 128), BF16)],
        [SMEM] + [VMEM] * 4,
        (flags, own, other, top, bottom),
    )
    edge = lax.ppermute(edge, "width", [(0, 1), (1, 0)])
    return other, top, bottom, edge


def shards(
    latent,
    exponents,
    cotangent,
    conv_first,
    conv_second,
    gain_first,
    shift_first,
    gain_second,
    shift_second,
):
    channels, frames, rows, cols = latent.shape
    groups = exponents.shape[0]
    devices = lax.axis_size("tm") * lax.axis_size("height") * lax.axis_size("width")
    here = channels // groups * frames * rows * cols
    count = float(here * devices)
    tm, height, width = (lax.axis_index(axis) for axis in ("tm", "height", "width"))
    flags = jnp.stack(
        [
            (tm > 0).astype(jnp.int32),
            (height > 0).astype(jnp.int32),
            (height < lax.axis_size("height") - 1).astype(jnp.int32),
            width.astype(jnp.int32),
        ]
    )
    scale = jnp.repeat(jnp.exp2(exponents.astype(F32)), channels // groups)
    zeros = jnp.zeros_like(scale)
    par = jnp.stack([scale, gain_first, shift_first, gain_second, shift_second, zeros, zeros, zeros])
    latent = latent.transpose(2, 1, 0, 3)
    cotangent = cotangent.transpose(2, 1, 0, 3)
    block = (rows, frames, channels, cols)
    stack = (rows + 2, 4, 3 * channels, cols)
    taps = (2 * channels, 36 * channels)
    conv_flops = 2 * 4 * 256 * 36 * channels * 2 * channels
    small = shape((8, channels), F32)

    (stats_first,) = call(stats_kernel, [small], [VMEM] * 2, (latent, par))
    past, top, bottom, edge = extended(flags, latent, 1)
    future_c, top_c, bottom_c, edge_c = extended(flags, cotangent, -1)
    stats_first = all_stats(stats_first, float(here))
    (weight_first,) = call(weight_forward_kernel, [shape(taps, BF16)], [VMEM], (conv_first,))
    (weight_second_t,) = call(weight_back_kernel, [shape(taps, BF16)], [VMEM], (conv_second,))
    (weight_first_t,) = call(weight_back_kernel, [shape(taps, BF16)], [VMEM], (conv_first,))

    hidden, stats_second, stack_first = call(
        functools.partial(conv_first_kernel, count=count),
        [shape(block, F32), small, shape(stack, BF16)],
        [SMEM] + [VMEM] * 8,
        (flags, latent, past, top, bottom, edge, par, stats_first, weight_first),
        flops=conv_flops,
        transcendentals=3 * latent.size,
    )
    stats_second = all_stats(stats_second, float(here))
    grad_second, stack_c = call(
        conv_back_kernel,
        [shape(block, F32), shape(stack, BF16)],
        [SMEM] + [VMEM] * 6,
        (flags, cotangent, future_c, top_c, bottom_c, edge_c, weight_second_t),
        flops=conv_flops,
    )
    act_second, scaled, sums = call(
        functools.partial(norm_second_kernel, count=count),
        [shape(block, BF16), shape(block, F32), small],
        [VMEM] * 4,
        (hidden, grad_second, par, stats_second),
        transcendentals=latent.size,
    )
    sums = all_sum(sums)
    (conv_second_grad,) = call(
        weight_second_kernel,
        [shape((channels, 27 * channels), F32)],
        [VMEM] * 2,
        (stack_c, act_second),
        scratch=[pltpu.VMEM((rows * cols, frames * channels), BF16)],
        flops=conv_flops,
    )
    conv_second_grad, stages = reduce_weights(conv_second_grad, None)
    (hidden_grad,) = call(
        functools.partial(hidden_grad_kernel, count=count),
        [shape(block, BF16)],
        [VMEM] * 5,
        (hidden, scaled, par, stats_second, sums),
    )
    future, top, bottom, edge = extended(flags, hidden_grad, -1)
    (conv_first_grad,) = call(
        weight_first_kernel,
        [shape((channels, 27 * channels), F32)],
        [VMEM] * 2,
        (stack_first, hidden_grad),
        scratch=[pltpu.VMEM((rows * cols, frames * channels), BF16)],
        flops=conv_flops,
    )
    conv_first_grad, _ = reduce_weights(conv_first_grad, stages)
    scaled, sums = call(
        functools.partial(first_grad_kernel, count=count),
        [shape(block, F32), small],
        [SMEM] + [VMEM] * 9,
        (flags, hidden_grad, future, top, bottom, edge, weight_first_t, latent, par, stats_first),
        scratch=[pltpu.VMEM(stack, BF16)],
        flops=conv_flops,
        transcendentals=latent.size,
    )
    sums = all_sum(sums)
    (decoded_grad,) = call(
        functools.partial(decoded_grad_kernel, count=count),
        [shape(block, F32)],
        [VMEM] * 6,
        (scaled, latent, cotangent, par, stats_first, sums),
    )
    return decoded_grad.transpose(2, 1, 0, 3), conv_first_grad, conv_second_grad


def solution(mesh):
    block = P(None, "tm", "height", "width")
    return jax.shard_map(
        shards,
        mesh=mesh,
        in_specs=(block, P(), block, P(), P(), P(), P(), P(), P()),
        out_specs=(block, P(), P()),
        check_vma=False,
    )
```

time: 657 us -> 347 us (0.53); the launches traced: 646 us -> 342 us
  blocking collectives: 242 us -> 36.4 us
  local copies, waits for them, and re-layouts: 147 us -> 14 us
  waiting for transfers between devices: 78.7 us -> 177 us
  other arithmetic: 63.5 us -> 1.73 us
  matrix products: 42.9 us -> 0 us
  Pallas kernels: 0 us -> 36.6 us
  starting transfers between devices: 54.9 us -> 61.9 us
    psum x6 -> x0, blocking collectives: 242 us -> none  [across(): return lax.psum(terms, ('tm', 'height', 'width'))]
    reduce_scatter x0 -> x4, waiting for transfers between devices: none -> 54.2 us  [the longest x2 34.6 us: reduce_weights(): lax.psum_scatter(v, 'tm', scatter_dimension=0, tiled=True)]
    concatenate x32 -> x16, other arithmetic: 49.1 us -> 0.88 us  [the longest x10 0.72 us: all_stats(): jnp.concatenate([0.5 * (value[0:1] + other[0:1]), value[1:2] + other[1:2]...]
    ppermute x20 -> x32, waiting for transfers between devices: 3.33 us -> 50.1 us  [the longest x9 25.8 us: shifted(): lax.ppermute(value, axis, [(source, source + steps) for source in range(i...]
    dot_general x45 -> x0, matrix products: 42.9 us -> none  [the longest x18 18.1 us: weight_terms(): lax.dot_general(flat_grad, stacked, (((1,), (1,)), ((), ())), preferred_e...]
    slice x26 -> x0, local copies, waits for them, and re-layouts: 41.4 us -> none  [the longest x12 27.9 us: tap_stack(): padded[:, first:first + frame_count, top:top + row_count, col_tap:col_tap...]
    concatenate x18 -> x1, local copies, waits for them, and re-layouts: 36.9 us -> 0.08 us  [all_stats(): jnp.concatenate([0.5 * (value[0:1] + other[0:1]), value[1:2] + other[1:2]...]
    pallas_call x0 -> x15, Pallas kernels: none -> 36.6 us  [call(): pl.pallas_call(body, out_shape=tuple(outs), in_specs=specs, out_specs=tup...]
  transfers between devices with their start and end apart: 21 -> 40, of which waited for: 3 -> 29; matrix products, arithmetic and copies ran while one was open for 23% -> 1% of each run, Pallas kernels for 0% -> 9%
where the time goes in v1:
time: 347 us; the launch traced here: 342 us
  waiting for transfers between devices  177 us (51%)
  starting transfers between devices  61.9 us (18%)
  Pallas kernels  36.6 us (11%)
  blocking collectives  36.4 us (10%)
  between operations  14.6 us (4%)
  local copies, waits for them, and re-layouts  14 us (4%)
    psum x2, waiting for transfers between devices, reduce_weights(): lax.psum(v, 'height')  72 us
    pallas_call x15, Pallas kernels, call(): pl.pallas_call(body, out_shape=tuple(outs), in_specs=specs, out_specs=tup...  36.6 us
    all_gather x2, blocking collectives, reduce_weights(): lax.all_gather(v, 'tm', axis=0, tiled=True)  36.4 us
    reduce_scatter x2, waiting for transfers between devices, reduce_weights(): lax.psum_scatter(v, 'tm', scatter_dimension=0, tiled=True)  34.6 us
    ppermute x9, waiting for transfers between devices, shifted(): lax.ppermute(value, axis, [(source, source + steps) for source in range(i...  25.8 us
    ppermute x9, starting transfers between devices, shifted(): lax.ppermute(value, axis, [(source, source + steps) for source in range(i...  20 us
    reduce_scatter x2, waiting for transfers between devices, reduce_weights(): lax.psum_scatter(v, 'width', scatter_dimension=0, tiled=True)  19.6 us
    ppermute x10, starting transfers between devices, all_sum(): value = value + lax.ppermute(value, axis, pairs)  14.8 us
  transfers between devices with their start and end apart: 40, of which 29 were waited for; matrix products, arithmetic and copies ran while one was open for 1% of the time, Pallas kernels for 9%

profile of v1, /device:TPU:1, one launch (start us, length us, event | category | flops | bytes accessed | tf_op | source)
XLA Modules:
  0.0 342.3 jit_solution(9809282823081760224)
XLA Ops:
  11.5 2.4 collective-permute-start.5
  13.8 3.2 collective-permute-start
  21.0 2.4 collective-permute-start.7
  24.1 7.5 %collective-permute-done.7 = f32[8,128]{1,0:T(8,128)S(1)} collective-permute-done((f32[8,128]{1,0:T(8,128)S(1)}, f32[8,128]{1,0:T(8,128)S(1)}, u32[]{:S(2)}, u32[]{:S(2)}) %collective-permute-start.7) | collective-permute-done | bytes 4128 | tf_op jit(solution)/shard_map/ppermute | solution.py:395
  31.7 2.3 collective-permute-start.8
  35.3 4.0 %collective-permute-start.1 = (bf16[4,128,256]{2,1,0:T(8,128)(2,1)S(1)}, bf16[4,128,256]{2,1,0:T(8,128)(2,1)S(1)}, u32[]{:S(2)}, u32[]{:S(2)}) collective-permute-start(bf16[4,128,256]{2,1,0:T(8,128)(2,1)S(1)} %pad_maximum_fusion), channel_id=1, source_target_pairs={{0,2},{2,4},{4,6},{1,3},{3,5},{5,7},{8,10},{10,12},{12,14},{9,11},... | collective-permute-start | bytes 786440 | tf_op jit(solution)/shard_map/ppermute | solution.py:376
  42.6 2.1 shard_map.112
  44.8 4.6 %collective-permute-start.3 = (bf16[128,128]{1,0:T(8,128)(2,1)S(1)}, bf16[128,128]{1,0:T(8,128)(2,1)S(1)}, u32[]{:S(2)}, u32[]{:S(2)}) collective-permute-start(bf16[128,128]{1,0:T(8,128)(2,1)S(1)} %shard_map.112), channel_id=1, source_target_pairs={{0,1},{1,0},{2,3},{3,2},{4,5},{5,4},{6,7},{7,6},{8,9},{9,8},{10,11... | collective-permute-start | bytes 98312 | tf_op jit(solution)/shard_map/ppermute | solution.py:438
  51.3 7.2 %shard_map.115 = (f32[4,2,128,256]{3,2,1,0:T(8,128)S(1)}, f32[8,128]{1,0:T(8,128)S(1)}, bf16[6,4,384,256]{3,2,1,0:T(8,128)(2,1)}) custom-call(s32[4]{0:T(128)S(1)} %pad_add_fusion.flag_ref, bf16[4,2,128,256]{3,2,1,0:T(8,128)(2,1)S(1)} %get-tuple-element.72.own.planes_ref.latent, bf16[4,2,128,256]{3,2,1,0:T(8,128)(2,1)S(1)} %copy-done.4, ...), custom_call_target="tpu_custom_call" | custom-call | flops 2415919104 | bytes 9744400 | tf_op jit(solution)/shard_map/pallas_call | solution.py:21
  59.7 2.4 collective-permute-start.14
  64.1 3.4 collective-permute-start.15
  69.5 9.2 %collective-permute-done.11.bottom = bf16[4,128,256]{2,1,0:T(8,128)(2,1)S(1)} collective-permute-done((bf16[4,128,256]{2,1,0:T(8,128)(2,1)S(1)}, bf16[4,128,256]{2,1,0:T(8,128)(2,1)S(1)}, u32[]{:S(2)}, u32[]{:S(2)}) %collective-permute-start.11) | collective-permute-done | bytes 262176 | tf_op jit(solution)/shard_map/ppermute | solution.py:376
  78.7 2.1 shard_map.116
  83.3 5.3 %shard_map.118 = (f32[4,2,128,256]{3,2,1,0:T(8,128)S(1)}, bf16[6,4,384,256]{3,2,1,0:T(8,128)(2,1)}) custom-call(s32[4]{0:T(128)S(1)} %pad_add_fusion.flag_ref, bf16[4,2,128,256]{3,2,1,0:T(8,128)(2,1)S(1)} %get-tuple-element.71.own.cotangent, bf16[4,2,128,256]{3,2,1,0:T(8,128)(2,1)S(1)} %collective-permute-done.9.other.future, ...), custom_call_target="tpu_custom_call" | custom-call | flops 2415919104 | bytes 9732112 | tf_op jit(solution)/shard_map/pallas_call | solution.py:21
  90.7 5.0 %shard_map.126 = f32[128,3456]{1,0:T(8,128)S(1)} custom-call(bf16[6,4,384,256]{3,2,1,0:T(8,128)(2,1)} %get-tuple-element.26.stack_ref, bf16[4,2,128,256]{3,2,1,0:T(8,128)(2,1)S(1)} %get-tuple-element.27.act_ref), custom_call_target="tpu_custom_call" | custom-call | flops 2415919104 | bytes 7012352 | tf_op jit(solution)/shard_map/pallas_call | solution.py:21
  97.0 7.9 %reduce-scatter.5.cloned.1.call-done = f32[64,3456]{1,0:T(8,128)} async-done(((f32[128,3456]{1,0:T(8,128)}), f32[64,3456]{1,0:T(8,128)}) %reduce-scatter.5.cloned.1.call-update) | async-done | bytes 884752 | tf_op jit(solution)/shard_map/reduce_scatter | solution.py:411
  113.7 2.4 collective-permute-start.22
  118.9 5.1 %shard_map.125 = f32[128,3456]{1,0:T(8,128)S(1)} custom-call(bf16[6,4,384,256]{3,2,1,0:T(8,128)(2,1)} %get-tuple-element.25.stack_ref, bf16[4,2,128,256]{3,2,1,0:T(8,128)(2,1)S(1)} %shard_map.120.own.grad_ref), custom_call_target="tpu_custom_call" | custom-call | flops 2415919104 | bytes 7012352 | tf_op jit(solution)/shard_map/pallas_call | solution.py:21
  125.3 7.5 %reduce-scatter.9.cloned.1.call-done = f32[16,3456]{1,0:T(8,128)} async-done(((f32[64,3456]{1,0:T(8,128)}), f32[16,3456]{1,0:T(8,128)}) %reduce-scatter.9.cloned.1.call-update) | async-done | bytes 221200 | tf_op jit(solution)/shard_map/reduce_scatter | solution.py:412
  132.8 11.7 %reduce-scatter.7.cloned.1.call-done = f32[64,3456]{1,0:T(8,128)} async-done(((f32[128,3456]{1,0:T(8,128)}), f32[64,3456]{1,0:T(8,128)}) %reduce-scatter.7.cloned.1.call-update) | async-done | bytes 884752 | tf_op jit(solution)/shard_map/reduce_scatter | solution.py:411
  145.1 45.3 %all-reduce.3.cloned.1.call-done = f32[16,3456]{1,0:T(8,128)} async-done(((f32[16,3456]{1,0:T(8,128)}), f32[16,3456]{1,0:T(8,128)}) %all-reduce.3.cloned.1.call-update) | async-done | bytes 221200 | tf_op jit(solution)/shard_map/psum | solution.py:413
  190.4 27.1 %reduce-scatter.11.cloned.1.call-done = f32[16,3456]{1,0:T(8,128)} async-done(((f32[64,3456]{1,0:T(8,128)}), f32[16,3456]{1,0:T(8,128)}) %reduce-scatter.11.cloned.1.call-update) | async-done | bytes 221200 | tf_op jit(solution)/shard_map/reduce_scatter | solution.py:412
  217.6 17.7 %all_gather.12 = f32[64,3456]{1,0:T(8,128)} all-gather(f32[16,3456]{1,0:T(8,128)} %all-reduce.3.cloned.1.call-done), channel_id=1, replica_groups=mesh['tm'=4,'height'=4,'width'=2] {'tm'}, dimensions={0}, use_global_device_ids=true | all-gather | bytes 1105920 | tf_op jit(solution)/shard_map/all_gather | solution.py:414
  235.4 26.7 %all-reduce.5.cloned.1.call-done = f32[16,3456]{1,0:T(8,128)} async-done(((f32[16,3456]{1,0:T(8,128)}), f32[16,3456]{1,0:T(8,128)}) %all-reduce.5.cloned.1.call-update) | async-done | bytes 221200 | tf_op jit(solution)/shard_map/psum | solution.py:413
  262.1 18.6 %all_gather.13 = f32[64,3456]{1,0:T(8,128)} all-gather(f32[16,3456]{1,0:T(8,128)} %all-reduce.5.cloned.1.call-done), channel_id=1, replica_groups=mesh['tm'=4,'height'=4,'width'=2] {'tm'}, dimensions={0}, use_global_device_ids=true | all-gather | bytes 1105920 | tf_op jit(solution)/shard_map/all_gather | solution.py:414
  282.1 10.5 %collective-permute-done.23.other.future = bf16[4,2,128,256]{3,2,1,0:T(8,128)(2,1)S(1)} collective-permute-done((bf16[4,2,128,256]{3,2,1,0:T(8,128)(2,1)S(1)}, bf16[4,2,128,256]{3,2,1,0:T(8,128)(2,1)S(1)}, u32[]{:S(2)}, u32[]{:S(2)}) %collective-permute-start.23) | collective-permute-done | bytes 524320 | tf_op jit(solution)/shard_map/ppermute | solution.py:376
  294.0 4.2 %collective-permute-start.24 = (bf16[4,128,256]{2,1,0:T(8,128)(2,1)S(1)}, bf16[4,128,256]{2,1,0:T(8,128)(2,1)S(1)}, u32[]{:S(2)}, u32[]{:S(2)}) collective-permute-start(bf16[4,128,256]{2,1,0:T(8,128)(2,1)S(1)} %pad_maximum_fusion.4), channel_id=1, source_target_pairs={{0,2},{2,4},{4,6},{1,3},{3,5},{5,7},{8,10},{10,12},{12,14},{9,11},... | collective-permute-start | bytes 786440 | tf_op jit(solution)/shard_map/ppermute | solution.py:376
  303.5 6.1 %collective-permute-start.26 = (bf16[128,128]{1,0:T(8,128)(2,1)S(1)}, bf16[128,128]{1,0:T(8,128)(2,1)S(1)}, u32[]{:S(2)}, u32[]{:S(2)}) collective-permute-start(bf16[128,128]{1,0:T(8,128)(2,1)S(1)} %shard_map.121), channel_id=1, source_target_pairs={{0,1},{1,0},{2,3},{3,2},{4,5},{5,4},{6,7},{7,6},{8,9},{9,8},{10,11... | collective-permute-start | bytes 98312 | tf_op jit(solution)/shard_map/ppermute | solution.py:438
  310.4 4.1 %shard_map.123 = (f32[4,2,128,256]{3,2,1,0:T(8,128)S(1)}, f32[8,128]{1,0:T(8,128)S(1)}) custom-call(s32[4]{0:T(128)S(1)} %pad_add_fusion.flag_ref, bf16[4,2,128,256]{3,2,1,0:T(8,128)(2,1)S(1)} %shard_map.120.own.grad_ref, bf16[4,2,128,256]{3,2,1,0:T(8,128)(2,1)S(1)} %collective-permute-done.23.other.future, ...), custom_call_target="tpu_custom_call" | custom-call | flops 2415919104 | bytes 5550096 | tf_op jit(solution)/shard_map/pallas_call | solution.py:21
  318.8 3.4 collective-permute-start.29
  326.9 2.2 collective-permute-done.31
  331.3 2.9 copy.24
  (158 shorter events, 61.1 us)
Async XLA Ops:
  7.2 97.7 %reduce-scatter.5.cloned.1.call-start = ((), (), s32[]{:S(2)}) async-start(), calls=%async_computation.4 | async-start | bytes 2654208 | tf_op jit(solution)/shard_map/reduce_scatter | solution.py:411
  11.5 6.9 %collective-permute-start.5 = (f32[8,128]{1,0:T(8,128)S(1)}, f32[8,128]{1,0:T(8,128)S(1)}, u32[]{:S(2)}, u32[]{:S(2)}) collective-permute-start(f32[8,128]{1,0:T(8,128)S(1)} %maximum_maximum_fusion), channel_id=1, source_target_pairs={{0,2},{2,0},{4,6},{6,4},{1,3},{3,1},{5,7},{7,5},{8,10},{10,8},{12,... | collective-permute-start | bytes 12296 | tf_op jit(solution)/shard_map/ppermute | solution.py:395
  13.8 20.1 %collective-permute-start = (bf16[4,2,128,256]{3,2,1,0:T(8,128)(2,1)S(1)}, bf16[4,2,128,256]{3,2,1,0:T(8,128)(2,1)S(1)}, u32[]{:S(2)}, u32[]{:S(2)}) collective-permute-start(bf16[4,2,128,256]{3,2,1,0:T(8,128)(2,1)S(1)} %get-tuple-element.72.own.planes_ref.latent), channel_id=1, source_target_pairs={{0,8},{8,16},{16,24},{1,9},{9,17},{17,25},{2,10},{10,18},{18,26},{... | collective-permute-start | bytes 1572872 | tf_op jit(solution)/shard_map/ppermute | solution.py:376
  17.1 41.7 %collective-permute-start.9 = (bf16[4,2,128,256]{3,2,1,0:T(8,128)(2,1)S(1)}, bf16[4,2,128,256]{3,2,1,0:T(8,128)(2,1)S(1)}, u32[]{:S(2)}, u32[]{:S(2)}) collective-permute-start(bf16[4,2,128,256]{3,2,1,0:T(8,128)(2,1)S(1)} %get-tuple-element.71.own.cotangent), channel_id=1, source_target_pairs={{8,0},{16,8},{24,16},{9,1},{17,9},{25,17},{10,2},{18,10},{26,18},{... | collective-permute-start | bytes 1572872 | tf_op jit(solution)/shard_map/ppermute | solution.py:376
  21.0 10.6 %collective-permute-start.7 = (f32[8,128]{1,0:T(8,128)S(1)}, f32[8,128]{1,0:T(8,128)S(1)}, u32[]{:S(2)}, u32[]{:S(2)}) collective-permute-start(f32[8,128]{1,0:T(8,128)S(1)} %maximum_maximum_fusion.2), channel_id=1, source_target_pairs={{0,8},{8,0},{16,24},{24,16},{1,9},{9,1},{17,25},{25,17},{2,10},{10... | collective-permute-start | bytes 12296 | tf_op jit(solution)/shard_map/ppermute | solution.py:395
  31.7 8.0 %collective-permute-start.8 = (f32[8,128]{1,0:T(8,128)S(1)}, f32[8,128]{1,0:T(8,128)S(1)}, u32[]{:S(2)}, u32[]{:S(2)}) collective-permute-start(f32[8,128]{1,0:T(8,128)S(1)} %maximum_maximum_fusion.3), channel_id=1, source_target_pairs={{0,16},{8,24},{16,0},{24,8},{1,17},{9,25},{17,1},{25,9},{2,18},{10... | collective-permute-start | bytes 12296 | tf_op jit(solution)/shard_map/ppermute | solution.py:395
  34.0 7.6 %collective-permute-start.2 = (bf16[4,128,256]{2,1,0:T(8,128)(2,1)S(1)}, bf16[4,128,256]{2,1,0:T(8,128)(2,1)S(1)}, u32[]{:S(2)}, u32[]{:S(2)}) collective-permute-start(bf16[4,128,256]{2,1,0:T(8,128)(2,1)S(1)} %pad_maximum_fusion.1), channel_id=1, source_target_pairs={{2,0},{4,2},{6,4},{3,1},{5,3},{7,5},{10,8},{12,10},{14,12},{11,9},... | collective-permute-start | bytes 786440 | tf_op jit(solution)/shard_map/ppermute | solution.py:376
  35.3 7.3 %collective-permute-start.1 = (bf16[4,128,256]{2,1,0:T(8,128)(2,1)S(1)}, bf16[4,128,256]{2,1,0:T(8,128)(2,1)S(1)}, u32[]{:S(2)}, u32[]{:S(2)}) collective-permute-start(bf16[4,128,256]{2,1,0:T(8,128)(2,1)S(1)} %pad_maximum_fusion), channel_id=1, source_target_pairs={{0,2},{2,4},{4,6},{1,3},{3,5},{5,7},{8,10},{10,12},{12,14},{9,11},... | collective-permute-start | bytes 786440 | tf_op jit(solution)/shard_map/ppermute | solution.py:376
  44.8 5.4 %collective-permute-start.3 = (bf16[128,128]{1,0:T(8,128)(2,1)S(1)}, bf16[128,128]{1,0:T(8,128)(2,1)S(1)}, u32[]{:S(2)}, u32[]{:S(2)}) collective-permute-start(bf16[128,128]{1,0:T(8,128)(2,1)S(1)} %shard_map.112), channel_id=1, source_target_pairs={{0,1},{1,0},{2,3},{3,2},{4,5},{5,4},{6,7},{7,6},{8,9},{9,8},{10,11... | collective-permute-start | bytes 98312 | tf_op jit(solution)/shard_map/ppermute | solution.py:438
  59.7 4.4 %collective-permute-start.14 = (f32[8,128]{1,0:T(8,128)S(1)}, f32[8,128]{1,0:T(8,128)S(1)}, u32[]{:S(2)}, u32[]{:S(2)}) collective-permute-start(f32[8,128]{1,0:T(8,128)S(1)} %maximum_maximum_fusion.5), channel_id=1, source_target_pairs={{0,2},{2,0},{4,6},{6,4},{1,3},{3,1},{5,7},{7,5},{8,10},{10,8},{12,... | collective-permute-start | bytes 12296 | tf_op jit(solution)/shard_map/ppermute | solution.py:395
  62.1 7.4 %collective-permute-start.10 = (bf16[4,128,256]{2,1,0:T(8,128)(2,1)S(1)}, bf16[4,128,256]{2,1,0:T(8,128)(2,1)S(1)}, u32[]{:S(2)}, u32[]{:S(2)}) collective-permute-start(bf16[4,128,256]{2,1,0:T(8,128)(2,1)S(1)} %pad_maximum_fusion.2), channel_id=1, source_target_pairs={{0,2},{2,4},{4,6},{1,3},{3,5},{5,7},{8,10},{10,12},{12,14},{9,11},... | collective-permute-start | bytes 786440 | tf_op jit(solution)/shard_map/ppermute | solution.py:376
  64.1 4.9 %collective-permute-start.15 = (f32[8,128]{1,0:T(8,128)S(1)}, f32[8,128]{1,0:T(8,128)S(1)}, u32[]{:S(2)}, u32[]{:S(2)}) collective-permute-start(f32[8,128]{1,0:T(8,128)S(1)} %maximum_maximum_fusion.6), channel_id=1, source_target_pairs={{0,4},{2,6},{4,0},{6,2},{1,5},{3,7},{5,1},{7,3},{8,12},{10,14},{12... | collective-permute-start | bytes 12296 | tf_op jit(solution)/shard_map/ppermute | solution.py:395
  67.5 11.2 %collective-permute-start.11 = (bf16[4,128,256]{2,1,0:T(8,128)(2,1)S(1)}, bf16[4,128,256]{2,1,0:T(8,128)(2,1)S(1)}, u32[]{:S(2)}, u32[]{:S(2)}) collective-permute-start(bf16[4,128,256]{2,1,0:T(8,128)(2,1)S(1)} %pad_maximum_fusion.3), channel_id=1, source_target_pairs={{2,0},{4,2},{6,4},{3,1},{5,3},{7,5},{10,8},{12,10},{14,12},{11,9},... | collective-permute-start | bytes 786440 | tf_op jit(solution)/shard_map/ppermute | solution.py:376
  69.1 13.4 %collective-permute-start.16 = (f32[8,128]{1,0:T(8,128)S(1)}, f32[8,128]{1,0:T(8,128)S(1)}, u32[]{:S(2)}, u32[]{:S(2)}) collective-permute-start(f32[8,128]{1,0:T(8,128)S(1)} %maximum_maximum_fusion.7), channel_id=1, source_target_pairs={{0,8},{8,0},{16,24},{24,16},{1,9},{9,1},{17,25},{25,17},{2,10},{10... | collective-permute-start | bytes 12296 | tf_op jit(solution)/shard_map/ppermute | solution.py:395
  82.5 6.1 %collective-permute-start.17 = (f32[8,128]{1,0:T(8,128)S(1)}, f32[8,128]{1,0:T(8,128)S(1)}, u32[]{:S(2)}, u32[]{:S(2)}) collective-permute-start(f32[8,128]{1,0:T(8,128)S(1)} %maximum_maximum_fusion.8), channel_id=1, source_target_pairs={{0,16},{8,24},{16,0},{24,8},{1,17},{9,25},{17,1},{25,9},{2,18},{10... | collective-permute-start | bytes 12296 | tf_op jit(solution)/shard_map/ppermute | solution.py:395
  96.9 35.8 %reduce-scatter.9.cloned.1.call-start = ((), (), s32[]{:S(2)}) async-start(), calls=%async_computation.6 | async-start | bytes 1105920 | tf_op jit(solution)/shard_map/reduce_scatter | solution.py:412
  104.9 39.6 %reduce-scatter.7.cloned.1.call-start = ((), (), s32[]{:S(2)}) async-start(), calls=%async_computation.5 | async-start | bytes 2654208 | tf_op jit(solution)/shard_map/reduce_scatter | solution.py:411
  106.2 2.6 collective-permute-start.19
  108.8 2.5 collective-permute-start.20
  113.7 3.4 %collective-permute-start.22 = (f32[8,128]{1,0:T(8,128)S(1)}, f32[8,128]{1,0:T(8,128)S(1)}, u32[]{:S(2)}, u32[]{:S(2)}) collective-permute-start(f32[8,128]{1,0:T(8,128)S(1)} %add.165), channel_id=1, source_target_pairs={{0,16},{8,24},{16,0},{24,8},{1,17},{9,25},{17,1},{25,9},{2,18},{10... | collective-permute-start | bytes 12296 | tf_op jit(solution)/shard_map/ppermute | solution.py:389
  125.2 65.2 %all-reduce.3.cloned.1.call-start = ((), (), s32[]{:S(2)}) async-start(), calls=%async_computation.8 | async-start | bytes 442368 | tf_op jit(solution)/shard_map/psum | solution.py:413
  144.5 73.0 %reduce-scatter.11.cloned.1.call-start = ((), (), s32[]{:S(2)}) async-start(), calls=%async_computation.7 | async-start | bytes 1105920 | tf_op jit(solution)/shard_map/reduce_scatter | solution.py:412
  145.1 117.0 %all-reduce.5.cloned.1.call-start = ((), (), s32[]{:S(2)}) async-start(), calls=%async_computation.9 | async-start | bytes 442368 | tf_op jit(solution)/shard_map/psum | solution.py:413
  217.6 63.2 %all-gather.3.cloned.1.call-start = ((), (), s32[]{:S(2)}) async-start(), calls=%async_computation.10 | async-start | bytes 2654208 | tf_op jit(solution)/shard_map/all_gather | solution.py:415
  235.4 95.9 %all-gather.5.cloned.1.call-start = ((), (), s32[]{:S(2)}) async-start(), calls=%async_computation.11 | async-start | bytes 2654208 | tf_op jit(solution)/shard_map/all_gather | solution.py:415
  280.8 11.8 %collective-permute-start.23 = (bf16[4,2,128,256]{3,2,1,0:T(8,128)(2,1)S(1)}, bf16[4,2,128,256]{3,2,1,0:T(8,128)(2,1)S(1)}, u32[]{:S(2)}, u32[]{:S(2)}) collective-permute-start(bf16[4,2,128,256]{3,2,1,0:T(8,128)(2,1)S(1)} %shard_map.120.own.grad_ref), channel_id=1, source_target_pairs={{8,0},{16,8},{24,16},{9,1},{17,9},{25,17},{10,2},{18,10},{26,18},{... | collective-permute-start | bytes 1572872 | tf_op jit(solution)/shard_map/ppermute | solution.py:376
  292.7 7.1 %collective-permute-start.25 = (bf16[4,128,256]{2,1,0:T(8,128)(2,1)S(1)}, bf16[4,128,256]{2,1,0:T(8,128)(2,1)S(1)}, u32[]{:S(2)}, u32[]{:S(2)}) collective-permute-start(bf16[4,128,256]{2,1,0:T(8,128)(2,1)S(1)} %pad_maximum_fusion.5), channel_id=1, source_target_pairs={{2,0},{4,2},{6,4},{3,1},{5,3},{7,5},{10,8},{12,10},{14,12},{11,9},... | collective-permute-start | bytes 786440 | tf_op jit(solution)/shard_map/ppermute | solution.py:376
  294.0 7.3 %collective-permute-start.24 = (bf16[4,128,256]{2,1,0:T(8,128)(2,1)S(1)}, bf16[4,128,256]{2,1,0:T(8,128)(2,1)S(1)}, u32[]{:S(2)}, u32[]{:S(2)}) collective-permute-start(bf16[4,128,256]{2,1,0:T(8,128)(2,1)S(1)} %pad_maximum_fusion.4), channel_id=1, source_target_pairs={{0,2},{2,4},{4,6},{1,3},{3,5},{5,7},{8,10},{10,12},{12,14},{9,11},... | collective-permute-start | bytes 786440 | tf_op jit(solution)/shard_map/ppermute | solution.py:376
  303.5 6.9 %collective-permute-start.26 = (bf16[128,128]{1,0:T(8,128)(2,1)S(1)}, bf16[128,128]{1,0:T(8,128)(2,1)S(1)}, u32[]{:S(2)}, u32[]{:S(2)}) collective-permute-start(bf16[128,128]{1,0:T(8,128)(2,1)S(1)} %shard_map.121), channel_id=1, source_target_pairs={{0,1},{1,0},{2,3},{3,2},{4,5},{5,4},{6,7},{7,6},{8,9},{9,8},{10,11... | collective-permute-start | bytes 98312 | tf_op jit(solution)/shard_map/ppermute | solution.py:438
  315.8 3.1 collective-permute-start.28
  318.8 4.4 %collective-permute-start.29 = (f32[8,128]{1,0:T(8,128)S(1)}, f32[8,128]{1,0:T(8,128)S(1)}, u32[]{:S(2)}, u32[]{:S(2)}) collective-permute-start(f32[8,128]{1,0:T(8,128)S(1)} %add.168), channel_id=1, source_target_pairs={{0,4},{2,6},{4,0},{6,2},{1,5},{3,7},{5,1},{7,3},{8,12},{10,14},{12... | collective-permute-start | bytes 12296 | tf_op jit(solution)/shard_map/ppermute | solution.py:389
  325.7 3.4 collective-permute-start.31
  (23 other events, 109.2 us)
Sparse Core Ops, SparseCore 0:
  97.0 7.8 reduce-scatter.4
  107.3 25.4 reduce-scatter.8
  135.7 8.7 reduce-scatter.6
  147.3 43.0 all-reduce.2
  192.7 24.8 reduce-scatter.10
  220.6 41.4 all-reduce.4
  263.7 10.8 all-gather.2
  280.9 11.9 all-gather.4

commit v2 on v1

--- a/solution.py
+++ b/solution.py
@@ -13,6 +13,7 @@
 GROUP = 4
 VMEM = pl.BlockSpec(memory_space=pltpu.VMEM)
 SMEM = pl.BlockSpec(memory_space=pltpu.SMEM)
+ANY = pl.BlockSpec(memory_space=pl.ANY)
 
 
 def call(body, outs, specs, args, scratch=(), flops=0, transcendentals=0, limit=48):
@@ -58,7 +59,7 @@
     channels = first.shape[0]
     lane = lax.broadcasted_iota(jnp.int32, (channels, 128), 1)
     both = jnp.where(lane == 0, first, jnp.where(lane == 1, second, 0.0))
-    return jnp.transpose(both)[:8]
+    return jnp.transpose(both)[:2]
 
 
 def local_stats(planes, count):
@@ -75,8 +76,10 @@
     return as_rows(mean, group_sums(acc))
 
 
-def columns_of(rows):
-    return jnp.transpose(rows)
+def columns_of(*rows):
+    rows = list(rows) + [jnp.zeros_like(rows[0])] * (8 - len(rows))
+    cols = jnp.transpose(jnp.concatenate(rows, axis=0))
+    return [cols[:, i : i + 1] for i in range(8)]
 
 
 def sigmoid(value):
@@ -85,7 +88,7 @@
 
 def stats_kernel(planes_ref, par_ref, out_ref):
     rows, frames, _, cols = planes_ref.shape
-    scale = columns_of(par_ref[...])[:, 0:1]
+    scale = columns_of(par_ref[0:1])[0]
     planes = [
         functools.partial(lambda r, t: planes_ref[r, t].astype(F32) * scale, r, t)
         for r in range(rows)
@@ -94,47 +97,50 @@
     out_ref[...] = local_stats(planes, float(GROUP * rows * frames * cols))
 
 
-def source(own, other, top, bottom, other_first):
+def source(own, other, near, far, other_first):
     def at(row, frame):
-        if row == 0:
-            return top, (frame,)
-        if row == own.shape[0] + 1:
-            return bottom, (frame,)
-        if (frame < 2) == other_first:
-            return other, (row - 1, frame % 2)
-        return own, (row - 1, frame % 2)
+        is_other = (frame < 2) == other_first
+        if row == 0 or row == own.shape[0] + 1:
+            return (far if is_other else near), (0 if row == 0 else 1, frame % 2)
+        return (other if is_other else own), (row - 1, frame % 2)
 
     return at
 
 
-def edges_kernel(flag_ref, own, other, top, bottom, out_ref, *, other_first):
-    at = source(own, other, top, bottom, other_first)
+def edges_kernel(flag_ref, *refs):
+    planes, out_ref = refs[:-1], refs[-1]
     is_first = flag_ref[3] == 0
-    channels = own.shape[2]
+    channels = planes[0].shape[2]
     lane = lax.broadcasted_iota(jnp.int32, (channels, 128), 1)
     acc = jnp.zeros((channels, 128), F32)
-    for row in range(own.shape[0] + 2):
-        for frame in range(4):
-            ref, index = at(row, frame)
-            plane = ref[index]
-            last = pltpu.roll(plane[:, -128:].astype(F32), 1, axis=1)
-            edge = jnp.where(is_first, last, plane[:, :128].astype(F32))
-            number = 4 * row + frame
-            moved = pltpu.roll(edge, number, axis=1) if number else edge
-            acc = jnp.where(lane == number, moved, acc)
+    number = 0
+    for ref in planes:
+        for row in range(ref.shape[0]):
+            for frame in range(ref.shape[1]):
+                last = pltpu.roll(ref[row, frame, :, -128:].astype(F32), 1, axis=1)
+                edge = jnp.where(is_first, last, ref[row, frame, :, :128].astype(F32))
+                moved = pltpu.roll(edge, number, axis=1) if number else edge
+                acc = jnp.where(lane == number, moved, acc)
+                number += 1
     out_ref[...] = acc.astype(BF16)
 
 
-def fill_stack(stack, row, frame, plane, edge, on_left, on_right):
+def edge_lane(row, frame, rows, other_first):
+    is_other = int((frame < 2) == other_first)
+    if row == 0 or row == rows + 1:
+        return 1, 4 * is_other + 2 * int(row > 0) + frame % 2
+    return 0, 2 * rows * is_other + 2 * (row - 1) + frame % 2
+
+
+def fill_stack(stack, row, frame, plane, column, on_left, on_right):
     channels, cols = plane.shape
     lane = lax.broadcasted_iota(jnp.int32, (channels, cols), 1)
-    number = 4 * row + frame
-    column = edge[:, number : number + 1]
-    left = jnp.where(lane == 0, column * on_left, pltpu.roll(plane, 1, axis=1))
-    right = jnp.where(lane == cols - 1, column * on_right, pltpu.roll(plane, cols - 1, axis=1))
-    stack[row, frame, 0:channels] = left.astype(BF16)
-    stack[row, frame, channels : 2 * channels] = plane.astype(BF16)
-    stack[row, frame, 2 * channels : 3 * channels] = right.astype(BF16)
+    column = column.astype(F32)
+    left = jnp.where(lane == 0, (column * on_left).astype(BF16), pltpu.roll(plane, 1, axis=1))
+    right = jnp.where(lane == cols - 1, (column * on_right).astype(BF16), pltpu.roll(plane, cols - 1, axis=1))
+    stack[row, frame, 0:channels] = left
+    stack[row, frame, channels : 2 * channels] = plane
+    stack[row, frame, 2 * channels : 3 * channels] = right
 
 
 def sides(flag_ref):
@@ -155,16 +161,15 @@
     inverse = 1.0 / jnp.sqrt(stats[1:2] / count + epsilon)
     gain = par[gain_row : gain_row + 1]
     shift = par[gain_row + 1 : gain_row + 2]
-    rows = jnp.concatenate([mean, inverse, gain, shift, par[0:1], stats[2:5]], axis=0)
-    cols = columns_of(rows)
-    return [cols[:, i : i + 1] for i in range(5)]
+    return columns_of(mean, inverse, gain, shift, par[0:1])[:5]
 
 
 def conv_first_kernel(
-    flag_ref, own, past, top, bottom, edge_ref, par_ref, st_ref, weight, hidden_ref, st_out, stack_ref, *, count
+    flag_ref, own, past, near, far, edge_ref, rim_ref, par_ref, st_ref, weight, after, hidden_ref, st_out, stack_ref,
+    *, count
 ):
     rows, frames, channels, cols = own.shape
-    at = source(own, past, top, bottom, True)
+    at = source(own, past, near, far, True)
     mean, inverse, gain, shift, scale = norm_columns(par_ref, st_ref, count, 1)
 
     def act(latent):
@@ -175,15 +180,13 @@
     has_top = flag_ref[1].astype(F32)
     has_bottom = flag_ref[2].astype(F32)
     on_left, on_right = sides(flag_ref)
-    lane = lax.broadcasted_iota(jnp.int32, (channels, 128), 1)
-    edge = act(edge_ref[...])
-    edge = edge * jnp.where((lane & 3) < 2, has_past, 1.0)
-    edge = edge * jnp.where(lane < 4, has_top, 1.0)
-    edge = edge * jnp.where(lane >= 4 * (rows + 1), has_bottom, 1.0)
+    edges = (act(edge_ref[...]), act(rim_ref[...]))
     for row in range(rows + 2):
         for frame in range(4):
             ref, index = at(row, frame)
+            which, number = edge_lane(row, frame, rows, True)
             plane = act(ref[index])
+            column = edges[which][:, number : number + 1]
             factor = None
             if frame < 2:
                 factor = has_past
@@ -192,7 +195,8 @@
                 factor = beside if factor is None else factor * beside
             if factor is not None:
                 plane = plane * factor
-            fill_stack(stack_ref, row, frame, plane, edge, on_left, on_right)
+                column = column * factor
+            fill_stack(stack_ref, row, frame, plane.astype(BF16), column, on_left, on_right)
     for row in range(rows):
         out = conv_rows(stack_ref, weight, row)
         for frame in range(frames):
@@ -203,15 +207,21 @@
     st_out[...] = local_stats(planes, float(GROUP * rows * frames * cols))
 
 
-def conv_back_kernel(flag_ref, own, future, top, bottom, edge_ref, weight, grad_ref, stack_ref):
-    rows, frames, channels, cols = own.shape
-    at = source(own, future, top, bottom, False)
+def fill_future(stack, flag_ref, own, future, near, far, edge_ref, rim_ref):
+    rows = own.shape[0]
+    at = source(own, future, near, far, False)
     on_left, on_right = sides(flag_ref)
-    edge = edge_ref[...].astype(F32)
+    edges = (edge_ref[...], rim_ref[...])
     for row in range(rows + 2):
         for frame in range(4):
             ref, index = at(row, frame)
-            fill_stack(stack_ref, row, frame, ref[index].astype(F32), edge, on_left, on_right)
+            which, number = edge_lane(row, frame, rows, False)
+            fill_stack(stack, row, frame, ref[index], edges[which][:, number : number + 1], on_left, on_right)
+
+
+def conv_back_kernel(flag_ref, own, future, near, far, edge_ref, rim_ref, weight, grad_ref, stack_ref):
+    rows, frames, channels, cols = own.shape
+    fill_future(stack_ref, flag_ref, own, future, near, far, edge_ref, rim_ref)
     for row in range(rows):
         out = conv_rows(stack_ref, weight, row)
         for frame in range(frames):
@@ -240,15 +250,46 @@
 def hidden_grad_kernel(hidden, scaled, par_ref, st_ref, sums_ref, out_ref, *, count):
     rows, frames, channels, cols = hidden.shape
     mean, inverse, _, _, _ = norm_columns(par_ref, st_ref, count, 3)
-    means = columns_of(sums_ref[...] / count)
-    first, second = means[:, 0:1], means[:, 1:2]
+    means = sums_ref[...] / count
+    first, second = columns_of(means[0:1], means[1:2])[:2]
     for row in range(rows):
         for frame in range(frames):
             normed = (hidden[row, frame] - mean) * inverse
             out_ref[row, frame] = (inverse * (scaled[row, frame] - first - normed * second)).astype(BF16)
 
 
-def weight_second_kernel(stack_ref, act_ref, out_ref, right_ref):
+def put_halves(flag_ref, mine_ref, theirs_ref, tap, block):
+    channels = block.shape[0]
+    here = slice(tap * channels, (tap + 1) * channels)
+    upper, lower = block[: channels // 2], block[channels // 2 :]
+    is_first = flag_ref[3] == 0
+    mine_ref[:, here] = jnp.where(is_first, upper, lower)
+    theirs_ref[:, here] = jnp.where(is_first, lower, upper)
+
+
+def add_kernel(mine_ref, other_ref, after, *outs):
+    start = 0
+    for out in outs:
+        end = start + out.shape[0]
+        out[...] = mine_ref[start:end] + other_ref[start:end]
+        start = end
+
+
+def join_kernel(flag_ref, *refs):
+    out_ref = refs[-1]
+    pieces = len(refs[:-1]) // 2
+    mine, theirs = refs[:pieces], refs[pieces : 2 * pieces]
+    is_first = flag_ref[3] == 0
+    half = out_ref.shape[0] // 2
+    start = 0
+    for a, b in zip(mine, theirs):
+        end = start + a.shape[0]
+        out_ref[start:end] = jnp.where(is_first, a[...], b[...])
+        out_ref[half + start : half + end] = jnp.where(is_first, b[...], a[...])
+        start = end
+
+
+def weight_second_kernel(flag_ref, stack_ref, act_ref, mine_ref, theirs_ref, right_ref):
     rows, frames, channels, cols = act_ref.shape
     for row in range(rows):
         right_ref[row * cols : (row + 1) * cols] = jnp.transpose(
@@ -264,12 +305,10 @@
             term = parts[2 - kt][:, :channels] + parts[3 - kt][:, channels:]
             for across in range(3):
                 tap = 9 * kt + 3 * (2 - down) + (2 - across)
-                out_ref[:, tap * channels : (tap + 1) * channels] = term[
-                    across * channels : (across + 1) * channels
-                ]
-
-
-def weight_first_kernel(stack_ref, grad_ref, out_ref, right_ref):
+                put_halves(flag_ref, mine_ref, theirs_ref, tap, term[across * channels : (across + 1) * channels])
+
+
+def weight_first_kernel(flag_ref, stack_ref, grad_ref, mine_ref, theirs_ref, right_ref):
     rows, frames, channels, cols = grad_ref.shape
     for row in range(rows):
         right_ref[row * cols : (row + 1) * cols] = jnp.transpose(
@@ -285,24 +324,17 @@
             term = parts[kt][:, :channels] + parts[kt + 1][:, channels:]
             for across in range(3):
                 tap = 9 * kt + 3 * down + across
-                out_ref[:, tap * channels : (tap + 1) * channels] = jnp.transpose(
-                    term[across * channels : (across + 1) * channels]
-                )
+                block = jnp.transpose(term[across * channels : (across + 1) * channels])
+                put_halves(flag_ref, mine_ref, theirs_ref, tap, block)
 
 
 def first_grad_kernel(
-    flag_ref, own, future, top, bottom, edge_ref, weight, latent, par_ref, st_ref, scaled_ref, sums_ref, stack_ref,
-    *, count
+    flag_ref, own, future, near, far, edge_ref, rim_ref, weight, latent, par_ref, st_ref, scaled_ref, sums_ref,
+    stack_ref, *, count
 ):
     rows, frames, channels, cols = own.shape
-    at = source(own, future, top, bottom, False)
-    on_left, on_right = sides(flag_ref)
-    edge = edge_ref[...].astype(F32)
     mean, inverse, gain, shift, scale = norm_columns(par_ref, st_ref, count, 1)
-    for row in range(rows + 2):
-        for frame in range(4):
-            ref, index = at(row, frame)
-            fill_stack(stack_ref, row, frame, ref[index].astype(F32), edge, on_left, on_right)
+    fill_future(stack_ref, flag_ref, own, future, near, far, edge_ref, rim_ref)
     first = jnp.zeros((channels, 128), F32)
     second = jnp.zeros((channels, 128), F32)
     for row in range(rows):
@@ -322,8 +354,8 @@
 def decoded_grad_kernel(scaled, latent, cotangent, par_ref, st_ref, sums_ref, out_ref, *, count):
     rows, frames, channels, cols = latent.shape
     mean, inverse, _, _, scale = norm_columns(par_ref, st_ref, count, 1)
-    means = columns_of(sums_ref[...] / count)
-    first, second = means[:, 0:1], means[:, 1:2]
+    means = sums_ref[...] / count
+    first, second = columns_of(means[0:1], means[1:2])[:2]
     for row in range(rows):
         for frame in range(frames):
             normed = (latent[row, frame].astype(F32) * scale - mean) * inverse
@@ -376,67 +408,83 @@
     return lax.ppermute(value, axis, [(source, source + steps) for source in range(initial, last)])
 
 
-def rounds():
+def rounds(radix=2):
     for axis in ("width", "height", "tm"):
+        count = lax.axis_size(axis)
         step = 1
-        while step < lax.axis_size(axis):
-            yield axis, [(i, i ^ step) for i in range(lax.axis_size(axis))]
-            step *= 2
-
-
-def all_sum(value):
-    for axis, pairs in rounds():
-        value = value + lax.ppermute(value, axis, pairs)
+        while step < count:
+            wide = radix if step * radix <= count else 2
+            yield axis, [[(i, i ^ (step * k)) for i in range(count)] for k in range(1, wide)]
+            step *= wide
+
+
+def all_sum(value, radix=2):
+    for axis, exchanges in rounds(radix):
+        parts = [value] + [lax.ppermute(value, axis, pairs) for pairs in exchanges]
+        while len(parts) > 1:
+            parts = [a + b for a, b in zip(parts[::2], parts[1::2])]
+        (value,) = parts
     return value
 
 
-def all_stats(value, count):
-    for axis, pairs in rounds():
-        other = lax.ppermute(value, axis, pairs)
-        gap = value[0:1] - other[0:1]
-        value = jnp.concatenate(
-            [
-                0.5 * (value[0:1] + other[0:1]),
-                value[1:2] + other[1:2] + gap * gap * (0.5 * count),
-                jnp.zeros_like(value[2:]),
-            ],
-            axis=0,
-        )
-        count = 2.0 * count
+def gathered_sum(value):
+    return jnp.sum(lax.all_gather(value, ("tm", "height", "width")), axis=0)
+
+
+def all_stats(value, count, radix=2):
+    for axis, exchanges in rounds(radix):
+        parts = [value] + [lax.ppermute(value, axis, pairs) for pairs in exchanges]
+        while len(parts) > 1:
+            joined = []
+            for a, b in zip(parts[::2], parts[1::2]):
+                gap = a[0:1] - b[0:1]
+                mean = 0.5 * (a[0:1] + b[0:1])
+                joined.append(jnp.concatenate([mean, a[1:2] + b[1:2] + gap * gap * (0.5 * count)], axis=0))
+            parts = joined
+            count = 2.0 * count
+        (value,) = parts
     return value
 
 
-def reduce_weights(term, after):
-    stages = (
-        lambda v: lax.psum_scatter(v, "width", scatter_dimension=0, tiled=True),
-        lambda v: lax.psum_scatter(v, "tm", scatter_dimension=0, tiled=True),
-        lambda v: lax.psum(v, "height"),
-        lambda v: lax.all_gather(v, "tm", axis=0, tiled=True),
-        lambda v: lax.all_gather(v, "width", axis=0, tiled=True),
-    )
-    results = []
-    for number, stage in enumerate(stages):
-        if after:
-            term, _ = lax.optimization_barrier((term, after[number]))
-        term = stage(term)
-        results.append(term)
-    return term, results
+def swapped(value):
+    return lax.ppermute(value, "width", [(0, 1), (1, 0)])
+
+
+def reduce_weights(flags, mine, theirs, pieces, axes, after_first, after_sum):
+    other = swapped(theirs)
+    half, cols = mine.shape
+    parts = call(
+        add_kernel,
+        [shape((half // pieces, cols), F32)] * pieces,
+        [VMEM, VMEM, ANY],
+        (mine, other, after_first),
+    )
+    parts = lax.psum(tuple(parts), axes)
+    parts, _ = lax.optimization_barrier((parts, after_sum))
+    others = [swapped(part) for part in parts]
+    (total,) = call(
+        join_kernel, [shape((2 * half, cols), F32)], [SMEM] + [VMEM] * (2 * pieces), (flags, *parts, *others)
+    )
+    return total
+
+
+def row_exchange(block):
+    return jnp.stack([shifted(block[-1], "height", 1), shifted(block[0], "height", -1)])
+
+
+def edges(flags, first, second):
+    channels = first.shape[2]
+    (columns,) = call(edges_kernel, [shape((channels, 128), BF16)], [SMEM, VMEM, VMEM], (flags, first, second))
+    return columns
 
 
 def extended(flags, own, steps):
     other = shifted(own, "tm", steps)
-    pair = (other, own) if steps > 0 else (own, other)
-    top = shifted(jnp.concatenate([part[-1] for part in pair], axis=0), "height", 1)
-    bottom = shifted(jnp.concatenate([part[0] for part in pair], axis=0), "height", -1)
-    channels = own.shape[2]
-    (edge,) = call(
-        functools.partial(edges_kernel, other_first=steps > 0),
-        [shape((channels, 128), BF16)],
-        [SMEM] + [VMEM] * 4,
-        (flags, own, other, top, bottom),
-    )
-    edge = lax.ppermute(edge, "width", [(0, 1), (1, 0)])
-    return other, top, bottom, edge
+    near = row_exchange(own)
+    far = row_exchange(other)
+    edge = swapped(edges(flags, own, other))
+    rim = edges(flags, near, far)
+    return (other, near, far, edge, swapped(rim)), rim
 
 
 def shards(
@@ -472,12 +520,13 @@
     block = (rows, frames, channels, cols)
     stack = (rows + 2, 4, 3 * channels, cols)
     taps = (2 * channels, 36 * channels)
+    halves = [shape((channels // 2, 27 * channels), F32)] * 2
     conv_flops = 2 * 4 * 256 * 36 * channels * 2 * channels
-    small = shape((8, channels), F32)
+    small = shape((2, channels), F32)
 
     (stats_first,) = call(stats_kernel, [small], [VMEM] * 2, (latent, par))
-    past, top, bottom, edge = extended(flags, latent, 1)
-    future_c, top_c, bottom_c, edge_c = extended(flags, cotangent, -1)
+    around, _ = extended(flags, latent, 1)
+    around_c, ready_c = extended(flags, cotangent, -1)
     stats_first = all_stats(stats_first, float(here))
     (weight_first,) = call(weight_forward_kernel, [shape(taps, BF16)], [VMEM], (conv_first,))
     (weight_second_t,) = call(weight_back_kernel, [shape(taps, BF16)], [VMEM], (conv_second,))
@@ -486,17 +535,17 @@
     hidden, stats_second, stack_first = call(
         functools.partial(conv_first_kernel, count=count),
         [shape(block, F32), small, shape(stack, BF16)],
-        [SMEM] + [VMEM] * 8,
-        (flags, latent, past, top, bottom, edge, par, stats_first, weight_first),
+        [SMEM] + [VMEM] * 9 + [ANY],
+        (flags, latent, *around, par, stats_first, weight_first, ready_c),
         flops=conv_flops,
         transcendentals=3 * latent.size,
     )
-    stats_second = all_stats(stats_second, float(here))
+    stats_second = all_stats(stats_second, float(here), 4)
     grad_second, stack_c = call(
         conv_back_kernel,
         [shape(block, F32), shape(stack, BF16)],
-        [SMEM] + [VMEM] * 6,
-        (flags, cotangent, future_c, top_c, bottom_c, edge_c, weight_second_t),
+        [SMEM] + [VMEM] * 7,
+        (flags, cotangent, *around_c, weight_second_t),
         flops=conv_flops,
     )
     act_second, scaled, sums = call(
@@ -506,47 +555,47 @@
         (hidden, grad_second, par, stats_second),
         transcendentals=latent.size,
     )
-    sums = all_sum(sums)
-    (conv_second_grad,) = call(
+    sums = gathered_sum(sums)
+    halves_second = call(
         weight_second_kernel,
-        [shape((channels, 27 * channels), F32)],
-        [VMEM] * 2,
-        (stack_c, act_second),
+        halves,
+        [SMEM] + [VMEM] * 2,
+        (flags, stack_c, act_second),
         scratch=[pltpu.VMEM((rows * cols, frames * channels), BF16)],
         flops=conv_flops,
     )
-    conv_second_grad, stages = reduce_weights(conv_second_grad, None)
     (hidden_grad,) = call(
         functools.partial(hidden_grad_kernel, count=count),
         [shape(block, BF16)],
         [VMEM] * 5,
         (hidden, scaled, par, stats_second, sums),
     )
-    future, top, bottom, edge = extended(flags, hidden_grad, -1)
-    (conv_first_grad,) = call(
+    around, _ = extended(flags, hidden_grad, -1)
+    halves_first = call(
         weight_first_kernel,
-        [shape((channels, 27 * channels), F32)],
-        [VMEM] * 2,
-        (stack_first, hidden_grad),
+        halves,
+        [SMEM] + [VMEM] * 2,
+        (flags, stack_first, hidden_grad),
         scratch=[pltpu.VMEM((rows * cols, frames * channels), BF16)],
         flops=conv_flops,
     )
-    conv_first_grad, _ = reduce_weights(conv_first_grad, stages)
-    scaled, sums = call(
+    scaled, sums_first = call(
         functools.partial(first_grad_kernel, count=count),
         [shape(block, F32), small],
-        [SMEM] + [VMEM] * 9,
-        (flags, hidden_grad, future, top, bottom, edge, weight_first_t, latent, par, stats_first),
+        [SMEM] + [VMEM] * 10,
+        (flags, hidden_grad, *around, weight_first_t, latent, par, stats_first),
         scratch=[pltpu.VMEM(stack, BF16)],
         flops=conv_flops,
         transcendentals=latent.size,
     )
-    sums = all_sum(sums)
+    sums_first = all_sum(sums_first)
+    conv_second_grad = reduce_weights(flags, *halves_second, 2, ("height", "tm"), sums, sums_first)
+    conv_first_grad = reduce_weights(flags, *halves_first, 4, ("tm", "height"), hidden_grad, sums_first)
     (decoded_grad,) = call(
         functools.partial(decoded_grad_kernel, count=count),
         [shape(block, F32)],
         [VMEM] * 6,
-        (scaled, latent, cotangent, par, stats_first, sums),
+        (scaled, latent, cotangent, par, stats_first, sums_first),
     )
     return decoded_grad.transpose(2, 1, 0, 3), conv_first_grad, conv_second_grad
 

time: 347 us -> 399 us (1.15)
  waiting for transfers between devices: 177 us -> 216 us
  Pallas kernels: 36.6 us -> 43.8 us
  blocking collectives: 36.4 us -> 41.1 us
  starting transfers between devices: 61.9 us -> 66.6 us
    psum x2, waiting for transfers between devices: 72 us -> 173 us  [reduce_weights(): parts = lax.psum(tuple(parts), axes)]
    reduce_scatter x4 -> x0, waiting for transfers between devices: 54.2 us -> none  [the longest x2 34.6 us: reduce_weights(): lax.psum_scatter(v, 'tm', scatter_dimension=0, tiled=True)]
    ppermute x9 -> x15, starting transfers between devices: 20 us -> 31.9 us  [shifted(): lax.ppermute(value, axis, [(source, source + steps) for source in range(i...]
    ppermute x9 -> x15, waiting for transfers between devices: 25.8 us -> 17.6 us  [shifted(): lax.ppermute(value, axis, [(source, source + steps) for source in range(i...]
    pallas_call x15 -> x22, Pallas kernels: 36.6 us -> 43.8 us  [call(): pl.pallas_call(body, out_shape=tuple(outs), in_specs=specs, out_specs=tup...]
    ppermute x23 -> x31, starting transfers between devices: 41.5 us -> 34.6 us  [the longest x12 19.3 us: all_stats(): parts = [value] + [lax.ppermute(value, axis, pairs) for pairs in exchanges]]
    all_gather x2 -> x1, blocking collectives: 36.4 us -> 41.1 us  [gathered_sum(): return jnp.sum(lax.all_gather(value, ('tm', 'height', 'width')), axis=0)]
    ppermute x23 -> x31, waiting for transfers between devices: 24.3 us -> 25.6 us  [the longest x12 13 us: all_stats(): parts = [value] + [lax.ppermute(value, axis, pairs) for pairs in exchanges]]
  transfers between devices with their start and end apart: 40 -> 48, of which waited for: 29 -> 15; matrix products, arithmetic and copies ran while one was open for 1% -> 1% of each run, Pallas kernels for 9% -> 7%
where the time goes in v2:
time: 399 us; the launch traced here: 398 us
  waiting for transfers between devices  216 us (54%)
  starting transfers between devices  66.6 us (17%)
  Pallas kernels  43.8 us (11%)
  blocking collectives  41.1 us (10%)
  between operations  14.7 us (4%)
  local copies, waits for them, and re-layouts  13.7 us (3%)
    psum x2, waiting for transfers between devices, reduce_weights(): parts = lax.psum(tuple(parts), axes)  173 us
    pallas_call x22, Pallas kernels, call(): pl.pallas_call(body, out_shape=tuple(outs), in_specs=specs, out_specs=tup...  43.8 us
    all_gather x1, blocking collectives, gathered_sum(): return jnp.sum(lax.all_gather(value, ('tm', 'height', 'width')), axis=0)  41.1 us
    ppermute x15, starting transfers between devices, shifted(): lax.ppermute(value, axis, [(source, source + steps) for source in range(i...  31.9 us
    ppermute x12, starting transfers between devices, all_stats(): parts = [value] + [lax.ppermute(value, axis, pairs) for pairs in exchanges]  19.3 us
    ppermute x15, waiting for transfers between devices, shifted(): lax.ppermute(value, axis, [(source, source + steps) for source in range(i...  17.6 us
    ppermute x14, starting transfers between devices, swapped(): return lax.ppermute(value, 'width', [(0, 1), (1, 0)])  14.3 us
    ppermute x12, waiting for transfers between devices, all_stats(): parts = [value] + [lax.ppermute(value, axis, pairs) for pairs in exchanges]  13 us
  transfers between devices with their start and end apart: 48, of which 15 were waited for; matrix products, arithmetic and copies ran while one was open for 1% of the time, Pallas kernels for 7%

profile of v2, /device:TPU:1, one launch (start us, length us, event | category | flops | bytes accessed | tf_op | source)
XLA Modules:
  0.0 397.9 jit_solution(3101576075000698824)
XLA Ops:
  11.8 2.5 collective-permute-start.8
  14.3 3.2 collective-permute-start
  19.5 2.2 collective-permute-start.1
  24.4 2.1 collective-permute-start.10
  26.6 10.4 %collective-permute-done.10 = f32[2,128]{1,0:T(2,128)S(1)} collective-permute-done((f32[2,128]{1,0:T(2,128)S(1)}, f32[2,128]{1,0:T(2,128)S(1)}, u32[]{:S(2)}, u32[]{:S(2)}) %collective-permute-start.10) | collective-permute-done | bytes 1056 | tf_op jit(solution)/shard_map/ppermute | solution.py:436
  37.0 2.3 collective-permute-start.11
  40.4 3.7 collective-permute-start.12
  46.4 4.6 %collective-permute-start.3 = (bf16[2,128,256]{2,1,0:T(8,128)(2,1)S(1)}, bf16[2,128,256]{2,1,0:T(8,128)(2,1)S(1)}, u32[]{:S(2)}, u32[]{:S(2)}) collective-permute-start(bf16[2,128,256]{2,1,0:T(8,128)(2,1)S(1)} %get-tuple-element.78), channel_id=1, source_target_pairs={{0,2},{2,4},{4,6},{1,3},{3,5},{5,7},{8,10},{10,12},{12,14},{9,11},... | collective-permute-start | bytes 393224 | tf_op jit(solution)/shard_map/ppermute | solution.py:408
  52.4 4.9 %collective-permute-start.15 = (bf16[2,128,256]{2,1,0:T(8,128)(2,1)S(1)}, bf16[2,128,256]{2,1,0:T(8,128)(2,1)S(1)}, u32[]{:S(2)}, u32[]{:S(2)}) collective-permute-start(bf16[2,128,256]{2,1,0:T(8,128)(2,1)S(1)} %get-tuple-element.74), channel_id=1, source_target_pairs={{0,2},{2,4},{4,6},{1,3},{3,5},{5,7},{8,10},{10,12},{12,14},{9,11},... | collective-permute-start | bytes 393224 | tf_op jit(solution)/shard_map/ppermute | solution.py:408
  60.3 5.0 %collective-permute-start.5 = (bf16[128,128]{1,0:T(8,128)(2,1)S(1)}, bf16[128,128]{1,0:T(8,128)(2,1)S(1)}, u32[]{:S(2)}, u32[]{:S(2)}) collective-permute-start(bf16[128,128]{1,0:T(8,128)(2,1)S(1)} %shard_map.112), channel_id=1, source_target_pairs={{0,1},{1,0},{2,3},{3,2},{4,5},{5,4},{6,7},{7,6},{8,9},{9,8},{10,11... | collective-permute-start | bytes 98312 | tf_op jit(solution)/shard_map/ppermute | solution.py:450
  68.6 6.6 %shard_map.117 = (f32[4,2,128,256]{3,2,1,0:T(8,128)S(1)}, f32[2,128]{1,0:T(2,128)S(1)}, bf16[6,4,384,256]{3,2,1,0:T(8,128)(2,1)}) custom-call(s32[4]{0:T(128)S(1)} %pad_add_fusion.flag_ref, bf16[4,2,128,256]{3,2,1,0:T(8,128)(2,1)S(1)} %bitcast.56, bf16[4,2,128,256]{3,2,1,0:T(8,128)(2,1)S(1)} %copy-done.2, ...), custom_call_target="tpu_custom_call" | custom-call | flops 2415919104 | bytes 9803792 | tf_op jit(solution)/shard_map/pallas_call | solution.py:22
  75.2 3.4 collective-permute-start.19
  79.4 2.7 collective-permute-start.20
  86.4 2.4 collective-permute-start.24
  89.9 5.3 %shard_map.120 = (f32[4,2,128,256]{3,2,1,0:T(8,128)S(1)}, bf16[6,4,384,256]{3,2,1,0:T(8,128)(2,1)}) custom-call(s32[4]{0:T(128)S(1)} %pad_add_fusion.flag_ref, bf16[4,2,128,256]{3,2,1,0:T(8,128)(2,1)S(1)} %bitcast.62, bf16[4,2,128,256]{3,2,1,0:T(8,128)(2,1)S(1)} %collective-permute-done.14.refs_1_.future, ...), custom_call_target="tpu_custom_call" | custom-call | flops 2415919104 | bytes 9764880 | tf_op jit(solution)/shard_map/pallas_call | solution.py:22
  98.0 41.1 %all-gather.1 = f32[32,2,128]{2,1,0:T(2,128)S(1)} all-gather(f32[1,2,128]{2,1,0:T(2,128)S(1)} %bitcast.65), channel_id=2, replica_groups=mesh['tm'=4,'height'=4,'width'=2] {'tm','height','width'}, dimensions={0}, use_global_device_ids=true | all-gather | bytes 33792 | tf_op jit(solution)/shard_map/all_gather | solution.py:431
  140.9 5.2 %shard_map.128 = (f32[64,3456]{1,0:T(8,128)S(1)}, f32[64,3456]{1,0:T(8,128)S(1)}) custom-call(s32[4]{0:T(128)S(1)} %pad_add_fusion.flag_ref, bf16[6,4,384,256]{3,2,1,0:T(8,128)(2,1)} %get-tuple-element.36.stack_ref, bf16[4,2,128,256]{3,2,1,0:T(8,128)(2,1)S(1)} %shard_map.122.refs_0_.own.grad_ref.after), custom_call_target="tpu_custom_call" | custom-call | flops 2415919104 | bytes 7012368 | tf_op jit(solution)/shard_map/pallas_call | solution.py:22
  146.4 5.9 %shard_map.131 = (f32[64,3456]{1,0:T(8,128)S(1)}, f32[64,3456]{1,0:T(8,128)}) custom-call(s32[4]{0:T(128)S(1)} %pad_add_fusion.flag_ref, bf16[6,4,384,256]{3,2,1,0:T(8,128)(2,1)} %get-tuple-element.47.stack_ref, bf16[4,2,128,256]{3,2,1,0:T(8,128)(2,1)S(1)} %copy-done.19), custom_call_target="tpu_custom_call" | custom-call | flops 2415919104 | bytes 7012368 | tf_op jit(solution)/shard_map/pallas_call | solution.py:22
  159.0 2.1 shard_map.132
  163.7 14.9 %collective-permute-done.26.refs_1_.future = bf16[4,2,128,256]{3,2,1,0:T(8,128)(2,1)S(1)} collective-permute-done((bf16[4,2,128,256]{3,2,1,0:T(8,128)(2,1)S(1)}, bf16[4,2,128,256]{3,2,1,0:T(8,128)(2,1)S(1)}, u32[]{:S(2)}, u32[]{:S(2)}) %collective-permute-start.26) | collective-permute-done | bytes 524320 | tf_op jit(solution)/shard_map/ppermute | solution.py:408
  184.4 2.7 collective-permute-done.30
  190.3 4.1 %shard_map.126 = (f32[4,2,128,256]{3,2,1,0:T(8,128)S(1)}, f32[2,128]{1,0:T(2,128)S(1)}) custom-call(s32[4]{0:T(128)S(1)} %pad_add_fusion.flag_ref, bf16[4,2,128,256]{3,2,1,0:T(8,128)(2,1)S(1)} %shard_map.122.refs_0_.own.grad_ref.after, bf16[4,2,128,256]{3,2,1,0:T(8,128)(2,1)S(1)} %collective-permute-done.26.refs_1_.future, ...), custom_call_target="tpu_custom_call" | custom-call | flops 2415919104 | bytes 5576720 | tf_op jit(solution)/shard_map/pallas_call | solution.py:22
  196.2 1.8 collective-permute-done.34
  198.0 2.8 collective-permute-done.35
  200.8 2.8 collective-permute-done.36
  203.7 3.6 collective-permute-done.37
  207.3 58.8 %all-reduce.5.cloned.1.call-done = (f32[16,3456]{1,0:T(8,128)}, f32[16,3456]{1,0:T(8,128)}, f32[16,3456]{1,0:T(8,128)}, f32[16,3456]{1,0:T(8,128)}) async-done(((f32[16,3456]{1,0:T(8,128)}, f32[16,3456]{1,0:T(8,128)}, f32[16,3456]{1,0:T(8,128)}, f32[16,3456]{1,0:T(8,128)}), (f32[16,3456]{1,0:T(8,128)}, f32[16,3456]{1,0:T(8,128)}, f32[16,3456]{1,0:T(8,128)}, ...) | async-done | bytes 884752 | tf_op jit(solution)/shard_map/psum | solution.py:462
  266.1 1.8 collective-permute-start.39
  267.9 113.9 %all-reduce.7.cloned.1.call-done = (f32[32,3456]{1,0:T(8,128)}, f32[32,3456]{1,0:T(8,128)}) async-done(((f32[32,3456]{1,0:T(8,128)}, f32[32,3456]{1,0:T(8,128)}), (f32[32,3456]{1,0:T(8,128)}, f32[32,3456]{1,0:T(8,128)})) %all-reduce.7.cloned.1.call-update) | async-done | bytes 884752 | tf_op jit(solution)/shard_map/psum | solution.py:462
  381.8 2.0 collective-permute-start.44
  387.2 1.9 shard_map.130
  389.1 2.0 shard_map.133
  (175 shorter events, 54.5 us)
Async XLA Ops:
  7.2 258.9 %all-reduce.5.cloned.1.call-start = ((), (), s32[]{:S(2)}) async-start(), calls=%async_computation | async-start | bytes 1769472 | tf_op jit(solution)/shard_map/psum | solution.py:462
  11.8 5.7 %collective-permute-start.8 = (f32[2,128]{1,0:T(2,128)S(1)}, f32[2,128]{1,0:T(2,128)S(1)}, u32[]{:S(2)}, u32[]{:S(2)}) collective-permute-start(f32[2,128]{1,0:T(2,128)S(1)} %pad_maximum_fusion.6), channel_id=1, source_target_pairs={{0,2},{2,0},{4,6},{6,4},{1,3},{3,1},{5,7},{7,5},{8,10},{10,8},{12,... | collective-permute-start | bytes 3080 | tf_op jit(solution)/shard_map/ppermute | solution.py:436
  14.3 32.1 %collective-permute-start = (bf16[4,2,128,256]{3,2,1,0:T(8,128)(2,1)S(1)}, bf16[4,2,128,256]{3,2,1,0:T(8,128)(2,1)S(1)}, u32[]{:S(2)}, u32[]{:S(2)}) collective-permute-start(bf16[4,2,128,256]{3,2,1,0:T(8,128)(2,1)S(1)} %bitcast.53), channel_id=1, source_target_pairs={{0,8},{8,16},{16,24},{1,9},{9,17},{17,25},{2,10},{10,18},{18,26},{... | collective-permute-start | bytes 1572872 | tf_op jit(solution)/shard_map/ppermute | solution.py:408
  17.5 6.9 %collective-permute-start.9 = (f32[2,128]{1,0:T(2,128)S(1)}, f32[2,128]{1,0:T(2,128)S(1)}, u32[]{:S(2)}, u32[]{:S(2)}) collective-permute-start(f32[2,128]{1,0:T(2,128)S(1)} %pad_maximum_fusion.7), channel_id=1, source_target_pairs={{0,4},{2,6},{4,0},{6,2},{1,5},{3,7},{5,1},{7,3},{8,12},{10,14},{12... | collective-permute-start | bytes 3080 | tf_op jit(solution)/shard_map/ppermute | solution.py:436
  19.5 24.6 %collective-permute-start.1 = (bf16[2,128,256]{2,1,0:T(8,128)(2,1)}, bf16[2,128,256]{2,1,0:T(8,128)(2,1)S(1)}, u32[]{:S(2)}, u32[]{:S(2)}) collective-permute-start(bf16[2,128,256]{2,1,0:T(8,128)(2,1)} %get-tuple-element.80), channel_id=1, source_target_pairs={{0,2},{2,4},{4,6},{1,3},{3,5},{5,7},{8,10},{10,12},{12,14},{9,11},... | collective-permute-start | bytes 393224 | tf_op jit(solution)/shard_map/ppermute | solution.py:408
  21.7 23.8 %collective-permute-start.2 = (bf16[2,128,256]{2,1,0:T(8,128)(2,1)S(1)}, bf16[2,128,256]{2,1,0:T(8,128)(2,1)}, u32[]{:S(2)}, u32[]{:S(2)}) collective-permute-start(bf16[2,128,256]{2,1,0:T(8,128)(2,1)S(1)} %get-tuple-element.81), channel_id=1, source_target_pairs={{2,0},{4,2},{6,4},{3,1},{5,3},{7,5},{10,8},{12,10},{14,12},{11,9},... | collective-permute-start | bytes 393224 | tf_op jit(solution)/shard_map/ppermute | solution.py:408
  23.1 29.2 %collective-permute-start.14 = (bf16[4,2,128,256]{3,2,1,0:T(8,128)(2,1)S(1)}, bf16[4,2,128,256]{3,2,1,0:T(8,128)(2,1)S(1)}, u32[]{:S(2)}, u32[]{:S(2)}) collective-permute-start(bf16[4,2,128,256]{3,2,1,0:T(8,128)(2,1)S(1)} %bitcast.59), channel_id=1, source_target_pairs={{8,0},{16,8},{24,16},{9,1},{17,9},{25,17},{10,2},{18,10},{26,18},{... | collective-permute-start | bytes 1572872 | tf_op jit(solution)/shard_map/ppermute | solution.py:408
  24.4 12.5 %collective-permute-start.10 = (f32[2,128]{1,0:T(2,128)S(1)}, f32[2,128]{1,0:T(2,128)S(1)}, u32[]{:S(2)}, u32[]{:S(2)}) collective-permute-start(f32[2,128]{1,0:T(2,128)S(1)} %pad_maximum_fusion.8), channel_id=1, source_target_pairs={{0,8},{8,0},{16,24},{24,16},{1,9},{9,1},{17,25},{25,17},{2,10},{10... | collective-permute-start | bytes 3080 | tf_op jit(solution)/shard_map/ppermute | solution.py:436
  40.4 16.9 %collective-permute-start.12 = (bf16[2,128,256]{2,1,0:T(8,128)(2,1)S(1)}, bf16[2,128,256]{2,1,0:T(8,128)(2,1)S(1)}, u32[]{:S(2)}, u32[]{:S(2)}) collective-permute-start(bf16[2,128,256]{2,1,0:T(8,128)(2,1)S(1)} %get-tuple-element.76), channel_id=1, source_target_pairs={{0,2},{2,4},{4,6},{1,3},{3,5},{5,7},{8,10},{10,12},{12,14},{9,11},... | collective-permute-start | bytes 393224 | tf_op jit(solution)/shard_map/ppermute | solution.py:408
  44.1 14.6 %collective-permute-start.13 = (bf16[2,128,256]{2,1,0:T(8,128)(2,1)S(1)}, bf16[2,128,256]{2,1,0:T(8,128)(2,1)S(1)}, u32[]{:S(2)}, u32[]{:S(2)}) collective-permute-start(bf16[2,128,256]{2,1,0:T(8,128)(2,1)S(1)} %get-tuple-element.77), channel_id=1, source_target_pairs={{2,0},{4,2},{6,4},{3,1},{5,3},{7,5},{10,8},{12,10},{14,12},{11,9},... | collective-permute-start | bytes 393224 | tf_op jit(solution)/shard_map/ppermute | solution.py:408
  46.4 18.9 %collective-permute-start.3 = (bf16[2,128,256]{2,1,0:T(8,128)(2,1)S(1)}, bf16[2,128,256]{2,1,0:T(8,128)(2,1)S(1)}, u32[]{:S(2)}, u32[]{:S(2)}) collective-permute-start(bf16[2,128,256]{2,1,0:T(8,128)(2,1)S(1)} %get-tuple-element.78), channel_id=1, source_target_pairs={{0,2},{2,4},{4,6},{1,3},{3,5},{5,7},{8,10},{10,12},{12,14},{9,11},... | collective-permute-start | bytes 393224 | tf_op jit(solution)/shard_map/ppermute | solution.py:408
  51.0 14.3 %collective-permute-start.4 = (bf16[2,128,256]{2,1,0:T(8,128)(2,1)S(1)}, bf16[2,128,256]{2,1,0:T(8,128)(2,1)S(1)}, u32[]{:S(2)}, u32[]{:S(2)}) collective-permute-start(bf16[2,128,256]{2,1,0:T(8,128)(2,1)S(1)} %get-tuple-element.79), channel_id=1, source_target_pairs={{2,0},{4,2},{6,4},{3,1},{5,3},{7,5},{10,8},{12,10},{14,12},{11,9},... | collective-permute-start | bytes 393224 | tf_op jit(solution)/shard_map/ppermute | solution.py:408
  52.4 14.0 %collective-permute-start.15 = (bf16[2,128,256]{2,1,0:T(8,128)(2,1)S(1)}, bf16[2,128,256]{2,1,0:T(8,128)(2,1)S(1)}, u32[]{:S(2)}, u32[]{:S(2)}) collective-permute-start(bf16[2,128,256]{2,1,0:T(8,128)(2,1)S(1)} %get-tuple-element.74), channel_id=1, source_target_pairs={{0,2},{2,4},{4,6},{1,3},{3,5},{5,7},{8,10},{10,12},{12,14},{9,11},... | collective-permute-start | bytes 393224 | tf_op jit(solution)/shard_map/ppermute | solution.py:408
  57.3 9.1 %collective-permute-start.16 = (bf16[2,128,256]{2,1,0:T(8,128)(2,1)S(1)}, bf16[2,128,256]{2,1,0:T(8,128)(2,1)S(1)}, u32[]{:S(2)}, u32[]{:S(2)}) collective-permute-start(bf16[2,128,256]{2,1,0:T(8,128)(2,1)S(1)} %get-tuple-element.75), channel_id=1, source_target_pairs={{2,0},{4,2},{6,4},{3,1},{5,3},{7,5},{10,8},{12,10},{14,12},{11,9},... | collective-permute-start | bytes 393224 | tf_op jit(solution)/shard_map/ppermute | solution.py:408
  60.3 7.0 %collective-permute-start.5 = (bf16[128,128]{1,0:T(8,128)(2,1)S(1)}, bf16[128,128]{1,0:T(8,128)(2,1)S(1)}, u32[]{:S(2)}, u32[]{:S(2)}) collective-permute-start(bf16[128,128]{1,0:T(8,128)(2,1)S(1)} %shard_map.112), channel_id=1, source_target_pairs={{0,1},{1,0},{2,3},{3,2},{4,5},{5,4},{6,7},{7,6},{8,9},{9,8},{10,11... | collective-permute-start | bytes 98312 | tf_op jit(solution)/shard_map/ppermute | solution.py:450
  79.4 6.9 %collective-permute-start.20 = (f32[2,128]{1,0:T(2,128)S(1)}, f32[2,128]{1,0:T(2,128)S(1)}, u32[]{:S(2)}, u32[]{:S(2)}) collective-permute-start(f32[2,128]{1,0:T(2,128)S(1)} %pad_maximum_fusion.11), channel_id=1, source_target_pairs={{0,2},{2,0},{4,6},{6,4},{1,3},{3,1},{5,7},{7,5},{8,10},{10,8},{12,... | collective-permute-start | bytes 3080 | tf_op jit(solution)/shard_map/ppermute | solution.py:436
  85.2 4.7 %collective-permute-start.17 = (bf16[128,128]{1,0:T(8,128)(2,1)S(1)}, bf16[128,128]{1,0:T(8,128)(2,1)S(1)}, u32[]{:S(2)}, u32[]{:S(2)}) collective-permute-start(bf16[128,128]{1,0:T(8,128)(2,1)S(1)} %shard_map.118), channel_id=1, source_target_pairs={{0,1},{1,0},{2,3},{3,2},{4,5},{5,4},{6,7},{7,6},{8,9},{9,8},{10,11... | collective-permute-start | bytes 98312 | tf_op jit(solution)/shard_map/ppermute | solution.py:450
  86.3 8.9 %collective-permute-start.23 = (f32[2,128]{1,0:T(2,128)S(1)}, f32[2,128]{1,0:T(2,128)S(1)}, u32[]{:S(2)}, u32[]{:S(2)}) collective-permute-start(f32[2,128]{1,0:T(2,128)S(1)} %pad_maximum_fusion.12), channel_id=1, source_target_pairs={{0,8},{8,0},{16,24},{24,16},{1,9},{9,1},{17,25},{25,17},{2,10},{10... | collective-permute-start | bytes 3080 | tf_op jit(solution)/shard_map/ppermute | solution.py:436
  86.4 8.9 %collective-permute-start.24 = (f32[2,128]{1,0:T(2,128)S(1)}, f32[2,128]{1,0:T(2,128)S(1)}, u32[]{:S(2)}, u32[]{:S(2)}) collective-permute-start(f32[2,128]{1,0:T(2,128)S(1)} %pad_maximum_fusion.12), channel_id=1, source_target_pairs={{0,16},{8,24},{16,0},{24,8},{1,17},{9,25},{17,1},{25,9},{2,18},{10... | collective-permute-start | bytes 3080 | tf_op jit(solution)/shard_map/ppermute | solution.py:436
  88.8 6.5 %collective-permute-start.25 = (f32[2,128]{1,0:T(2,128)S(1)}, f32[2,128]{1,0:T(2,128)S(1)}, u32[]{:S(2)}, u32[]{:S(2)}) collective-permute-start(f32[2,128]{1,0:T(2,128)S(1)} %pad_maximum_fusion.12), channel_id=1, source_target_pairs={{0,24},{8,16},{16,8},{24,0},{1,25},{9,17},{17,9},{25,1},{2,26},{10... | collective-permute-start | bytes 3080 | tf_op jit(solution)/shard_map/ppermute | solution.py:436
  146.1 7.4 %collective-permute-start.38 = (f32[64,3456]{1,0:T(8,128)S(1)}, f32[64,3456]{1,0:T(8,128)S(1)}, u32[]{:S(2)}, u32[]{:S(2)}) collective-permute-start(f32[64,3456]{1,0:T(8,128)S(1)} %get-tuple-element.38), channel_id=1, source_target_pairs={{0,1},{1,0},{2,3},{3,2},{4,5},{5,4},{6,7},{7,6},{8,9},{9,8},{10,11... | collective-permute-start | bytes 2654216 | tf_op jit(solution)/shard_map/ppermute | solution.py:450
  153.2 4.5 %collective-permute-start.43 = (f32[64,3456]{1,0:T(8,128)}, f32[64,3456]{1,0:T(8,128)}, u32[]{:S(2)}, u32[]{:S(2)}) collective-permute-start(f32[64,3456]{1,0:T(8,128)} %get-tuple-element.50), channel_id=1, source_target_pairs={{0,1},{1,0},{2,3},{3,2},{4,5},{5,4},{6,7},{7,6},{8,9},{9,8},{10,11... | collective-permute-start | bytes 2654216 | tf_op jit(solution)/shard_map/ppermute | solution.py:450
  156.4 225.5 %all-reduce.7.cloned.1.call-start = ((), (), s32[]{:S(2)}) async-start(), calls=%async_computation.1 | async-start | bytes 1769472 | tf_op jit(solution)/shard_map/psum | solution.py:462
  156.4 22.2 %collective-permute-start.26 = (bf16[4,2,128,256]{3,2,1,0:T(8,128)(2,1)S(1)}, bf16[4,2,128,256]{3,2,1,0:T(8,128)(2,1)S(1)}, u32[]{:S(2)}, u32[]{:S(2)}) collective-permute-start(bf16[4,2,128,256]{3,2,1,0:T(8,128)(2,1)S(1)} %shard_map.122.refs_0_.own.grad_ref.after), channel_id=1, source_target_pairs={{8,0},{16,8},{24,16},{9,1},{17,9},{25,17},{10,2},{18,10},{26,18},{... | collective-permute-start | bytes 1572872 | tf_op jit(solution)/shard_map/ppermute | solution.py:408
  161.1 20.4 %collective-permute-start.27 = (bf16[2,128,256]{2,1,0:T(8,128)(2,1)S(1)}, bf16[2,128,256]{2,1,0:T(8,128)(2,1)S(1)}, u32[]{:S(2)}, u32[]{:S(2)}) collective-permute-start(bf16[2,128,256]{2,1,0:T(8,128)(2,1)S(1)} %get-tuple-element.72), channel_id=1, source_target_pairs={{0,2},{2,4},{4,6},{1,3},{3,5},{5,7},{8,10},{10,12},{12,14},{9,11},... | collective-permute-start | bytes 393224 | tf_op jit(solution)/shard_map/ppermute | solution.py:408
  162.4 19.1 %collective-permute-start.28 = (bf16[2,128,256]{2,1,0:T(8,128)(2,1)S(1)}, bf16[2,128,256]{2,1,0:T(8,128)(2,1)S(1)}, u32[]{:S(2)}, u32[]{:S(2)}) collective-permute-start(bf16[2,128,256]{2,1,0:T(8,128)(2,1)S(1)} %get-tuple-element.73), channel_id=1, source_target_pairs={{2,0},{4,2},{6,4},{3,1},{5,3},{7,5},{10,8},{12,10},{14,12},{11,9},... | collective-permute-start | bytes 393224 | tf_op jit(solution)/shard_map/ppermute | solution.py:408
  178.7 5.7 %collective-permute-start.29 = (bf16[2,128,256]{2,1,0:T(8,128)(2,1)S(1)}, bf16[2,128,256]{2,1,0:T(8,128)(2,1)S(1)}, u32[]{:S(2)}, u32[]{:S(2)}) collective-permute-start(bf16[2,128,256]{2,1,0:T(8,128)(2,1)S(1)} %get-tuple-element.70), channel_id=1, source_target_pairs={{0,2},{2,4},{4,6},{1,3},{3,5},{5,7},{8,10},{10,12},{12,14},{9,11},... | collective-permute-start | bytes 393224 | tf_op jit(solution)/shard_map/ppermute | solution.py:408
  180.0 7.1 %collective-permute-start.30 = (bf16[2,128,256]{2,1,0:T(8,128)(2,1)S(1)}, bf16[2,128,256]{2,1,0:T(8,128)(2,1)S(1)}, u32[]{:S(2)}, u32[]{:S(2)}) collective-permute-start(bf16[2,128,256]{2,1,0:T(8,128)(2,1)S(1)} %get-tuple-element.71), channel_id=1, source_target_pairs={{2,0},{4,2},{6,4},{3,1},{5,3},{7,5},{10,8},{12,10},{14,12},{11,9},... | collective-permute-start | bytes 393224 | tf_op jit(solution)/shard_map/ppermute | solution.py:408
  183.1 6.7 %collective-permute-start.31 = (bf16[128,128]{1,0:T(8,128)(2,1)S(1)}, bf16[128,128]{1,0:T(8,128)(2,1)S(1)}, u32[]{:S(2)}, u32[]{:S(2)}) collective-permute-start(bf16[128,128]{1,0:T(8,128)(2,1)S(1)} %shard_map.123), channel_id=1, source_target_pairs={{0,1},{1,0},{2,3},{3,2},{4,5},{5,4},{6,7},{7,6},{8,9},{9,8},{10,11... | collective-permute-start | bytes 98312 | tf_op jit(solution)/shard_map/ppermute | solution.py:450
  266.1 118.3 %collective-permute-start.39 = (f32[16,3456]{1,0:T(8,128)}, f32[16,3456]{1,0:T(8,128)S(1)}, u32[]{:S(2)}, u32[]{:S(2)}) collective-permute-start(f32[16,3456]{1,0:T(8,128)} %get-tuple-element.43.refs_0_), channel_id=1, source_target_pairs={{0,1},{1,0},{2,3},{3,2},{4,5},{5,4},{6,7},{7,6},{8,9},{9,8},{10,11... | collective-permute-start | bytes 663560 | tf_op jit(solution)/shard_map/ppermute | solution.py:450
  381.8 7.2 %collective-permute-start.44 = (f32[32,3456]{1,0:T(8,128)}, f32[32,3456]{1,0:T(8,128)S(1)}, u32[]{:S(2)}, u32[]{:S(2)}) collective-permute-start(f32[32,3456]{1,0:T(8,128)} %get-tuple-element.53.refs_0_), channel_id=1, source_target_pairs={{0,1},{1,0},{2,3},{3,2},{4,5},{5,4},{6,7},{7,6},{8,9},{9,8},{10,11... | collective-permute-start | bytes 1327112 | tf_op jit(solution)/shard_map/ppermute | solution.py:450
  383.9 5.2 %collective-permute-start.45 = (f32[32,3456]{1,0:T(8,128)}, f32[32,3456]{1,0:T(8,128)S(1)}, u32[]{:S(2)}, u32[]{:S(2)}) collective-permute-start(f32[32,3456]{1,0:T(8,128)} %get-tuple-element.54.refs_1_), channel_id=1, source_target_pairs={{0,1},{1,0},{2,3},{3,2},{4,5},{5,4},{6,7},{7,6},{8,9},{9,8},{10,11... | collective-permute-start | bytes 1327112 | tf_op jit(solution)/shard_map/ppermute | solution.py:450
  (37 other events, 160.6 us)
Sparse Core Ops, SparseCore 0:
  156.5 109.5 all-reduce.4
  272.0 109.7 all-reduce.6

commit v3 on v2

--- a/solution.py
+++ b/solution.py
@@ -11,6 +11,9 @@
 F32 = jnp.float32
 BF16 = jnp.bfloat16
 GROUP = 4
+TAPS, SLOTS = 27, 32
+FULL = 32760.0
+LN2 = 0.6931471805599453
 VMEM = pl.BlockSpec(memory_space=pltpu.VMEM)
 SMEM = pl.BlockSpec(memory_space=pltpu.SMEM)
 ANY = pl.BlockSpec(memory_space=pl.ANY)
@@ -86,22 +89,28 @@
     return 0.5 + 0.5 * jnp.tanh(0.5 * value)
 
 
-def stats_kernel(planes_ref, par_ref, out_ref):
-    rows, frames, _, cols = planes_ref.shape
-    scale = columns_of(par_ref[0:1])[0]
+def planes_kernel(natural_ref, *refs):
+    out_ref = refs[-1] if len(refs) == 2 else refs[-2]
+    _, frames, rows, cols = natural_ref.shape
+    for row in range(rows):
+        for frame in range(frames):
+            out_ref[row, frame] = natural_ref[:, frame, row, :]
+    if len(refs) == 2:
+        return
+    scale = columns_of(refs[0][0:1])[0]
     planes = [
-        functools.partial(lambda r, t: planes_ref[r, t].astype(F32) * scale, r, t)
+        functools.partial(lambda r, t: out_ref[r, t].astype(F32) * scale, r, t)
         for r in range(rows)
         for t in range(frames)
     ]
-    out_ref[...] = local_stats(planes, float(GROUP * rows * frames * cols))
+    refs[-1][...] = local_stats(planes, float(GROUP * rows * frames * cols))
 
 
 def source(own, other, near, far, other_first):
     def at(row, frame):
         is_other = (frame < 2) == other_first
         if row == 0 or row == own.shape[0] + 1:
-            return (far if is_other else near), (0 if row == 0 else 1, frame % 2)
+            return (far if is_other else near)[0 if row == 0 else 1], (0, frame % 2)
         return (other if is_other else own), (row - 1, frame % 2)
 
     return at
@@ -165,11 +174,11 @@
 
 
 def conv_first_kernel(
-    flag_ref, own, past, near, far, edge_ref, rim_ref, par_ref, st_ref, weight, after, hidden_ref, st_out, stack_ref,
+    flag_ref, own, past, above, below, far_above, far_below, edge_ref, rim_ref, par_ref, st_ref, weight, hidden_ref, st_out, stack_ref,
     *, count
 ):
     rows, frames, channels, cols = own.shape
-    at = source(own, past, near, far, True)
+    at = source(own, past, (above, below), (far_above, far_below), True)
     mean, inverse, gain, shift, scale = norm_columns(par_ref, st_ref, count, 1)
 
     def act(latent):
@@ -207,9 +216,9 @@
     st_out[...] = local_stats(planes, float(GROUP * rows * frames * cols))
 
 
-def fill_future(stack, flag_ref, own, future, near, far, edge_ref, rim_ref):
+def fill_future(stack, flag_ref, own, future, above, below, far_above, far_below, edge_ref, rim_ref):
     rows = own.shape[0]
-    at = source(own, future, near, far, False)
+    at = source(own, future, (above, below), (far_above, far_below), False)
     on_left, on_right = sides(flag_ref)
     edges = (edge_ref[...], rim_ref[...])
     for row in range(rows + 2):
@@ -219,9 +228,10 @@
             fill_stack(stack, row, frame, ref[index], edges[which][:, number : number + 1], on_left, on_right)
 
 
-def conv_back_kernel(flag_ref, own, future, near, far, edge_ref, rim_ref, weight, grad_ref, stack_ref):
-    rows, frames, channels, cols = own.shape
-    fill_future(stack_ref, flag_ref, own, future, near, far, edge_ref, rim_ref)
+def conv_back_kernel(flag_ref, *refs):
+    weight, grad_ref, stack_ref = refs[-3:]
+    rows, frames, channels, _ = grad_ref.shape
+    fill_future(stack_ref, flag_ref, *refs[:-3])
     for row in range(rows):
         out = conv_rows(stack_ref, weight, row)
         for frame in range(frames):
@@ -259,37 +269,56 @@
 
 
 def put_halves(flag_ref, mine_ref, theirs_ref, tap, block):
-    channels = block.shape[0]
-    here = slice(tap * channels, (tap + 1) * channels)
-    upper, lower = block[: channels // 2], block[channels // 2 :]
+    half = block.shape[0] // 2
+    here = pl.ds(tap, half, stride=SLOTS)
+    upper, lower = block[:half], block[half:]
     is_first = flag_ref[3] == 0
-    mine_ref[:, here] = jnp.where(is_first, upper, lower)
-    theirs_ref[:, here] = jnp.where(is_first, lower, upper)
-
-
-def add_kernel(mine_ref, other_ref, after, *outs):
-    start = 0
-    for out in outs:
-        end = start + out.shape[0]
-        out[...] = mine_ref[start:end] + other_ref[start:end]
-        start = end
-
-
-def join_kernel(flag_ref, *refs):
-    out_ref = refs[-1]
-    pieces = len(refs[:-1]) // 2
-    mine, theirs = refs[:pieces], refs[pieces : 2 * pieces]
+    mine_ref[here, :] = jnp.where(is_first, upper, lower)
+    theirs_ref[here, :] = jnp.where(is_first, lower, upper)
+
+
+def encoded(value):
+    slot = lax.broadcasted_iota(jnp.int32, value.shape, 1)
+    value = jnp.where(slot < TAPS, value, 0.0)
+    top = jnp.max(jnp.abs(value), axis=1, keepdims=True)
+    power = jnp.ceil(jnp.log(jnp.maximum(top, 1e-30)) * (1.0 / LN2))
+    number = jnp.round(value * (FULL * jnp.exp(power * -LN2)))
+    return jnp.where(slot < TAPS, number, power).astype(jnp.int32).astype(jnp.int16)
+
+
+def decoded_value(number):
+    number = number.astype(jnp.int32).astype(F32)
+    return number * (jnp.exp(number[:, SLOTS - 1 : SLOTS] * LN2) * (1.0 / FULL))
+
+
+def first_scatter_kernel(mine_ref, other_ref, out_ref):
+    out_ref[...] = encoded(mine_ref[...] + other_ref[...])
+
+
+def scatter_kernel(received, out_ref, *, copies):
+    total = decoded_value(received[0])
+    for number in range(1, received.shape[0]):
+        total = total + decoded_value(received[number])
+    total = encoded(total)
+    if copies:
+        for number in range(copies):
+            out_ref[number] = total
+    else:
+        out_ref[...] = total
+
+
+def join_kernel(flag_ref, mine_ref, theirs_ref, after, out_ref, first_ref, second_ref):
+    half, _, channels = mine_ref.shape
     is_first = flag_ref[3] == 0
-    half = out_ref.shape[0] // 2
-    start = 0
-    for a, b in zip(mine, theirs):
-        end = start + a.shape[0]
-        out_ref[start:end] = jnp.where(is_first, a[...], b[...])
-        out_ref[half + start : half + end] = jnp.where(is_first, b[...], a[...])
-        start = end
-
-
-def weight_second_kernel(flag_ref, stack_ref, act_ref, mine_ref, theirs_ref, right_ref):
+    first_ref[...] = decoded_value(jnp.where(is_first, mine_ref[...], theirs_ref[...])).reshape(first_ref.shape)
+    second_ref[...] = decoded_value(jnp.where(is_first, theirs_ref[...], mine_ref[...])).reshape(second_ref.shape)
+    for tap in range(TAPS):
+        here = slice(tap * channels, (tap + 1) * channels)
+        out_ref[:half, here] = first_ref[pl.ds(tap, half, stride=SLOTS), :]
+        out_ref[half:, here] = second_ref[pl.ds(tap, half, stride=SLOTS), :]
+
+
+def weight_second_kernel(flag_ref, stack_ref, act_ref, after, mine_ref, theirs_ref, right_ref):
     rows, frames, channels, cols = act_ref.shape
     for row in range(rows):
         right_ref[row * cols : (row + 1) * cols] = jnp.transpose(
@@ -308,7 +337,7 @@
                 put_halves(flag_ref, mine_ref, theirs_ref, tap, term[across * channels : (across + 1) * channels])
 
 
-def weight_first_kernel(flag_ref, stack_ref, grad_ref, mine_ref, theirs_ref, right_ref):
+def weight_first_kernel(flag_ref, stack_ref, grad_ref, after, mine_ref, theirs_ref, right_ref):
     rows, frames, channels, cols = grad_ref.shape
     for row in range(rows):
         right_ref[row * cols : (row + 1) * cols] = jnp.transpose(
@@ -328,13 +357,11 @@
                 put_halves(flag_ref, mine_ref, theirs_ref, tap, block)
 
 
-def first_grad_kernel(
-    flag_ref, own, future, near, far, edge_ref, rim_ref, weight, latent, par_ref, st_ref, scaled_ref, sums_ref,
-    stack_ref, *, count
-):
-    rows, frames, channels, cols = own.shape
+def first_grad_kernel(flag_ref, *refs, count):
+    weight, latent, par_ref, st_ref, scaled_ref, sums_ref, stack_ref = refs[-7:]
+    rows, frames, channels, cols = latent.shape
     mean, inverse, gain, shift, scale = norm_columns(par_ref, st_ref, count, 1)
-    fill_future(stack_ref, flag_ref, own, future, near, far, edge_ref, rim_ref)
+    fill_future(stack_ref, flag_ref, *refs[:-7])
     first = jnp.zeros((channels, 128), F32)
     second = jnp.zeros((channels, 128), F32)
     for row in range(rows):
@@ -359,7 +386,7 @@
     for row in range(rows):
         for frame in range(frames):
             normed = (latent[row, frame].astype(F32) * scale - mean) * inverse
-            out_ref[row, frame] = cotangent[row, frame].astype(F32) + inverse * (
+            out_ref[:, frame, row, :] = cotangent[row, frame].astype(F32) + inverse * (
                 scaled[row, frame] - first - normed * second
             )
 
@@ -408,18 +435,18 @@
     return lax.ppermute(value, axis, [(source, source + steps) for source in range(initial, last)])
 
 
-def rounds(radix=2):
-    for axis in ("width", "height", "tm"):
+def rounds():
+    for axis in ("tm", "height", "width"):
         count = lax.axis_size(axis)
         step = 1
         while step < count:
-            wide = radix if step * radix <= count else 2
-            yield axis, [[(i, i ^ (step * k)) for i in range(count)] for k in range(1, wide)]
+            wide = 4 if 4 * step <= count else 2
+            yield axis, step, [[(i, i ^ (step * k)) for i in range(count)] for k in range(1, wide)]
             step *= wide
 
 
-def all_sum(value, radix=2):
-    for axis, exchanges in rounds(radix):
+def all_sum(value):
+    for axis, _, exchanges in rounds():
         parts = [value] + [lax.ppermute(value, axis, pairs) for pairs in exchanges]
         while len(parts) > 1:
             parts = [a + b for a, b in zip(parts[::2], parts[1::2])]
@@ -427,12 +454,15 @@
     return value
 
 
-def gathered_sum(value):
-    return jnp.sum(lax.all_gather(value, ("tm", "height", "width")), axis=0)
-
-
-def all_stats(value, count, radix=2):
-    for axis, exchanges in rounds(radix):
+def exchanged_sum(value):
+    axes = ("tm", "height", "width")
+    devices = lax.axis_size(axes)
+    value = jnp.broadcast_to(value[None], (devices, *value.shape))
+    return jnp.sum(lax.all_to_all(value, axes, 0, 0, tiled=True), axis=0)
+
+
+def all_stats(value, count):
+    for axis, _, exchanges in rounds():
         parts = [value] + [lax.ppermute(value, axis, pairs) for pairs in exchanges]
         while len(parts) > 1:
             joined = []
@@ -450,41 +480,63 @@
     return lax.ppermute(value, "width", [(0, 1), (1, 0)])
 
 
-def reduce_weights(flags, mine, theirs, pieces, axes, after_first, after_sum):
-    other = swapped(theirs)
-    half, cols = mine.shape
-    parts = call(
-        add_kernel,
-        [shape((half // pieces, cols), F32)] * pieces,
-        [VMEM, VMEM, ANY],
-        (mine, other, after_first),
-    )
-    parts = lax.psum(tuple(parts), axes)
-    parts, _ = lax.optimization_barrier((parts, after_sum))
-    others = [swapped(part) for part in parts]
+def exchanged(value, axis):
+    return lax.all_to_all(value, axis, 0, 0, tiled=True)
+
+
+def reduce_weights(flags, mine, theirs, after):
+    half, _, channels = mine.shape
+    by_height, by_tm = lax.axis_size("height"), lax.axis_size("tm")
+    coded = functools.partial(lambda *dims: shape((*dims, SLOTS, channels), jnp.int16))
+    (value,) = call(first_scatter_kernel, [coded(half)], [VMEM] * 2, (mine, swapped(theirs)))
+    value = exchanged(value, "height")
+    rows = half // by_height
+    (value,) = call(
+        functools.partial(scatter_kernel, copies=0),
+        [coded(rows)],
+        [VMEM],
+        (value.reshape(by_height, rows, SLOTS, channels),),
+    )
+    value = exchanged(value, "tm")
+    rows = rows // by_tm
+    (value,) = call(
+        functools.partial(scatter_kernel, copies=by_tm),
+        [coded(by_tm, rows)],
+        [VMEM],
+        (value.reshape(by_tm, rows, SLOTS, channels),),
+    )
+    value = exchanged(value, "tm").reshape(1, by_tm * rows, SLOTS, channels)
+    value = exchanged(jnp.broadcast_to(value, (by_height, *value.shape[1:])), "height")
+    value = value.reshape(half, SLOTS, channels)
     (total,) = call(
-        join_kernel, [shape((2 * half, cols), F32)], [SMEM] + [VMEM] * (2 * pieces), (flags, *parts, *others)
+        join_kernel,
+        [shape((2 * half, TAPS * channels), F32)],
+        [SMEM] + [VMEM] * 2 + [ANY],
+        (flags, value, swapped(value), after),
+        scratch=[pltpu.VMEM((half * SLOTS, channels), F32)] * 2,
     )
     return total
 
 
 def row_exchange(block):
-    return jnp.stack([shifted(block[-1], "height", 1), shifted(block[0], "height", -1)])
-
-
-def edges(flags, first, second):
-    channels = first.shape[2]
-    (columns,) = call(edges_kernel, [shape((channels, 128), BF16)], [SMEM, VMEM, VMEM], (flags, first, second))
+    return shifted(block[-1:], "height", 1), shifted(block[:1], "height", -1)
+
+
+def edges(flags, *planes):
+    channels = planes[0].shape[2]
+    (columns,) = call(
+        edges_kernel, [shape((channels, 128), BF16)], [SMEM] + [VMEM] * len(planes), (flags, *planes)
+    )
     return columns
 
 
 def extended(flags, own, steps):
     other = shifted(own, "tm", steps)
     near = row_exchange(own)
-    far = row_exchange(other)
+    far = [shifted(row, "tm", steps) for row in near]
     edge = swapped(edges(flags, own, other))
-    rim = edges(flags, near, far)
-    return (other, near, far, edge, swapped(rim)), rim
+    rim = swapped(edges(flags, *near, *far))
+    return other, *near, *far, edge, rim
 
 
 def shards(
@@ -515,18 +567,19 @@
     scale = jnp.repeat(jnp.exp2(exponents.astype(F32)), channels // groups)
     zeros = jnp.zeros_like(scale)
     par = jnp.stack([scale, gain_first, shift_first, gain_second, shift_second, zeros, zeros, zeros])
-    latent = latent.transpose(2, 1, 0, 3)
-    cotangent = cotangent.transpose(2, 1, 0, 3)
     block = (rows, frames, channels, cols)
     stack = (rows + 2, 4, 3 * channels, cols)
     taps = (2 * channels, 36 * channels)
-    halves = [shape((channels // 2, 27 * channels), F32)] * 2
+    halves = [shape((channels // 2 * SLOTS, channels), F32)] * 2
     conv_flops = 2 * 4 * 256 * 36 * channels * 2 * channels
     small = shape((2, channels), F32)
 
-    (stats_first,) = call(stats_kernel, [small], [VMEM] * 2, (latent, par))
-    around, _ = extended(flags, latent, 1)
-    around_c, ready_c = extended(flags, cotangent, -1)
+    latent, stats_first = call(
+        planes_kernel, [shape(block, BF16), small], [VMEM] * 2, (latent, par)
+    )
+    around = extended(flags, latent, 1)
+    (cotangent,) = call(planes_kernel, [shape(block, BF16)], [VMEM, ANY], (cotangent, around[0]))
+    around_c = extended(flags, cotangent, -1)
     stats_first = all_stats(stats_first, float(here))
     (weight_first,) = call(weight_forward_kernel, [shape(taps, BF16)], [VMEM], (conv_first,))
     (weight_second_t,) = call(weight_back_kernel, [shape(taps, BF16)], [VMEM], (conv_second,))
@@ -535,16 +588,16 @@
     hidden, stats_second, stack_first = call(
         functools.partial(conv_first_kernel, count=count),
         [shape(block, F32), small, shape(stack, BF16)],
-        [SMEM] + [VMEM] * 9 + [ANY],
-        (flags, latent, *around, par, stats_first, weight_first, ready_c),
+        [SMEM] + [VMEM] * 11,
+        (flags, latent, *around, par, stats_first, weight_first),
         flops=conv_flops,
         transcendentals=3 * latent.size,
     )
-    stats_second = all_stats(stats_second, float(here), 4)
+    stats_second = all_stats(stats_second, float(here))
     grad_second, stack_c = call(
         conv_back_kernel,
         [shape(block, F32), shape(stack, BF16)],
-        [SMEM] + [VMEM] * 7,
+        [SMEM] + [VMEM] * 9,
         (flags, cotangent, *around_c, weight_second_t),
         flops=conv_flops,
     )
@@ -555,12 +608,12 @@
         (hidden, grad_second, par, stats_second),
         transcendentals=latent.size,
     )
-    sums = gathered_sum(sums)
+    sums = all_sum(sums)
     halves_second = call(
         weight_second_kernel,
         halves,
-        [SMEM] + [VMEM] * 2,
-        (flags, stack_c, act_second),
+        [SMEM] + [VMEM] * 2 + [ANY],
+        (flags, stack_c, act_second, act_second),
         scratch=[pltpu.VMEM((rows * cols, frames * channels), BF16)],
         flops=conv_flops,
     )
@@ -570,34 +623,37 @@
         [VMEM] * 5,
         (hidden, scaled, par, stats_second, sums),
     )
-    around, _ = extended(flags, hidden_grad, -1)
+    around = extended(flags, hidden_grad, -1)
     halves_first = call(
         weight_first_kernel,
         halves,
-        [SMEM] + [VMEM] * 2,
-        (flags, stack_first, hidden_grad),
+        [SMEM] + [VMEM] * 2 + [ANY],
+        (flags, stack_first, hidden_grad, around[1]),
         scratch=[pltpu.VMEM((rows * cols, frames * channels), BF16)],
         flops=conv_flops,
     )
     scaled, sums_first = call(
         functools.partial(first_grad_kernel, count=count),
         [shape(block, F32), small],
-        [SMEM] + [VMEM] * 10,
+        [SMEM] + [VMEM] * 12,
         (flags, hidden_grad, *around, weight_first_t, latent, par, stats_first),
         scratch=[pltpu.VMEM(stack, BF16)],
         flops=conv_flops,
         transcendentals=latent.size,
     )
-    sums_first = all_sum(sums_first)
-    conv_second_grad = reduce_weights(flags, *halves_second, 2, ("height", "tm"), sums, sums_first)
-    conv_first_grad = reduce_weights(flags, *halves_first, 4, ("tm", "height"), hidden_grad, sums_first)
+    sums_first = exchanged_sum(sums_first)
+    halves_second, halves_first = (
+        [v.reshape(channels // 2, SLOTS, channels) for v in halves] for halves in (halves_second, halves_first)
+    )
+    conv_second_grad = reduce_weights(flags, *halves_second, sums_first)
+    conv_first_grad = reduce_weights(flags, *halves_first, sums_first)
     (decoded_grad,) = call(
         functools.partial(decoded_grad_kernel, count=count),
-        [shape(block, F32)],
+        [shape((channels, frames, rows, cols), F32)],
         [VMEM] * 6,
         (scaled, latent, cotangent, par, stats_first, sums_first),
     )
-    return decoded_grad.transpose(2, 1, 0, 3), conv_first_grad, conv_second_grad
+    return decoded_grad, conv_first_grad, conv_second_grad
 
 
 def solution(mesh):

time: 399 us -> 256 us (0.64)
  waiting for transfers between devices: 216 us -> 55.9 us
  starting transfers between devices: 66.6 us -> 102 us
  Pallas kernels: 43.8 us -> 60 us
  blocking collectives: 41.1 us -> 26.7 us
  between operations: 14.7 us -> 1.23 us
  local copies, waits for them, and re-layouts: 13.7 us -> 7.92 us
    psum x2 -> x0, waiting for transfers between devices: 173 us -> none  [reduce_weights(): parts = lax.psum(tuple(parts), axes)]
    all_gather x1 -> x0, blocking collectives: 41.1 us -> none  [gathered_sum(): return jnp.sum(lax.all_gather(value, ('tm', 'height', 'width')), axis=0)]
    all_to_all x0 -> x3, blocking collectives: none -> 26.7 us  [the longest x2 15.7 us: exchanged(): return lax.all_to_all(value, axis, 0, 0, tiled=True)]
    all_to_all x0 -> x6, waiting for transfers between devices: none -> 25.7 us  [exchanged(): return lax.all_to_all(value, axis, 0, 0, tiled=True)]
    all_to_all x0 -> x6, starting transfers between devices: none -> 21.2 us  [exchanged(): return lax.all_to_all(value, axis, 0, 0, tiled=True)]
    pallas_call x22 -> x27, Pallas kernels: 43.8 us -> 60 us  [call(): pl.pallas_call(body, out_shape=tuple(outs), in_specs=specs, out_specs=tup...]
    ppermute x12 -> x14, waiting for transfers between devices: 13 us -> 2.7 us  [all_stats(): parts = [value] + [lax.ppermute(value, axis, pairs) for pairs in exchanges]]
    ppermute x5 -> x7, starting transfers between devices: 0.97 us -> 10.9 us  [all_sum(): parts = [value] + [lax.ppermute(value, axis, pairs) for pairs in exchanges]]
  transfers between devices with their start and end apart: 48 -> 52, of which waited for: 15 -> 22; matrix products, arithmetic and copies ran while one was open for 1% -> 0% of each run, Pallas kernels for 7% -> 16%
where the time goes in v3:
time: 256 us; the launch traced here: 254 us
  starting transfers between devices  102 us (40%)
  Pallas kernels  60 us (23%)
  waiting for transfers between devices  55.9 us (22%)
  blocking collectives  26.7 us (10%)
  local copies, waits for them, and re-layouts  7.92 us (3%)
    pallas_call x27, Pallas kernels, call(): pl.pallas_call(body, out_shape=tuple(outs), in_specs=specs, out_specs=tup...  60 us
    ppermute x15, starting transfers between devices, shifted(): lax.ppermute(value, axis, [(source, source + steps) for source in range(i...  30.3 us
    all_to_all x6, waiting for transfers between devices, exchanged(): return lax.all_to_all(value, axis, 0, 0, tiled=True)  25.7 us
    ppermute x14, starting transfers between devices, all_stats(): parts = [value] + [lax.ppermute(value, axis, pairs) for pairs in exchanges]  21.9 us
    all_to_all x6, starting transfers between devices, exchanged(): return lax.all_to_all(value, axis, 0, 0, tiled=True)  21.2 us
    ppermute x15, waiting for transfers between devices, shifted(): lax.ppermute(value, axis, [(source, source + steps) for source in range(i...  20 us
    ppermute x10, starting transfers between devices, swapped(): return lax.ppermute(value, 'width', [(0, 1), (1, 0)])  17.4 us
    all_to_all x2, blocking collectives, exchanged(): return lax.all_to_all(value, axis, 0, 0, tiled=True)  15.7 us
  transfers between devices with their start and end apart: 52, of which 22 were waited for; matrix products, arithmetic and copies ran while one was open for 0% of the time, Pallas kernels for 16%

profile of v3, /device:TPU:1, one launch (start us, length us, event | category | flops | bytes accessed | tf_op | source)
XLA Modules:
  0.0 254.5 jit_solution(6847637114028285425)
XLA Ops:
  11.4 3.1 %collective-permute-start.1 = (bf16[1,2,128,256]{3,2,1,0:T(8,128)(2,1)S(1)}, bf16[1,2,128,256]{3,2,1,0:T(8,128)(2,1)S(1)}, u32[]{:S(2)}, u32[]{:S(2)}) collective-permute-start(bf16[1,2,128,256]{3,2,1,0:T(8,128)(2,1)S(1)} %get-tuple-element.40), channel_id=1, source_target_pairs={{0,2},{2,4},{4,6},{1,3},{3,5},{5,7},{8,10},{10,12},{12,14},{9,11},... | collective-permute-start | bytes 393224 | tf_op jit(solution)/shard_map/ppermute | solution.py:435
  19.4 4.0 %collective-permute-start.13 = (f32[2,128]{1,0:T(2,128)S(1)}, f32[2,128]{1,0:T(2,128)S(1)}, u32[]{:S(2)}, u32[]{:S(2)}) collective-permute-start(f32[2,128]{1,0:T(2,128)S(1)} %pad_maximum_fusion.1), channel_id=1, source_target_pairs={{0,1},{1,0},{2,3},{3,2},{4,5},{5,4},{6,7},{7,6},{8,9},{9,8},{10,11... | collective-permute-start | bytes 3080 | tf_op jit(solution)/shard_map/ppermute | solution.py:466
  27.5 4.1 %collective-permute-start.4 = (bf16[1,2,128,256]{3,2,1,0:T(8,128)(2,1)S(1)}, bf16[1,2,128,256]{3,2,1,0:T(8,128)(2,1)S(1)}, u32[]{:S(2)}, u32[]{:S(2)}) collective-permute-start(bf16[1,2,128,256]{3,2,1,0:T(8,128)(2,1)S(1)} %collective-permute-done.2.refs_1_.below), channel_id=1, source_target_pairs={{0,8},{8,16},{16,24},{1,9},{9,17},{17,25},{2,10},{10,18},{18,26},{... | collective-permute-start | bytes 393224 | tf_op jit(solution)/shard_map/ppermute | solution.py:435
  39.1 6.7 %shard_map.116 = (f32[4,2,128,256]{3,2,1,0:T(8,128)S(1)}, f32[2,128]{1,0:T(2,128)S(1)}, bf16[6,4,384,256]{3,2,1,0:T(8,128)(2,1)}) custom-call(s32[4]{0:T(128)S(1)} %pad_add_fusion.flag_ref, bf16[4,2,128,256]{3,2,1,0:T(8,128)(2,1)S(1)} %get-tuple-element.19.refs_0_.own.refs_9_.latent, bf16[4,2,128,256]{3,2,1,0:T(8,128)(2,1)S(1)} %collective-permute-done.refs_1_.past.refs_0_, ...), custom_call_target="tpu_custom_call" | custom-call | flops 2415919104 | bytes 9771024 | tf_op jit(solution)/shard_map/pallas_call | solution.py:25
  57.5 3.2 %collective-permute-start.15 = (bf16[1,2,128,256]{3,2,1,0:T(8,128)(2,1)S(1)}, bf16[1,2,128,256]{3,2,1,0:T(8,128)(2,1)S(1)}, u32[]{:S(2)}, u32[]{:S(2)}) collective-permute-start(bf16[1,2,128,256]{3,2,1,0:T(8,128)(2,1)S(1)} %get-tuple-element.38), channel_id=1, source_target_pairs={{0,2},{2,4},{4,6},{1,3},{3,5},{5,7},{8,10},{10,12},{12,14},{9,11},... | collective-permute-start | bytes 393224 | tf_op jit(solution)/shard_map/ppermute | solution.py:435
  62.1 3.1 %collective-permute-start.27 = (f32[2,128]{1,0:T(2,128)S(1)}, f32[2,128]{1,0:T(2,128)S(1)}, u32[]{:S(2)}, u32[]{:S(2)}) collective-permute-start(f32[2,128]{1,0:T(2,128)S(1)} %pad_maximum_fusion.4), channel_id=1, source_target_pairs={{0,1},{1,0},{2,3},{3,2},{4,5},{5,4},{6,7},{7,6},{8,9},{9,8},{10,11... | collective-permute-start | bytes 3080 | tf_op jit(solution)/shard_map/ppermute | solution.py:466
  68.5 5.5 %collective-permute-done.17.refs_2_.refs_4_ = bf16[1,2,128,256]{3,2,1,0:T(8,128)(2,1)S(1)} collective-permute-done((bf16[1,2,128,256]{3,2,1,0:T(8,128)(2,1)S(1)}, bf16[1,2,128,256]{3,2,1,0:T(8,128)(2,1)S(1)}, u32[]{:S(2)}, u32[]{:S(2)}) %collective-permute-start.17) | collective-permute-done | bytes 131104 | tf_op jit(solution)/shard_map/ppermute | solution.py:435
  81.8 5.3 %shard_map.121 = (f32[4,2,128,256]{3,2,1,0:T(8,128)S(1)}, bf16[6,4,384,256]{3,2,1,0:T(8,128)(2,1)}) custom-call(s32[4]{0:T(128)S(1)} %pad_add_fusion.flag_ref, bf16[4,2,128,256]{3,2,1,0:T(8,128)(2,1)S(1)} %shard_map.117.refs_0_.cotangent, bf16[4,2,128,256]{3,2,1,0:T(8,128)(2,1)S(1)} %collective-permute-done.14.refs_1_, ...), custom_call_target="tpu_custom_call" | custom-call | flops 2415919104 | bytes 9764880 | tf_op jit(solution)/shard_map/pallas_call | solution.py:25
  100.1 3.3 %collective-permute-start.34 = (f32[2,128]{1,0:T(2,128)S(1)}, f32[2,128]{1,0:T(2,128)S(1)}, u32[]{:S(2)}, u32[]{:S(2)}) collective-permute-start(f32[2,128]{1,0:T(2,128)S(1)} %add_add_fusion), channel_id=1, source_target_pairs={{0,1},{1,0},{2,3},{3,2},{4,5},{5,4},{6,7},{7,6},{8,9},{9,8},{10,11... | collective-permute-start | bytes 3080 | tf_op jit(solution)/shard_map/ppermute | solution.py:450
  103.4 6.4 %shard_map.134 = (f32[2048,128]{1,0:T(8,128)S(1)}, f32[2048,128]{1,0:T(8,128)S(1)}) custom-call(s32[4]{0:T(128)S(1)} %pad_add_fusion.flag_ref, bf16[6,4,384,256]{3,2,1,0:T(8,128)(2,1)} %get-tuple-element.31.stack_ref, bf16[4,2,128,256]{3,2,1,0:T(8,128)(2,1)S(1)} %get-tuple-element.32.act_ref.after, bf16[4,2,128,256]{3,2,1,0:T(8,128)(2,1)S(1)} %get-tuple-element.32.act_ref.after), custom_call_target="tpu_custom_call" | custom-call | flops 2415919104 | bytes 7864336 | tf_op jit(solution)/shard_map/pallas_call | solution.py:25
  111.1 3.2 %collective-permute-start.36 = (bf16[1,2,128,256]{3,2,1,0:T(8,128)(2,1)S(1)}, bf16[1,2,128,256]{3,2,1,0:T(8,128)(2,1)S(1)}, u32[]{:S(2)}, u32[]{:S(2)}) collective-permute-start(bf16[1,2,128,256]{3,2,1,0:T(8,128)(2,1)S(1)} %get-tuple-element.36), channel_id=1, source_target_pairs={{0,2},{2,4},{4,6},{1,3},{3,5},{5,7},{8,10},{10,12},{12,14},{9,11},... | collective-permute-start | bytes 393224 | tf_op jit(solution)/shard_map/ppermute | solution.py:435
  116.6 7.5 %shard_map.129 = (f32[2048,128]{1,0:T(8,128)S(1)}, f32[2048,128]{1,0:T(8,128)}) custom-call(s32[4]{0:T(128)S(1)} %pad_add_fusion.flag_ref, bf16[6,4,384,256]{3,2,1,0:T(8,128)(2,1)} %get-tuple-element.28.stack_ref, bf16[4,2,128,256]{3,2,1,0:T(8,128)(2,1)S(1)} %shard_map.123.refs_0_.grad_ref, ...), custom_call_target="tpu_custom_call" | custom-call | flops 2415919104 | bytes 7471120 | tf_op jit(solution)/shard_map/pallas_call | solution.py:25
  126.5 4.1 %all-to-all-start.5 = ((s16[64,32,128]{2,1,0:T(8,128)(2,1)}), s16[64,32,128]{2,1,0:T(8,128)(2,1)S(1)}, u32[]{:S(2)}, u32[]{:S(2)}) async-start(s16[64,32,128]{2,1,0:T(8,128)(2,1)} %shard_map.135), calls=%async_computation.5 | async-start | bytes 1048576 | tf_op jit(solution)/shard_map/all_to_all | solution.py:484
  133.0 6.7 %all-to-all-done.5 = s16[64,32,128]{2,1,0:T(8,128)(2,1)S(1)} async-done(((s16[64,32,128]{2,1,0:T(8,128)(2,1)}), s16[64,32,128]{2,1,0:T(8,128)(2,1)S(1)}, u32[]{:S(2)}, u32[]{:S(2)}) %all-to-all-start.5) | async-done | bytes 524320 | tf_op jit(solution)/shard_map/all_to_all | solution.py:484
  139.7 3.5 %all-to-all-start.1 = ((s16[64,32,128]{2,1,0:T(8,128)(2,1)}), s16[64,32,128]{2,1,0:T(8,128)(2,1)S(1)}, u32[]{:S(2)}, u32[]{:S(2)}) async-start(s16[64,32,128]{2,1,0:T(8,128)(2,1)} %shard_map.130), calls=%async_computation.1 | async-start | bytes 1048576 | tf_op jit(solution)/shard_map/all_to_all | solution.py:484
  144.1 6.6 %all-to-all-done.1 = s16[64,32,128]{2,1,0:T(8,128)(2,1)S(1)} async-done(((s16[64,32,128]{2,1,0:T(8,128)(2,1)}), s16[64,32,128]{2,1,0:T(8,128)(2,1)S(1)}, u32[]{:S(2)}, u32[]{:S(2)}) %all-to-all-start.1) | async-done | bytes 524320 | tf_op jit(solution)/shard_map/all_to_all | solution.py:484
  150.8 3.5 %all-to-all-start.6 = ((s16[16,32,128]{2,1,0:T(8,128)(2,1)}), s16[16,32,128]{2,1,0:T(8,128)(2,1)S(1)}, u32[]{:S(2)}, u32[]{:S(2)}) async-start(s16[16,32,128]{2,1,0:T(8,128)(2,1)} %shard_map.136), calls=%async_computation.6 | async-start | bytes 262144 | tf_op jit(solution)/shard_map/all_to_all | solution.py:484
  155.2 3.7 %all-to-all-done.6 = s16[16,32,128]{2,1,0:T(8,128)(2,1)S(1)} async-done(((s16[16,32,128]{2,1,0:T(8,128)(2,1)}), s16[16,32,128]{2,1,0:T(8,128)(2,1)S(1)}, u32[]{:S(2)}, u32[]{:S(2)}) %all-to-all-start.6) | async-done | bytes 131104 | tf_op jit(solution)/shard_map/all_to_all | solution.py:484
  159.0 3.3 %all-to-all-start.2 = ((s16[16,32,128]{2,1,0:T(8,128)(2,1)}), s16[16,32,128]{2,1,0:T(8,128)(2,1)S(1)}, u32[]{:S(2)}, u32[]{:S(2)}) async-start(s16[16,32,128]{2,1,0:T(8,128)(2,1)} %shard_map.131), calls=%async_computation.2 | async-start | bytes 262144 | tf_op jit(solution)/shard_map/all_to_all | solution.py:484
  163.0 4.0 %all-to-all-done.2 = s16[16,32,128]{2,1,0:T(8,128)(2,1)S(1)} async-done(((s16[16,32,128]{2,1,0:T(8,128)(2,1)}), s16[16,32,128]{2,1,0:T(8,128)(2,1)S(1)}, u32[]{:S(2)}, u32[]{:S(2)}) %all-to-all-start.2) | async-done | bytes 131104 | tf_op jit(solution)/shard_map/all_to_all | solution.py:484
  167.0 3.3 %all-to-all-start.7 = ((s16[4,4,32,128]{3,2,1,0:T(8,128)(2,1)}), s16[4,4,32,128]{3,2,1,0:T(8,128)(2,1)S(1)}, u32[]{:S(2)}, u32[]{:S(2)}) async-start(s16[4,4,32,128]{3,2,1,0:T(8,128)(2,1)} %shard_map.137), calls=%async_computation.7 | async-start | bytes 262144 | tf_op jit(solution)/shard_map/all_to_all | solution.py:484
  170.5 4.6 %all-to-all-done.7 = s16[4,4,32,128]{3,2,1,0:T(8,128)(2,1)S(1)} async-done(((s16[4,4,32,128]{3,2,1,0:T(8,128)(2,1)}), s16[4,4,32,128]{3,2,1,0:T(8,128)(2,1)S(1)}, u32[]{:S(2)}, u32[]{:S(2)}) %all-to-all-start.7) | async-done | bytes 131104 | tf_op jit(solution)/shard_map/all_to_all | solution.py:484
  175.1 7.2 %all_to_all.45 = s16[4,4,32,128]{3,2,1,0:T(8,128)(2,1)S(1)} all-to-all(s16[4,4,32,128]{3,2,1,0:T(8,128)(2,1)S(1)} %shard_map.132), channel_id=1, replica_groups=mesh['tm'=4,'height'=4,'width'=2] {'tm'}, dimensions={0} | all-to-all | bytes 262144 | tf_op jit(solution)/shard_map/all_to_all | solution.py:484
  182.4 8.5 %all_to_all.46 = s16[4,16,32,128]{3,2,1,0:T(8,128)(2,1)S(1)} all-to-all(s16[4,16,32,128]{3,2,1,0:T(8,128)(2,1)S(1)} %broadcast_in_dim.28), channel_id=1, replica_groups=mesh['tm'=4,'height'=4,'width'=2] {'height'}, dimensions={0} | all-to-all | bytes 1048576 | tf_op jit(solution)/shard_map/all_to_all | solution.py:484
  191.7 3.5 %all-to-all-start.4 = ((s16[4,16,32,128]{3,2,1,0:T(8,128)(2,1)}), s16[4,16,32,128]{3,2,1,0:T(8,128)(2,1)S(1)}, u32[]{:S(2)}, u32[]{:S(2)}) async-start(s16[4,16,32,128]{3,2,1,0:T(8,128)(2,1)} %broadcast_in_dim.26), calls=%async_computation.4 | async-start | bytes 1048576 | tf_op jit(solution)/shard_map/all_to_all | solution.py:484
  197.8 7.7 %collective-permute-start.45 = (s16[64,32,128]{2,1,0:T(8,128)(2,1)S(1)}, s16[64,32,128]{2,1,0:T(8,128)(2,1)}, u32[]{:S(2)}, u32[]{:S(2)}) collective-permute-start(s16[64,32,128]{2,1,0:T(8,128)(2,1)S(1)} %bitcast.24), channel_id=1, source_target_pairs={{0,1},{1,0},{2,3},{3,2},{4,5},{5,4},{6,7},{7,6},{8,9},{9,8},{10,11... | collective-permute-start | bytes 1572872 | tf_op jit(solution)/shard_map/ppermute | solution.py:480
  205.5 3.9 %collective-permute-start.43 = (s16[64,32,128]{2,1,0:T(8,128)(2,1)S(1)}, s16[64,32,128]{2,1,0:T(8,128)(2,1)}, u32[]{:S(2)}, u32[]{:S(2)}) collective-permute-start(s16[64,32,128]{2,1,0:T(8,128)(2,1)S(1)} %bitcast.22), channel_id=1, source_target_pairs={{0,1},{1,0},{2,3},{3,2},{4,5},{5,4},{6,7},{7,6},{8,9},{9,8},{10,11... | collective-permute-start | bytes 1572872 | tf_op jit(solution)/shard_map/ppermute | solution.py:480
  212.0 4.6 %collective-permute-done.38.refs_2_.refs_4_ = bf16[1,2,128,256]{3,2,1,0:T(8,128)(2,1)S(1)} collective-permute-done((bf16[1,2,128,256]{3,2,1,0:T(8,128)(2,1)}, bf16[1,2,128,256]{3,2,1,0:T(8,128)(2,1)S(1)}, u32[]{:S(2)}, u32[]{:S(2)}) %collective-permute-start.38) | collective-permute-done | bytes 131104 | tf_op jit(solution)/shard_map/ppermute | solution.py:435
  225.8 4.6 %shard_map.127 = (f32[4,2,128,256]{3,2,1,0:T(8,128)S(1)}, f32[2,128]{1,0:T(2,128)S(1)}) custom-call(s32[4]{0:T(128)S(1)} %pad_add_fusion.flag_ref, bf16[4,2,128,256]{3,2,1,0:T(8,128)(2,1)S(1)} %shard_map.123.refs_0_.grad_ref, bf16[4,2,128,256]{3,2,1,0:T(8,128)(2,1)} %collective-permute-done.35.refs_1_, bf16[1,2,128,256]{3,2,1,0:T(8,128)(2,1)S(1)} %copy-done.9, ...), custom_call_target="tpu_custom_call" | custom-call | flops 2415919104 | bytes 5576720 | tf_op jit(solution)/shard_map/pallas_call | solution.py:25
  231.4 11.0 %all_to_all.47 = f32[32,2,128]{2,1,0:T(2,128)S(1)} all-to-all(f32[32,2,128]{2,1,0:T(2,128)S(1)} %broadcast_in_dim.24), channel_id=1, replica_groups=mesh['tm'=4,'height'=4,'width'=2] {'tm','height','width'}, dimensions={0} | all-to-all | bytes 65536 | tf_op jit(solution)/shard_map/all_to_all | solution.py:461
  245.6 4.4 %shard_map.138 = f32[128,3456]{1,0:T(8,128)} custom-call(s32[4]{0:T(128)S(1)} %pad_add_fusion.flag_ref, s16[64,32,128]{2,1,0:T(8,128)(2,1)S(1)} %bitcast.25, s16[64,32,128]{2,1,0:T(8,128)(2,1)} %collective-permute-done.45.theirs_ref, f32[2,128]{1,0:T(2,128)S(1)} %reduce_sum.9.sums_ref.after), custom_call_target="tpu_custom_call" | custom-call | bytes 2819088 | tf_op jit(solution)/shard_map/pallas_call | solution.py:25
  250.0 4.4 %shard_map.133 = f32[128,3456]{1,0:T(8,128)} custom-call(s32[4]{0:T(128)S(1)} %pad_add_fusion.flag_ref, s16[64,32,128]{2,1,0:T(8,128)(2,1)S(1)} %bitcast.23, s16[64,32,128]{2,1,0:T(8,128)(2,1)} %collective-permute-done.43.theirs_ref, f32[2,128]{1,0:T(2,128)S(1)} %reduce_sum.9.sums_ref.after), custom_call_target="tpu_custom_call" | custom-call | bytes 2819088 | tf_op jit(solution)/shard_map/pallas_call | solution.py:25
  (151 shorter events, 94.8 us)
Async XLA Ops:
  4.6 9.9 %collective-permute-start.7 = (f32[2,128]{1,0:T(2,128)S(1)}, f32[2,128]{1,0:T(2,128)S(1)}, u32[]{:S(2)}, u32[]{:S(2)}) collective-permute-start(f32[2,128]{1,0:T(2,128)S(1)} %get-tuple-element.20), channel_id=1, source_target_pairs={{0,8},{8,0},{16,24},{24,16},{1,9},{9,1},{17,25},{25,17},{2,10},{10... | collective-permute-start | bytes 3080 | tf_op jit(solution)/shard_map/ppermute | solution.py:466
  6.8 7.8 %collective-permute-start.8 = (f32[2,128]{1,0:T(2,128)S(1)}, f32[2,128]{1,0:T(2,128)S(1)}, u32[]{:S(2)}, u32[]{:S(2)}) collective-permute-start(f32[2,128]{1,0:T(2,128)S(1)} %get-tuple-element.20), channel_id=1, source_target_pairs={{0,16},{8,24},{16,0},{24,8},{1,17},{9,25},{17,1},{25,9},{2,18},{10... | collective-permute-start | bytes 3080 | tf_op jit(solution)/shard_map/ppermute | solution.py:466
  9.1 27.2 %collective-permute-start = (bf16[4,2,128,256]{3,2,1,0:T(8,128)(2,1)S(1)}, bf16[4,2,128,256]{3,2,1,0:T(8,128)(2,1)S(1)}, u32[]{:S(2)}, u32[]{:S(2)}) collective-permute-start(bf16[4,2,128,256]{3,2,1,0:T(8,128)(2,1)S(1)} %get-tuple-element.19.refs_0_.own.refs_9_.latent), channel_id=1, source_target_pairs={{0,8},{8,16},{16,24},{1,9},{9,17},{17,25},{2,10},{10,18},{18,26},{... | collective-permute-start | bytes 1572872 | tf_op jit(solution)/shard_map/ppermute | solution.py:435
  11.4 13.4 %collective-permute-start.1 = (bf16[1,2,128,256]{3,2,1,0:T(8,128)(2,1)S(1)}, bf16[1,2,128,256]{3,2,1,0:T(8,128)(2,1)S(1)}, u32[]{:S(2)}, u32[]{:S(2)}) collective-permute-start(bf16[1,2,128,256]{3,2,1,0:T(8,128)(2,1)S(1)} %get-tuple-element.40), channel_id=1, source_target_pairs={{0,2},{2,4},{4,6},{1,3},{3,5},{5,7},{8,10},{10,12},{12,14},{9,11},... | collective-permute-start | bytes 393224 | tf_op jit(solution)/shard_map/ppermute | solution.py:435
  18.0 9.5 %collective-permute-start.2 = (bf16[1,2,128,256]{3,2,1,0:T(8,128)(2,1)S(1)}, bf16[1,2,128,256]{3,2,1,0:T(8,128)(2,1)S(1)}, u32[]{:S(2)}, u32[]{:S(2)}) collective-permute-start(bf16[1,2,128,256]{3,2,1,0:T(8,128)(2,1)S(1)} %get-tuple-element.39), channel_id=1, source_target_pairs={{2,0},{4,2},{6,4},{3,1},{5,3},{7,5},{10,8},{12,10},{14,12},{11,9},... | collective-permute-start | bytes 393224 | tf_op jit(solution)/shard_map/ppermute | solution.py:435
  19.4 12.3 %collective-permute-start.13 = (f32[2,128]{1,0:T(2,128)S(1)}, f32[2,128]{1,0:T(2,128)S(1)}, u32[]{:S(2)}, u32[]{:S(2)}) collective-permute-start(f32[2,128]{1,0:T(2,128)S(1)} %pad_maximum_fusion.1), channel_id=1, source_target_pairs={{0,1},{1,0},{2,3},{3,2},{4,5},{5,4},{6,7},{7,6},{8,9},{9,8},{10,11... | collective-permute-start | bytes 3080 | tf_op jit(solution)/shard_map/ppermute | solution.py:466
  24.8 6.9 %collective-permute-start.3 = (bf16[1,2,128,256]{3,2,1,0:T(8,128)(2,1)S(1)}, bf16[1,2,128,256]{3,2,1,0:T(8,128)(2,1)S(1)}, u32[]{:S(2)}, u32[]{:S(2)}) collective-permute-start(bf16[1,2,128,256]{3,2,1,0:T(8,128)(2,1)S(1)} %collective-permute-done.1.refs_0_.above), channel_id=1, source_target_pairs={{0,8},{8,16},{16,24},{1,9},{9,17},{17,25},{2,10},{10,18},{18,26},{... | collective-permute-start | bytes 393224 | tf_op jit(solution)/shard_map/ppermute | solution.py:435
  27.5 6.7 %collective-permute-start.4 = (bf16[1,2,128,256]{3,2,1,0:T(8,128)(2,1)S(1)}, bf16[1,2,128,256]{3,2,1,0:T(8,128)(2,1)S(1)}, u32[]{:S(2)}, u32[]{:S(2)}) collective-permute-start(bf16[1,2,128,256]{3,2,1,0:T(8,128)(2,1)S(1)} %collective-permute-done.2.refs_1_.below), channel_id=1, source_target_pairs={{0,8},{8,16},{16,24},{1,9},{9,17},{17,25},{2,10},{10,18},{18,26},{... | collective-permute-start | bytes 393224 | tf_op jit(solution)/shard_map/ppermute | solution.py:435
  52.9 7.9 %collective-permute-start.24 = (f32[2,128]{1,0:T(2,128)S(1)}, f32[2,128]{1,0:T(2,128)S(1)}, u32[]{:S(2)}, u32[]{:S(2)}) collective-permute-start(f32[2,128]{1,0:T(2,128)S(1)} %pad_maximum_fusion.3), channel_id=1, source_target_pairs={{0,2},{2,0},{4,6},{6,4},{1,3},{3,1},{5,7},{7,5},{8,10},{10,8},{12,... | collective-permute-start | bytes 3080 | tf_op jit(solution)/shard_map/ppermute | solution.py:466
  54.8 7.2 %collective-permute-start.25 = (f32[2,128]{1,0:T(2,128)S(1)}, f32[2,128]{1,0:T(2,128)S(1)}, u32[]{:S(2)}, u32[]{:S(2)}) collective-permute-start(f32[2,128]{1,0:T(2,128)S(1)} %pad_maximum_fusion.3), channel_id=1, source_target_pairs={{0,4},{2,6},{4,0},{6,2},{1,5},{3,7},{5,1},{7,3},{8,12},{10,14},{12... | collective-permute-start | bytes 3080 | tf_op jit(solution)/shard_map/ppermute | solution.py:466
  55.3 6.7 %collective-permute-start.26 = (f32[2,128]{1,0:T(2,128)S(1)}, f32[2,128]{1,0:T(2,128)S(1)}, u32[]{:S(2)}, u32[]{:S(2)}) collective-permute-start(f32[2,128]{1,0:T(2,128)S(1)} %pad_maximum_fusion.3), channel_id=1, source_target_pairs={{0,6},{2,4},{4,2},{6,0},{1,7},{3,5},{5,3},{7,1},{8,14},{10,12},{12... | collective-permute-start | bytes 3080 | tf_op jit(solution)/shard_map/ppermute | solution.py:466
  56.2 22.8 %collective-permute-start.14 = (bf16[4,2,128,256]{3,2,1,0:T(8,128)(2,1)S(1)}, bf16[4,2,128,256]{3,2,1,0:T(8,128)(2,1)S(1)}, u32[]{:S(2)}, u32[]{:S(2)}) collective-permute-start(bf16[4,2,128,256]{3,2,1,0:T(8,128)(2,1)S(1)} %shard_map.117.refs_0_.cotangent), channel_id=1, source_target_pairs={{8,0},{16,8},{24,16},{9,1},{17,9},{25,17},{10,2},{18,10},{26,18},{... | collective-permute-start | bytes 1572872 | tf_op jit(solution)/shard_map/ppermute | solution.py:435
  57.5 8.0 %collective-permute-start.15 = (bf16[1,2,128,256]{3,2,1,0:T(8,128)(2,1)S(1)}, bf16[1,2,128,256]{3,2,1,0:T(8,128)(2,1)S(1)}, u32[]{:S(2)}, u32[]{:S(2)}) collective-permute-start(bf16[1,2,128,256]{3,2,1,0:T(8,128)(2,1)S(1)} %get-tuple-element.38), channel_id=1, source_target_pairs={{0,2},{2,4},{4,6},{1,3},{3,5},{5,7},{8,10},{10,12},{12,14},{9,11},... | collective-permute-start | bytes 393224 | tf_op jit(solution)/shard_map/ppermute | solution.py:435
  60.7 6.2 %collective-permute-start.16 = (bf16[1,2,128,256]{3,2,1,0:T(8,128)(2,1)S(1)}, bf16[1,2,128,256]{3,2,1,0:T(8,128)(2,1)S(1)}, u32[]{:S(2)}, u32[]{:S(2)}) collective-permute-start(bf16[1,2,128,256]{3,2,1,0:T(8,128)(2,1)S(1)} %get-tuple-element.37), channel_id=1, source_target_pairs={{2,0},{4,2},{6,4},{3,1},{5,3},{7,5},{10,8},{12,10},{14,12},{11,9},... | collective-permute-start | bytes 393224 | tf_op jit(solution)/shard_map/ppermute | solution.py:435
  62.1 6.3 %collective-permute-start.27 = (f32[2,128]{1,0:T(2,128)S(1)}, f32[2,128]{1,0:T(2,128)S(1)}, u32[]{:S(2)}, u32[]{:S(2)}) collective-permute-start(f32[2,128]{1,0:T(2,128)S(1)} %pad_maximum_fusion.4), channel_id=1, source_target_pairs={{0,1},{1,0},{2,3},{3,2},{4,5},{5,4},{6,7},{7,6},{8,9},{9,8},{10,11... | collective-permute-start | bytes 3080 | tf_op jit(solution)/shard_map/ppermute | solution.py:466
  65.5 8.4 %collective-permute-start.17 = (bf16[1,2,128,256]{3,2,1,0:T(8,128)(2,1)S(1)}, bf16[1,2,128,256]{3,2,1,0:T(8,128)(2,1)S(1)}, u32[]{:S(2)}, u32[]{:S(2)}) collective-permute-start(bf16[1,2,128,256]{3,2,1,0:T(8,128)(2,1)S(1)} %collective-permute-done.15.refs_0_.refs_2_), channel_id=1, source_target_pairs={{8,0},{16,8},{24,16},{9,1},{17,9},{25,17},{10,2},{18,10},{26,18},{... | collective-permute-start | bytes 393224 | tf_op jit(solution)/shard_map/ppermute | solution.py:435
  67.0 9.0 %collective-permute-start.18 = (bf16[1,2,128,256]{3,2,1,0:T(8,128)(2,1)S(1)}, bf16[1,2,128,256]{3,2,1,0:T(8,128)(2,1)S(1)}, u32[]{:S(2)}, u32[]{:S(2)}) collective-permute-start(bf16[1,2,128,256]{3,2,1,0:T(8,128)(2,1)S(1)} %collective-permute-done.16.refs_1_.refs_3_), channel_id=1, source_target_pairs={{8,0},{16,8},{24,16},{9,1},{17,9},{25,17},{10,2},{18,10},{26,18},{... | collective-permute-start | bytes 393224 | tf_op jit(solution)/shard_map/ppermute | solution.py:435
  100.1 9.8 %collective-permute-start.34 = (f32[2,128]{1,0:T(2,128)S(1)}, f32[2,128]{1,0:T(2,128)S(1)}, u32[]{:S(2)}, u32[]{:S(2)}) collective-permute-start(f32[2,128]{1,0:T(2,128)S(1)} %add_add_fusion), channel_id=1, source_target_pairs={{0,1},{1,0},{2,3},{3,2},{4,5},{5,4},{6,7},{7,6},{8,9},{9,8},{10,11... | collective-permute-start | bytes 3080 | tf_op jit(solution)/shard_map/ppermute | solution.py:450
  109.8 15.6 %collective-permute-start.44 = (f32[64,32,128]{2,1,0:T(8,128)S(1)}, f32[64,32,128]{2,1,0:T(8,128)S(1)}, u32[]{:S(2)}, u32[]{:S(2)}) collective-permute-start(f32[64,32,128]{2,1,0:T(8,128)S(1)} %bitcast.30), channel_id=1, source_target_pairs={{0,1},{1,0},{2,3},{3,2},{4,5},{5,4},{6,7},{7,6},{8,9},{9,8},{10,11... | collective-permute-start | bytes 3145736 | tf_op jit(solution)/shard_map/ppermute | solution.py:480
  124.1 6.6 %collective-permute-start.42 = (f32[64,32,128]{2,1,0:T(8,128)}, f32[64,32,128]{2,1,0:T(8,128)}, u32[]{:S(2)}, u32[]{:S(2)}) collective-permute-start(f32[64,32,128]{2,1,0:T(8,128)} %bitcast.9), channel_id=1, source_target_pairs={{0,1},{1,0},{2,3},{3,2},{4,5},{5,4},{6,7},{7,6},{8,9},{9,8},{10,11... | collective-permute-start | bytes 3145736 | tf_op jit(solution)/shard_map/ppermute | solution.py:480
  126.5 13.2 %all-to-all-start.5 = ((s16[64,32,128]{2,1,0:T(8,128)(2,1)}), s16[64,32,128]{2,1,0:T(8,128)(2,1)S(1)}, u32[]{:S(2)}, u32[]{:S(2)}) async-start(s16[64,32,128]{2,1,0:T(8,128)(2,1)} %shard_map.135), calls=%async_computation.5 | async-start | bytes 1048576 | tf_op jit(solution)/shard_map/all_to_all | solution.py:484
  139.7 11.0 %all-to-all-start.1 = ((s16[64,32,128]{2,1,0:T(8,128)(2,1)}), s16[64,32,128]{2,1,0:T(8,128)(2,1)S(1)}, u32[]{:S(2)}, u32[]{:S(2)}) async-start(s16[64,32,128]{2,1,0:T(8,128)(2,1)} %shard_map.130), calls=%async_computation.1 | async-start | bytes 1048576 | tf_op jit(solution)/shard_map/all_to_all | solution.py:484
  150.8 8.2 %all-to-all-start.6 = ((s16[16,32,128]{2,1,0:T(8,128)(2,1)}), s16[16,32,128]{2,1,0:T(8,128)(2,1)S(1)}, u32[]{:S(2)}, u32[]{:S(2)}) async-start(s16[16,32,128]{2,1,0:T(8,128)(2,1)} %shard_map.136), calls=%async_computation.6 | async-start | bytes 262144 | tf_op jit(solution)/shard_map/all_to_all | solution.py:484
  159.0 8.1 %all-to-all-start.2 = ((s16[16,32,128]{2,1,0:T(8,128)(2,1)}), s16[16,32,128]{2,1,0:T(8,128)(2,1)S(1)}, u32[]{:S(2)}, u32[]{:S(2)}) async-start(s16[16,32,128]{2,1,0:T(8,128)(2,1)} %shard_map.131), calls=%async_computation.2 | async-start | bytes 262144 | tf_op jit(solution)/shard_map/all_to_all | solution.py:484
  167.0 8.1 %all-to-all-start.7 = ((s16[4,4,32,128]{3,2,1,0:T(8,128)(2,1)}), s16[4,4,32,128]{3,2,1,0:T(8,128)(2,1)S(1)}, u32[]{:S(2)}, u32[]{:S(2)}) async-start(s16[4,4,32,128]{3,2,1,0:T(8,128)(2,1)} %shard_map.137), calls=%async_computation.7 | async-start | bytes 262144 | tf_op jit(solution)/shard_map/all_to_all | solution.py:484
  191.7 13.8 %all-to-all-start.4 = ((s16[4,16,32,128]{3,2,1,0:T(8,128)(2,1)}), s16[4,16,32,128]{3,2,1,0:T(8,128)(2,1)S(1)}, u32[]{:S(2)}, u32[]{:S(2)}) async-start(s16[4,16,32,128]{3,2,1,0:T(8,128)(2,1)} %broadcast_in_dim.26), calls=%async_computation.4 | async-start | bytes 1048576 | tf_op jit(solution)/shard_map/all_to_all | solution.py:484
  195.2 27.3 %collective-permute-start.35 = (bf16[4,2,128,256]{3,2,1,0:T(8,128)(2,1)S(1)}, bf16[4,2,128,256]{3,2,1,0:T(8,128)(2,1)}, u32[]{:S(2)}, u32[]{:S(2)}) collective-permute-start(bf16[4,2,128,256]{3,2,1,0:T(8,128)(2,1)S(1)} %shard_map.123.refs_0_.grad_ref), channel_id=1, source_target_pairs={{8,0},{16,8},{24,16},{9,1},{17,9},{25,17},{10,2},{18,10},{26,18},{... | collective-permute-start | bytes 1572872 | tf_op jit(solution)/shard_map/ppermute | solution.py:435
  196.5 14.2 %collective-permute-start.37 = (bf16[1,2,128,256]{3,2,1,0:T(8,128)(2,1)}, bf16[1,2,128,256]{3,2,1,0:T(8,128)(2,1)}, u32[]{:S(2)}, u32[]{:S(2)}) collective-permute-start(bf16[1,2,128,256]{3,2,1,0:T(8,128)(2,1)} %get-tuple-element.35), channel_id=1, source_target_pairs={{2,0},{4,2},{6,4},{3,1},{5,3},{7,5},{10,8},{12,10},{14,12},{11,9},... | collective-permute-start | bytes 393224 | tf_op jit(solution)/shard_map/ppermute | solution.py:435
  197.8 47.8 %collective-permute-start.45 = (s16[64,32,128]{2,1,0:T(8,128)(2,1)S(1)}, s16[64,32,128]{2,1,0:T(8,128)(2,1)}, u32[]{:S(2)}, u32[]{:S(2)}) collective-permute-start(s16[64,32,128]{2,1,0:T(8,128)(2,1)S(1)} %bitcast.24), channel_id=1, source_target_pairs={{0,1},{1,0},{2,3},{3,2},{4,5},{5,4},{6,7},{7,6},{8,9},{9,8},{10,11... | collective-permute-start | bytes 1572872 | tf_op jit(solution)/shard_map/ppermute | solution.py:480
  205.5 44.5 %collective-permute-start.43 = (s16[64,32,128]{2,1,0:T(8,128)(2,1)S(1)}, s16[64,32,128]{2,1,0:T(8,128)(2,1)}, u32[]{:S(2)}, u32[]{:S(2)}) collective-permute-start(s16[64,32,128]{2,1,0:T(8,128)(2,1)S(1)} %bitcast.22), channel_id=1, source_target_pairs={{0,1},{1,0},{2,3},{3,2},{4,5},{5,4},{6,7},{7,6},{8,9},{9,8},{10,11... | collective-permute-start | bytes 1572872 | tf_op jit(solution)/shard_map/ppermute | solution.py:480
  209.4 7.2 %collective-permute-start.38 = (bf16[1,2,128,256]{3,2,1,0:T(8,128)(2,1)}, bf16[1,2,128,256]{3,2,1,0:T(8,128)(2,1)S(1)}, u32[]{:S(2)}, u32[]{:S(2)}) collective-permute-start(bf16[1,2,128,256]{3,2,1,0:T(8,128)(2,1)} %copy-done.7), channel_id=1, source_target_pairs={{8,0},{16,8},{24,16},{9,1},{17,9},{25,17},{10,2},{18,10},{26,18},{... | collective-permute-start | bytes 393224 | tf_op jit(solution)/shard_map/ppermute | solution.py:435
  210.7 8.7 %collective-permute-start.39 = (bf16[1,2,128,256]{3,2,1,0:T(8,128)(2,1)}, bf16[1,2,128,256]{3,2,1,0:T(8,128)(2,1)S(1)}, u32[]{:S(2)}, u32[]{:S(2)}) collective-permute-start(bf16[1,2,128,256]{3,2,1,0:T(8,128)(2,1)} %collective-permute-done.37.refs_1_.refs_3_), channel_id=1, source_target_pairs={{8,0},{16,8},{24,16},{9,1},{17,9},{25,17},{10,2},{18,10},{26,18},{... | collective-permute-start | bytes 393224 | tf_op jit(solution)/shard_map/ppermute | solution.py:435
  (30 other events, 160.7 us)

commit v4 on v3

--- a/solution.py
+++ b/solution.py
@@ -76,7 +76,19 @@
         off = plane() - mean
         part = lanes_of(off * off)
         acc = part if acc is None else acc + part
-    return as_rows(mean, group_sums(acc))
+    return mean, group_sums(acc)
+
+
+def put_rows(out_ref, first, second):
+    out_ref[...] = jnp.broadcast_to(as_rows(first, second)[None], out_ref.shape)
+
+
+def combined(st_ref, count):
+    devices = st_ref.shape[0]
+    mean = jnp.mean(st_ref[:, 0:1], axis=0)
+    off = st_ref[:, 0:1] - mean[None]
+    squares = jnp.sum(st_ref[:, 1:2] + off * off * (count / devices), axis=0)
+    return mean, squares / count
 
 
 def columns_of(*rows):
@@ -90,12 +102,12 @@
 
 
 def planes_kernel(natural_ref, *refs):
-    out_ref = refs[-1] if len(refs) == 2 else refs[-2]
+    out_ref = refs[-1] if len(refs) == 1 else refs[-2]
     _, frames, rows, cols = natural_ref.shape
     for row in range(rows):
         for frame in range(frames):
             out_ref[row, frame] = natural_ref[:, frame, row, :]
-    if len(refs) == 2:
+    if len(refs) == 1:
         return
     scale = columns_of(refs[0][0:1])[0]
     planes = [
@@ -103,7 +115,7 @@
         for r in range(rows)
         for t in range(frames)
     ]
-    refs[-1][...] = local_stats(planes, float(GROUP * rows * frames * cols))
+    put_rows(refs[-1], *local_stats(planes, float(GROUP * rows * frames * cols)))
 
 
 def source(own, other, near, far, other_first):
@@ -165,16 +177,15 @@
 
 def norm_columns(par_ref, st_ref, count, gain_row):
     par = par_ref[...]
-    stats = st_ref[...]
-    mean = stats[0:1]
-    inverse = 1.0 / jnp.sqrt(stats[1:2] / count + epsilon)
+    mean, variance = combined(st_ref, count)
+    inverse = 1.0 / jnp.sqrt(variance + epsilon)
     gain = par[gain_row : gain_row + 1]
     shift = par[gain_row + 1 : gain_row + 2]
     return columns_of(mean, inverse, gain, shift, par[0:1])[:5]
 
 
 def conv_first_kernel(
-    flag_ref, own, past, above, below, far_above, far_below, edge_ref, rim_ref, par_ref, st_ref, weight, hidden_ref, st_out, stack_ref,
+    flag_ref, own, past, above, below, far_above, far_below, edge_ref, rim_ref, par_ref, st_ref, weight, after, hidden_ref, st_out, stack_ref,
     *, count
 ):
     rows, frames, channels, cols = own.shape
@@ -213,7 +224,7 @@
     planes = [
         functools.partial(lambda r, t: hidden_ref[r, t], r, t) for r in range(rows) for t in range(frames)
     ]
-    st_out[...] = local_stats(planes, float(GROUP * rows * frames * cols))
+    put_rows(st_out, *local_stats(planes, float(GROUP * rows * frames * cols)))
 
 
 def fill_future(stack, flag_ref, own, future, above, below, far_above, far_below, edge_ref, rim_ref):
@@ -254,13 +265,13 @@
             scaled_ref[row, frame] = scaled
             first = first + lanes_of(scaled)
             second = second + lanes_of(scaled * normed)
-    sums_ref[...] = as_rows(group_sums(first), group_sums(second))
+    put_rows(sums_ref, group_sums(first), group_sums(second))
 
 
 def hidden_grad_kernel(hidden, scaled, par_ref, st_ref, sums_ref, out_ref, *, count):
     rows, frames, channels, cols = hidden.shape
     mean, inverse, _, _, _ = norm_columns(par_ref, st_ref, count, 3)
-    means = sums_ref[...] / count
+    means = jnp.sum(sums_ref[...], axis=0) / count
     first, second = columns_of(means[0:1], means[1:2])[:2]
     for row in range(rows):
         for frame in range(frames):
@@ -291,23 +302,44 @@
     return number * (jnp.exp(number[:, SLOTS - 1 : SLOTS] * LN2) * (1.0 / FULL))
 
 
-def first_scatter_kernel(mine_ref, other_ref, out_ref):
-    out_ref[...] = encoded(mine_ref[...] + other_ref[...])
-
-
-def scatter_kernel(received, out_ref, *, copies):
-    total = decoded_value(received[0])
-    for number in range(1, received.shape[0]):
-        total = total + decoded_value(received[number])
-    total = encoded(total)
-    if copies:
-        for number in range(copies):
-            out_ref[number] = total
-    else:
-        out_ref[...] = total
-
-
-def join_kernel(flag_ref, mine_ref, theirs_ref, after, out_ref, first_ref, second_ref):
+def first_scatter_kernel(*refs):
+    out_ref = refs[-1]
+    chunks, _, rows = out_ref.shape[:3]
+    for which in range(2):
+        mine_ref, other_ref = refs[2 * which], refs[2 * which + 1]
+        for chunk in range(chunks):
+            here = slice(chunk * rows, (chunk + 1) * rows)
+            out_ref[chunk, which] = encoded(mine_ref[here] + other_ref[here])
+
+
+def second_scatter_kernel(received, after, out_ref):
+    chunks, _, rows = out_ref.shape[:3]
+    for which in range(2):
+        for chunk in range(chunks):
+            here = slice(chunk * rows, (chunk + 1) * rows)
+            total = decoded_value(received[0, which, here])
+            for number in range(1, received.shape[0]):
+                total = total + decoded_value(received[number, which, here])
+            out_ref[chunk, which] = encoded(total)
+
+
+def total_kernel(received, out_ref):
+    for which in range(2):
+        total = decoded_value(received[0, which])
+        for number in range(1, received.shape[0]):
+            total = total + decoded_value(received[number, which])
+        total = encoded(total)
+        for copy in range(out_ref.shape[0]):
+            out_ref[copy, which] = total
+
+
+def copies_kernel(value, after, *outs):
+    for which, out_ref in enumerate(outs):
+        for copy in range(out_ref.shape[0]):
+            out_ref[copy] = value[:, which]
+
+
+def join_kernel(flag_ref, mine_ref, theirs_ref, out_ref, first_ref, second_ref):
     half, _, channels = mine_ref.shape
     is_first = flag_ref[3] == 0
     first_ref[...] = decoded_value(jnp.where(is_first, mine_ref[...], theirs_ref[...])).reshape(first_ref.shape)
@@ -318,7 +350,7 @@
         out_ref[half:, here] = second_ref[pl.ds(tap, half, stride=SLOTS), :]
 
 
-def weight_second_kernel(flag_ref, stack_ref, act_ref, after, mine_ref, theirs_ref, right_ref):
+def weight_second_kernel(flag_ref, stack_ref, act_ref, after, after_too, mine_ref, theirs_ref, right_ref):
     rows, frames, channels, cols = act_ref.shape
     for row in range(rows):
         right_ref[row * cols : (row + 1) * cols] = jnp.transpose(
@@ -358,10 +390,10 @@
 
 
 def first_grad_kernel(flag_ref, *refs, count):
-    weight, latent, par_ref, st_ref, scaled_ref, sums_ref, stack_ref = refs[-7:]
+    weight, latent, par_ref, st_ref, _, scaled_ref, sums_ref, stack_ref = refs[-8:]
     rows, frames, channels, cols = latent.shape
     mean, inverse, gain, shift, scale = norm_columns(par_ref, st_ref, count, 1)
-    fill_future(stack_ref, flag_ref, *refs[:-7])
+    fill_future(stack_ref, flag_ref, *refs[:-8])
     first = jnp.zeros((channels, 128), F32)
     second = jnp.zeros((channels, 128), F32)
     for row in range(rows):
@@ -375,13 +407,13 @@
             scaled_ref[row, frame] = scaled
             first = first + lanes_of(scaled)
             second = second + lanes_of(scaled * normed)
-    sums_ref[...] = as_rows(group_sums(first), group_sums(second))
-
-
-def decoded_grad_kernel(scaled, latent, cotangent, par_ref, st_ref, sums_ref, out_ref, *, count):
+    put_rows(sums_ref, group_sums(first), group_sums(second))
+
+
+def decoded_grad_kernel(scaled, latent, cotangent, par_ref, st_ref, sums_ref, after, out_ref, *, count):
     rows, frames, channels, cols = latent.shape
     mean, inverse, _, _, scale = norm_columns(par_ref, st_ref, count, 1)
-    means = sums_ref[...] / count
+    means = jnp.sum(sums_ref[...], axis=0) / count
     first, second = columns_of(means[0:1], means[1:2])[:2]
     for row in range(rows):
         for frame in range(frames):
@@ -435,84 +467,64 @@
     return lax.ppermute(value, axis, [(source, source + steps) for source in range(initial, last)])
 
 
-def rounds():
-    for axis in ("tm", "height", "width"):
-        count = lax.axis_size(axis)
-        step = 1
-        while step < count:
-            wide = 4 if 4 * step <= count else 2
-            yield axis, step, [[(i, i ^ (step * k)) for i in range(count)] for k in range(1, wide)]
-            step *= wide
-
-
-def all_sum(value):
-    for axis, _, exchanges in rounds():
-        parts = [value] + [lax.ppermute(value, axis, pairs) for pairs in exchanges]
-        while len(parts) > 1:
-            parts = [a + b for a, b in zip(parts[::2], parts[1::2])]
-        (value,) = parts
-    return value
-
-
-def exchanged_sum(value):
-    axes = ("tm", "height", "width")
-    devices = lax.axis_size(axes)
-    value = jnp.broadcast_to(value[None], (devices, *value.shape))
-    return jnp.sum(lax.all_to_all(value, axes, 0, 0, tiled=True), axis=0)
-
-
-def all_stats(value, count):
-    for axis, _, exchanges in rounds():
-        parts = [value] + [lax.ppermute(value, axis, pairs) for pairs in exchanges]
-        while len(parts) > 1:
-            joined = []
-            for a, b in zip(parts[::2], parts[1::2]):
-                gap = a[0:1] - b[0:1]
-                mean = 0.5 * (a[0:1] + b[0:1])
-                joined.append(jnp.concatenate([mean, a[1:2] + b[1:2] + gap * gap * (0.5 * count)], axis=0))
-            parts = joined
-            count = 2.0 * count
-        (value,) = parts
-    return value
+def exchanged(value, axis):
+    return lax.all_to_all(value, axis, 0, 0, tiled=True)
+
+
+def shared(value):
+    return exchanged(value, ("tm", "height", "width"))
 
 
 def swapped(value):
     return lax.ppermute(value, "width", [(0, 1), (1, 0)])
 
 
-def exchanged(value, axis):
-    return lax.all_to_all(value, axis, 0, 0, tiled=True)
-
-
-def reduce_weights(flags, mine, theirs, after):
+def scattered(second, first, after):
+    half, _, channels = second[0].shape
+    by_height = lax.axis_size("height")
+    terms = [part for mine, theirs in (second, first) for part in (mine, swapped(theirs))]
+    (value,) = call(
+        first_scatter_kernel,
+        [shape((by_height, 2, half // by_height, SLOTS, channels), jnp.int16)],
+        [VMEM] * 4 + [ANY] * len(after),
+        (*terms, *after),
+    )
+    return exchanged(value, "height"), value
+
+
+def summed(value, after):
+    by_tm = lax.axis_size("tm")
+    _, _, rows, _, channels = value.shape
+    (value,) = call(
+        second_scatter_kernel,
+        [shape((by_tm, 2, rows // by_tm, SLOTS, channels), jnp.int16)],
+        [VMEM, ANY],
+        (value, after),
+    )
+    return exchanged(value, "tm"), value
+
+
+def gathered(value, after_last):
+    (value,) = call(total_kernel, [shape(value.shape, jnp.int16)], [VMEM], (value,))
+    value = exchanged(value, "tm")
+    by_height = lax.axis_size("height")
+    by_tm, _, rows, _, channels = value.shape
+    copies = call(
+        copies_kernel,
+        [shape((by_height, by_tm, rows, SLOTS, channels), jnp.int16)] * 2,
+        [VMEM, ANY],
+        (value, after_last),
+    )
+    return [exchanged(copy, "height").reshape(-1, SLOTS, channels) for copy in copies]
+
+
+def joined(flags, mine, theirs):
     half, _, channels = mine.shape
-    by_height, by_tm = lax.axis_size("height"), lax.axis_size("tm")
-    coded = functools.partial(lambda *dims: shape((*dims, SLOTS, channels), jnp.int16))
-    (value,) = call(first_scatter_kernel, [coded(half)], [VMEM] * 2, (mine, swapped(theirs)))
-    value = exchanged(value, "height")
-    rows = half // by_height
-    (value,) = call(
-        functools.partial(scatter_kernel, copies=0),
-        [coded(rows)],
-        [VMEM],
-        (value.reshape(by_height, rows, SLOTS, channels),),
-    )
-    value = exchanged(value, "tm")
-    rows = rows // by_tm
-    (value,) = call(
-        functools.partial(scatter_kernel, copies=by_tm),
-        [coded(by_tm, rows)],
-        [VMEM],
-        (value.reshape(by_tm, rows, SLOTS, channels),),
-    )
-    value = exchanged(value, "tm").reshape(1, by_tm * rows, SLOTS, channels)
-    value = exchanged(jnp.broadcast_to(value, (by_height, *value.shape[1:])), "height")
-    value = value.reshape(half, SLOTS, channels)
     (total,) = call(
         join_kernel,
         [shape((2 * half, TAPS * channels), F32)],
-        [SMEM] + [VMEM] * 2 + [ANY],
-        (flags, value, swapped(value), after),
+        [SMEM] + [VMEM] * 2,
+        (flags, mine, theirs),
         scratch=[pltpu.VMEM((half * SLOTS, channels), F32)] * 2,
     )
     return total
@@ -553,8 +565,7 @@
     channels, frames, rows, cols = latent.shape
     groups = exponents.shape[0]
     devices = lax.axis_size("tm") * lax.axis_size("height") * lax.axis_size("width")
-    here = channels // groups * frames * rows * cols
-    count = float(here * devices)
+    count = float(channels // groups * frames * rows * cols * devices)
     tm, height, width = (lax.axis_index(axis) for axis in ("tm", "height", "width"))
     flags = jnp.stack(
         [
@@ -572,15 +583,15 @@
     taps = (2 * channels, 36 * channels)
     halves = [shape((channels // 2 * SLOTS, channels), F32)] * 2
     conv_flops = 2 * 4 * 256 * 36 * channels * 2 * channels
-    small = shape((2, channels), F32)
+    small = shape((devices, 2, channels), F32)
 
     latent, stats_first = call(
         planes_kernel, [shape(block, BF16), small], [VMEM] * 2, (latent, par)
     )
     around = extended(flags, latent, 1)
-    (cotangent,) = call(planes_kernel, [shape(block, BF16)], [VMEM, ANY], (cotangent, around[0]))
+    (cotangent,) = call(planes_kernel, [shape(block, BF16)], [VMEM], (cotangent,))
     around_c = extended(flags, cotangent, -1)
-    stats_first = all_stats(stats_first, float(here))
+    stats_first = shared(stats_first)
     (weight_first,) = call(weight_forward_kernel, [shape(taps, BF16)], [VMEM], (conv_first,))
     (weight_second_t,) = call(weight_back_kernel, [shape(taps, BF16)], [VMEM], (conv_second,))
     (weight_first_t,) = call(weight_back_kernel, [shape(taps, BF16)], [VMEM], (conv_first,))
@@ -588,12 +599,12 @@
     hidden, stats_second, stack_first = call(
         functools.partial(conv_first_kernel, count=count),
         [shape(block, F32), small, shape(stack, BF16)],
-        [SMEM] + [VMEM] * 11,
-        (flags, latent, *around, par, stats_first, weight_first),
+        [SMEM] + [VMEM] * 11 + [ANY],
+        (flags, latent, *around, par, stats_first, weight_first, around_c[0]),
         flops=conv_flops,
         transcendentals=3 * latent.size,
     )
-    stats_second = all_stats(stats_second, float(here))
+    stats_second = shared(stats_second)
     grad_second, stack_c = call(
         conv_back_kernel,
         [shape(block, F32), shape(stack, BF16)],
@@ -608,15 +619,7 @@
         (hidden, grad_second, par, stats_second),
         transcendentals=latent.size,
     )
-    sums = all_sum(sums)
-    halves_second = call(
-        weight_second_kernel,
-        halves,
-        [SMEM] + [VMEM] * 2 + [ANY],
-        (flags, stack_c, act_second, act_second),
-        scratch=[pltpu.VMEM((rows * cols, frames * channels), BF16)],
-        flops=conv_flops,
-    )
+    sums = shared(sums)
     (hidden_grad,) = call(
         functools.partial(hidden_grad_kernel, count=count),
         [shape(block, BF16)],
@@ -624,35 +627,46 @@
         (hidden, scaled, par, stats_second, sums),
     )
     around = extended(flags, hidden_grad, -1)
+    halves_second = call(
+        weight_second_kernel,
+        halves,
+        [SMEM] + [VMEM] * 2 + [ANY] * 2,
+        (flags, stack_c, act_second, around[1], around[2]),
+        scratch=[pltpu.VMEM((rows * cols, frames * channels), BF16)],
+        flops=conv_flops,
+    )
     halves_first = call(
         weight_first_kernel,
         halves,
         [SMEM] + [VMEM] * 2 + [ANY],
-        (flags, stack_first, hidden_grad, around[1]),
+        (flags, stack_first, hidden_grad, around[0]),
         scratch=[pltpu.VMEM((rows * cols, frames * channels), BF16)],
         flops=conv_flops,
     )
+    halves_second, halves_first = (
+        [v.reshape(channels // 2, SLOTS, channels) for v in halves] for halves in (halves_second, halves_first)
+    )
+    weights, sent = scattered(halves_second, halves_first, (around[3], around[4]))
     scaled, sums_first = call(
         functools.partial(first_grad_kernel, count=count),
         [shape(block, F32), small],
-        [SMEM] + [VMEM] * 12,
-        (flags, hidden_grad, *around, weight_first_t, latent, par, stats_first),
+        [SMEM] + [VMEM] * 12 + [ANY],
+        (flags, hidden_grad, *around, weight_first_t, latent, par, stats_first, sent),
         scratch=[pltpu.VMEM(stack, BF16)],
         flops=conv_flops,
         transcendentals=latent.size,
     )
-    sums_first = exchanged_sum(sums_first)
-    halves_second, halves_first = (
-        [v.reshape(channels // 2, SLOTS, channels) for v in halves] for halves in (halves_second, halves_first)
-    )
-    conv_second_grad = reduce_weights(flags, *halves_second, sums_first)
-    conv_first_grad = reduce_weights(flags, *halves_first, sums_first)
+    weights, sent = summed(weights, sums_first)
+    sums_first = shared(sums_first)
     (decoded_grad,) = call(
         functools.partial(decoded_grad_kernel, count=count),
         [shape((channels, frames, rows, cols), F32)],
-        [VMEM] * 6,
-        (scaled, latent, cotangent, par, stats_first, sums_first),
-    )
+        [VMEM] * 6 + [ANY],
+        (scaled, latent, cotangent, par, stats_first, sums_first, sent),
+    )
+    second, first = gathered(weights, decoded_grad)
+    conv_second_grad = joined(flags, second, swapped(second))
+    conv_first_grad = joined(flags, first, swapped(first))
     return decoded_grad, conv_first_grad, conv_second_grad
 
 

time: 256 us -> 229 us (0.89)
  waiting for transfers between devices: 55.9 us -> 27.3 us
  starting transfers between devices: 102 us -> 77.6 us
  local copies, waits for them, and re-layouts: 7.92 us -> 29.3 us
  blocking collectives: 26.7 us -> 31.2 us
    ppermute x21 -> x0, starting transfers between devices: 32.8 us -> none  [the longest x14 21.9 us: all_stats(): parts = [value] + [lax.ppermute(value, axis, pairs) for pairs in exchanges]]
    unnamed x20 -> x88, local copies, waits for them, and re-layouts: 5.34 us -> 28.3 us
    all_to_all x2 -> x3, blocking collectives: 15.7 us -> 31.2 us  [exchanged(): return lax.all_to_all(value, axis, 0, 0, tiled=True)]
    all_to_all x6, waiting for transfers between devices: 25.7 us -> 13.5 us  [exchanged(): return lax.all_to_all(value, axis, 0, 0, tiled=True)]
    all_to_all x6, starting transfers between devices: 21.2 us -> 33.2 us  [exchanged(): return lax.all_to_all(value, axis, 0, 0, tiled=True)]
    all_to_all x1 -> x0, blocking collectives: 11 us -> none  [exchanged_sum(): return jnp.sum(lax.all_to_all(value, axes, 0, 0, tiled=True), axis=0)]
    ppermute x21 -> x0, waiting for transfers between devices: 7.09 us -> none  [the longest x7 4.39 us: all_sum(): parts = [value] + [lax.ppermute(value, axis, pairs) for pairs in exchanges]]
    ppermute x15, waiting for transfers between devices: 20 us -> 13.8 us  [shifted(): lax.ppermute(value, axis, [(source, source + steps) for source in range(i...]
  transfers between devices with their start and end apart: 52 -> 31, of which waited for: 22 -> 7; matrix products, arithmetic and copies ran while one was open for 0% -> 0% of each run, Pallas kernels for 16% -> 22%
where the time goes in v4:
time: 229 us; the launch traced here: 227 us
  starting transfers between devices  77.6 us (34%)
  Pallas kernels  60 us (26%)
  blocking collectives  31.2 us (14%)
  local copies, waits for them, and re-layouts  29.3 us (13%)
  waiting for transfers between devices  27.3 us (12%)
    pallas_call x25, Pallas kernels, call(): pl.pallas_call(body, out_shape=tuple(outs), in_specs=specs, out_specs=tup...  60 us
    all_to_all x6, starting transfers between devices, exchanged(): return lax.all_to_all(value, axis, 0, 0, tiled=True)  33.2 us
    ppermute x15, starting transfers between devices, shifted(): lax.ppermute(value, axis, [(source, source + steps) for source in range(i...  32.7 us
    all_to_all x3, blocking collectives, exchanged(): return lax.all_to_all(value, axis, 0, 0, tiled=True)  31.2 us
    unnamed x88, local copies, waits for them, and re-layouts  28.3 us
    ppermute x15, waiting for transfers between devices, shifted(): lax.ppermute(value, axis, [(source, source + steps) for source in range(i...  13.8 us
    all_to_all x6, waiting for transfers between devices, exchanged(): return lax.all_to_all(value, axis, 0, 0, tiled=True)  13.5 us
    ppermute x10, starting transfers between devices, swapped(): return lax.ppermute(value, 'width', [(0, 1), (1, 0)])  11.7 us
  transfers between devices with their start and end apart: 31, of which 7 were waited for; matrix products, arithmetic and copies ran while one was open for 0% of the time, Pallas kernels for 22%

profile of v4, /device:TPU:1, one launch (start us, length us, event | category | flops | bytes accessed | tf_op | source)
XLA Modules:
  0.0 227.4 jit_solution(16808085421089870690)
XLA Ops:
  5.3 4.8 %collective-permute-start = (bf16[4,2,128,256]{3,2,1,0:T(8,128)(2,1)S(1)}, bf16[4,2,128,256]{3,2,1,0:T(8,128)(2,1)}, u32[]{:S(2)}, u32[]{:S(2)}) collective-permute-start(bf16[4,2,128,256]{3,2,1,0:T(8,128)(2,1)S(1)} %get-tuple-element.21.refs_0_.own.refs_9_.latent), channel_id=1, source_target_pairs={{0,8},{8,16},{16,24},{1,9},{9,17},{17,25},{2,10},{10,18},{18,26},{... | collective-permute-start | bytes 1572872 | tf_op jit(solution)/shard_map/ppermute | solution.py:467
  10.2 3.1 %collective-permute-start.1 = (bf16[1,2,128,256]{3,2,1,0:T(8,128)(2,1)S(1)}, bf16[1,2,128,256]{3,2,1,0:T(8,128)(2,1)S(1)}, u32[]{:S(2)}, u32[]{:S(2)}) collective-permute-start(bf16[1,2,128,256]{3,2,1,0:T(8,128)(2,1)S(1)} %get-tuple-element.44), channel_id=1, source_target_pairs={{0,2},{2,4},{4,6},{1,3},{3,5},{5,7},{8,10},{10,12},{12,14},{9,11},... | collective-permute-start | bytes 393224 | tf_op jit(solution)/shard_map/ppermute | solution.py:467
  17.8 4.0 %collective-permute-start.8 = (bf16[1,2,128,256]{3,2,1,0:T(8,128)(2,1)S(1)}, bf16[1,2,128,256]{3,2,1,0:T(8,128)(2,1)S(1)}, u32[]{:S(2)}, u32[]{:S(2)}) collective-permute-start(bf16[1,2,128,256]{3,2,1,0:T(8,128)(2,1)S(1)} %get-tuple-element.42), channel_id=1, source_target_pairs={{0,2},{2,4},{4,6},{1,3},{3,5},{5,7},{8,10},{10,12},{12,14},{9,11},... | collective-permute-start | bytes 393224 | tf_op jit(solution)/shard_map/ppermute | solution.py:467
  23.1 4.0 %collective-permute-start.3 = (bf16[1,2,128,256]{3,2,1,0:T(8,128)(2,1)S(1)}, bf16[1,2,128,256]{3,2,1,0:T(8,128)(2,1)S(1)}, u32[]{:S(2)}, u32[]{:S(2)}) collective-permute-start(bf16[1,2,128,256]{3,2,1,0:T(8,128)(2,1)S(1)} %collective-permute-done.1.refs_0_.above), channel_id=1, source_target_pairs={{0,8},{8,16},{16,24},{1,9},{9,17},{17,25},{2,10},{10,18},{18,26},{... | collective-permute-start | bytes 393224 | tf_op jit(solution)/shard_map/ppermute | solution.py:467
  27.8 3.0 %collective-permute-start.4 = (bf16[1,2,128,256]{3,2,1,0:T(8,128)(2,1)}, bf16[1,2,128,256]{3,2,1,0:T(8,128)(2,1)}, u32[]{:S(2)}, u32[]{:S(2)}) collective-permute-start(bf16[1,2,128,256]{3,2,1,0:T(8,128)(2,1)} %collective-permute-done.2.refs_1_.below), channel_id=1, source_target_pairs={{0,8},{8,16},{16,24},{1,9},{9,17},{17,25},{2,10},{10,18},{18,26},{... | collective-permute-start | bytes 393224 | tf_op jit(solution)/shard_map/ppermute | solution.py:467
  30.8 8.0 %all-to-all-start = ((f32[32,2,128]{2,1,0:T(2,128)}), f32[32,2,128]{2,1,0:T(2,128)S(1)}, u32[]{:S(2)}, u32[]{:S(2)}) async-start(f32[32,2,128]{2,1,0:T(2,128)} %get-tuple-element.22), calls=%async_computation | async-start | bytes 65536 | tf_op jit(solution)/shard_map/all_to_all | solution.py:471
  45.7 2.6 %shard_map.113 = bf16[128,128]{1,0:T(8,128)(2,1)} custom-call(s32[4]{0:T(128)S(1)} %pad_add_fusion.flag_ref, bf16[4,2,128,256]{3,2,1,0:T(8,128)(2,1)S(1)} %get-tuple-element.21.refs_0_.own.refs_9_.latent, bf16[4,2,128,256]{3,2,1,0:T(8,128)(2,1)} %collective-permute-done.refs_1_.past), custom_call_target="tpu_custom_call" | custom-call | bytes 1081360 | tf_op jit(solution)/shard_map/pallas_call | solution.py:25
  52.0 2.0 shard_map.119
  54.3 2.1 shard_map.118
  60.1 7.2 %shard_map.117 = (f32[4,2,128,256]{3,2,1,0:T(8,128)S(1)}, f32[32,2,128]{2,1,0:T(2,128)S(1)}, bf16[6,4,384,256]{3,2,1,0:T(8,128)(2,1)}) custom-call(s32[4]{0:T(128)S(1)} %pad_add_fusion.flag_ref, bf16[4,2,128,256]{3,2,1,0:T(8,128)(2,1)S(1)} %get-tuple-element.21.refs_0_.own.refs_9_.latent, bf16[4,2,128,256]{3,2,1,0:T(8,128)(2,1)} %collective-permute-done.refs_1_.past, ...), custom_call_target="tpu_custom_call" | custom-call | flops 2415919104 | bytes 10358800 | tf_op jit(solution)/shard_map/pallas_call | solution.py:25
  67.9 8.1 %all-to-all-start.1 = ((f32[32,2,128]{2,1,0:T(2,128)}), f32[32,2,128]{2,1,0:T(2,128)S(1)}, u32[]{:S(2)}, u32[]{:S(2)}) async-start(f32[32,2,128]{2,1,0:T(2,128)} %copy-done.43), calls=%async_computation.1 | async-start | bytes 65536 | tf_op jit(solution)/shard_map/all_to_all | solution.py:471
  80.4 5.7 %shard_map.121 = (f32[4,2,128,256]{3,2,1,0:T(8,128)S(1)}, bf16[6,4,384,256]{3,2,1,0:T(8,128)(2,1)}) custom-call(s32[4]{0:T(128)S(1)} %pad_add_fusion.flag_ref, bf16[4,2,128,256]{3,2,1,0:T(8,128)(2,1)S(1)} %shard_map.116.refs_0_.cotangent, bf16[4,2,128,256]{3,2,1,0:T(8,128)(2,1)S(1)} %collective-permute-done.7.after.refs_1_, ...), custom_call_target="tpu_custom_call" | custom-call | flops 2415919104 | bytes 9764880 | tf_op jit(solution)/shard_map/pallas_call | solution.py:25
  89.4 12.8 %all_to_all.45.sums_ref = f32[32,2,128]{2,1,0:T(2,128)S(1)} all-to-all(f32[32,2,128]{2,1,0:T(2,128)S(1)} %get-tuple-element.27), channel_id=1, replica_groups=mesh['tm'=4,'height'=4,'width'=2] {'tm','height','width'}, dimensions={0} | all-to-all | bytes 65536 | tf_op jit(solution)/shard_map/all_to_all | solution.py:471
  104.0 2.1 collective-permute-start.15
  108.6 5.0 %collective-permute-done.16.refs_1_.after_too.refs_3_ = bf16[1,2,128,256]{3,2,1,0:T(8,128)(2,1)S(1)} collective-permute-done((bf16[1,2,128,256]{3,2,1,0:T(8,128)(2,1)S(1)}, bf16[1,2,128,256]{3,2,1,0:T(8,128)(2,1)S(1)}, u32[]{:S(2)}, u32[]{:S(2)}) %collective-permute-start.16) | collective-permute-done | bytes 131104 | tf_op jit(solution)/shard_map/ppermute | solution.py:467
  113.6 5.9 %shard_map.127 = (f32[2048,128]{1,0:T(8,128)S(1)}, f32[2048,128]{1,0:T(8,128)S(1)}) custom-call(s32[4]{0:T(128)S(1)} %pad_add_fusion.flag_ref, bf16[6,4,384,256]{3,2,1,0:T(8,128)(2,1)} %get-tuple-element.28.stack_ref, bf16[4,2,128,256]{3,2,1,0:T(8,128)(2,1)S(1)} %get-tuple-element.29.act_ref, ...), custom_call_target="tpu_custom_call" | custom-call | flops 2415919104 | bytes 7602192 | tf_op jit(solution)/shard_map/pallas_call | solution.py:25
  120.6 6.1 %shard_map.128 = (f32[2048,128]{1,0:T(8,128)S(1)}, f32[2048,128]{1,0:T(8,128)S(1)}) custom-call(s32[4]{0:T(128)S(1)} %pad_add_fusion.flag_ref, bf16[6,4,384,256]{3,2,1,0:T(8,128)(2,1)} %get-tuple-element.32.stack_ref, bf16[4,2,128,256]{3,2,1,0:T(8,128)(2,1)S(1)} %shard_map.123.refs_0_.grad_ref, bf16[4,2,128,256]{3,2,1,0:T(8,128)(2,1)S(1)} %collective-permute-done.14.refs_1_.after), custom_call_target="tpu_custom_call" | custom-call | flops 2415919104 | bytes 7864336 | tf_op jit(solution)/shard_map/pallas_call | solution.py:25
  129.4 4.8 %collective-permute-done.17.refs_2_.refs_4_ = bf16[1,2,128,256]{3,2,1,0:T(8,128)(2,1)S(1)} collective-permute-done((bf16[1,2,128,256]{3,2,1,0:T(8,128)(2,1)S(1)}, bf16[1,2,128,256]{3,2,1,0:T(8,128)(2,1)S(1)}, u32[]{:S(2)}, u32[]{:S(2)}) %collective-permute-start.17) | collective-permute-done | bytes 131104 | tf_op jit(solution)/shard_map/ppermute | solution.py:467
  134.2 2.8 %collective-permute-done.18.refs_3_.refs_5_ = bf16[1,2,128,256]{3,2,1,0:T(8,128)(2,1)S(1)} collective-permute-done((bf16[1,2,128,256]{3,2,1,0:T(8,128)(2,1)S(1)}, bf16[1,2,128,256]{3,2,1,0:T(8,128)(2,1)S(1)}, u32[]{:S(2)}, u32[]{:S(2)}) %collective-permute-start.18) | collective-permute-done | bytes 131104 | tf_op jit(solution)/shard_map/ppermute | solution.py:467
  140.0 3.7 %all-to-all-start.4 = ((s16[4,2,16,32,128]{4,3,2,1,0:T(8,128)(2,1)}), s16[4,2,16,32,128]{4,3,2,1,0:T(8,128)(2,1)S(1)}, u32[]{:S(2)}, u32[]{:S(2)}) async-start(s16[4,2,16,32,128]{4,3,2,1,0:T(8,128)(2,1)} %shard_map.129.refs_12_), calls=%async_computation.4 | async-start | bytes 2097152 | tf_op jit(solution)/shard_map/all_to_all | solution.py:471
  153.8 5.8 %shard_map.130 = (f32[4,2,128,256]{3,2,1,0:T(8,128)S(1)}, f32[32,2,128]{2,1,0:T(2,128)}) custom-call(s32[4]{0:T(128)S(1)} %pad_add_fusion.flag_ref, bf16[4,2,128,256]{3,2,1,0:T(8,128)(2,1)S(1)} %shard_map.123.refs_0_.grad_ref, bf16[4,2,128,256]{3,2,1,0:T(8,128)(2,1)S(1)} %copy-done.22, bf16[1,2,128,256]{3,2,1,0:T(8,128)(2,1)S(1)} %copy-done.35, ...), custom_call_target="tpu_custom_call" | custom-call | flops 2415919104 | bytes 6688784 | tf_op jit(solution)/shard_map/pallas_call | solution.py:25
  161.1 10.0 %all_to_all.46.received = s16[4,2,4,32,128]{4,3,2,1,0:T(8,128)(2,1)S(1)} all-to-all(s16[4,2,4,32,128]{4,3,2,1,0:T(8,128)(2,1)S(1)} %shard_map.131.after), channel_id=1, replica_groups=mesh['tm'=4,'height'=4,'width'=2] {'tm'}, dimensions={0} | all-to-all | bytes 524288 | tf_op jit(solution)/shard_map/all_to_all | solution.py:471
  171.1 6.5 %all-to-all-start.3 = ((f32[32,2,128]{2,1,0:T(2,128)}), f32[32,2,128]{2,1,0:T(2,128)S(1)}, u32[]{:S(2)}, u32[]{:S(2)}) async-start(f32[32,2,128]{2,1,0:T(2,128)} %get-tuple-element.36.after), calls=%async_computation.3 | async-start | bytes 65536 | tf_op jit(solution)/shard_map/all_to_all | solution.py:471
  178.4 6.2 %all-to-all-done.3.sums_ref = f32[32,2,128]{2,1,0:T(2,128)S(1)} async-done(((f32[32,2,128]{2,1,0:T(2,128)}), f32[32,2,128]{2,1,0:T(2,128)S(1)}, u32[]{:S(2)}, u32[]{:S(2)}) %all-to-all-start.3) | async-done | bytes 32800 | tf_op jit(solution)/shard_map/all_to_all | solution.py:471
  184.6 3.4 %all-to-all-start.6 = ((s16[4,2,4,32,128]{4,3,2,1,0:T(8,128)(2,1)}), s16[4,2,4,32,128]{4,3,2,1,0:T(8,128)(2,1)S(1)}, u32[]{:S(2)}, u32[]{:S(2)}) async-start(s16[4,2,4,32,128]{4,3,2,1,0:T(8,128)(2,1)} %shard_map.133), calls=%async_computation.6 | async-start | bytes 524288 | tf_op jit(solution)/shard_map/all_to_all | solution.py:471
  190.0 5.4 %all-to-all-done.6.value = s16[4,2,4,32,128]{4,3,2,1,0:T(8,128)(2,1)S(1)} async-done(((s16[4,2,4,32,128]{4,3,2,1,0:T(8,128)(2,1)}), s16[4,2,4,32,128]{4,3,2,1,0:T(8,128)(2,1)S(1)}, u32[]{:S(2)}, u32[]{:S(2)}) %all-to-all-start.6) | async-done | bytes 262176 | tf_op jit(solution)/shard_map/all_to_all | solution.py:471
  197.6 8.4 %all_to_all.47 = s16[4,4,4,32,128]{4,3,2,1,0:T(8,128)(2,1)S(1)} all-to-all(s16[4,4,4,32,128]{4,3,2,1,0:T(8,128)(2,1)S(1)} %get-tuple-element.38), channel_id=1, replica_groups=mesh['tm'=4,'height'=4,'width'=2] {'height'}, dimensions={0} | all-to-all | bytes 1048576 | tf_op jit(solution)/shard_map/all_to_all | solution.py:471
  206.0 3.5 %all-to-all-start.7 = ((s16[4,4,4,32,128]{4,3,2,1,0:T(8,128)(2,1)}), s16[4,4,4,32,128]{4,3,2,1,0:T(8,128)(2,1)S(1)}, u32[]{:S(2)}, u32[]{:S(2)}) async-start(s16[4,4,4,32,128]{4,3,2,1,0:T(8,128)(2,1)} %get-tuple-element.37), calls=%async_computation.7 | async-start | bytes 1048576 | tf_op jit(solution)/shard_map/all_to_all | solution.py:471
  209.5 3.6 %collective-permute-start.24 = (s16[64,32,128]{2,1,0:T(8,128)(2,1)S(1)}, s16[64,32,128]{2,1,0:T(8,128)(2,1)S(1)}, u32[]{:S(2)}, u32[]{:S(2)}) collective-permute-start(s16[64,32,128]{2,1,0:T(8,128)(2,1)S(1)} %bitcast.16), channel_id=1, source_target_pairs={{0,1},{1,0},{2,3},{3,2},{4,5},{5,4},{6,7},{7,6},{8,9},{9,8},{10,11... | collective-permute-start | bytes 1572872 | tf_op jit(solution)/shard_map/ppermute | solution.py:479
  214.9 4.6 %collective-permute-start.23 = (s16[64,32,128]{2,1,0:T(8,128)(2,1)S(1)}, s16[64,32,128]{2,1,0:T(8,128)(2,1)S(1)}, u32[]{:S(2)}, u32[]{:S(2)}) collective-permute-start(s16[64,32,128]{2,1,0:T(8,128)(2,1)S(1)} %bitcast.14), channel_id=1, source_target_pairs={{0,1},{1,0},{2,3},{3,2},{4,5},{5,4},{6,7},{7,6},{8,9},{9,8},{10,11... | collective-permute-start | bytes 1572872 | tf_op jit(solution)/shard_map/ppermute | solution.py:479
  219.6 3.9 %shard_map.136 = f32[128,3456]{1,0:T(8,128)} custom-call(s32[4]{0:T(128)S(1)} %pad_add_fusion.flag_ref, s16[64,32,128]{2,1,0:T(8,128)(2,1)S(1)} %bitcast.17, s16[64,32,128]{2,1,0:T(8,128)(2,1)S(1)} %collective-permute-done.24.theirs_ref), custom_call_target="tpu_custom_call" | custom-call | bytes 2818064 | tf_op jit(solution)/shard_map/pallas_call | solution.py:25
  223.4 3.9 %shard_map.135 = f32[128,3456]{1,0:T(8,128)} custom-call(s32[4]{0:T(128)S(1)} %pad_add_fusion.flag_ref, s16[64,32,128]{2,1,0:T(8,128)(2,1)S(1)} %bitcast.15, s16[64,32,128]{2,1,0:T(8,128)(2,1)S(1)} %collective-permute-done.23.theirs_ref), custom_call_target="tpu_custom_call" | custom-call | bytes 2818064 | tf_op jit(solution)/shard_map/pallas_call | solution.py:25
  (156 shorter events, 63.0 us)
Async XLA Ops:
  0.6 48.0 %copy-start.1 = (bf16[128,3456]{1,0:T(8,128)(2,1)S(1)}, bf16[128,3456]{1,0:T(8,128)(2,1)}, u32[]{:S(2)}) copy-start(bf16[128,3456]{1,0:T(8,128)(2,1)} %weight.5) | copy-start | bytes 2654212
  5.3 40.4 %collective-permute-start = (bf16[4,2,128,256]{3,2,1,0:T(8,128)(2,1)S(1)}, bf16[4,2,128,256]{3,2,1,0:T(8,128)(2,1)}, u32[]{:S(2)}, u32[]{:S(2)}) collective-permute-start(bf16[4,2,128,256]{3,2,1,0:T(8,128)(2,1)S(1)} %get-tuple-element.21.refs_0_.own.refs_9_.latent), channel_id=1, source_target_pairs={{0,8},{8,16},{16,24},{1,9},{9,17},{17,25},{2,10},{10,18},{18,26},{... | collective-permute-start | bytes 1572872 | tf_op jit(solution)/shard_map/ppermute | solution.py:467
  10.2 11.6 %collective-permute-start.1 = (bf16[1,2,128,256]{3,2,1,0:T(8,128)(2,1)S(1)}, bf16[1,2,128,256]{3,2,1,0:T(8,128)(2,1)S(1)}, u32[]{:S(2)}, u32[]{:S(2)}) collective-permute-start(bf16[1,2,128,256]{3,2,1,0:T(8,128)(2,1)S(1)} %get-tuple-element.44), channel_id=1, source_target_pairs={{0,2},{2,4},{4,6},{1,3},{3,5},{5,7},{8,10},{10,12},{12,14},{9,11},... | collective-permute-start | bytes 393224 | tf_op jit(solution)/shard_map/ppermute | solution.py:467
  13.3 9.8 %collective-permute-start.2 = (bf16[1,2,128,256]{3,2,1,0:T(8,128)(2,1)S(1)}, bf16[1,2,128,256]{3,2,1,0:T(8,128)(2,1)}, u32[]{:S(2)}, u32[]{:S(2)}) collective-permute-start(bf16[1,2,128,256]{3,2,1,0:T(8,128)(2,1)S(1)} %get-tuple-element.43), channel_id=1, source_target_pairs={{2,0},{4,2},{6,4},{3,1},{5,3},{7,5},{10,8},{12,10},{14,12},{11,9},... | collective-permute-start | bytes 393224 | tf_op jit(solution)/shard_map/ppermute | solution.py:467
  16.5 37.8 %collective-permute-start.7 = (bf16[4,2,128,256]{3,2,1,0:T(8,128)(2,1)S(1)}, bf16[4,2,128,256]{3,2,1,0:T(8,128)(2,1)S(1)}, u32[]{:S(2)}, u32[]{:S(2)}) collective-permute-start(bf16[4,2,128,256]{3,2,1,0:T(8,128)(2,1)S(1)} %shard_map.116.refs_0_.cotangent), channel_id=1, source_target_pairs={{8,0},{16,8},{24,16},{9,1},{17,9},{25,17},{10,2},{18,10},{26,18},{... | collective-permute-start | bytes 1572872 | tf_op jit(solution)/shard_map/ppermute | solution.py:467
  17.8 10.0 %collective-permute-start.8 = (bf16[1,2,128,256]{3,2,1,0:T(8,128)(2,1)S(1)}, bf16[1,2,128,256]{3,2,1,0:T(8,128)(2,1)S(1)}, u32[]{:S(2)}, u32[]{:S(2)}) collective-permute-start(bf16[1,2,128,256]{3,2,1,0:T(8,128)(2,1)S(1)} %get-tuple-element.42), channel_id=1, source_target_pairs={{0,2},{2,4},{4,6},{1,3},{3,5},{5,7},{8,10},{10,12},{12,14},{9,11},... | collective-permute-start | bytes 393224 | tf_op jit(solution)/shard_map/ppermute | solution.py:467
  21.8 17.0 %collective-permute-start.9 = (bf16[1,2,128,256]{3,2,1,0:T(8,128)(2,1)S(1)}, bf16[1,2,128,256]{3,2,1,0:T(8,128)(2,1)}, u32[]{:S(2)}, u32[]{:S(2)}) collective-permute-start(bf16[1,2,128,256]{3,2,1,0:T(8,128)(2,1)S(1)} %get-tuple-element.41), channel_id=1, source_target_pairs={{2,0},{4,2},{6,4},{3,1},{5,3},{7,5},{10,8},{12,10},{14,12},{11,9},... | collective-permute-start | bytes 393224 | tf_op jit(solution)/shard_map/ppermute | solution.py:467
  23.1 17.0 %collective-permute-start.3 = (bf16[1,2,128,256]{3,2,1,0:T(8,128)(2,1)S(1)}, bf16[1,2,128,256]{3,2,1,0:T(8,128)(2,1)S(1)}, u32[]{:S(2)}, u32[]{:S(2)}) collective-permute-start(bf16[1,2,128,256]{3,2,1,0:T(8,128)(2,1)S(1)} %collective-permute-done.1.refs_0_.above), channel_id=1, source_target_pairs={{0,8},{8,16},{16,24},{1,9},{9,17},{17,25},{2,10},{10,18},{18,26},{... | collective-permute-start | bytes 393224 | tf_op jit(solution)/shard_map/ppermute | solution.py:467
  27.8 14.4 %collective-permute-start.4 = (bf16[1,2,128,256]{3,2,1,0:T(8,128)(2,1)}, bf16[1,2,128,256]{3,2,1,0:T(8,128)(2,1)}, u32[]{:S(2)}, u32[]{:S(2)}) collective-permute-start(bf16[1,2,128,256]{3,2,1,0:T(8,128)(2,1)} %collective-permute-done.2.refs_1_.below), channel_id=1, source_target_pairs={{0,8},{8,16},{16,24},{1,9},{9,17},{17,25},{2,10},{10,18},{18,26},{... | collective-permute-start | bytes 393224 | tf_op jit(solution)/shard_map/ppermute | solution.py:467
  30.8 25.8 %all-to-all-start = ((f32[32,2,128]{2,1,0:T(2,128)}), f32[32,2,128]{2,1,0:T(2,128)S(1)}, u32[]{:S(2)}, u32[]{:S(2)}) async-start(f32[32,2,128]{2,1,0:T(2,128)} %get-tuple-element.22), calls=%async_computation | async-start | bytes 65536 | tf_op jit(solution)/shard_map/all_to_all | solution.py:471
  38.8 13.2 %collective-permute-start.10 = (bf16[1,2,128,256]{3,2,1,0:T(8,128)(2,1)S(1)}, bf16[1,2,128,256]{3,2,1,0:T(8,128)(2,1)S(1)}, u32[]{:S(2)}, u32[]{:S(2)}) collective-permute-start(bf16[1,2,128,256]{3,2,1,0:T(8,128)(2,1)S(1)} %collective-permute-done.8.refs_0_.refs_2_), channel_id=1, source_target_pairs={{8,0},{16,8},{24,16},{9,1},{17,9},{25,17},{10,2},{18,10},{26,18},{... | collective-permute-start | bytes 393224 | tf_op jit(solution)/shard_map/ppermute | solution.py:467
  40.8 11.2 %collective-permute-start.11 = (bf16[1,2,128,256]{3,2,1,0:T(8,128)(2,1)}, bf16[1,2,128,256]{3,2,1,0:T(8,128)(2,1)S(1)}, u32[]{:S(2)}, u32[]{:S(2)}) collective-permute-start(bf16[1,2,128,256]{3,2,1,0:T(8,128)(2,1)} %collective-permute-done.9.refs_1_.refs_3_), channel_id=1, source_target_pairs={{8,0},{16,8},{24,16},{9,1},{17,9},{25,17},{10,2},{18,10},{26,18},{... | collective-permute-start | bytes 393224 | tf_op jit(solution)/shard_map/ppermute | solution.py:467
  45.4 11.2 %collective-permute-start.6 = (bf16[128,128]{1,0:T(8,128)(2,1)S(1)}, bf16[128,128]{1,0:T(8,128)(2,1)}, u32[]{:S(2)}, u32[]{:S(2)}) collective-permute-start(bf16[128,128]{1,0:T(8,128)(2,1)S(1)} %shard_map.114), channel_id=1, source_target_pairs={{0,1},{1,0},{2,3},{3,2},{4,5},{5,4},{6,7},{7,6},{8,9},{9,8},{10,11... | collective-permute-start | bytes 98312 | tf_op jit(solution)/shard_map/ppermute | solution.py:479
  48.4 8.3 %collective-permute-start.5 = (bf16[128,128]{1,0:T(8,128)(2,1)}, bf16[128,128]{1,0:T(8,128)(2,1)}, u32[]{:S(2)}, u32[]{:S(2)}) collective-permute-start(bf16[128,128]{1,0:T(8,128)(2,1)} %shard_map.113), channel_id=1, source_target_pairs={{0,1},{1,0},{2,3},{3,2},{4,5},{5,4},{6,7},{7,6},{8,9},{9,8},{10,11... | collective-permute-start | bytes 98312 | tf_op jit(solution)/shard_map/ppermute | solution.py:479
  54.0 22.0 %collective-permute-start.13 = (bf16[128,128]{1,0:T(8,128)(2,1)}, bf16[128,128]{1,0:T(8,128)(2,1)}, u32[]{:S(2)}, u32[]{:S(2)}) collective-permute-start(bf16[128,128]{1,0:T(8,128)(2,1)} %shard_map.119), channel_id=1, source_target_pairs={{0,1},{1,0},{2,3},{3,2},{4,5},{5,4},{6,7},{7,6},{8,9},{9,8},{10,11... | collective-permute-start | bytes 98312 | tf_op jit(solution)/shard_map/ppermute | solution.py:479
  56.4 19.6 %collective-permute-start.12 = (bf16[128,128]{1,0:T(8,128)(2,1)}, bf16[128,128]{1,0:T(8,128)(2,1)}, u32[]{:S(2)}, u32[]{:S(2)}) collective-permute-start(bf16[128,128]{1,0:T(8,128)(2,1)} %shard_map.118), channel_id=1, source_target_pairs={{0,1},{1,0},{2,3},{3,2},{4,5},{5,4},{6,7},{7,6},{8,9},{9,8},{10,11... | collective-permute-start | bytes 98312 | tf_op jit(solution)/shard_map/ppermute | solution.py:479
  67.9 19.2 %all-to-all-start.1 = ((f32[32,2,128]{2,1,0:T(2,128)}), f32[32,2,128]{2,1,0:T(2,128)S(1)}, u32[]{:S(2)}, u32[]{:S(2)}) async-start(f32[32,2,128]{2,1,0:T(2,128)} %copy-done.43), calls=%async_computation.1 | async-start | bytes 65536 | tf_op jit(solution)/shard_map/all_to_all | solution.py:471
  102.7 17.9 %collective-permute-start.14 = (bf16[4,2,128,256]{3,2,1,0:T(8,128)(2,1)S(1)}, bf16[4,2,128,256]{3,2,1,0:T(8,128)(2,1)S(1)}, u32[]{:S(2)}, u32[]{:S(2)}) collective-permute-start(bf16[4,2,128,256]{3,2,1,0:T(8,128)(2,1)S(1)} %shard_map.123.refs_0_.grad_ref), channel_id=1, source_target_pairs={{8,0},{16,8},{24,16},{9,1},{17,9},{25,17},{10,2},{18,10},{26,18},{... | collective-permute-start | bytes 1572872 | tf_op jit(solution)/shard_map/ppermute | solution.py:467
  104.0 4.6 %collective-permute-start.15 = (bf16[1,2,128,256]{3,2,1,0:T(8,128)(2,1)S(1)}, bf16[1,2,128,256]{3,2,1,0:T(8,128)(2,1)S(1)}, u32[]{:S(2)}, u32[]{:S(2)}) collective-permute-start(bf16[1,2,128,256]{3,2,1,0:T(8,128)(2,1)S(1)} %get-tuple-element.40), channel_id=1, source_target_pairs={{0,2},{2,4},{4,6},{1,3},{3,5},{5,7},{8,10},{10,12},{12,14},{9,11},... | collective-permute-start | bytes 393224 | tf_op jit(solution)/shard_map/ppermute | solution.py:467
  106.1 7.4 %collective-permute-start.16 = (bf16[1,2,128,256]{3,2,1,0:T(8,128)(2,1)S(1)}, bf16[1,2,128,256]{3,2,1,0:T(8,128)(2,1)S(1)}, u32[]{:S(2)}, u32[]{:S(2)}) collective-permute-start(bf16[1,2,128,256]{3,2,1,0:T(8,128)(2,1)S(1)} %get-tuple-element.39), channel_id=1, source_target_pairs={{2,0},{4,2},{6,4},{3,1},{5,3},{7,5},{10,8},{12,10},{14,12},{11,9},... | collective-permute-start | bytes 393224 | tf_op jit(solution)/shard_map/ppermute | solution.py:467
  119.5 17.5 %collective-permute-start.21 = (f32[64,32,128]{2,1,0:T(8,128)S(1)}, f32[64,32,128]{2,1,0:T(8,128)S(1)}, u32[]{:S(2)}, u32[]{:S(2)}) collective-permute-start(f32[64,32,128]{2,1,0:T(8,128)S(1)} %bitcast.20), channel_id=1, source_target_pairs={{0,1},{1,0},{2,3},{3,2},{4,5},{5,4},{6,7},{7,6},{8,9},{9,8},{10,11... | collective-permute-start | bytes 3145736 | tf_op jit(solution)/shard_map/ppermute | solution.py:479
  126.7 10.3 %collective-permute-start.22 = (f32[64,32,128]{2,1,0:T(8,128)S(1)}, f32[64,32,128]{2,1,0:T(8,128)S(1)}, u32[]{:S(2)}, u32[]{:S(2)}) collective-permute-start(f32[64,32,128]{2,1,0:T(8,128)S(1)} %bitcast.21), channel_id=1, source_target_pairs={{0,1},{1,0},{2,3},{3,2},{4,5},{5,4},{6,7},{7,6},{8,9},{9,8},{10,11... | collective-permute-start | bytes 3145736 | tf_op jit(solution)/shard_map/ppermute | solution.py:479
  126.8 7.4 %collective-permute-start.17 = (bf16[1,2,128,256]{3,2,1,0:T(8,128)(2,1)S(1)}, bf16[1,2,128,256]{3,2,1,0:T(8,128)(2,1)S(1)}, u32[]{:S(2)}, u32[]{:S(2)}) collective-permute-start(bf16[1,2,128,256]{3,2,1,0:T(8,128)(2,1)S(1)} %collective-permute-done.15.refs_0_.after.refs_2_), channel_id=1, source_target_pairs={{8,0},{16,8},{24,16},{9,1},{17,9},{25,17},{10,2},{18,10},{26,18},{... | collective-permute-start | bytes 393224 | tf_op jit(solution)/shard_map/ppermute | solution.py:467
  128.1 8.9 %collective-permute-start.18 = (bf16[1,2,128,256]{3,2,1,0:T(8,128)(2,1)S(1)}, bf16[1,2,128,256]{3,2,1,0:T(8,128)(2,1)S(1)}, u32[]{:S(2)}, u32[]{:S(2)}) collective-permute-start(bf16[1,2,128,256]{3,2,1,0:T(8,128)(2,1)S(1)} %collective-permute-done.16.refs_1_.after_too.refs_3_), channel_id=1, source_target_pairs={{8,0},{16,8},{24,16},{9,1},{17,9},{25,17},{10,2},{18,10},{26,18},{... | collective-permute-start | bytes 393224 | tf_op jit(solution)/shard_map/ppermute | solution.py:467
  140.0 20.6 %all-to-all-start.4 = ((s16[4,2,16,32,128]{4,3,2,1,0:T(8,128)(2,1)}), s16[4,2,16,32,128]{4,3,2,1,0:T(8,128)(2,1)S(1)}, u32[]{:S(2)}, u32[]{:S(2)}) async-start(s16[4,2,16,32,128]{4,3,2,1,0:T(8,128)(2,1)} %shard_map.129.refs_12_), calls=%async_computation.4 | async-start | bytes 2097152 | tf_op jit(solution)/shard_map/all_to_all | solution.py:471
  148.3 5.5 %collective-permute-start.20 = (bf16[128,128]{1,0:T(8,128)(2,1)S(1)}, bf16[128,128]{1,0:T(8,128)(2,1)S(1)}, u32[]{:S(2)}, u32[]{:S(2)}) collective-permute-start(bf16[128,128]{1,0:T(8,128)(2,1)S(1)} %shard_map.125), channel_id=1, source_target_pairs={{0,1},{1,0},{2,3},{3,2},{4,5},{5,4},{6,7},{7,6},{8,9},{9,8},{10,11... | collective-permute-start | bytes 98312 | tf_op jit(solution)/shard_map/ppermute | solution.py:479
  151.9 1.9 collective-permute-start.19
  171.1 13.6 %all-to-all-start.3 = ((f32[32,2,128]{2,1,0:T(2,128)}), f32[32,2,128]{2,1,0:T(2,128)S(1)}, u32[]{:S(2)}, u32[]{:S(2)}) async-start(f32[32,2,128]{2,1,0:T(2,128)} %get-tuple-element.36.after), calls=%async_computation.3 | async-start | bytes 65536 | tf_op jit(solution)/shard_map/all_to_all | solution.py:471
  184.6 10.8 %all-to-all-start.6 = ((s16[4,2,4,32,128]{4,3,2,1,0:T(8,128)(2,1)}), s16[4,2,4,32,128]{4,3,2,1,0:T(8,128)(2,1)S(1)}, u32[]{:S(2)}, u32[]{:S(2)}) async-start(s16[4,2,4,32,128]{4,3,2,1,0:T(8,128)(2,1)} %shard_map.133), calls=%async_computation.6 | async-start | bytes 524288 | tf_op jit(solution)/shard_map/all_to_all | solution.py:471
  206.0 8.9 %all-to-all-start.7 = ((s16[4,4,4,32,128]{4,3,2,1,0:T(8,128)(2,1)}), s16[4,4,4,32,128]{4,3,2,1,0:T(8,128)(2,1)S(1)}, u32[]{:S(2)}, u32[]{:S(2)}) async-start(s16[4,4,4,32,128]{4,3,2,1,0:T(8,128)(2,1)} %get-tuple-element.37), calls=%async_computation.7 | async-start | bytes 1048576 | tf_op jit(solution)/shard_map/all_to_all | solution.py:471
  209.5 10.1 %collective-permute-start.24 = (s16[64,32,128]{2,1,0:T(8,128)(2,1)S(1)}, s16[64,32,128]{2,1,0:T(8,128)(2,1)S(1)}, u32[]{:S(2)}, u32[]{:S(2)}) collective-permute-start(s16[64,32,128]{2,1,0:T(8,128)(2,1)S(1)} %bitcast.16), channel_id=1, source_target_pairs={{0,1},{1,0},{2,3},{3,2},{4,5},{5,4},{6,7},{7,6},{8,9},{9,8},{10,11... | collective-permute-start | bytes 1572872 | tf_op jit(solution)/shard_map/ppermute | solution.py:479
  214.9 8.5 %collective-permute-start.23 = (s16[64,32,128]{2,1,0:T(8,128)(2,1)S(1)}, s16[64,32,128]{2,1,0:T(8,128)(2,1)S(1)}, u32[]{:S(2)}, u32[]{:S(2)}) collective-permute-start(s16[64,32,128]{2,1,0:T(8,128)(2,1)S(1)} %bitcast.14), channel_id=1, source_target_pairs={{0,1},{1,0},{2,3},{3,2},{4,5},{5,4},{6,7},{7,6},{8,9},{9,8},{10,11... | collective-permute-start | bytes 1572872 | tf_op jit(solution)/shard_map/ppermute | solution.py:479
  (43 other events, 181.3 us)

commit v5 on v4

--- a/solution.py
+++ b/solution.py
@@ -16,7 +16,6 @@
 LN2 = 0.6931471805599453
 VMEM = pl.BlockSpec(memory_space=pltpu.VMEM)
 SMEM = pl.BlockSpec(memory_space=pltpu.SMEM)
-ANY = pl.BlockSpec(memory_space=pl.ANY)
 
 
 def call(body, outs, specs, args, scratch=(), flops=0, transcendentals=0, limit=48):
@@ -129,7 +128,7 @@
 
 
 def edges_kernel(flag_ref, *refs):
-    planes, out_ref = refs[:-1], refs[-1]
+    planes, out_ref = [ref for ref in refs[:-1] if len(ref.shape) == 4], refs[-1]
     is_first = flag_ref[3] == 0
     channels = planes[0].shape[2]
     lane = lax.broadcasted_iota(jnp.int32, (channels, 128), 1)
@@ -268,7 +267,7 @@
     put_rows(sums_ref, group_sums(first), group_sums(second))
 
 
-def hidden_grad_kernel(hidden, scaled, par_ref, st_ref, sums_ref, out_ref, *, count):
+def hidden_grad_kernel(hidden, scaled, par_ref, st_ref, sums_ref, after, out_ref, *, count):
     rows, frames, channels, cols = hidden.shape
     mean, inverse, _, _, _ = norm_columns(par_ref, st_ref, count, 3)
     means = jnp.sum(sums_ref[...], axis=0) / count
@@ -312,7 +311,8 @@
             out_ref[chunk, which] = encoded(mine_ref[here] + other_ref[here])
 
 
-def second_scatter_kernel(received, after, out_ref):
+def second_scatter_kernel(received, *refs):
+    out_ref = refs[-1]
     chunks, _, rows = out_ref.shape[:3]
     for which in range(2):
         for chunk in range(chunks):
@@ -323,7 +323,8 @@
             out_ref[chunk, which] = encoded(total)
 
 
-def total_kernel(received, out_ref):
+def total_kernel(received, *refs):
+    out_ref = refs[-1]
     for which in range(2):
         total = decoded_value(received[0, which])
         for number in range(1, received.shape[0]):
@@ -339,7 +340,7 @@
             out_ref[copy] = value[:, which]
 
 
-def join_kernel(flag_ref, mine_ref, theirs_ref, out_ref, first_ref, second_ref):
+def join_kernel(flag_ref, mine_ref, theirs_ref, after, out_ref, first_ref, second_ref):
     half, _, channels = mine_ref.shape
     is_first = flag_ref[3] == 0
     first_ref[...] = decoded_value(jnp.where(is_first, mine_ref[...], theirs_ref[...])).reshape(first_ref.shape)
@@ -350,7 +351,7 @@
         out_ref[half:, here] = second_ref[pl.ds(tap, half, stride=SLOTS), :]
 
 
-def weight_second_kernel(flag_ref, stack_ref, act_ref, after, after_too, mine_ref, theirs_ref, right_ref):
+def weight_second_kernel(flag_ref, stack_ref, act_ref, mine_ref, theirs_ref, right_ref):
     rows, frames, channels, cols = act_ref.shape
     for row in range(rows):
         right_ref[row * cols : (row + 1) * cols] = jnp.transpose(
@@ -369,7 +370,7 @@
                 put_halves(flag_ref, mine_ref, theirs_ref, tap, term[across * channels : (across + 1) * channels])
 
 
-def weight_first_kernel(flag_ref, stack_ref, grad_ref, after, mine_ref, theirs_ref, right_ref):
+def weight_first_kernel(flag_ref, stack_ref, grad_ref, mine_ref, theirs_ref, right_ref):
     rows, frames, channels, cols = grad_ref.shape
     for row in range(rows):
         right_ref[row * cols : (row + 1) * cols] = jnp.transpose(
@@ -390,10 +391,10 @@
 
 
 def first_grad_kernel(flag_ref, *refs, count):
-    weight, latent, par_ref, st_ref, _, scaled_ref, sums_ref, stack_ref = refs[-8:]
+    weight, latent, par_ref, st_ref, scaled_ref, sums_ref, stack_ref = refs[-7:]
     rows, frames, channels, cols = latent.shape
     mean, inverse, gain, shift, scale = norm_columns(par_ref, st_ref, count, 1)
-    fill_future(stack_ref, flag_ref, *refs[:-8])
+    fill_future(stack_ref, flag_ref, *refs[:-7])
     first = jnp.zeros((channels, 128), F32)
     second = jnp.zeros((channels, 128), F32)
     for row in range(rows):
@@ -410,7 +411,7 @@
     put_rows(sums_ref, group_sums(first), group_sums(second))
 
 
-def decoded_grad_kernel(scaled, latent, cotangent, par_ref, st_ref, sums_ref, after, out_ref, *, count):
+def decoded_grad_kernel(scaled, latent, cotangent, par_ref, st_ref, sums_ref, out_ref, *, count):
     rows, frames, channels, cols = latent.shape
     mean, inverse, _, _, scale = norm_columns(par_ref, st_ref, count, 1)
     means = jnp.sum(sums_ref[...], axis=0) / count
@@ -471,6 +472,35 @@
     return lax.all_to_all(value, axis, 0, 0, tiled=True)
 
 
+def all_stats(value, count):
+    value = value[0]
+    for axis in ("tm", "height", "width"):
+        size = lax.axis_size(axis)
+        step = 1
+        while step < size:
+            wide = 4 if 4 * step <= size else 2
+            parts = [value] + [
+                lax.ppermute(value, axis, [(i, i ^ (step * k)) for i in range(size)]) for k in range(1, wide)
+            ]
+            while len(parts) > 1:
+                joined = []
+                for a, b in zip(parts[::2], parts[1::2]):
+                    gap = a[0:1] - b[0:1]
+                    mean = 0.5 * (a[0:1] + b[0:1])
+                    joined.append(jnp.concatenate([mean, a[1:2] + b[1:2] + gap * gap * (0.5 * count)], axis=0))
+                parts = joined
+                count = 2.0 * count
+            (value,) = parts
+            step *= wide
+    return value[None]
+
+
+def token(value):
+    if value.ndim > 2:
+        value = value[(0,) * (value.ndim - 2)]
+    return value[:16, :128]
+
+
 def shared(value):
     return exchanged(value, ("tm", "height", "width"))
 
@@ -479,15 +509,15 @@
     return lax.ppermute(value, "width", [(0, 1), (1, 0)])
 
 
-def scattered(second, first, after):
+def scattered(second, first):
     half, _, channels = second[0].shape
     by_height = lax.axis_size("height")
     terms = [part for mine, theirs in (second, first) for part in (mine, swapped(theirs))]
     (value,) = call(
         first_scatter_kernel,
         [shape((by_height, 2, half // by_height, SLOTS, channels), jnp.int16)],
-        [VMEM] * 4 + [ANY] * len(after),
-        (*terms, *after),
+        [VMEM] * 4,
+        terms,
     )
     return exchanged(value, "height"), value
 
@@ -498,33 +528,33 @@
     (value,) = call(
         second_scatter_kernel,
         [shape((by_tm, 2, rows // by_tm, SLOTS, channels), jnp.int16)],
-        [VMEM, ANY],
-        (value, after),
-    )
-    return exchanged(value, "tm"), value
-
-
-def gathered(value, after_last):
-    (value,) = call(total_kernel, [shape(value.shape, jnp.int16)], [VMEM], (value,))
+        [VMEM] * (1 + len(after)),
+        (value, *map(token, after)),
+    )
+    return exchanged(value, "tm")
+
+
+def gathered(value, after, after_last):
+    (value,) = call(total_kernel, [shape(value.shape, jnp.int16)], [VMEM] * (1 + len(after)), (value, *map(token, after)))
     value = exchanged(value, "tm")
     by_height = lax.axis_size("height")
     by_tm, _, rows, _, channels = value.shape
     copies = call(
         copies_kernel,
         [shape((by_height, by_tm, rows, SLOTS, channels), jnp.int16)] * 2,
-        [VMEM, ANY],
-        (value, after_last),
+        [VMEM] * 2,
+        (value, token(after_last)),
     )
     return [exchanged(copy, "height").reshape(-1, SLOTS, channels) for copy in copies]
 
 
-def joined(flags, mine, theirs):
+def joined(flags, mine, theirs, after):
     half, _, channels = mine.shape
     (total,) = call(
         join_kernel,
         [shape((2 * half, TAPS * channels), F32)],
-        [SMEM] + [VMEM] * 2,
-        (flags, mine, theirs),
+        [SMEM] + [VMEM] * 3,
+        (flags, mine, theirs, token(after)),
         scratch=[pltpu.VMEM((half * SLOTS, channels), F32)] * 2,
     )
     return total
@@ -534,21 +564,24 @@
     return shifted(block[-1:], "height", 1), shifted(block[:1], "height", -1)
 
 
-def edges(flags, *planes):
+def edges(flags, planes, after):
     channels = planes[0].shape[2]
-    (columns,) = call(
-        edges_kernel, [shape((channels, 128), BF16)], [SMEM] + [VMEM] * len(planes), (flags, *planes)
-    )
+    args = (*planes, *map(token, after))
+    (columns,) = call(edges_kernel, [shape((channels, 128), BF16)], [SMEM] + [VMEM] * len(args), (flags, *args))
     return columns
 
 
-def extended(flags, own, steps):
+def halo(own, steps):
     other = shifted(own, "tm", steps)
     near = row_exchange(own)
     far = [shifted(row, "tm", steps) for row in near]
-    edge = swapped(edges(flags, own, other))
-    rim = swapped(edges(flags, *near, *far))
-    return other, *near, *far, edge, rim
+    return other, *near, *far
+
+
+def with_columns(flags, own, around, after=()):
+    edge = swapped(edges(flags, (own, around[0]), after))
+    rim = swapped(edges(flags, around[1:], after))
+    return *around, edge, rim
 
 
 def shards(
@@ -582,16 +615,16 @@
     stack = (rows + 2, 4, 3 * channels, cols)
     taps = (2 * channels, 36 * channels)
     halves = [shape((channels // 2 * SLOTS, channels), F32)] * 2
-    conv_flops = 2 * 4 * 256 * 36 * channels * 2 * channels
+    conv_flops = 3 * 2 * 4 * 256 * 36 * channels * 2 * channels
     small = shape((devices, 2, channels), F32)
 
     latent, stats_first = call(
         planes_kernel, [shape(block, BF16), small], [VMEM] * 2, (latent, par)
     )
-    around = extended(flags, latent, 1)
+    around = with_columns(flags, latent, halo(latent, 1))
     (cotangent,) = call(planes_kernel, [shape(block, BF16)], [VMEM], (cotangent,))
-    around_c = extended(flags, cotangent, -1)
-    stats_first = shared(stats_first)
+    around_c = with_columns(flags, cotangent, halo(cotangent, -1))
+    stats_first = all_stats(stats_first, count / devices)
     (weight_first,) = call(weight_forward_kernel, [shape(taps, BF16)], [VMEM], (conv_first,))
     (weight_second_t,) = call(weight_back_kernel, [shape(taps, BF16)], [VMEM], (conv_second,))
     (weight_first_t,) = call(weight_back_kernel, [shape(taps, BF16)], [VMEM], (conv_first,))
@@ -599,8 +632,8 @@
     hidden, stats_second, stack_first = call(
         functools.partial(conv_first_kernel, count=count),
         [shape(block, F32), small, shape(stack, BF16)],
-        [SMEM] + [VMEM] * 11 + [ANY],
-        (flags, latent, *around, par, stats_first, weight_first, around_c[0]),
+        [SMEM] + [VMEM] * 12,
+        (flags, latent, *around, par, stats_first, weight_first, token(around_c[0])),
         flops=conv_flops,
         transcendentals=3 * latent.size,
     )
@@ -620,53 +653,54 @@
         transcendentals=latent.size,
     )
     sums = shared(sums)
+    halves_second = call(
+        weight_second_kernel,
+        halves,
+        [SMEM] + [VMEM] * 2,
+        (flags, stack_c, act_second),
+        scratch=[pltpu.VMEM((rows * cols, frames * channels), BF16)],
+        flops=conv_flops,
+    )
     (hidden_grad,) = call(
         functools.partial(hidden_grad_kernel, count=count),
         [shape(block, BF16)],
-        [VMEM] * 5,
-        (hidden, scaled, par, stats_second, sums),
-    )
-    around = extended(flags, hidden_grad, -1)
-    halves_second = call(
-        weight_second_kernel,
-        halves,
-        [SMEM] + [VMEM] * 2 + [ANY] * 2,
-        (flags, stack_c, act_second, around[1], around[2]),
-        scratch=[pltpu.VMEM((rows * cols, frames * channels), BF16)],
-        flops=conv_flops,
-    )
+        [VMEM] * 6,
+        (hidden, scaled, par, stats_second, sums, token(halves_second[0])),
+    )
+    around = halo(hidden_grad, -1)
     halves_first = call(
         weight_first_kernel,
         halves,
-        [SMEM] + [VMEM] * 2 + [ANY],
-        (flags, stack_first, hidden_grad, around[0]),
+        [SMEM] + [VMEM] * 2,
+        (flags, stack_first, hidden_grad),
         scratch=[pltpu.VMEM((rows * cols, frames * channels), BF16)],
         flops=conv_flops,
     )
     halves_second, halves_first = (
         [v.reshape(channels // 2, SLOTS, channels) for v in halves] for halves in (halves_second, halves_first)
     )
-    weights, sent = scattered(halves_second, halves_first, (around[3], around[4]))
+    weights, sent = scattered(halves_second, halves_first)
+    around = with_columns(flags, hidden_grad, around, (sent,))
     scaled, sums_first = call(
         functools.partial(first_grad_kernel, count=count),
         [shape(block, F32), small],
-        [SMEM] + [VMEM] * 12 + [ANY],
-        (flags, hidden_grad, *around, weight_first_t, latent, par, stats_first, sent),
+        [SMEM] + [VMEM] * 12,
+        (flags, hidden_grad, *around, weight_first_t, latent, par, stats_first),
         scratch=[pltpu.VMEM(stack, BF16)],
         flops=conv_flops,
         transcendentals=latent.size,
     )
-    weights, sent = summed(weights, sums_first)
+    weights = summed(weights, around[:3])
+    second, first = gathered(weights, around[3:5], sums_first)
     sums_first = shared(sums_first)
     (decoded_grad,) = call(
         functools.partial(decoded_grad_kernel, count=count),
         [shape((channels, frames, rows, cols), F32)],
-        [VMEM] * 6 + [ANY],
-        (scaled, latent, cotangent, par, stats_first, sums_first, sent),
-    )
-    second, first = gathered(weights, decoded_grad)
-    conv_second_grad = joined(flags, second, swapped(second))
-    conv_first_grad = joined(flags, first, swapped(first))
+        [VMEM] * 6,
+        (scaled, latent, cotangent, par, stats_first, sums_first),
+    )
+    conv_second_grad = joined(flags, second, swapped(second), sums_first)
+    conv_first_grad = joined(flags, first, swapped(first), sums_first)
     return decoded_grad, conv_first_grad, conv_second_grad
 
 

time: 229 us -> 218 us (0.952)
  blocking collectives: 31.2 us -> 20 us
  waiting for transfers between devices: 27.3 us -> 19.1 us
  starting transfers between devices: 77.6 us -> 84.6 us
  Pallas kernels: 60 us -> 62.4 us
    all_to_all x3 -> x2, blocking collectives: 31.2 us -> 20 us  [exchanged(): return lax.all_to_all(value, axis, 0, 0, tiled=True)]
    ppermute x0 -> x7, starting transfers between devices: none -> 10.8 us  [all_stats(): lax.ppermute(value, axis, [(i, i ^ step * k) for i in range(size)])]
    unnamed x88 -> x58, local copies, waits for them, and re-layouts: 28.3 us -> 21.4 us
    all_to_all x6, starting transfers between devices: 33.2 us -> 27.5 us  [exchanged(): return lax.all_to_all(value, axis, 0, 0, tiled=True)]
    ppermute x15, waiting for transfers between devices: 13.8 us -> 8.8 us  [shifted(): lax.ppermute(value, axis, [(source, source + steps) for source in range(i...]
    all_to_all x6, waiting for transfers between devices: 13.5 us -> 9.03 us  [exchanged(): return lax.all_to_all(value, axis, 0, 0, tiled=True)]
    pallas_call x25, Pallas kernels: 60 us -> 62.4 us  [call(): pl.pallas_call(body, out_shape=tuple(outs), in_specs=specs, out_specs=tup...]
    squeeze x0 -> x9, local copies, waits for them, and re-layouts: none -> 2.36 us  [the longest x8 2.34 us: token(): value = value[(0,) * (value.ndim - 2)]]
  transfers between devices with their start and end apart: 31 -> 38, of which waited for: 7 -> 8; matrix products, arithmetic and copies ran while one was open for 0% -> 2% of each run, Pallas kernels for 22% -> 25%
where the time goes in v5:
time: 218 us; the launch traced here: 216 us
  starting transfers between devices  84.6 us (39%)
  Pallas kernels  62.4 us (29%)
  local copies, waits for them, and re-layouts  27.5 us (13%)
  blocking collectives  20 us (9%)
  waiting for transfers between devices  19.1 us (9%)
    pallas_call x25, Pallas kernels, call(): pl.pallas_call(body, out_shape=tuple(outs), in_specs=specs, out_specs=tup...  62.4 us
    ppermute x15, starting transfers between devices, shifted(): lax.ppermute(value, axis, [(source, source + steps) for source in range(i...  33 us
    all_to_all x6, starting transfers between devices, exchanged(): return lax.all_to_all(value, axis, 0, 0, tiled=True)  27.5 us
    unnamed x58, local copies, waits for them, and re-layouts  21.4 us
    all_to_all x2, blocking collectives, exchanged(): return lax.all_to_all(value, axis, 0, 0, tiled=True)  20 us
    ppermute x10, starting transfers between devices, swapped(): return lax.ppermute(value, 'width', [(0, 1), (1, 0)])  13.4 us
    ppermute x7, starting transfers between devices, all_stats(): lax.ppermute(value, axis, [(i, i ^ step * k) for i in range(size)])  10.8 us
    all_to_all x6, waiting for transfers between devices, exchanged(): return lax.all_to_all(value, axis, 0, 0, tiled=True)  9.03 us
  transfers between devices with their start and end apart: 38, of which 8 were waited for; matrix products, arithmetic and copies ran while one was open for 2% of the time, Pallas kernels for 25%

profile of v5, /device:TPU:1, one launch (start us, length us, event | category | flops | bytes accessed | tf_op | source)
XLA Modules:
  0.0 215.9 jit_solution(7999740683184655905)
XLA Ops:
  4.7 2.2 %collective-permute-start.7 = (f32[2,128]{1,0:T(2,128)S(1)}, f32[2,128]{1,0:T(2,128)S(1)}, u32[]{:S(2)}, u32[]{:S(2)}) collective-permute-start(f32[2,128]{1,0:T(2,128)S(1)} %slice_bitcast_fusion.9), channel_id=1, source_target_pairs={{0,8},{8,0},{16,24},{24,16},{1,9},{9,1},{17,25},{25,17},{2,10},{10... | collective-permute-start | bytes 3080 | tf_op jit(solution)/shard_map/ppermute | solution.py:483
  6.9 2.3 %collective-permute-start.8 = (f32[2,128]{1,0:T(2,128)S(1)}, f32[2,128]{1,0:T(2,128)S(1)}, u32[]{:S(2)}, u32[]{:S(2)}) collective-permute-start(f32[2,128]{1,0:T(2,128)S(1)} %slice_bitcast_fusion.9), channel_id=1, source_target_pairs={{0,16},{8,24},{16,0},{24,8},{1,17},{9,25},{17,1},{25,9},{2,18},{10... | collective-permute-start | bytes 3080 | tf_op jit(solution)/shard_map/ppermute | solution.py:483
  9.2 3.1 %collective-permute-start = (bf16[4,2,128,256]{3,2,1,0:T(8,128)(2,1)S(1)}, bf16[4,2,128,256]{3,2,1,0:T(8,128)(2,1)}, u32[]{:S(2)}, u32[]{:S(2)}) collective-permute-start(bf16[4,2,128,256]{3,2,1,0:T(8,128)(2,1)S(1)} %get-tuple-element.21.refs_0_.own.refs_9_.latent), channel_id=1, source_target_pairs={{0,8},{8,16},{16,24},{1,9},{9,17},{17,25},{2,10},{10,18},{18,26},{... | collective-permute-start | bytes 1572872 | tf_op jit(solution)/shard_map/ppermute | solution.py:468
  16.2 3.3 %collective-permute-start.1 = (bf16[1,2,128,256]{3,2,1,0:T(8,128)(2,1)S(1)}, bf16[1,2,128,256]{3,2,1,0:T(8,128)(2,1)S(1)}, u32[]{:S(2)}, u32[]{:S(2)}) collective-permute-start(bf16[1,2,128,256]{3,2,1,0:T(8,128)(2,1)S(1)} %get-tuple-element.44), channel_id=1, source_target_pairs={{0,2},{2,4},{4,6},{1,3},{3,5},{5,7},{8,10},{10,12},{12,14},{9,11},... | collective-permute-start | bytes 393224 | tf_op jit(solution)/shard_map/ppermute | solution.py:468
  24.0 3.6 %collective-permute-start.13 = (f32[2,128]{1,0:T(2,128)S(1)}, f32[2,128]{1,0:T(2,128)S(1)}, u32[]{:S(2)}, u32[]{:S(2)}) collective-permute-start(f32[2,128]{1,0:T(2,128)S(1)} %pad_maximum_fusion.1), channel_id=1, source_target_pairs={{0,1},{1,0},{2,3},{3,2},{4,5},{5,4},{6,7},{7,6},{8,9},{9,8},{10,11... | collective-permute-start | bytes 3080 | tf_op jit(solution)/shard_map/ppermute | solution.py:483
  28.4 4.9 %collective-permute-start.15 = (bf16[1,2,128,256]{3,2,1,0:T(8,128)(2,1)}, bf16[1,2,128,256]{3,2,1,0:T(8,128)(2,1)}, u32[]{:S(2)}, u32[]{:S(2)}) collective-permute-start(bf16[1,2,128,256]{3,2,1,0:T(8,128)(2,1)} %get-tuple-element.42), channel_id=1, source_target_pairs={{0,2},{2,4},{4,6},{1,3},{3,5},{5,7},{8,10},{10,12},{12,14},{9,11},... | collective-permute-start | bytes 393224 | tf_op jit(solution)/shard_map/ppermute | solution.py:468
  34.6 4.9 %collective-permute-start.3 = (bf16[1,2,128,256]{3,2,1,0:T(8,128)(2,1)S(1)}, bf16[1,2,128,256]{3,2,1,0:T(8,128)(2,1)}, u32[]{:S(2)}, u32[]{:S(2)}) collective-permute-start(bf16[1,2,128,256]{3,2,1,0:T(8,128)(2,1)S(1)} %collective-permute-done.1.refs_0_.above), channel_id=1, source_target_pairs={{0,8},{8,16},{16,24},{1,9},{9,17},{17,25},{2,10},{10,18},{18,26},{... | collective-permute-start | bytes 393224 | tf_op jit(solution)/shard_map/ppermute | solution.py:468
  49.2 3.3 %collective-permute-done.18.refs_3_.refs_5_ = bf16[1,2,128,256]{3,2,1,0:T(8,128)(2,1)S(1)} collective-permute-done((bf16[1,2,128,256]{3,2,1,0:T(8,128)(2,1)}, bf16[1,2,128,256]{3,2,1,0:T(8,128)(2,1)S(1)}, u32[]{:S(2)}, u32[]{:S(2)}) %collective-permute-start.18) | collective-permute-done | bytes 131104 | tf_op jit(solution)/shard_map/ppermute | solution.py:468
  52.5 2.0 shard_map.119
  55.8 2.0 shard_map.113
  57.9 2.1 shard_map.118
  60.6 7.2 %shard_map.117 = (f32[4,2,128,256]{3,2,1,0:T(8,128)S(1)}, f32[32,2,128]{2,1,0:T(2,128)S(1)}, bf16[6,4,384,256]{3,2,1,0:T(8,128)(2,1)}) custom-call(s32[4]{0:T(128)S(1)} %pad_add_fusion.flag_ref, bf16[4,2,128,256]{3,2,1,0:T(8,128)(2,1)S(1)} %get-tuple-element.21.refs_0_.own.refs_9_.latent, bf16[4,2,128,256]{3,2,1,0:T(8,128)(2,1)} %collective-permute-done.refs_1_.past, ...), custom_call_target="tpu_custom_call" | custom-call | flops 7247757312 | bytes 9806864 | tf_op jit(solution)/shard_map/pallas_call | solution.py:24
  68.4 6.0 %all-to-all-start = ((f32[32,2,128]{2,1,0:T(2,128)}), f32[32,2,128]{2,1,0:T(2,128)S(1)}, u32[]{:S(2)}, u32[]{:S(2)}) async-start(f32[32,2,128]{2,1,0:T(2,128)} %copy-done.24), calls=%async_computation | async-start | bytes 65536 | tf_op jit(solution)/shard_map/all_to_all | solution.py:472
  77.8 5.7 %shard_map.121 = (f32[4,2,128,256]{3,2,1,0:T(8,128)S(1)}, bf16[6,4,384,256]{3,2,1,0:T(8,128)(2,1)}) custom-call(s32[4]{0:T(128)S(1)} %pad_add_fusion.flag_ref, bf16[4,2,128,256]{3,2,1,0:T(8,128)(2,1)S(1)} %shard_map.116.refs_0_.cotangent, bf16[4,2,128,256]{3,2,1,0:T(8,128)(2,1)S(1)} %collective-permute-done.14.refs_1_, ...), custom_call_target="tpu_custom_call" | custom-call | flops 7247757312 | bytes 9764880 | tf_op jit(solution)/shard_map/pallas_call | solution.py:24
  89.2 5.8 %all-to-all-start.1 = ((f32[32,2,128]{2,1,0:T(2,128)}), f32[32,2,128]{2,1,0:T(2,128)S(1)}, u32[]{:S(2)}, u32[]{:S(2)}) async-start(f32[32,2,128]{2,1,0:T(2,128)} %get-tuple-element.27), calls=%async_computation.1 | async-start | bytes 65536 | tf_op jit(solution)/shard_map/all_to_all | solution.py:472
  96.1 7.4 %shard_map.123 = (f32[2048,128]{1,0:T(8,128)S(1)}, f32[2048,128]{1,0:T(8,128)}) custom-call(s32[4]{0:T(128)S(1)} %pad_add_fusion.flag_ref, bf16[6,4,384,256]{3,2,1,0:T(8,128)(2,1)} %get-tuple-element.28.stack_ref, bf16[4,2,128,256]{3,2,1,0:T(8,128)(2,1)S(1)} %copy-done.28), custom_call_target="tpu_custom_call" | custom-call | flops 7247757312 | bytes 7340048 | tf_op jit(solution)/shard_map/pallas_call | solution.py:24
  107.8 6.4 %shard_map.125 = (f32[2048,128]{1,0:T(8,128)S(1)}, f32[2048,128]{1,0:T(8,128)S(1)}) custom-call(s32[4]{0:T(128)S(1)} %pad_add_fusion.flag_ref, bf16[6,4,384,256]{3,2,1,0:T(8,128)(2,1)} %get-tuple-element.32.stack_ref, bf16[4,2,128,256]{3,2,1,0:T(8,128)(2,1)S(1)} %shard_map.124.grad_ref.refs_0_), custom_call_target="tpu_custom_call" | custom-call | flops 7247757312 | bytes 7340048 | tf_op jit(solution)/shard_map/pallas_call | solution.py:24
  115.3 3.9 %collective-permute-start.22 = (bf16[1,2,128,256]{3,2,1,0:T(8,128)(2,1)}, bf16[1,2,128,256]{3,2,1,0:T(8,128)(2,1)}, u32[]{:S(2)}, u32[]{:S(2)}) collective-permute-start(bf16[1,2,128,256]{3,2,1,0:T(8,128)(2,1)} %get-tuple-element.40), channel_id=1, source_target_pairs={{0,2},{2,4},{4,6},{1,3},{3,5},{5,7},{8,10},{10,12},{12,14},{9,11},... | collective-permute-start | bytes 393224 | tf_op jit(solution)/shard_map/ppermute | solution.py:468
  123.6 2.9 %shard_map.126 = s16[4,2,16,32,128]{4,3,2,1,0:T(8,128)(2,1)} custom-call(f32[64,32,128]{2,1,0:T(8,128)S(1)} %bitcast.63, f32[64,32,128]{2,1,0:T(8,128)} %collective-permute-done.26.refs_1_, f32[64,32,128]{2,1,0:T(8,128)S(1)} %bitcast.64, f32[64,32,128]{2,1,0:T(8,128)S(1)} %collective-permute-done.27.refs_3_), custom_call_target="tpu_custom_call" | custom-call | bytes 5242880 | tf_op jit(solution)/shard_map/pallas_call | solution.py:24
  126.6 3.6 %all-to-all-start.3 = ((s16[4,2,16,32,128]{4,3,2,1,0:T(8,128)(2,1)}), s16[4,2,16,32,128]{4,3,2,1,0:T(8,128)(2,1)S(1)}, u32[]{:S(2)}, u32[]{:S(2)}) async-start(s16[4,2,16,32,128]{4,3,2,1,0:T(8,128)(2,1)} %shard_map.126), calls=%async_computation.3 | async-start | bytes 2097152 | tf_op jit(solution)/shard_map/all_to_all | solution.py:472
  133.6 4.7 %collective-permute-done.24.refs_2_.refs_4_ = bf16[1,2,128,256]{3,2,1,0:T(8,128)(2,1)S(1)} collective-permute-done((bf16[1,2,128,256]{3,2,1,0:T(8,128)(2,1)}, bf16[1,2,128,256]{3,2,1,0:T(8,128)(2,1)S(1)}, u32[]{:S(2)}, u32[]{:S(2)}) %collective-permute-start.24) | collective-permute-done | bytes 131104 | tf_op jit(solution)/shard_map/ppermute | solution.py:468
  139.0 5.9 %all-to-all-done.3.received = s16[4,2,16,32,128]{4,3,2,1,0:T(8,128)(2,1)S(1)} async-done(((s16[4,2,16,32,128]{4,3,2,1,0:T(8,128)(2,1)}), s16[4,2,16,32,128]{4,3,2,1,0:T(8,128)(2,1)S(1)}, u32[]{:S(2)}, u32[]{:S(2)}) %all-to-all-start.3) | async-done | bytes 1048608 | tf_op jit(solution)/shard_map/all_to_all | solution.py:472
  146.1 5.2 %all-to-all-start.4 = ((s16[4,2,4,32,128]{4,3,2,1,0:T(8,128)(2,1)}), s16[4,2,4,32,128]{4,3,2,1,0:T(8,128)(2,1)S(1)}, u32[]{:S(2)}, u32[]{:S(2)}) async-start(s16[4,2,4,32,128]{4,3,2,1,0:T(8,128)(2,1)} %shard_map.132), calls=%async_computation.4 | async-start | bytes 524288 | tf_op jit(solution)/shard_map/all_to_all | solution.py:472
  159.7 3.4 %all-to-all-start.5 = ((s16[4,2,4,32,128]{4,3,2,1,0:T(8,128)(2,1)}), s16[4,2,4,32,128]{4,3,2,1,0:T(8,128)(2,1)S(1)}, u32[]{:S(2)}, u32[]{:S(2)}) async-start(s16[4,2,4,32,128]{4,3,2,1,0:T(8,128)(2,1)} %shard_map.133), calls=%async_computation.5 | async-start | bytes 524288 | tf_op jit(solution)/shard_map/all_to_all | solution.py:472
  164.8 4.5 %shard_map.130 = (f32[4,2,128,256]{3,2,1,0:T(8,128)S(1)}, f32[32,2,128]{2,1,0:T(2,128)S(1)}) custom-call(s32[4]{0:T(128)S(1)} %pad_add_fusion.flag_ref, bf16[4,2,128,256]{3,2,1,0:T(8,128)(2,1)S(1)} %shard_map.124.grad_ref.refs_0_, bf16[4,2,128,256]{3,2,1,0:T(8,128)(2,1)S(1)} %collective-permute-done.21.refs_1_, ...), custom_call_target="tpu_custom_call" | custom-call | flops 7247757312 | bytes 5608464 | tf_op jit(solution)/shard_map/pallas_call | solution.py:24
  171.2 8.6 %all_to_all.40 = s16[4,4,4,32,128]{4,3,2,1,0:T(8,128)(2,1)S(1)} all-to-all(s16[4,4,4,32,128]{4,3,2,1,0:T(8,128)(2,1)S(1)} %get-tuple-element.38), channel_id=1, replica_groups=mesh['tm'=4,'height'=4,'width'=2] {'height'}, dimensions={0} | all-to-all | bytes 1048576 | tf_op jit(solution)/shard_map/all_to_all | solution.py:472
  179.8 3.5 %all-to-all-start.6 = ((s16[4,4,4,32,128]{4,3,2,1,0:T(8,128)(2,1)}), s16[4,4,4,32,128]{4,3,2,1,0:T(8,128)(2,1)S(1)}, u32[]{:S(2)}, u32[]{:S(2)}) async-start(s16[4,4,4,32,128]{4,3,2,1,0:T(8,128)(2,1)} %get-tuple-element.37), calls=%async_computation.6 | async-start | bytes 1048576 | tf_op jit(solution)/shard_map/all_to_all | solution.py:472
  183.3 3.7 %collective-permute-start.31 = (s16[64,32,128]{2,1,0:T(8,128)(2,1)S(1)}, s16[64,32,128]{2,1,0:T(8,128)(2,1)S(1)}, u32[]{:S(2)}, u32[]{:S(2)}) collective-permute-start(s16[64,32,128]{2,1,0:T(8,128)(2,1)S(1)} %bitcast.61), channel_id=1, source_target_pairs={{0,1},{1,0},{2,3},{3,2},{4,5},{5,4},{6,7},{7,6},{8,9},{9,8},{10,11... | collective-permute-start | bytes 1572872 | tf_op jit(solution)/shard_map/ppermute | solution.py:509
  188.7 4.8 %collective-permute-start.30 = (s16[64,32,128]{2,1,0:T(8,128)(2,1)S(1)}, s16[64,32,128]{2,1,0:T(8,128)(2,1)S(1)}, u32[]{:S(2)}, u32[]{:S(2)}) collective-permute-start(s16[64,32,128]{2,1,0:T(8,128)(2,1)S(1)} %bitcast.59), channel_id=1, source_target_pairs={{0,1},{1,0},{2,3},{3,2},{4,5},{5,4},{6,7},{7,6},{8,9},{9,8},{10,11... | collective-permute-start | bytes 1572872 | tf_op jit(solution)/shard_map/ppermute | solution.py:509
  193.5 11.4 %all_to_all.41.sums_ref = f32[32,2,128]{2,1,0:T(2,128)S(1)} all-to-all(f32[32,2,128]{2,1,0:T(2,128)S(1)} %get-tuple-element.36), channel_id=1, replica_groups=mesh['tm'=4,'height'=4,'width'=2] {'tm','height','width'}, dimensions={0} | all-to-all | bytes 65536 | tf_op jit(solution)/shard_map/all_to_all | solution.py:472
  208.0 3.9 %shard_map.136 = f32[128,3456]{1,0:T(8,128)} custom-call(s32[4]{0:T(128)S(1)} %pad_add_fusion.flag_ref, s16[64,32,128]{2,1,0:T(8,128)(2,1)S(1)} %bitcast.62, s16[64,32,128]{2,1,0:T(8,128)(2,1)S(1)} %collective-permute-done.31.theirs_ref, f32[2,128]{1,0:T(2,128)S(1)} %slice_bitcast_fusion.7.after), custom_call_target="tpu_custom_call" | custom-call | bytes 2819088 | tf_op jit(solution)/shard_map/pallas_call | solution.py:24
  212.0 3.9 %shard_map.135 = f32[128,3456]{1,0:T(8,128)} custom-call(s32[4]{0:T(128)S(1)} %pad_add_fusion.flag_ref, s16[64,32,128]{2,1,0:T(8,128)(2,1)S(1)} %bitcast.60, s16[64,32,128]{2,1,0:T(8,128)(2,1)S(1)} %collective-permute-done.30.theirs_ref, f32[2,128]{1,0:T(2,128)S(1)} %slice_bitcast_fusion.7.after), custom_call_target="tpu_custom_call" | custom-call | bytes 2819088 | tf_op jit(solution)/shard_map/pallas_call | solution.py:24
  (162 shorter events, 68.5 us)
Async XLA Ops:
  4.7 7.6 %collective-permute-start.7 = (f32[2,128]{1,0:T(2,128)S(1)}, f32[2,128]{1,0:T(2,128)S(1)}, u32[]{:S(2)}, u32[]{:S(2)}) collective-permute-start(f32[2,128]{1,0:T(2,128)S(1)} %slice_bitcast_fusion.9), channel_id=1, source_target_pairs={{0,8},{8,0},{16,24},{24,16},{1,9},{9,1},{17,25},{25,17},{2,10},{10... | collective-permute-start | bytes 3080 | tf_op jit(solution)/shard_map/ppermute | solution.py:483
  9.2 46.6 %collective-permute-start = (bf16[4,2,128,256]{3,2,1,0:T(8,128)(2,1)S(1)}, bf16[4,2,128,256]{3,2,1,0:T(8,128)(2,1)}, u32[]{:S(2)}, u32[]{:S(2)}) collective-permute-start(bf16[4,2,128,256]{3,2,1,0:T(8,128)(2,1)S(1)} %get-tuple-element.21.refs_0_.own.refs_9_.latent), channel_id=1, source_target_pairs={{0,8},{8,16},{16,24},{1,9},{9,17},{17,25},{2,10},{10,18},{18,26},{... | collective-permute-start | bytes 1572872 | tf_op jit(solution)/shard_map/ppermute | solution.py:468
  13.5 7.9 %collective-permute-start.10 = (f32[2,128]{1,0:T(2,128)S(1)}, f32[2,128]{1,0:T(2,128)S(1)}, u32[]{:S(2)}, u32[]{:S(2)}) collective-permute-start(f32[2,128]{1,0:T(2,128)S(1)} %pad_maximum_fusion), channel_id=1, source_target_pairs={{0,2},{2,0},{4,6},{6,4},{1,3},{3,1},{5,7},{7,5},{8,10},{10,8},{12,... | collective-permute-start | bytes 3080 | tf_op jit(solution)/shard_map/ppermute | solution.py:483
  14.7 7.9 %collective-permute-start.11 = (f32[2,128]{1,0:T(2,128)S(1)}, f32[2,128]{1,0:T(2,128)S(1)}, u32[]{:S(2)}, u32[]{:S(2)}) collective-permute-start(f32[2,128]{1,0:T(2,128)S(1)} %pad_maximum_fusion), channel_id=1, source_target_pairs={{0,4},{2,6},{4,0},{6,2},{1,5},{3,7},{5,1},{7,3},{8,12},{10,14},{12... | collective-permute-start | bytes 3080 | tf_op jit(solution)/shard_map/ppermute | solution.py:483
  16.0 8.0 %collective-permute-start.12 = (f32[2,128]{1,0:T(2,128)S(1)}, f32[2,128]{1,0:T(2,128)S(1)}, u32[]{:S(2)}, u32[]{:S(2)}) collective-permute-start(f32[2,128]{1,0:T(2,128)S(1)} %pad_maximum_fusion), channel_id=1, source_target_pairs={{0,6},{2,4},{4,2},{6,0},{1,7},{3,5},{5,3},{7,1},{8,14},{10,12},{12... | collective-permute-start | bytes 3080 | tf_op jit(solution)/shard_map/ppermute | solution.py:483
  16.2 17.1 %collective-permute-start.1 = (bf16[1,2,128,256]{3,2,1,0:T(8,128)(2,1)S(1)}, bf16[1,2,128,256]{3,2,1,0:T(8,128)(2,1)S(1)}, u32[]{:S(2)}, u32[]{:S(2)}) collective-permute-start(bf16[1,2,128,256]{3,2,1,0:T(8,128)(2,1)S(1)} %get-tuple-element.44), channel_id=1, source_target_pairs={{0,2},{2,4},{4,6},{1,3},{3,5},{5,7},{8,10},{10,12},{12,14},{9,11},... | collective-permute-start | bytes 393224 | tf_op jit(solution)/shard_map/ppermute | solution.py:468
  21.3 13.3 %collective-permute-start.2 = (bf16[1,2,128,256]{3,2,1,0:T(8,128)(2,1)S(1)}, bf16[1,2,128,256]{3,2,1,0:T(8,128)(2,1)}, u32[]{:S(2)}, u32[]{:S(2)}) collective-permute-start(bf16[1,2,128,256]{3,2,1,0:T(8,128)(2,1)S(1)} %get-tuple-element.43), channel_id=1, source_target_pairs={{2,0},{4,2},{6,4},{3,1},{5,3},{7,5},{10,8},{12,10},{14,12},{11,9},... | collective-permute-start | bytes 393224 | tf_op jit(solution)/shard_map/ppermute | solution.py:468
  22.7 35.2 %collective-permute-start.14 = (bf16[4,2,128,256]{3,2,1,0:T(8,128)(2,1)S(1)}, bf16[4,2,128,256]{3,2,1,0:T(8,128)(2,1)S(1)}, u32[]{:S(2)}, u32[]{:S(2)}) collective-permute-start(bf16[4,2,128,256]{3,2,1,0:T(8,128)(2,1)S(1)} %shard_map.116.refs_0_.cotangent), channel_id=1, source_target_pairs={{8,0},{16,8},{24,16},{9,1},{17,9},{25,17},{10,2},{18,10},{26,18},{... | collective-permute-start | bytes 1572872 | tf_op jit(solution)/shard_map/ppermute | solution.py:468
  28.4 13.3 %collective-permute-start.15 = (bf16[1,2,128,256]{3,2,1,0:T(8,128)(2,1)}, bf16[1,2,128,256]{3,2,1,0:T(8,128)(2,1)}, u32[]{:S(2)}, u32[]{:S(2)}) collective-permute-start(bf16[1,2,128,256]{3,2,1,0:T(8,128)(2,1)} %get-tuple-element.42), channel_id=1, source_target_pairs={{0,2},{2,4},{4,6},{1,3},{3,5},{5,7},{8,10},{10,12},{12,14},{9,11},... | collective-permute-start | bytes 393224 | tf_op jit(solution)/shard_map/ppermute | solution.py:468
  33.3 9.6 %collective-permute-start.16 = (bf16[1,2,128,256]{3,2,1,0:T(8,128)(2,1)}, bf16[1,2,128,256]{3,2,1,0:T(8,128)(2,1)}, u32[]{:S(2)}, u32[]{:S(2)}) collective-permute-start(bf16[1,2,128,256]{3,2,1,0:T(8,128)(2,1)} %get-tuple-element.41), channel_id=1, source_target_pairs={{2,0},{4,2},{6,4},{3,1},{5,3},{7,5},{10,8},{12,10},{14,12},{11,9},... | collective-permute-start | bytes 393224 | tf_op jit(solution)/shard_map/ppermute | solution.py:468
  34.6 9.6 %collective-permute-start.3 = (bf16[1,2,128,256]{3,2,1,0:T(8,128)(2,1)S(1)}, bf16[1,2,128,256]{3,2,1,0:T(8,128)(2,1)}, u32[]{:S(2)}, u32[]{:S(2)}) collective-permute-start(bf16[1,2,128,256]{3,2,1,0:T(8,128)(2,1)S(1)} %collective-permute-done.1.refs_0_.above), channel_id=1, source_target_pairs={{0,8},{8,16},{16,24},{1,9},{9,17},{17,25},{2,10},{10,18},{18,26},{... | collective-permute-start | bytes 393224 | tf_op jit(solution)/shard_map/ppermute | solution.py:468
  44.3 8.2 %collective-permute-start.18 = (bf16[1,2,128,256]{3,2,1,0:T(8,128)(2,1)}, bf16[1,2,128,256]{3,2,1,0:T(8,128)(2,1)S(1)}, u32[]{:S(2)}, u32[]{:S(2)}) collective-permute-start(bf16[1,2,128,256]{3,2,1,0:T(8,128)(2,1)} %collective-permute-done.16.refs_1_.refs_3_), channel_id=1, source_target_pairs={{8,0},{16,8},{24,16},{9,1},{17,9},{25,17},{10,2},{18,10},{26,18},{... | collective-permute-start | bytes 393224 | tf_op jit(solution)/shard_map/ppermute | solution.py:468
  47.0 13.6 %collective-permute-start.6 = (bf16[128,128]{1,0:T(8,128)(2,1)S(1)}, bf16[128,128]{1,0:T(8,128)(2,1)S(1)}, u32[]{:S(2)}, u32[]{:S(2)}) collective-permute-start(bf16[128,128]{1,0:T(8,128)(2,1)S(1)} %shard_map.114), channel_id=1, source_target_pairs={{0,1},{1,0},{2,3},{3,2},{4,5},{5,4},{6,7},{7,6},{8,9},{9,8},{10,11... | collective-permute-start | bytes 98312 | tf_op jit(solution)/shard_map/ppermute | solution.py:509
  54.4 19.9 %collective-permute-start.20 = (bf16[128,128]{1,0:T(8,128)(2,1)}, bf16[128,128]{1,0:T(8,128)(2,1)}, u32[]{:S(2)}, u32[]{:S(2)}) collective-permute-start(bf16[128,128]{1,0:T(8,128)(2,1)} %shard_map.119), channel_id=1, source_target_pairs={{0,1},{1,0},{2,3},{3,2},{4,5},{5,4},{6,7},{7,6},{8,9},{9,8},{10,11... | collective-permute-start | bytes 98312 | tf_op jit(solution)/shard_map/ppermute | solution.py:509
  60.0 14.3 %collective-permute-start.19 = (bf16[128,128]{1,0:T(8,128)(2,1)}, bf16[128,128]{1,0:T(8,128)(2,1)}, u32[]{:S(2)}, u32[]{:S(2)}) collective-permute-start(bf16[128,128]{1,0:T(8,128)(2,1)} %shard_map.118), channel_id=1, source_target_pairs={{0,1},{1,0},{2,3},{3,2},{4,5},{5,4},{6,7},{7,6},{8,9},{9,8},{10,11... | collective-permute-start | bytes 98312 | tf_op jit(solution)/shard_map/ppermute | solution.py:509
  68.4 16.1 %all-to-all-start = ((f32[32,2,128]{2,1,0:T(2,128)}), f32[32,2,128]{2,1,0:T(2,128)S(1)}, u32[]{:S(2)}, u32[]{:S(2)}) async-start(f32[32,2,128]{2,1,0:T(2,128)} %copy-done.24), calls=%async_computation | async-start | bytes 65536 | tf_op jit(solution)/shard_map/all_to_all | solution.py:472
  89.2 15.5 %all-to-all-start.1 = ((f32[32,2,128]{2,1,0:T(2,128)}), f32[32,2,128]{2,1,0:T(2,128)S(1)}, u32[]{:S(2)}, u32[]{:S(2)}) async-start(f32[32,2,128]{2,1,0:T(2,128)} %get-tuple-element.27), calls=%async_computation.1 | async-start | bytes 65536 | tf_op jit(solution)/shard_map/all_to_all | solution.py:472
  104.4 19.2 %collective-permute-start.26 = (f32[64,32,128]{2,1,0:T(8,128)}, f32[64,32,128]{2,1,0:T(8,128)}, u32[]{:S(2)}, u32[]{:S(2)}) collective-permute-start(f32[64,32,128]{2,1,0:T(8,128)} %bitcast.14), channel_id=1, source_target_pairs={{0,1},{1,0},{2,3},{3,2},{4,5},{5,4},{6,7},{7,6},{8,9},{9,8},{10,11... | collective-permute-start | bytes 3145736 | tf_op jit(solution)/shard_map/ppermute | solution.py:509
  114.3 9.4 %collective-permute-start.27 = (f32[64,32,128]{2,1,0:T(8,128)S(1)}, f32[64,32,128]{2,1,0:T(8,128)S(1)}, u32[]{:S(2)}, u32[]{:S(2)}) collective-permute-start(f32[64,32,128]{2,1,0:T(8,128)S(1)} %bitcast.65), channel_id=1, source_target_pairs={{0,1},{1,0},{2,3},{3,2},{4,5},{5,4},{6,7},{7,6},{8,9},{9,8},{10,11... | collective-permute-start | bytes 3145736 | tf_op jit(solution)/shard_map/ppermute | solution.py:509
  115.3 14.8 %collective-permute-start.22 = (bf16[1,2,128,256]{3,2,1,0:T(8,128)(2,1)}, bf16[1,2,128,256]{3,2,1,0:T(8,128)(2,1)}, u32[]{:S(2)}, u32[]{:S(2)}) collective-permute-start(bf16[1,2,128,256]{3,2,1,0:T(8,128)(2,1)} %get-tuple-element.40), channel_id=1, source_target_pairs={{0,2},{2,4},{4,6},{1,3},{3,5},{5,7},{8,10},{10,12},{12,14},{9,11},... | collective-permute-start | bytes 393224 | tf_op jit(solution)/shard_map/ppermute | solution.py:468
  121.0 17.9 %collective-permute-start.21 = (bf16[4,2,128,256]{3,2,1,0:T(8,128)(2,1)S(1)}, bf16[4,2,128,256]{3,2,1,0:T(8,128)(2,1)S(1)}, u32[]{:S(2)}, u32[]{:S(2)}) collective-permute-start(bf16[4,2,128,256]{3,2,1,0:T(8,128)(2,1)S(1)} %shard_map.124.grad_ref.refs_0_), channel_id=1, source_target_pairs={{8,0},{16,8},{24,16},{9,1},{17,9},{25,17},{10,2},{18,10},{26,18},{... | collective-permute-start | bytes 1572872 | tf_op jit(solution)/shard_map/ppermute | solution.py:468
  122.3 10.0 %collective-permute-start.23 = (bf16[1,2,128,256]{3,2,1,0:T(8,128)(2,1)}, bf16[1,2,128,256]{3,2,1,0:T(8,128)(2,1)S(1)}, u32[]{:S(2)}, u32[]{:S(2)}) collective-permute-start(bf16[1,2,128,256]{3,2,1,0:T(8,128)(2,1)} %get-tuple-element.39), channel_id=1, source_target_pairs={{2,0},{4,2},{6,4},{3,1},{5,3},{7,5},{10,8},{12,10},{14,12},{11,9},... | collective-permute-start | bytes 393224 | tf_op jit(solution)/shard_map/ppermute | solution.py:468
  126.6 18.3 %all-to-all-start.3 = ((s16[4,2,16,32,128]{4,3,2,1,0:T(8,128)(2,1)}), s16[4,2,16,32,128]{4,3,2,1,0:T(8,128)(2,1)S(1)}, u32[]{:S(2)}, u32[]{:S(2)}) async-start(s16[4,2,16,32,128]{4,3,2,1,0:T(8,128)(2,1)} %shard_map.126), calls=%async_computation.3 | async-start | bytes 2097152 | tf_op jit(solution)/shard_map/all_to_all | solution.py:472
  131.0 7.3 %collective-permute-start.24 = (bf16[1,2,128,256]{3,2,1,0:T(8,128)(2,1)}, bf16[1,2,128,256]{3,2,1,0:T(8,128)(2,1)S(1)}, u32[]{:S(2)}, u32[]{:S(2)}) collective-permute-start(bf16[1,2,128,256]{3,2,1,0:T(8,128)(2,1)} %collective-permute-done.22.refs_0_.refs_2_), channel_id=1, source_target_pairs={{8,0},{16,8},{24,16},{9,1},{17,9},{25,17},{10,2},{18,10},{26,18},{... | collective-permute-start | bytes 393224 | tf_op jit(solution)/shard_map/ppermute | solution.py:468
  132.3 19.6 %collective-permute-start.25 = (bf16[1,2,128,256]{3,2,1,0:T(8,128)(2,1)S(1)}, bf16[1,2,128,256]{3,2,1,0:T(8,128)(2,1)}, u32[]{:S(2)}, u32[]{:S(2)}) collective-permute-start(bf16[1,2,128,256]{3,2,1,0:T(8,128)(2,1)S(1)} %collective-permute-done.23.refs_1_.refs_3_), channel_id=1, source_target_pairs={{8,0},{16,8},{24,16},{9,1},{17,9},{25,17},{10,2},{18,10},{26,18},{... | collective-permute-start | bytes 393224 | tf_op jit(solution)/shard_map/ppermute | solution.py:468
  146.1 12.8 %all-to-all-start.4 = ((s16[4,2,4,32,128]{4,3,2,1,0:T(8,128)(2,1)}), s16[4,2,4,32,128]{4,3,2,1,0:T(8,128)(2,1)S(1)}, u32[]{:S(2)}, u32[]{:S(2)}) async-start(s16[4,2,4,32,128]{4,3,2,1,0:T(8,128)(2,1)} %shard_map.132), calls=%async_computation.4 | async-start | bytes 524288 | tf_op jit(solution)/shard_map/all_to_all | solution.py:472
  153.3 9.8 %collective-permute-start.29 = (bf16[128,128]{1,0:T(8,128)(2,1)S(1)}, bf16[128,128]{1,0:T(8,128)(2,1)S(1)}, u32[]{:S(2)}, u32[]{:S(2)}) collective-permute-start(bf16[128,128]{1,0:T(8,128)(2,1)S(1)} %shard_map.128), channel_id=1, source_target_pairs={{0,1},{1,0},{2,3},{3,2},{4,5},{5,4},{6,7},{7,6},{8,9},{9,8},{10,11... | collective-permute-start | bytes 98312 | tf_op jit(solution)/shard_map/ppermute | solution.py:509
  155.8 7.3 %collective-permute-start.28 = (bf16[128,128]{1,0:T(8,128)(2,1)S(1)}, bf16[128,128]{1,0:T(8,128)(2,1)S(1)}, u32[]{:S(2)}, u32[]{:S(2)}) collective-permute-start(bf16[128,128]{1,0:T(8,128)(2,1)S(1)} %shard_map.127), channel_id=1, source_target_pairs={{0,1},{1,0},{2,3},{3,2},{4,5},{5,4},{6,7},{7,6},{8,9},{9,8},{10,11... | collective-permute-start | bytes 98312 | tf_op jit(solution)/shard_map/ppermute | solution.py:509
  159.7 10.6 %all-to-all-start.5 = ((s16[4,2,4,32,128]{4,3,2,1,0:T(8,128)(2,1)}), s16[4,2,4,32,128]{4,3,2,1,0:T(8,128)(2,1)S(1)}, u32[]{:S(2)}, u32[]{:S(2)}) async-start(s16[4,2,4,32,128]{4,3,2,1,0:T(8,128)(2,1)} %shard_map.133), calls=%async_computation.5 | async-start | bytes 524288 | tf_op jit(solution)/shard_map/all_to_all | solution.py:472
  179.8 8.9 %all-to-all-start.6 = ((s16[4,4,4,32,128]{4,3,2,1,0:T(8,128)(2,1)}), s16[4,4,4,32,128]{4,3,2,1,0:T(8,128)(2,1)S(1)}, u32[]{:S(2)}, u32[]{:S(2)}) async-start(s16[4,4,4,32,128]{4,3,2,1,0:T(8,128)(2,1)} %get-tuple-element.37), calls=%async_computation.6 | async-start | bytes 1048576 | tf_op jit(solution)/shard_map/all_to_all | solution.py:472
  183.3 24.7 %collective-permute-start.31 = (s16[64,32,128]{2,1,0:T(8,128)(2,1)S(1)}, s16[64,32,128]{2,1,0:T(8,128)(2,1)S(1)}, u32[]{:S(2)}, u32[]{:S(2)}) collective-permute-start(s16[64,32,128]{2,1,0:T(8,128)(2,1)S(1)} %bitcast.61), channel_id=1, source_target_pairs={{0,1},{1,0},{2,3},{3,2},{4,5},{5,4},{6,7},{7,6},{8,9},{9,8},{10,11... | collective-permute-start | bytes 1572872 | tf_op jit(solution)/shard_map/ppermute | solution.py:509
  188.7 23.2 %collective-permute-start.30 = (s16[64,32,128]{2,1,0:T(8,128)(2,1)S(1)}, s16[64,32,128]{2,1,0:T(8,128)(2,1)S(1)}, u32[]{:S(2)}, u32[]{:S(2)}) collective-permute-start(s16[64,32,128]{2,1,0:T(8,128)(2,1)S(1)} %bitcast.59), channel_id=1, source_target_pairs={{0,1},{1,0},{2,3},{3,2},{4,5},{5,4},{6,7},{7,6},{8,9},{9,8},{10,11... | collective-permute-start | bytes 1572872 | tf_op jit(solution)/shard_map/ppermute | solution.py:509
  (35 other events, 211.9 us)

commit v6 on v5

--- a/solution.py
+++ b/solution.py
@@ -18,7 +18,7 @@
 SMEM = pl.BlockSpec(memory_space=pltpu.SMEM)
 
 
-def call(body, outs, specs, args, scratch=(), flops=0, transcendentals=0, limit=48):
+def call(body, outs, specs, args, scratch=(), flops=0, transcendentals=0, limit=20):
     moved = sum(a.size * a.dtype.itemsize for a in args)
     moved += sum(o.size * o.dtype.itemsize for o in outs)
     return pl.pallas_call(
@@ -100,35 +100,44 @@
     return 0.5 + 0.5 * jnp.tanh(0.5 * value)
 
 
-def planes_kernel(natural_ref, *refs):
-    out_ref = refs[-1] if len(refs) == 1 else refs[-2]
-    _, frames, rows, cols = natural_ref.shape
-    for row in range(rows):
-        for frame in range(frames):
-            out_ref[row, frame] = natural_ref[:, frame, row, :]
-    if len(refs) == 1:
-        return
-    scale = columns_of(refs[0][0:1])[0]
+def planes_kernel(latent_ref, cotangent_ref, par_ref, latent_out, cotangent_out, down_ref, up_ref, st_ref):
+    _, frames, rows, cols = latent_ref.shape
+    for which, (natural, out) in enumerate(((latent_ref, latent_out), (cotangent_ref, cotangent_out))):
+        for row in range(rows):
+            for frame in range(frames):
+                plane = natural[:, frame, row, :]
+                out[row, frame] = plane
+                if row == rows - 1:
+                    down_ref[which, frame] = plane
+                if row == 0:
+                    up_ref[which, frame] = plane
+    scale = columns_of(par_ref[0:1])[0]
     planes = [
-        functools.partial(lambda r, t: out_ref[r, t].astype(F32) * scale, r, t)
+        functools.partial(lambda r, t: latent_out[r, t].astype(F32) * scale, r, t)
         for r in range(rows)
         for t in range(frames)
     ]
-    put_rows(refs[-1], *local_stats(planes, float(GROUP * rows * frames * cols)))
+    put_rows(st_ref, *local_stats(planes, float(GROUP * rows * frames * cols)))
+
+
+def rows_kernel(above_ref, below_ref, *outs):
+    for which, out in enumerate(outs):
+        out[0] = above_ref[which]
+        out[1] = below_ref[which]
 
 
 def source(own, other, near, far, other_first):
     def at(row, frame):
         is_other = (frame < 2) == other_first
         if row == 0 or row == own.shape[0] + 1:
-            return (far if is_other else near)[0 if row == 0 else 1], (0, frame % 2)
+            return (far if is_other else near), (0 if row == 0 else 1, frame % 2)
         return (other if is_other else own), (row - 1, frame % 2)
 
     return at
 
 
-def edges_kernel(flag_ref, *refs):
-    planes, out_ref = [ref for ref in refs[:-1] if len(ref.shape) == 4], refs[-1]
+def edges_kernel(flag_ref, first_ref, second_ref, *refs):
+    planes, out_ref = (first_ref, second_ref), refs[-1]
     is_first = flag_ref[3] == 0
     channels = planes[0].shape[2]
     lane = lax.broadcasted_iota(jnp.int32, (channels, 128), 1)
@@ -184,11 +193,11 @@
 
 
 def conv_first_kernel(
-    flag_ref, own, past, above, below, far_above, far_below, edge_ref, rim_ref, par_ref, st_ref, weight, after, hidden_ref, st_out, stack_ref,
+    flag_ref, own, past, near, far, edge_ref, rim_ref, par_ref, st_ref, weight, after, hidden_ref, st_out, stack_ref,
     *, count
 ):
     rows, frames, channels, cols = own.shape
-    at = source(own, past, (above, below), (far_above, far_below), True)
+    at = source(own, past, near, far, True)
     mean, inverse, gain, shift, scale = norm_columns(par_ref, st_ref, count, 1)
 
     def act(latent):
@@ -226,9 +235,9 @@
     put_rows(st_out, *local_stats(planes, float(GROUP * rows * frames * cols)))
 
 
-def fill_future(stack, flag_ref, own, future, above, below, far_above, far_below, edge_ref, rim_ref):
+def fill_future(stack, flag_ref, own, future, near, far, edge_ref, rim_ref):
     rows = own.shape[0]
-    at = source(own, future, (above, below), (far_above, far_below), False)
+    at = source(own, future, near, far, False)
     on_left, on_right = sides(flag_ref)
     edges = (edge_ref[...], rim_ref[...])
     for row in range(rows + 2):
@@ -267,7 +276,9 @@
     put_rows(sums_ref, group_sums(first), group_sums(second))
 
 
-def hidden_grad_kernel(hidden, scaled, par_ref, st_ref, sums_ref, after, out_ref, *, count):
+def hidden_grad_kernel(
+    hidden, scaled, par_ref, st_ref, sums_ref, after, out_ref, down_ref, up_ref, *, count
+):
     rows, frames, channels, cols = hidden.shape
     mean, inverse, _, _, _ = norm_columns(par_ref, st_ref, count, 3)
     means = jnp.sum(sums_ref[...], axis=0) / count
@@ -275,7 +286,12 @@
     for row in range(rows):
         for frame in range(frames):
             normed = (hidden[row, frame] - mean) * inverse
-            out_ref[row, frame] = (inverse * (scaled[row, frame] - first - normed * second)).astype(BF16)
+            plane = (inverse * (scaled[row, frame] - first - normed * second)).astype(BF16)
+            out_ref[row, frame] = plane
+            if row == rows - 1:
+                down_ref[0, frame] = plane
+            if row == 0:
+                up_ref[0, frame] = plane
 
 
 def put_halves(flag_ref, mine_ref, theirs_ref, tap, block):
@@ -340,7 +356,7 @@
             out_ref[copy] = value[:, which]
 
 
-def join_kernel(flag_ref, mine_ref, theirs_ref, after, out_ref, first_ref, second_ref):
+def join_kernel(flag_ref, mine_ref, theirs_ref, out_ref, first_ref, second_ref):
     half, _, channels = mine_ref.shape
     is_first = flag_ref[3] == 0
     first_ref[...] = decoded_value(jnp.where(is_first, mine_ref[...], theirs_ref[...])).reshape(first_ref.shape)
@@ -411,7 +427,8 @@
     put_rows(sums_ref, group_sums(first), group_sums(second))
 
 
-def decoded_grad_kernel(scaled, latent, cotangent, par_ref, st_ref, sums_ref, out_ref, *, count):
+def decoded_grad_kernel(scaled, latent, cotangent, par_ref, st_ref, sums_ref, out_ref, token_ref, *, count):
+    token_ref[...] = jnp.zeros(token_ref.shape, F32)
     rows, frames, channels, cols = latent.shape
     mean, inverse, _, _, scale = norm_columns(par_ref, st_ref, count, 1)
     means = jnp.sum(sums_ref[...], axis=0) / count
@@ -495,12 +512,6 @@
     return value[None]
 
 
-def token(value):
-    if value.ndim > 2:
-        value = value[(0,) * (value.ndim - 2)]
-    return value[:16, :128]
-
-
 def shared(value):
     return exchanged(value, ("tm", "height", "width"))
 
@@ -529,13 +540,13 @@
         second_scatter_kernel,
         [shape((by_tm, 2, rows // by_tm, SLOTS, channels), jnp.int16)],
         [VMEM] * (1 + len(after)),
-        (value, *map(token, after)),
+        (value, *after),
     )
     return exchanged(value, "tm")
 
 
 def gathered(value, after, after_last):
-    (value,) = call(total_kernel, [shape(value.shape, jnp.int16)], [VMEM] * (1 + len(after)), (value, *map(token, after)))
+    (value,) = call(total_kernel, [shape(value.shape, jnp.int16)], [VMEM] * (1 + len(after)), (value, *after))
     value = exchanged(value, "tm")
     by_height = lax.axis_size("height")
     by_tm, _, rows, _, channels = value.shape
@@ -543,39 +554,37 @@
         copies_kernel,
         [shape((by_height, by_tm, rows, SLOTS, channels), jnp.int16)] * 2,
         [VMEM] * 2,
-        (value, token(after_last)),
+        (value, after_last),
     )
     return [exchanged(copy, "height").reshape(-1, SLOTS, channels) for copy in copies]
 
 
-def joined(flags, mine, theirs, after):
+def joined(flags, mine, theirs):
     half, _, channels = mine.shape
     (total,) = call(
         join_kernel,
         [shape((2 * half, TAPS * channels), F32)],
-        [SMEM] + [VMEM] * 3,
-        (flags, mine, theirs, token(after)),
+        [SMEM] + [VMEM] * 2,
+        (flags, mine, theirs),
         scratch=[pltpu.VMEM((half * SLOTS, channels), F32)] * 2,
     )
     return total
-
-
-def row_exchange(block):
-    return shifted(block[-1:], "height", 1), shifted(block[:1], "height", -1)
 
 
 def edges(flags, planes, after):
     channels = planes[0].shape[2]
-    args = (*planes, *map(token, after))
+    args = (*planes, *after)
     (columns,) = call(edges_kernel, [shape((channels, 128), BF16)], [SMEM] + [VMEM] * len(args), (flags, *args))
     return columns
 
 
-def halo(own, steps):
-    other = shifted(own, "tm", steps)
-    near = row_exchange(own)
-    far = [shifted(row, "tm", steps) for row in near]
-    return other, *near, *far
+def row_halos(down, up):
+    above, below = shifted(down, "height", 1), shifted(up, "height", -1)
+    return call(rows_kernel, [shape((2, *down.shape[1:]), BF16)] * down.shape[0], [VMEM] * 2, (above, below))
+
+
+def halo(own, near, steps):
+    return shifted(own, "tm", steps), near, shifted(near, "tm", steps)
 
 
 def with_columns(flags, own, around, after=()):
@@ -618,12 +627,16 @@
     conv_flops = 3 * 2 * 4 * 256 * 36 * channels * 2 * channels
     small = shape((devices, 2, channels), F32)
 
-    latent, stats_first = call(
-        planes_kernel, [shape(block, BF16), small], [VMEM] * 2, (latent, par)
-    )
-    around = with_columns(flags, latent, halo(latent, 1))
-    (cotangent,) = call(planes_kernel, [shape(block, BF16)], [VMEM], (cotangent,))
-    around_c = with_columns(flags, cotangent, halo(cotangent, -1))
+    message = shape((2, frames, channels, cols), BF16)
+    latent, cotangent, down, up, stats_first = call(
+        planes_kernel,
+        [shape(block, BF16), shape(block, BF16), message, message, small],
+        [VMEM] * 3,
+        (latent, cotangent, par),
+    )
+    near, near_c = row_halos(down, up)
+    around = with_columns(flags, latent, halo(latent, near, 1))
+    around_c = halo(cotangent, near_c, -1)
     stats_first = all_stats(stats_first, count / devices)
     (weight_first,) = call(weight_forward_kernel, [shape(taps, BF16)], [VMEM], (conv_first,))
     (weight_second_t,) = call(weight_back_kernel, [shape(taps, BF16)], [VMEM], (conv_second,))
@@ -632,16 +645,17 @@
     hidden, stats_second, stack_first = call(
         functools.partial(conv_first_kernel, count=count),
         [shape(block, F32), small, shape(stack, BF16)],
-        [SMEM] + [VMEM] * 12,
-        (flags, latent, *around, par, stats_first, weight_first, token(around_c[0])),
+        [SMEM] + [VMEM] * 10,
+        (flags, latent, *around, par, stats_first, weight_first, around_c[0]),
         flops=conv_flops,
         transcendentals=3 * latent.size,
     )
+    around_c = with_columns(flags, cotangent, around_c, (stats_second,))
     stats_second = shared(stats_second)
     grad_second, stack_c = call(
         conv_back_kernel,
         [shape(block, F32), shape(stack, BF16)],
-        [SMEM] + [VMEM] * 9,
+        [SMEM] + [VMEM] * 7,
         (flags, cotangent, *around_c, weight_second_t),
         flops=conv_flops,
     )
@@ -661,13 +675,15 @@
         scratch=[pltpu.VMEM((rows * cols, frames * channels), BF16)],
         flops=conv_flops,
     )
-    (hidden_grad,) = call(
+    message = shape((1, frames, channels, cols), BF16)
+    hidden_grad, down, up = call(
         functools.partial(hidden_grad_kernel, count=count),
-        [shape(block, BF16)],
+        [shape(block, BF16), message, message],
         [VMEM] * 6,
-        (hidden, scaled, par, stats_second, sums, token(halves_second[0])),
-    )
-    around = halo(hidden_grad, -1)
+        (hidden, scaled, par, stats_second, sums, halves_second[0]),
+    )
+    (near,) = row_halos(down, up)
+    around = halo(hidden_grad, near, -1)
     halves_first = call(
         weight_first_kernel,
         halves,
@@ -684,23 +700,23 @@
     scaled, sums_first = call(
         functools.partial(first_grad_kernel, count=count),
         [shape(block, F32), small],
-        [SMEM] + [VMEM] * 12,
+        [SMEM] + [VMEM] * 10,
         (flags, hidden_grad, *around, weight_first_t, latent, par, stats_first),
         scratch=[pltpu.VMEM(stack, BF16)],
         flops=conv_flops,
         transcendentals=latent.size,
     )
-    weights = summed(weights, around[:3])
-    second, first = gathered(weights, around[3:5], sums_first)
+    weights = summed(weights, around[:2])
     sums_first = shared(sums_first)
-    (decoded_grad,) = call(
+    decoded_grad, token = call(
         functools.partial(decoded_grad_kernel, count=count),
-        [shape((channels, frames, rows, cols), F32)],
+        [shape((channels, frames, rows, cols), F32), shape((8, 128), F32)],
         [VMEM] * 6,
         (scaled, latent, cotangent, par, stats_first, sums_first),
     )
-    conv_second_grad = joined(flags, second, swapped(second), sums_first)
-    conv_first_grad = joined(flags, first, swapped(first), sums_first)
+    second, first = gathered(weights, (sums_first,), token)
+    conv_second_grad = joined(flags, second, swapped(second))
+    conv_first_grad = joined(flags, first, swapped(first))
     return decoded_grad, conv_first_grad, conv_second_grad
 
 

time: 218 us -> 205 us (0.940)
  starting transfers between devices: 84.6 us -> 76 us
  Pallas kernels: 62.4 us -> 55.3 us
  waiting for transfers between devices: 19.1 us -> 26.2 us
  local copies, waits for them, and re-layouts: 27.5 us -> 25.1 us
    ppermute x15 -> x10, starting transfers between devices: 33 us -> 19.6 us  [shifted(): lax.ppermute(value, axis, [(source, source + steps) for source in range(i...]
    pallas_call x25 -> x26, Pallas kernels: 62.4 us -> 55.3 us  [call(): pl.pallas_call(body, out_shape=tuple(outs), in_specs=specs, out_specs=tup...]
    ppermute x15 -> x10, waiting for transfers between devices: 8.8 us -> 13.6 us  [shifted(): lax.ppermute(value, axis, [(source, source + steps) for source in range(i...]
    ppermute x10, starting transfers between devices: 13.4 us -> 17.7 us  [swapped(): return lax.ppermute(value, 'width', [(0, 1), (1, 0)])]
    slice x11 -> x0, local copies, waits for them, and re-layouts: 2.87 us -> none  [the longest x3 1.48 us: row_exchange(): return (shifted(block[-1:], 'height', 1), shifted(block[:1], 'height', -1))]
    unnamed x58 -> x42, local copies, waits for them, and re-layouts: 21.4 us -> 24.2 us
    squeeze x8 -> x0, local copies, waits for them, and re-layouts: 2.34 us -> none  [token(): value = value[(0,) * (value.ndim - 2)]]
  transfers between devices with their start and end apart: 38 -> 33, of which waited for: 8 -> 11; matrix products, arithmetic and copies ran while one was open for 2% -> 0% of each run, Pallas kernels for 25% -> 22%
where the time goes in v6:
time: 205 us; the launch traced here: 204 us
  starting transfers between devices  76 us (37%)
  Pallas kernels  55.3 us (27%)
  waiting for transfers between devices  26.2 us (13%)
  local copies, waits for them, and re-layouts  25.1 us (12%)
  blocking collectives  19 us (9%)
    pallas_call x26, Pallas kernels, call(): pl.pallas_call(body, out_shape=tuple(outs), in_specs=specs, out_specs=tup...  55.3 us
    all_to_all x6, starting transfers between devices, exchanged(): return lax.all_to_all(value, axis, 0, 0, tiled=True)  27.5 us
    unnamed x42, local copies, waits for them, and re-layouts  24.2 us
    ppermute x10, starting transfers between devices, shifted(): lax.ppermute(value, axis, [(source, source + steps) for source in range(i...  19.6 us
    all_to_all x2, blocking collectives, exchanged(): return lax.all_to_all(value, axis, 0, 0, tiled=True)  19 us
    ppermute x10, starting transfers between devices, swapped(): return lax.ppermute(value, 'width', [(0, 1), (1, 0)])  17.7 us
    ppermute x10, waiting for transfers between devices, shifted(): lax.ppermute(value, axis, [(source, source + steps) for source in range(i...  13.6 us
    ppermute x7, starting transfers between devices, all_stats(): lax.ppermute(value, axis, [(i, i ^ step * k) for i in range(size)])  11.3 us
  transfers between devices with their start and end apart: 33, of which 11 were waited for; matrix products, arithmetic and copies ran while one was open for 0% of the time, Pallas kernels for 22%

profile of v6, /device:TPU:1, one launch (start us, length us, event | category | flops | bytes accessed | tf_op | source)
XLA Modules:
  0.0 203.7 jit_solution(17721432242814895156)
XLA Ops:
  4.3 2.7 %shard_map.112 = (bf16[4,2,128,256]{3,2,1,0:T(8,128)(2,1)S(1)}, bf16[4,2,128,256]{3,2,1,0:T(8,128)(2,1)S(1)}, bf16[2,2,128,256]{3,2,1,0:T(8,128)(2,1)S(1)}, bf16...) custom-call(bf16[128,2,4,256]{3,2,1,0:T(4,128)(2,1)S(1)} %copy-done.9, bf16[128,2,4,256]{3,2,1,0:T(4,128)(2,1)S(1)} %copy-done.10, ...), custom_call_target="tpu_custom_call" | custom-call | bytes 2658304 | tf_op jit(solution)/shard_map/pallas_call | solution.py:24
  9.2 2.3 %collective-permute-start.7 = (f32[2,128]{1,0:T(2,128)S(1)}, f32[2,128]{1,0:T(2,128)S(1)}, u32[]{:S(2)}, u32[]{:S(2)}) collective-permute-start(f32[2,128]{1,0:T(2,128)S(1)} %slice_bitcast_fusion), channel_id=1, source_target_pairs={{0,16},{8,24},{16,0},{24,8},{1,17},{9,25},{17,1},{25,9},{2,18},{10... | collective-permute-start | bytes 3080 | tf_op jit(solution)/shard_map/ppermute | solution.py:500
  11.5 3.1 %collective-permute-start.1 = (bf16[2,2,128,256]{3,2,1,0:T(8,128)(2,1)S(1)}, bf16[2,2,128,256]{3,2,1,0:T(8,128)(2,1)S(1)}, u32[]{:S(2)}, u32[]{:S(2)}) collective-permute-start(bf16[2,2,128,256]{3,2,1,0:T(8,128)(2,1)S(1)} %get-tuple-element.32), channel_id=1, source_target_pairs={{0,2},{2,4},{4,6},{1,3},{3,5},{5,7},{8,10},{10,12},{12,14},{9,11},... | collective-permute-start | bytes 786440 | tf_op jit(solution)/shard_map/ppermute | solution.py:485
  16.0 3.1 %collective-permute-start.10 = (f32[2,128]{1,0:T(2,128)S(1)}, f32[2,128]{1,0:T(2,128)S(1)}, u32[]{:S(2)}, u32[]{:S(2)}) collective-permute-start(f32[2,128]{1,0:T(2,128)S(1)} %pad_maximum_fusion), channel_id=1, source_target_pairs={{0,4},{2,6},{4,0},{6,2},{1,5},{3,7},{5,1},{7,3},{8,12},{10,14},{12... | collective-permute-start | bytes 3080 | tf_op jit(solution)/shard_map/ppermute | solution.py:500
  26.4 2.5 %collective-permute-start.12 = (f32[2,128]{1,0:T(2,128)S(1)}, f32[2,128]{1,0:T(2,128)S(1)}, u32[]{:S(2)}, u32[]{:S(2)}) collective-permute-start(f32[2,128]{1,0:T(2,128)S(1)} %pad_maximum_fusion.1), channel_id=1, source_target_pairs={{0,1},{1,0},{2,3},{3,2},{4,5},{5,4},{6,7},{7,6},{8,9},{9,8},{10,11... | collective-permute-start | bytes 3080 | tf_op jit(solution)/shard_map/ppermute | solution.py:500
  28.9 3.0 %collective-permute-start.3 = (bf16[2,2,128,256]{3,2,1,0:T(8,128)(2,1)S(1)}, bf16[2,2,128,256]{3,2,1,0:T(8,128)(2,1)S(1)}, u32[]{:S(2)}, u32[]{:S(2)}) collective-permute-start(bf16[2,2,128,256]{3,2,1,0:T(8,128)(2,1)S(1)} %get-tuple-element.34.first_ref.near), channel_id=1, source_target_pairs={{0,8},{8,16},{16,24},{1,9},{9,17},{17,25},{2,10},{10,18},{18,26},{... | collective-permute-start | bytes 786440 | tf_op jit(solution)/shard_map/ppermute | solution.py:485
  33.4 4.7 %collective-permute-done.3.second_ref.far = bf16[2,2,128,256]{3,2,1,0:T(8,128)(2,1)S(1)} collective-permute-done((bf16[2,2,128,256]{3,2,1,0:T(8,128)(2,1)S(1)}, bf16[2,2,128,256]{3,2,1,0:T(8,128)(2,1)S(1)}, u32[]{:S(2)}, u32[]{:S(2)}) %collective-permute-start.3) | collective-permute-done | bytes 262176 | tf_op jit(solution)/shard_map/ppermute | solution.py:485
  44.4 5.3 %shard_map.117 = (f32[4,2,128,256]{3,2,1,0:T(8,128)S(1)}, f32[32,2,128]{2,1,0:T(2,128)}, bf16[6,4,384,256]{3,2,1,0:T(8,128)(2,1)S(1)}) custom-call(s32[4]{0:T(128)S(1)} %pad_add_fusion.flag_ref, bf16[4,2,128,256]{3,2,1,0:T(8,128)(2,1)S(1)} %get-tuple-element.31.first_ref.own.refs_7_.latent, ...), custom_call_target="tpu_custom_call" | custom-call | flops 7247757312 | bytes 10327056 | tf_op jit(solution)/shard_map/pallas_call | solution.py:24
  59.8 5.3 %all-to-all-start = ((f32[32,2,128]{2,1,0:T(2,128)}), f32[32,2,128]{2,1,0:T(2,128)S(1)}, u32[]{:S(2)}, u32[]{:S(2)}) async-start(f32[32,2,128]{2,1,0:T(2,128)} %get-tuple-element.39.refs_0_), calls=%async_computation | async-start | bytes 65536 | tf_op jit(solution)/shard_map/all_to_all | solution.py:489
  68.8 3.4 %shard_map.121 = (f32[4,2,128,256]{3,2,1,0:T(8,128)S(1)}, bf16[6,4,384,256]{3,2,1,0:T(8,128)(2,1)S(1)}) custom-call(s32[4]{0:T(128)S(1)} %pad_add_fusion.flag_ref, bf16[4,2,128,256]{3,2,1,0:T(8,128)(2,1)S(1)} %get-tuple-element.36.first_ref.refs_0_.cotangent, bf16[4,2,128,256]{3,2,1,0:T(8,128)(2,1)S(1)} %copy-done.12, ...), custom_call_target="tpu_custom_call" | custom-call | flops 7247757312 | bytes 9764880 | tf_op jit(solution)/shard_map/pallas_call | solution.py:24
  77.8 5.8 %all-to-all-start.1 = ((f32[32,2,128]{2,1,0:T(2,128)}), f32[32,2,128]{2,1,0:T(2,128)S(1)}, u32[]{:S(2)}, u32[]{:S(2)}) async-start(f32[32,2,128]{2,1,0:T(2,128)} %get-tuple-element.42), calls=%async_computation.1 | async-start | bytes 65536 | tf_op jit(solution)/shard_map/all_to_all | solution.py:489
  84.7 2.3 %copy-done.20 = bf16[6,4,384,256]{3,2,1,0:T(8,128)(2,1)S(1)} copy-done((bf16[6,4,384,256]{3,2,1,0:T(8,128)(2,1)S(1)}, bf16[6,4,384,256]{3,2,1,0:T(8,128)(2,1)}, u32[]{:S(2)}) %copy-start.20) | copy-done | bytes 4718616
  87.1 5.6 %shard_map.123 = (f32[2048,128]{1,0:T(8,128)S(1)}, f32[2048,128]{1,0:T(8,128)}) custom-call(s32[4]{0:T(128)S(1)} %pad_add_fusion.flag_ref, bf16[6,4,384,256]{3,2,1,0:T(8,128)(2,1)S(1)} %copy-done.20, bf16[4,2,128,256]{3,2,1,0:T(8,128)(2,1)S(1)} %copy-done.16), custom_call_target="tpu_custom_call" | custom-call | flops 7247757312 | bytes 7340048 | tf_op jit(solution)/shard_map/pallas_call | solution.py:24
  95.5 2.3 %copy-done.18 = bf16[6,4,384,256]{3,2,1,0:T(8,128)(2,1)S(1)} copy-done((bf16[6,4,384,256]{3,2,1,0:T(8,128)(2,1)S(1)}, bf16[6,4,384,256]{3,2,1,0:T(8,128)(2,1)}, u32[]{:S(2)}) %copy-start.18) | copy-done | bytes 4718616
  97.8 5.2 %shard_map.126 = (f32[2048,128]{1,0:T(8,128)S(1)}, f32[2048,128]{1,0:T(8,128)S(1)}) custom-call(s32[4]{0:T(128)S(1)} %pad_add_fusion.flag_ref, bf16[6,4,384,256]{3,2,1,0:T(8,128)(2,1)S(1)} %copy-done.18, bf16[4,2,128,256]{3,2,1,0:T(8,128)(2,1)} %get-tuple-element.46.grad_ref.first_ref.refs_0_), custom_call_target="tpu_custom_call" | custom-call | flops 7247757312 | bytes 7340048 | tf_op jit(solution)/shard_map/pallas_call | solution.py:24
  104.6 3.3 %collective-permute-start.18 = (bf16[1,2,128,256]{3,2,1,0:T(8,128)(2,1)S(1)}, bf16[1,2,128,256]{3,2,1,0:T(8,128)(2,1)S(1)}, u32[]{:S(2)}, u32[]{:S(2)}) collective-permute-start(bf16[1,2,128,256]{3,2,1,0:T(8,128)(2,1)S(1)} %get-tuple-element.47), channel_id=1, source_target_pairs={{0,2},{2,4},{4,6},{1,3},{3,5},{5,7},{8,10},{10,12},{12,14},{9,11},... | collective-permute-start | bytes 393224 | tf_op jit(solution)/shard_map/ppermute | solution.py:485
  110.4 5.0 %collective-permute-done.19.below_ref = bf16[1,2,128,256]{3,2,1,0:T(8,128)(2,1)S(1)} collective-permute-done((bf16[1,2,128,256]{3,2,1,0:T(8,128)(2,1)S(1)}, bf16[1,2,128,256]{3,2,1,0:T(8,128)(2,1)S(1)}, u32[]{:S(2)}, u32[]{:S(2)}) %collective-permute-start.19) | collective-permute-done | bytes 131104 | tf_op jit(solution)/shard_map/ppermute | solution.py:485
  116.7 2.9 %shard_map.127.refs_0_ = s16[4,2,16,32,128]{4,3,2,1,0:T(8,128)(2,1)} custom-call(f32[64,32,128]{2,1,0:T(8,128)S(1)} %bitcast.41, f32[64,32,128]{2,1,0:T(8,128)} %collective-permute-done.21.refs_1_, f32[64,32,128]{2,1,0:T(8,128)S(1)} %bitcast.46, f32[64,32,128]{2,1,0:T(8,128)S(1)} %collective-permute-done.22.refs_3_), custom_call_target="tpu_custom_call" | custom-call | bytes 5242880 | tf_op jit(solution)/shard_map/pallas_call | solution.py:24
  119.6 3.7 %all-to-all-start.3 = ((s16[4,2,16,32,128]{4,3,2,1,0:T(8,128)(2,1)}), s16[4,2,16,32,128]{4,3,2,1,0:T(8,128)(2,1)S(1)}, u32[]{:S(2)}, u32[]{:S(2)}) async-start(s16[4,2,16,32,128]{4,3,2,1,0:T(8,128)(2,1)} %shard_map.127.refs_0_), calls=%async_computation.3 | async-start | bytes 2097152 | tf_op jit(solution)/shard_map/all_to_all | solution.py:489
  128.0 2.4 %shard_map.128 = bf16[128,128]{1,0:T(8,128)(2,1)S(1)} custom-call(s32[4]{0:T(128)S(1)} %pad_add_fusion.flag_ref, bf16[4,2,128,256]{3,2,1,0:T(8,128)(2,1)} %get-tuple-element.46.grad_ref.first_ref.refs_0_, bf16[4,2,128,256]{3,2,1,0:T(8,128)(2,1)S(1)} %collective-permute-done.17.second_ref.refs_1_.refs_0_, s16[4,2,16,32,128]{4,3,2,1,0:T(8,128)(2,1)} %shard_map.127.refs_0_), custom_call_target="tpu_custom_call" | custom-call | bytes 2129936 | tf_op jit(solution)/shard_map/pallas_call | solution.py:24
  131.6 5.2 %shard_map.131 = (f32[4,2,128,256]{3,2,1,0:T(8,128)S(1)}, f32[32,2,128]{2,1,0:T(2,128)}) custom-call(s32[4]{0:T(128)S(1)} %pad_add_fusion.flag_ref, bf16[4,2,128,256]{3,2,1,0:T(8,128)(2,1)} %get-tuple-element.46.grad_ref.first_ref.refs_0_, bf16[4,2,128,256]{3,2,1,0:T(8,128)(2,1)S(1)} %collective-permute-done.17.second_ref.refs_1_.refs_0_, ...), custom_call_target="tpu_custom_call" | custom-call | flops 7247757312 | bytes 5608464 | tf_op jit(solution)/shard_map/pallas_call | solution.py:24
  137.8 5.7 %all-to-all-start.2 = ((f32[32,2,128]{2,1,0:T(2,128)}), f32[32,2,128]{2,1,0:T(2,128)S(1)}, u32[]{:S(2)}, u32[]{:S(2)}) async-start(f32[32,2,128]{2,1,0:T(2,128)} %get-tuple-element.54), calls=%async_computation.2 | async-start | bytes 65536 | tf_op jit(solution)/shard_map/all_to_all | solution.py:489
  144.1 6.6 %all-to-all-done.2.sums_ref.refs_0_ = f32[32,2,128]{2,1,0:T(2,128)S(1)} async-done(((f32[32,2,128]{2,1,0:T(2,128)}), f32[32,2,128]{2,1,0:T(2,128)S(1)}, u32[]{:S(2)}, u32[]{:S(2)}) %all-to-all-start.2) | async-done | bytes 32800 | tf_op jit(solution)/shard_map/all_to_all | solution.py:489
  150.7 10.6 %all_to_all.40.received = s16[4,2,4,32,128]{4,3,2,1,0:T(8,128)(2,1)S(1)} all-to-all(s16[4,2,4,32,128]{4,3,2,1,0:T(8,128)(2,1)S(1)} %shard_map.133), channel_id=1, replica_groups=mesh['tm'=4,'height'=4,'width'=2] {'tm'}, dimensions={0} | all-to-all | bytes 524288 | tf_op jit(solution)/shard_map/all_to_all | solution.py:489
  162.2 3.4 %all-to-all-start.5 = ((s16[4,2,4,32,128]{4,3,2,1,0:T(8,128)(2,1)}), s16[4,2,4,32,128]{4,3,2,1,0:T(8,128)(2,1)S(1)}, u32[]{:S(2)}, u32[]{:S(2)}) async-start(s16[4,2,4,32,128]{4,3,2,1,0:T(8,128)(2,1)} %shard_map.134), calls=%async_computation.5 | async-start | bytes 524288 | tf_op jit(solution)/shard_map/all_to_all | solution.py:489
  168.7 2.6 %all-to-all-done.5.value = s16[4,2,4,32,128]{4,3,2,1,0:T(8,128)(2,1)S(1)} async-done(((s16[4,2,4,32,128]{4,3,2,1,0:T(8,128)(2,1)}), s16[4,2,4,32,128]{4,3,2,1,0:T(8,128)(2,1)S(1)}, u32[]{:S(2)}, u32[]{:S(2)}) %all-to-all-start.5) | async-done | bytes 262176 | tf_op jit(solution)/shard_map/all_to_all | solution.py:489
  172.2 8.4 %all_to_all.41 = s16[4,4,4,32,128]{4,3,2,1,0:T(8,128)(2,1)S(1)} all-to-all(s16[4,4,4,32,128]{4,3,2,1,0:T(8,128)(2,1)S(1)} %get-tuple-element.58), channel_id=1, replica_groups=mesh['tm'=4,'height'=4,'width'=2] {'height'}, dimensions={0} | all-to-all | bytes 1048576 | tf_op jit(solution)/shard_map/all_to_all | solution.py:489
  180.6 3.5 %all-to-all-start.6 = ((s16[4,4,4,32,128]{4,3,2,1,0:T(8,128)(2,1)}), s16[4,4,4,32,128]{4,3,2,1,0:T(8,128)(2,1)S(1)}, u32[]{:S(2)}, u32[]{:S(2)}) async-start(s16[4,4,4,32,128]{4,3,2,1,0:T(8,128)(2,1)} %get-tuple-element.57), calls=%async_computation.6 | async-start | bytes 1048576 | tf_op jit(solution)/shard_map/all_to_all | solution.py:489
  184.1 5.3 %collective-permute-start.26 = (s16[64,32,128]{2,1,0:T(8,128)(2,1)S(1)}, s16[64,32,128]{2,1,0:T(8,128)(2,1)S(1)}, u32[]{:S(2)}, u32[]{:S(2)}) collective-permute-start(s16[64,32,128]{2,1,0:T(8,128)(2,1)S(1)} %bitcast.44), channel_id=1, source_target_pairs={{0,1},{1,0},{2,3},{3,2},{4,5},{5,4},{6,7},{7,6},{8,9},{9,8},{10,11... | collective-permute-start | bytes 1572872 | tf_op jit(solution)/shard_map/ppermute | solution.py:520
  189.5 6.4 %collective-permute-start.25 = (s16[64,32,128]{2,1,0:T(8,128)(2,1)S(1)}, s16[64,32,128]{2,1,0:T(8,128)(2,1)S(1)}, u32[]{:S(2)}, u32[]{:S(2)}) collective-permute-start(s16[64,32,128]{2,1,0:T(8,128)(2,1)S(1)} %bitcast.42), channel_id=1, source_target_pairs={{0,1},{1,0},{2,3},{3,2},{4,5},{5,4},{6,7},{7,6},{8,9},{9,8},{10,11... | collective-permute-start | bytes 1572872 | tf_op jit(solution)/shard_map/ppermute | solution.py:520
  195.9 3.9 %shard_map.137 = f32[128,3456]{1,0:T(8,128)} custom-call(s32[4]{0:T(128)S(1)} %pad_add_fusion.flag_ref, s16[64,32,128]{2,1,0:T(8,128)(2,1)S(1)} %bitcast.45, s16[64,32,128]{2,1,0:T(8,128)(2,1)S(1)} %collective-permute-done.26.theirs_ref), custom_call_target="tpu_custom_call" | custom-call | bytes 2818064 | tf_op jit(solution)/shard_map/pallas_call | solution.py:24
  199.8 3.9 %shard_map.136 = f32[128,3456]{1,0:T(8,128)} custom-call(s32[4]{0:T(128)S(1)} %pad_add_fusion.flag_ref, s16[64,32,128]{2,1,0:T(8,128)(2,1)S(1)} %bitcast.43, s16[64,32,128]{2,1,0:T(8,128)(2,1)S(1)} %collective-permute-done.25.theirs_ref), custom_call_target="tpu_custom_call" | custom-call | bytes 2818064 | tf_op jit(solution)/shard_map/pallas_call | solution.py:24
  (118 shorter events, 63.2 us)
Async XLA Ops:
  7.0 8.9 %collective-permute-start.6 = (f32[2,128]{1,0:T(2,128)S(1)}, f32[2,128]{1,0:T(2,128)S(1)}, u32[]{:S(2)}, u32[]{:S(2)}) collective-permute-start(f32[2,128]{1,0:T(2,128)S(1)} %slice_bitcast_fusion), channel_id=1, source_target_pairs={{0,8},{8,0},{16,24},{24,16},{1,9},{9,1},{17,25},{25,17},{2,10},{10... | collective-permute-start | bytes 3080 | tf_op jit(solution)/shard_map/ppermute | solution.py:500
  9.2 6.8 %collective-permute-start.7 = (f32[2,128]{1,0:T(2,128)S(1)}, f32[2,128]{1,0:T(2,128)S(1)}, u32[]{:S(2)}, u32[]{:S(2)}) collective-permute-start(f32[2,128]{1,0:T(2,128)S(1)} %slice_bitcast_fusion), channel_id=1, source_target_pairs={{0,16},{8,24},{16,0},{24,8},{1,17},{9,25},{17,1},{25,9},{2,18},{10... | collective-permute-start | bytes 3080 | tf_op jit(solution)/shard_map/ppermute | solution.py:500
  11.5 4.5 %collective-permute-start.8 = (f32[2,128]{1,0:T(2,128)S(1)}, f32[2,128]{1,0:T(2,128)S(1)}, u32[]{:S(2)}, u32[]{:S(2)}) collective-permute-start(f32[2,128]{1,0:T(2,128)S(1)} %slice_bitcast_fusion), channel_id=1, source_target_pairs={{0,24},{8,16},{16,8},{24,0},{1,25},{9,17},{17,9},{25,1},{2,26},{10... | collective-permute-start | bytes 3080 | tf_op jit(solution)/shard_map/ppermute | solution.py:500
  11.5 17.4 %collective-permute-start.1 = (bf16[2,2,128,256]{3,2,1,0:T(8,128)(2,1)S(1)}, bf16[2,2,128,256]{3,2,1,0:T(8,128)(2,1)S(1)}, u32[]{:S(2)}, u32[]{:S(2)}) collective-permute-start(bf16[2,2,128,256]{3,2,1,0:T(8,128)(2,1)S(1)} %get-tuple-element.32), channel_id=1, source_target_pairs={{0,2},{2,4},{4,6},{1,3},{3,5},{5,7},{8,10},{10,12},{12,14},{9,11},... | collective-permute-start | bytes 786440 | tf_op jit(solution)/shard_map/ppermute | solution.py:485
  14.6 14.2 %collective-permute-start.2 = (bf16[2,2,128,256]{3,2,1,0:T(8,128)(2,1)S(1)}, bf16[2,2,128,256]{3,2,1,0:T(8,128)(2,1)S(1)}, u32[]{:S(2)}, u32[]{:S(2)}) collective-permute-start(bf16[2,2,128,256]{3,2,1,0:T(8,128)(2,1)S(1)} %get-tuple-element.33), channel_id=1, source_target_pairs={{2,0},{4,2},{6,4},{3,1},{5,3},{7,5},{10,8},{12,10},{14,12},{11,9},... | collective-permute-start | bytes 786440 | tf_op jit(solution)/shard_map/ppermute | solution.py:485
  16.0 4.3 %collective-permute-start.10 = (f32[2,128]{1,0:T(2,128)S(1)}, f32[2,128]{1,0:T(2,128)S(1)}, u32[]{:S(2)}, u32[]{:S(2)}) collective-permute-start(f32[2,128]{1,0:T(2,128)S(1)} %pad_maximum_fusion), channel_id=1, source_target_pairs={{0,4},{2,6},{4,0},{6,2},{1,5},{3,7},{5,1},{7,3},{8,12},{10,14},{12... | collective-permute-start | bytes 3080 | tf_op jit(solution)/shard_map/ppermute | solution.py:500
  19.0 4.2 %collective-permute-start.11 = (f32[2,128]{1,0:T(2,128)S(1)}, f32[2,128]{1,0:T(2,128)S(1)}, u32[]{:S(2)}, u32[]{:S(2)}) collective-permute-start(f32[2,128]{1,0:T(2,128)S(1)} %pad_maximum_fusion), channel_id=1, source_target_pairs={{0,6},{2,4},{4,2},{6,0},{1,7},{3,5},{5,3},{7,1},{8,14},{10,12},{12... | collective-permute-start | bytes 3080 | tf_op jit(solution)/shard_map/ppermute | solution.py:500
  19.3 7.0 %collective-permute-start.9 = (f32[2,128]{1,0:T(2,128)S(1)}, f32[2,128]{1,0:T(2,128)S(1)}, u32[]{:S(2)}, u32[]{:S(2)}) collective-permute-start(f32[2,128]{1,0:T(2,128)S(1)} %pad_maximum_fusion), channel_id=1, source_target_pairs={{0,2},{2,0},{4,6},{6,4},{1,3},{3,1},{5,7},{7,5},{8,10},{10,8},{12,... | collective-permute-start | bytes 3080 | tf_op jit(solution)/shard_map/ppermute | solution.py:500
  20.3 20.9 %collective-permute-start = (bf16[4,2,128,256]{3,2,1,0:T(8,128)(2,1)S(1)}, bf16[4,2,128,256]{3,2,1,0:T(8,128)(2,1)S(1)}, u32[]{:S(2)}, u32[]{:S(2)}) collective-permute-start(bf16[4,2,128,256]{3,2,1,0:T(8,128)(2,1)S(1)} %get-tuple-element.31.first_ref.own.refs_7_.latent), channel_id=1, source_target_pairs={{0,8},{8,16},{16,24},{1,9},{9,17},{17,25},{2,10},{10,18},{18,26},{... | collective-permute-start | bytes 1572872 | tf_op jit(solution)/shard_map/ppermute | solution.py:485
  23.2 21.1 %collective-permute-start.13 = (bf16[4,2,128,256]{3,2,1,0:T(8,128)(2,1)S(1)}, bf16[4,2,128,256]{3,2,1,0:T(8,128)(2,1)S(1)}, u32[]{:S(2)}, u32[]{:S(2)}) collective-permute-start(bf16[4,2,128,256]{3,2,1,0:T(8,128)(2,1)S(1)} %get-tuple-element.36.first_ref.refs_0_.cotangent), channel_id=1, source_target_pairs={{8,0},{16,8},{24,16},{9,1},{17,9},{25,17},{10,2},{18,10},{26,18},{... | collective-permute-start | bytes 1572872 | tf_op jit(solution)/shard_map/ppermute | solution.py:485
  26.4 7.0 %collective-permute-start.12 = (f32[2,128]{1,0:T(2,128)S(1)}, f32[2,128]{1,0:T(2,128)S(1)}, u32[]{:S(2)}, u32[]{:S(2)}) collective-permute-start(f32[2,128]{1,0:T(2,128)S(1)} %pad_maximum_fusion.1), channel_id=1, source_target_pairs={{0,1},{1,0},{2,3},{3,2},{4,5},{5,4},{6,7},{7,6},{8,9},{9,8},{10,11... | collective-permute-start | bytes 3080 | tf_op jit(solution)/shard_map/ppermute | solution.py:500
  28.9 9.2 %collective-permute-start.3 = (bf16[2,2,128,256]{3,2,1,0:T(8,128)(2,1)S(1)}, bf16[2,2,128,256]{3,2,1,0:T(8,128)(2,1)S(1)}, u32[]{:S(2)}, u32[]{:S(2)}) collective-permute-start(bf16[2,2,128,256]{3,2,1,0:T(8,128)(2,1)S(1)} %get-tuple-element.34.first_ref.near), channel_id=1, source_target_pairs={{0,8},{8,16},{16,24},{1,9},{9,17},{17,25},{2,10},{10,18},{18,26},{... | collective-permute-start | bytes 786440 | tf_op jit(solution)/shard_map/ppermute | solution.py:485
  39.0 5.4 %collective-permute-start.5 = (bf16[128,128]{1,0:T(8,128)(2,1)S(1)}, bf16[128,128]{1,0:T(8,128)(2,1)S(1)}, u32[]{:S(2)}, u32[]{:S(2)}) collective-permute-start(bf16[128,128]{1,0:T(8,128)(2,1)S(1)} %shard_map.115), channel_id=1, source_target_pairs={{0,1},{1,0},{2,3},{3,2},{4,5},{5,4},{6,7},{7,6},{8,9},{9,8},{10,11... | collective-permute-start | bytes 98312 | tf_op jit(solution)/shard_map/ppermute | solution.py:520
  42.8 1.6 collective-permute-start.4
  42.9 10.5 %collective-permute-start.14 = (bf16[2,2,128,256]{3,2,1,0:T(8,128)(2,1)S(1)}, bf16[2,2,128,256]{3,2,1,0:T(8,128)(2,1)S(1)}, u32[]{:S(2)}, u32[]{:S(2)}) collective-permute-start(bf16[2,2,128,256]{3,2,1,0:T(8,128)(2,1)S(1)} %get-tuple-element.38.first_ref.refs_2_), channel_id=1, source_target_pairs={{8,0},{16,8},{24,16},{9,1},{17,9},{25,17},{10,2},{18,10},{26,18},{... | collective-permute-start | bytes 786440 | tf_op jit(solution)/shard_map/ppermute | solution.py:485
  55.2 9.9 %collective-permute-start.16 = (bf16[128,128]{1,0:T(8,128)(2,1)S(1)}, bf16[128,128]{1,0:T(8,128)(2,1)S(1)}, u32[]{:S(2)}, u32[]{:S(2)}) collective-permute-start(bf16[128,128]{1,0:T(8,128)(2,1)S(1)} %shard_map.119), channel_id=1, source_target_pairs={{0,1},{1,0},{2,3},{3,2},{4,5},{5,4},{6,7},{7,6},{8,9},{9,8},{10,11... | collective-permute-start | bytes 98312 | tf_op jit(solution)/shard_map/ppermute | solution.py:520
  57.9 7.2 %collective-permute-start.15 = (bf16[128,128]{1,0:T(8,128)(2,1)S(1)}, bf16[128,128]{1,0:T(8,128)(2,1)S(1)}, u32[]{:S(2)}, u32[]{:S(2)}) collective-permute-start(bf16[128,128]{1,0:T(8,128)(2,1)S(1)} %shard_map.118), channel_id=1, source_target_pairs={{0,1},{1,0},{2,3},{3,2},{4,5},{5,4},{6,7},{7,6},{8,9},{9,8},{10,11... | collective-permute-start | bytes 98312 | tf_op jit(solution)/shard_map/ppermute | solution.py:520
  59.8 14.6 %all-to-all-start = ((f32[32,2,128]{2,1,0:T(2,128)}), f32[32,2,128]{2,1,0:T(2,128)S(1)}, u32[]{:S(2)}, u32[]{:S(2)}) async-start(f32[32,2,128]{2,1,0:T(2,128)} %get-tuple-element.39.refs_0_), calls=%async_computation | async-start | bytes 65536 | tf_op jit(solution)/shard_map/all_to_all | solution.py:489
  77.8 15.1 %all-to-all-start.1 = ((f32[32,2,128]{2,1,0:T(2,128)}), f32[32,2,128]{2,1,0:T(2,128)S(1)}, u32[]{:S(2)}, u32[]{:S(2)}) async-start(f32[32,2,128]{2,1,0:T(2,128)} %get-tuple-element.42), calls=%async_computation.1 | async-start | bytes 65536 | tf_op jit(solution)/shard_map/all_to_all | solution.py:489
  92.6 24.0 %collective-permute-start.21 = (f32[64,32,128]{2,1,0:T(8,128)}, f32[64,32,128]{2,1,0:T(8,128)}, u32[]{:S(2)}, u32[]{:S(2)}) collective-permute-start(f32[64,32,128]{2,1,0:T(8,128)} %bitcast.13), channel_id=1, source_target_pairs={{0,1},{1,0},{2,3},{3,2},{4,5},{5,4},{6,7},{7,6},{8,9},{9,8},{10,11... | collective-permute-start | bytes 3145736 | tf_op jit(solution)/shard_map/ppermute | solution.py:520
  103.0 13.7 %collective-permute-start.22 = (f32[64,32,128]{2,1,0:T(8,128)S(1)}, f32[64,32,128]{2,1,0:T(8,128)S(1)}, u32[]{:S(2)}, u32[]{:S(2)}) collective-permute-start(f32[64,32,128]{2,1,0:T(8,128)S(1)} %bitcast.47), channel_id=1, source_target_pairs={{0,1},{1,0},{2,3},{3,2},{4,5},{5,4},{6,7},{7,6},{8,9},{9,8},{10,11... | collective-permute-start | bytes 3145736 | tf_op jit(solution)/shard_map/ppermute | solution.py:520
  103.3 24.7 %collective-permute-start.17 = (bf16[4,2,128,256]{3,2,1,0:T(8,128)(2,1)}, bf16[4,2,128,256]{3,2,1,0:T(8,128)(2,1)S(1)}, u32[]{:S(2)}, u32[]{:S(2)}) collective-permute-start(bf16[4,2,128,256]{3,2,1,0:T(8,128)(2,1)} %get-tuple-element.46.grad_ref.first_ref.refs_0_), channel_id=1, source_target_pairs={{8,0},{16,8},{24,16},{9,1},{17,9},{25,17},{10,2},{18,10},{26,18},{... | collective-permute-start | bytes 1572872 | tf_op jit(solution)/shard_map/ppermute | solution.py:485
  104.6 5.8 %collective-permute-start.18 = (bf16[1,2,128,256]{3,2,1,0:T(8,128)(2,1)S(1)}, bf16[1,2,128,256]{3,2,1,0:T(8,128)(2,1)S(1)}, u32[]{:S(2)}, u32[]{:S(2)}) collective-permute-start(bf16[1,2,128,256]{3,2,1,0:T(8,128)(2,1)S(1)} %get-tuple-element.47), channel_id=1, source_target_pairs={{0,2},{2,4},{4,6},{1,3},{3,5},{5,7},{8,10},{10,12},{12,14},{9,11},... | collective-permute-start | bytes 393224 | tf_op jit(solution)/shard_map/ppermute | solution.py:485
  107.9 7.5 %collective-permute-start.19 = (bf16[1,2,128,256]{3,2,1,0:T(8,128)(2,1)S(1)}, bf16[1,2,128,256]{3,2,1,0:T(8,128)(2,1)S(1)}, u32[]{:S(2)}, u32[]{:S(2)}) collective-permute-start(bf16[1,2,128,256]{3,2,1,0:T(8,128)(2,1)S(1)} %get-tuple-element.48), channel_id=1, source_target_pairs={{2,0},{4,2},{6,4},{3,1},{5,3},{7,5},{10,8},{12,10},{14,12},{11,9},... | collective-permute-start | bytes 393224 | tf_op jit(solution)/shard_map/ppermute | solution.py:485
  115.4 9.1 %collective-permute-start.20 = (bf16[2,2,128,256]{3,2,1,0:T(8,128)(2,1)S(1)}, bf16[2,2,128,256]{3,2,1,0:T(8,128)(2,1)S(1)}, u32[]{:S(2)}, u32[]{:S(2)}) collective-permute-start(bf16[2,2,128,256]{3,2,1,0:T(8,128)(2,1)S(1)} %shard_map.125.first_ref.refs_2_.refs_1_), channel_id=1, source_target_pairs={{8,0},{16,8},{24,16},{9,1},{17,9},{25,17},{10,2},{18,10},{26,18},{... | collective-permute-start | bytes 786440 | tf_op jit(solution)/shard_map/ppermute | solution.py:485
  119.6 18.3 %all-to-all-start.3 = ((s16[4,2,16,32,128]{4,3,2,1,0:T(8,128)(2,1)}), s16[4,2,16,32,128]{4,3,2,1,0:T(8,128)(2,1)S(1)}, u32[]{:S(2)}, u32[]{:S(2)}) async-start(s16[4,2,16,32,128]{4,3,2,1,0:T(8,128)(2,1)} %shard_map.127.refs_0_), calls=%async_computation.3 | async-start | bytes 2097152 | tf_op jit(solution)/shard_map/all_to_all | solution.py:489
  126.1 4.8 %collective-permute-start.24 = (bf16[128,128]{1,0:T(8,128)(2,1)S(1)}, bf16[128,128]{1,0:T(8,128)(2,1)S(1)}, u32[]{:S(2)}, u32[]{:S(2)}) collective-permute-start(bf16[128,128]{1,0:T(8,128)(2,1)S(1)} %shard_map.129), channel_id=1, source_target_pairs={{0,1},{1,0},{2,3},{3,2},{4,5},{5,4},{6,7},{7,6},{8,9},{9,8},{10,11... | collective-permute-start | bytes 98312 | tf_op jit(solution)/shard_map/ppermute | solution.py:520
  137.8 12.9 %all-to-all-start.2 = ((f32[32,2,128]{2,1,0:T(2,128)}), f32[32,2,128]{2,1,0:T(2,128)S(1)}, u32[]{:S(2)}, u32[]{:S(2)}) async-start(f32[32,2,128]{2,1,0:T(2,128)} %get-tuple-element.54), calls=%async_computation.2 | async-start | bytes 65536 | tf_op jit(solution)/shard_map/all_to_all | solution.py:489
  162.2 9.1 %all-to-all-start.5 = ((s16[4,2,4,32,128]{4,3,2,1,0:T(8,128)(2,1)}), s16[4,2,4,32,128]{4,3,2,1,0:T(8,128)(2,1)S(1)}, u32[]{:S(2)}, u32[]{:S(2)}) async-start(s16[4,2,4,32,128]{4,3,2,1,0:T(8,128)(2,1)} %shard_map.134), calls=%async_computation.5 | async-start | bytes 524288 | tf_op jit(solution)/shard_map/all_to_all | solution.py:489
  180.6 8.9 %all-to-all-start.6 = ((s16[4,4,4,32,128]{4,3,2,1,0:T(8,128)(2,1)}), s16[4,4,4,32,128]{4,3,2,1,0:T(8,128)(2,1)S(1)}, u32[]{:S(2)}, u32[]{:S(2)}) async-start(s16[4,4,4,32,128]{4,3,2,1,0:T(8,128)(2,1)} %get-tuple-element.57), calls=%async_computation.6 | async-start | bytes 1048576 | tf_op jit(solution)/shard_map/all_to_all | solution.py:489
  184.1 11.8 %collective-permute-start.26 = (s16[64,32,128]{2,1,0:T(8,128)(2,1)S(1)}, s16[64,32,128]{2,1,0:T(8,128)(2,1)S(1)}, u32[]{:S(2)}, u32[]{:S(2)}) collective-permute-start(s16[64,32,128]{2,1,0:T(8,128)(2,1)S(1)} %bitcast.44), channel_id=1, source_target_pairs={{0,1},{1,0},{2,3},{3,2},{4,5},{5,4},{6,7},{7,6},{8,9},{9,8},{10,11... | collective-permute-start | bytes 1572872 | tf_op jit(solution)/shard_map/ppermute | solution.py:520
  189.5 10.2 %collective-permute-start.25 = (s16[64,32,128]{2,1,0:T(8,128)(2,1)S(1)}, s16[64,32,128]{2,1,0:T(8,128)(2,1)S(1)}, u32[]{:S(2)}, u32[]{:S(2)}) collective-permute-start(s16[64,32,128]{2,1,0:T(8,128)(2,1)S(1)} %bitcast.42), channel_id=1, source_target_pairs={{0,1},{1,0},{2,3},{3,2},{4,5},{5,4},{6,7},{7,6},{8,9},{9,8},{10,11... | collective-permute-start | bytes 1572872 | tf_op jit(solution)/shard_map/ppermute | solution.py:520
  (22 other events, 59.7 us)

commit v7 on v6

--- a/solution.py
+++ b/solution.py
@@ -79,15 +79,11 @@
 
 
 def put_rows(out_ref, first, second):
-    out_ref[...] = jnp.broadcast_to(as_rows(first, second)[None], out_ref.shape)
+    out_ref[0] = as_rows(first, second)
 
 
 def combined(st_ref, count):
-    devices = st_ref.shape[0]
-    mean = jnp.mean(st_ref[:, 0:1], axis=0)
-    off = st_ref[:, 0:1] - mean[None]
-    squares = jnp.sum(st_ref[:, 1:2] + off * off * (count / devices), axis=0)
-    return mean, squares / count
+    return st_ref[0, 0:1], st_ref[0, 1:2] / count
 
 
 def columns_of(*rows):
@@ -281,7 +277,7 @@
 ):
     rows, frames, channels, cols = hidden.shape
     mean, inverse, _, _, _ = norm_columns(par_ref, st_ref, count, 3)
-    means = jnp.sum(sums_ref[...], axis=0) / count
+    means = sums_ref[0] / count
     first, second = columns_of(means[0:1], means[1:2])[:2]
     for row in range(rows):
         for frame in range(frames):
@@ -317,43 +313,44 @@
     return number * (jnp.exp(number[:, SLOTS - 1 : SLOTS] * LN2) * (1.0 / FULL))
 
 
-def first_scatter_kernel(*refs):
-    out_ref = refs[-1]
-    chunks, _, rows = out_ref.shape[:3]
+def first_scatter_kernel(flag_ref, *refs, slot):
+    me = flag_ref[slot]
     for which in range(2):
-        mine_ref, other_ref = refs[2 * which], refs[2 * which + 1]
-        for chunk in range(chunks):
-            here = slice(chunk * rows, (chunk + 1) * rows)
-            out_ref[chunk, which] = encoded(mine_ref[here] + other_ref[here])
-
-
-def second_scatter_kernel(received, *refs):
-    out_ref = refs[-1]
-    chunks, _, rows = out_ref.shape[:3]
+        mine, other = refs[2 * which], refs[2 * which + 1]
+        for k, out in enumerate(refs[4:]):
+            total = mine[me ^ k] + other[me ^ k]
+            out[which] = total if k == 0 else encoded(total)
+
+
+def scatter_kernel(flag_ref, *refs, received, sent, slot):
+    me = flag_ref[slot]
     for which in range(2):
-        for chunk in range(chunks):
-            here = slice(chunk * rows, (chunk + 1) * rows)
-            total = decoded_value(received[0, which, here])
-            for number in range(1, received.shape[0]):
-                total = total + decoded_value(received[number, which, here])
-            out_ref[chunk, which] = encoded(total)
-
-
-def total_kernel(received, *refs):
-    out_ref = refs[-1]
+        for k, out in enumerate(refs[-sent:]):
+            total = refs[0][which, me ^ k]
+            for ref in refs[1:received]:
+                total = total + decoded_value(ref[which, me ^ k])
+            out[which] = total if k == 0 else encoded(total)
+
+
+def total_kernel(*refs, received):
     for which in range(2):
-        total = decoded_value(received[0, which])
-        for number in range(1, received.shape[0]):
-            total = total + decoded_value(received[number, which])
-        total = encoded(total)
-        for copy in range(out_ref.shape[0]):
-            out_ref[copy, which] = total
-
-
-def copies_kernel(value, after, *outs):
-    for which, out_ref in enumerate(outs):
-        for copy in range(out_ref.shape[0]):
-            out_ref[copy] = value[:, which]
+        total = refs[0][which]
+        for ref in refs[1:received]:
+            total = total + decoded_value(ref[which])
+        refs[-1][which] = encoded(total)
+
+
+def split_kernel(flag_ref, *refs, received, slot):
+    me = flag_ref[slot]
+    for which in range(2):
+        for k, ref in enumerate(refs[:received]):
+            refs[which - 2][me ^ k] = ref[which]
+
+
+def gather_kernel(flag_ref, *refs, slot):
+    me = flag_ref[slot]
+    for k, ref in enumerate(refs[:-1]):
+        refs[-1][me ^ k] = ref[...]
 
 
 def join_kernel(flag_ref, mine_ref, theirs_ref, out_ref, first_ref, second_ref):
@@ -431,7 +428,7 @@
     token_ref[...] = jnp.zeros(token_ref.shape, F32)
     rows, frames, channels, cols = latent.shape
     mean, inverse, _, _, scale = norm_columns(par_ref, st_ref, count, 1)
-    means = jnp.sum(sums_ref[...], axis=0) / count
+    means = sums_ref[0] / count
     first, second = columns_of(means[0:1], means[1:2])[:2]
     for row in range(rows):
         for frame in range(frames):
@@ -485,78 +482,114 @@
     return lax.ppermute(value, axis, [(source, source + steps) for source in range(initial, last)])
 
 
-def exchanged(value, axis):
-    return lax.all_to_all(value, axis, 0, 0, tiled=True)
+def rounds(axes):
+    for axis in axes:
+        count = lax.axis_size(axis)
+        step = 1
+        while step < count:
+            wide = 4 if 4 * step <= count else 2
+            yield axis, step, [[(i, i ^ (step * k)) for i in range(count)] for k in range(1, wide)]
+            step *= wide
+
+
+def pairwise(parts, join):
+    while len(parts) > 1:
+        parts = [join(a, b) for a, b in zip(parts[::2], parts[1::2])]
+    return parts[0]
+
+
+def all_sum(value):
+    for axis, _, exchanges in rounds(("tm", "height", "width")):
+        parts = [value] + [lax.ppermute(value, axis, pairs) for pairs in exchanges]
+        value = pairwise(parts, lambda a, b: a + b)
+    return value
 
 
 def all_stats(value, count):
-    value = value[0]
-    for axis in ("tm", "height", "width"):
-        size = lax.axis_size(axis)
-        step = 1
-        while step < size:
-            wide = 4 if 4 * step <= size else 2
-            parts = [value] + [
-                lax.ppermute(value, axis, [(i, i ^ (step * k)) for i in range(size)]) for k in range(1, wide)
-            ]
-            while len(parts) > 1:
-                joined = []
-                for a, b in zip(parts[::2], parts[1::2]):
-                    gap = a[0:1] - b[0:1]
-                    mean = 0.5 * (a[0:1] + b[0:1])
-                    joined.append(jnp.concatenate([mean, a[1:2] + b[1:2] + gap * gap * (0.5 * count)], axis=0))
-                parts = joined
-                count = 2.0 * count
-            (value,) = parts
-            step *= wide
-    return value[None]
-
-
-def shared(value):
-    return exchanged(value, ("tm", "height", "width"))
+    for axis, _, exchanges in rounds(("tm", "height", "width")):
+        parts = [(value, count)] + [(lax.ppermute(value, axis, pairs), count) for pairs in exchanges]
+        value, count = pairwise(parts, joined_stats)
+    return value
+
+
+def joined_stats(first, second):
+    (a, count), (b, _) = first, second
+    gap = a[:, 0:1] - b[:, 0:1]
+    squares = a[:, 1:2] + b[:, 1:2] + gap * gap * (0.5 * count)
+    return jnp.concatenate([0.5 * (a[:, 0:1] + b[:, 0:1]), squares], axis=1), 2.0 * count
 
 
 def swapped(value):
     return lax.ppermute(value, "width", [(0, 1), (1, 0)])
 
 
-def scattered(second, first):
+def weight_rounds():
+    return list(rounds(("height", "tm")))
+
+
+def scattered(flags, second, first):
     half, _, channels = second[0].shape
-    by_height = lax.axis_size("height")
+    axis, _, exchanges = weight_rounds()[0]
+    parts = len(exchanges) + 1
+    rows = half // parts
     terms = [part for mine, theirs in (second, first) for part in (mine, swapped(theirs))]
-    (value,) = call(
-        first_scatter_kernel,
-        [shape((by_height, 2, half // by_height, SLOTS, channels), jnp.int16)],
-        [VMEM] * 4,
-        terms,
-    )
-    return exchanged(value, "height"), value
-
-
-def summed(value, after):
-    by_tm = lax.axis_size("tm")
-    _, _, rows, _, channels = value.shape
-    (value,) = call(
-        second_scatter_kernel,
-        [shape((by_tm, 2, rows // by_tm, SLOTS, channels), jnp.int16)],
-        [VMEM] * (1 + len(after)),
-        (value, *after),
-    )
-    return exchanged(value, "tm")
-
-
-def gathered(value, after, after_last):
-    (value,) = call(total_kernel, [shape(value.shape, jnp.int16)], [VMEM] * (1 + len(after)), (value, *after))
-    value = exchanged(value, "tm")
-    by_height = lax.axis_size("height")
-    by_tm, _, rows, _, channels = value.shape
-    copies = call(
-        copies_kernel,
-        [shape((by_height, by_tm, rows, SLOTS, channels), jnp.int16)] * 2,
-        [VMEM] * 2,
-        (value, after_last),
-    )
-    return [exchanged(copy, "height").reshape(-1, SLOTS, channels) for copy in copies]
+    part = (2, rows, SLOTS, channels)
+    kept, *sent = call(
+        functools.partial(first_scatter_kernel, slot=4),
+        [shape(part, F32)] + [shape(part, jnp.int16)] * (parts - 1),
+        [SMEM] + [VMEM] * 4,
+        (flags, *[term.reshape(parts, rows, SLOTS, channels) for term in terms]),
+    )
+    return [kept] + [lax.ppermute(v, axis, pairs) for v, pairs in zip(sent, exchanges)], sent[0]
+
+
+def summed(flags, received, after):
+    for number, (axis, _, exchanges) in enumerate(weight_rounds()[1:], 5):
+        parts = len(exchanges) + 1
+        _, rows, _, channels = received[0].shape
+        part = (2, rows // parts, SLOTS, channels)
+        views = [v.reshape(2, parts, *part[1:]) for v in received]
+        kept, *sent = call(
+            functools.partial(scatter_kernel, received=len(views), sent=parts, slot=number),
+            [shape(part, F32)] + [shape(part, jnp.int16)] * (parts - 1),
+            [SMEM] + [VMEM] * (len(views) + len(after)),
+            (flags, *views, *after),
+        )
+        after = ()
+        received = [kept] + [lax.ppermute(v, axis, pairs) for v, pairs in zip(sent, exchanges)]
+    return received
+
+
+def gathered(flags, received, after, after_last):
+    (total,) = call(
+        functools.partial(total_kernel, received=len(received)),
+        [shape(received[0].shape, jnp.int16)],
+        [VMEM] * (len(received) + len(after)),
+        (*received, *after),
+    )
+    _, rows, _, channels = total.shape
+    back = list(enumerate(weight_rounds(), 4))[::-1]
+    number, (axis, _, exchanges) = back[0]
+    pieces = [total] + [lax.ppermute(total, axis, pairs) for pairs in exchanges]
+    values = call(
+        functools.partial(split_kernel, received=len(pieces), slot=number),
+        [shape((len(pieces), rows, SLOTS, channels), jnp.int16)] * 2,
+        [SMEM] + [VMEM] * (len(pieces) + 1),
+        (flags, *pieces, after_last),
+    )
+    results = []
+    for value in values:
+        for number, (axis, _, exchanges) in back[1:]:
+            value = value.reshape(-1, SLOTS, channels)
+            pieces = [value] + [lax.ppermute(value, axis, pairs) for pairs in exchanges]
+            (value,) = call(
+                functools.partial(gather_kernel, slot=number),
+                [shape((len(pieces), *value.shape), jnp.int16)],
+                [SMEM] + [VMEM] * len(pieces),
+                (flags, *pieces),
+            )
+        results.append(value.reshape(-1, SLOTS, channels))
+    return results
 
 
 def joined(flags, mine, theirs):
@@ -616,6 +649,10 @@
             (height < lax.axis_size("height") - 1).astype(jnp.int32),
             width.astype(jnp.int32),
         ]
+        + [
+            (lax.axis_index(axis) // step % (len(exchanges) + 1)).astype(jnp.int32)
+            for axis, step, exchanges in weight_rounds()
+        ]
     )
     scale = jnp.repeat(jnp.exp2(exponents.astype(F32)), channels // groups)
     zeros = jnp.zeros_like(scale)
@@ -625,7 +662,7 @@
     taps = (2 * channels, 36 * channels)
     halves = [shape((channels // 2 * SLOTS, channels), F32)] * 2
     conv_flops = 3 * 2 * 4 * 256 * 36 * channels * 2 * channels
-    small = shape((devices, 2, channels), F32)
+    small = shape((1, 2, channels), F32)
 
     message = shape((2, frames, channels, cols), BF16)
     latent, cotangent, down, up, stats_first = call(
@@ -651,7 +688,7 @@
         transcendentals=3 * latent.size,
     )
     around_c = with_columns(flags, cotangent, around_c, (stats_second,))
-    stats_second = shared(stats_second)
+    stats_second = all_stats(stats_second, count / devices)
     grad_second, stack_c = call(
         conv_back_kernel,
         [shape(block, F32), shape(stack, BF16)],
@@ -666,7 +703,7 @@
         (hidden, grad_second, par, stats_second),
         transcendentals=latent.size,
     )
-    sums = shared(sums)
+    sums = all_sum(sums)
     halves_second = call(
         weight_second_kernel,
         halves,
@@ -695,7 +732,7 @@
     halves_second, halves_first = (
         [v.reshape(channels // 2, SLOTS, channels) for v in halves] for halves in (halves_second, halves_first)
     )
-    weights, sent = scattered(halves_second, halves_first)
+    weights, sent = scattered(flags, halves_second, halves_first)
     around = with_columns(flags, hidden_grad, around, (sent,))
     scaled, sums_first = call(
         functools.partial(first_grad_kernel, count=count),
@@ -706,15 +743,15 @@
         flops=conv_flops,
         transcendentals=latent.size,
     )
-    weights = summed(weights, around[:2])
-    sums_first = shared(sums_first)
+    weights = summed(flags, weights, around[:2])
+    sums_first = all_sum(sums_first)
     decoded_grad, token = call(
         functools.partial(decoded_grad_kernel, count=count),
         [shape((channels, frames, rows, cols), F32), shape((8, 128), F32)],
         [VMEM] * 6,
         (scaled, latent, cotangent, par, stats_first, sums_first),
     )
-    second, first = gathered(weights, (sums_first,), token)
+    second, first = gathered(flags, weights, (sums_first,), token)
     conv_second_grad = joined(flags, second, swapped(second))
     conv_first_grad = joined(flags, first, swapped(first))
     return decoded_grad, conv_first_grad, conv_second_grad

time: 205 us -> 192 us (0.937)
  starting transfers between devices: 76 us -> 101 us
  local copies, waits for them, and re-layouts: 25.1 us -> 4.96 us
  blocking collectives: 19 us -> 0 us
  waiting for transfers between devices: 26.2 us -> 32.8 us
  Pallas kernels: 55.3 us -> 50.7 us
    ppermute x7 -> x43, starting transfers between devices: 11.3 us -> 59.6 us  [the longest x14 24.1 us: all_stats(): lax.ppermute(value, axis, pairs)]
    all_to_all x6 -> x0, starting transfers between devices: 27.5 us -> none  [exchanged(): return lax.all_to_all(value, axis, 0, 0, tiled=True)]
    unnamed x42 -> x14, local copies, waits for them, and re-layouts: 24.2 us -> 3.96 us
    all_to_all x2 -> x0, blocking collectives: 19 us -> none  [exchanged(): return lax.all_to_all(value, axis, 0, 0, tiled=True)]
    ppermute x7 -> x43, waiting for transfers between devices: 2.47 us -> 17.3 us  [the longest x14 8.24 us: all_sum(): parts = [value] + [lax.ppermute(value, axis, pairs) for pairs in exchanges]]
    all_to_all x6 -> x0, waiting for transfers between devices: 9.33 us -> none  [exchanged(): return lax.all_to_all(value, axis, 0, 0, tiled=True)]
    pallas_call x26 -> x28, Pallas kernels: 55.3 us -> 50.7 us  [call(): pl.pallas_call(body, out_shape=tuple(outs), in_specs=specs, out_specs=tup...]
    ppermute x10, starting transfers between devices: 17.7 us -> 20.6 us  [swapped(): return lax.ppermute(value, 'width', [(0, 1), (1, 0)])]
  transfers between devices with their start and end apart: 33 -> 63, of which waited for: 11 -> 20; matrix products, arithmetic and copies ran while one was open for 0% -> 0% of each run, Pallas kernels for 22% -> 17%
where the time goes in v7:
time: 192 us; the launch traced here: 191 us
  starting transfers between devices  101 us (53%)
  Pallas kernels  50.7 us (26%)
  waiting for transfers between devices  32.8 us (17%)
  local copies, waits for them, and re-layouts  4.96 us (3%)
    pallas_call x28, Pallas kernels, call(): pl.pallas_call(body, out_shape=tuple(outs), in_specs=specs, out_specs=tup...  50.7 us
    ppermute x14, starting transfers between devices, all_stats(): lax.ppermute(value, axis, pairs)  24.1 us
    ppermute x10, starting transfers between devices, swapped(): return lax.ppermute(value, 'width', [(0, 1), (1, 0)])  20.6 us
    ppermute x10, starting transfers between devices, shifted(): lax.ppermute(value, axis, [(source, source + steps) for source in range(i...  20.4 us
    ppermute x14, starting transfers between devices, all_sum(): parts = [value] + [lax.ppermute(value, axis, pairs) for pairs in exchanges]  20.2 us
    ppermute x10, waiting for transfers between devices, shifted(): lax.ppermute(value, axis, [(source, source + steps) for source in range(i...  13.2 us
    ppermute x14, waiting for transfers between devices, all_sum(): parts = [value] + [lax.ppermute(value, axis, pairs) for pairs in exchanges]  8.24 us
    ppermute x14, waiting for transfers between devices, all_stats(): lax.ppermute(value, axis, pairs)  6.83 us
  transfers between devices with their start and end apart: 63, of which 20 were waited for; matrix products, arithmetic and copies ran while one was open for 0% of the time, Pallas kernels for 17%

profile of v7, /device:TPU:1, one launch (start us, length us, event | category | flops | bytes accessed | tf_op | source)
XLA Modules:
  0.0 191.1 jit_solution(3387938785784079103)
XLA Ops:
  4.3 2.6 %shard_map.112 = (bf16[4,2,128,256]{3,2,1,0:T(8,128)(2,1)S(1)}, bf16[4,2,128,256]{3,2,1,0:T(8,128)(2,1)S(1)}, bf16[2,2,128,256]{3,2,1,0:T(8,128)(2,1)S(1)}, bf16...) custom-call(bf16[128,2,4,256]{3,2,1,0:T(4,128)(2,1)S(1)} %copy-done.3, bf16[128,2,4,256]{3,2,1,0:T(4,128)(2,1)S(1)} %copy-done.4, ...), custom_call_target="tpu_custom_call" | custom-call | bytes 2626560 | tf_op jit(solution)/shard_map/pallas_call | solution.py:24
  7.0 2.2 %collective-permute-start.6 = (f32[1,2,128]{2,1,0:T(2,128)S(1)}, f32[1,2,128]{2,1,0:T(2,128)S(1)}, u32[]{:S(2)}, u32[]{:S(2)}) collective-permute-start(f32[1,2,128]{2,1,0:T(2,128)S(1)} %get-tuple-element.43), channel_id=1, source_target_pairs={{0,8},{8,0},{16,24},{24,16},{1,9},{9,1},{17,25},{25,17},{2,10},{10... | collective-permute-start | bytes 3080 | tf_op jit(solution)/shard_map/ppermute | solution.py:510
  9.2 2.3 %collective-permute-start.7 = (f32[1,2,128]{2,1,0:T(2,128)S(1)}, f32[1,2,128]{2,1,0:T(2,128)S(1)}, u32[]{:S(2)}, u32[]{:S(2)}) collective-permute-start(f32[1,2,128]{2,1,0:T(2,128)S(1)} %get-tuple-element.43), channel_id=1, source_target_pairs={{0,16},{8,24},{16,0},{24,8},{1,17},{9,25},{17,1},{25,9},{2,18},{10... | collective-permute-start | bytes 3080 | tf_op jit(solution)/shard_map/ppermute | solution.py:510
  11.5 3.1 %collective-permute-start.1 = (bf16[2,2,128,256]{3,2,1,0:T(8,128)(2,1)S(1)}, bf16[2,2,128,256]{3,2,1,0:T(8,128)(2,1)S(1)}, u32[]{:S(2)}, u32[]{:S(2)}) collective-permute-start(bf16[2,2,128,256]{3,2,1,0:T(8,128)(2,1)S(1)} %get-tuple-element.40), channel_id=1, source_target_pairs={{0,2},{2,4},{4,6},{1,3},{3,5},{5,7},{8,10},{10,12},{12,14},{9,11},... | collective-permute-start | bytes 786440 | tf_op jit(solution)/shard_map/ppermute | solution.py:482
  16.0 3.1 %collective-permute-start.10 = (f32[1,2,128]{2,1,0:T(2,128)S(1)}, f32[1,2,128]{2,1,0:T(2,128)S(1)}, u32[]{:S(2)}, u32[]{:S(2)}) collective-permute-start(f32[1,2,128]{2,1,0:T(2,128)S(1)} %pad_maximum_fusion), channel_id=1, source_target_pairs={{0,4},{2,6},{4,0},{6,2},{1,5},{3,7},{5,1},{7,3},{8,12},{10,14},{12... | collective-permute-start | bytes 3080 | tf_op jit(solution)/shard_map/ppermute | solution.py:510
  20.3 3.0 %collective-permute-start = (bf16[4,2,128,256]{3,2,1,0:T(8,128)(2,1)S(1)}, bf16[4,2,128,256]{3,2,1,0:T(8,128)(2,1)}, u32[]{:S(2)}, u32[]{:S(2)}) collective-permute-start(bf16[4,2,128,256]{3,2,1,0:T(8,128)(2,1)S(1)} %get-tuple-element.39.first_ref.own.refs_7_.latent), channel_id=1, source_target_pairs={{0,8},{8,16},{16,24},{1,9},{9,17},{17,25},{2,10},{10,18},{18,26},{... | collective-permute-start | bytes 1572872 | tf_op jit(solution)/shard_map/ppermute | solution.py:482
  27.8 3.0 %collective-permute-start.3 = (bf16[2,2,128,256]{3,2,1,0:T(8,128)(2,1)}, bf16[2,2,128,256]{3,2,1,0:T(8,128)(2,1)}, u32[]{:S(2)}, u32[]{:S(2)}) collective-permute-start(bf16[2,2,128,256]{3,2,1,0:T(8,128)(2,1)} %get-tuple-element.42.first_ref.near), channel_id=1, source_target_pairs={{0,8},{8,16},{16,24},{1,9},{9,17},{17,25},{2,10},{10,18},{18,26},{... | collective-permute-start | bytes 786440 | tf_op jit(solution)/shard_map/ppermute | solution.py:482
  30.8 3.5 %collective-permute-start.12 = (f32[1,2,128]{2,1,0:T(2,128)S(1)}, f32[1,2,128]{2,1,0:T(2,128)S(1)}, u32[]{:S(2)}, u32[]{:S(2)}) collective-permute-start(f32[1,2,128]{2,1,0:T(2,128)S(1)} %pad_maximum_fusion.1), channel_id=1, source_target_pairs={{0,1},{1,0},{2,3},{3,2},{4,5},{5,4},{6,7},{7,6},{8,9},{9,8},{10,11... | collective-permute-start | bytes 3080 | tf_op jit(solution)/shard_map/ppermute | solution.py:510
  38.2 3.6 %collective-permute-start.5 = (bf16[128,128]{1,0:T(8,128)(2,1)S(1)}, bf16[128,128]{1,0:T(8,128)(2,1)S(1)}, u32[]{:S(2)}, u32[]{:S(2)}) collective-permute-start(bf16[128,128]{1,0:T(8,128)(2,1)S(1)} %shard_map.115), channel_id=1, source_target_pairs={{0,1},{1,0},{2,3},{3,2},{4,5},{5,4},{6,7},{7,6},{8,9},{9,8},{10,11... | collective-permute-start | bytes 98312 | tf_op jit(solution)/shard_map/ppermute | solution.py:523
  45.1 5.4 %shard_map.117 = (f32[4,2,128,256]{3,2,1,0:T(8,128)S(1)}, f32[1,2,128]{2,1,0:T(2,128)S(1)}, bf16[6,4,384,256]{3,2,1,0:T(8,128)(2,1)S(1)}) custom-call(s32[6]{0:T(128)S(1)} %stack.57.flag_ref, bf16[4,2,128,256]{3,2,1,0:T(8,128)(2,1)S(1)} %get-tuple-element.39.first_ref.own.refs_7_.latent, bf16[4,2,128,256]{3,2,1,0:T(8,128)(2,1)} %collective-permute-done.second_ref.past, ...), custom_call_target="tpu_custom_call" | custom-call | flops 7247757312 | bytes 10295320 | tf_op jit(solution)/shard_map/pallas_call | solution.py:24
  50.6 2.2 %collective-permute-start.17 = (f32[1,2,128]{2,1,0:T(2,128)S(1)}, f32[1,2,128]{2,1,0:T(2,128)S(1)}, u32[]{:S(2)}, u32[]{:S(2)}) collective-permute-start(f32[1,2,128]{2,1,0:T(2,128)S(1)} %get-tuple-element.47.refs_0_), channel_id=1, source_target_pairs={{0,8},{8,0},{16,24},{24,16},{1,9},{9,1},{17,25},{25,17},{2,10},{10... | collective-permute-start | bytes 3080 | tf_op jit(solution)/shard_map/ppermute | solution.py:510
  52.8 3.2 %collective-permute-start.18 = (f32[1,2,128]{2,1,0:T(2,128)S(1)}, f32[1,2,128]{2,1,0:T(2,128)S(1)}, u32[]{:S(2)}, u32[]{:S(2)}) collective-permute-start(f32[1,2,128]{2,1,0:T(2,128)S(1)} %get-tuple-element.47.refs_0_), channel_id=1, source_target_pairs={{0,16},{8,24},{16,0},{24,8},{1,17},{9,25},{17,1},{25,9},{2,18},{10... | collective-permute-start | bytes 3080 | tf_op jit(solution)/shard_map/ppermute | solution.py:510
  57.0 3.3 %collective-permute-done.19 = f32[1,2,128]{2,1,0:T(2,128)S(1)} collective-permute-done((f32[1,2,128]{2,1,0:T(2,128)S(1)}, f32[1,2,128]{2,1,0:T(2,128)S(1)}, u32[]{:S(2)}, u32[]{:S(2)}) %collective-permute-start.19) | collective-permute-done | bytes 1056 | tf_op jit(solution)/shard_map/ppermute | solution.py:510
  65.4 3.6 %collective-permute-start.23 = (f32[1,2,128]{2,1,0:T(2,128)S(1)}, f32[1,2,128]{2,1,0:T(2,128)S(1)}, u32[]{:S(2)}, u32[]{:S(2)}) collective-permute-start(f32[1,2,128]{2,1,0:T(2,128)S(1)} %pad_maximum_fusion.4), channel_id=1, source_target_pairs={{0,1},{1,0},{2,3},{3,2},{4,5},{5,4},{6,7},{7,6},{8,9},{9,8},{10,11... | collective-permute-start | bytes 3080 | tf_op jit(solution)/shard_map/ppermute | solution.py:510
  71.0 3.9 %collective-permute-start.16 = (bf16[128,128]{1,0:T(8,128)(2,1)S(1)}, bf16[128,128]{1,0:T(8,128)(2,1)S(1)}, u32[]{:S(2)}, u32[]{:S(2)}) collective-permute-start(bf16[128,128]{1,0:T(8,128)(2,1)S(1)} %shard_map.119), channel_id=1, source_target_pairs={{0,1},{1,0},{2,3},{3,2},{4,5},{5,4},{6,7},{7,6},{8,9},{9,8},{10,11... | collective-permute-start | bytes 98312 | tf_op jit(solution)/shard_map/ppermute | solution.py:523
  78.2 3.9 %shard_map.121 = (f32[4,2,128,256]{3,2,1,0:T(8,128)S(1)}, bf16[6,4,384,256]{3,2,1,0:T(8,128)(2,1)S(1)}) custom-call(s32[6]{0:T(128)S(1)} %stack.57.flag_ref, bf16[4,2,128,256]{3,2,1,0:T(8,128)(2,1)S(1)} %get-tuple-element.44.first_ref.refs_0_.cotangent, bf16[4,2,128,256]{3,2,1,0:T(8,128)(2,1)} %collective-permute-done.13.after.second_ref.refs_1_, ...), custom_call_target="tpu_custom_call" | custom-call | flops 7247757312 | bytes 9764888 | tf_op jit(solution)/shard_map/pallas_call | solution.py:24
  83.2 3.5 %collective-permute-start.26 = (f32[1,2,128]{2,1,0:T(2,128)S(1)}, f32[1,2,128]{2,1,0:T(2,128)S(1)}, u32[]{:S(2)}, u32[]{:S(2)}) collective-permute-start(f32[1,2,128]{2,1,0:T(2,128)S(1)} %get-tuple-element.50), channel_id=1, source_target_pairs={{0,24},{8,16},{16,8},{24,0},{1,25},{9,17},{17,9},{25,1},{2,26},{10... | collective-permute-start | bytes 3080 | tf_op jit(solution)/shard_map/ppermute | solution.py:503
  90.6 2.1 %collective-permute-done.29 = f32[1,2,128]{2,1,0:T(2,128)S(1)} collective-permute-done((f32[1,2,128]{2,1,0:T(2,128)S(1)}, f32[1,2,128]{2,1,0:T(2,128)S(1)}, u32[]{:S(2)}, u32[]{:S(2)}) %collective-permute-start.29) | collective-permute-done | bytes 1056 | tf_op jit(solution)/shard_map/ppermute | solution.py:503
  92.7 3.3 %collective-permute-start.30 = (f32[1,2,128]{2,1,0:T(2,128)S(1)}, f32[1,2,128]{2,1,0:T(2,128)S(1)}, u32[]{:S(2)}, u32[]{:S(2)}) collective-permute-start(f32[1,2,128]{2,1,0:T(2,128)S(1)} %add_add_fusion.2), channel_id=1, source_target_pairs={{0,1},{1,0},{2,3},{3,2},{4,5},{5,4},{6,7},{7,6},{8,9},{9,8},{10,11... | collective-permute-start | bytes 3080 | tf_op jit(solution)/shard_map/ppermute | solution.py:503
  96.1 4.6 %shard_map.123 = (f32[2048,128]{1,0:T(8,128)S(1)}, f32[2048,128]{1,0:T(8,128)S(1)}) custom-call(s32[6]{0:T(128)S(1)} %stack.57.flag_ref, bf16[6,4,384,256]{3,2,1,0:T(8,128)(2,1)S(1)} %get-tuple-element.51.stack_ref, bf16[4,2,128,256]{3,2,1,0:T(8,128)(2,1)S(1)} %get-tuple-element.52.act_ref), custom_call_target="tpu_custom_call" | custom-call | flops 7247757312 | bytes 7340056 | tf_op jit(solution)/shard_map/pallas_call | solution.py:24
  101.3 4.6 %shard_map.126 = (f32[2048,128]{1,0:T(8,128)S(1)}, f32[2048,128]{1,0:T(8,128)S(1)}) custom-call(s32[6]{0:T(128)S(1)} %stack.57.flag_ref, bf16[6,4,384,256]{3,2,1,0:T(8,128)(2,1)S(1)} %get-tuple-element.58.stack_ref, bf16[4,2,128,256]{3,2,1,0:T(8,128)(2,1)S(1)} %get-tuple-element.54.grad_ref.first_ref.refs_0_), custom_call_target="tpu_custom_call" | custom-call | flops 7247757312 | bytes 7340056 | tf_op jit(solution)/shard_map/pallas_call | solution.py:24
  107.8 3.1 %collective-permute-start.32 = (bf16[1,2,128,256]{3,2,1,0:T(8,128)(2,1)S(1)}, bf16[1,2,128,256]{3,2,1,0:T(8,128)(2,1)S(1)}, u32[]{:S(2)}, u32[]{:S(2)}) collective-permute-start(bf16[1,2,128,256]{3,2,1,0:T(8,128)(2,1)S(1)} %get-tuple-element.55), channel_id=1, source_target_pairs={{0,2},{2,4},{4,6},{1,3},{3,5},{5,7},{8,10},{10,12},{12,14},{9,11},... | collective-permute-start | bytes 393224 | tf_op jit(solution)/shard_map/ppermute | solution.py:482
  113.7 3.8 %collective-permute-done.33.below_ref = bf16[1,2,128,256]{3,2,1,0:T(8,128)(2,1)S(1)} collective-permute-done((bf16[1,2,128,256]{3,2,1,0:T(8,128)(2,1)S(1)}, bf16[1,2,128,256]{3,2,1,0:T(8,128)(2,1)S(1)}, u32[]{:S(2)}, u32[]{:S(2)}) %collective-permute-start.33) | collective-permute-done | bytes 131104 | tf_op jit(solution)/shard_map/ppermute | solution.py:482
  120.2 6.2 %collective-permute-done.34.second_ref.refs_3_ = bf16[2,2,128,256]{3,2,1,0:T(8,128)(2,1)S(1)} collective-permute-done((bf16[2,2,128,256]{3,2,1,0:T(8,128)(2,1)S(1)}, bf16[2,2,128,256]{3,2,1,0:T(8,128)(2,1)S(1)}, u32[]{:S(2)}, u32[]{:S(2)}) %collective-permute-start.34) | collective-permute-done | bytes 262176 | tf_op jit(solution)/shard_map/ppermute | solution.py:482
  127.3 2.2 %collective-permute-start.38 = (bf16[128,128]{1,0:T(8,128)(2,1)S(1)}, bf16[128,128]{1,0:T(8,128)(2,1)S(1)}, u32[]{:S(2)}, u32[]{:S(2)}) collective-permute-start(bf16[128,128]{1,0:T(8,128)(2,1)S(1)} %shard_map.129), channel_id=1, source_target_pairs={{0,1},{1,0},{2,3},{3,2},{4,5},{5,4},{6,7},{7,6},{8,9},{9,8},{10,11... | collective-permute-start | bytes 98312 | tf_op jit(solution)/shard_map/ppermute | solution.py:523
  134.1 4.1 %shard_map.131 = (f32[4,2,128,256]{3,2,1,0:T(8,128)S(1)}, f32[1,2,128]{2,1,0:T(2,128)S(1)}) custom-call(s32[6]{0:T(128)S(1)} %stack.57.flag_ref, bf16[4,2,128,256]{3,2,1,0:T(8,128)(2,1)S(1)} %get-tuple-element.54.grad_ref.first_ref.refs_0_, bf16[4,2,128,256]{3,2,1,0:T(8,128)(2,1)S(1)} %collective-permute-done.31.second_ref.refs_1_.refs_4_, ...), custom_call_target="tpu_custom_call" | custom-call | flops 7247757312 | bytes 5576728 | tf_op jit(solution)/shard_map/pallas_call | solution.py:24
  152.5 5.1 %collective-permute-start.45 = (f32[1,2,128]{2,1,0:T(2,128)S(1)}, f32[1,2,128]{2,1,0:T(2,128)S(1)}, u32[]{:S(2)}, u32[]{:S(2)}) collective-permute-start(f32[1,2,128]{2,1,0:T(2,128)S(1)} %add_add_fusion), channel_id=1, source_target_pairs={{0,1},{1,0},{2,3},{3,2},{4,5},{5,4},{6,7},{7,6},{8,9},{9,8},{10,11... | collective-permute-start | bytes 3080 | tf_op jit(solution)/shard_map/ppermute | solution.py:503
  159.9 2.3 %collective-permute-start.54 = (s16[2,4,32,128]{3,2,1,0:T(8,128)(2,1)S(1)}, s16[2,4,32,128]{3,2,1,0:T(8,128)(2,1)S(1)}, u32[]{:S(2)}, u32[]{:S(2)}) collective-permute-start(s16[2,4,32,128]{3,2,1,0:T(8,128)(2,1)S(1)} %shard_map.134.refs_0_), channel_id=1, source_target_pairs={{0,24},{8,16},{16,8},{24,0},{1,25},{9,17},{17,9},{25,1},{2,26},{10... | collective-permute-start | bytes 196616 | tf_op jit(solution)/shard_map/ppermute | solution.py:573
  172.7 6.9 %collective-permute-start.62 = (s16[64,32,128]{2,1,0:T(8,128)(2,1)S(1)}, s16[64,32,128]{2,1,0:T(8,128)(2,1)S(1)}, u32[]{:S(2)}, u32[]{:S(2)}) collective-permute-start(s16[64,32,128]{2,1,0:T(8,128)(2,1)S(1)} %bitcast.25), channel_id=1, source_target_pairs={{0,1},{1,0},{2,3},{3,2},{4,5},{5,4},{6,7},{7,6},{8,9},{9,8},{10,11... | collective-permute-start | bytes 1572872 | tf_op jit(solution)/shard_map/ppermute | solution.py:523
  180.2 3.1 %collective-permute-start.58 = (s16[64,32,128]{2,1,0:T(8,128)(2,1)S(1)}, s16[64,32,128]{2,1,0:T(8,128)(2,1)S(1)}, u32[]{:S(2)}, u32[]{:S(2)}) collective-permute-start(s16[64,32,128]{2,1,0:T(8,128)(2,1)S(1)} %bitcast.27), channel_id=1, source_target_pairs={{0,1},{1,0},{2,3},{3,2},{4,5},{5,4},{6,7},{7,6},{8,9},{9,8},{10,11... | collective-permute-start | bytes 1572872 | tf_op jit(solution)/shard_map/ppermute | solution.py:523
  183.3 3.9 %shard_map.139 = f32[128,3456]{1,0:T(8,128)} custom-call(s32[6]{0:T(128)S(1)} %stack.57.flag_ref, s16[64,32,128]{2,1,0:T(8,128)(2,1)S(1)} %bitcast.26, s16[64,32,128]{2,1,0:T(8,128)(2,1)S(1)} %collective-permute-done.62.theirs_ref), custom_call_target="tpu_custom_call" | custom-call | bytes 2818072 | tf_op jit(solution)/shard_map/pallas_call | solution.py:24
  187.2 3.9 %shard_map.137 = f32[128,3456]{1,0:T(8,128)} custom-call(s32[6]{0:T(128)S(1)} %stack.57.flag_ref, s16[64,32,128]{2,1,0:T(8,128)(2,1)S(1)} %bitcast.28, s16[64,32,128]{2,1,0:T(8,128)(2,1)S(1)} %collective-permute-done.58.theirs_ref), custom_call_target="tpu_custom_call" | custom-call | bytes 2818072 | tf_op jit(solution)/shard_map/pallas_call | solution.py:24
  (161 shorter events, 75.2 us)
Async XLA Ops:
  7.0 8.9 %collective-permute-start.6 = (f32[1,2,128]{2,1,0:T(2,128)S(1)}, f32[1,2,128]{2,1,0:T(2,128)S(1)}, u32[]{:S(2)}, u32[]{:S(2)}) collective-permute-start(f32[1,2,128]{2,1,0:T(2,128)S(1)} %get-tuple-element.43), channel_id=1, source_target_pairs={{0,8},{8,0},{16,24},{24,16},{1,9},{9,1},{17,25},{25,17},{2,10},{10... | collective-permute-start | bytes 3080 | tf_op jit(solution)/shard_map/ppermute | solution.py:510
  9.2 6.8 %collective-permute-start.7 = (f32[1,2,128]{2,1,0:T(2,128)S(1)}, f32[1,2,128]{2,1,0:T(2,128)S(1)}, u32[]{:S(2)}, u32[]{:S(2)}) collective-permute-start(f32[1,2,128]{2,1,0:T(2,128)S(1)} %get-tuple-element.43), channel_id=1, source_target_pairs={{0,16},{8,24},{16,0},{24,8},{1,17},{9,25},{17,1},{25,9},{2,18},{10... | collective-permute-start | bytes 3080 | tf_op jit(solution)/shard_map/ppermute | solution.py:510
  11.5 14.9 %collective-permute-start.1 = (bf16[2,2,128,256]{3,2,1,0:T(8,128)(2,1)S(1)}, bf16[2,2,128,256]{3,2,1,0:T(8,128)(2,1)S(1)}, u32[]{:S(2)}, u32[]{:S(2)}) collective-permute-start(bf16[2,2,128,256]{3,2,1,0:T(8,128)(2,1)S(1)} %get-tuple-element.40), channel_id=1, source_target_pairs={{0,2},{2,4},{4,6},{1,3},{3,5},{5,7},{8,10},{10,12},{12,14},{9,11},... | collective-permute-start | bytes 786440 | tf_op jit(solution)/shard_map/ppermute | solution.py:482
  14.6 11.7 %collective-permute-start.2 = (bf16[2,2,128,256]{3,2,1,0:T(8,128)(2,1)S(1)}, bf16[2,2,128,256]{3,2,1,0:T(8,128)(2,1)S(1)}, u32[]{:S(2)}, u32[]{:S(2)}) collective-permute-start(bf16[2,2,128,256]{3,2,1,0:T(8,128)(2,1)S(1)} %get-tuple-element.41), channel_id=1, source_target_pairs={{2,0},{4,2},{6,4},{3,1},{5,3},{7,5},{10,8},{12,10},{14,12},{11,9},... | collective-permute-start | bytes 786440 | tf_op jit(solution)/shard_map/ppermute | solution.py:482
  19.3 7.0 %collective-permute-start.9 = (f32[1,2,128]{2,1,0:T(2,128)S(1)}, f32[1,2,128]{2,1,0:T(2,128)S(1)}, u32[]{:S(2)}, u32[]{:S(2)}) collective-permute-start(f32[1,2,128]{2,1,0:T(2,128)S(1)} %pad_maximum_fusion), channel_id=1, source_target_pairs={{0,2},{2,0},{4,6},{6,4},{1,3},{3,1},{5,7},{7,5},{8,10},{10,8},{12,... | collective-permute-start | bytes 3080 | tf_op jit(solution)/shard_map/ppermute | solution.py:510
  20.3 21.5 %collective-permute-start = (bf16[4,2,128,256]{3,2,1,0:T(8,128)(2,1)S(1)}, bf16[4,2,128,256]{3,2,1,0:T(8,128)(2,1)}, u32[]{:S(2)}, u32[]{:S(2)}) collective-permute-start(bf16[4,2,128,256]{3,2,1,0:T(8,128)(2,1)S(1)} %get-tuple-element.39.first_ref.own.refs_7_.latent), channel_id=1, source_target_pairs={{0,8},{8,16},{16,24},{1,9},{9,17},{17,25},{2,10},{10,18},{18,26},{... | collective-permute-start | bytes 1572872 | tf_op jit(solution)/shard_map/ppermute | solution.py:482
  23.3 20.6 %collective-permute-start.13 = (bf16[4,2,128,256]{3,2,1,0:T(8,128)(2,1)S(1)}, bf16[4,2,128,256]{3,2,1,0:T(8,128)(2,1)}, u32[]{:S(2)}, u32[]{:S(2)}) collective-permute-start(bf16[4,2,128,256]{3,2,1,0:T(8,128)(2,1)S(1)} %get-tuple-element.44.first_ref.refs_0_.cotangent), channel_id=1, source_target_pairs={{8,0},{16,8},{24,16},{9,1},{17,9},{25,17},{10,2},{18,10},{26,18},{... | collective-permute-start | bytes 1572872 | tf_op jit(solution)/shard_map/ppermute | solution.py:482
  27.8 9.0 %collective-permute-start.3 = (bf16[2,2,128,256]{3,2,1,0:T(8,128)(2,1)}, bf16[2,2,128,256]{3,2,1,0:T(8,128)(2,1)}, u32[]{:S(2)}, u32[]{:S(2)}) collective-permute-start(bf16[2,2,128,256]{3,2,1,0:T(8,128)(2,1)} %get-tuple-element.42.first_ref.near), channel_id=1, source_target_pairs={{0,8},{8,16},{16,24},{1,9},{9,17},{17,25},{2,10},{10,18},{18,26},{... | collective-permute-start | bytes 786440 | tf_op jit(solution)/shard_map/ppermute | solution.py:482
  63.0 7.1 %collective-permute-start.14 = (bf16[2,2,128,256]{3,2,1,0:T(8,128)(2,1)S(1)}, bf16[2,2,128,256]{3,2,1,0:T(8,128)(2,1)S(1)}, u32[]{:S(2)}, u32[]{:S(2)}) collective-permute-start(bf16[2,2,128,256]{3,2,1,0:T(8,128)(2,1)S(1)} %copy-done.6), channel_id=1, source_target_pairs={{8,0},{16,8},{24,16},{9,1},{17,9},{25,17},{10,2},{18,10},{26,18},{... | collective-permute-start | bytes 786440 | tf_op jit(solution)/shard_map/ppermute | solution.py:482
  65.4 11.6 %collective-permute-start.23 = (f32[1,2,128]{2,1,0:T(2,128)S(1)}, f32[1,2,128]{2,1,0:T(2,128)S(1)}, u32[]{:S(2)}, u32[]{:S(2)}) collective-permute-start(f32[1,2,128]{2,1,0:T(2,128)S(1)} %pad_maximum_fusion.4), channel_id=1, source_target_pairs={{0,1},{1,0},{2,3},{3,2},{4,5},{5,4},{6,7},{7,6},{8,9},{9,8},{10,11... | collective-permute-start | bytes 3080 | tf_op jit(solution)/shard_map/ppermute | solution.py:510
  71.0 6.1 %collective-permute-start.16 = (bf16[128,128]{1,0:T(8,128)(2,1)S(1)}, bf16[128,128]{1,0:T(8,128)(2,1)S(1)}, u32[]{:S(2)}, u32[]{:S(2)}) collective-permute-start(bf16[128,128]{1,0:T(8,128)(2,1)S(1)} %shard_map.119), channel_id=1, source_target_pairs={{0,1},{1,0},{2,3},{3,2},{4,5},{5,4},{6,7},{7,6},{8,9},{9,8},{10,11... | collective-permute-start | bytes 98312 | tf_op jit(solution)/shard_map/ppermute | solution.py:523
  92.7 8.0 %collective-permute-start.30 = (f32[1,2,128]{2,1,0:T(2,128)S(1)}, f32[1,2,128]{2,1,0:T(2,128)S(1)}, u32[]{:S(2)}, u32[]{:S(2)}) collective-permute-start(f32[1,2,128]{2,1,0:T(2,128)S(1)} %add_add_fusion.2), channel_id=1, source_target_pairs={{0,1},{1,0},{2,3},{3,2},{4,5},{5,4},{6,7},{7,6},{8,9},{9,8},{10,11... | collective-permute-start | bytes 3080 | tf_op jit(solution)/shard_map/ppermute | solution.py:503
  100.7 18.4 %collective-permute-start.35 = (f32[64,32,128]{2,1,0:T(8,128)S(1)}, f32[64,32,128]{2,1,0:T(8,128)S(1)}, u32[]{:S(2)}, u32[]{:S(2)}) collective-permute-start(f32[64,32,128]{2,1,0:T(8,128)S(1)} %bitcast.44), channel_id=1, source_target_pairs={{0,1},{1,0},{2,3},{3,2},{4,5},{5,4},{6,7},{7,6},{8,9},{9,8},{10,11... | collective-permute-start | bytes 3145736 | tf_op jit(solution)/shard_map/ppermute | solution.py:523
  105.9 13.2 %collective-permute-start.36 = (f32[64,32,128]{2,1,0:T(8,128)S(1)}, f32[64,32,128]{2,1,0:T(8,128)S(1)}, u32[]{:S(2)}, u32[]{:S(2)}) collective-permute-start(f32[64,32,128]{2,1,0:T(8,128)S(1)} %bitcast.45), channel_id=1, source_target_pairs={{0,1},{1,0},{2,3},{3,2},{4,5},{5,4},{6,7},{7,6},{8,9},{9,8},{10,11... | collective-permute-start | bytes 3145736 | tf_op jit(solution)/shard_map/ppermute | solution.py:523
  106.5 23.0 %collective-permute-start.31 = (bf16[4,2,128,256]{3,2,1,0:T(8,128)(2,1)S(1)}, bf16[4,2,128,256]{3,2,1,0:T(8,128)(2,1)S(1)}, u32[]{:S(2)}, u32[]{:S(2)}) collective-permute-start(bf16[4,2,128,256]{3,2,1,0:T(8,128)(2,1)S(1)} %get-tuple-element.54.grad_ref.first_ref.refs_0_), channel_id=1, source_target_pairs={{8,0},{16,8},{24,16},{9,1},{17,9},{25,17},{10,2},{18,10},{26,18},{... | collective-permute-start | bytes 1572872 | tf_op jit(solution)/shard_map/ppermute | solution.py:482
  107.8 6.0 %collective-permute-start.32 = (bf16[1,2,128,256]{3,2,1,0:T(8,128)(2,1)S(1)}, bf16[1,2,128,256]{3,2,1,0:T(8,128)(2,1)S(1)}, u32[]{:S(2)}, u32[]{:S(2)}) collective-permute-start(bf16[1,2,128,256]{3,2,1,0:T(8,128)(2,1)S(1)} %get-tuple-element.55), channel_id=1, source_target_pairs={{0,2},{2,4},{4,6},{1,3},{3,5},{5,7},{8,10},{10,12},{12,14},{9,11},... | collective-permute-start | bytes 393224 | tf_op jit(solution)/shard_map/ppermute | solution.py:482
  110.9 6.7 %collective-permute-start.33 = (bf16[1,2,128,256]{3,2,1,0:T(8,128)(2,1)S(1)}, bf16[1,2,128,256]{3,2,1,0:T(8,128)(2,1)S(1)}, u32[]{:S(2)}, u32[]{:S(2)}) collective-permute-start(bf16[1,2,128,256]{3,2,1,0:T(8,128)(2,1)S(1)} %get-tuple-element.56), channel_id=1, source_target_pairs={{2,0},{4,2},{6,4},{3,1},{5,3},{7,5},{10,8},{12,10},{14,12},{11,9},... | collective-permute-start | bytes 393224 | tf_op jit(solution)/shard_map/ppermute | solution.py:482
  117.6 8.8 %collective-permute-start.34 = (bf16[2,2,128,256]{3,2,1,0:T(8,128)(2,1)S(1)}, bf16[2,2,128,256]{3,2,1,0:T(8,128)(2,1)S(1)}, u32[]{:S(2)}, u32[]{:S(2)}) collective-permute-start(bf16[2,2,128,256]{3,2,1,0:T(8,128)(2,1)S(1)} %shard_map.125.first_ref.refs_2_.refs_5_), channel_id=1, source_target_pairs={{8,0},{16,8},{24,16},{9,1},{17,9},{25,17},{10,2},{18,10},{26,18},{... | collective-permute-start | bytes 786440 | tf_op jit(solution)/shard_map/ppermute | solution.py:482
  127.3 6.9 %collective-permute-start.38 = (bf16[128,128]{1,0:T(8,128)(2,1)S(1)}, bf16[128,128]{1,0:T(8,128)(2,1)S(1)}, u32[]{:S(2)}, u32[]{:S(2)}) collective-permute-start(bf16[128,128]{1,0:T(8,128)(2,1)S(1)} %shard_map.129), channel_id=1, source_target_pairs={{0,1},{1,0},{2,3},{3,2},{4,5},{5,4},{6,7},{7,6},{8,9},{9,8},{10,11... | collective-permute-start | bytes 98312 | tf_op jit(solution)/shard_map/ppermute | solution.py:523
  131.4 14.9 %collective-permute-start.46 = (s16[2,16,32,128]{3,2,1,0:T(8,128)(2,1)S(1)}, s16[2,16,32,128]{3,2,1,0:T(8,128)(2,1)S(1)}, u32[]{:S(2)}, u32[]{:S(2)}) collective-permute-start(s16[2,16,32,128]{3,2,1,0:T(8,128)(2,1)S(1)} %get-tuple-element.61.refs_0_), channel_id=1, source_target_pairs={{0,2},{2,0},{4,6},{6,4},{1,3},{3,1},{5,7},{7,5},{8,10},{10,8},{12,... | collective-permute-start | bytes 786440 | tf_op jit(solution)/shard_map/ppermute | solution.py:543
  132.6 15.3 %collective-permute-start.47 = (s16[2,16,32,128]{3,2,1,0:T(8,128)(2,1)S(1)}, s16[2,16,32,128]{3,2,1,0:T(8,128)(2,1)S(1)}, u32[]{:S(2)}, u32[]{:S(2)}) collective-permute-start(s16[2,16,32,128]{3,2,1,0:T(8,128)(2,1)S(1)} %get-tuple-element.66), channel_id=1, source_target_pairs={{0,4},{2,6},{4,0},{6,2},{1,5},{3,7},{5,1},{7,3},{8,12},{10,14},{12... | collective-permute-start | bytes 786440 | tf_op jit(solution)/shard_map/ppermute | solution.py:543
  132.6 15.3 %collective-permute-start.48 = (s16[2,16,32,128]{3,2,1,0:T(8,128)(2,1)S(1)}, s16[2,16,32,128]{3,2,1,0:T(8,128)(2,1)S(1)}, u32[]{:S(2)}, u32[]{:S(2)}) collective-permute-start(s16[2,16,32,128]{3,2,1,0:T(8,128)(2,1)S(1)} %get-tuple-element.67), channel_id=1, source_target_pairs={{0,6},{2,4},{4,2},{6,0},{1,7},{3,5},{5,3},{7,1},{8,14},{10,12},{12... | collective-permute-start | bytes 786440 | tf_op jit(solution)/shard_map/ppermute | solution.py:543
  146.3 6.1 %collective-permute-start.43 = (f32[1,2,128]{2,1,0:T(2,128)S(1)}, f32[1,2,128]{2,1,0:T(2,128)S(1)}, u32[]{:S(2)}, u32[]{:S(2)}) collective-permute-start(f32[1,2,128]{2,1,0:T(2,128)S(1)} %add_add_fusion.1), channel_id=1, source_target_pairs={{0,4},{2,6},{4,0},{6,2},{1,5},{3,7},{5,1},{7,3},{8,12},{10,14},{12... | collective-permute-start | bytes 3080 | tf_op jit(solution)/shard_map/ppermute | solution.py:503
  146.3 6.1 %collective-permute-start.44 = (f32[1,2,128]{2,1,0:T(2,128)S(1)}, f32[1,2,128]{2,1,0:T(2,128)S(1)}, u32[]{:S(2)}, u32[]{:S(2)}) collective-permute-start(f32[1,2,128]{2,1,0:T(2,128)S(1)} %add_add_fusion.1), channel_id=1, source_target_pairs={{0,6},{2,4},{4,2},{6,0},{1,7},{3,5},{5,3},{7,1},{8,14},{10,12},{12... | collective-permute-start | bytes 3080 | tf_op jit(solution)/shard_map/ppermute | solution.py:503
  148.8 9.5 %collective-permute-start.49 = (s16[2,4,32,128]{3,2,1,0:T(8,128)(2,1)S(1)}, s16[2,4,32,128]{3,2,1,0:T(8,128)(2,1)S(1)}, u32[]{:S(2)}, u32[]{:S(2)}) collective-permute-start(s16[2,4,32,128]{3,2,1,0:T(8,128)(2,1)S(1)} %get-tuple-element.69), channel_id=1, source_target_pairs={{0,8},{8,0},{16,24},{24,16},{1,9},{9,1},{17,25},{25,17},{2,10},{10... | collective-permute-start | bytes 196616 | tf_op jit(solution)/shard_map/ppermute | solution.py:559
  148.9 9.5 %collective-permute-start.50 = (s16[2,4,32,128]{3,2,1,0:T(8,128)(2,1)S(1)}, s16[2,4,32,128]{3,2,1,0:T(8,128)(2,1)S(1)}, u32[]{:S(2)}, u32[]{:S(2)}) collective-permute-start(s16[2,4,32,128]{3,2,1,0:T(8,128)(2,1)S(1)} %get-tuple-element.70), channel_id=1, source_target_pairs={{0,16},{8,24},{16,0},{24,8},{1,17},{9,25},{17,1},{25,9},{2,18},{10... | collective-permute-start | bytes 196616 | tf_op jit(solution)/shard_map/ppermute | solution.py:559
  150.5 7.9 %collective-permute-start.51 = (s16[2,4,32,128]{3,2,1,0:T(8,128)(2,1)S(1)}, s16[2,4,32,128]{3,2,1,0:T(8,128)(2,1)S(1)}, u32[]{:S(2)}, u32[]{:S(2)}) collective-permute-start(s16[2,4,32,128]{3,2,1,0:T(8,128)(2,1)S(1)} %get-tuple-element.71), channel_id=1, source_target_pairs={{0,24},{8,16},{16,8},{24,0},{1,25},{9,17},{17,9},{25,1},{2,26},{10... | collective-permute-start | bytes 196616 | tf_op jit(solution)/shard_map/ppermute | solution.py:559
  168.3 11.3 %collective-permute-start.55 = (s16[16,32,128]{2,1,0:T(8,128)(2,1)S(1)}, s16[16,32,128]{2,1,0:T(8,128)(2,1)S(1)}, u32[]{:S(2)}, u32[]{:S(2)}) collective-permute-start(s16[16,32,128]{2,1,0:T(8,128)(2,1)S(1)} %bitcast.36), channel_id=1, source_target_pairs={{0,2},{2,0},{4,6},{6,4},{1,3},{3,1},{5,7},{7,5},{8,10},{10,8},{12,... | collective-permute-start | bytes 393224 | tf_op jit(solution)/shard_map/ppermute | solution.py:584
  169.5 10.0 %collective-permute-start.56 = (s16[16,32,128]{2,1,0:T(8,128)(2,1)S(1)}, s16[16,32,128]{2,1,0:T(8,128)(2,1)S(1)}, u32[]{:S(2)}, u32[]{:S(2)}) collective-permute-start(s16[16,32,128]{2,1,0:T(8,128)(2,1)S(1)} %bitcast.37), channel_id=1, source_target_pairs={{0,4},{2,6},{4,0},{6,2},{1,5},{3,7},{5,1},{7,3},{8,12},{10,14},{12... | collective-permute-start | bytes 393224 | tf_op jit(solution)/shard_map/ppermute | solution.py:584
  169.7 9.8 %collective-permute-start.57 = (s16[16,32,128]{2,1,0:T(8,128)(2,1)S(1)}, s16[16,32,128]{2,1,0:T(8,128)(2,1)S(1)}, u32[]{:S(2)}, u32[]{:S(2)}) collective-permute-start(s16[16,32,128]{2,1,0:T(8,128)(2,1)S(1)} %bitcast.38), channel_id=1, source_target_pairs={{0,6},{2,4},{4,2},{6,0},{1,7},{3,5},{5,3},{7,1},{8,14},{10,12},{12... | collective-permute-start | bytes 393224 | tf_op jit(solution)/shard_map/ppermute | solution.py:584
  172.7 10.6 %collective-permute-start.62 = (s16[64,32,128]{2,1,0:T(8,128)(2,1)S(1)}, s16[64,32,128]{2,1,0:T(8,128)(2,1)S(1)}, u32[]{:S(2)}, u32[]{:S(2)}) collective-permute-start(s16[64,32,128]{2,1,0:T(8,128)(2,1)S(1)} %bitcast.25), channel_id=1, source_target_pairs={{0,1},{1,0},{2,3},{3,2},{4,5},{5,4},{6,7},{7,6},{8,9},{9,8},{10,11... | collective-permute-start | bytes 1572872 | tf_op jit(solution)/shard_map/ppermute | solution.py:523
  180.2 7.0 %collective-permute-start.58 = (s16[64,32,128]{2,1,0:T(8,128)(2,1)S(1)}, s16[64,32,128]{2,1,0:T(8,128)(2,1)S(1)}, u32[]{:S(2)}, u32[]{:S(2)}) collective-permute-start(s16[64,32,128]{2,1,0:T(8,128)(2,1)S(1)} %bitcast.27), channel_id=1, source_target_pairs={{0,1},{1,0},{2,3},{3,2},{4,5},{5,4},{6,7},{7,6},{8,9},{9,8},{10,11... | collective-permute-start | bytes 1572872 | tf_op jit(solution)/shard_map/ppermute | solution.py:523
  (38 other events, 186.8 us)

commit v8 on v7

--- a/solution.py
+++ b/solution.py
@@ -116,8 +116,8 @@
     put_rows(st_ref, *local_stats(planes, float(GROUP * rows * frames * cols)))
 
 
-def rows_kernel(above_ref, below_ref, *outs):
-    for which, out in enumerate(outs):
+def rows_kernel(above_ref, below_ref, *refs):
+    for which, out in enumerate(refs[-above_ref.shape[0] :]):
         out[0] = above_ref[which]
         out[1] = below_ref[which]
 
@@ -273,7 +273,7 @@
 
 
 def hidden_grad_kernel(
-    hidden, scaled, par_ref, st_ref, sums_ref, after, out_ref, down_ref, up_ref, *, count
+    hidden, scaled, par_ref, st_ref, sums_ref, out_ref, down_ref, up_ref, *, count
 ):
     rows, frames, channels, cols = hidden.shape
     mean, inverse, _, _, _ = norm_columns(par_ref, st_ref, count, 3)
@@ -364,7 +364,7 @@
         out_ref[half:, here] = second_ref[pl.ds(tap, half, stride=SLOTS), :]
 
 
-def weight_second_kernel(flag_ref, stack_ref, act_ref, mine_ref, theirs_ref, right_ref):
+def weight_second_kernel(flag_ref, stack_ref, act_ref, after, mine_ref, theirs_ref, right_ref):
     rows, frames, channels, cols = act_ref.shape
     for row in range(rows):
         right_ref[row * cols : (row + 1) * cols] = jnp.transpose(
@@ -611,13 +611,11 @@
     return columns
 
 
-def row_halos(down, up):
+def row_halos(down, up, after=()):
     above, below = shifted(down, "height", 1), shifted(up, "height", -1)
-    return call(rows_kernel, [shape((2, *down.shape[1:]), BF16)] * down.shape[0], [VMEM] * 2, (above, below))
-
-
-def halo(own, near, steps):
-    return shifted(own, "tm", steps), near, shifted(near, "tm", steps)
+    return call(
+        rows_kernel, [shape((2, *down.shape[1:]), BF16)] * down.shape[0], [VMEM] * (2 + len(after)), (above, below, *after)
+    )
 
 
 def with_columns(flags, own, around, after=()):
@@ -671,9 +669,10 @@
         [VMEM] * 3,
         (latent, cotangent, par),
     )
-    near, near_c = row_halos(down, up)
-    around = with_columns(flags, latent, halo(latent, near, 1))
-    around_c = halo(cotangent, near_c, -1)
+    past, future_c = shifted(latent, "tm", 1), shifted(cotangent, "tm", -1)
+    near, near_c = row_halos(down, up, (past, future_c))
+    around = with_columns(flags, latent, (past, near, shifted(near, "tm", 1)))
+    around_c = (future_c, near_c, shifted(near_c, "tm", -1))
     stats_first = all_stats(stats_first, count / devices)
     (weight_first,) = call(weight_forward_kernel, [shape(taps, BF16)], [VMEM], (conv_first,))
     (weight_second_t,) = call(weight_back_kernel, [shape(taps, BF16)], [VMEM], (conv_second,))
@@ -683,7 +682,7 @@
         functools.partial(conv_first_kernel, count=count),
         [shape(block, F32), small, shape(stack, BF16)],
         [SMEM] + [VMEM] * 10,
-        (flags, latent, *around, par, stats_first, weight_first, around_c[0]),
+        (flags, latent, *around, par, stats_first, weight_first, around_c[2]),
         flops=conv_flops,
         transcendentals=3 * latent.size,
     )
@@ -704,23 +703,23 @@
         transcendentals=latent.size,
     )
     sums = all_sum(sums)
-    halves_second = call(
-        weight_second_kernel,
-        halves,
-        [SMEM] + [VMEM] * 2,
-        (flags, stack_c, act_second),
-        scratch=[pltpu.VMEM((rows * cols, frames * channels), BF16)],
-        flops=conv_flops,
-    )
     message = shape((1, frames, channels, cols), BF16)
     hidden_grad, down, up = call(
         functools.partial(hidden_grad_kernel, count=count),
         [shape(block, BF16), message, message],
-        [VMEM] * 6,
-        (hidden, scaled, par, stats_second, sums, halves_second[0]),
+        [VMEM] * 5,
+        (hidden, scaled, par, stats_second, sums),
     )
     (near,) = row_halos(down, up)
-    around = halo(hidden_grad, near, -1)
+    around = (shifted(hidden_grad, "tm", -1), near, shifted(near, "tm", -1))
+    halves_second = call(
+        weight_second_kernel,
+        halves,
+        [SMEM] + [VMEM] * 3,
+        (flags, stack_c, act_second, near),
+        scratch=[pltpu.VMEM((rows * cols, frames * channels), BF16)],
+        flops=conv_flops,
+    )
     halves_first = call(
         weight_first_kernel,
         halves,

time: 192 us -> 207 us (1.078)
  waiting for transfers between devices: 32.8 us -> 53.6 us
  starting transfers between devices: 101 us -> 92.1 us
  local copies, waits for them, and re-layouts: 4.96 us -> 9.71 us
    ppermute x14, waiting for transfers between devices: 6.83 us -> 18.2 us  [all_stats(): lax.ppermute(value, axis, pairs)]
    ppermute x10, waiting for transfers between devices: 13.2 us -> 21.2 us  [shifted(): lax.ppermute(value, axis, [(source, source + steps) for source in range(i...]
    ppermute x10, starting transfers between devices: 20.6 us -> 14.1 us  [swapped(): return lax.ppermute(value, 'width', [(0, 1), (1, 0)])]
    unnamed x14 -> x34, local copies, waits for them, and re-layouts: 3.96 us -> 8.71 us
    ppermute x14, waiting for transfers between devices: 8.24 us -> 11.6 us  [all_sum(): parts = [value] + [lax.ppermute(value, axis, pairs) for pairs in exchanges]]
  transfers between devices with their start and end apart: 63 -> 63, of which waited for: 20 -> 19; matrix products, arithmetic and copies ran while one was open for 0% -> 0% of each run, Pallas kernels for 17% -> 14%
where the time goes in v8:
time: 207 us; the launch traced here: 206 us
  starting transfers between devices  92.1 us (44%)
  waiting for transfers between devices  53.6 us (26%)
  Pallas kernels  48.7 us (24%)
  local copies, waits for them, and re-layouts  9.71 us (5%)
    pallas_call x28, Pallas kernels, call(): pl.pallas_call(body, out_shape=tuple(outs), in_specs=specs, out_specs=tup...  48.7 us
    ppermute x14, starting transfers between devices, all_stats(): lax.ppermute(value, axis, pairs)  23.4 us
    ppermute x10, waiting for transfers between devices, shifted(): lax.ppermute(value, axis, [(source, source + steps) for source in range(i...  21.2 us
    ppermute x10, starting transfers between devices, shifted(): lax.ppermute(value, axis, [(source, source + steps) for source in range(i...  19.8 us
    ppermute x14, starting transfers between devices, all_sum(): parts = [value] + [lax.ppermute(value, axis, pairs) for pairs in exchanges]  18.7 us
    ppermute x14, waiting for transfers between devices, all_stats(): lax.ppermute(value, axis, pairs)  18.2 us
    ppermute x10, starting transfers between devices, swapped(): return lax.ppermute(value, 'width', [(0, 1), (1, 0)])  14.1 us
    ppermute x14, waiting for transfers between devices, all_sum(): parts = [value] + [lax.ppermute(value, axis, pairs) for pairs in exchanges]  11.6 us
  transfers between devices with their start and end apart: 63, of which 19 were waited for; matrix products, arithmetic and copies ran while one was open for 0% of the time, Pallas kernels for 14%

profile of v8, /device:TPU:1, one launch (start us, length us, event | category | flops | bytes accessed | tf_op | source)
XLA Modules:
  0.0 206.2 jit_solution(7763679124937422168)
XLA Ops:
  4.4 3.4 %shard_map.112 = (bf16[4,2,128,256]{3,2,1,0:T(8,128)(2,1)S(1)}, bf16[4,2,128,256]{3,2,1,0:T(8,128)(2,1)S(1)}, bf16[2,2,128,256]{3,2,1,0:T(8,128)(2,1)}, bf16[2,2,128,256]{3,2,1,0:T(8,128)(2,1)}, f32[1,2,128]{2,1,0:T(2,128)S(1)}) custom-call(bf16[128,2,4,256]{3,2,1,0:T(4,128)(2,1)S(1)} %copy-done.13, bf16[128,2,4,256]{3,2,1,0:T(4,128)(2,1)S(1)} %copy-done.14, ...), custom_call_target="tpu_custom_call" | custom-call | bytes 2626560 | tf_op jit(solution)/shard_map/pallas_call | solution.py:24
  7.8 2.1 %collective-permute-start.7 = (f32[1,2,128]{2,1,0:T(2,128)S(1)}, f32[1,2,128]{2,1,0:T(2,128)S(1)}, u32[]{:S(2)}, u32[]{:S(2)}) collective-permute-start(f32[1,2,128]{2,1,0:T(2,128)S(1)} %get-tuple-element.44), channel_id=1, source_target_pairs={{0,8},{8,0},{16,24},{24,16},{1,9},{9,1},{17,25},{25,17},{2,10},{10... | collective-permute-start | bytes 3080 | tf_op jit(solution)/shard_map/ppermute | solution.py:510
  9.9 2.3 %collective-permute-start.8 = (f32[1,2,128]{2,1,0:T(2,128)S(1)}, f32[1,2,128]{2,1,0:T(2,128)S(1)}, u32[]{:S(2)}, u32[]{:S(2)}) collective-permute-start(f32[1,2,128]{2,1,0:T(2,128)S(1)} %get-tuple-element.44), channel_id=1, source_target_pairs={{0,16},{8,24},{16,0},{24,8},{1,17},{9,25},{17,1},{25,9},{2,18},{10... | collective-permute-start | bytes 3080 | tf_op jit(solution)/shard_map/ppermute | solution.py:510
  12.2 2.3 %collective-permute-start = (bf16[4,2,128,256]{3,2,1,0:T(8,128)(2,1)S(1)}, bf16[4,2,128,256]{3,2,1,0:T(8,128)(2,1)S(1)}, u32[]{:S(2)}, u32[]{:S(2)}) collective-permute-start(bf16[4,2,128,256]{3,2,1,0:T(8,128)(2,1)S(1)} %get-tuple-element.39.first_ref.own.refs_7_.latent), channel_id=1, source_target_pairs={{0,8},{8,16},{16,24},{1,9},{9,17},{17,25},{2,10},{10,18},{18,26},{... | collective-permute-start | bytes 1572872 | tf_op jit(solution)/shard_map/ppermute | solution.py:482
  15.8 3.1 %collective-permute-start.1 = (bf16[2,2,128,256]{3,2,1,0:T(8,128)(2,1)}, bf16[2,2,128,256]{3,2,1,0:T(8,128)(2,1)S(1)}, u32[]{:S(2)}, u32[]{:S(2)}) collective-permute-start(bf16[2,2,128,256]{3,2,1,0:T(8,128)(2,1)} %get-tuple-element.40), channel_id=1, source_target_pairs={{0,2},{2,4},{4,6},{1,3},{3,5},{5,7},{8,10},{10,12},{12,14},{9,11},... | collective-permute-start | bytes 786440 | tf_op jit(solution)/shard_map/ppermute | solution.py:482
  20.3 2.1 %collective-permute-start.10 = (f32[1,2,128]{2,1,0:T(2,128)S(1)}, f32[1,2,128]{2,1,0:T(2,128)S(1)}, u32[]{:S(2)}, u32[]{:S(2)}) collective-permute-start(f32[1,2,128]{2,1,0:T(2,128)S(1)} %pad_maximum_fusion), channel_id=1, source_target_pairs={{0,2},{2,0},{4,6},{6,4},{1,3},{3,1},{5,7},{7,5},{8,10},{10,8},{12,... | collective-permute-start | bytes 3080 | tf_op jit(solution)/shard_map/ppermute | solution.py:510
  22.4 8.1 %collective-permute-done.10 = f32[1,2,128]{2,1,0:T(2,128)S(1)} collective-permute-done((f32[1,2,128]{2,1,0:T(2,128)S(1)}, f32[1,2,128]{2,1,0:T(2,128)S(1)}, u32[]{:S(2)}, u32[]{:S(2)}) %collective-permute-start.10) | collective-permute-done | bytes 1056 | tf_op jit(solution)/shard_map/ppermute | solution.py:510
  30.5 2.4 %collective-permute-done.11 = f32[1,2,128]{2,1,0:T(2,128)S(1)} collective-permute-done((f32[1,2,128]{2,1,0:T(2,128)S(1)}, f32[1,2,128]{2,1,0:T(2,128)S(1)}, u32[]{:S(2)}, u32[]{:S(2)}) %collective-permute-start.11) | collective-permute-done | bytes 1056 | tf_op jit(solution)/shard_map/ppermute | solution.py:510
  34.1 2.1 %collective-permute-done.12 = f32[1,2,128]{2,1,0:T(2,128)S(1)} collective-permute-done((f32[1,2,128]{2,1,0:T(2,128)S(1)}, f32[1,2,128]{2,1,0:T(2,128)S(1)}, u32[]{:S(2)}, u32[]{:S(2)}) %collective-permute-start.12) | collective-permute-done | bytes 1056 | tf_op jit(solution)/shard_map/ppermute | solution.py:510
  39.5 4.6 %collective-permute-start.4 = (bf16[2,2,128,256]{3,2,1,0:T(8,128)(2,1)}, bf16[2,2,128,256]{3,2,1,0:T(8,128)(2,1)}, u32[]{:S(2)}, u32[]{:S(2)}) collective-permute-start(bf16[2,2,128,256]{3,2,1,0:T(8,128)(2,1)} %get-tuple-element.43.first_ref.near), channel_id=1, source_target_pairs={{0,8},{8,16},{16,24},{1,9},{9,17},{17,25},{2,10},{10,18},{18,26},{... | collective-permute-start | bytes 786440 | tf_op jit(solution)/shard_map/ppermute | solution.py:482
  44.2 5.4 %collective-permute-start.13 = (f32[1,2,128]{2,1,0:T(2,128)S(1)}, f32[1,2,128]{2,1,0:T(2,128)S(1)}, u32[]{:S(2)}, u32[]{:S(2)}) collective-permute-start(f32[1,2,128]{2,1,0:T(2,128)S(1)} %pad_maximum_fusion.1), channel_id=1, source_target_pairs={{0,1},{1,0},{2,3},{3,2},{4,5},{5,4},{6,7},{7,6},{8,9},{9,8},{10,11... | collective-permute-start | bytes 3080 | tf_op jit(solution)/shard_map/ppermute | solution.py:510
  57.1 2.6 %collective-permute-done.14.after.second_ref.refs_3_ = bf16[2,2,128,256]{3,2,1,0:T(8,128)(2,1)S(1)} collective-permute-done((bf16[2,2,128,256]{3,2,1,0:T(8,128)(2,1)S(1)}, bf16[2,2,128,256]{3,2,1,0:T(8,128)(2,1)S(1)}, u32[]{:S(2)}, u32[]{:S(2)}) %collective-permute-start.14) | collective-permute-done | bytes 262176 | tf_op jit(solution)/shard_map/ppermute | solution.py:482
  61.8 5.2 %shard_map.117 = (f32[4,2,128,256]{3,2,1,0:T(8,128)S(1)}, f32[1,2,128]{2,1,0:T(2,128)S(1)}, bf16[6,4,384,256]{3,2,1,0:T(8,128)(2,1)S(1)}) custom-call(s32[6]{0:T(128)S(1)} %stack.57.flag_ref, bf16[4,2,128,256]{3,2,1,0:T(8,128)(2,1)S(1)} %copy-done.7, bf16[4,2,128,256]{3,2,1,0:T(8,128)(2,1)S(1)} %copy-done.11, ...), custom_call_target="tpu_custom_call" | custom-call | flops 7247757312 | bytes 10033176 | tf_op jit(solution)/shard_map/pallas_call | solution.py:24
  71.8 2.5 %collective-permute-done.19 = f32[1,2,128]{2,1,0:T(2,128)S(1)} collective-permute-done((f32[1,2,128]{2,1,0:T(2,128)S(1)}, f32[1,2,128]{2,1,0:T(2,128)S(1)}, u32[]{:S(2)}, u32[]{:S(2)}) %collective-permute-start.19) | collective-permute-done | bytes 1056 | tf_op jit(solution)/shard_map/ppermute | solution.py:510
  79.2 3.7 %collective-permute-start.23 = (f32[1,2,128]{2,1,0:T(2,128)S(1)}, f32[1,2,128]{2,1,0:T(2,128)S(1)}, u32[]{:S(2)}, u32[]{:S(2)}) collective-permute-start(f32[1,2,128]{2,1,0:T(2,128)S(1)} %pad_maximum_fusion.4), channel_id=1, source_target_pairs={{0,1},{1,0},{2,3},{3,2},{4,5},{5,4},{6,7},{7,6},{8,9},{9,8},{10,11... | collective-permute-start | bytes 3080 | tf_op jit(solution)/shard_map/ppermute | solution.py:510
  87.2 3.4 %shard_map.121 = (f32[4,2,128,256]{3,2,1,0:T(8,128)S(1)}, bf16[6,4,384,256]{3,2,1,0:T(8,128)(2,1)S(1)}) custom-call(s32[6]{0:T(128)S(1)} %stack.57.flag_ref, bf16[4,2,128,256]{3,2,1,0:T(8,128)(2,1)S(1)} %copy-done.2, bf16[4,2,128,256]{3,2,1,0:T(8,128)(2,1)S(1)} %copy-done.4, bf16[2,2,128,256]{3,2,1,0:T(8,128)(2,1)S(1)} %get-tuple-element.45.first_ref.refs_2_, ...), custom_call_target="tpu_custom_call" | custom-call | flops 7247757312 | bytes 9764888 | tf_op jit(solution)/shard_map/pallas_call | solution.py:24
  93.0 2.1 %collective-permute-start.26 = (f32[1,2,128]{2,1,0:T(2,128)S(1)}, f32[1,2,128]{2,1,0:T(2,128)S(1)}, u32[]{:S(2)}, u32[]{:S(2)}) collective-permute-start(f32[1,2,128]{2,1,0:T(2,128)S(1)} %get-tuple-element.50), channel_id=1, source_target_pairs={{0,24},{8,16},{16,8},{24,0},{1,25},{9,17},{17,9},{25,1},{2,26},{10... | collective-permute-start | bytes 3080 | tf_op jit(solution)/shard_map/ppermute | solution.py:503
  99.9 2.2 %collective-permute-done.29 = f32[1,2,128]{2,1,0:T(2,128)S(1)} collective-permute-done((f32[1,2,128]{2,1,0:T(2,128)S(1)}, f32[1,2,128]{2,1,0:T(2,128)S(1)}, u32[]{:S(2)}, u32[]{:S(2)}) %collective-permute-start.29) | collective-permute-done | bytes 1056 | tf_op jit(solution)/shard_map/ppermute | solution.py:503
  102.1 3.8 %collective-permute-start.30 = (f32[1,2,128]{2,1,0:T(2,128)S(1)}, f32[1,2,128]{2,1,0:T(2,128)S(1)}, u32[]{:S(2)}, u32[]{:S(2)}) collective-permute-start(f32[1,2,128]{2,1,0:T(2,128)S(1)} %add_add_fusion.2), channel_id=1, source_target_pairs={{0,1},{1,0},{2,3},{3,2},{4,5},{5,4},{6,7},{7,6},{8,9},{9,8},{10,11... | collective-permute-start | bytes 3080 | tf_op jit(solution)/shard_map/ppermute | solution.py:503
  110.4 4.1 %shard_map.126 = (f32[2048,128]{1,0:T(8,128)S(1)}, f32[2048,128]{1,0:T(8,128)S(1)}) custom-call(s32[6]{0:T(128)S(1)} %stack.57.flag_ref, bf16[6,4,384,256]{3,2,1,0:T(8,128)(2,1)S(1)} %get-tuple-element.58.stack_ref, bf16[4,2,128,256]{3,2,1,0:T(8,128)(2,1)S(1)} %get-tuple-element.51.grad_ref.first_ref.refs_0_), custom_call_target="tpu_custom_call" | custom-call | flops 7247757312 | bytes 7340056 | tf_op jit(solution)/shard_map/pallas_call | solution.py:24
  116.4 4.1 %shard_map.125 = (f32[2048,128]{1,0:T(8,128)S(1)}, f32[2048,128]{1,0:T(8,128)S(1)}) custom-call(s32[6]{0:T(128)S(1)} %stack.57.flag_ref, bf16[6,4,384,256]{3,2,1,0:T(8,128)(2,1)S(1)} %get-tuple-element.54.stack_ref, bf16[4,2,128,256]{3,2,1,0:T(8,128)(2,1)S(1)} %get-tuple-element.55.act_ref, ...), custom_call_target="tpu_custom_call" | custom-call | flops 7247757312 | bytes 7602200 | tf_op jit(solution)/shard_map/pallas_call | solution.py:24
  125.2 17.3 %collective-permute-done.34.second_ref.refs_3_ = bf16[2,2,128,256]{3,2,1,0:T(8,128)(2,1)S(1)} collective-permute-done((bf16[2,2,128,256]{3,2,1,0:T(8,128)(2,1)S(1)}, bf16[2,2,128,256]{3,2,1,0:T(8,128)(2,1)S(1)}, u32[]{:S(2)}, u32[]{:S(2)}) %collective-permute-start.34) | collective-permute-done | bytes 262176 | tf_op jit(solution)/shard_map/ppermute | solution.py:482
  149.2 4.1 %shard_map.131 = (f32[4,2,128,256]{3,2,1,0:T(8,128)S(1)}, f32[1,2,128]{2,1,0:T(2,128)S(1)}) custom-call(s32[6]{0:T(128)S(1)} %stack.57.flag_ref, bf16[4,2,128,256]{3,2,1,0:T(8,128)(2,1)S(1)} %get-tuple-element.51.grad_ref.first_ref.refs_0_, bf16[4,2,128,256]{3,2,1,0:T(8,128)(2,1)S(1)} %collective-permute-done.31.second_ref.refs_1_.refs_4_, ...), custom_call_target="tpu_custom_call" | custom-call | flops 7247757312 | bytes 5576728 | tf_op jit(solution)/shard_map/pallas_call | solution.py:24
  153.8 2.3 %collective-permute-done.39 = f32[1,2,128]{2,1,0:T(2,128)S(1)} collective-permute-done((f32[1,2,128]{2,1,0:T(2,128)S(1)}, f32[1,2,128]{2,1,0:T(2,128)S(1)}, u32[]{:S(2)}, u32[]{:S(2)}) %collective-permute-start.39) | collective-permute-done | bytes 1056 | tf_op jit(solution)/shard_map/ppermute | solution.py:503
  157.0 3.2 %collective-permute-done.41 = f32[1,2,128]{2,1,0:T(2,128)S(1)} collective-permute-done((f32[1,2,128]{2,1,0:T(2,128)S(1)}, f32[1,2,128]{2,1,0:T(2,128)S(1)}, u32[]{:S(2)}, u32[]{:S(2)}) %collective-permute-start.41) | collective-permute-done | bytes 1056 | tf_op jit(solution)/shard_map/ppermute | solution.py:503
  165.1 2.4 %collective-permute-start.51 = (s16[2,4,32,128]{3,2,1,0:T(8,128)(2,1)S(1)}, s16[2,4,32,128]{3,2,1,0:T(8,128)(2,1)S(1)}, u32[]{:S(2)}, u32[]{:S(2)}) collective-permute-start(s16[2,4,32,128]{3,2,1,0:T(8,128)(2,1)S(1)} %get-tuple-element.71), channel_id=1, source_target_pairs={{0,24},{8,16},{16,8},{24,0},{1,25},{9,17},{17,9},{25,1},{2,26},{10... | collective-permute-start | bytes 196616 | tf_op jit(solution)/shard_map/ppermute | solution.py:559
  167.6 4.8 %collective-permute-start.45 = (f32[1,2,128]{2,1,0:T(2,128)S(1)}, f32[1,2,128]{2,1,0:T(2,128)S(1)}, u32[]{:S(2)}, u32[]{:S(2)}) collective-permute-start(f32[1,2,128]{2,1,0:T(2,128)S(1)} %add_add_fusion), channel_id=1, source_target_pairs={{0,1},{1,0},{2,3},{3,2},{4,5},{5,4},{6,7},{7,6},{8,9},{9,8},{10,11... | collective-permute-start | bytes 3080 | tf_op jit(solution)/shard_map/ppermute | solution.py:503
  174.2 2.7 %collective-permute-start.54 = (s16[2,4,32,128]{3,2,1,0:T(8,128)(2,1)S(1)}, s16[2,4,32,128]{3,2,1,0:T(8,128)(2,1)S(1)}, u32[]{:S(2)}, u32[]{:S(2)}) collective-permute-start(s16[2,4,32,128]{3,2,1,0:T(8,128)(2,1)S(1)} %shard_map.134.refs_0_), channel_id=1, source_target_pairs={{0,24},{8,16},{16,8},{24,0},{1,25},{9,17},{17,9},{25,1},{2,26},{10... | collective-permute-start | bytes 196616 | tf_op jit(solution)/shard_map/ppermute | solution.py:573
  187.6 7.3 %collective-permute-start.62 = (s16[64,32,128]{2,1,0:T(8,128)(2,1)S(1)}, s16[64,32,128]{2,1,0:T(8,128)(2,1)S(1)}, u32[]{:S(2)}, u32[]{:S(2)}) collective-permute-start(s16[64,32,128]{2,1,0:T(8,128)(2,1)S(1)} %bitcast.24), channel_id=1, source_target_pairs={{0,1},{1,0},{2,3},{3,2},{4,5},{5,4},{6,7},{7,6},{8,9},{9,8},{10,11... | collective-permute-start | bytes 1572872 | tf_op jit(solution)/shard_map/ppermute | solution.py:523
  195.5 2.9 %collective-permute-start.58 = (s16[64,32,128]{2,1,0:T(8,128)(2,1)S(1)}, s16[64,32,128]{2,1,0:T(8,128)(2,1)S(1)}, u32[]{:S(2)}, u32[]{:S(2)}) collective-permute-start(s16[64,32,128]{2,1,0:T(8,128)(2,1)S(1)} %bitcast.26), channel_id=1, source_target_pairs={{0,1},{1,0},{2,3},{3,2},{4,5},{5,4},{6,7},{7,6},{8,9},{9,8},{10,11... | collective-permute-start | bytes 1572872 | tf_op jit(solution)/shard_map/ppermute | solution.py:523
  198.4 3.9 %shard_map.139 = f32[128,3456]{1,0:T(8,128)} custom-call(s32[6]{0:T(128)S(1)} %stack.57.flag_ref, s16[64,32,128]{2,1,0:T(8,128)(2,1)S(1)} %bitcast.25, s16[64,32,128]{2,1,0:T(8,128)(2,1)S(1)} %collective-permute-done.62.theirs_ref), custom_call_target="tpu_custom_call" | custom-call | bytes 2818072 | tf_op jit(solution)/shard_map/pallas_call | solution.py:24
  202.3 3.9 %shard_map.137 = f32[128,3456]{1,0:T(8,128)} custom-call(s32[6]{0:T(128)S(1)} %stack.57.flag_ref, s16[64,32,128]{2,1,0:T(8,128)(2,1)S(1)} %bitcast.27, s16[64,32,128]{2,1,0:T(8,128)(2,1)S(1)} %collective-permute-done.58.theirs_ref), custom_call_target="tpu_custom_call" | custom-call | bytes 2818072 | tf_op jit(solution)/shard_map/pallas_call | solution.py:24
  (181 shorter events, 78.6 us)
Async XLA Ops:
  7.8 8.0 %collective-permute-start.7 = (f32[1,2,128]{2,1,0:T(2,128)S(1)}, f32[1,2,128]{2,1,0:T(2,128)S(1)}, u32[]{:S(2)}, u32[]{:S(2)}) collective-permute-start(f32[1,2,128]{2,1,0:T(2,128)S(1)} %get-tuple-element.44), channel_id=1, source_target_pairs={{0,8},{8,0},{16,24},{24,16},{1,9},{9,1},{17,25},{25,17},{2,10},{10... | collective-permute-start | bytes 3080 | tf_op jit(solution)/shard_map/ppermute | solution.py:510
  9.9 9.0 %collective-permute-start.8 = (f32[1,2,128]{2,1,0:T(2,128)S(1)}, f32[1,2,128]{2,1,0:T(2,128)S(1)}, u32[]{:S(2)}, u32[]{:S(2)}) collective-permute-start(f32[1,2,128]{2,1,0:T(2,128)S(1)} %get-tuple-element.44), channel_id=1, source_target_pairs={{0,16},{8,24},{16,0},{24,8},{1,17},{9,25},{17,1},{25,9},{2,18},{10... | collective-permute-start | bytes 3080 | tf_op jit(solution)/shard_map/ppermute | solution.py:510
  12.2 8.0 %collective-permute-start.9 = (f32[1,2,128]{2,1,0:T(2,128)S(1)}, f32[1,2,128]{2,1,0:T(2,128)S(1)}, u32[]{:S(2)}, u32[]{:S(2)}) collective-permute-start(f32[1,2,128]{2,1,0:T(2,128)S(1)} %get-tuple-element.44), channel_id=1, source_target_pairs={{0,24},{8,16},{16,8},{24,0},{1,25},{9,17},{17,9},{25,1},{2,26},{10... | collective-permute-start | bytes 3080 | tf_op jit(solution)/shard_map/ppermute | solution.py:510
  12.2 24.8 %collective-permute-start = (bf16[4,2,128,256]{3,2,1,0:T(8,128)(2,1)S(1)}, bf16[4,2,128,256]{3,2,1,0:T(8,128)(2,1)S(1)}, u32[]{:S(2)}, u32[]{:S(2)}) collective-permute-start(bf16[4,2,128,256]{3,2,1,0:T(8,128)(2,1)S(1)} %get-tuple-element.39.first_ref.own.refs_7_.latent), channel_id=1, source_target_pairs={{0,8},{8,16},{16,24},{1,9},{9,17},{17,25},{2,10},{10,18},{18,26},{... | collective-permute-start | bytes 1572872 | tf_op jit(solution)/shard_map/ppermute | solution.py:482
  14.5 22.5 %collective-permute-start.3 = (bf16[4,2,128,256]{3,2,1,0:T(8,128)(2,1)S(1)}, bf16[4,2,128,256]{3,2,1,0:T(8,128)(2,1)S(1)}, u32[]{:S(2)}, u32[]{:S(2)}) collective-permute-start(bf16[4,2,128,256]{3,2,1,0:T(8,128)(2,1)S(1)} %get-tuple-element.42.first_ref.refs_0_.cotangent), channel_id=1, source_target_pairs={{8,0},{16,8},{24,16},{9,1},{17,9},{25,17},{10,2},{18,10},{26,18},{... | collective-permute-start | bytes 1572872 | tf_op jit(solution)/shard_map/ppermute | solution.py:482
  15.8 20.5 %collective-permute-start.1 = (bf16[2,2,128,256]{3,2,1,0:T(8,128)(2,1)}, bf16[2,2,128,256]{3,2,1,0:T(8,128)(2,1)S(1)}, u32[]{:S(2)}, u32[]{:S(2)}) collective-permute-start(bf16[2,2,128,256]{3,2,1,0:T(8,128)(2,1)} %get-tuple-element.40), channel_id=1, source_target_pairs={{0,2},{2,4},{4,6},{1,3},{3,5},{5,7},{8,10},{10,12},{12,14},{9,11},... | collective-permute-start | bytes 786440 | tf_op jit(solution)/shard_map/ppermute | solution.py:482
  18.9 17.3 %collective-permute-start.2 = (bf16[2,2,128,256]{3,2,1,0:T(8,128)(2,1)}, bf16[2,2,128,256]{3,2,1,0:T(8,128)(2,1)S(1)}, u32[]{:S(2)}, u32[]{:S(2)}) collective-permute-start(bf16[2,2,128,256]{3,2,1,0:T(8,128)(2,1)} %get-tuple-element.41), channel_id=1, source_target_pairs={{2,0},{4,2},{6,4},{3,1},{5,3},{7,5},{10,8},{12,10},{14,12},{11,9},... | collective-permute-start | bytes 786440 | tf_op jit(solution)/shard_map/ppermute | solution.py:482
  20.3 10.2 %collective-permute-start.10 = (f32[1,2,128]{2,1,0:T(2,128)S(1)}, f32[1,2,128]{2,1,0:T(2,128)S(1)}, u32[]{:S(2)}, u32[]{:S(2)}) collective-permute-start(f32[1,2,128]{2,1,0:T(2,128)S(1)} %pad_maximum_fusion), channel_id=1, source_target_pairs={{0,2},{2,0},{4,6},{6,4},{1,3},{3,1},{5,7},{7,5},{8,10},{10,8},{12,... | collective-permute-start | bytes 3080 | tf_op jit(solution)/shard_map/ppermute | solution.py:510
  39.5 15.6 %collective-permute-start.4 = (bf16[2,2,128,256]{3,2,1,0:T(8,128)(2,1)}, bf16[2,2,128,256]{3,2,1,0:T(8,128)(2,1)}, u32[]{:S(2)}, u32[]{:S(2)}) collective-permute-start(bf16[2,2,128,256]{3,2,1,0:T(8,128)(2,1)} %get-tuple-element.43.first_ref.near), channel_id=1, source_target_pairs={{0,8},{8,16},{16,24},{1,9},{9,17},{17,25},{2,10},{10,18},{18,26},{... | collective-permute-start | bytes 786440 | tf_op jit(solution)/shard_map/ppermute | solution.py:482
  44.2 7.2 %collective-permute-start.13 = (f32[1,2,128]{2,1,0:T(2,128)S(1)}, f32[1,2,128]{2,1,0:T(2,128)S(1)}, u32[]{:S(2)}, u32[]{:S(2)}) collective-permute-start(f32[1,2,128]{2,1,0:T(2,128)S(1)} %pad_maximum_fusion.1), channel_id=1, source_target_pairs={{0,1},{1,0},{2,3},{3,2},{4,5},{5,4},{6,7},{7,6},{8,9},{9,8},{10,11... | collective-permute-start | bytes 3080 | tf_op jit(solution)/shard_map/ppermute | solution.py:510
  49.9 9.8 %collective-permute-start.14 = (bf16[2,2,128,256]{3,2,1,0:T(8,128)(2,1)S(1)}, bf16[2,2,128,256]{3,2,1,0:T(8,128)(2,1)S(1)}, u32[]{:S(2)}, u32[]{:S(2)}) collective-permute-start(bf16[2,2,128,256]{3,2,1,0:T(8,128)(2,1)S(1)} %get-tuple-element.45.first_ref.refs_2_), channel_id=1, source_target_pairs={{8,0},{16,8},{24,16},{9,1},{17,9},{25,17},{10,2},{18,10},{26,18},{... | collective-permute-start | bytes 786440 | tf_op jit(solution)/shard_map/ppermute | solution.py:482
  79.2 7.1 %collective-permute-start.23 = (f32[1,2,128]{2,1,0:T(2,128)S(1)}, f32[1,2,128]{2,1,0:T(2,128)S(1)}, u32[]{:S(2)}, u32[]{:S(2)}) collective-permute-start(f32[1,2,128]{2,1,0:T(2,128)S(1)} %pad_maximum_fusion.4), channel_id=1, source_target_pairs={{0,1},{1,0},{2,3},{3,2},{4,5},{5,4},{6,7},{7,6},{8,9},{9,8},{10,11... | collective-permute-start | bytes 3080 | tf_op jit(solution)/shard_map/ppermute | solution.py:510
  107.1 8.0 %collective-permute-start.32 = (bf16[1,2,128,256]{3,2,1,0:T(8,128)(2,1)S(1)}, bf16[1,2,128,256]{3,2,1,0:T(8,128)(2,1)S(1)}, u32[]{:S(2)}, u32[]{:S(2)}) collective-permute-start(bf16[1,2,128,256]{3,2,1,0:T(8,128)(2,1)S(1)} %get-tuple-element.52), channel_id=1, source_target_pairs={{0,2},{2,4},{4,6},{1,3},{3,5},{5,7},{8,10},{10,12},{12,14},{9,11},... | collective-permute-start | bytes 393224 | tf_op jit(solution)/shard_map/ppermute | solution.py:482
  108.9 7.5 %collective-permute-start.33 = (bf16[1,2,128,256]{3,2,1,0:T(8,128)(2,1)S(1)}, bf16[1,2,128,256]{3,2,1,0:T(8,128)(2,1)S(1)}, u32[]{:S(2)}, u32[]{:S(2)}) collective-permute-start(bf16[1,2,128,256]{3,2,1,0:T(8,128)(2,1)S(1)} %get-tuple-element.53), channel_id=1, source_target_pairs={{2,0},{4,2},{6,4},{3,1},{5,3},{7,5},{10,8},{12,10},{14,12},{11,9},... | collective-permute-start | bytes 393224 | tf_op jit(solution)/shard_map/ppermute | solution.py:482
  114.5 9.6 %collective-permute-start.36 = (f32[64,32,128]{2,1,0:T(8,128)S(1)}, f32[64,32,128]{2,1,0:T(8,128)S(1)}, u32[]{:S(2)}, u32[]{:S(2)}) collective-permute-start(f32[64,32,128]{2,1,0:T(8,128)S(1)} %bitcast.44), channel_id=1, source_target_pairs={{0,1},{1,0},{2,3},{3,2},{4,5},{5,4},{6,7},{7,6},{8,9},{9,8},{10,11... | collective-permute-start | bytes 3145736 | tf_op jit(solution)/shard_map/ppermute | solution.py:523
  121.5 22.8 %collective-permute-start.31 = (bf16[4,2,128,256]{3,2,1,0:T(8,128)(2,1)S(1)}, bf16[4,2,128,256]{3,2,1,0:T(8,128)(2,1)S(1)}, u32[]{:S(2)}, u32[]{:S(2)}) collective-permute-start(bf16[4,2,128,256]{3,2,1,0:T(8,128)(2,1)S(1)} %get-tuple-element.51.grad_ref.first_ref.refs_0_), channel_id=1, source_target_pairs={{8,0},{16,8},{24,16},{9,1},{17,9},{25,17},{10,2},{18,10},{26,18},{... | collective-permute-start | bytes 1572872 | tf_op jit(solution)/shard_map/ppermute | solution.py:482
  122.7 19.7 %collective-permute-start.34 = (bf16[2,2,128,256]{3,2,1,0:T(8,128)(2,1)S(1)}, bf16[2,2,128,256]{3,2,1,0:T(8,128)(2,1)S(1)}, u32[]{:S(2)}, u32[]{:S(2)}) collective-permute-start(bf16[2,2,128,256]{3,2,1,0:T(8,128)(2,1)S(1)} %shard_map.124.after.first_ref.refs_2_.refs_5_), channel_id=1, source_target_pairs={{8,0},{16,8},{24,16},{9,1},{17,9},{25,17},{10,2},{18,10},{26,18},{... | collective-permute-start | bytes 786440 | tf_op jit(solution)/shard_map/ppermute | solution.py:482
  143.4 5.8 %collective-permute-start.38 = (bf16[128,128]{1,0:T(8,128)(2,1)S(1)}, bf16[128,128]{1,0:T(8,128)(2,1)S(1)}, u32[]{:S(2)}, u32[]{:S(2)}) collective-permute-start(bf16[128,128]{1,0:T(8,128)(2,1)S(1)} %shard_map.129), channel_id=1, source_target_pairs={{0,1},{1,0},{2,3},{3,2},{4,5},{5,4},{6,7},{7,6},{8,9},{9,8},{10,11... | collective-permute-start | bytes 98312 | tf_op jit(solution)/shard_map/ppermute | solution.py:523
  146.2 15.7 %collective-permute-start.46 = (s16[2,16,32,128]{3,2,1,0:T(8,128)(2,1)S(1)}, s16[2,16,32,128]{3,2,1,0:T(8,128)(2,1)S(1)}, u32[]{:S(2)}, u32[]{:S(2)}) collective-permute-start(s16[2,16,32,128]{3,2,1,0:T(8,128)(2,1)S(1)} %get-tuple-element.61.refs_0_), channel_id=1, source_target_pairs={{0,2},{2,0},{4,6},{6,4},{1,3},{3,1},{5,7},{7,5},{8,10},{10,8},{12,... | collective-permute-start | bytes 786440 | tf_op jit(solution)/shard_map/ppermute | solution.py:543
  148.0 15.0 %collective-permute-start.47 = (s16[2,16,32,128]{3,2,1,0:T(8,128)(2,1)S(1)}, s16[2,16,32,128]{3,2,1,0:T(8,128)(2,1)S(1)}, u32[]{:S(2)}, u32[]{:S(2)}) collective-permute-start(s16[2,16,32,128]{3,2,1,0:T(8,128)(2,1)S(1)} %get-tuple-element.66), channel_id=1, source_target_pairs={{0,4},{2,6},{4,0},{6,2},{1,5},{3,7},{5,1},{7,3},{8,12},{10,14},{12... | collective-permute-start | bytes 786440 | tf_op jit(solution)/shard_map/ppermute | solution.py:543
  148.2 14.7 %collective-permute-start.48 = (s16[2,16,32,128]{3,2,1,0:T(8,128)(2,1)S(1)}, s16[2,16,32,128]{3,2,1,0:T(8,128)(2,1)S(1)}, u32[]{:S(2)}, u32[]{:S(2)}) collective-permute-start(s16[2,16,32,128]{3,2,1,0:T(8,128)(2,1)S(1)} %get-tuple-element.67), channel_id=1, source_target_pairs={{0,6},{2,4},{4,2},{6,0},{1,7},{3,5},{5,3},{7,1},{8,14},{10,12},{12... | collective-permute-start | bytes 786440 | tf_op jit(solution)/shard_map/ppermute | solution.py:543
  161.7 5.9 %collective-permute-start.43 = (f32[1,2,128]{2,1,0:T(2,128)S(1)}, f32[1,2,128]{2,1,0:T(2,128)S(1)}, u32[]{:S(2)}, u32[]{:S(2)}) collective-permute-start(f32[1,2,128]{2,1,0:T(2,128)S(1)} %add_add_fusion.1), channel_id=1, source_target_pairs={{0,4},{2,6},{4,0},{6,2},{1,5},{3,7},{5,1},{7,3},{8,12},{10,14},{12... | collective-permute-start | bytes 3080 | tf_op jit(solution)/shard_map/ppermute | solution.py:503
  162.0 5.6 %collective-permute-start.44 = (f32[1,2,128]{2,1,0:T(2,128)S(1)}, f32[1,2,128]{2,1,0:T(2,128)S(1)}, u32[]{:S(2)}, u32[]{:S(2)}) collective-permute-start(f32[1,2,128]{2,1,0:T(2,128)S(1)} %add_add_fusion.1), channel_id=1, source_target_pairs={{0,6},{2,4},{4,2},{6,0},{1,7},{3,5},{5,3},{7,1},{8,14},{10,12},{12... | collective-permute-start | bytes 3080 | tf_op jit(solution)/shard_map/ppermute | solution.py:503
  163.9 9.3 %collective-permute-start.49 = (s16[2,4,32,128]{3,2,1,0:T(8,128)(2,1)S(1)}, s16[2,4,32,128]{3,2,1,0:T(8,128)(2,1)S(1)}, u32[]{:S(2)}, u32[]{:S(2)}) collective-permute-start(s16[2,4,32,128]{3,2,1,0:T(8,128)(2,1)S(1)} %get-tuple-element.69), channel_id=1, source_target_pairs={{0,8},{8,0},{16,24},{24,16},{1,9},{9,1},{17,25},{25,17},{2,10},{10... | collective-permute-start | bytes 196616 | tf_op jit(solution)/shard_map/ppermute | solution.py:559
  164.0 9.2 %collective-permute-start.50 = (s16[2,4,32,128]{3,2,1,0:T(8,128)(2,1)S(1)}, s16[2,4,32,128]{3,2,1,0:T(8,128)(2,1)S(1)}, u32[]{:S(2)}, u32[]{:S(2)}) collective-permute-start(s16[2,4,32,128]{3,2,1,0:T(8,128)(2,1)S(1)} %get-tuple-element.70), channel_id=1, source_target_pairs={{0,16},{8,24},{16,0},{24,8},{1,17},{9,25},{17,1},{25,9},{2,18},{10... | collective-permute-start | bytes 196616 | tf_op jit(solution)/shard_map/ppermute | solution.py:559
  165.1 8.1 %collective-permute-start.51 = (s16[2,4,32,128]{3,2,1,0:T(8,128)(2,1)S(1)}, s16[2,4,32,128]{3,2,1,0:T(8,128)(2,1)S(1)}, u32[]{:S(2)}, u32[]{:S(2)}) collective-permute-start(s16[2,4,32,128]{3,2,1,0:T(8,128)(2,1)S(1)} %get-tuple-element.71), channel_id=1, source_target_pairs={{0,24},{8,16},{16,8},{24,0},{1,25},{9,17},{17,9},{25,1},{2,26},{10... | collective-permute-start | bytes 196616 | tf_op jit(solution)/shard_map/ppermute | solution.py:559
  167.6 5.6 %collective-permute-start.45 = (f32[1,2,128]{2,1,0:T(2,128)S(1)}, f32[1,2,128]{2,1,0:T(2,128)S(1)}, u32[]{:S(2)}, u32[]{:S(2)}) collective-permute-start(f32[1,2,128]{2,1,0:T(2,128)S(1)} %add_add_fusion), channel_id=1, source_target_pairs={{0,1},{1,0},{2,3},{3,2},{4,5},{5,4},{6,7},{7,6},{8,9},{9,8},{10,11... | collective-permute-start | bytes 3080 | tf_op jit(solution)/shard_map/ppermute | solution.py:503
  183.1 11.9 %collective-permute-start.55 = (s16[16,32,128]{2,1,0:T(8,128)(2,1)S(1)}, s16[16,32,128]{2,1,0:T(8,128)(2,1)S(1)}, u32[]{:S(2)}, u32[]{:S(2)}) collective-permute-start(s16[16,32,128]{2,1,0:T(8,128)(2,1)S(1)} %bitcast.36), channel_id=1, source_target_pairs={{0,2},{2,0},{4,6},{6,4},{1,3},{3,1},{5,7},{7,5},{8,10},{10,8},{12,... | collective-permute-start | bytes 393224 | tf_op jit(solution)/shard_map/ppermute | solution.py:584
  184.5 10.5 %collective-permute-start.56 = (s16[16,32,128]{2,1,0:T(8,128)(2,1)S(1)}, s16[16,32,128]{2,1,0:T(8,128)(2,1)S(1)}, u32[]{:S(2)}, u32[]{:S(2)}) collective-permute-start(s16[16,32,128]{2,1,0:T(8,128)(2,1)S(1)} %bitcast.37), channel_id=1, source_target_pairs={{0,4},{2,6},{4,0},{6,2},{1,5},{3,7},{5,1},{7,3},{8,12},{10,14},{12... | collective-permute-start | bytes 393224 | tf_op jit(solution)/shard_map/ppermute | solution.py:584
  184.7 10.2 %collective-permute-start.57 = (s16[16,32,128]{2,1,0:T(8,128)(2,1)S(1)}, s16[16,32,128]{2,1,0:T(8,128)(2,1)S(1)}, u32[]{:S(2)}, u32[]{:S(2)}) collective-permute-start(s16[16,32,128]{2,1,0:T(8,128)(2,1)S(1)} %bitcast.38), channel_id=1, source_target_pairs={{0,6},{2,4},{4,2},{6,0},{1,7},{3,5},{5,3},{7,1},{8,14},{10,12},{12... | collective-permute-start | bytes 393224 | tf_op jit(solution)/shard_map/ppermute | solution.py:584
  187.6 10.8 %collective-permute-start.62 = (s16[64,32,128]{2,1,0:T(8,128)(2,1)S(1)}, s16[64,32,128]{2,1,0:T(8,128)(2,1)S(1)}, u32[]{:S(2)}, u32[]{:S(2)}) collective-permute-start(s16[64,32,128]{2,1,0:T(8,128)(2,1)S(1)} %bitcast.24), channel_id=1, source_target_pairs={{0,1},{1,0},{2,3},{3,2},{4,5},{5,4},{6,7},{7,6},{8,9},{9,8},{10,11... | collective-permute-start | bytes 1572872 | tf_op jit(solution)/shard_map/ppermute | solution.py:523
  195.5 6.8 %collective-permute-start.58 = (s16[64,32,128]{2,1,0:T(8,128)(2,1)S(1)}, s16[64,32,128]{2,1,0:T(8,128)(2,1)S(1)}, u32[]{:S(2)}, u32[]{:S(2)}) collective-permute-start(s16[64,32,128]{2,1,0:T(8,128)(2,1)S(1)} %bitcast.26), channel_id=1, source_target_pairs={{0,1},{1,0},{2,3},{3,2},{4,5},{5,4},{6,7},{7,6},{8,9},{9,8},{10,11... | collective-permute-start | bytes 1572872 | tf_op jit(solution)/shard_map/ppermute | solution.py:523
  (48 other events, 327.1 us)

commit v9 on v7

--- a/solution.py
+++ b/solution.py
@@ -96,30 +96,31 @@
     return 0.5 + 0.5 * jnp.tanh(0.5 * value)
 
 
-def planes_kernel(latent_ref, cotangent_ref, par_ref, latent_out, cotangent_out, down_ref, up_ref, st_ref):
-    _, frames, rows, cols = latent_ref.shape
-    for which, (natural, out) in enumerate(((latent_ref, latent_out), (cotangent_ref, cotangent_out))):
-        for row in range(rows):
-            for frame in range(frames):
-                plane = natural[:, frame, row, :]
-                out[row, frame] = plane
-                if row == rows - 1:
-                    down_ref[which, frame] = plane
-                if row == 0:
-                    up_ref[which, frame] = plane
-    scale = columns_of(par_ref[0:1])[0]
+def planes_kernel(natural_ref, *refs):
+    out_ref, down_ref, up_ref = refs[:3] if len(refs) == 3 else refs[1:4]
+    _, frames, rows, cols = natural_ref.shape
+    for row in range(rows):
+        for frame in range(frames):
+            plane = natural_ref[:, frame, row, :]
+            out_ref[row, frame] = plane
+            if row == rows - 1:
+                down_ref[0, frame] = plane
+            if row == 0:
+                up_ref[0, frame] = plane
+    if len(refs) == 3:
+        return
+    scale = columns_of(refs[0][0:1])[0]
     planes = [
-        functools.partial(lambda r, t: latent_out[r, t].astype(F32) * scale, r, t)
+        functools.partial(lambda r, t: out_ref[r, t].astype(F32) * scale, r, t)
         for r in range(rows)
         for t in range(frames)
     ]
-    put_rows(st_ref, *local_stats(planes, float(GROUP * rows * frames * cols)))
-
-
-def rows_kernel(above_ref, below_ref, *outs):
-    for which, out in enumerate(outs):
-        out[0] = above_ref[which]
-        out[1] = below_ref[which]
+    put_rows(refs[-1], *local_stats(planes, float(GROUP * rows * frames * cols)))
+
+
+def rows_kernel(above_ref, below_ref, *refs):
+    refs[-1][0] = above_ref[0]
+    refs[-1][1] = below_ref[0]
 
 
 def source(own, other, near, far, other_first):
@@ -505,8 +506,8 @@
     return value
 
 
-def all_stats(value, count):
-    for axis, _, exchanges in rounds(("tm", "height", "width")):
+def all_stats(value, count, axes=("tm", "height", "width")):
+    for axis, _, exchanges in rounds(axes):
         parts = [(value, count)] + [(lax.ppermute(value, axis, pairs), count) for pairs in exchanges]
         value, count = pairwise(parts, joined_stats)
     return value
@@ -611,13 +612,12 @@
     return columns
 
 
-def row_halos(down, up):
+def row_halos(down, up, after=()):
     above, below = shifted(down, "height", 1), shifted(up, "height", -1)
-    return call(rows_kernel, [shape((2, *down.shape[1:]), BF16)] * down.shape[0], [VMEM] * 2, (above, below))
-
-
-def halo(own, near, steps):
-    return shifted(own, "tm", steps), near, shifted(near, "tm", steps)
+    (near,) = call(
+        rows_kernel, [shape((2, *down.shape[1:]), BF16)], [VMEM] * (2 + len(after)), (above, below, *after)
+    )
+    return near
 
 
 def with_columns(flags, own, around, after=()):
@@ -664,17 +664,17 @@
     conv_flops = 3 * 2 * 4 * 256 * 36 * channels * 2 * channels
     small = shape((1, 2, channels), F32)
 
-    message = shape((2, frames, channels, cols), BF16)
-    latent, cotangent, down, up, stats_first = call(
-        planes_kernel,
-        [shape(block, BF16), shape(block, BF16), message, message, small],
-        [VMEM] * 3,
-        (latent, cotangent, par),
-    )
-    near, near_c = row_halos(down, up)
-    around = with_columns(flags, latent, halo(latent, near, 1))
-    around_c = halo(cotangent, near_c, -1)
-    stats_first = all_stats(stats_first, count / devices)
+    message = shape((1, frames, channels, cols), BF16)
+    latent, down, up, stats_first = call(
+        planes_kernel, [shape(block, BF16), message, message, small], [VMEM] * 2, (latent, par)
+    )
+    cotangent, down_c, up_c = call(planes_kernel, [shape(block, BF16), message, message], [VMEM], (cotangent,))
+    past, future_c = shifted(latent, "tm", 1), shifted(cotangent, "tm", -1)
+    near = row_halos(down, up, (past,))
+    near_c = row_halos(down_c, up_c, (future_c,))
+    around = with_columns(flags, latent, (past, near, shifted(near, "tm", 1)))
+    around_c = (future_c, near_c, shifted(near_c, "tm", -1))
+    stats_first = all_stats(stats_first, count / devices, ("height", "width", "tm"))
     (weight_first,) = call(weight_forward_kernel, [shape(taps, BF16)], [VMEM], (conv_first,))
     (weight_second_t,) = call(weight_back_kernel, [shape(taps, BF16)], [VMEM], (conv_second,))
     (weight_first_t,) = call(weight_back_kernel, [shape(taps, BF16)], [VMEM], (conv_first,))
@@ -683,7 +683,7 @@
         functools.partial(conv_first_kernel, count=count),
         [shape(block, F32), small, shape(stack, BF16)],
         [SMEM] + [VMEM] * 10,
-        (flags, latent, *around, par, stats_first, weight_first, around_c[0]),
+        (flags, latent, *around, par, stats_first, weight_first, near_c),
         flops=conv_flops,
         transcendentals=3 * latent.size,
     )
@@ -712,15 +712,14 @@
         scratch=[pltpu.VMEM((rows * cols, frames * channels), BF16)],
         flops=conv_flops,
     )
-    message = shape((1, frames, channels, cols), BF16)
     hidden_grad, down, up = call(
         functools.partial(hidden_grad_kernel, count=count),
         [shape(block, BF16), message, message],
         [VMEM] * 6,
         (hidden, scaled, par, stats_second, sums, halves_second[0]),
     )
-    (near,) = row_halos(down, up)
-    around = halo(hidden_grad, near, -1)
+    near = row_halos(down, up)
+    around = (shifted(hidden_grad, "tm", -1), near, shifted(near, "tm", -1))
     halves_first = call(
         weight_first_kernel,
         halves,

time: 192 us -> 195 us (1.016)
  starting transfers between devices: 101 us -> 107 us
  waiting for transfers between devices: 32.8 us -> 29.2 us
    ppermute x10 -> x12, starting transfers between devices: 20.4 us -> 28.5 us  [shifted(): lax.ppermute(value, axis, [(source, source + steps) for source in range(i...]
    unnamed x14 -> x24, local copies, waits for them, and re-layouts: 3.96 us -> 4.82 us
    ppermute x10 -> x12, waiting for transfers between devices: 13.2 us -> 12.5 us  [shifted(): lax.ppermute(value, axis, [(source, source + steps) for source in range(i...]
    pallas_call x28 -> x30, Pallas kernels: 50.7 us -> 50.8 us  [call(): pl.pallas_call(body, out_shape=tuple(outs), in_specs=specs, out_specs=tup...]
  transfers between devices with their start and end apart: 63 -> 65, of which waited for: 20 -> 21; matrix products, arithmetic and copies ran while one was open for 0% -> 0% of each run, Pallas kernels for 17% -> 18%
where the time goes in v9:
time: 195 us
  starting transfers between devices  107 us (55%)
  Pallas kernels  50.8 us (26%)
  waiting for transfers between devices  29.2 us (15%)
  local copies, waits for them, and re-layouts  5.82 us (3%)
    pallas_call x30, Pallas kernels, call(): pl.pallas_call(body, out_shape=tuple(outs), in_specs=specs, out_specs=tup...  50.8 us
    ppermute x12, starting transfers between devices, shifted(): lax.ppermute(value, axis, [(source, source + steps) for source in range(i...  28.5 us
    ppermute x14, starting transfers between devices, all_stats(): lax.ppermute(value, axis, pairs)  22.5 us
    ppermute x10, starting transfers between devices, swapped(): return lax.ppermute(value, 'width', [(0, 1), (1, 0)])  20.3 us
    ppermute x14, starting transfers between devices, all_sum(): parts = [value] + [lax.ppermute(value, axis, pairs) for pairs in exchanges]  20.1 us
    ppermute x12, waiting for transfers between devices, shifted(): lax.ppermute(value, axis, [(source, source + steps) for source in range(i...  12.5 us
    ppermute x14, waiting for transfers between devices, all_sum(): parts = [value] + [lax.ppermute(value, axis, pairs) for pairs in exchanges]  8.12 us
    ppermute x14, waiting for transfers between devices, all_stats(): lax.ppermute(value, axis, pairs)  6.02 us
  transfers between devices with their start and end apart: 65, of which 21 were waited for; matrix products, arithmetic and copies ran while one was open for 0% of the time, Pallas kernels for 18%

profile of v9, /device:TPU:1, one launch (start us, length us, event | category | flops | bytes accessed | tf_op | source)
XLA Modules:
  0.0 194.5 jit_solution(3975141075207766711)
XLA Ops:
  4.7 2.1 %collective-permute-start.6 = (f32[1,2,128]{2,1,0:T(2,128)S(1)}, f32[1,2,128]{2,1,0:T(2,128)S(1)}, u32[]{:S(2)}, u32[]{:S(2)}) collective-permute-start(f32[1,2,128]{2,1,0:T(2,128)S(1)} %get-tuple-element.42), channel_id=1, source_target_pairs={{0,2},{2,0},{4,6},{6,4},{1,3},{3,1},{5,7},{7,5},{8,10},{10,8},{12,... | collective-permute-start | bytes 3080 | tf_op jit(solution)/shard_map/ppermute | solution.py:511
  8.0 3.4 %collective-permute-start = (bf16[4,2,128,256]{3,2,1,0:T(8,128)(2,1)S(1)}, bf16[4,2,128,256]{3,2,1,0:T(8,128)(2,1)S(1)}, u32[]{:S(2)}, u32[]{:S(2)}) collective-permute-start(bf16[4,2,128,256]{3,2,1,0:T(8,128)(2,1)S(1)} %get-tuple-element.39.first_ref.own.refs_7_.latent), channel_id=1, source_target_pairs={{0,8},{8,16},{16,24},{1,9},{9,17},{17,25},{2,10},{10,18},{18,26},{... | collective-permute-start | bytes 1572872 | tf_op jit(solution)/shard_map/ppermute | solution.py:483
  11.4 3.1 %collective-permute-start.1 = (bf16[1,2,128,256]{3,2,1,0:T(8,128)(2,1)S(1)}, bf16[1,2,128,256]{3,2,1,0:T(8,128)(2,1)S(1)}, u32[]{:S(2)}, u32[]{:S(2)}) collective-permute-start(bf16[1,2,128,256]{3,2,1,0:T(8,128)(2,1)S(1)} %get-tuple-element.40), channel_id=1, source_target_pairs={{0,2},{2,4},{4,6},{1,3},{3,5},{5,7},{8,10},{10,12},{12,14},{9,11},... | collective-permute-start | bytes 393224 | tf_op jit(solution)/shard_map/ppermute | solution.py:483
  20.5 2.1 %collective-permute-start.9 = (f32[1,2,128]{2,1,0:T(2,128)S(1)}, f32[1,2,128]{2,1,0:T(2,128)S(1)}, u32[]{:S(2)}, u32[]{:S(2)}) collective-permute-start(f32[1,2,128]{2,1,0:T(2,128)S(1)} %pad_maximum_fusion), channel_id=1, source_target_pairs={{0,1},{1,0},{2,3},{3,2},{4,5},{5,4},{6,7},{7,6},{8,9},{9,8},{10,11... | collective-permute-start | bytes 3080 | tf_op jit(solution)/shard_map/ppermute | solution.py:511
  23.6 4.9 %collective-permute-start.3 = (bf16[2,2,128,256]{3,2,1,0:T(8,128)(2,1)S(1)}, bf16[2,2,128,256]{3,2,1,0:T(8,128)(2,1)}, u32[]{:S(2)}, u32[]{:S(2)}) collective-permute-start(bf16[2,2,128,256]{3,2,1,0:T(8,128)(2,1)S(1)} %shard_map.113.first_ref.near), channel_id=1, source_target_pairs={{0,8},{8,16},{16,24},{1,9},{9,17},{17,25},{2,10},{10,18},{18,26},{... | collective-permute-start | bytes 786440 | tf_op jit(solution)/shard_map/ppermute | solution.py:483
  32.7 4.0 %collective-permute-start.13 = (bf16[1,2,128,256]{3,2,1,0:T(8,128)(2,1)}, bf16[1,2,128,256]{3,2,1,0:T(8,128)(2,1)S(1)}, u32[]{:S(2)}, u32[]{:S(2)}) collective-permute-start(bf16[1,2,128,256]{3,2,1,0:T(8,128)(2,1)} %copy-done.11), channel_id=1, source_target_pairs={{0,2},{2,4},{4,6},{1,3},{3,5},{5,7},{8,10},{10,12},{12,14},{9,11},... | collective-permute-start | bytes 393224 | tf_op jit(solution)/shard_map/ppermute | solution.py:483
  41.7 3.3 %collective-permute-start.4 = (bf16[128,128]{1,0:T(8,128)(2,1)S(1)}, bf16[128,128]{1,0:T(8,128)(2,1)S(1)}, u32[]{:S(2)}, u32[]{:S(2)}) collective-permute-start(bf16[128,128]{1,0:T(8,128)(2,1)S(1)} %shard_map.114), channel_id=1, source_target_pairs={{0,1},{1,0},{2,3},{3,2},{4,5},{5,4},{6,7},{7,6},{8,9},{9,8},{10,11... | collective-permute-start | bytes 98312 | tf_op jit(solution)/shard_map/ppermute | solution.py:524
  47.7 5.1 %shard_map.119 = (f32[4,2,128,256]{3,2,1,0:T(8,128)S(1)}, f32[1,2,128]{2,1,0:T(2,128)S(1)}, bf16[6,4,384,256]{3,2,1,0:T(8,128)(2,1)S(1)}) custom-call(s32[6]{0:T(128)S(1)} %stack.57.flag_ref, bf16[4,2,128,256]{3,2,1,0:T(8,128)(2,1)S(1)} %copy-done.3, bf16[4,2,128,256]{3,2,1,0:T(8,128)(2,1)S(1)} %copy-done.6, ...), custom_call_target="tpu_custom_call" | custom-call | flops 7247757312 | bytes 10033176 | tf_op jit(solution)/shard_map/pallas_call | solution.py:24
  54.3 3.1 %collective-permute-start.20 = (f32[1,2,128]{2,1,0:T(2,128)S(1)}, f32[1,2,128]{2,1,0:T(2,128)S(1)}, u32[]{:S(2)}, u32[]{:S(2)}) collective-permute-start(f32[1,2,128]{2,1,0:T(2,128)S(1)} %get-tuple-element.47.refs_0_), channel_id=1, source_target_pairs={{0,16},{8,24},{16,0},{24,8},{1,17},{9,25},{17,1},{25,9},{2,18},{10... | collective-permute-start | bytes 3080 | tf_op jit(solution)/shard_map/ppermute | solution.py:511
  58.4 3.3 %collective-permute-done.21 = f32[1,2,128]{2,1,0:T(2,128)S(1)} collective-permute-done((f32[1,2,128]{2,1,0:T(2,128)S(1)}, f32[1,2,128]{2,1,0:T(2,128)S(1)}, u32[]{:S(2)}, u32[]{:S(2)}) %collective-permute-start.21) | collective-permute-done | bytes 1056 | tf_op jit(solution)/shard_map/ppermute | solution.py:511
  61.7 2.4 %collective-permute-start.22 = (f32[1,2,128]{2,1,0:T(2,128)S(1)}, f32[1,2,128]{2,1,0:T(2,128)S(1)}, u32[]{:S(2)}, u32[]{:S(2)}) collective-permute-start(f32[1,2,128]{2,1,0:T(2,128)S(1)} %pad_maximum_fusion.3), channel_id=1, source_target_pairs={{0,2},{2,0},{4,6},{6,4},{1,3},{3,1},{5,7},{7,5},{8,10},{10,8},{12,... | collective-permute-start | bytes 3080 | tf_op jit(solution)/shard_map/ppermute | solution.py:511
  69.0 3.7 %collective-permute-start.25 = (f32[1,2,128]{2,1,0:T(2,128)S(1)}, f32[1,2,128]{2,1,0:T(2,128)S(1)}, u32[]{:S(2)}, u32[]{:S(2)}) collective-permute-start(f32[1,2,128]{2,1,0:T(2,128)S(1)} %pad_maximum_fusion.4), channel_id=1, source_target_pairs={{0,1},{1,0},{2,3},{3,2},{4,5},{5,4},{6,7},{7,6},{8,9},{9,8},{10,11... | collective-permute-start | bytes 3080 | tf_op jit(solution)/shard_map/ppermute | solution.py:511
  74.7 3.9 %collective-permute-start.18 = (bf16[128,128]{1,0:T(8,128)(2,1)S(1)}, bf16[128,128]{1,0:T(8,128)(2,1)S(1)}, u32[]{:S(2)}, u32[]{:S(2)}) collective-permute-start(bf16[128,128]{1,0:T(8,128)(2,1)S(1)} %shard_map.121), channel_id=1, source_target_pairs={{0,1},{1,0},{2,3},{3,2},{4,5},{5,4},{6,7},{7,6},{8,9},{9,8},{10,11... | collective-permute-start | bytes 98312 | tf_op jit(solution)/shard_map/ppermute | solution.py:524
  78.7 2.2 %shard_map.120 = bf16[128,128]{1,0:T(8,128)(2,1)S(1)} custom-call(s32[6]{0:T(128)S(1)} %stack.57.flag_ref, bf16[4,2,128,256]{3,2,1,0:T(8,128)(2,1)} %get-tuple-element.45.first_ref.refs_0_.cotangent, bf16[4,2,128,256]{3,2,1,0:T(8,128)(2,1)} %collective-permute-done.15.refs_0_.second_ref.refs_1_, f32[1,2,128]{2,1,0:T(2,128)S(1)} %get-tuple-element.47.refs_0_), custom_call_target="tpu_custom_call" | custom-call | bytes 1082392 | tf_op jit(solution)/shard_map/pallas_call | solution.py:24
  82.1 4.1 %shard_map.123 = (f32[4,2,128,256]{3,2,1,0:T(8,128)S(1)}, bf16[6,4,384,256]{3,2,1,0:T(8,128)(2,1)S(1)}) custom-call(s32[6]{0:T(128)S(1)} %stack.57.flag_ref, bf16[4,2,128,256]{3,2,1,0:T(8,128)(2,1)} %get-tuple-element.45.first_ref.refs_0_.cotangent, bf16[4,2,128,256]{3,2,1,0:T(8,128)(2,1)} %collective-permute-done.15.refs_0_.second_ref.refs_1_, ...), custom_call_target="tpu_custom_call" | custom-call | flops 7247757312 | bytes 9764888 | tf_op jit(solution)/shard_map/pallas_call | solution.py:24
  87.3 3.5 %collective-permute-start.28 = (f32[1,2,128]{2,1,0:T(2,128)S(1)}, f32[1,2,128]{2,1,0:T(2,128)S(1)}, u32[]{:S(2)}, u32[]{:S(2)}) collective-permute-start(f32[1,2,128]{2,1,0:T(2,128)S(1)} %get-tuple-element.50), channel_id=1, source_target_pairs={{0,24},{8,16},{16,8},{24,0},{1,25},{9,17},{17,9},{25,1},{2,26},{10... | collective-permute-start | bytes 3080 | tf_op jit(solution)/shard_map/ppermute | solution.py:504
  96.9 3.0 %collective-permute-start.32 = (f32[1,2,128]{2,1,0:T(2,128)S(1)}, f32[1,2,128]{2,1,0:T(2,128)S(1)}, u32[]{:S(2)}, u32[]{:S(2)}) collective-permute-start(f32[1,2,128]{2,1,0:T(2,128)S(1)} %add_add_fusion.2), channel_id=1, source_target_pairs={{0,1},{1,0},{2,3},{3,2},{4,5},{5,4},{6,7},{7,6},{8,9},{9,8},{10,11... | collective-permute-start | bytes 3080 | tf_op jit(solution)/shard_map/ppermute | solution.py:504
  99.9 4.1 %shard_map.125 = (f32[2048,128]{1,0:T(8,128)S(1)}, f32[2048,128]{1,0:T(8,128)S(1)}) custom-call(s32[6]{0:T(128)S(1)} %stack.57.flag_ref, bf16[6,4,384,256]{3,2,1,0:T(8,128)(2,1)S(1)} %get-tuple-element.51.stack_ref, bf16[4,2,128,256]{3,2,1,0:T(8,128)(2,1)S(1)} %get-tuple-element.52.act_ref), custom_call_target="tpu_custom_call" | custom-call | flops 7247757312 | bytes 7340056 | tf_op jit(solution)/shard_map/pallas_call | solution.py:24
  104.6 4.1 %shard_map.128 = (f32[2048,128]{1,0:T(8,128)S(1)}, f32[2048,128]{1,0:T(8,128)S(1)}) custom-call(s32[6]{0:T(128)S(1)} %stack.57.flag_ref, bf16[6,4,384,256]{3,2,1,0:T(8,128)(2,1)S(1)} %get-tuple-element.58.stack_ref, bf16[4,2,128,256]{3,2,1,0:T(8,128)(2,1)S(1)} %get-tuple-element.54.grad_ref.first_ref.refs_0_), custom_call_target="tpu_custom_call" | custom-call | flops 7247757312 | bytes 7340056 | tf_op jit(solution)/shard_map/pallas_call | solution.py:24
  110.6 3.6 %collective-permute-start.34 = (bf16[1,2,128,256]{3,2,1,0:T(8,128)(2,1)S(1)}, bf16[1,2,128,256]{3,2,1,0:T(8,128)(2,1)S(1)}, u32[]{:S(2)}, u32[]{:S(2)}) collective-permute-start(bf16[1,2,128,256]{3,2,1,0:T(8,128)(2,1)S(1)} %get-tuple-element.55), channel_id=1, source_target_pairs={{0,2},{2,4},{4,6},{1,3},{3,5},{5,7},{8,10},{10,12},{12,14},{9,11},... | collective-permute-start | bytes 393224 | tf_op jit(solution)/shard_map/ppermute | solution.py:483
  117.0 3.8 %collective-permute-done.35.below_ref = bf16[1,2,128,256]{3,2,1,0:T(8,128)(2,1)S(1)} collective-permute-done((bf16[1,2,128,256]{3,2,1,0:T(8,128)(2,1)S(1)}, bf16[1,2,128,256]{3,2,1,0:T(8,128)(2,1)S(1)}, u32[]{:S(2)}, u32[]{:S(2)}) %collective-permute-start.35) | collective-permute-done | bytes 131104 | tf_op jit(solution)/shard_map/ppermute | solution.py:483
  123.5 6.2 %collective-permute-done.36.second_ref.refs_3_ = bf16[2,2,128,256]{3,2,1,0:T(8,128)(2,1)S(1)} collective-permute-done((bf16[2,2,128,256]{3,2,1,0:T(8,128)(2,1)S(1)}, bf16[2,2,128,256]{3,2,1,0:T(8,128)(2,1)S(1)}, u32[]{:S(2)}, u32[]{:S(2)}) %collective-permute-start.36) | collective-permute-done | bytes 262176 | tf_op jit(solution)/shard_map/ppermute | solution.py:483
  130.6 2.2 %collective-permute-start.40 = (bf16[128,128]{1,0:T(8,128)(2,1)S(1)}, bf16[128,128]{1,0:T(8,128)(2,1)S(1)}, u32[]{:S(2)}, u32[]{:S(2)}) collective-permute-start(bf16[128,128]{1,0:T(8,128)(2,1)S(1)} %shard_map.131), channel_id=1, source_target_pairs={{0,1},{1,0},{2,3},{3,2},{4,5},{5,4},{6,7},{7,6},{8,9},{9,8},{10,11... | collective-permute-start | bytes 98312 | tf_op jit(solution)/shard_map/ppermute | solution.py:524
  137.4 4.1 %shard_map.133 = (f32[4,2,128,256]{3,2,1,0:T(8,128)S(1)}, f32[1,2,128]{2,1,0:T(2,128)S(1)}) custom-call(s32[6]{0:T(128)S(1)} %stack.57.flag_ref, bf16[4,2,128,256]{3,2,1,0:T(8,128)(2,1)S(1)} %get-tuple-element.54.grad_ref.first_ref.refs_0_, bf16[4,2,128,256]{3,2,1,0:T(8,128)(2,1)S(1)} %collective-permute-done.33.second_ref.refs_1_.refs_4_, ...), custom_call_target="tpu_custom_call" | custom-call | flops 7247757312 | bytes 5576728 | tf_op jit(solution)/shard_map/pallas_call | solution.py:24
  153.7 2.0 %collective-permute-start.53 = (s16[2,4,32,128]{3,2,1,0:T(8,128)(2,1)S(1)}, s16[2,4,32,128]{3,2,1,0:T(8,128)(2,1)S(1)}, u32[]{:S(2)}, u32[]{:S(2)}) collective-permute-start(s16[2,4,32,128]{3,2,1,0:T(8,128)(2,1)S(1)} %get-tuple-element.71), channel_id=1, source_target_pairs={{0,24},{8,16},{16,8},{24,0},{1,25},{9,17},{17,9},{25,1},{2,26},{10... | collective-permute-start | bytes 196616 | tf_op jit(solution)/shard_map/ppermute | solution.py:560
  155.7 5.1 %collective-permute-start.47 = (f32[1,2,128]{2,1,0:T(2,128)S(1)}, f32[1,2,128]{2,1,0:T(2,128)S(1)}, u32[]{:S(2)}, u32[]{:S(2)}) collective-permute-start(f32[1,2,128]{2,1,0:T(2,128)S(1)} %add_add_fusion), channel_id=1, source_target_pairs={{0,1},{1,0},{2,3},{3,2},{4,5},{5,4},{6,7},{7,6},{8,9},{9,8},{10,11... | collective-permute-start | bytes 3080 | tf_op jit(solution)/shard_map/ppermute | solution.py:504
  163.1 2.3 %collective-permute-start.56 = (s16[2,4,32,128]{3,2,1,0:T(8,128)(2,1)S(1)}, s16[2,4,32,128]{3,2,1,0:T(8,128)(2,1)S(1)}, u32[]{:S(2)}, u32[]{:S(2)}) collective-permute-start(s16[2,4,32,128]{3,2,1,0:T(8,128)(2,1)S(1)} %shard_map.136.refs_0_), channel_id=1, source_target_pairs={{0,24},{8,16},{16,8},{24,0},{1,25},{9,17},{17,9},{25,1},{2,26},{10... | collective-permute-start | bytes 196616 | tf_op jit(solution)/shard_map/ppermute | solution.py:574
  165.4 2.9 %shard_map.134 = (f32[128,2,4,256]{3,2,1,0:T(4,128)}, f32[8,128]{1,0:T(8,128)S(1)}) custom-call(f32[4,2,128,256]{3,2,1,0:T(8,128)S(1)} %get-tuple-element.62.scaled, bf16[4,2,128,256]{3,2,1,0:T(8,128)(2,1)S(1)} %copy-done.3, bf16[4,2,128,256]{3,2,1,0:T(8,128)(2,1)} %get-tuple-element.45.first_ref.refs_0_.cotangent, ...), custom_call_target="tpu_custom_call" | custom-call | bytes 3155968 | tf_op jit(solution)/shard_map/pallas_call | solution.py:24
  176.1 6.7 %collective-permute-start.64 = (s16[64,32,128]{2,1,0:T(8,128)(2,1)S(1)}, s16[64,32,128]{2,1,0:T(8,128)(2,1)S(1)}, u32[]{:S(2)}, u32[]{:S(2)}) collective-permute-start(s16[64,32,128]{2,1,0:T(8,128)(2,1)S(1)} %bitcast.25), channel_id=1, source_target_pairs={{0,1},{1,0},{2,3},{3,2},{4,5},{5,4},{6,7},{7,6},{8,9},{9,8},{10,11... | collective-permute-start | bytes 1572872 | tf_op jit(solution)/shard_map/ppermute | solution.py:524
  183.4 3.3 %collective-permute-start.60 = (s16[64,32,128]{2,1,0:T(8,128)(2,1)S(1)}, s16[64,32,128]{2,1,0:T(8,128)(2,1)S(1)}, u32[]{:S(2)}, u32[]{:S(2)}) collective-permute-start(s16[64,32,128]{2,1,0:T(8,128)(2,1)S(1)} %bitcast.27), channel_id=1, source_target_pairs={{0,1},{1,0},{2,3},{3,2},{4,5},{5,4},{6,7},{7,6},{8,9},{9,8},{10,11... | collective-permute-start | bytes 1572872 | tf_op jit(solution)/shard_map/ppermute | solution.py:524
  186.7 3.9 %shard_map.141 = f32[128,3456]{1,0:T(8,128)} custom-call(s32[6]{0:T(128)S(1)} %stack.57.flag_ref, s16[64,32,128]{2,1,0:T(8,128)(2,1)S(1)} %bitcast.26, s16[64,32,128]{2,1,0:T(8,128)(2,1)S(1)} %collective-permute-done.64.theirs_ref), custom_call_target="tpu_custom_call" | custom-call | bytes 2818072 | tf_op jit(solution)/shard_map/pallas_call | solution.py:24
  190.6 3.9 %shard_map.139 = f32[128,3456]{1,0:T(8,128)} custom-call(s32[6]{0:T(128)S(1)} %stack.57.flag_ref, s16[64,32,128]{2,1,0:T(8,128)(2,1)S(1)} %bitcast.28, s16[64,32,128]{2,1,0:T(8,128)(2,1)S(1)} %collective-permute-done.60.theirs_ref), custom_call_target="tpu_custom_call" | custom-call | bytes 2818072 | tf_op jit(solution)/shard_map/pallas_call | solution.py:24
  (177 shorter events, 77.8 us)
Async XLA Ops:
  4.7 12.6 %collective-permute-start.6 = (f32[1,2,128]{2,1,0:T(2,128)S(1)}, f32[1,2,128]{2,1,0:T(2,128)S(1)}, u32[]{:S(2)}, u32[]{:S(2)}) collective-permute-start(f32[1,2,128]{2,1,0:T(2,128)S(1)} %get-tuple-element.42), channel_id=1, source_target_pairs={{0,2},{2,0},{4,6},{6,4},{1,3},{3,1},{5,7},{7,5},{8,10},{10,8},{12,... | collective-permute-start | bytes 3080 | tf_op jit(solution)/shard_map/ppermute | solution.py:511
  6.8 12.4 %collective-permute-start.7 = (f32[1,2,128]{2,1,0:T(2,128)S(1)}, f32[1,2,128]{2,1,0:T(2,128)S(1)}, u32[]{:S(2)}, u32[]{:S(2)}) collective-permute-start(f32[1,2,128]{2,1,0:T(2,128)S(1)} %get-tuple-element.42), channel_id=1, source_target_pairs={{0,4},{2,6},{4,0},{6,2},{1,5},{3,7},{5,1},{7,3},{8,12},{10,14},{12... | collective-permute-start | bytes 3080 | tf_op jit(solution)/shard_map/ppermute | solution.py:511
  8.0 12.5 %collective-permute-start.8 = (f32[1,2,128]{2,1,0:T(2,128)S(1)}, f32[1,2,128]{2,1,0:T(2,128)S(1)}, u32[]{:S(2)}, u32[]{:S(2)}) collective-permute-start(f32[1,2,128]{2,1,0:T(2,128)S(1)} %get-tuple-element.42), channel_id=1, source_target_pairs={{0,6},{2,4},{4,2},{6,0},{1,7},{3,5},{5,3},{7,1},{8,14},{10,12},{12... | collective-permute-start | bytes 3080 | tf_op jit(solution)/shard_map/ppermute | solution.py:511
  8.0 15.5 %collective-permute-start = (bf16[4,2,128,256]{3,2,1,0:T(8,128)(2,1)S(1)}, bf16[4,2,128,256]{3,2,1,0:T(8,128)(2,1)S(1)}, u32[]{:S(2)}, u32[]{:S(2)}) collective-permute-start(bf16[4,2,128,256]{3,2,1,0:T(8,128)(2,1)S(1)} %get-tuple-element.39.first_ref.own.refs_7_.latent), channel_id=1, source_target_pairs={{0,8},{8,16},{16,24},{1,9},{9,17},{17,25},{2,10},{10,18},{18,26},{... | collective-permute-start | bytes 1572872 | tf_op jit(solution)/shard_map/ppermute | solution.py:483
  11.4 12.0 %collective-permute-start.1 = (bf16[1,2,128,256]{3,2,1,0:T(8,128)(2,1)S(1)}, bf16[1,2,128,256]{3,2,1,0:T(8,128)(2,1)S(1)}, u32[]{:S(2)}, u32[]{:S(2)}) collective-permute-start(bf16[1,2,128,256]{3,2,1,0:T(8,128)(2,1)S(1)} %get-tuple-element.40), channel_id=1, source_target_pairs={{0,2},{2,4},{4,6},{1,3},{3,5},{5,7},{8,10},{10,12},{12,14},{9,11},... | collective-permute-start | bytes 393224 | tf_op jit(solution)/shard_map/ppermute | solution.py:483
  19.2 27.3 %collective-permute-start.15 = (bf16[4,2,128,256]{3,2,1,0:T(8,128)(2,1)}, bf16[4,2,128,256]{3,2,1,0:T(8,128)(2,1)}, u32[]{:S(2)}, u32[]{:S(2)}) collective-permute-start(bf16[4,2,128,256]{3,2,1,0:T(8,128)(2,1)} %get-tuple-element.45.first_ref.refs_0_.cotangent), channel_id=1, source_target_pairs={{8,0},{16,8},{24,16},{9,1},{17,9},{25,17},{10,2},{18,10},{26,18},{... | collective-permute-start | bytes 1572872 | tf_op jit(solution)/shard_map/ppermute | solution.py:483
  23.6 21.5 %collective-permute-start.3 = (bf16[2,2,128,256]{3,2,1,0:T(8,128)(2,1)S(1)}, bf16[2,2,128,256]{3,2,1,0:T(8,128)(2,1)}, u32[]{:S(2)}, u32[]{:S(2)}) collective-permute-start(bf16[2,2,128,256]{3,2,1,0:T(8,128)(2,1)S(1)} %shard_map.113.first_ref.near), channel_id=1, source_target_pairs={{0,8},{8,16},{16,24},{1,9},{9,17},{17,25},{2,10},{10,18},{18,26},{... | collective-permute-start | bytes 786440 | tf_op jit(solution)/shard_map/ppermute | solution.py:483
  29.2 7.6 %collective-permute-start.11 = (f32[1,2,128]{2,1,0:T(2,128)S(1)}, f32[1,2,128]{2,1,0:T(2,128)S(1)}, u32[]{:S(2)}, u32[]{:S(2)}) collective-permute-start(f32[1,2,128]{2,1,0:T(2,128)S(1)} %pad_maximum_fusion.1), channel_id=1, source_target_pairs={{0,16},{8,24},{16,0},{24,8},{1,17},{9,25},{17,1},{25,9},{2,18},{10... | collective-permute-start | bytes 3080 | tf_op jit(solution)/shard_map/ppermute | solution.py:511
  31.1 7.0 %collective-permute-start.12 = (f32[1,2,128]{2,1,0:T(2,128)S(1)}, f32[1,2,128]{2,1,0:T(2,128)S(1)}, u32[]{:S(2)}, u32[]{:S(2)}) collective-permute-start(f32[1,2,128]{2,1,0:T(2,128)S(1)} %pad_maximum_fusion.1), channel_id=1, source_target_pairs={{0,24},{8,16},{16,8},{24,0},{1,25},{9,17},{17,9},{25,1},{2,26},{10... | collective-permute-start | bytes 3080 | tf_op jit(solution)/shard_map/ppermute | solution.py:511
  32.7 13.7 %collective-permute-start.13 = (bf16[1,2,128,256]{3,2,1,0:T(8,128)(2,1)}, bf16[1,2,128,256]{3,2,1,0:T(8,128)(2,1)S(1)}, u32[]{:S(2)}, u32[]{:S(2)}) collective-permute-start(bf16[1,2,128,256]{3,2,1,0:T(8,128)(2,1)} %copy-done.11), channel_id=1, source_target_pairs={{0,2},{2,4},{4,6},{1,3},{3,5},{5,7},{8,10},{10,12},{12,14},{9,11},... | collective-permute-start | bytes 393224 | tf_op jit(solution)/shard_map/ppermute | solution.py:483
  36.8 9.7 %collective-permute-start.14 = (bf16[1,2,128,256]{3,2,1,0:T(8,128)(2,1)}, bf16[1,2,128,256]{3,2,1,0:T(8,128)(2,1)S(1)}, u32[]{:S(2)}, u32[]{:S(2)}) collective-permute-start(bf16[1,2,128,256]{3,2,1,0:T(8,128)(2,1)} %copy-done.10), channel_id=1, source_target_pairs={{2,0},{4,2},{6,4},{3,1},{5,3},{7,5},{10,8},{12,10},{14,12},{11,9},... | collective-permute-start | bytes 393224 | tf_op jit(solution)/shard_map/ppermute | solution.py:483
  61.7 6.5 %collective-permute-start.22 = (f32[1,2,128]{2,1,0:T(2,128)S(1)}, f32[1,2,128]{2,1,0:T(2,128)S(1)}, u32[]{:S(2)}, u32[]{:S(2)}) collective-permute-start(f32[1,2,128]{2,1,0:T(2,128)S(1)} %pad_maximum_fusion.3), channel_id=1, source_target_pairs={{0,2},{2,0},{4,6},{6,4},{1,3},{3,1},{5,7},{7,5},{8,10},{10,8},{12,... | collective-permute-start | bytes 3080 | tf_op jit(solution)/shard_map/ppermute | solution.py:511
  66.7 7.1 %collective-permute-start.16 = (bf16[2,2,128,256]{3,2,1,0:T(8,128)(2,1)S(1)}, bf16[2,2,128,256]{3,2,1,0:T(8,128)(2,1)S(1)}, u32[]{:S(2)}, u32[]{:S(2)}) collective-permute-start(bf16[2,2,128,256]{3,2,1,0:T(8,128)(2,1)S(1)} %shard_map.118.after.first_ref.refs_2_), channel_id=1, source_target_pairs={{8,0},{16,8},{24,16},{9,1},{17,9},{25,17},{10,2},{18,10},{26,18},{... | collective-permute-start | bytes 786440 | tf_op jit(solution)/shard_map/ppermute | solution.py:483
  69.0 12.0 %collective-permute-start.25 = (f32[1,2,128]{2,1,0:T(2,128)S(1)}, f32[1,2,128]{2,1,0:T(2,128)S(1)}, u32[]{:S(2)}, u32[]{:S(2)}) collective-permute-start(f32[1,2,128]{2,1,0:T(2,128)S(1)} %pad_maximum_fusion.4), channel_id=1, source_target_pairs={{0,1},{1,0},{2,3},{3,2},{4,5},{5,4},{6,7},{7,6},{8,9},{9,8},{10,11... | collective-permute-start | bytes 3080 | tf_op jit(solution)/shard_map/ppermute | solution.py:511
  96.9 7.2 %collective-permute-start.32 = (f32[1,2,128]{2,1,0:T(2,128)S(1)}, f32[1,2,128]{2,1,0:T(2,128)S(1)}, u32[]{:S(2)}, u32[]{:S(2)}) collective-permute-start(f32[1,2,128]{2,1,0:T(2,128)S(1)} %add_add_fusion.2), channel_id=1, source_target_pairs={{0,1},{1,0},{2,3},{3,2},{4,5},{5,4},{6,7},{7,6},{8,9},{9,8},{10,11... | collective-permute-start | bytes 3080 | tf_op jit(solution)/shard_map/ppermute | solution.py:504
  104.0 18.3 %collective-permute-start.37 = (f32[64,32,128]{2,1,0:T(8,128)S(1)}, f32[64,32,128]{2,1,0:T(8,128)S(1)}, u32[]{:S(2)}, u32[]{:S(2)}) collective-permute-start(f32[64,32,128]{2,1,0:T(8,128)S(1)} %bitcast.44), channel_id=1, source_target_pairs={{0,1},{1,0},{2,3},{3,2},{4,5},{5,4},{6,7},{7,6},{8,9},{9,8},{10,11... | collective-permute-start | bytes 3145736 | tf_op jit(solution)/shard_map/ppermute | solution.py:524
  108.7 13.6 %collective-permute-start.38 = (f32[64,32,128]{2,1,0:T(8,128)S(1)}, f32[64,32,128]{2,1,0:T(8,128)S(1)}, u32[]{:S(2)}, u32[]{:S(2)}) collective-permute-start(f32[64,32,128]{2,1,0:T(8,128)S(1)} %bitcast.45), channel_id=1, source_target_pairs={{0,1},{1,0},{2,3},{3,2},{4,5},{5,4},{6,7},{7,6},{8,9},{9,8},{10,11... | collective-permute-start | bytes 3145736 | tf_op jit(solution)/shard_map/ppermute | solution.py:524
  109.3 23.4 %collective-permute-start.33 = (bf16[4,2,128,256]{3,2,1,0:T(8,128)(2,1)S(1)}, bf16[4,2,128,256]{3,2,1,0:T(8,128)(2,1)S(1)}, u32[]{:S(2)}, u32[]{:S(2)}) collective-permute-start(bf16[4,2,128,256]{3,2,1,0:T(8,128)(2,1)S(1)} %get-tuple-element.54.grad_ref.first_ref.refs_0_), channel_id=1, source_target_pairs={{8,0},{16,8},{24,16},{9,1},{17,9},{25,17},{10,2},{18,10},{26,18},{... | collective-permute-start | bytes 1572872 | tf_op jit(solution)/shard_map/ppermute | solution.py:483
  114.2 6.7 %collective-permute-start.35 = (bf16[1,2,128,256]{3,2,1,0:T(8,128)(2,1)S(1)}, bf16[1,2,128,256]{3,2,1,0:T(8,128)(2,1)S(1)}, u32[]{:S(2)}, u32[]{:S(2)}) collective-permute-start(bf16[1,2,128,256]{3,2,1,0:T(8,128)(2,1)S(1)} %get-tuple-element.56), channel_id=1, source_target_pairs={{2,0},{4,2},{6,4},{3,1},{5,3},{7,5},{10,8},{12,10},{14,12},{11,9},... | collective-permute-start | bytes 393224 | tf_op jit(solution)/shard_map/ppermute | solution.py:483
  120.8 8.8 %collective-permute-start.36 = (bf16[2,2,128,256]{3,2,1,0:T(8,128)(2,1)S(1)}, bf16[2,2,128,256]{3,2,1,0:T(8,128)(2,1)S(1)}, u32[]{:S(2)}, u32[]{:S(2)}) collective-permute-start(bf16[2,2,128,256]{3,2,1,0:T(8,128)(2,1)S(1)} %shard_map.127.first_ref.refs_2_.refs_5_), channel_id=1, source_target_pairs={{8,0},{16,8},{24,16},{9,1},{17,9},{25,17},{10,2},{18,10},{26,18},{... | collective-permute-start | bytes 786440 | tf_op jit(solution)/shard_map/ppermute | solution.py:483
  130.6 6.9 %collective-permute-start.40 = (bf16[128,128]{1,0:T(8,128)(2,1)S(1)}, bf16[128,128]{1,0:T(8,128)(2,1)S(1)}, u32[]{:S(2)}, u32[]{:S(2)}) collective-permute-start(bf16[128,128]{1,0:T(8,128)(2,1)S(1)} %shard_map.131), channel_id=1, source_target_pairs={{0,1},{1,0},{2,3},{3,2},{4,5},{5,4},{6,7},{7,6},{8,9},{9,8},{10,11... | collective-permute-start | bytes 98312 | tf_op jit(solution)/shard_map/ppermute | solution.py:524
  134.7 14.8 %collective-permute-start.48 = (s16[2,16,32,128]{3,2,1,0:T(8,128)(2,1)S(1)}, s16[2,16,32,128]{3,2,1,0:T(8,128)(2,1)S(1)}, u32[]{:S(2)}, u32[]{:S(2)}) collective-permute-start(s16[2,16,32,128]{3,2,1,0:T(8,128)(2,1)S(1)} %get-tuple-element.61.refs_0_), channel_id=1, source_target_pairs={{0,2},{2,0},{4,6},{6,4},{1,3},{3,1},{5,7},{7,5},{8,10},{10,8},{12,... | collective-permute-start | bytes 786440 | tf_op jit(solution)/shard_map/ppermute | solution.py:544
  135.8 15.3 %collective-permute-start.49 = (s16[2,16,32,128]{3,2,1,0:T(8,128)(2,1)S(1)}, s16[2,16,32,128]{3,2,1,0:T(8,128)(2,1)S(1)}, u32[]{:S(2)}, u32[]{:S(2)}) collective-permute-start(s16[2,16,32,128]{3,2,1,0:T(8,128)(2,1)S(1)} %get-tuple-element.66), channel_id=1, source_target_pairs={{0,4},{2,6},{4,0},{6,2},{1,5},{3,7},{5,1},{7,3},{8,12},{10,14},{12... | collective-permute-start | bytes 786440 | tf_op jit(solution)/shard_map/ppermute | solution.py:544
  135.8 15.3 %collective-permute-start.50 = (s16[2,16,32,128]{3,2,1,0:T(8,128)(2,1)S(1)}, s16[2,16,32,128]{3,2,1,0:T(8,128)(2,1)S(1)}, u32[]{:S(2)}, u32[]{:S(2)}) collective-permute-start(s16[2,16,32,128]{3,2,1,0:T(8,128)(2,1)S(1)} %get-tuple-element.67), channel_id=1, source_target_pairs={{0,6},{2,4},{4,2},{6,0},{1,7},{3,5},{5,3},{7,1},{8,14},{10,12},{12... | collective-permute-start | bytes 786440 | tf_op jit(solution)/shard_map/ppermute | solution.py:544
  152.1 9.5 %collective-permute-start.51 = (s16[2,4,32,128]{3,2,1,0:T(8,128)(2,1)S(1)}, s16[2,4,32,128]{3,2,1,0:T(8,128)(2,1)S(1)}, u32[]{:S(2)}, u32[]{:S(2)}) collective-permute-start(s16[2,4,32,128]{3,2,1,0:T(8,128)(2,1)S(1)} %get-tuple-element.69), channel_id=1, source_target_pairs={{0,8},{8,0},{16,24},{24,16},{1,9},{9,1},{17,25},{25,17},{2,10},{10... | collective-permute-start | bytes 196616 | tf_op jit(solution)/shard_map/ppermute | solution.py:560
  152.2 9.5 %collective-permute-start.52 = (s16[2,4,32,128]{3,2,1,0:T(8,128)(2,1)S(1)}, s16[2,4,32,128]{3,2,1,0:T(8,128)(2,1)S(1)}, u32[]{:S(2)}, u32[]{:S(2)}) collective-permute-start(s16[2,4,32,128]{3,2,1,0:T(8,128)(2,1)S(1)} %get-tuple-element.70), channel_id=1, source_target_pairs={{0,16},{8,24},{16,0},{24,8},{1,17},{9,25},{17,1},{25,9},{2,18},{10... | collective-permute-start | bytes 196616 | tf_op jit(solution)/shard_map/ppermute | solution.py:560
  153.7 8.0 %collective-permute-start.53 = (s16[2,4,32,128]{3,2,1,0:T(8,128)(2,1)S(1)}, s16[2,4,32,128]{3,2,1,0:T(8,128)(2,1)S(1)}, u32[]{:S(2)}, u32[]{:S(2)}) collective-permute-start(s16[2,4,32,128]{3,2,1,0:T(8,128)(2,1)S(1)} %get-tuple-element.71), channel_id=1, source_target_pairs={{0,24},{8,16},{16,8},{24,0},{1,25},{9,17},{17,9},{25,1},{2,26},{10... | collective-permute-start | bytes 196616 | tf_op jit(solution)/shard_map/ppermute | solution.py:560
  171.6 11.2 %collective-permute-start.57 = (s16[16,32,128]{2,1,0:T(8,128)(2,1)S(1)}, s16[16,32,128]{2,1,0:T(8,128)(2,1)S(1)}, u32[]{:S(2)}, u32[]{:S(2)}) collective-permute-start(s16[16,32,128]{2,1,0:T(8,128)(2,1)S(1)} %bitcast.36), channel_id=1, source_target_pairs={{0,2},{2,0},{4,6},{6,4},{1,3},{3,1},{5,7},{7,5},{8,10},{10,8},{12,... | collective-permute-start | bytes 393224 | tf_op jit(solution)/shard_map/ppermute | solution.py:585
  172.9 9.9 %collective-permute-start.58 = (s16[16,32,128]{2,1,0:T(8,128)(2,1)S(1)}, s16[16,32,128]{2,1,0:T(8,128)(2,1)S(1)}, u32[]{:S(2)}, u32[]{:S(2)}) collective-permute-start(s16[16,32,128]{2,1,0:T(8,128)(2,1)S(1)} %bitcast.37), channel_id=1, source_target_pairs={{0,4},{2,6},{4,0},{6,2},{1,5},{3,7},{5,1},{7,3},{8,12},{10,14},{12... | collective-permute-start | bytes 393224 | tf_op jit(solution)/shard_map/ppermute | solution.py:585
  173.1 9.7 %collective-permute-start.59 = (s16[16,32,128]{2,1,0:T(8,128)(2,1)S(1)}, s16[16,32,128]{2,1,0:T(8,128)(2,1)S(1)}, u32[]{:S(2)}, u32[]{:S(2)}) collective-permute-start(s16[16,32,128]{2,1,0:T(8,128)(2,1)S(1)} %bitcast.38), channel_id=1, source_target_pairs={{0,6},{2,4},{4,2},{6,0},{1,7},{3,5},{5,3},{7,1},{8,14},{10,12},{12... | collective-permute-start | bytes 393224 | tf_op jit(solution)/shard_map/ppermute | solution.py:585
  176.1 10.6 %collective-permute-start.64 = (s16[64,32,128]{2,1,0:T(8,128)(2,1)S(1)}, s16[64,32,128]{2,1,0:T(8,128)(2,1)S(1)}, u32[]{:S(2)}, u32[]{:S(2)}) collective-permute-start(s16[64,32,128]{2,1,0:T(8,128)(2,1)S(1)} %bitcast.25), channel_id=1, source_target_pairs={{0,1},{1,0},{2,3},{3,2},{4,5},{5,4},{6,7},{7,6},{8,9},{9,8},{10,11... | collective-permute-start | bytes 1572872 | tf_op jit(solution)/shard_map/ppermute | solution.py:524
  183.4 7.2 %collective-permute-start.60 = (s16[64,32,128]{2,1,0:T(8,128)(2,1)S(1)}, s16[64,32,128]{2,1,0:T(8,128)(2,1)S(1)}, u32[]{:S(2)}, u32[]{:S(2)}) collective-permute-start(s16[64,32,128]{2,1,0:T(8,128)(2,1)S(1)} %bitcast.27), channel_id=1, source_target_pairs={{0,1},{1,0},{2,3},{3,2},{4,5},{5,4},{6,7},{7,6},{8,9},{9,8},{10,11... | collective-permute-start | bytes 1572872 | tf_op jit(solution)/shard_map/ppermute | solution.py:524
  (45 other events, 272.0 us)

commit v10 on v7

--- a/solution.py
+++ b/solution.py
@@ -116,8 +116,8 @@
     put_rows(st_ref, *local_stats(planes, float(GROUP * rows * frames * cols)))
 
 
-def rows_kernel(above_ref, below_ref, *outs):
-    for which, out in enumerate(outs):
+def rows_kernel(above_ref, below_ref, *refs):
+    for which, out in enumerate(refs[-above_ref.shape[0] :]):
         out[0] = above_ref[which]
         out[1] = below_ref[which]
 
@@ -273,7 +273,7 @@
 
 
 def hidden_grad_kernel(
-    hidden, scaled, par_ref, st_ref, sums_ref, after, out_ref, down_ref, up_ref, *, count
+    hidden, scaled, par_ref, st_ref, sums_ref, out_ref, down_ref, up_ref, *, count
 ):
     rows, frames, channels, cols = hidden.shape
     mean, inverse, _, _, _ = norm_columns(par_ref, st_ref, count, 3)
@@ -355,13 +355,19 @@
 
 def join_kernel(flag_ref, mine_ref, theirs_ref, out_ref, first_ref, second_ref):
     half, _, channels = mine_ref.shape
-    is_first = flag_ref[3] == 0
-    first_ref[...] = decoded_value(jnp.where(is_first, mine_ref[...], theirs_ref[...])).reshape(first_ref.shape)
-    second_ref[...] = decoded_value(jnp.where(is_first, theirs_ref[...], mine_ref[...])).reshape(second_ref.shape)
-    for tap in range(TAPS):
-        here = slice(tap * channels, (tap + 1) * channels)
-        out_ref[:half, here] = first_ref[pl.ds(tap, half, stride=SLOTS), :]
-        out_ref[half:, here] = second_ref[pl.ds(tap, half, stride=SLOTS), :]
+
+    @pl.when(pl.program_id(0) == 0)
+    def _():
+        is_first = flag_ref[3] == 0
+        mine, theirs = mine_ref[...], theirs_ref[...]
+        first_ref[...] = decoded_value(jnp.where(is_first, mine, theirs)).reshape(first_ref.shape)
+        second_ref[...] = decoded_value(jnp.where(is_first, theirs, mine)).reshape(second_ref.shape)
+
+    for number in range(3):
+        here = pl.ds(3 * pl.program_id(0) + number, half, stride=SLOTS)
+        there = slice(number * channels, (number + 1) * channels)
+        out_ref[:half, there] = first_ref[here, :]
+        out_ref[half:, there] = second_ref[here, :]
 
 
 def weight_second_kernel(flag_ref, stack_ref, act_ref, mine_ref, theirs_ref, right_ref):
@@ -594,13 +600,16 @@
 
 def joined(flags, mine, theirs):
     half, _, channels = mine.shape
-    (total,) = call(
+    total = pl.pallas_call(
         join_kernel,
-        [shape((2 * half, TAPS * channels), F32)],
-        [SMEM] + [VMEM] * 2,
-        (flags, mine, theirs),
-        scratch=[pltpu.VMEM((half * SLOTS, channels), F32)] * 2,
-    )
+        grid=(TAPS // 3,),
+        out_shape=shape((2 * half, TAPS * channels), F32),
+        in_specs=[SMEM, VMEM, VMEM],
+        out_specs=pl.BlockSpec((2 * half, 3 * channels), lambda step: (0, step)),
+        scratch_shapes=[pltpu.VMEM((half * SLOTS, channels), F32)] * 2,
+        compiler_params=pltpu.CompilerParams(vmem_limit_bytes=20 << 20),
+        cost_estimate=pl.CostEstimate(flops=0, bytes_accessed=8 << 20, transcendentals=0),
+    )(flags, mine, theirs)
     return total
 
 
@@ -611,13 +620,14 @@
     return columns
 
 
-def row_halos(down, up):
+def row_halos(down, up, after=()):
     above, below = shifted(down, "height", 1), shifted(up, "height", -1)
-    return call(rows_kernel, [shape((2, *down.shape[1:]), BF16)] * down.shape[0], [VMEM] * 2, (above, below))
-
-
-def halo(own, near, steps):
-    return shifted(own, "tm", steps), near, shifted(near, "tm", steps)
+    return call(
+        rows_kernel,
+        [shape((2, *down.shape[1:]), BF16)] * down.shape[0],
+        [VMEM] * (2 + len(after)),
+        (above, below, *after),
+    )
 
 
 def with_columns(flags, own, around, after=()):
@@ -672,8 +682,8 @@
         (latent, cotangent, par),
     )
     near, near_c = row_halos(down, up)
-    around = with_columns(flags, latent, halo(latent, near, 1))
-    around_c = halo(cotangent, near_c, -1)
+    around = with_columns(flags, latent, (shifted(latent, "tm", 1), near, shifted(near, "tm", 1)))
+    around_c = (shifted(cotangent, "tm", -1), near_c, shifted(near_c, "tm", -1))
     stats_first = all_stats(stats_first, count / devices)
     (weight_first,) = call(weight_forward_kernel, [shape(taps, BF16)], [VMEM], (conv_first,))
     (weight_second_t,) = call(weight_back_kernel, [shape(taps, BF16)], [VMEM], (conv_second,))
@@ -683,7 +693,7 @@
         functools.partial(conv_first_kernel, count=count),
         [shape(block, F32), small, shape(stack, BF16)],
         [SMEM] + [VMEM] * 10,
-        (flags, latent, *around, par, stats_first, weight_first, around_c[0]),
+        (flags, latent, *around, par, stats_first, weight_first, around_c[2]),
         flops=conv_flops,
         transcendentals=3 * latent.size,
     )
@@ -716,11 +726,12 @@
     hidden_grad, down, up = call(
         functools.partial(hidden_grad_kernel, count=count),
         [shape(block, BF16), message, message],
-        [VMEM] * 6,
-        (hidden, scaled, par, stats_second, sums, halves_second[0]),
-    )
-    (near,) = row_halos(down, up)
-    around = halo(hidden_grad, near, -1)
+        [VMEM] * 5,
+        (hidden, scaled, par, stats_second, sums),
+    )
+    future = shifted(hidden_grad, "tm", -1)
+    (near,) = row_halos(down, up, (future,))
+    around = (future, near, shifted(near, "tm", -1))
     halves_first = call(
         weight_first_kernel,
         halves,

time: 192 us -> 195 us (1.016)
  waiting for transfers between devices: 32.8 us -> 39.8 us
  starting transfers between devices: 101 us -> 95.9 us
    pallas_call x0 -> x2, Pallas kernels: none -> 10.4 us  [joined(): pl.pallas_call(join_kernel, grid=(TAPS // 3,), out_shape=shape((2 * half,...]
    pallas_call x28 -> x26, Pallas kernels: 50.7 us -> 41.6 us  [call(): pl.pallas_call(body, out_shape=tuple(outs), in_specs=specs, out_specs=tup...]
    ppermute x10, waiting for transfers between devices: 13.2 us -> 17.7 us  [shifted(): lax.ppermute(value, axis, [(source, source + steps) for source in range(i...]
    ppermute x14, waiting for transfers between devices: 8.24 us -> 10.8 us  [all_sum(): parts = [value] + [lax.ppermute(value, axis, pairs) for pairs in exchanges]]
    ppermute x10, starting transfers between devices: 20.6 us -> 18.1 us  [swapped(): return lax.ppermute(value, 'width', [(0, 1), (1, 0)])]
  transfers between devices with their start and end apart: 63 -> 63, of which waited for: 20 -> 23; matrix products, arithmetic and copies ran while one was open for 0% -> 0% of each run, Pallas kernels for 17% -> 17%
where the time goes in v10:
time: 195 us
  starting transfers between devices  95.9 us (49%)
  Pallas kernels  51.9 us (27%)
  waiting for transfers between devices  39.8 us (20%)
  local copies, waits for them, and re-layouts  4.96 us (3%)
    pallas_call x26, Pallas kernels, call(): pl.pallas_call(body, out_shape=tuple(outs), in_specs=specs, out_specs=tup...  41.6 us
    ppermute x14, starting transfers between devices, all_stats(): lax.ppermute(value, axis, pairs)  23.4 us
    ppermute x10, starting transfers between devices, shifted(): lax.ppermute(value, axis, [(source, source + steps) for source in range(i...  20.3 us
    ppermute x14, starting transfers between devices, all_sum(): parts = [value] + [lax.ppermute(value, axis, pairs) for pairs in exchanges]  19.1 us
    ppermute x10, starting transfers between devices, swapped(): return lax.ppermute(value, 'width', [(0, 1), (1, 0)])  18.1 us
    ppermute x10, waiting for transfers between devices, shifted(): lax.ppermute(value, axis, [(source, source + steps) for source in range(i...  17.7 us
    ppermute x14, waiting for transfers between devices, all_sum(): parts = [value] + [lax.ppermute(value, axis, pairs) for pairs in exchanges]  10.8 us
    pallas_call x2, Pallas kernels, joined(): pl.pallas_call(join_kernel, grid=(TAPS // 3,), out_shape=shape((2 * half,...  10.4 us
  transfers between devices with their start and end apart: 63, of which 23 were waited for; matrix products, arithmetic and copies ran while one was open for 0% of the time, Pallas kernels for 17%

profile of v10, /device:TPU:1, one launch (start us, length us, event | category | flops | bytes accessed | tf_op | source)
XLA Modules:
  0.0 194.6 jit_solution(11094401940011621330)
XLA Ops:
  4.3 2.6 %shard_map.112 = (bf16[4,2,128,256]{3,2,1,0:T(8,128)(2,1)S(1)}, bf16[4,2,128,256]{3,2,1,0:T(8,128)(2,1)S(1)}, bf16[2,2,128,256]{3,2,1,0:T(8,128)(2,1)S(1)}, bf16...) custom-call(bf16[128,2,4,256]{3,2,1,0:T(4,128)(2,1)S(1)} %copy-done.3, bf16[128,2,4,256]{3,2,1,0:T(4,128)(2,1)S(1)} %copy-done.4, ...), custom_call_target="tpu_custom_call" | custom-call | bytes 2626560 | tf_op jit(solution)/shard_map/pallas_call | solution.py:24
  7.0 2.2 %collective-permute-start.6 = (f32[1,2,128]{2,1,0:T(2,128)S(1)}, f32[1,2,128]{2,1,0:T(2,128)S(1)}, u32[]{:S(2)}, u32[]{:S(2)}) collective-permute-start(f32[1,2,128]{2,1,0:T(2,128)S(1)} %get-tuple-element.43), channel_id=1, source_target_pairs={{0,8},{8,0},{16,24},{24,16},{1,9},{9,1},{17,25},{25,17},{2,10},{10... | collective-permute-start | bytes 3080 | tf_op jit(solution)/shard_map/ppermute | solution.py:516
  9.2 2.3 %collective-permute-start.7 = (f32[1,2,128]{2,1,0:T(2,128)S(1)}, f32[1,2,128]{2,1,0:T(2,128)S(1)}, u32[]{:S(2)}, u32[]{:S(2)}) collective-permute-start(f32[1,2,128]{2,1,0:T(2,128)S(1)} %get-tuple-element.43), channel_id=1, source_target_pairs={{0,16},{8,24},{16,0},{24,8},{1,17},{9,25},{17,1},{25,9},{2,18},{10... | collective-permute-start | bytes 3080 | tf_op jit(solution)/shard_map/ppermute | solution.py:516
  11.5 3.1 %collective-permute-start.1 = (bf16[2,2,128,256]{3,2,1,0:T(8,128)(2,1)S(1)}, bf16[2,2,128,256]{3,2,1,0:T(8,128)(2,1)S(1)}, u32[]{:S(2)}, u32[]{:S(2)}) collective-permute-start(bf16[2,2,128,256]{3,2,1,0:T(8,128)(2,1)S(1)} %get-tuple-element.40), channel_id=1, source_target_pairs={{0,2},{2,4},{4,6},{1,3},{3,5},{5,7},{8,10},{10,12},{12,14},{9,11},... | collective-permute-start | bytes 786440 | tf_op jit(solution)/shard_map/ppermute | solution.py:488
  16.0 3.1 %collective-permute-start.10 = (f32[1,2,128]{2,1,0:T(2,128)S(1)}, f32[1,2,128]{2,1,0:T(2,128)S(1)}, u32[]{:S(2)}, u32[]{:S(2)}) collective-permute-start(f32[1,2,128]{2,1,0:T(2,128)S(1)} %pad_maximum_fusion), channel_id=1, source_target_pairs={{0,4},{2,6},{4,0},{6,2},{1,5},{3,7},{5,1},{7,3},{8,12},{10,14},{12... | collective-permute-start | bytes 3080 | tf_op jit(solution)/shard_map/ppermute | solution.py:516
  20.3 3.0 %collective-permute-start = (bf16[4,2,128,256]{3,2,1,0:T(8,128)(2,1)S(1)}, bf16[4,2,128,256]{3,2,1,0:T(8,128)(2,1)}, u32[]{:S(2)}, u32[]{:S(2)}) collective-permute-start(bf16[4,2,128,256]{3,2,1,0:T(8,128)(2,1)S(1)} %get-tuple-element.39.first_ref.own.refs_7_.latent), channel_id=1, source_target_pairs={{0,8},{8,16},{16,24},{1,9},{9,17},{17,25},{2,10},{10,18},{18,26},{... | collective-permute-start | bytes 1572872 | tf_op jit(solution)/shard_map/ppermute | solution.py:488
  23.3 3.0 %collective-permute-done.9 = f32[1,2,128]{2,1,0:T(2,128)S(1)} collective-permute-done((f32[1,2,128]{2,1,0:T(2,128)S(1)}, f32[1,2,128]{2,1,0:T(2,128)S(1)}, u32[]{:S(2)}, u32[]{:S(2)}) %collective-permute-start.9) | collective-permute-done | bytes 1056 | tf_op jit(solution)/shard_map/ppermute | solution.py:516
  27.8 2.9 %collective-permute-start.3 = (bf16[2,2,128,256]{3,2,1,0:T(8,128)(2,1)}, bf16[2,2,128,256]{3,2,1,0:T(8,128)(2,1)}, u32[]{:S(2)}, u32[]{:S(2)}) collective-permute-start(bf16[2,2,128,256]{3,2,1,0:T(8,128)(2,1)} %get-tuple-element.42.first_ref.near), channel_id=1, source_target_pairs={{0,8},{8,16},{16,24},{1,9},{9,17},{17,25},{2,10},{10,18},{18,26},{... | collective-permute-start | bytes 786440 | tf_op jit(solution)/shard_map/ppermute | solution.py:488
  30.7 2.8 %collective-permute-start.12 = (f32[1,2,128]{2,1,0:T(2,128)S(1)}, f32[1,2,128]{2,1,0:T(2,128)S(1)}, u32[]{:S(2)}, u32[]{:S(2)}) collective-permute-start(f32[1,2,128]{2,1,0:T(2,128)S(1)} %pad_maximum_fusion.1), channel_id=1, source_target_pairs={{0,1},{1,0},{2,3},{3,2},{4,5},{5,4},{6,7},{7,6},{8,9},{9,8},{10,11... | collective-permute-start | bytes 3080 | tf_op jit(solution)/shard_map/ppermute | solution.py:516
  38.2 3.6 %collective-permute-start.5 = (bf16[128,128]{1,0:T(8,128)(2,1)S(1)}, bf16[128,128]{1,0:T(8,128)(2,1)S(1)}, u32[]{:S(2)}, u32[]{:S(2)}) collective-permute-start(bf16[128,128]{1,0:T(8,128)(2,1)S(1)} %shard_map.115), channel_id=1, source_target_pairs={{0,1},{1,0},{2,3},{3,2},{4,5},{5,4},{6,7},{7,6},{8,9},{9,8},{10,11... | collective-permute-start | bytes 98312 | tf_op jit(solution)/shard_map/ppermute | solution.py:529
  45.2 5.2 %shard_map.117 = (f32[4,2,128,256]{3,2,1,0:T(8,128)S(1)}, f32[1,2,128]{2,1,0:T(2,128)S(1)}, bf16[6,4,384,256]{3,2,1,0:T(8,128)(2,1)S(1)}) custom-call(s32[6]{0:T(128)S(1)} %stack.57.flag_ref, bf16[4,2,128,256]{3,2,1,0:T(8,128)(2,1)S(1)} %get-tuple-element.39.first_ref.own.refs_7_.latent, bf16[4,2,128,256]{3,2,1,0:T(8,128)(2,1)} %collective-permute-done.second_ref.past, ...), custom_call_target="tpu_custom_call" | custom-call | flops 7247757312 | bytes 10033176 | tf_op jit(solution)/shard_map/pallas_call | solution.py:24
  50.4 2.3 %collective-permute-start.17 = (f32[1,2,128]{2,1,0:T(2,128)S(1)}, f32[1,2,128]{2,1,0:T(2,128)S(1)}, u32[]{:S(2)}, u32[]{:S(2)}) collective-permute-start(f32[1,2,128]{2,1,0:T(2,128)S(1)} %get-tuple-element.47.refs_0_), channel_id=1, source_target_pairs={{0,8},{8,0},{16,24},{24,16},{1,9},{9,1},{17,25},{25,17},{2,10},{10... | collective-permute-start | bytes 3080 | tf_op jit(solution)/shard_map/ppermute | solution.py:516
  52.6 3.2 %collective-permute-start.18 = (f32[1,2,128]{2,1,0:T(2,128)S(1)}, f32[1,2,128]{2,1,0:T(2,128)S(1)}, u32[]{:S(2)}, u32[]{:S(2)}) collective-permute-start(f32[1,2,128]{2,1,0:T(2,128)S(1)} %get-tuple-element.47.refs_0_), channel_id=1, source_target_pairs={{0,16},{8,24},{16,0},{24,8},{1,17},{9,25},{17,1},{25,9},{2,18},{10... | collective-permute-start | bytes 3080 | tf_op jit(solution)/shard_map/ppermute | solution.py:516
  57.3 2.7 %collective-permute-done.19 = f32[1,2,128]{2,1,0:T(2,128)S(1)} collective-permute-done((f32[1,2,128]{2,1,0:T(2,128)S(1)}, f32[1,2,128]{2,1,0:T(2,128)S(1)}, u32[]{:S(2)}, u32[]{:S(2)}) %collective-permute-start.19) | collective-permute-done | bytes 1056 | tf_op jit(solution)/shard_map/ppermute | solution.py:516
  65.3 3.7 %collective-permute-start.23 = (f32[1,2,128]{2,1,0:T(2,128)S(1)}, f32[1,2,128]{2,1,0:T(2,128)S(1)}, u32[]{:S(2)}, u32[]{:S(2)}) collective-permute-start(f32[1,2,128]{2,1,0:T(2,128)S(1)} %pad_maximum_fusion.4), channel_id=1, source_target_pairs={{0,1},{1,0},{2,3},{3,2},{4,5},{5,4},{6,7},{7,6},{8,9},{9,8},{10,11... | collective-permute-start | bytes 3080 | tf_op jit(solution)/shard_map/ppermute | solution.py:516
  74.5 3.4 %shard_map.121 = (f32[4,2,128,256]{3,2,1,0:T(8,128)S(1)}, bf16[6,4,384,256]{3,2,1,0:T(8,128)(2,1)S(1)}) custom-call(s32[6]{0:T(128)S(1)} %stack.57.flag_ref, bf16[4,2,128,256]{3,2,1,0:T(8,128)(2,1)S(1)} %get-tuple-element.46.first_ref.refs_0_.cotangent, bf16[4,2,128,256]{3,2,1,0:T(8,128)(2,1)S(1)} %collective-permute-done.14.second_ref.refs_1_, ...), custom_call_target="tpu_custom_call" | custom-call | flops 7247757312 | bytes 9764888 | tf_op jit(solution)/shard_map/pallas_call | solution.py:24
  89.8 3.5 %collective-permute-start.30 = (f32[1,2,128]{2,1,0:T(2,128)S(1)}, f32[1,2,128]{2,1,0:T(2,128)S(1)}, u32[]{:S(2)}, u32[]{:S(2)}) collective-permute-start(f32[1,2,128]{2,1,0:T(2,128)S(1)} %add_add_fusion.2), channel_id=1, source_target_pairs={{0,1},{1,0},{2,3},{3,2},{4,5},{5,4},{6,7},{7,6},{8,9},{9,8},{10,11... | collective-permute-start | bytes 3080 | tf_op jit(solution)/shard_map/ppermute | solution.py:509
  93.3 4.6 %shard_map.125 = (f32[2048,128]{1,0:T(8,128)S(1)}, f32[2048,128]{1,0:T(8,128)S(1)}) custom-call(s32[6]{0:T(128)S(1)} %stack.57.flag_ref, bf16[6,4,384,256]{3,2,1,0:T(8,128)(2,1)S(1)} %get-tuple-element.54.stack_ref, bf16[4,2,128,256]{3,2,1,0:T(8,128)(2,1)S(1)} %get-tuple-element.55.act_ref), custom_call_target="tpu_custom_call" | custom-call | flops 7247757312 | bytes 7340056 | tf_op jit(solution)/shard_map/pallas_call | solution.py:24
  98.5 4.6 %shard_map.126 = (f32[2048,128]{1,0:T(8,128)S(1)}, f32[2048,128]{1,0:T(8,128)S(1)}) custom-call(s32[6]{0:T(128)S(1)} %stack.57.flag_ref, bf16[6,4,384,256]{3,2,1,0:T(8,128)(2,1)S(1)} %get-tuple-element.58.stack_ref, bf16[4,2,128,256]{3,2,1,0:T(8,128)(2,1)S(1)} %get-tuple-element.51.grad_ref.first_ref.refs_0_), custom_call_target="tpu_custom_call" | custom-call | flops 7247757312 | bytes 7340056 | tf_op jit(solution)/shard_map/pallas_call | solution.py:24
  105.0 3.1 %collective-permute-start.32 = (bf16[1,2,128,256]{3,2,1,0:T(8,128)(2,1)S(1)}, bf16[1,2,128,256]{3,2,1,0:T(8,128)(2,1)S(1)}, u32[]{:S(2)}, u32[]{:S(2)}) collective-permute-start(bf16[1,2,128,256]{3,2,1,0:T(8,128)(2,1)S(1)} %get-tuple-element.52), channel_id=1, source_target_pairs={{0,2},{2,4},{4,6},{1,3},{3,5},{5,7},{8,10},{10,12},{12,14},{9,11},... | collective-permute-start | bytes 393224 | tf_op jit(solution)/shard_map/ppermute | solution.py:488
  110.9 3.8 %collective-permute-done.33.below_ref = bf16[1,2,128,256]{3,2,1,0:T(8,128)(2,1)S(1)} collective-permute-done((bf16[1,2,128,256]{3,2,1,0:T(8,128)(2,1)S(1)}, bf16[1,2,128,256]{3,2,1,0:T(8,128)(2,1)S(1)}, u32[]{:S(2)}, u32[]{:S(2)}) %collective-permute-start.33) | collective-permute-done | bytes 131104 | tf_op jit(solution)/shard_map/ppermute | solution.py:488
  114.7 4.3 %collective-permute-done.31.refs_0_.second_ref.refs_1_.refs_4_ = bf16[4,2,128,256]{3,2,1,0:T(8,128)(2,1)S(1)} collective-permute-done((bf16[4,2,128,256]{3,2,1,0:T(8,128)(2,1)S(1)}, bf16[4,2,128,256]{3,2,1,0:T(8,128)(2,1)S(1)}, u32[]{:S(2)}, u32[]{:S(2)}) %collective-permute-start.31) | collective-permute-done | bytes 524320 | tf_op jit(solution)/shard_map/ppermute | solution.py:488
  121.8 6.3 %collective-permute-done.34.second_ref.refs_3_ = bf16[2,2,128,256]{3,2,1,0:T(8,128)(2,1)S(1)} collective-permute-done((bf16[2,2,128,256]{3,2,1,0:T(8,128)(2,1)S(1)}, bf16[2,2,128,256]{3,2,1,0:T(8,128)(2,1)S(1)}, u32[]{:S(2)}, u32[]{:S(2)}) %collective-permute-start.34) | collective-permute-done | bytes 262176 | tf_op jit(solution)/shard_map/ppermute | solution.py:488
  135.4 4.0 %shard_map.131 = (f32[4,2,128,256]{3,2,1,0:T(8,128)S(1)}, f32[1,2,128]{2,1,0:T(2,128)S(1)}) custom-call(s32[6]{0:T(128)S(1)} %stack.57.flag_ref, bf16[4,2,128,256]{3,2,1,0:T(8,128)(2,1)S(1)} %get-tuple-element.51.grad_ref.first_ref.refs_0_, bf16[4,2,128,256]{3,2,1,0:T(8,128)(2,1)S(1)} %collective-permute-done.31.refs_0_.second_ref.refs_1_.refs_4_, ...), custom_call_target="tpu_custom_call" | custom-call | flops 7247757312 | bytes 5576728 | tf_op jit(solution)/shard_map/pallas_call | solution.py:24
  143.1 3.2 %collective-permute-done.41 = f32[1,2,128]{2,1,0:T(2,128)S(1)} collective-permute-done((f32[1,2,128]{2,1,0:T(2,128)S(1)}, f32[1,2,128]{2,1,0:T(2,128)S(1)}, u32[]{:S(2)}, u32[]{:S(2)}) %collective-permute-start.41) | collective-permute-done | bytes 1056 | tf_op jit(solution)/shard_map/ppermute | solution.py:509
  151.2 2.4 %collective-permute-start.51 = (s16[2,4,32,128]{3,2,1,0:T(8,128)(2,1)S(1)}, s16[2,4,32,128]{3,2,1,0:T(8,128)(2,1)S(1)}, u32[]{:S(2)}, u32[]{:S(2)}) collective-permute-start(s16[2,4,32,128]{3,2,1,0:T(8,128)(2,1)S(1)} %get-tuple-element.71), channel_id=1, source_target_pairs={{0,24},{8,16},{16,8},{24,0},{1,25},{9,17},{17,9},{25,1},{2,26},{10... | collective-permute-start | bytes 196616 | tf_op jit(solution)/shard_map/ppermute | solution.py:565
  153.6 5.1 %collective-permute-start.45 = (f32[1,2,128]{2,1,0:T(2,128)S(1)}, f32[1,2,128]{2,1,0:T(2,128)S(1)}, u32[]{:S(2)}, u32[]{:S(2)}) collective-permute-start(f32[1,2,128]{2,1,0:T(2,128)S(1)} %add_add_fusion), channel_id=1, source_target_pairs={{0,1},{1,0},{2,3},{3,2},{4,5},{5,4},{6,7},{7,6},{8,9},{9,8},{10,11... | collective-permute-start | bytes 3080 | tf_op jit(solution)/shard_map/ppermute | solution.py:509
  160.5 2.7 %collective-permute-start.54 = (s16[2,4,32,128]{3,2,1,0:T(8,128)(2,1)S(1)}, s16[2,4,32,128]{3,2,1,0:T(8,128)(2,1)S(1)}, u32[]{:S(2)}, u32[]{:S(2)}) collective-permute-start(s16[2,4,32,128]{3,2,1,0:T(8,128)(2,1)S(1)} %shard_map.134.refs_0_), channel_id=1, source_target_pairs={{0,24},{8,16},{16,8},{24,0},{1,25},{9,17},{17,9},{25,1},{2,26},{10... | collective-permute-start | bytes 196616 | tf_op jit(solution)/shard_map/ppermute | solution.py:579
  173.4 7.3 %collective-permute-start.62 = (s16[64,32,128]{2,1,0:T(8,128)(2,1)S(1)}, s16[64,32,128]{2,1,0:T(8,128)(2,1)S(1)}, u32[]{:S(2)}, u32[]{:S(2)}) collective-permute-start(s16[64,32,128]{2,1,0:T(8,128)(2,1)S(1)} %bitcast.24), channel_id=1, source_target_pairs={{0,1},{1,0},{2,3},{3,2},{4,5},{5,4},{6,7},{7,6},{8,9},{9,8},{10,11... | collective-permute-start | bytes 1572872 | tf_op jit(solution)/shard_map/ppermute | solution.py:529
  181.3 2.9 %collective-permute-start.58 = (s16[64,32,128]{2,1,0:T(8,128)(2,1)S(1)}, s16[64,32,128]{2,1,0:T(8,128)(2,1)S(1)}, u32[]{:S(2)}, u32[]{:S(2)}) collective-permute-start(s16[64,32,128]{2,1,0:T(8,128)(2,1)S(1)} %bitcast.26), channel_id=1, source_target_pairs={{0,1},{1,0},{2,3},{3,2},{4,5},{5,4},{6,7},{7,6},{8,9},{9,8},{10,11... | collective-permute-start | bytes 1572872 | tf_op jit(solution)/shard_map/ppermute | solution.py:529
  184.2 5.2 %shard_map.139 = f32[128,3456]{1,0:T(8,128)} custom-call(s32[6]{0:T(128)S(1)} %stack.57.flag_ref, s16[64,32,128]{2,1,0:T(8,128)(2,1)S(1)} %bitcast.25, s16[64,32,128]{2,1,0:T(8,128)(2,1)S(1)} %collective-permute-done.62.theirs_ref), custom_call_target="tpu_custom_call" | custom-call | bytes 8388608 | tf_op jit(solution)/shard_map/pallas_call | solution.py:603
  189.4 5.2 %shard_map.137 = f32[128,3456]{1,0:T(8,128)} custom-call(s32[6]{0:T(128)S(1)} %stack.57.flag_ref, s16[64,32,128]{2,1,0:T(8,128)(2,1)S(1)} %bitcast.27, s16[64,32,128]{2,1,0:T(8,128)(2,1)S(1)} %collective-permute-done.58.theirs_ref), custom_call_target="tpu_custom_call" | custom-call | bytes 8388608 | tf_op jit(solution)/shard_map/pallas_call | solution.py:603
  (161 shorter events, 76.1 us)
Async XLA Ops:
  7.0 8.9 %collective-permute-start.6 = (f32[1,2,128]{2,1,0:T(2,128)S(1)}, f32[1,2,128]{2,1,0:T(2,128)S(1)}, u32[]{:S(2)}, u32[]{:S(2)}) collective-permute-start(f32[1,2,128]{2,1,0:T(2,128)S(1)} %get-tuple-element.43), channel_id=1, source_target_pairs={{0,8},{8,0},{16,24},{24,16},{1,9},{9,1},{17,25},{25,17},{2,10},{10... | collective-permute-start | bytes 3080 | tf_op jit(solution)/shard_map/ppermute | solution.py:516
  9.2 6.8 %collective-permute-start.7 = (f32[1,2,128]{2,1,0:T(2,128)S(1)}, f32[1,2,128]{2,1,0:T(2,128)S(1)}, u32[]{:S(2)}, u32[]{:S(2)}) collective-permute-start(f32[1,2,128]{2,1,0:T(2,128)S(1)} %get-tuple-element.43), channel_id=1, source_target_pairs={{0,16},{8,24},{16,0},{24,8},{1,17},{9,25},{17,1},{25,9},{2,18},{10... | collective-permute-start | bytes 3080 | tf_op jit(solution)/shard_map/ppermute | solution.py:516
  11.5 14.9 %collective-permute-start.1 = (bf16[2,2,128,256]{3,2,1,0:T(8,128)(2,1)S(1)}, bf16[2,2,128,256]{3,2,1,0:T(8,128)(2,1)S(1)}, u32[]{:S(2)}, u32[]{:S(2)}) collective-permute-start(bf16[2,2,128,256]{3,2,1,0:T(8,128)(2,1)S(1)} %get-tuple-element.40), channel_id=1, source_target_pairs={{0,2},{2,4},{4,6},{1,3},{3,5},{5,7},{8,10},{10,12},{12,14},{9,11},... | collective-permute-start | bytes 786440 | tf_op jit(solution)/shard_map/ppermute | solution.py:488
  14.6 11.7 %collective-permute-start.2 = (bf16[2,2,128,256]{3,2,1,0:T(8,128)(2,1)S(1)}, bf16[2,2,128,256]{3,2,1,0:T(8,128)(2,1)S(1)}, u32[]{:S(2)}, u32[]{:S(2)}) collective-permute-start(bf16[2,2,128,256]{3,2,1,0:T(8,128)(2,1)S(1)} %get-tuple-element.41), channel_id=1, source_target_pairs={{2,0},{4,2},{6,4},{3,1},{5,3},{7,5},{10,8},{12,10},{14,12},{11,9},... | collective-permute-start | bytes 786440 | tf_op jit(solution)/shard_map/ppermute | solution.py:488
  19.3 7.0 %collective-permute-start.9 = (f32[1,2,128]{2,1,0:T(2,128)S(1)}, f32[1,2,128]{2,1,0:T(2,128)S(1)}, u32[]{:S(2)}, u32[]{:S(2)}) collective-permute-start(f32[1,2,128]{2,1,0:T(2,128)S(1)} %pad_maximum_fusion), channel_id=1, source_target_pairs={{0,2},{2,0},{4,6},{6,4},{1,3},{3,1},{5,7},{7,5},{8,10},{10,8},{12,... | collective-permute-start | bytes 3080 | tf_op jit(solution)/shard_map/ppermute | solution.py:516
  20.3 21.5 %collective-permute-start = (bf16[4,2,128,256]{3,2,1,0:T(8,128)(2,1)S(1)}, bf16[4,2,128,256]{3,2,1,0:T(8,128)(2,1)}, u32[]{:S(2)}, u32[]{:S(2)}) collective-permute-start(bf16[4,2,128,256]{3,2,1,0:T(8,128)(2,1)S(1)} %get-tuple-element.39.first_ref.own.refs_7_.latent), channel_id=1, source_target_pairs={{0,8},{8,16},{16,24},{1,9},{9,17},{17,25},{2,10},{10,18},{18,26},{... | collective-permute-start | bytes 1572872 | tf_op jit(solution)/shard_map/ppermute | solution.py:488
  27.8 9.0 %collective-permute-start.3 = (bf16[2,2,128,256]{3,2,1,0:T(8,128)(2,1)}, bf16[2,2,128,256]{3,2,1,0:T(8,128)(2,1)}, u32[]{:S(2)}, u32[]{:S(2)}) collective-permute-start(bf16[2,2,128,256]{3,2,1,0:T(8,128)(2,1)} %get-tuple-element.42.first_ref.near), channel_id=1, source_target_pairs={{0,8},{8,16},{16,24},{1,9},{9,17},{17,25},{2,10},{10,18},{18,26},{... | collective-permute-start | bytes 786440 | tf_op jit(solution)/shard_map/ppermute | solution.py:488
  34.9 10.0 %collective-permute-start.13 = (bf16[2,2,128,256]{3,2,1,0:T(8,128)(2,1)}, bf16[2,2,128,256]{3,2,1,0:T(8,128)(2,1)S(1)}, u32[]{:S(2)}, u32[]{:S(2)}) collective-permute-start(bf16[2,2,128,256]{3,2,1,0:T(8,128)(2,1)} %copy-done.5), channel_id=1, source_target_pairs={{8,0},{16,8},{24,16},{9,1},{17,9},{25,17},{10,2},{18,10},{26,18},{... | collective-permute-start | bytes 786440 | tf_op jit(solution)/shard_map/ppermute | solution.py:488
  38.2 6.7 %collective-permute-start.5 = (bf16[128,128]{1,0:T(8,128)(2,1)S(1)}, bf16[128,128]{1,0:T(8,128)(2,1)S(1)}, u32[]{:S(2)}, u32[]{:S(2)}) collective-permute-start(bf16[128,128]{1,0:T(8,128)(2,1)S(1)} %shard_map.115), channel_id=1, source_target_pairs={{0,1},{1,0},{2,3},{3,2},{4,5},{5,4},{6,7},{7,6},{8,9},{9,8},{10,11... | collective-permute-start | bytes 98312 | tf_op jit(solution)/shard_map/ppermute | solution.py:529
  50.4 6.9 %collective-permute-start.17 = (f32[1,2,128]{2,1,0:T(2,128)S(1)}, f32[1,2,128]{2,1,0:T(2,128)S(1)}, u32[]{:S(2)}, u32[]{:S(2)}) collective-permute-start(f32[1,2,128]{2,1,0:T(2,128)S(1)} %get-tuple-element.47.refs_0_), channel_id=1, source_target_pairs={{0,8},{8,0},{16,24},{24,16},{1,9},{9,1},{17,25},{25,17},{2,10},{10... | collective-permute-start | bytes 3080 | tf_op jit(solution)/shard_map/ppermute | solution.py:516
  55.9 14.6 %collective-permute-start.14 = (bf16[4,2,128,256]{3,2,1,0:T(8,128)(2,1)S(1)}, bf16[4,2,128,256]{3,2,1,0:T(8,128)(2,1)S(1)}, u32[]{:S(2)}, u32[]{:S(2)}) collective-permute-start(bf16[4,2,128,256]{3,2,1,0:T(8,128)(2,1)S(1)} %get-tuple-element.46.first_ref.refs_0_.cotangent), channel_id=1, source_target_pairs={{8,0},{16,8},{24,16},{9,1},{17,9},{25,17},{10,2},{18,10},{26,18},{... | collective-permute-start | bytes 1572872 | tf_op jit(solution)/shard_map/ppermute | solution.py:488
  65.3 8.4 %collective-permute-start.23 = (f32[1,2,128]{2,1,0:T(2,128)S(1)}, f32[1,2,128]{2,1,0:T(2,128)S(1)}, u32[]{:S(2)}, u32[]{:S(2)}) collective-permute-start(f32[1,2,128]{2,1,0:T(2,128)S(1)} %pad_maximum_fusion.4), channel_id=1, source_target_pairs={{0,1},{1,0},{2,3},{3,2},{4,5},{5,4},{6,7},{7,6},{8,9},{9,8},{10,11... | collective-permute-start | bytes 3080 | tf_op jit(solution)/shard_map/ppermute | solution.py:516
  89.8 8.2 %collective-permute-start.30 = (f32[1,2,128]{2,1,0:T(2,128)S(1)}, f32[1,2,128]{2,1,0:T(2,128)S(1)}, u32[]{:S(2)}, u32[]{:S(2)}) collective-permute-start(f32[1,2,128]{2,1,0:T(2,128)S(1)} %add_add_fusion.2), channel_id=1, source_target_pairs={{0,1},{1,0},{2,3},{3,2},{4,5},{5,4},{6,7},{7,6},{8,9},{9,8},{10,11... | collective-permute-start | bytes 3080 | tf_op jit(solution)/shard_map/ppermute | solution.py:509
  97.9 22.8 %collective-permute-start.35 = (f32[64,32,128]{2,1,0:T(8,128)S(1)}, f32[64,32,128]{2,1,0:T(8,128)S(1)}, u32[]{:S(2)}, u32[]{:S(2)}) collective-permute-start(f32[64,32,128]{2,1,0:T(8,128)S(1)} %bitcast.44), channel_id=1, source_target_pairs={{0,1},{1,0},{2,3},{3,2},{4,5},{5,4},{6,7},{7,6},{8,9},{9,8},{10,11... | collective-permute-start | bytes 3145736 | tf_op jit(solution)/shard_map/ppermute | solution.py:529
  103.1 17.5 %collective-permute-start.36 = (f32[64,32,128]{2,1,0:T(8,128)S(1)}, f32[64,32,128]{2,1,0:T(8,128)S(1)}, u32[]{:S(2)}, u32[]{:S(2)}) collective-permute-start(f32[64,32,128]{2,1,0:T(8,128)S(1)} %bitcast.45), channel_id=1, source_target_pairs={{0,1},{1,0},{2,3},{3,2},{4,5},{5,4},{6,7},{7,6},{8,9},{9,8},{10,11... | collective-permute-start | bytes 3145736 | tf_op jit(solution)/shard_map/ppermute | solution.py:529
  103.7 15.4 %collective-permute-start.31 = (bf16[4,2,128,256]{3,2,1,0:T(8,128)(2,1)S(1)}, bf16[4,2,128,256]{3,2,1,0:T(8,128)(2,1)S(1)}, u32[]{:S(2)}, u32[]{:S(2)}) collective-permute-start(bf16[4,2,128,256]{3,2,1,0:T(8,128)(2,1)S(1)} %get-tuple-element.51.grad_ref.first_ref.refs_0_), channel_id=1, source_target_pairs={{8,0},{16,8},{24,16},{9,1},{17,9},{25,17},{10,2},{18,10},{26,18},{... | collective-permute-start | bytes 1572872 | tf_op jit(solution)/shard_map/ppermute | solution.py:488
  108.1 6.7 %collective-permute-start.33 = (bf16[1,2,128,256]{3,2,1,0:T(8,128)(2,1)S(1)}, bf16[1,2,128,256]{3,2,1,0:T(8,128)(2,1)S(1)}, u32[]{:S(2)}, u32[]{:S(2)}) collective-permute-start(bf16[1,2,128,256]{3,2,1,0:T(8,128)(2,1)S(1)} %get-tuple-element.53), channel_id=1, source_target_pairs={{2,0},{4,2},{6,4},{3,1},{5,3},{7,5},{10,8},{12,10},{14,12},{11,9},... | collective-permute-start | bytes 393224 | tf_op jit(solution)/shard_map/ppermute | solution.py:488
  119.1 8.9 %collective-permute-start.34 = (bf16[2,2,128,256]{3,2,1,0:T(8,128)(2,1)S(1)}, bf16[2,2,128,256]{3,2,1,0:T(8,128)(2,1)S(1)}, u32[]{:S(2)}, u32[]{:S(2)}) collective-permute-start(bf16[2,2,128,256]{3,2,1,0:T(8,128)(2,1)S(1)} %shard_map.124.first_ref.refs_2_.refs_5_), channel_id=1, source_target_pairs={{8,0},{16,8},{24,16},{9,1},{17,9},{25,17},{10,2},{18,10},{26,18},{... | collective-permute-start | bytes 786440 | tf_op jit(solution)/shard_map/ppermute | solution.py:488
  128.9 6.5 %collective-permute-start.38 = (bf16[128,128]{1,0:T(8,128)(2,1)S(1)}, bf16[128,128]{1,0:T(8,128)(2,1)S(1)}, u32[]{:S(2)}, u32[]{:S(2)}) collective-permute-start(bf16[128,128]{1,0:T(8,128)(2,1)S(1)} %shard_map.129), channel_id=1, source_target_pairs={{0,1},{1,0},{2,3},{3,2},{4,5},{5,4},{6,7},{7,6},{8,9},{9,8},{10,11... | collective-permute-start | bytes 98312 | tf_op jit(solution)/shard_map/ppermute | solution.py:529
  132.6 14.9 %collective-permute-start.46 = (s16[2,16,32,128]{3,2,1,0:T(8,128)(2,1)S(1)}, s16[2,16,32,128]{3,2,1,0:T(8,128)(2,1)S(1)}, u32[]{:S(2)}, u32[]{:S(2)}) collective-permute-start(s16[2,16,32,128]{3,2,1,0:T(8,128)(2,1)S(1)} %get-tuple-element.61.refs_0_), channel_id=1, source_target_pairs={{0,2},{2,0},{4,6},{6,4},{1,3},{3,1},{5,7},{7,5},{8,10},{10,8},{12,... | collective-permute-start | bytes 786440 | tf_op jit(solution)/shard_map/ppermute | solution.py:549
  133.9 15.1 %collective-permute-start.47 = (s16[2,16,32,128]{3,2,1,0:T(8,128)(2,1)S(1)}, s16[2,16,32,128]{3,2,1,0:T(8,128)(2,1)S(1)}, u32[]{:S(2)}, u32[]{:S(2)}) collective-permute-start(s16[2,16,32,128]{3,2,1,0:T(8,128)(2,1)S(1)} %get-tuple-element.66), channel_id=1, source_target_pairs={{0,4},{2,6},{4,0},{6,2},{1,5},{3,7},{5,1},{7,3},{8,12},{10,14},{12... | collective-permute-start | bytes 786440 | tf_op jit(solution)/shard_map/ppermute | solution.py:549
  133.9 15.1 %collective-permute-start.48 = (s16[2,16,32,128]{3,2,1,0:T(8,128)(2,1)S(1)}, s16[2,16,32,128]{3,2,1,0:T(8,128)(2,1)S(1)}, u32[]{:S(2)}, u32[]{:S(2)}) collective-permute-start(s16[2,16,32,128]{3,2,1,0:T(8,128)(2,1)S(1)} %get-tuple-element.67), channel_id=1, source_target_pairs={{0,6},{2,4},{4,2},{6,0},{1,7},{3,5},{5,3},{7,1},{8,14},{10,12},{12... | collective-permute-start | bytes 786440 | tf_op jit(solution)/shard_map/ppermute | solution.py:549
  147.5 6.1 %collective-permute-start.43 = (f32[1,2,128]{2,1,0:T(2,128)S(1)}, f32[1,2,128]{2,1,0:T(2,128)S(1)}, u32[]{:S(2)}, u32[]{:S(2)}) collective-permute-start(f32[1,2,128]{2,1,0:T(2,128)S(1)} %add_add_fusion.1), channel_id=1, source_target_pairs={{0,4},{2,6},{4,0},{6,2},{1,5},{3,7},{5,1},{7,3},{8,12},{10,14},{12... | collective-permute-start | bytes 3080 | tf_op jit(solution)/shard_map/ppermute | solution.py:509
  147.5 6.1 %collective-permute-start.44 = (f32[1,2,128]{2,1,0:T(2,128)S(1)}, f32[1,2,128]{2,1,0:T(2,128)S(1)}, u32[]{:S(2)}, u32[]{:S(2)}) collective-permute-start(f32[1,2,128]{2,1,0:T(2,128)S(1)} %add_add_fusion.1), channel_id=1, source_target_pairs={{0,6},{2,4},{4,2},{6,0},{1,7},{3,5},{5,3},{7,1},{8,14},{10,12},{12... | collective-permute-start | bytes 3080 | tf_op jit(solution)/shard_map/ppermute | solution.py:509
  150.0 9.5 %collective-permute-start.49 = (s16[2,4,32,128]{3,2,1,0:T(8,128)(2,1)S(1)}, s16[2,4,32,128]{3,2,1,0:T(8,128)(2,1)S(1)}, u32[]{:S(2)}, u32[]{:S(2)}) collective-permute-start(s16[2,4,32,128]{3,2,1,0:T(8,128)(2,1)S(1)} %get-tuple-element.69), channel_id=1, source_target_pairs={{0,8},{8,0},{16,24},{24,16},{1,9},{9,1},{17,25},{25,17},{2,10},{10... | collective-permute-start | bytes 196616 | tf_op jit(solution)/shard_map/ppermute | solution.py:565
  150.0 9.5 %collective-permute-start.50 = (s16[2,4,32,128]{3,2,1,0:T(8,128)(2,1)S(1)}, s16[2,4,32,128]{3,2,1,0:T(8,128)(2,1)S(1)}, u32[]{:S(2)}, u32[]{:S(2)}) collective-permute-start(s16[2,4,32,128]{3,2,1,0:T(8,128)(2,1)S(1)} %get-tuple-element.70), channel_id=1, source_target_pairs={{0,16},{8,24},{16,0},{24,8},{1,17},{9,25},{17,1},{25,9},{2,18},{10... | collective-permute-start | bytes 196616 | tf_op jit(solution)/shard_map/ppermute | solution.py:565
  151.2 8.4 %collective-permute-start.51 = (s16[2,4,32,128]{3,2,1,0:T(8,128)(2,1)S(1)}, s16[2,4,32,128]{3,2,1,0:T(8,128)(2,1)S(1)}, u32[]{:S(2)}, u32[]{:S(2)}) collective-permute-start(s16[2,4,32,128]{3,2,1,0:T(8,128)(2,1)S(1)} %get-tuple-element.71), channel_id=1, source_target_pairs={{0,24},{8,16},{16,8},{24,0},{1,25},{9,17},{17,9},{25,1},{2,26},{10... | collective-permute-start | bytes 196616 | tf_op jit(solution)/shard_map/ppermute | solution.py:565
  169.1 11.6 %collective-permute-start.55 = (s16[16,32,128]{2,1,0:T(8,128)(2,1)S(1)}, s16[16,32,128]{2,1,0:T(8,128)(2,1)S(1)}, u32[]{:S(2)}, u32[]{:S(2)}) collective-permute-start(s16[16,32,128]{2,1,0:T(8,128)(2,1)S(1)} %bitcast.36), channel_id=1, source_target_pairs={{0,2},{2,0},{4,6},{6,4},{1,3},{3,1},{5,7},{7,5},{8,10},{10,8},{12,... | collective-permute-start | bytes 393224 | tf_op jit(solution)/shard_map/ppermute | solution.py:590
  170.3 10.4 %collective-permute-start.56 = (s16[16,32,128]{2,1,0:T(8,128)(2,1)S(1)}, s16[16,32,128]{2,1,0:T(8,128)(2,1)S(1)}, u32[]{:S(2)}, u32[]{:S(2)}) collective-permute-start(s16[16,32,128]{2,1,0:T(8,128)(2,1)S(1)} %bitcast.37), channel_id=1, source_target_pairs={{0,4},{2,6},{4,0},{6,2},{1,5},{3,7},{5,1},{7,3},{8,12},{10,14},{12... | collective-permute-start | bytes 393224 | tf_op jit(solution)/shard_map/ppermute | solution.py:590
  170.6 10.2 %collective-permute-start.57 = (s16[16,32,128]{2,1,0:T(8,128)(2,1)S(1)}, s16[16,32,128]{2,1,0:T(8,128)(2,1)S(1)}, u32[]{:S(2)}, u32[]{:S(2)}) collective-permute-start(s16[16,32,128]{2,1,0:T(8,128)(2,1)S(1)} %bitcast.38), channel_id=1, source_target_pairs={{0,6},{2,4},{4,2},{6,0},{1,7},{3,5},{5,3},{7,1},{8,14},{10,12},{12... | collective-permute-start | bytes 393224 | tf_op jit(solution)/shard_map/ppermute | solution.py:590
  173.4 10.8 %collective-permute-start.62 = (s16[64,32,128]{2,1,0:T(8,128)(2,1)S(1)}, s16[64,32,128]{2,1,0:T(8,128)(2,1)S(1)}, u32[]{:S(2)}, u32[]{:S(2)}) collective-permute-start(s16[64,32,128]{2,1,0:T(8,128)(2,1)S(1)} %bitcast.24), channel_id=1, source_target_pairs={{0,1},{1,0},{2,3},{3,2},{4,5},{5,4},{6,7},{7,6},{8,9},{9,8},{10,11... | collective-permute-start | bytes 1572872 | tf_op jit(solution)/shard_map/ppermute | solution.py:529
  181.3 8.1 %collective-permute-start.58 = (s16[64,32,128]{2,1,0:T(8,128)(2,1)S(1)}, s16[64,32,128]{2,1,0:T(8,128)(2,1)S(1)}, u32[]{:S(2)}, u32[]{:S(2)}) collective-permute-start(s16[64,32,128]{2,1,0:T(8,128)(2,1)S(1)} %bitcast.26), channel_id=1, source_target_pairs={{0,1},{1,0},{2,3},{3,2},{4,5},{5,4},{6,7},{7,6},{8,9},{9,8},{10,11... | collective-permute-start | bytes 1572872 | tf_op jit(solution)/shard_map/ppermute | solution.py:529
  (38 other events, 183.9 us)

commit v11 on v7

--- a/solution.py
+++ b/solution.py
@@ -116,8 +116,8 @@
     put_rows(st_ref, *local_stats(planes, float(GROUP * rows * frames * cols)))
 
 
-def rows_kernel(above_ref, below_ref, *outs):
-    for which, out in enumerate(outs):
+def rows_kernel(above_ref, below_ref, *refs):
+    for which, out in enumerate(refs[-above_ref.shape[0] :]):
         out[0] = above_ref[which]
         out[1] = below_ref[which]
 
@@ -273,7 +273,7 @@
 
 
 def hidden_grad_kernel(
-    hidden, scaled, par_ref, st_ref, sums_ref, after, out_ref, down_ref, up_ref, *, count
+    hidden, scaled, par_ref, st_ref, sums_ref, out_ref, down_ref, up_ref, *, count
 ):
     rows, frames, channels, cols = hidden.shape
     mean, inverse, _, _, _ = norm_columns(par_ref, st_ref, count, 3)
@@ -340,17 +340,14 @@
         refs[-1][which] = encoded(total)
 
 
-def split_kernel(flag_ref, *refs, received, slot):
+def gather_kernel(flag_ref, *refs, received, split, slot):
     me = flag_ref[slot]
     for which in range(2):
         for k, ref in enumerate(refs[:received]):
-            refs[which - 2][me ^ k] = ref[which]
-
-
-def gather_kernel(flag_ref, *refs, slot):
-    me = flag_ref[slot]
-    for k, ref in enumerate(refs[:-1]):
-        refs[-1][me ^ k] = ref[...]
+            if split:
+                refs[which - 2][me ^ k] = ref[which]
+            else:
+                refs[-1][which, me ^ k] = ref[which]
 
 
 def join_kernel(flag_ref, mine_ref, theirs_ref, out_ref, first_ref, second_ref):
@@ -404,10 +401,10 @@
 
 
 def first_grad_kernel(flag_ref, *refs, count):
-    weight, latent, par_ref, st_ref, scaled_ref, sums_ref, stack_ref = refs[-7:]
+    weight, latent, par_ref, st_ref, _, scaled_ref, sums_ref, stack_ref = refs[-8:]
     rows, frames, channels, cols = latent.shape
     mean, inverse, gain, shift, scale = norm_columns(par_ref, st_ref, count, 1)
-    fill_future(stack_ref, flag_ref, *refs[:-7])
+    fill_future(stack_ref, flag_ref, *refs[:-8])
     first = jnp.zeros((channels, 128), F32)
     second = jnp.zeros((channels, 128), F32)
     for row in range(rows):
@@ -557,39 +554,33 @@
         )
         after = ()
         received = [kept] + [lax.ppermute(v, axis, pairs) for v, pairs in zip(sent, exchanges)]
-    return received
-
-
-def gathered(flags, received, after, after_last):
+        last = sent[0]
+    return received, last
+
+
+def gathered(flags, received, after):
     (total,) = call(
         functools.partial(total_kernel, received=len(received)),
         [shape(received[0].shape, jnp.int16)],
-        [VMEM] * (len(received) + len(after)),
-        (*received, *after),
-    )
-    _, rows, _, channels = total.shape
+        [VMEM] * len(received),
+        tuple(received),
+    )
     back = list(enumerate(weight_rounds(), 4))[::-1]
-    number, (axis, _, exchanges) = back[0]
-    pieces = [total] + [lax.ppermute(total, axis, pairs) for pairs in exchanges]
-    values = call(
-        functools.partial(split_kernel, received=len(pieces), slot=number),
-        [shape((len(pieces), rows, SLOTS, channels), jnp.int16)] * 2,
-        [SMEM] + [VMEM] * (len(pieces) + 1),
-        (flags, *pieces, after_last),
-    )
-    results = []
-    for value in values:
-        for number, (axis, _, exchanges) in back[1:]:
-            value = value.reshape(-1, SLOTS, channels)
-            pieces = [value] + [lax.ppermute(value, axis, pairs) for pairs in exchanges]
-            (value,) = call(
-                functools.partial(gather_kernel, slot=number),
-                [shape((len(pieces), *value.shape), jnp.int16)],
-                [SMEM] + [VMEM] * len(pieces),
-                (flags, *pieces),
-            )
-        results.append(value.reshape(-1, SLOTS, channels))
-    return results
+    for number, (axis, _, exchanges) in back:
+        _, rows, _, channels = total.shape
+        pieces = [total] + [lax.ppermute(total, axis, pairs) for pairs in exchanges]
+        parts = len(pieces)
+        split = number == 4
+        dims = (parts, rows, SLOTS, channels)
+        values = call(
+            functools.partial(gather_kernel, received=parts, split=split, slot=number),
+            [shape(dims, jnp.int16)] * 2 if split else [shape((2, *dims), jnp.int16)],
+            [SMEM] + [VMEM] * (parts + len(after)),
+            (flags, *pieces, *after),
+        )
+        after = ()
+        total = values[0].reshape(2, -1, SLOTS, channels) if not split else None
+    return [value.reshape(-1, SLOTS, channels) for value in values]
 
 
 def joined(flags, mine, theirs):
@@ -611,13 +602,14 @@
     return columns
 
 
-def row_halos(down, up):
+def row_halos(down, up, after=()):
     above, below = shifted(down, "height", 1), shifted(up, "height", -1)
-    return call(rows_kernel, [shape((2, *down.shape[1:]), BF16)] * down.shape[0], [VMEM] * 2, (above, below))
-
-
-def halo(own, near, steps):
-    return shifted(own, "tm", steps), near, shifted(near, "tm", steps)
+    return call(
+        rows_kernel,
+        [shape((2, *down.shape[1:]), BF16)] * down.shape[0],
+        [VMEM] * (2 + len(after)),
+        (above, below, *after),
+    )
 
 
 def with_columns(flags, own, around, after=()):
@@ -672,8 +664,8 @@
         (latent, cotangent, par),
     )
     near, near_c = row_halos(down, up)
-    around = with_columns(flags, latent, halo(latent, near, 1))
-    around_c = halo(cotangent, near_c, -1)
+    around = with_columns(flags, latent, (shifted(latent, "tm", 1), near, shifted(near, "tm", 1)))
+    around_c = (shifted(cotangent, "tm", -1), near_c, shifted(near_c, "tm", -1))
     stats_first = all_stats(stats_first, count / devices)
     (weight_first,) = call(weight_forward_kernel, [shape(taps, BF16)], [VMEM], (conv_first,))
     (weight_second_t,) = call(weight_back_kernel, [shape(taps, BF16)], [VMEM], (conv_second,))
@@ -683,7 +675,7 @@
         functools.partial(conv_first_kernel, count=count),
         [shape(block, F32), small, shape(stack, BF16)],
         [SMEM] + [VMEM] * 10,
-        (flags, latent, *around, par, stats_first, weight_first, around_c[0]),
+        (flags, latent, *around, par, stats_first, weight_first, around_c[2]),
         flops=conv_flops,
         transcendentals=3 * latent.size,
     )
@@ -716,11 +708,12 @@
     hidden_grad, down, up = call(
         functools.partial(hidden_grad_kernel, count=count),
         [shape(block, BF16), message, message],
-        [VMEM] * 6,
-        (hidden, scaled, par, stats_second, sums, halves_second[0]),
-    )
-    (near,) = row_halos(down, up)
-    around = halo(hidden_grad, near, -1)
+        [VMEM] * 5,
+        (hidden, scaled, par, stats_second, sums),
+    )
+    future = shifted(hidden_grad, "tm", -1)
+    (near,) = row_halos(down, up, (future,))
+    around = (future, near, shifted(near, "tm", -1))
     halves_first = call(
         weight_first_kernel,
         halves,
@@ -734,16 +727,16 @@
     )
     weights, sent = scattered(flags, halves_second, halves_first)
     around = with_columns(flags, hidden_grad, around, (sent,))
+    weights, sent = summed(flags, weights, around[:2])
     scaled, sums_first = call(
         functools.partial(first_grad_kernel, count=count),
         [shape(block, F32), small],
-        [SMEM] + [VMEM] * 10,
-        (flags, hidden_grad, *around, weight_first_t, latent, par, stats_first),
+        [SMEM] + [VMEM] * 11,
+        (flags, hidden_grad, *around, weight_first_t, latent, par, stats_first, sent),
         scratch=[pltpu.VMEM(stack, BF16)],
         flops=conv_flops,
         transcendentals=latent.size,
     )
-    weights = summed(flags, weights, around[:2])
     sums_first = all_sum(sums_first)
     decoded_grad, token = call(
         functools.partial(decoded_grad_kernel, count=count),
@@ -751,7 +744,7 @@
         [VMEM] * 6,
         (scaled, latent, cotangent, par, stats_first, sums_first),
     )
-    second, first = gathered(flags, weights, (sums_first,), token)
+    second, first = gathered(flags, weights, (token,))
     conv_second_grad = joined(flags, second, swapped(second))
     conv_first_grad = joined(flags, first, swapped(first))
     return decoded_grad, conv_first_grad, conv_second_grad

time: 192 us -> 189 us (0.984)
  starting transfers between devices: 101 us -> 88.4 us
  waiting for transfers between devices: 32.8 us -> 44.9 us
  Pallas kernels: 50.7 us -> 48.3 us
    ppermute x10, starting transfers between devices: 20.6 us -> 9.5 us  [swapped(): return lax.ppermute(value, 'width', [(0, 1), (1, 0)])]
    ppermute x3 -> x6, waiting for transfers between devices: 0.98 us -> 10.7 us  [gathered(): pieces = [total] + [lax.ppermute(total, axis, pairs) for pairs in exchanges]]
    ppermute x6 -> x0, starting transfers between devices: 5.32 us -> none  [gathered(): pieces = [value] + [lax.ppermute(value, axis, pairs) for pairs in exchanges]]
    ppermute x14, waiting for transfers between devices: 8.24 us -> 5.46 us  [all_sum(): parts = [value] + [lax.ppermute(value, axis, pairs) for pairs in exchanges]]
    ppermute x3 -> x6, starting transfers between devices: 3.6 us -> 6.32 us  [gathered(): pieces = [total] + [lax.ppermute(total, axis, pairs) for pairs in exchanges]]
    ppermute x14, starting transfers between devices: 20.2 us -> 22.7 us  [all_sum(): parts = [value] + [lax.ppermute(value, axis, pairs) for pairs in exchanges]]
    pallas_call x28 -> x27, Pallas kernels: 50.7 us -> 48.3 us  [call(): pl.pallas_call(body, out_shape=tuple(outs), in_specs=specs, out_specs=tup...]
  transfers between devices with their start and end apart: 63 -> 60, of which waited for: 20 -> 24; matrix products, arithmetic and copies ran while one was open for 0% -> 0% of each run, Pallas kernels for 17% -> 14%
where the time goes in v11:
time: 189 us
  starting transfers between devices  88.4 us (47%)
  Pallas kernels  48.3 us (26%)
  waiting for transfers between devices  44.9 us (24%)
  local copies, waits for them, and re-layouts  4.96 us (3%)
    pallas_call x27, Pallas kernels, call(): pl.pallas_call(body, out_shape=tuple(outs), in_specs=specs, out_specs=tup...  48.3 us
    ppermute x14, starting transfers between devices, all_stats(): lax.ppermute(value, axis, pairs)  23.4 us
    ppermute x14, starting transfers between devices, all_sum(): parts = [value] + [lax.ppermute(value, axis, pairs) for pairs in exchanges]  22.7 us
    ppermute x10, starting transfers between devices, shifted(): lax.ppermute(value, axis, [(source, source + steps) for source in range(i...  20.2 us
    ppermute x10, waiting for transfers between devices, shifted(): lax.ppermute(value, axis, [(source, source + steps) for source in range(i...  15 us
    ppermute x6, waiting for transfers between devices, gathered(): pieces = [total] + [lax.ppermute(total, axis, pairs) for pairs in exchanges]  10.7 us
    ppermute x10, starting transfers between devices, swapped(): return lax.ppermute(value, 'width', [(0, 1), (1, 0)])  9.5 us
    ppermute x14, waiting for transfers between devices, all_stats(): lax.ppermute(value, axis, pairs)  8.13 us
  transfers between devices with their start and end apart: 60, of which 24 were waited for; matrix products, arithmetic and copies ran while one was open for 0% of the time, Pallas kernels for 14%

profile of v11, /device:TPU:1, one launch (start us, length us, event | category | flops | bytes accessed | tf_op | source)
XLA Modules:
  0.0 188.6 jit_solution(14318929259492446898)
XLA Ops:
  4.3 2.6 %shard_map.112 = (bf16[4,2,128,256]{3,2,1,0:T(8,128)(2,1)S(1)}, bf16[4,2,128,256]{3,2,1,0:T(8,128)(2,1)S(1)}, bf16[2,2,128,256]{3,2,1,0:T(8,128)(2,1)S(1)}, bf16...) custom-call(bf16[128,2,4,256]{3,2,1,0:T(4,128)(2,1)S(1)} %copy-done.3, bf16[128,2,4,256]{3,2,1,0:T(4,128)(2,1)S(1)} %copy-done.4, ...), custom_call_target="tpu_custom_call" | custom-call | bytes 2626560 | tf_op jit(solution)/shard_map/pallas_call | solution.py:24
  7.0 2.2 %collective-permute-start.6 = (f32[1,2,128]{2,1,0:T(2,128)S(1)}, f32[1,2,128]{2,1,0:T(2,128)S(1)}, u32[]{:S(2)}, u32[]{:S(2)}) collective-permute-start(f32[1,2,128]{2,1,0:T(2,128)S(1)} %get-tuple-element.43), channel_id=1, source_target_pairs={{0,8},{8,0},{16,24},{24,16},{1,9},{9,1},{17,25},{25,17},{2,10},{10... | collective-permute-start | bytes 3080 | tf_op jit(solution)/shard_map/ppermute | solution.py:507
  9.2 2.3 %collective-permute-start.7 = (f32[1,2,128]{2,1,0:T(2,128)S(1)}, f32[1,2,128]{2,1,0:T(2,128)S(1)}, u32[]{:S(2)}, u32[]{:S(2)}) collective-permute-start(f32[1,2,128]{2,1,0:T(2,128)S(1)} %get-tuple-element.43), channel_id=1, source_target_pairs={{0,16},{8,24},{16,0},{24,8},{1,17},{9,25},{17,1},{25,9},{2,18},{10... | collective-permute-start | bytes 3080 | tf_op jit(solution)/shard_map/ppermute | solution.py:507
  11.5 3.1 %collective-permute-start.1 = (bf16[2,2,128,256]{3,2,1,0:T(8,128)(2,1)S(1)}, bf16[2,2,128,256]{3,2,1,0:T(8,128)(2,1)S(1)}, u32[]{:S(2)}, u32[]{:S(2)}) collective-permute-start(bf16[2,2,128,256]{3,2,1,0:T(8,128)(2,1)S(1)} %get-tuple-element.40), channel_id=1, source_target_pairs={{0,2},{2,4},{4,6},{1,3},{3,5},{5,7},{8,10},{10,12},{12,14},{9,11},... | collective-permute-start | bytes 786440 | tf_op jit(solution)/shard_map/ppermute | solution.py:479
  16.0 3.1 %collective-permute-start.10 = (f32[1,2,128]{2,1,0:T(2,128)S(1)}, f32[1,2,128]{2,1,0:T(2,128)S(1)}, u32[]{:S(2)}, u32[]{:S(2)}) collective-permute-start(f32[1,2,128]{2,1,0:T(2,128)S(1)} %pad_maximum_fusion), channel_id=1, source_target_pairs={{0,4},{2,6},{4,0},{6,2},{1,5},{3,7},{5,1},{7,3},{8,12},{10,14},{12... | collective-permute-start | bytes 3080 | tf_op jit(solution)/shard_map/ppermute | solution.py:507
  20.3 3.0 %collective-permute-start = (bf16[4,2,128,256]{3,2,1,0:T(8,128)(2,1)S(1)}, bf16[4,2,128,256]{3,2,1,0:T(8,128)(2,1)}, u32[]{:S(2)}, u32[]{:S(2)}) collective-permute-start(bf16[4,2,128,256]{3,2,1,0:T(8,128)(2,1)S(1)} %get-tuple-element.39.first_ref.own.refs_7_.latent), channel_id=1, source_target_pairs={{0,8},{8,16},{16,24},{1,9},{9,17},{17,25},{2,10},{10,18},{18,26},{... | collective-permute-start | bytes 1572872 | tf_op jit(solution)/shard_map/ppermute | solution.py:479
  23.4 3.0 %collective-permute-done.9 = f32[1,2,128]{2,1,0:T(2,128)S(1)} collective-permute-done((f32[1,2,128]{2,1,0:T(2,128)S(1)}, f32[1,2,128]{2,1,0:T(2,128)S(1)}, u32[]{:S(2)}, u32[]{:S(2)}) %collective-permute-start.9) | collective-permute-done | bytes 1056 | tf_op jit(solution)/shard_map/ppermute | solution.py:507
  27.8 2.9 %collective-permute-start.3 = (bf16[2,2,128,256]{3,2,1,0:T(8,128)(2,1)}, bf16[2,2,128,256]{3,2,1,0:T(8,128)(2,1)}, u32[]{:S(2)}, u32[]{:S(2)}) collective-permute-start(bf16[2,2,128,256]{3,2,1,0:T(8,128)(2,1)} %get-tuple-element.42.first_ref.near), channel_id=1, source_target_pairs={{0,8},{8,16},{16,24},{1,9},{9,17},{17,25},{2,10},{10,18},{18,26},{... | collective-permute-start | bytes 786440 | tf_op jit(solution)/shard_map/ppermute | solution.py:479
  30.7 2.8 %collective-permute-start.12 = (f32[1,2,128]{2,1,0:T(2,128)S(1)}, f32[1,2,128]{2,1,0:T(2,128)S(1)}, u32[]{:S(2)}, u32[]{:S(2)}) collective-permute-start(f32[1,2,128]{2,1,0:T(2,128)S(1)} %pad_maximum_fusion.1), channel_id=1, source_target_pairs={{0,1},{1,0},{2,3},{3,2},{4,5},{5,4},{6,7},{7,6},{8,9},{9,8},{10,11... | collective-permute-start | bytes 3080 | tf_op jit(solution)/shard_map/ppermute | solution.py:507
  38.2 3.6 %collective-permute-start.5 = (bf16[128,128]{1,0:T(8,128)(2,1)S(1)}, bf16[128,128]{1,0:T(8,128)(2,1)S(1)}, u32[]{:S(2)}, u32[]{:S(2)}) collective-permute-start(bf16[128,128]{1,0:T(8,128)(2,1)S(1)} %shard_map.115), channel_id=1, source_target_pairs={{0,1},{1,0},{2,3},{3,2},{4,5},{5,4},{6,7},{7,6},{8,9},{9,8},{10,11... | collective-permute-start | bytes 98312 | tf_op jit(solution)/shard_map/ppermute | solution.py:520
  45.2 5.3 %shard_map.117 = (f32[4,2,128,256]{3,2,1,0:T(8,128)S(1)}, f32[1,2,128]{2,1,0:T(2,128)S(1)}, bf16[6,4,384,256]{3,2,1,0:T(8,128)(2,1)S(1)}) custom-call(s32[6]{0:T(128)S(1)} %stack.57.flag_ref, bf16[4,2,128,256]{3,2,1,0:T(8,128)(2,1)S(1)} %get-tuple-element.39.first_ref.own.refs_7_.latent, bf16[4,2,128,256]{3,2,1,0:T(8,128)(2,1)} %collective-permute-done.second_ref.past, ...), custom_call_target="tpu_custom_call" | custom-call | flops 7247757312 | bytes 10033176 | tf_op jit(solution)/shard_map/pallas_call | solution.py:24
  50.4 2.3 %collective-permute-start.17 = (f32[1,2,128]{2,1,0:T(2,128)S(1)}, f32[1,2,128]{2,1,0:T(2,128)S(1)}, u32[]{:S(2)}, u32[]{:S(2)}) collective-permute-start(f32[1,2,128]{2,1,0:T(2,128)S(1)} %get-tuple-element.47.refs_0_), channel_id=1, source_target_pairs={{0,8},{8,0},{16,24},{24,16},{1,9},{9,1},{17,25},{25,17},{2,10},{10... | collective-permute-start | bytes 3080 | tf_op jit(solution)/shard_map/ppermute | solution.py:507
  52.7 3.2 %collective-permute-start.18 = (f32[1,2,128]{2,1,0:T(2,128)S(1)}, f32[1,2,128]{2,1,0:T(2,128)S(1)}, u32[]{:S(2)}, u32[]{:S(2)}) collective-permute-start(f32[1,2,128]{2,1,0:T(2,128)S(1)} %get-tuple-element.47.refs_0_), channel_id=1, source_target_pairs={{0,16},{8,24},{16,0},{24,8},{1,17},{9,25},{17,1},{25,9},{2,18},{10... | collective-permute-start | bytes 3080 | tf_op jit(solution)/shard_map/ppermute | solution.py:507
  57.4 2.7 %collective-permute-done.19 = f32[1,2,128]{2,1,0:T(2,128)S(1)} collective-permute-done((f32[1,2,128]{2,1,0:T(2,128)S(1)}, f32[1,2,128]{2,1,0:T(2,128)S(1)}, u32[]{:S(2)}, u32[]{:S(2)}) %collective-permute-start.19) | collective-permute-done | bytes 1056 | tf_op jit(solution)/shard_map/ppermute | solution.py:507
  65.3 3.6 %collective-permute-start.23 = (f32[1,2,128]{2,1,0:T(2,128)S(1)}, f32[1,2,128]{2,1,0:T(2,128)S(1)}, u32[]{:S(2)}, u32[]{:S(2)}) collective-permute-start(f32[1,2,128]{2,1,0:T(2,128)S(1)} %pad_maximum_fusion.4), channel_id=1, source_target_pairs={{0,1},{1,0},{2,3},{3,2},{4,5},{5,4},{6,7},{7,6},{8,9},{9,8},{10,11... | collective-permute-start | bytes 3080 | tf_op jit(solution)/shard_map/ppermute | solution.py:507
  74.6 3.4 %shard_map.121 = (f32[4,2,128,256]{3,2,1,0:T(8,128)S(1)}, bf16[6,4,384,256]{3,2,1,0:T(8,128)(2,1)S(1)}) custom-call(s32[6]{0:T(128)S(1)} %stack.57.flag_ref, bf16[4,2,128,256]{3,2,1,0:T(8,128)(2,1)S(1)} %get-tuple-element.46.first_ref.refs_0_.cotangent, bf16[4,2,128,256]{3,2,1,0:T(8,128)(2,1)S(1)} %collective-permute-done.14.second_ref.refs_1_, ...), custom_call_target="tpu_custom_call" | custom-call | flops 7247757312 | bytes 9764888 | tf_op jit(solution)/shard_map/pallas_call | solution.py:24
  82.6 2.2 %collective-permute-done.26 = f32[1,2,128]{2,1,0:T(2,128)S(1)} collective-permute-done((f32[1,2,128]{2,1,0:T(2,128)S(1)}, f32[1,2,128]{2,1,0:T(2,128)S(1)}, u32[]{:S(2)}, u32[]{:S(2)}) %collective-permute-start.26) | collective-permute-done | bytes 1056 | tf_op jit(solution)/shard_map/ppermute | solution.py:500
  87.7 2.1 %collective-permute-done.29 = f32[1,2,128]{2,1,0:T(2,128)S(1)} collective-permute-done((f32[1,2,128]{2,1,0:T(2,128)S(1)}, f32[1,2,128]{2,1,0:T(2,128)S(1)}, u32[]{:S(2)}, u32[]{:S(2)}) %collective-permute-start.29) | collective-permute-done | bytes 1056 | tf_op jit(solution)/shard_map/ppermute | solution.py:500
  89.8 3.5 %collective-permute-start.30 = (f32[1,2,128]{2,1,0:T(2,128)S(1)}, f32[1,2,128]{2,1,0:T(2,128)S(1)}, u32[]{:S(2)}, u32[]{:S(2)}) collective-permute-start(f32[1,2,128]{2,1,0:T(2,128)S(1)} %add_add_fusion.2), channel_id=1, source_target_pairs={{0,1},{1,0},{2,3},{3,2},{4,5},{5,4},{6,7},{7,6},{8,9},{9,8},{10,11... | collective-permute-start | bytes 3080 | tf_op jit(solution)/shard_map/ppermute | solution.py:500
  93.3 4.6 %shard_map.125 = (f32[2048,128]{1,0:T(8,128)S(1)}, f32[2048,128]{1,0:T(8,128)S(1)}) custom-call(s32[6]{0:T(128)S(1)} %stack.57.flag_ref, bf16[6,4,384,256]{3,2,1,0:T(8,128)(2,1)S(1)} %get-tuple-element.54.stack_ref, bf16[4,2,128,256]{3,2,1,0:T(8,128)(2,1)S(1)} %get-tuple-element.55.act_ref), custom_call_target="tpu_custom_call" | custom-call | flops 7247757312 | bytes 7340056 | tf_op jit(solution)/shard_map/pallas_call | solution.py:24
  98.5 4.1 %shard_map.126 = (f32[2048,128]{1,0:T(8,128)S(1)}, f32[2048,128]{1,0:T(8,128)S(1)}) custom-call(s32[6]{0:T(128)S(1)} %stack.57.flag_ref, bf16[6,4,384,256]{3,2,1,0:T(8,128)(2,1)S(1)} %get-tuple-element.58.stack_ref, bf16[4,2,128,256]{3,2,1,0:T(8,128)(2,1)S(1)} %get-tuple-element.51.grad_ref.first_ref.refs_0_), custom_call_target="tpu_custom_call" | custom-call | flops 7247757312 | bytes 7340056 | tf_op jit(solution)/shard_map/pallas_call | solution.py:24
  104.5 3.1 %collective-permute-start.32 = (bf16[1,2,128,256]{3,2,1,0:T(8,128)(2,1)S(1)}, bf16[1,2,128,256]{3,2,1,0:T(8,128)(2,1)S(1)}, u32[]{:S(2)}, u32[]{:S(2)}) collective-permute-start(bf16[1,2,128,256]{3,2,1,0:T(8,128)(2,1)S(1)} %get-tuple-element.52), channel_id=1, source_target_pairs={{0,2},{2,4},{4,6},{1,3},{3,5},{5,7},{8,10},{10,12},{12,14},{9,11},... | collective-permute-start | bytes 393224 | tf_op jit(solution)/shard_map/ppermute | solution.py:479
  110.5 3.8 %collective-permute-done.33.below_ref = bf16[1,2,128,256]{3,2,1,0:T(8,128)(2,1)S(1)} collective-permute-done((bf16[1,2,128,256]{3,2,1,0:T(8,128)(2,1)S(1)}, bf16[1,2,128,256]{3,2,1,0:T(8,128)(2,1)S(1)}, u32[]{:S(2)}, u32[]{:S(2)}) %collective-permute-start.33) | collective-permute-done | bytes 131104 | tf_op jit(solution)/shard_map/ppermute | solution.py:479
  114.3 4.3 %collective-permute-done.31.refs_0_.second_ref.refs_4_.refs_1_ = bf16[4,2,128,256]{3,2,1,0:T(8,128)(2,1)S(1)} collective-permute-done((bf16[4,2,128,256]{3,2,1,0:T(8,128)(2,1)S(1)}, bf16[4,2,128,256]{3,2,1,0:T(8,128)(2,1)S(1)}, u32[]{:S(2)}, u32[]{:S(2)}) %collective-permute-start.31) | collective-permute-done | bytes 524320 | tf_op jit(solution)/shard_map/ppermute | solution.py:479
  124.0 3.5 %collective-permute-done.34.second_ref.refs_3_ = bf16[2,2,128,256]{3,2,1,0:T(8,128)(2,1)S(1)} collective-permute-done((bf16[2,2,128,256]{3,2,1,0:T(8,128)(2,1)S(1)}, bf16[2,2,128,256]{3,2,1,0:T(8,128)(2,1)S(1)}, u32[]{:S(2)}, u32[]{:S(2)}) %collective-permute-start.34) | collective-permute-done | bytes 262176 | tf_op jit(solution)/shard_map/ppermute | solution.py:479
  135.0 4.0 %shard_map.132 = (f32[4,2,128,256]{3,2,1,0:T(8,128)S(1)}, f32[1,2,128]{2,1,0:T(2,128)S(1)}) custom-call(s32[6]{0:T(128)S(1)} %stack.57.flag_ref, bf16[4,2,128,256]{3,2,1,0:T(8,128)(2,1)S(1)} %get-tuple-element.51.grad_ref.first_ref.refs_0_, bf16[4,2,128,256]{3,2,1,0:T(8,128)(2,1)S(1)} %collective-permute-done.31.refs_0_.second_ref.refs_4_.refs_1_, ...), custom_call_target="tpu_custom_call" | custom-call | flops 7247757312 | bytes 5642264 | tf_op jit(solution)/shard_map/pallas_call | solution.py:24
  151.9 2.3 %collective-permute-start.54 = (s16[2,4,32,128]{3,2,1,0:T(8,128)(2,1)S(1)}, s16[2,4,32,128]{3,2,1,0:T(8,128)(2,1)S(1)}, u32[]{:S(2)}, u32[]{:S(2)}) collective-permute-start(s16[2,4,32,128]{3,2,1,0:T(8,128)(2,1)S(1)} %shard_map.134.refs_0_), channel_id=1, source_target_pairs={{0,24},{8,16},{16,8},{24,0},{1,25},{9,17},{17,9},{25,1},{2,26},{10... | collective-permute-start | bytes 196616 | tf_op jit(solution)/shard_map/ppermute | solution.py:571
  154.3 6.2 %collective-permute-start.48 = (f32[1,2,128]{2,1,0:T(2,128)S(1)}, f32[1,2,128]{2,1,0:T(2,128)S(1)}, u32[]{:S(2)}, u32[]{:S(2)}) collective-permute-start(f32[1,2,128]{2,1,0:T(2,128)S(1)} %add_add_fusion), channel_id=1, source_target_pairs={{0,1},{1,0},{2,3},{3,2},{4,5},{5,4},{6,7},{7,6},{8,9},{9,8},{10,11... | collective-permute-start | bytes 3080 | tf_op jit(solution)/shard_map/ppermute | solution.py:500
  166.5 4.0 %collective-permute-done.55.refs_1_ = s16[2,16,32,128]{3,2,1,0:T(8,128)(2,1)S(1)} collective-permute-done((s16[2,16,32,128]{3,2,1,0:T(8,128)(2,1)S(1)}, s16[2,16,32,128]{3,2,1,0:T(8,128)(2,1)S(1)}, u32[]{:S(2)}, u32[]{:S(2)}) %collective-permute-start.55) | collective-permute-done | bytes 262176 | tf_op jit(solution)/shard_map/ppermute | solution.py:571
  171.1 6.0 %collective-permute-done.57.refs_3_ = s16[2,16,32,128]{3,2,1,0:T(8,128)(2,1)S(1)} collective-permute-done((s16[2,16,32,128]{3,2,1,0:T(8,128)(2,1)S(1)}, s16[2,16,32,128]{3,2,1,0:T(8,128)(2,1)S(1)}, u32[]{:S(2)}, u32[]{:S(2)}) %collective-permute-start.57) | collective-permute-done | bytes 262176 | tf_op jit(solution)/shard_map/ppermute | solution.py:571
  180.8 3.9 %shard_map.138 = f32[128,3456]{1,0:T(8,128)} custom-call(s32[6]{0:T(128)S(1)} %stack.57.flag_ref, s16[64,32,128]{2,1,0:T(8,128)(2,1)S(1)} %bitcast.35, s16[64,32,128]{2,1,0:T(8,128)(2,1)S(1)} %collective-permute-done.59.theirs_ref), custom_call_target="tpu_custom_call" | custom-call | bytes 2818072 | tf_op jit(solution)/shard_map/pallas_call | solution.py:24
  184.7 3.9 %shard_map.137 = f32[128,3456]{1,0:T(8,128)} custom-call(s32[6]{0:T(128)S(1)} %stack.57.flag_ref, s16[64,32,128]{2,1,0:T(8,128)(2,1)S(1)} %bitcast.33, s16[64,32,128]{2,1,0:T(8,128)(2,1)S(1)} %collective-permute-done.58.theirs_ref), custom_call_target="tpu_custom_call" | custom-call | bytes 2818072 | tf_op jit(solution)/shard_map/pallas_call | solution.py:24
  (154 shorter events, 76.7 us)
Async XLA Ops:
  7.0 8.9 %collective-permute-start.6 = (f32[1,2,128]{2,1,0:T(2,128)S(1)}, f32[1,2,128]{2,1,0:T(2,128)S(1)}, u32[]{:S(2)}, u32[]{:S(2)}) collective-permute-start(f32[1,2,128]{2,1,0:T(2,128)S(1)} %get-tuple-element.43), channel_id=1, source_target_pairs={{0,8},{8,0},{16,24},{24,16},{1,9},{9,1},{17,25},{25,17},{2,10},{10... | collective-permute-start | bytes 3080 | tf_op jit(solution)/shard_map/ppermute | solution.py:507
  9.2 6.8 %collective-permute-start.7 = (f32[1,2,128]{2,1,0:T(2,128)S(1)}, f32[1,2,128]{2,1,0:T(2,128)S(1)}, u32[]{:S(2)}, u32[]{:S(2)}) collective-permute-start(f32[1,2,128]{2,1,0:T(2,128)S(1)} %get-tuple-element.43), channel_id=1, source_target_pairs={{0,16},{8,24},{16,0},{24,8},{1,17},{9,25},{17,1},{25,9},{2,18},{10... | collective-permute-start | bytes 3080 | tf_op jit(solution)/shard_map/ppermute | solution.py:507
  11.5 14.9 %collective-permute-start.1 = (bf16[2,2,128,256]{3,2,1,0:T(8,128)(2,1)S(1)}, bf16[2,2,128,256]{3,2,1,0:T(8,128)(2,1)S(1)}, u32[]{:S(2)}, u32[]{:S(2)}) collective-permute-start(bf16[2,2,128,256]{3,2,1,0:T(8,128)(2,1)S(1)} %get-tuple-element.40), channel_id=1, source_target_pairs={{0,2},{2,4},{4,6},{1,3},{3,5},{5,7},{8,10},{10,12},{12,14},{9,11},... | collective-permute-start | bytes 786440 | tf_op jit(solution)/shard_map/ppermute | solution.py:479
  14.6 11.7 %collective-permute-start.2 = (bf16[2,2,128,256]{3,2,1,0:T(8,128)(2,1)S(1)}, bf16[2,2,128,256]{3,2,1,0:T(8,128)(2,1)S(1)}, u32[]{:S(2)}, u32[]{:S(2)}) collective-permute-start(bf16[2,2,128,256]{3,2,1,0:T(8,128)(2,1)S(1)} %get-tuple-element.41), channel_id=1, source_target_pairs={{2,0},{4,2},{6,4},{3,1},{5,3},{7,5},{10,8},{12,10},{14,12},{11,9},... | collective-permute-start | bytes 786440 | tf_op jit(solution)/shard_map/ppermute | solution.py:479
  19.3 7.0 %collective-permute-start.9 = (f32[1,2,128]{2,1,0:T(2,128)S(1)}, f32[1,2,128]{2,1,0:T(2,128)S(1)}, u32[]{:S(2)}, u32[]{:S(2)}) collective-permute-start(f32[1,2,128]{2,1,0:T(2,128)S(1)} %pad_maximum_fusion), channel_id=1, source_target_pairs={{0,2},{2,0},{4,6},{6,4},{1,3},{3,1},{5,7},{7,5},{8,10},{10,8},{12,... | collective-permute-start | bytes 3080 | tf_op jit(solution)/shard_map/ppermute | solution.py:507
  20.3 21.5 %collective-permute-start = (bf16[4,2,128,256]{3,2,1,0:T(8,128)(2,1)S(1)}, bf16[4,2,128,256]{3,2,1,0:T(8,128)(2,1)}, u32[]{:S(2)}, u32[]{:S(2)}) collective-permute-start(bf16[4,2,128,256]{3,2,1,0:T(8,128)(2,1)S(1)} %get-tuple-element.39.first_ref.own.refs_7_.latent), channel_id=1, source_target_pairs={{0,8},{8,16},{16,24},{1,9},{9,17},{17,25},{2,10},{10,18},{18,26},{... | collective-permute-start | bytes 1572872 | tf_op jit(solution)/shard_map/ppermute | solution.py:479
  27.8 9.0 %collective-permute-start.3 = (bf16[2,2,128,256]{3,2,1,0:T(8,128)(2,1)}, bf16[2,2,128,256]{3,2,1,0:T(8,128)(2,1)}, u32[]{:S(2)}, u32[]{:S(2)}) collective-permute-start(bf16[2,2,128,256]{3,2,1,0:T(8,128)(2,1)} %get-tuple-element.42.first_ref.near), channel_id=1, source_target_pairs={{0,8},{8,16},{16,24},{1,9},{9,17},{17,25},{2,10},{10,18},{18,26},{... | collective-permute-start | bytes 786440 | tf_op jit(solution)/shard_map/ppermute | solution.py:479
  34.9 10.0 %collective-permute-start.13 = (bf16[2,2,128,256]{3,2,1,0:T(8,128)(2,1)}, bf16[2,2,128,256]{3,2,1,0:T(8,128)(2,1)S(1)}, u32[]{:S(2)}, u32[]{:S(2)}) collective-permute-start(bf16[2,2,128,256]{3,2,1,0:T(8,128)(2,1)} %copy-done.5), channel_id=1, source_target_pairs={{8,0},{16,8},{24,16},{9,1},{17,9},{25,17},{10,2},{18,10},{26,18},{... | collective-permute-start | bytes 786440 | tf_op jit(solution)/shard_map/ppermute | solution.py:479
  38.2 6.7 %collective-permute-start.5 = (bf16[128,128]{1,0:T(8,128)(2,1)S(1)}, bf16[128,128]{1,0:T(8,128)(2,1)S(1)}, u32[]{:S(2)}, u32[]{:S(2)}) collective-permute-start(bf16[128,128]{1,0:T(8,128)(2,1)S(1)} %shard_map.115), channel_id=1, source_target_pairs={{0,1},{1,0},{2,3},{3,2},{4,5},{5,4},{6,7},{7,6},{8,9},{9,8},{10,11... | collective-permute-start | bytes 98312 | tf_op jit(solution)/shard_map/ppermute | solution.py:520
  50.4 6.9 %collective-permute-start.17 = (f32[1,2,128]{2,1,0:T(2,128)S(1)}, f32[1,2,128]{2,1,0:T(2,128)S(1)}, u32[]{:S(2)}, u32[]{:S(2)}) collective-permute-start(f32[1,2,128]{2,1,0:T(2,128)S(1)} %get-tuple-element.47.refs_0_), channel_id=1, source_target_pairs={{0,8},{8,0},{16,24},{24,16},{1,9},{9,1},{17,25},{25,17},{2,10},{10... | collective-permute-start | bytes 3080 | tf_op jit(solution)/shard_map/ppermute | solution.py:507
  55.9 14.6 %collective-permute-start.14 = (bf16[4,2,128,256]{3,2,1,0:T(8,128)(2,1)S(1)}, bf16[4,2,128,256]{3,2,1,0:T(8,128)(2,1)S(1)}, u32[]{:S(2)}, u32[]{:S(2)}) collective-permute-start(bf16[4,2,128,256]{3,2,1,0:T(8,128)(2,1)S(1)} %get-tuple-element.46.first_ref.refs_0_.cotangent), channel_id=1, source_target_pairs={{8,0},{16,8},{24,16},{9,1},{17,9},{25,17},{10,2},{18,10},{26,18},{... | collective-permute-start | bytes 1572872 | tf_op jit(solution)/shard_map/ppermute | solution.py:479
  65.3 8.4 %collective-permute-start.23 = (f32[1,2,128]{2,1,0:T(2,128)S(1)}, f32[1,2,128]{2,1,0:T(2,128)S(1)}, u32[]{:S(2)}, u32[]{:S(2)}) collective-permute-start(f32[1,2,128]{2,1,0:T(2,128)S(1)} %pad_maximum_fusion.4), channel_id=1, source_target_pairs={{0,1},{1,0},{2,3},{3,2},{4,5},{5,4},{6,7},{7,6},{8,9},{9,8},{10,11... | collective-permute-start | bytes 3080 | tf_op jit(solution)/shard_map/ppermute | solution.py:507
  89.8 8.2 %collective-permute-start.30 = (f32[1,2,128]{2,1,0:T(2,128)S(1)}, f32[1,2,128]{2,1,0:T(2,128)S(1)}, u32[]{:S(2)}, u32[]{:S(2)}) collective-permute-start(f32[1,2,128]{2,1,0:T(2,128)S(1)} %add_add_fusion.2), channel_id=1, source_target_pairs={{0,1},{1,0},{2,3},{3,2},{4,5},{5,4},{6,7},{7,6},{8,9},{9,8},{10,11... | collective-permute-start | bytes 3080 | tf_op jit(solution)/shard_map/ppermute | solution.py:500
  98.0 22.2 %collective-permute-start.35 = (f32[64,32,128]{2,1,0:T(8,128)S(1)}, f32[64,32,128]{2,1,0:T(8,128)S(1)}, u32[]{:S(2)}, u32[]{:S(2)}) collective-permute-start(f32[64,32,128]{2,1,0:T(8,128)S(1)} %bitcast.39), channel_id=1, source_target_pairs={{0,1},{1,0},{2,3},{3,2},{4,5},{5,4},{6,7},{7,6},{8,9},{9,8},{10,11... | collective-permute-start | bytes 3145736 | tf_op jit(solution)/shard_map/ppermute | solution.py:520
  102.7 17.5 %collective-permute-start.36 = (f32[64,32,128]{2,1,0:T(8,128)S(1)}, f32[64,32,128]{2,1,0:T(8,128)S(1)}, u32[]{:S(2)}, u32[]{:S(2)}) collective-permute-start(f32[64,32,128]{2,1,0:T(8,128)S(1)} %bitcast.40), channel_id=1, source_target_pairs={{0,1},{1,0},{2,3},{3,2},{4,5},{5,4},{6,7},{7,6},{8,9},{9,8},{10,11... | collective-permute-start | bytes 3145736 | tf_op jit(solution)/shard_map/ppermute | solution.py:520
  103.2 15.4 %collective-permute-start.31 = (bf16[4,2,128,256]{3,2,1,0:T(8,128)(2,1)S(1)}, bf16[4,2,128,256]{3,2,1,0:T(8,128)(2,1)S(1)}, u32[]{:S(2)}, u32[]{:S(2)}) collective-permute-start(bf16[4,2,128,256]{3,2,1,0:T(8,128)(2,1)S(1)} %get-tuple-element.51.grad_ref.first_ref.refs_0_), channel_id=1, source_target_pairs={{8,0},{16,8},{24,16},{9,1},{17,9},{25,17},{10,2},{18,10},{26,18},{... | collective-permute-start | bytes 1572872 | tf_op jit(solution)/shard_map/ppermute | solution.py:479
  107.6 6.7 %collective-permute-start.33 = (bf16[1,2,128,256]{3,2,1,0:T(8,128)(2,1)S(1)}, bf16[1,2,128,256]{3,2,1,0:T(8,128)(2,1)S(1)}, u32[]{:S(2)}, u32[]{:S(2)}) collective-permute-start(bf16[1,2,128,256]{3,2,1,0:T(8,128)(2,1)S(1)} %get-tuple-element.53), channel_id=1, source_target_pairs={{2,0},{4,2},{6,4},{3,1},{5,3},{7,5},{10,8},{12,10},{14,12},{11,9},... | collective-permute-start | bytes 393224 | tf_op jit(solution)/shard_map/ppermute | solution.py:479
  118.6 8.9 %collective-permute-start.34 = (bf16[2,2,128,256]{3,2,1,0:T(8,128)(2,1)S(1)}, bf16[2,2,128,256]{3,2,1,0:T(8,128)(2,1)S(1)}, u32[]{:S(2)}, u32[]{:S(2)}) collective-permute-start(bf16[2,2,128,256]{3,2,1,0:T(8,128)(2,1)S(1)} %shard_map.124.first_ref.refs_5_.refs_2_), channel_id=1, source_target_pairs={{8,0},{16,8},{24,16},{9,1},{17,9},{25,17},{10,2},{18,10},{26,18},{... | collective-permute-start | bytes 786440 | tf_op jit(solution)/shard_map/ppermute | solution.py:479
  121.3 10.9 %collective-permute-start.39 = (s16[2,16,32,128]{3,2,1,0:T(8,128)(2,1)S(1)}, s16[2,16,32,128]{3,2,1,0:T(8,128)(2,1)S(1)}, u32[]{:S(2)}, u32[]{:S(2)}) collective-permute-start(s16[2,16,32,128]{3,2,1,0:T(8,128)(2,1)S(1)} %get-tuple-element.61.refs_0_), channel_id=1, source_target_pairs={{0,2},{2,0},{4,6},{6,4},{1,3},{3,1},{5,7},{7,5},{8,10},{10,8},{12,... | collective-permute-start | bytes 786440 | tf_op jit(solution)/shard_map/ppermute | solution.py:540
  122.6 9.6 %collective-permute-start.40 = (s16[2,16,32,128]{3,2,1,0:T(8,128)(2,1)S(1)}, s16[2,16,32,128]{3,2,1,0:T(8,128)(2,1)S(1)}, u32[]{:S(2)}, u32[]{:S(2)}) collective-permute-start(s16[2,16,32,128]{3,2,1,0:T(8,128)(2,1)S(1)} %get-tuple-element.63), channel_id=1, source_target_pairs={{0,4},{2,6},{4,0},{6,2},{1,5},{3,7},{5,1},{7,3},{8,12},{10,14},{12... | collective-permute-start | bytes 786440 | tf_op jit(solution)/shard_map/ppermute | solution.py:540
  122.6 11.4 %collective-permute-start.41 = (s16[2,16,32,128]{3,2,1,0:T(8,128)(2,1)S(1)}, s16[2,16,32,128]{3,2,1,0:T(8,128)(2,1)S(1)}, u32[]{:S(2)}, u32[]{:S(2)}) collective-permute-start(s16[2,16,32,128]{3,2,1,0:T(8,128)(2,1)S(1)} %get-tuple-element.64), channel_id=1, source_target_pairs={{0,6},{2,4},{4,2},{6,0},{1,7},{3,5},{5,3},{7,1},{8,14},{10,12},{12... | collective-permute-start | bytes 786440 | tf_op jit(solution)/shard_map/ppermute | solution.py:540
  128.5 6.5 %collective-permute-start.38 = (bf16[128,128]{1,0:T(8,128)(2,1)S(1)}, bf16[128,128]{1,0:T(8,128)(2,1)S(1)}, u32[]{:S(2)}, u32[]{:S(2)}) collective-permute-start(bf16[128,128]{1,0:T(8,128)(2,1)S(1)} %shard_map.129), channel_id=1, source_target_pairs={{0,1},{1,0},{2,3},{3,2},{4,5},{5,4},{6,7},{7,6},{8,9},{9,8},{10,11... | collective-permute-start | bytes 98312 | tf_op jit(solution)/shard_map/ppermute | solution.py:520
  139.0 6.3 %collective-permute-start.42 = (f32[1,2,128]{2,1,0:T(2,128)S(1)}, f32[1,2,128]{2,1,0:T(2,128)S(1)}, u32[]{:S(2)}, u32[]{:S(2)}) collective-permute-start(f32[1,2,128]{2,1,0:T(2,128)S(1)} %get-tuple-element.67), channel_id=1, source_target_pairs={{0,8},{8,0},{16,24},{24,16},{1,9},{9,1},{17,25},{25,17},{2,10},{10... | collective-permute-start | bytes 3080 | tf_op jit(solution)/shard_map/ppermute | solution.py:500
  143.0 6.0 %collective-permute-start.49 = (s16[2,4,32,128]{3,2,1,0:T(8,128)(2,1)S(1)}, s16[2,4,32,128]{3,2,1,0:T(8,128)(2,1)S(1)}, u32[]{:S(2)}, u32[]{:S(2)}) collective-permute-start(s16[2,4,32,128]{3,2,1,0:T(8,128)(2,1)S(1)} %get-tuple-element.65.refs_10_), channel_id=1, source_target_pairs={{0,8},{8,0},{16,24},{24,16},{1,9},{9,1},{17,25},{25,17},{2,10},{10... | collective-permute-start | bytes 196616 | tf_op jit(solution)/shard_map/ppermute | solution.py:556
  147.5 6.8 %collective-permute-start.46 = (f32[1,2,128]{2,1,0:T(2,128)S(1)}, f32[1,2,128]{2,1,0:T(2,128)S(1)}, u32[]{:S(2)}, u32[]{:S(2)}) collective-permute-start(f32[1,2,128]{2,1,0:T(2,128)S(1)} %add_add_fusion.1), channel_id=1, source_target_pairs={{0,4},{2,6},{4,0},{6,2},{1,5},{3,7},{5,1},{7,3},{8,12},{10,14},{12... | collective-permute-start | bytes 3080 | tf_op jit(solution)/shard_map/ppermute | solution.py:500
  150.6 12.5 %collective-permute-start.52 = (s16[2,4,32,128]{3,2,1,0:T(8,128)(2,1)S(1)}, s16[2,4,32,128]{3,2,1,0:T(8,128)(2,1)S(1)}, u32[]{:S(2)}, u32[]{:S(2)}) collective-permute-start(s16[2,4,32,128]{3,2,1,0:T(8,128)(2,1)S(1)} %shard_map.134.refs_0_), channel_id=1, source_target_pairs={{0,8},{8,0},{16,24},{24,16},{1,9},{9,1},{17,25},{25,17},{2,10},{10... | collective-permute-start | bytes 196616 | tf_op jit(solution)/shard_map/ppermute | solution.py:571
  150.7 12.5 %collective-permute-start.53 = (s16[2,4,32,128]{3,2,1,0:T(8,128)(2,1)S(1)}, s16[2,4,32,128]{3,2,1,0:T(8,128)(2,1)S(1)}, u32[]{:S(2)}, u32[]{:S(2)}) collective-permute-start(s16[2,4,32,128]{3,2,1,0:T(8,128)(2,1)S(1)} %shard_map.134.refs_0_), channel_id=1, source_target_pairs={{0,16},{8,24},{16,0},{24,8},{1,17},{9,25},{17,1},{25,9},{2,18},{10... | collective-permute-start | bytes 196616 | tf_op jit(solution)/shard_map/ppermute | solution.py:571
  151.9 11.3 %collective-permute-start.54 = (s16[2,4,32,128]{3,2,1,0:T(8,128)(2,1)S(1)}, s16[2,4,32,128]{3,2,1,0:T(8,128)(2,1)S(1)}, u32[]{:S(2)}, u32[]{:S(2)}) collective-permute-start(s16[2,4,32,128]{3,2,1,0:T(8,128)(2,1)S(1)} %shard_map.134.refs_0_), channel_id=1, source_target_pairs={{0,24},{8,16},{16,8},{24,0},{1,25},{9,17},{17,9},{25,1},{2,26},{10... | collective-permute-start | bytes 196616 | tf_op jit(solution)/shard_map/ppermute | solution.py:571
  154.3 7.0 %collective-permute-start.48 = (f32[1,2,128]{2,1,0:T(2,128)S(1)}, f32[1,2,128]{2,1,0:T(2,128)S(1)}, u32[]{:S(2)}, u32[]{:S(2)}) collective-permute-start(f32[1,2,128]{2,1,0:T(2,128)S(1)} %add_add_fusion), channel_id=1, source_target_pairs={{0,1},{1,0},{2,3},{3,2},{4,5},{5,4},{6,7},{7,6},{8,9},{9,8},{10,11... | collective-permute-start | bytes 3080 | tf_op jit(solution)/shard_map/ppermute | solution.py:500
  163.8 6.7 %collective-permute-start.55 = (s16[2,16,32,128]{3,2,1,0:T(8,128)(2,1)S(1)}, s16[2,16,32,128]{3,2,1,0:T(8,128)(2,1)S(1)}, u32[]{:S(2)}, u32[]{:S(2)}) collective-permute-start(s16[2,16,32,128]{3,2,1,0:T(8,128)(2,1)S(1)} %bitcast.27), channel_id=1, source_target_pairs={{0,2},{2,0},{4,6},{6,4},{1,3},{3,1},{5,7},{7,5},{8,10},{10,8},{12,... | collective-permute-start | bytes 786440 | tf_op jit(solution)/shard_map/ppermute | solution.py:571
  164.1 7.0 %collective-permute-start.56 = (s16[2,16,32,128]{3,2,1,0:T(8,128)(2,1)S(1)}, s16[2,16,32,128]{3,2,1,0:T(8,128)(2,1)S(1)}, u32[]{:S(2)}, u32[]{:S(2)}) collective-permute-start(s16[2,16,32,128]{3,2,1,0:T(8,128)(2,1)S(1)} %bitcast.28), channel_id=1, source_target_pairs={{0,4},{2,6},{4,0},{6,2},{1,5},{3,7},{5,1},{7,3},{8,12},{10,14},{12... | collective-permute-start | bytes 786440 | tf_op jit(solution)/shard_map/ppermute | solution.py:571
  165.7 11.4 %collective-permute-start.57 = (s16[2,16,32,128]{3,2,1,0:T(8,128)(2,1)S(1)}, s16[2,16,32,128]{3,2,1,0:T(8,128)(2,1)S(1)}, u32[]{:S(2)}, u32[]{:S(2)}) collective-permute-start(s16[2,16,32,128]{3,2,1,0:T(8,128)(2,1)S(1)} %bitcast.29), channel_id=1, source_target_pairs={{0,6},{2,4},{4,2},{6,0},{1,7},{3,5},{5,3},{7,1},{8,14},{10,12},{12... | collective-permute-start | bytes 786440 | tf_op jit(solution)/shard_map/ppermute | solution.py:571
  (35 other events, 172.6 us)

commit v12 on v7

--- a/solution.py
+++ b/solution.py
@@ -116,8 +116,8 @@
     put_rows(st_ref, *local_stats(planes, float(GROUP * rows * frames * cols)))
 
 
-def rows_kernel(above_ref, below_ref, *outs):
-    for which, out in enumerate(outs):
+def rows_kernel(above_ref, below_ref, *refs):
+    for which, out in enumerate(refs[-above_ref.shape[0] :]):
         out[0] = above_ref[which]
         out[1] = below_ref[which]
 
@@ -273,7 +273,7 @@
 
 
 def hidden_grad_kernel(
-    hidden, scaled, par_ref, st_ref, sums_ref, after, out_ref, down_ref, up_ref, *, count
+    hidden, scaled, par_ref, st_ref, sums_ref, out_ref, down_ref, up_ref, *, count
 ):
     rows, frames, channels, cols = hidden.shape
     mean, inverse, _, _, _ = norm_columns(par_ref, st_ref, count, 3)
@@ -404,10 +404,10 @@
 
 
 def first_grad_kernel(flag_ref, *refs, count):
-    weight, latent, par_ref, st_ref, scaled_ref, sums_ref, stack_ref = refs[-7:]
+    weight, latent, par_ref, st_ref, _, scaled_ref, sums_ref, stack_ref = refs[-8:]
     rows, frames, channels, cols = latent.shape
     mean, inverse, gain, shift, scale = norm_columns(par_ref, st_ref, count, 1)
-    fill_future(stack_ref, flag_ref, *refs[:-7])
+    fill_future(stack_ref, flag_ref, *refs[:-8])
     first = jnp.zeros((channels, 128), F32)
     second = jnp.zeros((channels, 128), F32)
     for row in range(rows):
@@ -498,17 +498,38 @@
     return parts[0]
 
 
-def all_sum(value):
+def sum_kernel(*refs, parts):
+    refs[-1][...] = pairwise([ref[...] for ref in refs[:parts]], lambda a, b: a + b)
+
+
+def stats_kernel(*refs, parts, count):
+    refs[-1][...] = pairwise([(ref[...], count) for ref in refs[:parts]], joined_stats)[0]
+
+
+def all_sum(value, after=()):
     for axis, _, exchanges in rounds(("tm", "height", "width")):
         parts = [value] + [lax.ppermute(value, axis, pairs) for pairs in exchanges]
-        value = pairwise(parts, lambda a, b: a + b)
+        if after:
+            value = joined_after(functools.partial(sum_kernel, parts=len(parts)), parts, after)
+        else:
+            value = pairwise(parts, lambda a, b: a + b)
+        after = ()
     return value
 
 
-def all_stats(value, count):
+def joined_after(body, parts, after):
+    (value,) = call(body, [shape(parts[0].shape, F32)], [VMEM] * (len(parts) + len(after)), (*parts, *after))
+    return value
+
+
+def all_stats(value, count, after=()):
     for axis, _, exchanges in rounds(("tm", "height", "width")):
-        parts = [(value, count)] + [(lax.ppermute(value, axis, pairs), count) for pairs in exchanges]
-        value, count = pairwise(parts, joined_stats)
+        parts = [value] + [lax.ppermute(value, axis, pairs) for pairs in exchanges]
+        if after:
+            value = joined_after(functools.partial(stats_kernel, parts=len(parts), count=count), parts, after)
+        else:
+            value, _ = pairwise([(part, count) for part in parts], joined_stats)
+        count, after = count * len(parts), ()
     return value
 
 
@@ -557,7 +578,8 @@
         )
         after = ()
         received = [kept] + [lax.ppermute(v, axis, pairs) for v, pairs in zip(sent, exchanges)]
-    return received
+        last = sent[0]
+    return received, last
 
 
 def gathered(flags, received, after, after_last):
@@ -611,13 +633,14 @@
     return columns
 
 
-def row_halos(down, up):
+def row_halos(down, up, after=()):
     above, below = shifted(down, "height", 1), shifted(up, "height", -1)
-    return call(rows_kernel, [shape((2, *down.shape[1:]), BF16)] * down.shape[0], [VMEM] * 2, (above, below))
-
-
-def halo(own, near, steps):
-    return shifted(own, "tm", steps), near, shifted(near, "tm", steps)
+    return call(
+        rows_kernel,
+        [shape((2, *down.shape[1:]), BF16)] * down.shape[0],
+        [VMEM] * (2 + len(after)),
+        (above, below, *after),
+    )
 
 
 def with_columns(flags, own, around, after=()):
@@ -672,8 +695,8 @@
         (latent, cotangent, par),
     )
     near, near_c = row_halos(down, up)
-    around = with_columns(flags, latent, halo(latent, near, 1))
-    around_c = halo(cotangent, near_c, -1)
+    around = with_columns(flags, latent, (shifted(latent, "tm", 1), near, shifted(near, "tm", 1)))
+    around_c = (shifted(cotangent, "tm", -1), near_c, shifted(near_c, "tm", -1))
     stats_first = all_stats(stats_first, count / devices)
     (weight_first,) = call(weight_forward_kernel, [shape(taps, BF16)], [VMEM], (conv_first,))
     (weight_second_t,) = call(weight_back_kernel, [shape(taps, BF16)], [VMEM], (conv_second,))
@@ -683,12 +706,11 @@
         functools.partial(conv_first_kernel, count=count),
         [shape(block, F32), small, shape(stack, BF16)],
         [SMEM] + [VMEM] * 10,
-        (flags, latent, *around, par, stats_first, weight_first, around_c[0]),
+        (flags, latent, *around, par, stats_first, weight_first, around_c[2]),
         flops=conv_flops,
         transcendentals=3 * latent.size,
     )
     around_c = with_columns(flags, cotangent, around_c, (stats_second,))
-    stats_second = all_stats(stats_second, count / devices)
     grad_second, stack_c = call(
         conv_back_kernel,
         [shape(block, F32), shape(stack, BF16)],
@@ -696,6 +718,7 @@
         (flags, cotangent, *around_c, weight_second_t),
         flops=conv_flops,
     )
+    stats_second = all_stats(stats_second, count / devices, (grad_second,))
     act_second, scaled, sums = call(
         functools.partial(norm_second_kernel, count=count),
         [shape(block, BF16), shape(block, F32), small],
@@ -703,7 +726,6 @@
         (hidden, grad_second, par, stats_second),
         transcendentals=latent.size,
     )
-    sums = all_sum(sums)
     halves_second = call(
         weight_second_kernel,
         halves,
@@ -712,15 +734,17 @@
         scratch=[pltpu.VMEM((rows * cols, frames * channels), BF16)],
         flops=conv_flops,
     )
+    sums = all_sum(sums, (halves_second[0],))
     message = shape((1, frames, channels, cols), BF16)
     hidden_grad, down, up = call(
         functools.partial(hidden_grad_kernel, count=count),
         [shape(block, BF16), message, message],
-        [VMEM] * 6,
-        (hidden, scaled, par, stats_second, sums, halves_second[0]),
-    )
-    (near,) = row_halos(down, up)
-    around = halo(hidden_grad, near, -1)
+        [VMEM] * 5,
+        (hidden, scaled, par, stats_second, sums),
+    )
+    future = shifted(hidden_grad, "tm", -1)
+    (near,) = row_halos(down, up, (future,))
+    around = (future, near, shifted(near, "tm", -1))
     halves_first = call(
         weight_first_kernel,
         halves,
@@ -734,16 +758,16 @@
     )
     weights, sent = scattered(flags, halves_second, halves_first)
     around = with_columns(flags, hidden_grad, around, (sent,))
+    weights, sent = summed(flags, weights, around[:2])
     scaled, sums_first = call(
         functools.partial(first_grad_kernel, count=count),
         [shape(block, F32), small],
-        [SMEM] + [VMEM] * 10,
-        (flags, hidden_grad, *around, weight_first_t, latent, par, stats_first),
+        [SMEM] + [VMEM] * 11,
+        (flags, hidden_grad, *around, weight_first_t, latent, par, stats_first, sent),
         scratch=[pltpu.VMEM(stack, BF16)],
         flops=conv_flops,
         transcendentals=latent.size,
     )
-    weights = summed(flags, weights, around[:2])
     sums_first = all_sum(sums_first)
     decoded_grad, token = call(
         functools.partial(decoded_grad_kernel, count=count),
@@ -751,7 +775,7 @@
         [VMEM] * 6,
         (scaled, latent, cotangent, par, stats_first, sums_first),
     )
-    second, first = gathered(flags, weights, (sums_first,), token)
+    second, first = gathered(flags, weights, (), token)
     conv_second_grad = joined(flags, second, swapped(second))
     conv_first_grad = joined(flags, first, swapped(first))
     return decoded_grad, conv_first_grad, conv_second_grad

time: 192 us -> 181 us (0.943)
  starting transfers between devices: 101 us -> 95.1 us
  waiting for transfers between devices: 32.8 us -> 28.9 us
    ppermute x10, starting transfers between devices: 20.6 us -> 14 us  [swapped(): return lax.ppermute(value, 'width', [(0, 1), (1, 0)])]
    ppermute x14, waiting for transfers between devices: 8.24 us -> 3.8 us  [all_sum(): parts = [value] + [lax.ppermute(value, axis, pairs) for pairs in exchanges]]
    ppermute x3, waiting for transfers between devices: 0.01 us -> 2.73 us  [scattered(): lax.ppermute(v, axis, pairs)]
    ppermute x10, waiting for transfers between devices: 2.3 us -> 0.03 us  [swapped(): return lax.ppermute(value, 'width', [(0, 1), (1, 0)])]
    ppermute x14, waiting for transfers between devices: 6.83 us -> 4.82 us  [all_stats(): parts = [value] + [lax.ppermute(value, axis, pairs) for pairs in exchanges]]
    pallas_call x28 -> x30, Pallas kernels: 50.7 us -> 49.6 us  [call(): pl.pallas_call(body, out_shape=tuple(outs), in_specs=specs, out_specs=tup...]
  transfers between devices with their start and end apart: 63 -> 63, of which waited for: 20 -> 18; matrix products, arithmetic and copies ran while one was open for 0% -> 0% of each run, Pallas kernels for 17% -> 21%
where the time goes in v12:
time: 181 us
  starting transfers between devices  95.1 us (53%)
  Pallas kernels  49.6 us (27%)
  waiting for transfers between devices  28.9 us (16%)
  local copies, waits for them, and re-layouts  4.96 us (3%)
    pallas_call x30, Pallas kernels, call(): pl.pallas_call(body, out_shape=tuple(outs), in_specs=specs, out_specs=tup...  49.6 us
    ppermute x14, starting transfers between devices, all_stats(): parts = [value] + [lax.ppermute(value, axis, pairs) for pairs in exchanges]  23.5 us
    ppermute x14, starting transfers between devices, all_sum(): parts = [value] + [lax.ppermute(value, axis, pairs) for pairs in exchanges]  21.4 us
    ppermute x10, starting transfers between devices, shifted(): lax.ppermute(value, axis, [(source, source + steps) for source in range(i...  20.7 us
    ppermute x10, waiting for transfers between devices, shifted(): lax.ppermute(value, axis, [(source, source + steps) for source in range(i...  14.1 us
    ppermute x10, starting transfers between devices, swapped(): return lax.ppermute(value, 'width', [(0, 1), (1, 0)])  14 us
    ppermute x6, starting transfers between devices, gathered(): pieces = [value] + [lax.ppermute(value, axis, pairs) for pairs in exchanges]  5.36 us
    ppermute x14, waiting for transfers between devices, all_stats(): parts = [value] + [lax.ppermute(value, axis, pairs) for pairs in exchanges]  4.82 us
  transfers between devices with their start and end apart: 63, of which 18 were waited for; matrix products, arithmetic and copies ran while one was open for 0% of the time, Pallas kernels for 21%

profile of v12, /device:TPU:1, one launch (start us, length us, event | category | flops | bytes accessed | tf_op | source)
XLA Modules:
  0.0 180.5 jit_solution(17684446476823641912)
XLA Ops:
  4.3 2.6 %shard_map.112 = (bf16[4,2,128,256]{3,2,1,0:T(8,128)(2,1)S(1)}, bf16[4,2,128,256]{3,2,1,0:T(8,128)(2,1)S(1)}, bf16[2,2,128,256]{3,2,1,0:T(8,128)(2,1)S(1)}, bf16...) custom-call(bf16[128,2,4,256]{3,2,1,0:T(4,128)(2,1)S(1)} %copy-done.3, bf16[128,2,4,256]{3,2,1,0:T(4,128)(2,1)S(1)} %copy-done.4, ...), custom_call_target="tpu_custom_call" | custom-call | bytes 2626560 | tf_op jit(solution)/shard_map/pallas_call | solution.py:24
  7.0 2.2 %collective-permute-start.6 = (f32[1,2,128]{2,1,0:T(2,128)S(1)}, f32[1,2,128]{2,1,0:T(2,128)S(1)}, u32[]{:S(2)}, u32[]{:S(2)}) collective-permute-start(f32[1,2,128]{2,1,0:T(2,128)S(1)} %get-tuple-element.43), channel_id=1, source_target_pairs={{0,8},{8,0},{16,24},{24,16},{1,9},{9,1},{17,25},{25,17},{2,10},{10... | collective-permute-start | bytes 3080 | tf_op jit(solution)/shard_map/ppermute | solution.py:527
  9.2 2.3 %collective-permute-start.7 = (f32[1,2,128]{2,1,0:T(2,128)S(1)}, f32[1,2,128]{2,1,0:T(2,128)S(1)}, u32[]{:S(2)}, u32[]{:S(2)}) collective-permute-start(f32[1,2,128]{2,1,0:T(2,128)S(1)} %get-tuple-element.43), channel_id=1, source_target_pairs={{0,16},{8,24},{16,0},{24,8},{1,17},{9,25},{17,1},{25,9},{2,18},{10... | collective-permute-start | bytes 3080 | tf_op jit(solution)/shard_map/ppermute | solution.py:527
  11.5 3.1 %collective-permute-start.1 = (bf16[2,2,128,256]{3,2,1,0:T(8,128)(2,1)S(1)}, bf16[2,2,128,256]{3,2,1,0:T(8,128)(2,1)S(1)}, u32[]{:S(2)}, u32[]{:S(2)}) collective-permute-start(bf16[2,2,128,256]{3,2,1,0:T(8,128)(2,1)S(1)} %get-tuple-element.40), channel_id=1, source_target_pairs={{0,2},{2,4},{4,6},{1,3},{3,5},{5,7},{8,10},{10,12},{12,14},{9,11},... | collective-permute-start | bytes 786440 | tf_op jit(solution)/shard_map/ppermute | solution.py:482
  16.0 3.1 %collective-permute-start.10 = (f32[1,2,128]{2,1,0:T(2,128)S(1)}, f32[1,2,128]{2,1,0:T(2,128)S(1)}, u32[]{:S(2)}, u32[]{:S(2)}) collective-permute-start(f32[1,2,128]{2,1,0:T(2,128)S(1)} %pad_maximum_fusion), channel_id=1, source_target_pairs={{0,4},{2,6},{4,0},{6,2},{1,5},{3,7},{5,1},{7,3},{8,12},{10,14},{12... | collective-permute-start | bytes 3080 | tf_op jit(solution)/shard_map/ppermute | solution.py:527
  20.3 3.0 %collective-permute-start = (bf16[4,2,128,256]{3,2,1,0:T(8,128)(2,1)S(1)}, bf16[4,2,128,256]{3,2,1,0:T(8,128)(2,1)}, u32[]{:S(2)}, u32[]{:S(2)}) collective-permute-start(bf16[4,2,128,256]{3,2,1,0:T(8,128)(2,1)S(1)} %get-tuple-element.39.first_ref.own.refs_7_.latent), channel_id=1, source_target_pairs={{0,8},{8,16},{16,24},{1,9},{9,17},{17,25},{2,10},{10,18},{18,26},{... | collective-permute-start | bytes 1572872 | tf_op jit(solution)/shard_map/ppermute | solution.py:482
  27.8 3.0 %collective-permute-start.3 = (bf16[2,2,128,256]{3,2,1,0:T(8,128)(2,1)}, bf16[2,2,128,256]{3,2,1,0:T(8,128)(2,1)}, u32[]{:S(2)}, u32[]{:S(2)}) collective-permute-start(bf16[2,2,128,256]{3,2,1,0:T(8,128)(2,1)} %get-tuple-element.42.first_ref.near), channel_id=1, source_target_pairs={{0,8},{8,16},{16,24},{1,9},{9,17},{17,25},{2,10},{10,18},{18,26},{... | collective-permute-start | bytes 786440 | tf_op jit(solution)/shard_map/ppermute | solution.py:482
  30.8 3.5 %collective-permute-start.12 = (f32[1,2,128]{2,1,0:T(2,128)S(1)}, f32[1,2,128]{2,1,0:T(2,128)S(1)}, u32[]{:S(2)}, u32[]{:S(2)}) collective-permute-start(f32[1,2,128]{2,1,0:T(2,128)S(1)} %pad_maximum_fusion.1), channel_id=1, source_target_pairs={{0,1},{1,0},{2,3},{3,2},{4,5},{5,4},{6,7},{7,6},{8,9},{9,8},{10,11... | collective-permute-start | bytes 3080 | tf_op jit(solution)/shard_map/ppermute | solution.py:527
  38.7 3.1 %collective-permute-start.5 = (bf16[128,128]{1,0:T(8,128)(2,1)S(1)}, bf16[128,128]{1,0:T(8,128)(2,1)S(1)}, u32[]{:S(2)}, u32[]{:S(2)}) collective-permute-start(bf16[128,128]{1,0:T(8,128)(2,1)S(1)} %shard_map.115), channel_id=1, source_target_pairs={{0,1},{1,0},{2,3},{3,2},{4,5},{5,4},{6,7},{7,6},{8,9},{9,8},{10,11... | collective-permute-start | bytes 98312 | tf_op jit(solution)/shard_map/ppermute | solution.py:544
  41.8 2.0 %shard_map.114 = bf16[128,128]{1,0:T(8,128)(2,1)S(1)} custom-call(s32[6]{0:T(128)S(1)} %stack.57.flag_ref, bf16[4,2,128,256]{3,2,1,0:T(8,128)(2,1)S(1)} %get-tuple-element.39.first_ref.own.refs_7_.latent, bf16[4,2,128,256]{3,2,1,0:T(8,128)(2,1)} %collective-permute-done.second_ref.past), custom_call_target="tpu_custom_call" | custom-call | bytes 1081368 | tf_op jit(solution)/shard_map/pallas_call | solution.py:24
  45.8 5.2 %shard_map.117 = (f32[4,2,128,256]{3,2,1,0:T(8,128)S(1)}, f32[1,2,128]{2,1,0:T(2,128)S(1)}, bf16[6,4,384,256]{3,2,1,0:T(8,128)(2,1)S(1)}) custom-call(s32[6]{0:T(128)S(1)} %stack.57.flag_ref, bf16[4,2,128,256]{3,2,1,0:T(8,128)(2,1)S(1)} %get-tuple-element.39.first_ref.own.refs_7_.latent, bf16[4,2,128,256]{3,2,1,0:T(8,128)(2,1)} %collective-permute-done.second_ref.past, ...), custom_call_target="tpu_custom_call" | custom-call | flops 7247757312 | bytes 10033176 | tf_op jit(solution)/shard_map/pallas_call | solution.py:24
  52.8 2.0 %shard_map.118 = bf16[128,128]{1,0:T(8,128)(2,1)S(1)} custom-call(s32[6]{0:T(128)S(1)} %stack.57.flag_ref, bf16[4,2,128,256]{3,2,1,0:T(8,128)(2,1)S(1)} %get-tuple-element.46.first_ref.refs_0_.cotangent, bf16[4,2,128,256]{3,2,1,0:T(8,128)(2,1)} %collective-permute-done.14.second_ref.refs_1_, f32[1,2,128]{2,1,0:T(2,128)S(1)} %get-tuple-element.47.refs_0_), custom_call_target="tpu_custom_call" | custom-call | bytes 1082392 | tf_op jit(solution)/shard_map/pallas_call | solution.py:24
  56.8 3.0 %collective-permute-start.18 = (f32[1,2,128]{2,1,0:T(2,128)S(1)}, f32[1,2,128]{2,1,0:T(2,128)S(1)}, u32[]{:S(2)}, u32[]{:S(2)}) collective-permute-start(f32[1,2,128]{2,1,0:T(2,128)S(1)} %get-tuple-element.47.refs_0_), channel_id=1, source_target_pairs={{0,16},{8,24},{16,0},{24,8},{1,17},{9,25},{17,1},{25,9},{2,18},{10... | collective-permute-start | bytes 3080 | tf_op jit(solution)/shard_map/ppermute | solution.py:527
  59.8 3.9 %shard_map.121 = (f32[4,2,128,256]{3,2,1,0:T(8,128)S(1)}, bf16[6,4,384,256]{3,2,1,0:T(8,128)(2,1)S(1)}) custom-call(s32[6]{0:T(128)S(1)} %stack.57.flag_ref, bf16[4,2,128,256]{3,2,1,0:T(8,128)(2,1)S(1)} %get-tuple-element.46.first_ref.refs_0_.cotangent, bf16[4,2,128,256]{3,2,1,0:T(8,128)(2,1)} %collective-permute-done.14.second_ref.refs_1_, ...), custom_call_target="tpu_custom_call" | custom-call | flops 7247757312 | bytes 9764888 | tf_op jit(solution)/shard_map/pallas_call | solution.py:24
  64.0 2.6 %collective-permute-start.20 = (f32[1,2,128]{2,1,0:T(2,128)S(1)}, f32[1,2,128]{2,1,0:T(2,128)S(1)}, u32[]{:S(2)}, u32[]{:S(2)}) collective-permute-start(f32[1,2,128]{2,1,0:T(2,128)S(1)} %shard_map.122), channel_id=1, source_target_pairs={{0,2},{2,0},{4,6},{6,4},{1,3},{3,1},{5,7},{7,5},{8,10},{10,8},{12,... | collective-permute-start | bytes 3080 | tf_op jit(solution)/shard_map/ppermute | solution.py:527
  70.0 2.9 %collective-permute-start.23 = (f32[1,2,128]{2,1,0:T(2,128)S(1)}, f32[1,2,128]{2,1,0:T(2,128)S(1)}, u32[]{:S(2)}, u32[]{:S(2)}) collective-permute-start(f32[1,2,128]{2,1,0:T(2,128)S(1)} %pad_maximum_fusion.3), channel_id=1, source_target_pairs={{0,1},{1,0},{2,3},{3,2},{4,5},{5,4},{6,7},{7,6},{8,9},{9,8},{10,11... | collective-permute-start | bytes 3080 | tf_op jit(solution)/shard_map/ppermute | solution.py:527
  74.7 2.4 %collective-permute-start.25 = (f32[1,2,128]{2,1,0:T(2,128)S(1)}, f32[1,2,128]{2,1,0:T(2,128)S(1)}, u32[]{:S(2)}, u32[]{:S(2)}) collective-permute-start(f32[1,2,128]{2,1,0:T(2,128)S(1)} %get-tuple-element.50.refs_0_), channel_id=1, source_target_pairs={{0,16},{8,24},{16,0},{24,8},{1,17},{9,25},{17,1},{25,9},{2,18},{10... | collective-permute-start | bytes 3080 | tf_op jit(solution)/shard_map/ppermute | solution.py:511
  78.2 4.3 %shard_map.124 = (f32[2048,128]{1,0:T(8,128)S(1)}, f32[2048,128]{1,0:T(8,128)S(1)}) custom-call(s32[6]{0:T(128)S(1)} %stack.57.flag_ref, bf16[6,4,384,256]{3,2,1,0:T(8,128)(2,1)S(1)} %get-tuple-element.51.stack_ref, bf16[4,2,128,256]{3,2,1,0:T(8,128)(2,1)S(1)} %get-tuple-element.52.act_ref), custom_call_target="tpu_custom_call" | custom-call | flops 7247757312 | bytes 7340056 | tf_op jit(solution)/shard_map/pallas_call | solution.py:24
  87.8 2.6 %collective-permute-start.30 = (f32[1,2,128]{2,1,0:T(2,128)S(1)}, f32[1,2,128]{2,1,0:T(2,128)S(1)}, u32[]{:S(2)}, u32[]{:S(2)}) collective-permute-start(f32[1,2,128]{2,1,0:T(2,128)S(1)} %add_add_fusion.2), channel_id=1, source_target_pairs={{0,1},{1,0},{2,3},{3,2},{4,5},{5,4},{6,7},{7,6},{8,9},{9,8},{10,11... | collective-permute-start | bytes 3080 | tf_op jit(solution)/shard_map/ppermute | solution.py:511
  91.7 4.1 %shard_map.128 = (f32[2048,128]{1,0:T(8,128)S(1)}, f32[2048,128]{1,0:T(8,128)S(1)}) custom-call(s32[6]{0:T(128)S(1)} %stack.57.flag_ref, bf16[6,4,384,256]{3,2,1,0:T(8,128)(2,1)S(1)} %get-tuple-element.58.stack_ref, bf16[4,2,128,256]{3,2,1,0:T(8,128)(2,1)S(1)} %get-tuple-element.54.grad_ref.first_ref.refs_0_), custom_call_target="tpu_custom_call" | custom-call | flops 7247757312 | bytes 7340056 | tf_op jit(solution)/shard_map/pallas_call | solution.py:24
  97.4 3.6 %collective-permute-start.32 = (bf16[1,2,128,256]{3,2,1,0:T(8,128)(2,1)S(1)}, bf16[1,2,128,256]{3,2,1,0:T(8,128)(2,1)S(1)}, u32[]{:S(2)}, u32[]{:S(2)}) collective-permute-start(bf16[1,2,128,256]{3,2,1,0:T(8,128)(2,1)S(1)} %get-tuple-element.55), channel_id=1, source_target_pairs={{0,2},{2,4},{4,6},{1,3},{3,5},{5,7},{8,10},{10,12},{12,14},{9,11},... | collective-permute-start | bytes 393224 | tf_op jit(solution)/shard_map/ppermute | solution.py:482
  103.7 4.8 %collective-permute-done.33.below_ref = bf16[1,2,128,256]{3,2,1,0:T(8,128)(2,1)S(1)} collective-permute-done((bf16[1,2,128,256]{3,2,1,0:T(8,128)(2,1)S(1)}, bf16[1,2,128,256]{3,2,1,0:T(8,128)(2,1)S(1)}, u32[]{:S(2)}, u32[]{:S(2)}) %collective-permute-start.33) | collective-permute-done | bytes 131104 | tf_op jit(solution)/shard_map/ppermute | solution.py:482
  108.5 2.9 %collective-permute-done.31.refs_0_.second_ref.refs_4_.refs_1_ = bf16[4,2,128,256]{3,2,1,0:T(8,128)(2,1)S(1)} collective-permute-done((bf16[4,2,128,256]{3,2,1,0:T(8,128)(2,1)S(1)}, bf16[4,2,128,256]{3,2,1,0:T(8,128)(2,1)S(1)}, u32[]{:S(2)}, u32[]{:S(2)}) %collective-permute-start.31) | collective-permute-done | bytes 524320 | tf_op jit(solution)/shard_map/ppermute | solution.py:482
  116.8 3.3 %collective-permute-done.34.second_ref.refs_3_ = bf16[2,2,128,256]{3,2,1,0:T(8,128)(2,1)S(1)} collective-permute-done((bf16[2,2,128,256]{3,2,1,0:T(8,128)(2,1)S(1)}, bf16[2,2,128,256]{3,2,1,0:T(8,128)(2,1)S(1)}, u32[]{:S(2)}, u32[]{:S(2)}) %collective-permute-start.34) | collective-permute-done | bytes 262176 | tf_op jit(solution)/shard_map/ppermute | solution.py:482
  125.0 2.7 %collective-permute-done.41 = s16[2,16,32,128]{3,2,1,0:T(8,128)(2,1)S(1)} collective-permute-done((s16[2,16,32,128]{3,2,1,0:T(8,128)(2,1)S(1)}, s16[2,16,32,128]{3,2,1,0:T(8,128)(2,1)S(1)}, u32[]{:S(2)}, u32[]{:S(2)}) %collective-permute-start.41) | collective-permute-done | bytes 262176 | tf_op jit(solution)/shard_map/ppermute | solution.py:564
  128.7 4.0 %shard_map.134 = (f32[4,2,128,256]{3,2,1,0:T(8,128)S(1)}, f32[1,2,128]{2,1,0:T(2,128)S(1)}) custom-call(s32[6]{0:T(128)S(1)} %stack.57.flag_ref, bf16[4,2,128,256]{3,2,1,0:T(8,128)(2,1)S(1)} %get-tuple-element.54.grad_ref.first_ref.refs_0_, bf16[4,2,128,256]{3,2,1,0:T(8,128)(2,1)S(1)} %collective-permute-done.31.refs_0_.second_ref.refs_4_.refs_1_, ...), custom_call_target="tpu_custom_call" | custom-call | flops 7247757312 | bytes 5642264 | tf_op jit(solution)/shard_map/pallas_call | solution.py:24
  145.7 2.1 %collective-permute-start.54 = (s16[2,4,32,128]{3,2,1,0:T(8,128)(2,1)S(1)}, s16[2,4,32,128]{3,2,1,0:T(8,128)(2,1)S(1)}, u32[]{:S(2)}, u32[]{:S(2)}) collective-permute-start(s16[2,4,32,128]{3,2,1,0:T(8,128)(2,1)S(1)} %shard_map.136.refs_0_), channel_id=1, source_target_pairs={{0,24},{8,16},{16,8},{24,0},{1,25},{9,17},{17,9},{25,1},{2,26},{10... | collective-permute-start | bytes 196616 | tf_op jit(solution)/shard_map/ppermute | solution.py:595
  147.8 5.5 %collective-permute-start.48 = (f32[1,2,128]{2,1,0:T(2,128)S(1)}, f32[1,2,128]{2,1,0:T(2,128)S(1)}, u32[]{:S(2)}, u32[]{:S(2)}) collective-permute-start(f32[1,2,128]{2,1,0:T(2,128)S(1)} %add_add_fusion), channel_id=1, source_target_pairs={{0,1},{1,0},{2,3},{3,2},{4,5},{5,4},{6,7},{7,6},{8,9},{9,8},{10,11... | collective-permute-start | bytes 3080 | tf_op jit(solution)/shard_map/ppermute | solution.py:511
  164.4 4.5 %collective-permute-start.62 = (s16[64,32,128]{2,1,0:T(8,128)(2,1)S(1)}, s16[64,32,128]{2,1,0:T(8,128)(2,1)S(1)}, u32[]{:S(2)}, u32[]{:S(2)}) collective-permute-start(s16[64,32,128]{2,1,0:T(8,128)(2,1)S(1)} %bitcast.25), channel_id=1, source_target_pairs={{0,1},{1,0},{2,3},{3,2},{4,5},{5,4},{6,7},{7,6},{8,9},{9,8},{10,11... | collective-permute-start | bytes 1572872 | tf_op jit(solution)/shard_map/ppermute | solution.py:544
  169.9 2.9 %collective-permute-start.58 = (s16[64,32,128]{2,1,0:T(8,128)(2,1)S(1)}, s16[64,32,128]{2,1,0:T(8,128)(2,1)S(1)}, u32[]{:S(2)}, u32[]{:S(2)}) collective-permute-start(s16[64,32,128]{2,1,0:T(8,128)(2,1)S(1)} %bitcast.27), channel_id=1, source_target_pairs={{0,1},{1,0},{2,3},{3,2},{4,5},{5,4},{6,7},{7,6},{8,9},{9,8},{10,11... | collective-permute-start | bytes 1572872 | tf_op jit(solution)/shard_map/ppermute | solution.py:544
  172.7 3.9 %shard_map.141 = f32[128,3456]{1,0:T(8,128)} custom-call(s32[6]{0:T(128)S(1)} %stack.57.flag_ref, s16[64,32,128]{2,1,0:T(8,128)(2,1)S(1)} %bitcast.26, s16[64,32,128]{2,1,0:T(8,128)(2,1)S(1)} %collective-permute-done.62.theirs_ref), custom_call_target="tpu_custom_call" | custom-call | bytes 2818072 | tf_op jit(solution)/shard_map/pallas_call | solution.py:24
  176.6 3.9 %shard_map.139 = f32[128,3456]{1,0:T(8,128)} custom-call(s32[6]{0:T(128)S(1)} %stack.57.flag_ref, s16[64,32,128]{2,1,0:T(8,128)(2,1)S(1)} %bitcast.28, s16[64,32,128]{2,1,0:T(8,128)(2,1)S(1)} %collective-permute-done.58.theirs_ref), custom_call_target="tpu_custom_call" | custom-call | bytes 2818072 | tf_op jit(solution)/shard_map/pallas_call | solution.py:24
  (160 shorter events, 74.3 us)
Async XLA Ops:
  7.0 8.9 %collective-permute-start.6 = (f32[1,2,128]{2,1,0:T(2,128)S(1)}, f32[1,2,128]{2,1,0:T(2,128)S(1)}, u32[]{:S(2)}, u32[]{:S(2)}) collective-permute-start(f32[1,2,128]{2,1,0:T(2,128)S(1)} %get-tuple-element.43), channel_id=1, source_target_pairs={{0,8},{8,0},{16,24},{24,16},{1,9},{9,1},{17,25},{25,17},{2,10},{10... | collective-permute-start | bytes 3080 | tf_op jit(solution)/shard_map/ppermute | solution.py:527
  11.5 14.9 %collective-permute-start.1 = (bf16[2,2,128,256]{3,2,1,0:T(8,128)(2,1)S(1)}, bf16[2,2,128,256]{3,2,1,0:T(8,128)(2,1)S(1)}, u32[]{:S(2)}, u32[]{:S(2)}) collective-permute-start(bf16[2,2,128,256]{3,2,1,0:T(8,128)(2,1)S(1)} %get-tuple-element.40), channel_id=1, source_target_pairs={{0,2},{2,4},{4,6},{1,3},{3,5},{5,7},{8,10},{10,12},{12,14},{9,11},... | collective-permute-start | bytes 786440 | tf_op jit(solution)/shard_map/ppermute | solution.py:482
  14.6 11.7 %collective-permute-start.2 = (bf16[2,2,128,256]{3,2,1,0:T(8,128)(2,1)S(1)}, bf16[2,2,128,256]{3,2,1,0:T(8,128)(2,1)S(1)}, u32[]{:S(2)}, u32[]{:S(2)}) collective-permute-start(bf16[2,2,128,256]{3,2,1,0:T(8,128)(2,1)S(1)} %get-tuple-element.41), channel_id=1, source_target_pairs={{2,0},{4,2},{6,4},{3,1},{5,3},{7,5},{10,8},{12,10},{14,12},{11,9},... | collective-permute-start | bytes 786440 | tf_op jit(solution)/shard_map/ppermute | solution.py:482
  19.3 7.0 %collective-permute-start.9 = (f32[1,2,128]{2,1,0:T(2,128)S(1)}, f32[1,2,128]{2,1,0:T(2,128)S(1)}, u32[]{:S(2)}, u32[]{:S(2)}) collective-permute-start(f32[1,2,128]{2,1,0:T(2,128)S(1)} %pad_maximum_fusion), channel_id=1, source_target_pairs={{0,2},{2,0},{4,6},{6,4},{1,3},{3,1},{5,7},{7,5},{8,10},{10,8},{12,... | collective-permute-start | bytes 3080 | tf_op jit(solution)/shard_map/ppermute | solution.py:527
  20.3 21.5 %collective-permute-start = (bf16[4,2,128,256]{3,2,1,0:T(8,128)(2,1)S(1)}, bf16[4,2,128,256]{3,2,1,0:T(8,128)(2,1)}, u32[]{:S(2)}, u32[]{:S(2)}) collective-permute-start(bf16[4,2,128,256]{3,2,1,0:T(8,128)(2,1)S(1)} %get-tuple-element.39.first_ref.own.refs_7_.latent), channel_id=1, source_target_pairs={{0,8},{8,16},{16,24},{1,9},{9,17},{17,25},{2,10},{10,18},{18,26},{... | collective-permute-start | bytes 1572872 | tf_op jit(solution)/shard_map/ppermute | solution.py:482
  23.4 29.5 %collective-permute-start.14 = (bf16[4,2,128,256]{3,2,1,0:T(8,128)(2,1)S(1)}, bf16[4,2,128,256]{3,2,1,0:T(8,128)(2,1)}, u32[]{:S(2)}, u32[]{:S(2)}) collective-permute-start(bf16[4,2,128,256]{3,2,1,0:T(8,128)(2,1)S(1)} %get-tuple-element.46.first_ref.refs_0_.cotangent), channel_id=1, source_target_pairs={{8,0},{16,8},{24,16},{9,1},{17,9},{25,17},{10,2},{18,10},{26,18},{... | collective-permute-start | bytes 1572872 | tf_op jit(solution)/shard_map/ppermute | solution.py:482
  27.8 9.5 %collective-permute-start.3 = (bf16[2,2,128,256]{3,2,1,0:T(8,128)(2,1)}, bf16[2,2,128,256]{3,2,1,0:T(8,128)(2,1)}, u32[]{:S(2)}, u32[]{:S(2)}) collective-permute-start(bf16[2,2,128,256]{3,2,1,0:T(8,128)(2,1)} %get-tuple-element.42.first_ref.near), channel_id=1, source_target_pairs={{0,8},{8,16},{16,24},{1,9},{9,17},{17,25},{2,10},{10,18},{18,26},{... | collective-permute-start | bytes 786440 | tf_op jit(solution)/shard_map/ppermute | solution.py:482
  35.8 10.0 %collective-permute-start.13 = (bf16[2,2,128,256]{3,2,1,0:T(8,128)(2,1)}, bf16[2,2,128,256]{3,2,1,0:T(8,128)(2,1)S(1)}, u32[]{:S(2)}, u32[]{:S(2)}) collective-permute-start(bf16[2,2,128,256]{3,2,1,0:T(8,128)(2,1)} %copy-done.5), channel_id=1, source_target_pairs={{8,0},{16,8},{24,16},{9,1},{17,9},{25,17},{10,2},{18,10},{26,18},{... | collective-permute-start | bytes 786440 | tf_op jit(solution)/shard_map/ppermute | solution.py:482
  38.7 7.1 %collective-permute-start.5 = (bf16[128,128]{1,0:T(8,128)(2,1)S(1)}, bf16[128,128]{1,0:T(8,128)(2,1)S(1)}, u32[]{:S(2)}, u32[]{:S(2)}) collective-permute-start(bf16[128,128]{1,0:T(8,128)(2,1)S(1)} %shard_map.115), channel_id=1, source_target_pairs={{0,1},{1,0},{2,3},{3,2},{4,5},{5,4},{6,7},{7,6},{8,9},{9,8},{10,11... | collective-permute-start | bytes 98312 | tf_op jit(solution)/shard_map/ppermute | solution.py:544
  52.0 7.8 %collective-permute-start.16 = (bf16[128,128]{1,0:T(8,128)(2,1)S(1)}, bf16[128,128]{1,0:T(8,128)(2,1)S(1)}, u32[]{:S(2)}, u32[]{:S(2)}) collective-permute-start(bf16[128,128]{1,0:T(8,128)(2,1)S(1)} %shard_map.119), channel_id=1, source_target_pairs={{0,1},{1,0},{2,3},{3,2},{4,5},{5,4},{6,7},{7,6},{8,9},{9,8},{10,11... | collective-permute-start | bytes 98312 | tf_op jit(solution)/shard_map/ppermute | solution.py:544
  55.3 8.4 %collective-permute-start.17 = (f32[1,2,128]{2,1,0:T(2,128)S(1)}, f32[1,2,128]{2,1,0:T(2,128)S(1)}, u32[]{:S(2)}, u32[]{:S(2)}) collective-permute-start(f32[1,2,128]{2,1,0:T(2,128)S(1)} %get-tuple-element.47.refs_0_), channel_id=1, source_target_pairs={{0,8},{8,0},{16,24},{24,16},{1,9},{9,1},{17,25},{25,17},{2,10},{10... | collective-permute-start | bytes 3080 | tf_op jit(solution)/shard_map/ppermute | solution.py:527
  56.8 7.0 %collective-permute-start.18 = (f32[1,2,128]{2,1,0:T(2,128)S(1)}, f32[1,2,128]{2,1,0:T(2,128)S(1)}, u32[]{:S(2)}, u32[]{:S(2)}) collective-permute-start(f32[1,2,128]{2,1,0:T(2,128)S(1)} %get-tuple-element.47.refs_0_), channel_id=1, source_target_pairs={{0,16},{8,24},{16,0},{24,8},{1,17},{9,25},{17,1},{25,9},{2,18},{10... | collective-permute-start | bytes 3080 | tf_op jit(solution)/shard_map/ppermute | solution.py:527
  74.6 7.9 %collective-permute-start.24 = (f32[1,2,128]{2,1,0:T(2,128)S(1)}, f32[1,2,128]{2,1,0:T(2,128)S(1)}, u32[]{:S(2)}, u32[]{:S(2)}) collective-permute-start(f32[1,2,128]{2,1,0:T(2,128)S(1)} %get-tuple-element.50.refs_0_), channel_id=1, source_target_pairs={{0,8},{8,0},{16,24},{24,16},{1,9},{9,1},{17,25},{25,17},{2,10},{10... | collective-permute-start | bytes 3080 | tf_op jit(solution)/shard_map/ppermute | solution.py:511
  74.7 7.9 %collective-permute-start.25 = (f32[1,2,128]{2,1,0:T(2,128)S(1)}, f32[1,2,128]{2,1,0:T(2,128)S(1)}, u32[]{:S(2)}, u32[]{:S(2)}) collective-permute-start(f32[1,2,128]{2,1,0:T(2,128)S(1)} %get-tuple-element.50.refs_0_), channel_id=1, source_target_pairs={{0,16},{8,24},{16,0},{24,8},{1,17},{9,25},{17,1},{25,9},{2,18},{10... | collective-permute-start | bytes 3080 | tf_op jit(solution)/shard_map/ppermute | solution.py:511
  90.4 22.3 %collective-permute-start.35 = (f32[64,32,128]{2,1,0:T(8,128)S(1)}, f32[64,32,128]{2,1,0:T(8,128)S(1)}, u32[]{:S(2)}, u32[]{:S(2)}) collective-permute-start(f32[64,32,128]{2,1,0:T(8,128)S(1)} %bitcast.44), channel_id=1, source_target_pairs={{0,1},{1,0},{2,3},{3,2},{4,5},{5,4},{6,7},{7,6},{8,9},{9,8},{10,11... | collective-permute-start | bytes 3145736 | tf_op jit(solution)/shard_map/ppermute | solution.py:544
  95.8 16.9 %collective-permute-start.36 = (f32[64,32,128]{2,1,0:T(8,128)S(1)}, f32[64,32,128]{2,1,0:T(8,128)S(1)}, u32[]{:S(2)}, u32[]{:S(2)}) collective-permute-start(f32[64,32,128]{2,1,0:T(8,128)S(1)} %bitcast.45), channel_id=1, source_target_pairs={{0,1},{1,0},{2,3},{3,2},{4,5},{5,4},{6,7},{7,6},{8,9},{9,8},{10,11... | collective-permute-start | bytes 3145736 | tf_op jit(solution)/shard_map/ppermute | solution.py:544
  96.1 15.2 %collective-permute-start.31 = (bf16[4,2,128,256]{3,2,1,0:T(8,128)(2,1)S(1)}, bf16[4,2,128,256]{3,2,1,0:T(8,128)(2,1)S(1)}, u32[]{:S(2)}, u32[]{:S(2)}) collective-permute-start(bf16[4,2,128,256]{3,2,1,0:T(8,128)(2,1)S(1)} %get-tuple-element.54.grad_ref.first_ref.refs_0_), channel_id=1, source_target_pairs={{8,0},{16,8},{24,16},{9,1},{17,9},{25,17},{10,2},{18,10},{26,18},{... | collective-permute-start | bytes 1572872 | tf_op jit(solution)/shard_map/ppermute | solution.py:482
  101.0 7.5 %collective-permute-start.33 = (bf16[1,2,128,256]{3,2,1,0:T(8,128)(2,1)S(1)}, bf16[1,2,128,256]{3,2,1,0:T(8,128)(2,1)S(1)}, u32[]{:S(2)}, u32[]{:S(2)}) collective-permute-start(bf16[1,2,128,256]{3,2,1,0:T(8,128)(2,1)S(1)} %get-tuple-element.56), channel_id=1, source_target_pairs={{2,0},{4,2},{6,4},{3,1},{5,3},{7,5},{10,8},{12,10},{14,12},{11,9},... | collective-permute-start | bytes 393224 | tf_op jit(solution)/shard_map/ppermute | solution.py:482
  111.4 8.7 %collective-permute-start.34 = (bf16[2,2,128,256]{3,2,1,0:T(8,128)(2,1)S(1)}, bf16[2,2,128,256]{3,2,1,0:T(8,128)(2,1)S(1)}, u32[]{:S(2)}, u32[]{:S(2)}) collective-permute-start(bf16[2,2,128,256]{3,2,1,0:T(8,128)(2,1)S(1)} %shard_map.127.first_ref.refs_5_.refs_2_), channel_id=1, source_target_pairs={{8,0},{16,8},{24,16},{9,1},{17,9},{25,17},{10,2},{18,10},{26,18},{... | collective-permute-start | bytes 786440 | tf_op jit(solution)/shard_map/ppermute | solution.py:482
  113.8 11.1 %collective-permute-start.39 = (s16[2,16,32,128]{3,2,1,0:T(8,128)(2,1)S(1)}, s16[2,16,32,128]{3,2,1,0:T(8,128)(2,1)S(1)}, u32[]{:S(2)}, u32[]{:S(2)}) collective-permute-start(s16[2,16,32,128]{3,2,1,0:T(8,128)(2,1)S(1)} %get-tuple-element.61.refs_0_), channel_id=1, source_target_pairs={{0,2},{2,0},{4,6},{6,4},{1,3},{3,1},{5,7},{7,5},{8,10},{10,8},{12,... | collective-permute-start | bytes 786440 | tf_op jit(solution)/shard_map/ppermute | solution.py:564
  115.6 9.4 %collective-permute-start.40 = (s16[2,16,32,128]{3,2,1,0:T(8,128)(2,1)S(1)}, s16[2,16,32,128]{3,2,1,0:T(8,128)(2,1)S(1)}, u32[]{:S(2)}, u32[]{:S(2)}) collective-permute-start(s16[2,16,32,128]{3,2,1,0:T(8,128)(2,1)S(1)} %get-tuple-element.63), channel_id=1, source_target_pairs={{0,4},{2,6},{4,0},{6,2},{1,5},{3,7},{5,1},{7,3},{8,12},{10,14},{12... | collective-permute-start | bytes 786440 | tf_op jit(solution)/shard_map/ppermute | solution.py:564
  115.6 12.1 %collective-permute-start.41 = (s16[2,16,32,128]{3,2,1,0:T(8,128)(2,1)S(1)}, s16[2,16,32,128]{3,2,1,0:T(8,128)(2,1)S(1)}, u32[]{:S(2)}, u32[]{:S(2)}) collective-permute-start(s16[2,16,32,128]{3,2,1,0:T(8,128)(2,1)S(1)} %get-tuple-element.64), channel_id=1, source_target_pairs={{0,6},{2,4},{4,2},{6,0},{1,7},{3,5},{5,3},{7,1},{8,14},{10,12},{12... | collective-permute-start | bytes 786440 | tf_op jit(solution)/shard_map/ppermute | solution.py:564
  121.0 7.7 %collective-permute-start.38 = (bf16[128,128]{1,0:T(8,128)(2,1)S(1)}, bf16[128,128]{1,0:T(8,128)(2,1)S(1)}, u32[]{:S(2)}, u32[]{:S(2)}) collective-permute-start(bf16[128,128]{1,0:T(8,128)(2,1)S(1)} %shard_map.131), channel_id=1, source_target_pairs={{0,1},{1,0},{2,3},{3,2},{4,5},{5,4},{6,7},{7,6},{8,9},{9,8},{10,11... | collective-permute-start | bytes 98312 | tf_op jit(solution)/shard_map/ppermute | solution.py:544
  140.5 7.3 %collective-permute-start.46 = (f32[1,2,128]{2,1,0:T(2,128)S(1)}, f32[1,2,128]{2,1,0:T(2,128)S(1)}, u32[]{:S(2)}, u32[]{:S(2)}) collective-permute-start(f32[1,2,128]{2,1,0:T(2,128)S(1)} %add_add_fusion.1), channel_id=1, source_target_pairs={{0,4},{2,6},{4,0},{6,2},{1,5},{3,7},{5,1},{7,3},{8,12},{10,14},{12... | collective-permute-start | bytes 3080 | tf_op jit(solution)/shard_map/ppermute | solution.py:511
  144.1 11.8 %collective-permute-start.52 = (s16[2,4,32,128]{3,2,1,0:T(8,128)(2,1)S(1)}, s16[2,4,32,128]{3,2,1,0:T(8,128)(2,1)S(1)}, u32[]{:S(2)}, u32[]{:S(2)}) collective-permute-start(s16[2,4,32,128]{3,2,1,0:T(8,128)(2,1)S(1)} %shard_map.136.refs_0_), channel_id=1, source_target_pairs={{0,8},{8,0},{16,24},{24,16},{1,9},{9,1},{17,25},{25,17},{2,10},{10... | collective-permute-start | bytes 196616 | tf_op jit(solution)/shard_map/ppermute | solution.py:595
  144.2 11.8 %collective-permute-start.53 = (s16[2,4,32,128]{3,2,1,0:T(8,128)(2,1)S(1)}, s16[2,4,32,128]{3,2,1,0:T(8,128)(2,1)S(1)}, u32[]{:S(2)}, u32[]{:S(2)}) collective-permute-start(s16[2,4,32,128]{3,2,1,0:T(8,128)(2,1)S(1)} %shard_map.136.refs_0_), channel_id=1, source_target_pairs={{0,16},{8,24},{16,0},{24,8},{1,17},{9,25},{17,1},{25,9},{2,18},{10... | collective-permute-start | bytes 196616 | tf_op jit(solution)/shard_map/ppermute | solution.py:595
  145.7 10.3 %collective-permute-start.54 = (s16[2,4,32,128]{3,2,1,0:T(8,128)(2,1)S(1)}, s16[2,4,32,128]{3,2,1,0:T(8,128)(2,1)S(1)}, u32[]{:S(2)}, u32[]{:S(2)}) collective-permute-start(s16[2,4,32,128]{3,2,1,0:T(8,128)(2,1)S(1)} %shard_map.136.refs_0_), channel_id=1, source_target_pairs={{0,24},{8,16},{16,8},{24,0},{1,25},{9,17},{17,9},{25,1},{2,26},{10... | collective-permute-start | bytes 196616 | tf_op jit(solution)/shard_map/ppermute | solution.py:595
  159.3 9.6 %collective-permute-start.55 = (s16[16,32,128]{2,1,0:T(8,128)(2,1)S(1)}, s16[16,32,128]{2,1,0:T(8,128)(2,1)S(1)}, u32[]{:S(2)}, u32[]{:S(2)}) collective-permute-start(s16[16,32,128]{2,1,0:T(8,128)(2,1)S(1)} %bitcast.36), channel_id=1, source_target_pairs={{0,2},{2,0},{4,6},{6,4},{1,3},{3,1},{5,7},{7,5},{8,10},{10,8},{12,... | collective-permute-start | bytes 393224 | tf_op jit(solution)/shard_map/ppermute | solution.py:606
  159.5 9.4 %collective-permute-start.56 = (s16[16,32,128]{2,1,0:T(8,128)(2,1)S(1)}, s16[16,32,128]{2,1,0:T(8,128)(2,1)S(1)}, u32[]{:S(2)}, u32[]{:S(2)}) collective-permute-start(s16[16,32,128]{2,1,0:T(8,128)(2,1)S(1)} %bitcast.37), channel_id=1, source_target_pairs={{0,4},{2,6},{4,0},{6,2},{1,5},{3,7},{5,1},{7,3},{8,12},{10,14},{12... | collective-permute-start | bytes 393224 | tf_op jit(solution)/shard_map/ppermute | solution.py:606
  160.9 8.4 %collective-permute-start.57 = (s16[16,32,128]{2,1,0:T(8,128)(2,1)S(1)}, s16[16,32,128]{2,1,0:T(8,128)(2,1)S(1)}, u32[]{:S(2)}, u32[]{:S(2)}) collective-permute-start(s16[16,32,128]{2,1,0:T(8,128)(2,1)S(1)} %bitcast.38), channel_id=1, source_target_pairs={{0,6},{2,4},{4,2},{6,0},{1,7},{3,5},{5,3},{7,1},{8,14},{10,12},{12... | collective-permute-start | bytes 393224 | tf_op jit(solution)/shard_map/ppermute | solution.py:606
  164.4 8.3 %collective-permute-start.62 = (s16[64,32,128]{2,1,0:T(8,128)(2,1)S(1)}, s16[64,32,128]{2,1,0:T(8,128)(2,1)S(1)}, u32[]{:S(2)}, u32[]{:S(2)}) collective-permute-start(s16[64,32,128]{2,1,0:T(8,128)(2,1)S(1)} %bitcast.25), channel_id=1, source_target_pairs={{0,1},{1,0},{2,3},{3,2},{4,5},{5,4},{6,7},{7,6},{8,9},{9,8},{10,11... | collective-permute-start | bytes 1572872 | tf_op jit(solution)/shard_map/ppermute | solution.py:544
  169.9 6.8 %collective-permute-start.58 = (s16[64,32,128]{2,1,0:T(8,128)(2,1)S(1)}, s16[64,32,128]{2,1,0:T(8,128)(2,1)S(1)}, u32[]{:S(2)}, u32[]{:S(2)}) collective-permute-start(s16[64,32,128]{2,1,0:T(8,128)(2,1)S(1)} %bitcast.27), channel_id=1, source_target_pairs={{0,1},{1,0},{2,3},{3,2},{4,5},{5,4},{6,7},{7,6},{8,9},{9,8},{10,11... | collective-permute-start | bytes 1572872 | tf_op jit(solution)/shard_map/ppermute | solution.py:544
  (38 other events, 179.1 us)

commit v13 on v12

--- a/solution.py
+++ b/solution.py
@@ -12,7 +12,7 @@
 BF16 = jnp.bfloat16
 GROUP = 4
 TAPS, SLOTS = 27, 32
-FULL = 32760.0
+FULL, LOW = 32760.0, 65000.0
 LN2 = 0.6931471805599453
 VMEM = pl.BlockSpec(memory_space=pltpu.VMEM)
 SMEM = pl.BlockSpec(memory_space=pltpu.SMEM)
@@ -299,13 +299,31 @@
     theirs_ref[here, :] = jnp.where(is_first, lower, upper)
 
 
-def encoded(value):
+def encoded(value, digits=None):
     slot = lax.broadcasted_iota(jnp.int32, value.shape, 1)
     value = jnp.where(slot < TAPS, value, 0.0)
     top = jnp.max(jnp.abs(value), axis=1, keepdims=True)
     power = jnp.ceil(jnp.log(jnp.maximum(top, 1e-30)) * (1.0 / LN2))
     number = jnp.round(value * (FULL * jnp.exp(power * -LN2)))
-    return jnp.where(slot < TAPS, number, power).astype(jnp.int32).astype(jnp.int16)
+    number = jnp.where(slot < TAPS, number, power)
+    if digits is not None:
+        first_row = lax.broadcasted_iota(jnp.int32, value.shape, 0) == 0
+        for place, digit in enumerate(digits):
+            number = jnp.where(first_row & (slot == TAPS + place), digit[None], number)
+    return number.astype(jnp.int32).astype(jnp.int16)
+
+
+def digits_of(value):
+    power = jnp.ceil(jnp.log(jnp.maximum(jnp.abs(value), 1e-30)) * (1.0 / LN2))
+    scaled = value * (FULL * jnp.exp(power * -LN2))
+    high = jnp.round(scaled)
+    return high, jnp.round((scaled - high) * LOW), power
+
+
+def value_of(number):
+    number = number.astype(jnp.int32).astype(F32)
+    high, low, power = (number[TAPS + place : TAPS + place + 1] for place in range(3))
+    return (high + low * (1.0 / LOW)) * (jnp.exp(power * LN2) * (1.0 / FULL))
 
 
 def decoded_value(number):
@@ -322,22 +340,27 @@
             out[which] = total if k == 0 else encoded(total)
 
 
-def scatter_kernel(flag_ref, *refs, received, sent, slot):
+def scatter_kernel(flag_ref, sums_ref, *refs, received, sent, slot, last):
     me = flag_ref[slot]
     for which in range(2):
+        digits = digits_of(sums_ref[0, which : which + 1]) if last else None
         for k, out in enumerate(refs[-sent:]):
             total = refs[0][which, me ^ k]
             for ref in refs[1:received]:
                 total = total + decoded_value(ref[which, me ^ k])
-            out[which] = total if k == 0 else encoded(total)
-
-
-def total_kernel(*refs, received):
+            out[which] = total if k == 0 else encoded(total, digits)
+
+
+def total_kernel(sums_ref, *refs, received):
+    out_ref, sums_out = refs[-2:]
     for which in range(2):
         total = refs[0][which]
+        terms = sums_ref[0, which : which + 1]
         for ref in refs[1:received]:
             total = total + decoded_value(ref[which])
-        refs[-1][which] = encoded(total)
+            terms = terms + value_of(ref[which, 0])
+        out_ref[which] = encoded(total)
+        sums_out[0, which : which + 1] = terms
 
 
 def split_kernel(flag_ref, *refs, received, slot):
@@ -404,10 +427,11 @@
 
 
 def first_grad_kernel(flag_ref, *refs, count):
-    weight, latent, par_ref, st_ref, _, scaled_ref, sums_ref, stack_ref = refs[-8:]
+    weight, latent, par_ref, st_ref = refs[6:10]
+    scaled_ref, sums_ref, stack_ref = refs[-3:]
     rows, frames, channels, cols = latent.shape
     mean, inverse, gain, shift, scale = norm_columns(par_ref, st_ref, count, 1)
-    fill_future(stack_ref, flag_ref, *refs[:-8])
+    fill_future(stack_ref, flag_ref, *refs[:6])
     first = jnp.zeros((channels, 128), F32)
     second = jnp.zeros((channels, 128), F32)
     for row in range(rows):
@@ -506,8 +530,8 @@
     refs[-1][...] = pairwise([(ref[...], count) for ref in refs[:parts]], joined_stats)[0]
 
 
-def all_sum(value, after=()):
-    for axis, _, exchanges in rounds(("tm", "height", "width")):
+def all_sum(value, after=(), axes=("tm", "height", "width")):
+    for axis, _, exchanges in rounds(axes):
         parts = [value] + [lax.ppermute(value, axis, pairs) for pairs in exchanges]
         if after:
             value = joined_after(functools.partial(sum_kernel, parts=len(parts)), parts, after)
@@ -564,31 +588,31 @@
     return [kept] + [lax.ppermute(v, axis, pairs) for v, pairs in zip(sent, exchanges)], sent[0]
 
 
-def summed(flags, received, after):
-    for number, (axis, _, exchanges) in enumerate(weight_rounds()[1:], 5):
+def summed(flags, received, sums, after):
+    others = weight_rounds()[1:]
+    for number, (axis, _, exchanges) in enumerate(others, 5):
         parts = len(exchanges) + 1
         _, rows, _, channels = received[0].shape
         part = (2, rows // parts, SLOTS, channels)
         views = [v.reshape(2, parts, *part[1:]) for v in received]
+        last = number == len(others) + 4
         kept, *sent = call(
-            functools.partial(scatter_kernel, received=len(views), sent=parts, slot=number),
+            functools.partial(scatter_kernel, received=len(views), sent=parts, slot=number, last=last),
             [shape(part, F32)] + [shape(part, jnp.int16)] * (parts - 1),
-            [SMEM] + [VMEM] * (len(views) + len(after)),
-            (flags, *views, *after),
+            [SMEM] + [VMEM] * (1 + len(views) + len(after)),
+            (flags, sums, *views, *after),
         )
         after = ()
         received = [kept] + [lax.ppermute(v, axis, pairs) for v, pairs in zip(sent, exchanges)]
-        last = sent[0]
-    return received, last
-
-
-def gathered(flags, received, after, after_last):
-    (total,) = call(
+    return call(
         functools.partial(total_kernel, received=len(received)),
-        [shape(received[0].shape, jnp.int16)],
-        [VMEM] * (len(received) + len(after)),
-        (*received, *after),
-    )
+        [shape(received[0].shape, jnp.int16), shape(sums.shape, F32)],
+        [VMEM] * (1 + len(received)),
+        (sums, *received),
+    )
+
+
+def gathered(flags, total, after_last):
     _, rows, _, channels = total.shape
     back = list(enumerate(weight_rounds(), 4))[::-1]
     number, (axis, _, exchanges) = back[0]
@@ -743,8 +767,6 @@
         (hidden, scaled, par, stats_second, sums),
     )
     future = shifted(hidden_grad, "tm", -1)
-    (near,) = row_halos(down, up, (future,))
-    around = (future, near, shifted(near, "tm", -1))
     halves_first = call(
         weight_first_kernel,
         halves,
@@ -753,29 +775,31 @@
         scratch=[pltpu.VMEM((rows * cols, frames * channels), BF16)],
         flops=conv_flops,
     )
+    (near,) = row_halos(down, up, (future, halves_first[0]))
+    around = (future, near, shifted(near, "tm", -1))
     halves_second, halves_first = (
         [v.reshape(channels // 2, SLOTS, channels) for v in halves] for halves in (halves_second, halves_first)
     )
     weights, sent = scattered(flags, halves_second, halves_first)
     around = with_columns(flags, hidden_grad, around, (sent,))
-    weights, sent = summed(flags, weights, around[:2])
     scaled, sums_first = call(
         functools.partial(first_grad_kernel, count=count),
         [shape(block, F32), small],
-        [SMEM] + [VMEM] * 11,
-        (flags, hidden_grad, *around, weight_first_t, latent, par, stats_first, sent),
+        [SMEM] + [VMEM] * (9 + len(weights)),
+        (flags, hidden_grad, *around, weight_first_t, latent, par, stats_first, *weights[1:]),
         scratch=[pltpu.VMEM(stack, BF16)],
         flops=conv_flops,
         transcendentals=latent.size,
     )
-    sums_first = all_sum(sums_first)
+    total, sums_first = summed(flags, weights, sums_first, around[:2])
+    sums_first = all_sum(sums_first, axes=("height", "width"))
     decoded_grad, token = call(
         functools.partial(decoded_grad_kernel, count=count),
         [shape((channels, frames, rows, cols), F32), shape((8, 128), F32)],
         [VMEM] * 6,
         (scaled, latent, cotangent, par, stats_first, sums_first),
     )
-    second, first = gathered(flags, weights, (), token)
+    second, first = gathered(flags, total, token)
     conv_second_grad = joined(flags, second, swapped(second))
     conv_first_grad = joined(flags, first, swapped(first))
     return decoded_grad, conv_first_grad, conv_second_grad

time: 181 us -> 180 us (level)
  starting transfers between devices: 95.1 us -> 91.7 us
  waiting for transfers between devices: 28.9 us -> 30.9 us
    ppermute x14 -> x11, starting transfers between devices: 21.4 us -> 17.1 us  [all_sum(): parts = [value] + [lax.ppermute(value, axis, pairs) for pairs in exchanges]]
    ppermute x3, waiting for transfers between devices: 1.07 us -> 3.4 us  [summed(): lax.ppermute(v, axis, pairs)]
    ppermute x14 -> x11, waiting for transfers between devices: 3.8 us -> 3.8 us  [all_sum(): parts = [value] + [lax.ppermute(value, axis, pairs) for pairs in exchanges]]
  transfers between devices with their start and end apart: 63 -> 60, of which waited for: 18 -> 19; matrix products, arithmetic and copies ran while one was open for 0% -> 0% of each run, Pallas kernels for 21% -> 20%
where the time goes in v13:
time: 180 us; the launch traced here: 179 us
  starting transfers between devices  91.7 us (51%)
  Pallas kernels  49.7 us (28%)
  waiting for transfers between devices  30.9 us (17%)
  local copies, waits for them, and re-layouts  4.96 us (3%)
    pallas_call x30, Pallas kernels, call(): pl.pallas_call(body, out_shape=tuple(outs), in_specs=specs, out_specs=tup...  49.7 us
    ppermute x14, starting transfers between devices, all_stats(): parts = [value] + [lax.ppermute(value, axis, pairs) for pairs in exchanges]  23.5 us
    ppermute x10, starting transfers between devices, shifted(): lax.ppermute(value, axis, [(source, source + steps) for source in range(i...  20.7 us
    ppermute x11, starting transfers between devices, all_sum(): parts = [value] + [lax.ppermute(value, axis, pairs) for pairs in exchanges]  17.1 us
    ppermute x10, starting transfers between devices, swapped(): return lax.ppermute(value, 'width', [(0, 1), (1, 0)])  14.5 us
    ppermute x10, waiting for transfers between devices, shifted(): lax.ppermute(value, axis, [(source, source + steps) for source in range(i...  14.1 us
    ppermute x6, starting transfers between devices, gathered(): pieces = [value] + [lax.ppermute(value, axis, pairs) for pairs in exchanges]  5.36 us
    ppermute x14, waiting for transfers between devices, all_stats(): parts = [value] + [lax.ppermute(value, axis, pairs) for pairs in exchanges]  4.79 us
  transfers between devices with their start and end apart: 60, of which 19 were waited for; matrix products, arithmetic and copies ran while one was open for 0% of the time, Pallas kernels for 20%

profile of v13, /device:TPU:1, one launch (start us, length us, event | category | flops | bytes accessed | tf_op | source)
XLA Modules:
  0.0 179.2 jit_solution(2732257843953277955)
XLA Ops:
  4.3 2.6 %shard_map.112 = (bf16[4,2,128,256]{3,2,1,0:T(8,128)(2,1)S(1)}, bf16[4,2,128,256]{3,2,1,0:T(8,128)(2,1)S(1)}, bf16[2,2,128,256]{3,2,1,0:T(8,128)(2,1)S(1)}, bf16...) custom-call(bf16[128,2,4,256]{3,2,1,0:T(4,128)(2,1)S(1)} %copy-done.3, bf16[128,2,4,256]{3,2,1,0:T(4,128)(2,1)S(1)} %copy-done.4, ...), custom_call_target="tpu_custom_call" | custom-call | bytes 2626560 | tf_op jit(solution)/shard_map/pallas_call | solution.py:24
  7.0 2.2 %collective-permute-start.6 = (f32[1,2,128]{2,1,0:T(2,128)S(1)}, f32[1,2,128]{2,1,0:T(2,128)S(1)}, u32[]{:S(2)}, u32[]{:S(2)}) collective-permute-start(f32[1,2,128]{2,1,0:T(2,128)S(1)} %get-tuple-element.45), channel_id=1, source_target_pairs={{0,8},{8,0},{16,24},{24,16},{1,9},{9,1},{17,25},{25,17},{2,10},{10... | collective-permute-start | bytes 3080 | tf_op jit(solution)/shard_map/ppermute | solution.py:551
  9.2 2.3 %collective-permute-start.7 = (f32[1,2,128]{2,1,0:T(2,128)S(1)}, f32[1,2,128]{2,1,0:T(2,128)S(1)}, u32[]{:S(2)}, u32[]{:S(2)}) collective-permute-start(f32[1,2,128]{2,1,0:T(2,128)S(1)} %get-tuple-element.45), channel_id=1, source_target_pairs={{0,16},{8,24},{16,0},{24,8},{1,17},{9,25},{17,1},{25,9},{2,18},{10... | collective-permute-start | bytes 3080 | tf_op jit(solution)/shard_map/ppermute | solution.py:551
  11.5 3.1 %collective-permute-start.1 = (bf16[2,2,128,256]{3,2,1,0:T(8,128)(2,1)S(1)}, bf16[2,2,128,256]{3,2,1,0:T(8,128)(2,1)S(1)}, u32[]{:S(2)}, u32[]{:S(2)}) collective-permute-start(bf16[2,2,128,256]{3,2,1,0:T(8,128)(2,1)S(1)} %get-tuple-element.42), channel_id=1, source_target_pairs={{0,2},{2,4},{4,6},{1,3},{3,5},{5,7},{8,10},{10,12},{12,14},{9,11},... | collective-permute-start | bytes 786440 | tf_op jit(solution)/shard_map/ppermute | solution.py:506
  16.0 3.1 %collective-permute-start.10 = (f32[1,2,128]{2,1,0:T(2,128)S(1)}, f32[1,2,128]{2,1,0:T(2,128)S(1)}, u32[]{:S(2)}, u32[]{:S(2)}) collective-permute-start(f32[1,2,128]{2,1,0:T(2,128)S(1)} %pad_maximum_fusion), channel_id=1, source_target_pairs={{0,4},{2,6},{4,0},{6,2},{1,5},{3,7},{5,1},{7,3},{8,12},{10,14},{12... | collective-permute-start | bytes 3080 | tf_op jit(solution)/shard_map/ppermute | solution.py:551
  20.3 3.1 %collective-permute-start = (bf16[4,2,128,256]{3,2,1,0:T(8,128)(2,1)S(1)}, bf16[4,2,128,256]{3,2,1,0:T(8,128)(2,1)}, u32[]{:S(2)}, u32[]{:S(2)}) collective-permute-start(bf16[4,2,128,256]{3,2,1,0:T(8,128)(2,1)S(1)} %get-tuple-element.41.first_ref.own.refs_7_.latent), channel_id=1, source_target_pairs={{0,8},{8,16},{16,24},{1,9},{9,17},{17,25},{2,10},{10,18},{18,26},{... | collective-permute-start | bytes 1572872 | tf_op jit(solution)/shard_map/ppermute | solution.py:506
  27.8 3.0 %collective-permute-start.3 = (bf16[2,2,128,256]{3,2,1,0:T(8,128)(2,1)}, bf16[2,2,128,256]{3,2,1,0:T(8,128)(2,1)}, u32[]{:S(2)}, u32[]{:S(2)}) collective-permute-start(bf16[2,2,128,256]{3,2,1,0:T(8,128)(2,1)} %get-tuple-element.44.first_ref.near), channel_id=1, source_target_pairs={{0,8},{8,16},{16,24},{1,9},{9,17},{17,25},{2,10},{10,18},{18,26},{... | collective-permute-start | bytes 786440 | tf_op jit(solution)/shard_map/ppermute | solution.py:506
  30.8 3.5 %collective-permute-start.12 = (f32[1,2,128]{2,1,0:T(2,128)S(1)}, f32[1,2,128]{2,1,0:T(2,128)S(1)}, u32[]{:S(2)}, u32[]{:S(2)}) collective-permute-start(f32[1,2,128]{2,1,0:T(2,128)S(1)} %pad_maximum_fusion.1), channel_id=1, source_target_pairs={{0,1},{1,0},{2,3},{3,2},{4,5},{5,4},{6,7},{7,6},{8,9},{9,8},{10,11... | collective-permute-start | bytes 3080 | tf_op jit(solution)/shard_map/ppermute | solution.py:551
  38.7 3.1 %collective-permute-start.5 = (bf16[128,128]{1,0:T(8,128)(2,1)S(1)}, bf16[128,128]{1,0:T(8,128)(2,1)S(1)}, u32[]{:S(2)}, u32[]{:S(2)}) collective-permute-start(bf16[128,128]{1,0:T(8,128)(2,1)S(1)} %shard_map.115), channel_id=1, source_target_pairs={{0,1},{1,0},{2,3},{3,2},{4,5},{5,4},{6,7},{7,6},{8,9},{9,8},{10,11... | collective-permute-start | bytes 98312 | tf_op jit(solution)/shard_map/ppermute | solution.py:568
  41.8 2.0 %shard_map.114 = bf16[128,128]{1,0:T(8,128)(2,1)S(1)} custom-call(s32[6]{0:T(128)S(1)} %stack.57.flag_ref, bf16[4,2,128,256]{3,2,1,0:T(8,128)(2,1)S(1)} %get-tuple-element.41.first_ref.own.refs_7_.latent, bf16[4,2,128,256]{3,2,1,0:T(8,128)(2,1)} %collective-permute-done.second_ref.past), custom_call_target="tpu_custom_call" | custom-call | bytes 1081368 | tf_op jit(solution)/shard_map/pallas_call | solution.py:24
  45.8 5.3 %shard_map.117 = (f32[4,2,128,256]{3,2,1,0:T(8,128)S(1)}, f32[1,2,128]{2,1,0:T(2,128)S(1)}, bf16[6,4,384,256]{3,2,1,0:T(8,128)(2,1)S(1)}) custom-call(s32[6]{0:T(128)S(1)} %stack.57.flag_ref, bf16[4,2,128,256]{3,2,1,0:T(8,128)(2,1)S(1)} %get-tuple-element.41.first_ref.own.refs_7_.latent, bf16[4,2,128,256]{3,2,1,0:T(8,128)(2,1)} %collective-permute-done.second_ref.past, ...), custom_call_target="tpu_custom_call" | custom-call | flops 7247757312 | bytes 10033176 | tf_op jit(solution)/shard_map/pallas_call | solution.py:24
  52.9 2.0 %shard_map.118 = bf16[128,128]{1,0:T(8,128)(2,1)S(1)} custom-call(s32[6]{0:T(128)S(1)} %stack.57.flag_ref, bf16[4,2,128,256]{3,2,1,0:T(8,128)(2,1)S(1)} %get-tuple-element.48.first_ref.refs_0_.cotangent, bf16[4,2,128,256]{3,2,1,0:T(8,128)(2,1)} %collective-permute-done.14.second_ref.refs_1_, f32[1,2,128]{2,1,0:T(2,128)S(1)} %get-tuple-element.49.refs_0_), custom_call_target="tpu_custom_call" | custom-call | bytes 1082392 | tf_op jit(solution)/shard_map/pallas_call | solution.py:24
  56.8 3.0 %collective-permute-start.18 = (f32[1,2,128]{2,1,0:T(2,128)S(1)}, f32[1,2,128]{2,1,0:T(2,128)S(1)}, u32[]{:S(2)}, u32[]{:S(2)}) collective-permute-start(f32[1,2,128]{2,1,0:T(2,128)S(1)} %get-tuple-element.49.refs_0_), channel_id=1, source_target_pairs={{0,16},{8,24},{16,0},{24,8},{1,17},{9,25},{17,1},{25,9},{2,18},{10... | collective-permute-start | bytes 3080 | tf_op jit(solution)/shard_map/ppermute | solution.py:551
  59.9 3.9 %shard_map.121 = (f32[4,2,128,256]{3,2,1,0:T(8,128)S(1)}, bf16[6,4,384,256]{3,2,1,0:T(8,128)(2,1)S(1)}) custom-call(s32[6]{0:T(128)S(1)} %stack.57.flag_ref, bf16[4,2,128,256]{3,2,1,0:T(8,128)(2,1)S(1)} %get-tuple-element.48.first_ref.refs_0_.cotangent, bf16[4,2,128,256]{3,2,1,0:T(8,128)(2,1)} %collective-permute-done.14.second_ref.refs_1_, ...), custom_call_target="tpu_custom_call" | custom-call | flops 7247757312 | bytes 9764888 | tf_op jit(solution)/shard_map/pallas_call | solution.py:24
  64.1 2.6 %collective-permute-start.20 = (f32[1,2,128]{2,1,0:T(2,128)S(1)}, f32[1,2,128]{2,1,0:T(2,128)S(1)}, u32[]{:S(2)}, u32[]{:S(2)}) collective-permute-start(f32[1,2,128]{2,1,0:T(2,128)S(1)} %shard_map.122), channel_id=1, source_target_pairs={{0,2},{2,0},{4,6},{6,4},{1,3},{3,1},{5,7},{7,5},{8,10},{10,8},{12,... | collective-permute-start | bytes 3080 | tf_op jit(solution)/shard_map/ppermute | solution.py:551
  70.0 2.9 %collective-permute-start.23 = (f32[1,2,128]{2,1,0:T(2,128)S(1)}, f32[1,2,128]{2,1,0:T(2,128)S(1)}, u32[]{:S(2)}, u32[]{:S(2)}) collective-permute-start(f32[1,2,128]{2,1,0:T(2,128)S(1)} %pad_maximum_fusion.3), channel_id=1, source_target_pairs={{0,1},{1,0},{2,3},{3,2},{4,5},{5,4},{6,7},{7,6},{8,9},{9,8},{10,11... | collective-permute-start | bytes 3080 | tf_op jit(solution)/shard_map/ppermute | solution.py:551
  74.8 2.4 %collective-permute-start.25 = (f32[1,2,128]{2,1,0:T(2,128)S(1)}, f32[1,2,128]{2,1,0:T(2,128)S(1)}, u32[]{:S(2)}, u32[]{:S(2)}) collective-permute-start(f32[1,2,128]{2,1,0:T(2,128)S(1)} %get-tuple-element.52.refs_0_), channel_id=1, source_target_pairs={{0,16},{8,24},{16,0},{24,8},{1,17},{9,25},{17,1},{25,9},{2,18},{10... | collective-permute-start | bytes 3080 | tf_op jit(solution)/shard_map/ppermute | solution.py:535
  78.3 4.3 %shard_map.124 = (f32[2048,128]{1,0:T(8,128)S(1)}, f32[2048,128]{1,0:T(8,128)S(1)}) custom-call(s32[6]{0:T(128)S(1)} %stack.57.flag_ref, bf16[6,4,384,256]{3,2,1,0:T(8,128)(2,1)S(1)} %get-tuple-element.53.stack_ref, bf16[4,2,128,256]{3,2,1,0:T(8,128)(2,1)S(1)} %get-tuple-element.54.act_ref), custom_call_target="tpu_custom_call" | custom-call | flops 7247757312 | bytes 7340056 | tf_op jit(solution)/shard_map/pallas_call | solution.py:24
  87.9 2.6 %collective-permute-start.30 = (f32[1,2,128]{2,1,0:T(2,128)S(1)}, f32[1,2,128]{2,1,0:T(2,128)S(1)}, u32[]{:S(2)}, u32[]{:S(2)}) collective-permute-start(f32[1,2,128]{2,1,0:T(2,128)S(1)} %add_add_fusion.1), channel_id=1, source_target_pairs={{0,1},{1,0},{2,3},{3,2},{4,5},{5,4},{6,7},{7,6},{8,9},{9,8},{10,11... | collective-permute-start | bytes 3080 | tf_op jit(solution)/shard_map/ppermute | solution.py:535
  91.8 4.1 %shard_map.127 = (f32[2048,128]{1,0:T(8,128)S(1)}, f32[2048,128]{1,0:T(8,128)S(1)}) custom-call(s32[6]{0:T(128)S(1)} %stack.57.flag_ref, bf16[6,4,384,256]{3,2,1,0:T(8,128)(2,1)S(1)} %get-tuple-element.59.stack_ref, bf16[4,2,128,256]{3,2,1,0:T(8,128)(2,1)S(1)} %get-tuple-element.56.grad_ref.first_ref.refs_0_), custom_call_target="tpu_custom_call" | custom-call | flops 7247757312 | bytes 7340056 | tf_op jit(solution)/shard_map/pallas_call | solution.py:24
  97.5 3.6 %collective-permute-start.32 = (bf16[1,2,128,256]{3,2,1,0:T(8,128)(2,1)S(1)}, bf16[1,2,128,256]{3,2,1,0:T(8,128)(2,1)S(1)}, u32[]{:S(2)}, u32[]{:S(2)}) collective-permute-start(bf16[1,2,128,256]{3,2,1,0:T(8,128)(2,1)S(1)} %get-tuple-element.57), channel_id=1, source_target_pairs={{0,2},{2,4},{4,6},{1,3},{3,5},{5,7},{8,10},{10,12},{12,14},{9,11},... | collective-permute-start | bytes 393224 | tf_op jit(solution)/shard_map/ppermute | solution.py:506
  103.8 4.8 %collective-permute-done.33.below_ref = bf16[1,2,128,256]{3,2,1,0:T(8,128)(2,1)S(1)} collective-permute-done((bf16[1,2,128,256]{3,2,1,0:T(8,128)(2,1)S(1)}, bf16[1,2,128,256]{3,2,1,0:T(8,128)(2,1)S(1)}, u32[]{:S(2)}, u32[]{:S(2)}) %collective-permute-start.33) | collective-permute-done | bytes 131104 | tf_op jit(solution)/shard_map/ppermute | solution.py:506
  108.6 2.9 %collective-permute-done.31.refs_0_.second_ref.refs_1_.refs_4_ = bf16[4,2,128,256]{3,2,1,0:T(8,128)(2,1)S(1)} collective-permute-done((bf16[4,2,128,256]{3,2,1,0:T(8,128)(2,1)S(1)}, bf16[4,2,128,256]{3,2,1,0:T(8,128)(2,1)S(1)}, u32[]{:S(2)}, u32[]{:S(2)}) %collective-permute-start.31) | collective-permute-done | bytes 524320 | tf_op jit(solution)/shard_map/ppermute | solution.py:506
  116.9 3.3 %collective-permute-done.34.second_ref.refs_3_ = bf16[2,2,128,256]{3,2,1,0:T(8,128)(2,1)S(1)} collective-permute-done((bf16[2,2,128,256]{3,2,1,0:T(8,128)(2,1)S(1)}, bf16[2,2,128,256]{3,2,1,0:T(8,128)(2,1)S(1)}, u32[]{:S(2)}, u32[]{:S(2)}) %collective-permute-start.34) | collective-permute-done | bytes 262176 | tf_op jit(solution)/shard_map/ppermute | solution.py:506
  121.1 2.0 %collective-permute-start.38 = (bf16[128,128]{1,0:T(8,128)(2,1)S(1)}, bf16[128,128]{1,0:T(8,128)(2,1)S(1)}, u32[]{:S(2)}, u32[]{:S(2)}) collective-permute-start(bf16[128,128]{1,0:T(8,128)(2,1)S(1)} %shard_map.131), channel_id=1, source_target_pairs={{0,1},{1,0},{2,3},{3,2},{4,5},{5,4},{6,7},{7,6},{8,9},{9,8},{10,11... | collective-permute-start | bytes 98312 | tf_op jit(solution)/shard_map/ppermute | solution.py:568
  127.8 4.0 %shard_map.133 = (f32[4,2,128,256]{3,2,1,0:T(8,128)S(1)}, f32[1,2,128]{2,1,0:T(2,128)S(1)}) custom-call(s32[6]{0:T(128)S(1)} %stack.57.flag_ref, bf16[4,2,128,256]{3,2,1,0:T(8,128)(2,1)S(1)} %get-tuple-element.56.grad_ref.first_ref.refs_0_, bf16[4,2,128,256]{3,2,1,0:T(8,128)(2,1)S(1)} %collective-permute-done.31.refs_0_.second_ref.refs_1_.refs_4_, ...), custom_call_target="tpu_custom_call" | custom-call | flops 7247757312 | bytes 6363160 | tf_op jit(solution)/shard_map/pallas_call | solution.py:24
  136.8 2.5 %collective-permute-done.43.refs_2_ = s16[2,4,32,128]{3,2,1,0:T(8,128)(2,1)S(1)} collective-permute-done((s16[2,4,32,128]{3,2,1,0:T(8,128)(2,1)S(1)}, s16[2,4,32,128]{3,2,1,0:T(8,128)(2,1)S(1)}, u32[]{:S(2)}, u32[]{:S(2)}) %collective-permute-start.43) | collective-permute-done | bytes 65568 | tf_op jit(solution)/shard_map/ppermute | solution.py:606
  146.6 5.3 %collective-permute-start.48 = (f32[1,2,128]{2,1,0:T(2,128)S(1)}, f32[1,2,128]{2,1,0:T(2,128)S(1)}, u32[]{:S(2)}, u32[]{:S(2)}) collective-permute-start(f32[1,2,128]{2,1,0:T(2,128)S(1)} %add_add_fusion), channel_id=1, source_target_pairs={{0,1},{1,0},{2,3},{3,2},{4,5},{5,4},{6,7},{7,6},{8,9},{9,8},{10,11... | collective-permute-start | bytes 3080 | tf_op jit(solution)/shard_map/ppermute | solution.py:535
  163.0 4.8 %collective-permute-start.59 = (s16[64,32,128]{2,1,0:T(8,128)(2,1)S(1)}, s16[64,32,128]{2,1,0:T(8,128)(2,1)S(1)}, u32[]{:S(2)}, u32[]{:S(2)}) collective-permute-start(s16[64,32,128]{2,1,0:T(8,128)(2,1)S(1)} %bitcast.26), channel_id=1, source_target_pairs={{0,1},{1,0},{2,3},{3,2},{4,5},{5,4},{6,7},{7,6},{8,9},{9,8},{10,11... | collective-permute-start | bytes 1572872 | tf_op jit(solution)/shard_map/ppermute | solution.py:568
  168.4 3.0 %collective-permute-start.55 = (s16[64,32,128]{2,1,0:T(8,128)(2,1)S(1)}, s16[64,32,128]{2,1,0:T(8,128)(2,1)S(1)}, u32[]{:S(2)}, u32[]{:S(2)}) collective-permute-start(s16[64,32,128]{2,1,0:T(8,128)(2,1)S(1)} %bitcast.28), channel_id=1, source_target_pairs={{0,1},{1,0},{2,3},{3,2},{4,5},{5,4},{6,7},{7,6},{8,9},{9,8},{10,11... | collective-permute-start | bytes 1572872 | tf_op jit(solution)/shard_map/ppermute | solution.py:568
  171.4 3.9 %shard_map.141 = f32[128,3456]{1,0:T(8,128)} custom-call(s32[6]{0:T(128)S(1)} %stack.57.flag_ref, s16[64,32,128]{2,1,0:T(8,128)(2,1)S(1)} %bitcast.27, s16[64,32,128]{2,1,0:T(8,128)(2,1)S(1)} %collective-permute-done.59.theirs_ref), custom_call_target="tpu_custom_call" | custom-call | bytes 2818072 | tf_op jit(solution)/shard_map/pallas_call | solution.py:24
  175.3 3.9 %shard_map.139 = f32[128,3456]{1,0:T(8,128)} custom-call(s32[6]{0:T(128)S(1)} %stack.57.flag_ref, s16[64,32,128]{2,1,0:T(8,128)(2,1)S(1)} %bitcast.29, s16[64,32,128]{2,1,0:T(8,128)(2,1)S(1)} %collective-permute-done.55.theirs_ref), custom_call_target="tpu_custom_call" | custom-call | bytes 2818072 | tf_op jit(solution)/shard_map/pallas_call | solution.py:24
  (153 shorter events, 73.0 us)
Async XLA Ops:
  7.0 8.9 %collective-permute-start.6 = (f32[1,2,128]{2,1,0:T(2,128)S(1)}, f32[1,2,128]{2,1,0:T(2,128)S(1)}, u32[]{:S(2)}, u32[]{:S(2)}) collective-permute-start(f32[1,2,128]{2,1,0:T(2,128)S(1)} %get-tuple-element.45), channel_id=1, source_target_pairs={{0,8},{8,0},{16,24},{24,16},{1,9},{9,1},{17,25},{25,17},{2,10},{10... | collective-permute-start | bytes 3080 | tf_op jit(solution)/shard_map/ppermute | solution.py:551
  9.2 6.8 %collective-permute-start.7 = (f32[1,2,128]{2,1,0:T(2,128)S(1)}, f32[1,2,128]{2,1,0:T(2,128)S(1)}, u32[]{:S(2)}, u32[]{:S(2)}) collective-permute-start(f32[1,2,128]{2,1,0:T(2,128)S(1)} %get-tuple-element.45), channel_id=1, source_target_pairs={{0,16},{8,24},{16,0},{24,8},{1,17},{9,25},{17,1},{25,9},{2,18},{10... | collective-permute-start | bytes 3080 | tf_op jit(solution)/shard_map/ppermute | solution.py:551
  11.5 14.9 %collective-permute-start.1 = (bf16[2,2,128,256]{3,2,1,0:T(8,128)(2,1)S(1)}, bf16[2,2,128,256]{3,2,1,0:T(8,128)(2,1)S(1)}, u32[]{:S(2)}, u32[]{:S(2)}) collective-permute-start(bf16[2,2,128,256]{3,2,1,0:T(8,128)(2,1)S(1)} %get-tuple-element.42), channel_id=1, source_target_pairs={{0,2},{2,4},{4,6},{1,3},{3,5},{5,7},{8,10},{10,12},{12,14},{9,11},... | collective-permute-start | bytes 786440 | tf_op jit(solution)/shard_map/ppermute | solution.py:506
  14.6 11.7 %collective-permute-start.2 = (bf16[2,2,128,256]{3,2,1,0:T(8,128)(2,1)S(1)}, bf16[2,2,128,256]{3,2,1,0:T(8,128)(2,1)S(1)}, u32[]{:S(2)}, u32[]{:S(2)}) collective-permute-start(bf16[2,2,128,256]{3,2,1,0:T(8,128)(2,1)S(1)} %get-tuple-element.43), channel_id=1, source_target_pairs={{2,0},{4,2},{6,4},{3,1},{5,3},{7,5},{10,8},{12,10},{14,12},{11,9},... | collective-permute-start | bytes 786440 | tf_op jit(solution)/shard_map/ppermute | solution.py:506
  19.3 7.0 %collective-permute-start.9 = (f32[1,2,128]{2,1,0:T(2,128)S(1)}, f32[1,2,128]{2,1,0:T(2,128)S(1)}, u32[]{:S(2)}, u32[]{:S(2)}) collective-permute-start(f32[1,2,128]{2,1,0:T(2,128)S(1)} %pad_maximum_fusion), channel_id=1, source_target_pairs={{0,2},{2,0},{4,6},{6,4},{1,3},{3,1},{5,7},{7,5},{8,10},{10,8},{12,... | collective-permute-start | bytes 3080 | tf_op jit(solution)/shard_map/ppermute | solution.py:551
  20.3 21.5 %collective-permute-start = (bf16[4,2,128,256]{3,2,1,0:T(8,128)(2,1)S(1)}, bf16[4,2,128,256]{3,2,1,0:T(8,128)(2,1)}, u32[]{:S(2)}, u32[]{:S(2)}) collective-permute-start(bf16[4,2,128,256]{3,2,1,0:T(8,128)(2,1)S(1)} %get-tuple-element.41.first_ref.own.refs_7_.latent), channel_id=1, source_target_pairs={{0,8},{8,16},{16,24},{1,9},{9,17},{17,25},{2,10},{10,18},{18,26},{... | collective-permute-start | bytes 1572872 | tf_op jit(solution)/shard_map/ppermute | solution.py:506
  23.4 29.5 %collective-permute-start.14 = (bf16[4,2,128,256]{3,2,1,0:T(8,128)(2,1)S(1)}, bf16[4,2,128,256]{3,2,1,0:T(8,128)(2,1)}, u32[]{:S(2)}, u32[]{:S(2)}) collective-permute-start(bf16[4,2,128,256]{3,2,1,0:T(8,128)(2,1)S(1)} %get-tuple-element.48.first_ref.refs_0_.cotangent), channel_id=1, source_target_pairs={{8,0},{16,8},{24,16},{9,1},{17,9},{25,17},{10,2},{18,10},{26,18},{... | collective-permute-start | bytes 1572872 | tf_op jit(solution)/shard_map/ppermute | solution.py:506
  27.8 9.5 %collective-permute-start.3 = (bf16[2,2,128,256]{3,2,1,0:T(8,128)(2,1)}, bf16[2,2,128,256]{3,2,1,0:T(8,128)(2,1)}, u32[]{:S(2)}, u32[]{:S(2)}) collective-permute-start(bf16[2,2,128,256]{3,2,1,0:T(8,128)(2,1)} %get-tuple-element.44.first_ref.near), channel_id=1, source_target_pairs={{0,8},{8,16},{16,24},{1,9},{9,17},{17,25},{2,10},{10,18},{18,26},{... | collective-permute-start | bytes 786440 | tf_op jit(solution)/shard_map/ppermute | solution.py:506
  30.8 6.4 %collective-permute-start.12 = (f32[1,2,128]{2,1,0:T(2,128)S(1)}, f32[1,2,128]{2,1,0:T(2,128)S(1)}, u32[]{:S(2)}, u32[]{:S(2)}) collective-permute-start(f32[1,2,128]{2,1,0:T(2,128)S(1)} %pad_maximum_fusion.1), channel_id=1, source_target_pairs={{0,1},{1,0},{2,3},{3,2},{4,5},{5,4},{6,7},{7,6},{8,9},{9,8},{10,11... | collective-permute-start | bytes 3080 | tf_op jit(solution)/shard_map/ppermute | solution.py:551
  35.8 10.0 %collective-permute-start.13 = (bf16[2,2,128,256]{3,2,1,0:T(8,128)(2,1)}, bf16[2,2,128,256]{3,2,1,0:T(8,128)(2,1)S(1)}, u32[]{:S(2)}, u32[]{:S(2)}) collective-permute-start(bf16[2,2,128,256]{3,2,1,0:T(8,128)(2,1)} %copy-done.5), channel_id=1, source_target_pairs={{8,0},{16,8},{24,16},{9,1},{17,9},{25,17},{10,2},{18,10},{26,18},{... | collective-permute-start | bytes 786440 | tf_op jit(solution)/shard_map/ppermute | solution.py:506
  38.7 7.1 %collective-permute-start.5 = (bf16[128,128]{1,0:T(8,128)(2,1)S(1)}, bf16[128,128]{1,0:T(8,128)(2,1)S(1)}, u32[]{:S(2)}, u32[]{:S(2)}) collective-permute-start(bf16[128,128]{1,0:T(8,128)(2,1)S(1)} %shard_map.115), channel_id=1, source_target_pairs={{0,1},{1,0},{2,3},{3,2},{4,5},{5,4},{6,7},{7,6},{8,9},{9,8},{10,11... | collective-permute-start | bytes 98312 | tf_op jit(solution)/shard_map/ppermute | solution.py:568
  52.0 7.8 %collective-permute-start.16 = (bf16[128,128]{1,0:T(8,128)(2,1)S(1)}, bf16[128,128]{1,0:T(8,128)(2,1)S(1)}, u32[]{:S(2)}, u32[]{:S(2)}) collective-permute-start(bf16[128,128]{1,0:T(8,128)(2,1)S(1)} %shard_map.119), channel_id=1, source_target_pairs={{0,1},{1,0},{2,3},{3,2},{4,5},{5,4},{6,7},{7,6},{8,9},{9,8},{10,11... | collective-permute-start | bytes 98312 | tf_op jit(solution)/shard_map/ppermute | solution.py:568
  55.4 8.4 %collective-permute-start.17 = (f32[1,2,128]{2,1,0:T(2,128)S(1)}, f32[1,2,128]{2,1,0:T(2,128)S(1)}, u32[]{:S(2)}, u32[]{:S(2)}) collective-permute-start(f32[1,2,128]{2,1,0:T(2,128)S(1)} %get-tuple-element.49.refs_0_), channel_id=1, source_target_pairs={{0,8},{8,0},{16,24},{24,16},{1,9},{9,1},{17,25},{25,17},{2,10},{10... | collective-permute-start | bytes 3080 | tf_op jit(solution)/shard_map/ppermute | solution.py:551
  56.8 7.0 %collective-permute-start.18 = (f32[1,2,128]{2,1,0:T(2,128)S(1)}, f32[1,2,128]{2,1,0:T(2,128)S(1)}, u32[]{:S(2)}, u32[]{:S(2)}) collective-permute-start(f32[1,2,128]{2,1,0:T(2,128)S(1)} %get-tuple-element.49.refs_0_), channel_id=1, source_target_pairs={{0,16},{8,24},{16,0},{24,8},{1,17},{9,25},{17,1},{25,9},{2,18},{10... | collective-permute-start | bytes 3080 | tf_op jit(solution)/shard_map/ppermute | solution.py:551
  74.7 8.0 %collective-permute-start.24 = (f32[1,2,128]{2,1,0:T(2,128)S(1)}, f32[1,2,128]{2,1,0:T(2,128)S(1)}, u32[]{:S(2)}, u32[]{:S(2)}) collective-permute-start(f32[1,2,128]{2,1,0:T(2,128)S(1)} %get-tuple-element.52.refs_0_), channel_id=1, source_target_pairs={{0,8},{8,0},{16,24},{24,16},{1,9},{9,1},{17,25},{25,17},{2,10},{10... | collective-permute-start | bytes 3080 | tf_op jit(solution)/shard_map/ppermute | solution.py:535
  74.8 7.9 %collective-permute-start.25 = (f32[1,2,128]{2,1,0:T(2,128)S(1)}, f32[1,2,128]{2,1,0:T(2,128)S(1)}, u32[]{:S(2)}, u32[]{:S(2)}) collective-permute-start(f32[1,2,128]{2,1,0:T(2,128)S(1)} %get-tuple-element.52.refs_0_), channel_id=1, source_target_pairs={{0,16},{8,24},{16,0},{24,8},{1,17},{9,25},{17,1},{25,9},{2,18},{10... | collective-permute-start | bytes 3080 | tf_op jit(solution)/shard_map/ppermute | solution.py:535
  90.4 22.4 %collective-permute-start.35 = (f32[64,32,128]{2,1,0:T(8,128)S(1)}, f32[64,32,128]{2,1,0:T(8,128)S(1)}, u32[]{:S(2)}, u32[]{:S(2)}) collective-permute-start(f32[64,32,128]{2,1,0:T(8,128)S(1)} %bitcast.44), channel_id=1, source_target_pairs={{0,1},{1,0},{2,3},{3,2},{4,5},{5,4},{6,7},{7,6},{8,9},{9,8},{10,11... | collective-permute-start | bytes 3145736 | tf_op jit(solution)/shard_map/ppermute | solution.py:568
  95.9 16.9 %collective-permute-start.36 = (f32[64,32,128]{2,1,0:T(8,128)S(1)}, f32[64,32,128]{2,1,0:T(8,128)S(1)}, u32[]{:S(2)}, u32[]{:S(2)}) collective-permute-start(f32[64,32,128]{2,1,0:T(8,128)S(1)} %bitcast.45), channel_id=1, source_target_pairs={{0,1},{1,0},{2,3},{3,2},{4,5},{5,4},{6,7},{7,6},{8,9},{9,8},{10,11... | collective-permute-start | bytes 3145736 | tf_op jit(solution)/shard_map/ppermute | solution.py:568
  96.3 15.2 %collective-permute-start.31 = (bf16[4,2,128,256]{3,2,1,0:T(8,128)(2,1)S(1)}, bf16[4,2,128,256]{3,2,1,0:T(8,128)(2,1)S(1)}, u32[]{:S(2)}, u32[]{:S(2)}) collective-permute-start(bf16[4,2,128,256]{3,2,1,0:T(8,128)(2,1)S(1)} %get-tuple-element.56.grad_ref.first_ref.refs_0_), channel_id=1, source_target_pairs={{8,0},{16,8},{24,16},{9,1},{17,9},{25,17},{10,2},{18,10},{26,18},{... | collective-permute-start | bytes 1572872 | tf_op jit(solution)/shard_map/ppermute | solution.py:506
  101.1 7.5 %collective-permute-start.33 = (bf16[1,2,128,256]{3,2,1,0:T(8,128)(2,1)S(1)}, bf16[1,2,128,256]{3,2,1,0:T(8,128)(2,1)S(1)}, u32[]{:S(2)}, u32[]{:S(2)}) collective-permute-start(bf16[1,2,128,256]{3,2,1,0:T(8,128)(2,1)S(1)} %get-tuple-element.58), channel_id=1, source_target_pairs={{2,0},{4,2},{6,4},{3,1},{5,3},{7,5},{10,8},{12,10},{14,12},{11,9},... | collective-permute-start | bytes 393224 | tf_op jit(solution)/shard_map/ppermute | solution.py:506
  111.5 8.7 %collective-permute-start.34 = (bf16[2,2,128,256]{3,2,1,0:T(8,128)(2,1)S(1)}, bf16[2,2,128,256]{3,2,1,0:T(8,128)(2,1)S(1)}, u32[]{:S(2)}, u32[]{:S(2)}) collective-permute-start(bf16[2,2,128,256]{3,2,1,0:T(8,128)(2,1)S(1)} %shard_map.128.first_ref.refs_2_.refs_5_), channel_id=1, source_target_pairs={{8,0},{16,8},{24,16},{9,1},{17,9},{25,17},{10,2},{18,10},{26,18},{... | collective-permute-start | bytes 786440 | tf_op jit(solution)/shard_map/ppermute | solution.py:506
  113.9 11.9 %collective-permute-start.39 = (s16[2,16,32,128]{3,2,1,0:T(8,128)(2,1)S(1)}, s16[2,16,32,128]{3,2,1,0:T(8,128)(2,1)S(1)}, u32[]{:S(2)}, u32[]{:S(2)}) collective-permute-start(s16[2,16,32,128]{3,2,1,0:T(8,128)(2,1)S(1)} %get-tuple-element.63.refs_0_), channel_id=1, source_target_pairs={{0,2},{2,0},{4,6},{6,4},{1,3},{3,1},{5,7},{7,5},{8,10},{10,8},{12,... | collective-permute-start | bytes 786440 | tf_op jit(solution)/shard_map/ppermute | solution.py:588
  115.7 10.2 %collective-permute-start.40 = (s16[2,16,32,128]{3,2,1,0:T(8,128)(2,1)S(1)}, s16[2,16,32,128]{3,2,1,0:T(8,128)(2,1)S(1)}, u32[]{:S(2)}, u32[]{:S(2)}) collective-permute-start(s16[2,16,32,128]{3,2,1,0:T(8,128)(2,1)S(1)} %get-tuple-element.64), channel_id=1, source_target_pairs={{0,4},{2,6},{4,0},{6,2},{1,5},{3,7},{5,1},{7,3},{8,12},{10,14},{12... | collective-permute-start | bytes 786440 | tf_op jit(solution)/shard_map/ppermute | solution.py:588
  115.7 12.1 %collective-permute-start.41 = (s16[2,16,32,128]{3,2,1,0:T(8,128)(2,1)S(1)}, s16[2,16,32,128]{3,2,1,0:T(8,128)(2,1)S(1)}, u32[]{:S(2)}, u32[]{:S(2)}) collective-permute-start(s16[2,16,32,128]{3,2,1,0:T(8,128)(2,1)S(1)} %get-tuple-element.65), channel_id=1, source_target_pairs={{0,6},{2,4},{4,2},{6,0},{1,7},{3,5},{5,3},{7,1},{8,14},{10,12},{12... | collective-permute-start | bytes 786440 | tf_op jit(solution)/shard_map/ppermute | solution.py:588
  143.0 11.5 %collective-permute-start.49 = (s16[2,4,32,128]{3,2,1,0:T(8,128)(2,1)S(1)}, s16[2,4,32,128]{3,2,1,0:T(8,128)(2,1)S(1)}, u32[]{:S(2)}, u32[]{:S(2)}) collective-permute-start(s16[2,4,32,128]{3,2,1,0:T(8,128)(2,1)S(1)} %get-tuple-element.75.refs_0_), channel_id=1, source_target_pairs={{0,8},{8,0},{16,24},{24,16},{1,9},{9,1},{17,25},{25,17},{2,10},{10... | collective-permute-start | bytes 196616 | tf_op jit(solution)/shard_map/ppermute | solution.py:619
  143.9 10.7 %collective-permute-start.50 = (s16[2,4,32,128]{3,2,1,0:T(8,128)(2,1)S(1)}, s16[2,4,32,128]{3,2,1,0:T(8,128)(2,1)S(1)}, u32[]{:S(2)}, u32[]{:S(2)}) collective-permute-start(s16[2,4,32,128]{3,2,1,0:T(8,128)(2,1)S(1)} %get-tuple-element.75.refs_0_), channel_id=1, source_target_pairs={{0,16},{8,24},{16,0},{24,8},{1,17},{9,25},{17,1},{25,9},{2,18},{10... | collective-permute-start | bytes 196616 | tf_op jit(solution)/shard_map/ppermute | solution.py:619
  144.9 9.7 %collective-permute-start.51 = (s16[2,4,32,128]{3,2,1,0:T(8,128)(2,1)S(1)}, s16[2,4,32,128]{3,2,1,0:T(8,128)(2,1)S(1)}, u32[]{:S(2)}, u32[]{:S(2)}) collective-permute-start(s16[2,4,32,128]{3,2,1,0:T(8,128)(2,1)S(1)} %get-tuple-element.75.refs_0_), channel_id=1, source_target_pairs={{0,24},{8,16},{16,8},{24,0},{1,25},{9,17},{17,9},{25,1},{2,26},{10... | collective-permute-start | bytes 196616 | tf_op jit(solution)/shard_map/ppermute | solution.py:619
  157.8 10.0 %collective-permute-start.52 = (s16[16,32,128]{2,1,0:T(8,128)(2,1)S(1)}, s16[16,32,128]{2,1,0:T(8,128)(2,1)S(1)}, u32[]{:S(2)}, u32[]{:S(2)}) collective-permute-start(s16[16,32,128]{2,1,0:T(8,128)(2,1)S(1)} %bitcast.36), channel_id=1, source_target_pairs={{0,2},{2,0},{4,6},{6,4},{1,3},{3,1},{5,7},{7,5},{8,10},{10,8},{12,... | collective-permute-start | bytes 393224 | tf_op jit(solution)/shard_map/ppermute | solution.py:630
  158.2 9.6 %collective-permute-start.53 = (s16[16,32,128]{2,1,0:T(8,128)(2,1)S(1)}, s16[16,32,128]{2,1,0:T(8,128)(2,1)S(1)}, u32[]{:S(2)}, u32[]{:S(2)}) collective-permute-start(s16[16,32,128]{2,1,0:T(8,128)(2,1)S(1)} %bitcast.37), channel_id=1, source_target_pairs={{0,4},{2,6},{4,0},{6,2},{1,5},{3,7},{5,1},{7,3},{8,12},{10,14},{12... | collective-permute-start | bytes 393224 | tf_op jit(solution)/shard_map/ppermute | solution.py:630
  159.6 8.2 %collective-permute-start.54 = (s16[16,32,128]{2,1,0:T(8,128)(2,1)S(1)}, s16[16,32,128]{2,1,0:T(8,128)(2,1)S(1)}, u32[]{:S(2)}, u32[]{:S(2)}) collective-permute-start(s16[16,32,128]{2,1,0:T(8,128)(2,1)S(1)} %bitcast.38), channel_id=1, source_target_pairs={{0,6},{2,4},{4,2},{6,0},{1,7},{3,5},{5,3},{7,1},{8,14},{10,12},{12... | collective-permute-start | bytes 393224 | tf_op jit(solution)/shard_map/ppermute | solution.py:630
  163.0 8.4 %collective-permute-start.59 = (s16[64,32,128]{2,1,0:T(8,128)(2,1)S(1)}, s16[64,32,128]{2,1,0:T(8,128)(2,1)S(1)}, u32[]{:S(2)}, u32[]{:S(2)}) collective-permute-start(s16[64,32,128]{2,1,0:T(8,128)(2,1)S(1)} %bitcast.26), channel_id=1, source_target_pairs={{0,1},{1,0},{2,3},{3,2},{4,5},{5,4},{6,7},{7,6},{8,9},{9,8},{10,11... | collective-permute-start | bytes 1572872 | tf_op jit(solution)/shard_map/ppermute | solution.py:568
  168.4 6.9 %collective-permute-start.55 = (s16[64,32,128]{2,1,0:T(8,128)(2,1)S(1)}, s16[64,32,128]{2,1,0:T(8,128)(2,1)S(1)}, u32[]{:S(2)}, u32[]{:S(2)}) collective-permute-start(s16[64,32,128]{2,1,0:T(8,128)(2,1)S(1)} %bitcast.28), channel_id=1, source_target_pairs={{0,1},{1,0},{2,3},{3,2},{4,5},{5,4},{6,7},{7,6},{8,9},{9,8},{10,11... | collective-permute-start | bytes 1572872 | tf_op jit(solution)/shard_map/ppermute | solution.py:568
  (35 other events, 151.1 us)

commit v14 on v13

--- a/solution.py
+++ b/solution.py
@@ -120,6 +120,12 @@
     for which, out in enumerate(refs[-above_ref.shape[0] :]):
         out[0] = above_ref[which]
         out[1] = below_ref[which]
+
+
+def rows_and_term_kernel(above_ref, below_ref, after, theirs_ref, near_ref, term_ref):
+    near_ref[0] = above_ref[0]
+    near_ref[1] = below_ref[0]
+    term_ref[...] = encoded(theirs_ref[...])
 
 
 def source(own, other, near, far, other_first):
@@ -336,7 +342,8 @@
     for which in range(2):
         mine, other = refs[2 * which], refs[2 * which + 1]
         for k, out in enumerate(refs[4:]):
-            total = mine[me ^ k] + other[me ^ k]
+            total = other[me ^ k]
+            total = mine[me ^ k] + (total if total.dtype == F32 else decoded_value(total))
             out[which] = total if k == 0 else encoded(total)
 
 
@@ -577,7 +584,7 @@
     axis, _, exchanges = weight_rounds()[0]
     parts = len(exchanges) + 1
     rows = half // parts
-    terms = [part for mine, theirs in (second, first) for part in (mine, swapped(theirs))]
+    terms = [part for mine, theirs in (second, first) for part in (mine, theirs)]
     part = (2, rows, SLOTS, channels)
     kept, *sent = call(
         functools.partial(first_scatter_kernel, slot=4),
@@ -775,11 +782,18 @@
         scratch=[pltpu.VMEM((rows * cols, frames * channels), BF16)],
         flops=conv_flops,
     )
-    (near,) = row_halos(down, up, (future, halves_first[0]))
-    around = (future, near, shifted(near, "tm", -1))
     halves_second, halves_first = (
         [v.reshape(channels // 2, SLOTS, channels) for v in halves] for halves in (halves_second, halves_first)
     )
+    near, term = call(
+        rows_and_term_kernel,
+        [shape((2, frames, channels, cols), BF16), shape(halves_first[1].shape, jnp.int16)],
+        [VMEM] * 4,
+        (shifted(down, "height", 1), shifted(up, "height", -1), future, halves_first[1]),
+    )
+    around = (future, near, shifted(near, "tm", -1))
+    halves_second = halves_second[0], swapped(halves_second[1])
+    halves_first = halves_first[0], swapped(term)
     weights, sent = scattered(flags, halves_second, halves_first)
     around = with_columns(flags, hidden_grad, around, (sent,))
     scaled, sums_first = call(

time: 180 us -> 177 us (0.983)
  starting transfers between devices: 91.7 us -> 89.3 us
    ppermute x10, waiting for transfers between devices: 14.1 us -> 10.1 us  [shifted(): lax.ppermute(value, axis, [(source, source + steps) for source in range(i...]
    ppermute x11, starting transfers between devices: 17.1 us -> 15.1 us  [all_sum(): parts = [value] + [lax.ppermute(value, axis, pairs) for pairs in exchanges]]
  transfers between devices with their start and end apart: 60 -> 60, of which waited for: 19 -> 19; matrix products, arithmetic and copies ran while one was open for 0% -> 0% of each run, Pallas kernels for 20% -> 21%
where the time goes in v14:
time: 177 us; the launch traced here: 176 us
  starting transfers between devices  89.3 us (50%)
  Pallas kernels  50.6 us (29%)
  waiting for transfers between devices  29.4 us (17%)
  local copies, waits for them, and re-layouts  4.96 us (3%)
    pallas_call x30, Pallas kernels, call(): pl.pallas_call(body, out_shape=tuple(outs), in_specs=specs, out_specs=tup...  50.6 us
    ppermute x14, starting transfers between devices, all_stats(): parts = [value] + [lax.ppermute(value, axis, pairs) for pairs in exchanges]  23.5 us
    ppermute x10, starting transfers between devices, shifted(): lax.ppermute(value, axis, [(source, source + steps) for source in range(i...  20.7 us
    ppermute x11, starting transfers between devices, all_sum(): parts = [value] + [lax.ppermute(value, axis, pairs) for pairs in exchanges]  15.1 us
    ppermute x10, starting transfers between devices, swapped(): return lax.ppermute(value, 'width', [(0, 1), (1, 0)])  13 us
    ppermute x10, waiting for transfers between devices, shifted(): lax.ppermute(value, axis, [(source, source + steps) for source in range(i...  10.1 us
    ppermute x6, starting transfers between devices, gathered(): pieces = [value] + [lax.ppermute(value, axis, pairs) for pairs in exchanges]  5.36 us
    ppermute x14, waiting for transfers between devices, all_stats(): parts = [value] + [lax.ppermute(value, axis, pairs) for pairs in exchanges]  4.81 us
  transfers between devices with their start and end apart: 60, of which 19 were waited for; matrix products, arithmetic and copies ran while one was open for 0% of the time, Pallas kernels for 21%

profile of v14, /device:TPU:1, one launch (start us, length us, event | category | flops | bytes accessed | tf_op | source)
XLA Modules:
  0.0 176.2 jit_solution(716422412086251222)
XLA Ops:
  4.3 2.6 %shard_map.112 = (bf16[4,2,128,256]{3,2,1,0:T(8,128)(2,1)S(1)}, bf16[4,2,128,256]{3,2,1,0:T(8,128)(2,1)S(1)}, bf16[2,2,128,256]{3,2,1,0:T(8,128)(2,1)S(1)}, bf16...) custom-call(bf16[128,2,4,256]{3,2,1,0:T(4,128)(2,1)S(1)} %copy-done.3, bf16[128,2,4,256]{3,2,1,0:T(4,128)(2,1)S(1)} %copy-done.4, ...), custom_call_target="tpu_custom_call" | custom-call | bytes 2626560 | tf_op jit(solution)/shard_map/pallas_call | solution.py:24
  7.0 2.2 %collective-permute-start.6 = (f32[1,2,128]{2,1,0:T(2,128)S(1)}, f32[1,2,128]{2,1,0:T(2,128)S(1)}, u32[]{:S(2)}, u32[]{:S(2)}) collective-permute-start(f32[1,2,128]{2,1,0:T(2,128)S(1)} %get-tuple-element.47), channel_id=1, source_target_pairs={{0,8},{8,0},{16,24},{24,16},{1,9},{9,1},{17,25},{25,17},{2,10},{10... | collective-permute-start | bytes 3080 | tf_op jit(solution)/shard_map/ppermute | solution.py:558
  9.2 2.3 %collective-permute-start.7 = (f32[1,2,128]{2,1,0:T(2,128)S(1)}, f32[1,2,128]{2,1,0:T(2,128)S(1)}, u32[]{:S(2)}, u32[]{:S(2)}) collective-permute-start(f32[1,2,128]{2,1,0:T(2,128)S(1)} %get-tuple-element.47), channel_id=1, source_target_pairs={{0,16},{8,24},{16,0},{24,8},{1,17},{9,25},{17,1},{25,9},{2,18},{10... | collective-permute-start | bytes 3080 | tf_op jit(solution)/shard_map/ppermute | solution.py:558
  11.5 3.1 %collective-permute-start.1 = (bf16[2,2,128,256]{3,2,1,0:T(8,128)(2,1)S(1)}, bf16[2,2,128,256]{3,2,1,0:T(8,128)(2,1)S(1)}, u32[]{:S(2)}, u32[]{:S(2)}) collective-permute-start(bf16[2,2,128,256]{3,2,1,0:T(8,128)(2,1)S(1)} %get-tuple-element.44), channel_id=1, source_target_pairs={{0,2},{2,4},{4,6},{1,3},{3,5},{5,7},{8,10},{10,12},{12,14},{9,11},... | collective-permute-start | bytes 786440 | tf_op jit(solution)/shard_map/ppermute | solution.py:513
  16.0 3.1 %collective-permute-start.10 = (f32[1,2,128]{2,1,0:T(2,128)S(1)}, f32[1,2,128]{2,1,0:T(2,128)S(1)}, u32[]{:S(2)}, u32[]{:S(2)}) collective-permute-start(f32[1,2,128]{2,1,0:T(2,128)S(1)} %pad_maximum_fusion), channel_id=1, source_target_pairs={{0,4},{2,6},{4,0},{6,2},{1,5},{3,7},{5,1},{7,3},{8,12},{10,14},{12... | collective-permute-start | bytes 3080 | tf_op jit(solution)/shard_map/ppermute | solution.py:558
  20.3 3.1 %collective-permute-start = (bf16[4,2,128,256]{3,2,1,0:T(8,128)(2,1)S(1)}, bf16[4,2,128,256]{3,2,1,0:T(8,128)(2,1)}, u32[]{:S(2)}, u32[]{:S(2)}) collective-permute-start(bf16[4,2,128,256]{3,2,1,0:T(8,128)(2,1)S(1)} %get-tuple-element.43.first_ref.own.refs_7_.latent), channel_id=1, source_target_pairs={{0,8},{8,16},{16,24},{1,9},{9,17},{17,25},{2,10},{10,18},{18,26},{... | collective-permute-start | bytes 1572872 | tf_op jit(solution)/shard_map/ppermute | solution.py:513
  27.8 3.1 %collective-permute-start.3 = (bf16[2,2,128,256]{3,2,1,0:T(8,128)(2,1)}, bf16[2,2,128,256]{3,2,1,0:T(8,128)(2,1)}, u32[]{:S(2)}, u32[]{:S(2)}) collective-permute-start(bf16[2,2,128,256]{3,2,1,0:T(8,128)(2,1)} %get-tuple-element.46.first_ref.near), channel_id=1, source_target_pairs={{0,8},{8,16},{16,24},{1,9},{9,17},{17,25},{2,10},{10,18},{18,26},{... | collective-permute-start | bytes 786440 | tf_op jit(solution)/shard_map/ppermute | solution.py:513
  30.9 3.5 %collective-permute-start.12 = (f32[1,2,128]{2,1,0:T(2,128)S(1)}, f32[1,2,128]{2,1,0:T(2,128)S(1)}, u32[]{:S(2)}, u32[]{:S(2)}) collective-permute-start(f32[1,2,128]{2,1,0:T(2,128)S(1)} %pad_maximum_fusion.1), channel_id=1, source_target_pairs={{0,1},{1,0},{2,3},{3,2},{4,5},{5,4},{6,7},{7,6},{8,9},{9,8},{10,11... | collective-permute-start | bytes 3080 | tf_op jit(solution)/shard_map/ppermute | solution.py:558
  38.7 3.1 %collective-permute-start.5 = (bf16[128,128]{1,0:T(8,128)(2,1)S(1)}, bf16[128,128]{1,0:T(8,128)(2,1)S(1)}, u32[]{:S(2)}, u32[]{:S(2)}) collective-permute-start(bf16[128,128]{1,0:T(8,128)(2,1)S(1)} %shard_map.115), channel_id=1, source_target_pairs={{0,1},{1,0},{2,3},{3,2},{4,5},{5,4},{6,7},{7,6},{8,9},{9,8},{10,11... | collective-permute-start | bytes 98312 | tf_op jit(solution)/shard_map/ppermute | solution.py:575
  45.8 5.2 %shard_map.117 = (f32[4,2,128,256]{3,2,1,0:T(8,128)S(1)}, f32[1,2,128]{2,1,0:T(2,128)S(1)}, bf16[6,4,384,256]{3,2,1,0:T(8,128)(2,1)S(1)}) custom-call(s32[6]{0:T(128)S(1)} %stack.57.flag_ref, bf16[4,2,128,256]{3,2,1,0:T(8,128)(2,1)S(1)} %get-tuple-element.43.first_ref.own.refs_7_.latent, bf16[4,2,128,256]{3,2,1,0:T(8,128)(2,1)} %collective-permute-done.second_ref.past, ...), custom_call_target="tpu_custom_call" | custom-call | flops 7247757312 | bytes 10033176 | tf_op jit(solution)/shard_map/pallas_call | solution.py:24
  56.8 3.0 %collective-permute-start.18 = (f32[1,2,128]{2,1,0:T(2,128)S(1)}, f32[1,2,128]{2,1,0:T(2,128)S(1)}, u32[]{:S(2)}, u32[]{:S(2)}) collective-permute-start(f32[1,2,128]{2,1,0:T(2,128)S(1)} %get-tuple-element.51.refs_0_), channel_id=1, source_target_pairs={{0,16},{8,24},{16,0},{24,8},{1,17},{9,25},{17,1},{25,9},{2,18},{10... | collective-permute-start | bytes 3080 | tf_op jit(solution)/shard_map/ppermute | solution.py:558
  59.8 3.9 %shard_map.121 = (f32[4,2,128,256]{3,2,1,0:T(8,128)S(1)}, bf16[6,4,384,256]{3,2,1,0:T(8,128)(2,1)S(1)}) custom-call(s32[6]{0:T(128)S(1)} %stack.57.flag_ref, bf16[4,2,128,256]{3,2,1,0:T(8,128)(2,1)S(1)} %get-tuple-element.50.first_ref.refs_0_.cotangent, bf16[4,2,128,256]{3,2,1,0:T(8,128)(2,1)} %collective-permute-done.14.second_ref.refs_1_, ...), custom_call_target="tpu_custom_call" | custom-call | flops 7247757312 | bytes 9764888 | tf_op jit(solution)/shard_map/pallas_call | solution.py:24
  64.0 2.6 %collective-permute-start.20 = (f32[1,2,128]{2,1,0:T(2,128)S(1)}, f32[1,2,128]{2,1,0:T(2,128)S(1)}, u32[]{:S(2)}, u32[]{:S(2)}) collective-permute-start(f32[1,2,128]{2,1,0:T(2,128)S(1)} %shard_map.122), channel_id=1, source_target_pairs={{0,2},{2,0},{4,6},{6,4},{1,3},{3,1},{5,7},{7,5},{8,10},{10,8},{12,... | collective-permute-start | bytes 3080 | tf_op jit(solution)/shard_map/ppermute | solution.py:558
  70.0 2.9 %collective-permute-start.23 = (f32[1,2,128]{2,1,0:T(2,128)S(1)}, f32[1,2,128]{2,1,0:T(2,128)S(1)}, u32[]{:S(2)}, u32[]{:S(2)}) collective-permute-start(f32[1,2,128]{2,1,0:T(2,128)S(1)} %pad_maximum_fusion.3), channel_id=1, source_target_pairs={{0,1},{1,0},{2,3},{3,2},{4,5},{5,4},{6,7},{7,6},{8,9},{9,8},{10,11... | collective-permute-start | bytes 3080 | tf_op jit(solution)/shard_map/ppermute | solution.py:558
  74.7 2.4 %collective-permute-start.25 = (f32[1,2,128]{2,1,0:T(2,128)S(1)}, f32[1,2,128]{2,1,0:T(2,128)S(1)}, u32[]{:S(2)}, u32[]{:S(2)}) collective-permute-start(f32[1,2,128]{2,1,0:T(2,128)S(1)} %get-tuple-element.54.refs_0_), channel_id=1, source_target_pairs={{0,16},{8,24},{16,0},{24,8},{1,17},{9,25},{17,1},{25,9},{2,18},{10... | collective-permute-start | bytes 3080 | tf_op jit(solution)/shard_map/ppermute | solution.py:542
  78.2 4.3 %shard_map.124 = (f32[2048,128]{1,0:T(8,128)S(1)}, f32[2048,128]{1,0:T(8,128)S(1)}) custom-call(s32[6]{0:T(128)S(1)} %stack.57.flag_ref, bf16[6,4,384,256]{3,2,1,0:T(8,128)(2,1)S(1)} %get-tuple-element.55.stack_ref, bf16[4,2,128,256]{3,2,1,0:T(8,128)(2,1)S(1)} %get-tuple-element.56.act_ref), custom_call_target="tpu_custom_call" | custom-call | flops 7247757312 | bytes 7340056 | tf_op jit(solution)/shard_map/pallas_call | solution.py:24
  87.8 2.6 %collective-permute-start.30 = (f32[1,2,128]{2,1,0:T(2,128)S(1)}, f32[1,2,128]{2,1,0:T(2,128)S(1)}, u32[]{:S(2)}, u32[]{:S(2)}) collective-permute-start(f32[1,2,128]{2,1,0:T(2,128)S(1)} %add_add_fusion.1), channel_id=1, source_target_pairs={{0,1},{1,0},{2,3},{3,2},{4,5},{5,4},{6,7},{7,6},{8,9},{9,8},{10,11... | collective-permute-start | bytes 3080 | tf_op jit(solution)/shard_map/ppermute | solution.py:542
  93.0 3.6 %collective-permute-start.32 = (bf16[1,2,128,256]{3,2,1,0:T(8,128)(2,1)S(1)}, bf16[1,2,128,256]{3,2,1,0:T(8,128)(2,1)S(1)}, u32[]{:S(2)}, u32[]{:S(2)}) collective-permute-start(bf16[1,2,128,256]{3,2,1,0:T(8,128)(2,1)S(1)} %get-tuple-element.59), channel_id=1, source_target_pairs={{0,2},{2,4},{4,6},{1,3},{3,5},{5,7},{8,10},{10,12},{12,14},{9,11},... | collective-permute-start | bytes 393224 | tf_op jit(solution)/shard_map/ppermute | solution.py:513
  97.9 4.6 %shard_map.127 = (f32[2048,128]{1,0:T(8,128)S(1)}, f32[2048,128]{1,0:T(8,128)S(1)}) custom-call(s32[6]{0:T(128)S(1)} %stack.57.flag_ref, bf16[6,4,384,256]{3,2,1,0:T(8,128)(2,1)S(1)} %get-tuple-element.61.stack_ref, bf16[4,2,128,256]{3,2,1,0:T(8,128)(2,1)S(1)} %get-tuple-element.58.grad_ref.first_ref.refs_0_), custom_call_target="tpu_custom_call" | custom-call | flops 7247757312 | bytes 7340056 | tf_op jit(solution)/shard_map/pallas_call | solution.py:24
  104.0 2.8 %collective-permute-done.31.after.second_ref.refs_1_.refs_4_ = bf16[4,2,128,256]{3,2,1,0:T(8,128)(2,1)S(1)} collective-permute-done((bf16[4,2,128,256]{3,2,1,0:T(8,128)(2,1)S(1)}, bf16[4,2,128,256]{3,2,1,0:T(8,128)(2,1)S(1)}, u32[]{:S(2)}, u32[]{:S(2)}) %collective-permute-start.31) | collective-permute-done | bytes 524320 | tf_op jit(solution)/shard_map/ppermute | solution.py:513
  114.1 4.0 %collective-permute-done.34.second_ref.refs_3_ = bf16[2,2,128,256]{3,2,1,0:T(8,128)(2,1)S(1)} collective-permute-done((bf16[2,2,128,256]{3,2,1,0:T(8,128)(2,1)S(1)}, bf16[2,2,128,256]{3,2,1,0:T(8,128)(2,1)S(1)}, u32[]{:S(2)}, u32[]{:S(2)}) %collective-permute-start.34) | collective-permute-done | bytes 262176 | tf_op jit(solution)/shard_map/ppermute | solution.py:513
  122.7 3.0 %collective-permute-done.41.refs_12_ = s16[2,16,32,128]{3,2,1,0:T(8,128)(2,1)S(1)} collective-permute-done((s16[2,16,32,128]{3,2,1,0:T(8,128)(2,1)S(1)}, s16[2,16,32,128]{3,2,1,0:T(8,128)(2,1)S(1)}, u32[]{:S(2)}, u32[]{:S(2)}) %collective-permute-start.41) | collective-permute-done | bytes 262176 | tf_op jit(solution)/shard_map/ppermute | solution.py:595
  125.7 4.0 %shard_map.133 = (f32[4,2,128,256]{3,2,1,0:T(8,128)S(1)}, f32[1,2,128]{2,1,0:T(2,128)S(1)}) custom-call(s32[6]{0:T(128)S(1)} %stack.57.flag_ref, bf16[4,2,128,256]{3,2,1,0:T(8,128)(2,1)S(1)} %get-tuple-element.58.grad_ref.first_ref.refs_0_, bf16[4,2,128,256]{3,2,1,0:T(8,128)(2,1)S(1)} %collective-permute-done.31.after.second_ref.refs_1_.refs_4_, ...), custom_call_target="tpu_custom_call" | custom-call | flops 7247757312 | bytes 6363160 | tf_op jit(solution)/shard_map/pallas_call | solution.py:24
  132.6 2.2 %collective-permute-start.44 = (s16[2,4,32,128]{3,2,1,0:T(8,128)(2,1)S(1)}, s16[2,4,32,128]{3,2,1,0:T(8,128)(2,1)S(1)}, u32[]{:S(2)}, u32[]{:S(2)}) collective-permute-start(s16[2,4,32,128]{3,2,1,0:T(8,128)(2,1)S(1)} %get-tuple-element.76), channel_id=1, source_target_pairs={{0,24},{8,16},{16,8},{24,0},{1,25},{9,17},{17,9},{25,1},{2,26},{10... | collective-permute-start | bytes 196616 | tf_op jit(solution)/shard_map/ppermute | solution.py:613
  134.8 4.2 %collective-permute-done.43.refs_2_ = s16[2,4,32,128]{3,2,1,0:T(8,128)(2,1)S(1)} collective-permute-done((s16[2,4,32,128]{3,2,1,0:T(8,128)(2,1)S(1)}, s16[2,4,32,128]{3,2,1,0:T(8,128)(2,1)S(1)}, u32[]{:S(2)}, u32[]{:S(2)}) %collective-permute-start.43) | collective-permute-done | bytes 65568 | tf_op jit(solution)/shard_map/ppermute | solution.py:613
  141.8 2.4 %collective-permute-start.49 = (s16[2,4,32,128]{3,2,1,0:T(8,128)(2,1)S(1)}, s16[2,4,32,128]{3,2,1,0:T(8,128)(2,1)S(1)}, u32[]{:S(2)}, u32[]{:S(2)}) collective-permute-start(s16[2,4,32,128]{3,2,1,0:T(8,128)(2,1)S(1)} %get-tuple-element.79.refs_0_), channel_id=1, source_target_pairs={{0,8},{8,0},{16,24},{24,16},{1,9},{9,1},{17,25},{25,17},{2,10},{10... | collective-permute-start | bytes 196616 | tf_op jit(solution)/shard_map/ppermute | solution.py:626
  144.2 2.1 %collective-permute-start.51 = (s16[2,4,32,128]{3,2,1,0:T(8,128)(2,1)S(1)}, s16[2,4,32,128]{3,2,1,0:T(8,128)(2,1)S(1)}, u32[]{:S(2)}, u32[]{:S(2)}) collective-permute-start(s16[2,4,32,128]{3,2,1,0:T(8,128)(2,1)S(1)} %get-tuple-element.79.refs_0_), channel_id=1, source_target_pairs={{0,24},{8,16},{16,8},{24,0},{1,25},{9,17},{17,9},{25,1},{2,26},{10... | collective-permute-start | bytes 196616 | tf_op jit(solution)/shard_map/ppermute | solution.py:626
  146.3 3.3 %collective-permute-start.48 = (f32[1,2,128]{2,1,0:T(2,128)S(1)}, f32[1,2,128]{2,1,0:T(2,128)S(1)}, u32[]{:S(2)}, u32[]{:S(2)}) collective-permute-start(f32[1,2,128]{2,1,0:T(2,128)S(1)} %add_add_fusion), channel_id=1, source_target_pairs={{0,1},{1,0},{2,3},{3,2},{4,5},{5,4},{6,7},{7,6},{8,9},{9,8},{10,11... | collective-permute-start | bytes 3080 | tf_op jit(solution)/shard_map/ppermute | solution.py:542
  160.1 3.9 %collective-permute-start.59 = (s16[64,32,128]{2,1,0:T(8,128)(2,1)S(1)}, s16[64,32,128]{2,1,0:T(8,128)(2,1)S(1)}, u32[]{:S(2)}, u32[]{:S(2)}) collective-permute-start(s16[64,32,128]{2,1,0:T(8,128)(2,1)S(1)} %bitcast.25), channel_id=1, source_target_pairs={{0,1},{1,0},{2,3},{3,2},{4,5},{5,4},{6,7},{7,6},{8,9},{9,8},{10,11... | collective-permute-start | bytes 1572872 | tf_op jit(solution)/shard_map/ppermute | solution.py:575
  165.7 2.7 %collective-permute-start.55 = (s16[64,32,128]{2,1,0:T(8,128)(2,1)S(1)}, s16[64,32,128]{2,1,0:T(8,128)(2,1)S(1)}, u32[]{:S(2)}, u32[]{:S(2)}) collective-permute-start(s16[64,32,128]{2,1,0:T(8,128)(2,1)S(1)} %bitcast.27), channel_id=1, source_target_pairs={{0,1},{1,0},{2,3},{3,2},{4,5},{5,4},{6,7},{7,6},{8,9},{9,8},{10,11... | collective-permute-start | bytes 1572872 | tf_op jit(solution)/shard_map/ppermute | solution.py:575
  168.4 3.9 %shard_map.141 = f32[128,3456]{1,0:T(8,128)} custom-call(s32[6]{0:T(128)S(1)} %stack.57.flag_ref, s16[64,32,128]{2,1,0:T(8,128)(2,1)S(1)} %bitcast.26, s16[64,32,128]{2,1,0:T(8,128)(2,1)S(1)} %collective-permute-done.59.theirs_ref), custom_call_target="tpu_custom_call" | custom-call | bytes 2818072 | tf_op jit(solution)/shard_map/pallas_call | solution.py:24
  172.3 3.9 %shard_map.139 = f32[128,3456]{1,0:T(8,128)} custom-call(s32[6]{0:T(128)S(1)} %stack.57.flag_ref, s16[64,32,128]{2,1,0:T(8,128)(2,1)S(1)} %bitcast.28, s16[64,32,128]{2,1,0:T(8,128)(2,1)S(1)} %collective-permute-done.55.theirs_ref), custom_call_target="tpu_custom_call" | custom-call | bytes 2818072 | tf_op jit(solution)/shard_map/pallas_call | solution.py:24
  (153 shorter events, 71.6 us)
Async XLA Ops:
  7.0 8.9 %collective-permute-start.6 = (f32[1,2,128]{2,1,0:T(2,128)S(1)}, f32[1,2,128]{2,1,0:T(2,128)S(1)}, u32[]{:S(2)}, u32[]{:S(2)}) collective-permute-start(f32[1,2,128]{2,1,0:T(2,128)S(1)} %get-tuple-element.47), channel_id=1, source_target_pairs={{0,8},{8,0},{16,24},{24,16},{1,9},{9,1},{17,25},{25,17},{2,10},{10... | collective-permute-start | bytes 3080 | tf_op jit(solution)/shard_map/ppermute | solution.py:558
  9.2 6.8 %collective-permute-start.7 = (f32[1,2,128]{2,1,0:T(2,128)S(1)}, f32[1,2,128]{2,1,0:T(2,128)S(1)}, u32[]{:S(2)}, u32[]{:S(2)}) collective-permute-start(f32[1,2,128]{2,1,0:T(2,128)S(1)} %get-tuple-element.47), channel_id=1, source_target_pairs={{0,16},{8,24},{16,0},{24,8},{1,17},{9,25},{17,1},{25,9},{2,18},{10... | collective-permute-start | bytes 3080 | tf_op jit(solution)/shard_map/ppermute | solution.py:558
  11.5 14.9 %collective-permute-start.1 = (bf16[2,2,128,256]{3,2,1,0:T(8,128)(2,1)S(1)}, bf16[2,2,128,256]{3,2,1,0:T(8,128)(2,1)S(1)}, u32[]{:S(2)}, u32[]{:S(2)}) collective-permute-start(bf16[2,2,128,256]{3,2,1,0:T(8,128)(2,1)S(1)} %get-tuple-element.44), channel_id=1, source_target_pairs={{0,2},{2,4},{4,6},{1,3},{3,5},{5,7},{8,10},{10,12},{12,14},{9,11},... | collective-permute-start | bytes 786440 | tf_op jit(solution)/shard_map/ppermute | solution.py:513
  14.6 11.7 %collective-permute-start.2 = (bf16[2,2,128,256]{3,2,1,0:T(8,128)(2,1)S(1)}, bf16[2,2,128,256]{3,2,1,0:T(8,128)(2,1)S(1)}, u32[]{:S(2)}, u32[]{:S(2)}) collective-permute-start(bf16[2,2,128,256]{3,2,1,0:T(8,128)(2,1)S(1)} %get-tuple-element.45), channel_id=1, source_target_pairs={{2,0},{4,2},{6,4},{3,1},{5,3},{7,5},{10,8},{12,10},{14,12},{11,9},... | collective-permute-start | bytes 786440 | tf_op jit(solution)/shard_map/ppermute | solution.py:513
  19.3 7.0 %collective-permute-start.9 = (f32[1,2,128]{2,1,0:T(2,128)S(1)}, f32[1,2,128]{2,1,0:T(2,128)S(1)}, u32[]{:S(2)}, u32[]{:S(2)}) collective-permute-start(f32[1,2,128]{2,1,0:T(2,128)S(1)} %pad_maximum_fusion), channel_id=1, source_target_pairs={{0,2},{2,0},{4,6},{6,4},{1,3},{3,1},{5,7},{7,5},{8,10},{10,8},{12,... | collective-permute-start | bytes 3080 | tf_op jit(solution)/shard_map/ppermute | solution.py:558
  20.3 21.5 %collective-permute-start = (bf16[4,2,128,256]{3,2,1,0:T(8,128)(2,1)S(1)}, bf16[4,2,128,256]{3,2,1,0:T(8,128)(2,1)}, u32[]{:S(2)}, u32[]{:S(2)}) collective-permute-start(bf16[4,2,128,256]{3,2,1,0:T(8,128)(2,1)S(1)} %get-tuple-element.43.first_ref.own.refs_7_.latent), channel_id=1, source_target_pairs={{0,8},{8,16},{16,24},{1,9},{9,17},{17,25},{2,10},{10,18},{18,26},{... | collective-permute-start | bytes 1572872 | tf_op jit(solution)/shard_map/ppermute | solution.py:513
  23.4 29.5 %collective-permute-start.14 = (bf16[4,2,128,256]{3,2,1,0:T(8,128)(2,1)S(1)}, bf16[4,2,128,256]{3,2,1,0:T(8,128)(2,1)}, u32[]{:S(2)}, u32[]{:S(2)}) collective-permute-start(bf16[4,2,128,256]{3,2,1,0:T(8,128)(2,1)S(1)} %get-tuple-element.50.first_ref.refs_0_.cotangent), channel_id=1, source_target_pairs={{8,0},{16,8},{24,16},{9,1},{17,9},{25,17},{10,2},{18,10},{26,18},{... | collective-permute-start | bytes 1572872 | tf_op jit(solution)/shard_map/ppermute | solution.py:513
  27.8 9.5 %collective-permute-start.3 = (bf16[2,2,128,256]{3,2,1,0:T(8,128)(2,1)}, bf16[2,2,128,256]{3,2,1,0:T(8,128)(2,1)}, u32[]{:S(2)}, u32[]{:S(2)}) collective-permute-start(bf16[2,2,128,256]{3,2,1,0:T(8,128)(2,1)} %get-tuple-element.46.first_ref.near), channel_id=1, source_target_pairs={{0,8},{8,16},{16,24},{1,9},{9,17},{17,25},{2,10},{10,18},{18,26},{... | collective-permute-start | bytes 786440 | tf_op jit(solution)/shard_map/ppermute | solution.py:513
  35.8 10.0 %collective-permute-start.13 = (bf16[2,2,128,256]{3,2,1,0:T(8,128)(2,1)}, bf16[2,2,128,256]{3,2,1,0:T(8,128)(2,1)S(1)}, u32[]{:S(2)}, u32[]{:S(2)}) collective-permute-start(bf16[2,2,128,256]{3,2,1,0:T(8,128)(2,1)} %copy-done.5), channel_id=1, source_target_pairs={{8,0},{16,8},{24,16},{9,1},{17,9},{25,17},{10,2},{18,10},{26,18},{... | collective-permute-start | bytes 786440 | tf_op jit(solution)/shard_map/ppermute | solution.py:513
  38.7 7.1 %collective-permute-start.5 = (bf16[128,128]{1,0:T(8,128)(2,1)S(1)}, bf16[128,128]{1,0:T(8,128)(2,1)S(1)}, u32[]{:S(2)}, u32[]{:S(2)}) collective-permute-start(bf16[128,128]{1,0:T(8,128)(2,1)S(1)} %shard_map.115), channel_id=1, source_target_pairs={{0,1},{1,0},{2,3},{3,2},{4,5},{5,4},{6,7},{7,6},{8,9},{9,8},{10,11... | collective-permute-start | bytes 98312 | tf_op jit(solution)/shard_map/ppermute | solution.py:575
  52.0 7.8 %collective-permute-start.16 = (bf16[128,128]{1,0:T(8,128)(2,1)S(1)}, bf16[128,128]{1,0:T(8,128)(2,1)S(1)}, u32[]{:S(2)}, u32[]{:S(2)}) collective-permute-start(bf16[128,128]{1,0:T(8,128)(2,1)S(1)} %shard_map.119), channel_id=1, source_target_pairs={{0,1},{1,0},{2,3},{3,2},{4,5},{5,4},{6,7},{7,6},{8,9},{9,8},{10,11... | collective-permute-start | bytes 98312 | tf_op jit(solution)/shard_map/ppermute | solution.py:575
  55.3 8.4 %collective-permute-start.17 = (f32[1,2,128]{2,1,0:T(2,128)S(1)}, f32[1,2,128]{2,1,0:T(2,128)S(1)}, u32[]{:S(2)}, u32[]{:S(2)}) collective-permute-start(f32[1,2,128]{2,1,0:T(2,128)S(1)} %get-tuple-element.51.refs_0_), channel_id=1, source_target_pairs={{0,8},{8,0},{16,24},{24,16},{1,9},{9,1},{17,25},{25,17},{2,10},{10... | collective-permute-start | bytes 3080 | tf_op jit(solution)/shard_map/ppermute | solution.py:558
  56.8 7.0 %collective-permute-start.18 = (f32[1,2,128]{2,1,0:T(2,128)S(1)}, f32[1,2,128]{2,1,0:T(2,128)S(1)}, u32[]{:S(2)}, u32[]{:S(2)}) collective-permute-start(f32[1,2,128]{2,1,0:T(2,128)S(1)} %get-tuple-element.51.refs_0_), channel_id=1, source_target_pairs={{0,16},{8,24},{16,0},{24,8},{1,17},{9,25},{17,1},{25,9},{2,18},{10... | collective-permute-start | bytes 3080 | tf_op jit(solution)/shard_map/ppermute | solution.py:558
  74.6 7.9 %collective-permute-start.24 = (f32[1,2,128]{2,1,0:T(2,128)S(1)}, f32[1,2,128]{2,1,0:T(2,128)S(1)}, u32[]{:S(2)}, u32[]{:S(2)}) collective-permute-start(f32[1,2,128]{2,1,0:T(2,128)S(1)} %get-tuple-element.54.refs_0_), channel_id=1, source_target_pairs={{0,8},{8,0},{16,24},{24,16},{1,9},{9,1},{17,25},{25,17},{2,10},{10... | collective-permute-start | bytes 3080 | tf_op jit(solution)/shard_map/ppermute | solution.py:542
  74.7 7.9 %collective-permute-start.25 = (f32[1,2,128]{2,1,0:T(2,128)S(1)}, f32[1,2,128]{2,1,0:T(2,128)S(1)}, u32[]{:S(2)}, u32[]{:S(2)}) collective-permute-start(f32[1,2,128]{2,1,0:T(2,128)S(1)} %get-tuple-element.54.refs_0_), channel_id=1, source_target_pairs={{0,16},{8,24},{16,0},{24,8},{1,17},{9,25},{17,1},{25,9},{2,18},{10... | collective-permute-start | bytes 3080 | tf_op jit(solution)/shard_map/ppermute | solution.py:542
  90.4 19.2 %collective-permute-start.35 = (f32[64,32,128]{2,1,0:T(8,128)S(1)}, f32[64,32,128]{2,1,0:T(8,128)S(1)}, u32[]{:S(2)}, u32[]{:S(2)}) collective-permute-start(f32[64,32,128]{2,1,0:T(8,128)S(1)} %bitcast.45), channel_id=1, source_target_pairs={{0,1},{1,0},{2,3},{3,2},{4,5},{5,4},{6,7},{7,6},{8,9},{9,8},{10,11... | collective-permute-start | bytes 3145736 | tf_op jit(solution)/shard_map/ppermute | solution.py:575
  91.7 15.1 %collective-permute-start.31 = (bf16[4,2,128,256]{3,2,1,0:T(8,128)(2,1)S(1)}, bf16[4,2,128,256]{3,2,1,0:T(8,128)(2,1)S(1)}, u32[]{:S(2)}, u32[]{:S(2)}) collective-permute-start(bf16[4,2,128,256]{3,2,1,0:T(8,128)(2,1)S(1)} %get-tuple-element.58.grad_ref.first_ref.refs_0_), channel_id=1, source_target_pairs={{8,0},{16,8},{24,16},{9,1},{17,9},{25,17},{10,2},{18,10},{26,18},{... | collective-permute-start | bytes 1572872 | tf_op jit(solution)/shard_map/ppermute | solution.py:513
  93.0 9.5 %collective-permute-start.32 = (bf16[1,2,128,256]{3,2,1,0:T(8,128)(2,1)S(1)}, bf16[1,2,128,256]{3,2,1,0:T(8,128)(2,1)S(1)}, u32[]{:S(2)}, u32[]{:S(2)}) collective-permute-start(bf16[1,2,128,256]{3,2,1,0:T(8,128)(2,1)S(1)} %get-tuple-element.59), channel_id=1, source_target_pairs={{0,2},{2,4},{4,6},{1,3},{3,5},{5,7},{8,10},{10,12},{12,14},{9,11},... | collective-permute-start | bytes 393224 | tf_op jit(solution)/shard_map/ppermute | solution.py:513
  96.6 7.4 %collective-permute-start.33 = (bf16[1,2,128,256]{3,2,1,0:T(8,128)(2,1)S(1)}, bf16[1,2,128,256]{3,2,1,0:T(8,128)(2,1)S(1)}, u32[]{:S(2)}, u32[]{:S(2)}) collective-permute-start(bf16[1,2,128,256]{3,2,1,0:T(8,128)(2,1)S(1)} %get-tuple-element.60), channel_id=1, source_target_pairs={{2,0},{4,2},{6,4},{3,1},{5,3},{7,5},{10,8},{12,10},{14,12},{11,9},... | collective-permute-start | bytes 393224 | tf_op jit(solution)/shard_map/ppermute | solution.py:513
  108.3 9.8 %collective-permute-start.34 = (bf16[2,2,128,256]{3,2,1,0:T(8,128)(2,1)S(1)}, bf16[2,2,128,256]{3,2,1,0:T(8,128)(2,1)S(1)}, u32[]{:S(2)}, u32[]{:S(2)}) collective-permute-start(bf16[2,2,128,256]{3,2,1,0:T(8,128)(2,1)S(1)} %get-tuple-element.63.first_ref.refs_2_.refs_5_), channel_id=1, source_target_pairs={{8,0},{16,8},{24,16},{9,1},{17,9},{25,17},{10,2},{18,10},{26,18},{... | collective-permute-start | bytes 786440 | tf_op jit(solution)/shard_map/ppermute | solution.py:513
  111.1 11.6 %collective-permute-start.39 = (s16[2,16,32,128]{3,2,1,0:T(8,128)(2,1)S(1)}, s16[2,16,32,128]{3,2,1,0:T(8,128)(2,1)S(1)}, u32[]{:S(2)}, u32[]{:S(2)}) collective-permute-start(s16[2,16,32,128]{3,2,1,0:T(8,128)(2,1)S(1)} %get-tuple-element.67.refs_0_), channel_id=1, source_target_pairs={{0,2},{2,0},{4,6},{6,4},{1,3},{3,1},{5,7},{7,5},{8,10},{10,8},{12,... | collective-permute-start | bytes 786440 | tf_op jit(solution)/shard_map/ppermute | solution.py:595
  112.8 9.8 %collective-permute-start.40 = (s16[2,16,32,128]{3,2,1,0:T(8,128)(2,1)S(1)}, s16[2,16,32,128]{3,2,1,0:T(8,128)(2,1)S(1)}, u32[]{:S(2)}, u32[]{:S(2)}) collective-permute-start(s16[2,16,32,128]{3,2,1,0:T(8,128)(2,1)S(1)} %get-tuple-element.68), channel_id=1, source_target_pairs={{0,4},{2,6},{4,0},{6,2},{1,5},{3,7},{5,1},{7,3},{8,12},{10,14},{12... | collective-permute-start | bytes 786440 | tf_op jit(solution)/shard_map/ppermute | solution.py:595
  112.8 12.8 %collective-permute-start.41 = (s16[2,16,32,128]{3,2,1,0:T(8,128)(2,1)S(1)}, s16[2,16,32,128]{3,2,1,0:T(8,128)(2,1)S(1)}, u32[]{:S(2)}, u32[]{:S(2)}) collective-permute-start(s16[2,16,32,128]{3,2,1,0:T(8,128)(2,1)S(1)} %get-tuple-element.69), channel_id=1, source_target_pairs={{0,6},{2,4},{4,2},{6,0},{1,7},{3,5},{5,3},{7,1},{8,14},{10,12},{12... | collective-permute-start | bytes 786440 | tf_op jit(solution)/shard_map/ppermute | solution.py:595
  139.5 6.9 %collective-permute-start.46 = (f32[1,2,128]{2,1,0:T(2,128)S(1)}, f32[1,2,128]{2,1,0:T(2,128)S(1)}, u32[]{:S(2)}, u32[]{:S(2)}) collective-permute-start(f32[1,2,128]{2,1,0:T(2,128)S(1)} %get-tuple-element.77), channel_id=1, source_target_pairs={{0,4},{2,6},{4,0},{6,2},{1,5},{3,7},{5,1},{7,3},{8,12},{10,14},{12... | collective-permute-start | bytes 3080 | tf_op jit(solution)/shard_map/ppermute | solution.py:542
  141.8 10.4 %collective-permute-start.49 = (s16[2,4,32,128]{3,2,1,0:T(8,128)(2,1)S(1)}, s16[2,4,32,128]{3,2,1,0:T(8,128)(2,1)S(1)}, u32[]{:S(2)}, u32[]{:S(2)}) collective-permute-start(s16[2,4,32,128]{3,2,1,0:T(8,128)(2,1)S(1)} %get-tuple-element.79.refs_0_), channel_id=1, source_target_pairs={{0,8},{8,0},{16,24},{24,16},{1,9},{9,1},{17,25},{25,17},{2,10},{10... | collective-permute-start | bytes 196616 | tf_op jit(solution)/shard_map/ppermute | solution.py:626
  144.2 8.0 %collective-permute-start.50 = (s16[2,4,32,128]{3,2,1,0:T(8,128)(2,1)S(1)}, s16[2,4,32,128]{3,2,1,0:T(8,128)(2,1)S(1)}, u32[]{:S(2)}, u32[]{:S(2)}) collective-permute-start(s16[2,4,32,128]{3,2,1,0:T(8,128)(2,1)S(1)} %get-tuple-element.79.refs_0_), channel_id=1, source_target_pairs={{0,16},{8,24},{16,0},{24,8},{1,17},{9,25},{17,1},{25,9},{2,18},{10... | collective-permute-start | bytes 196616 | tf_op jit(solution)/shard_map/ppermute | solution.py:626
  144.2 8.0 %collective-permute-start.51 = (s16[2,4,32,128]{3,2,1,0:T(8,128)(2,1)S(1)}, s16[2,4,32,128]{3,2,1,0:T(8,128)(2,1)S(1)}, u32[]{:S(2)}, u32[]{:S(2)}) collective-permute-start(s16[2,4,32,128]{3,2,1,0:T(8,128)(2,1)S(1)} %get-tuple-element.79.refs_0_), channel_id=1, source_target_pairs={{0,24},{8,16},{16,8},{24,0},{1,25},{9,17},{17,9},{25,1},{2,26},{10... | collective-permute-start | bytes 196616 | tf_op jit(solution)/shard_map/ppermute | solution.py:626
  155.6 8.4 %collective-permute-start.52 = (s16[16,32,128]{2,1,0:T(8,128)(2,1)S(1)}, s16[16,32,128]{2,1,0:T(8,128)(2,1)S(1)}, u32[]{:S(2)}, u32[]{:S(2)}) collective-permute-start(s16[16,32,128]{2,1,0:T(8,128)(2,1)S(1)} %bitcast.37), channel_id=1, source_target_pairs={{0,2},{2,0},{4,6},{6,4},{1,3},{3,1},{5,7},{7,5},{8,10},{10,8},{12,... | collective-permute-start | bytes 393224 | tf_op jit(solution)/shard_map/ppermute | solution.py:637
  155.6 9.5 %collective-permute-start.53 = (s16[16,32,128]{2,1,0:T(8,128)(2,1)S(1)}, s16[16,32,128]{2,1,0:T(8,128)(2,1)S(1)}, u32[]{:S(2)}, u32[]{:S(2)}) collective-permute-start(s16[16,32,128]{2,1,0:T(8,128)(2,1)S(1)} %bitcast.38), channel_id=1, source_target_pairs={{0,4},{2,6},{4,0},{6,2},{1,5},{3,7},{5,1},{7,3},{8,12},{10,14},{12... | collective-permute-start | bytes 393224 | tf_op jit(solution)/shard_map/ppermute | solution.py:637
  157.0 8.2 %collective-permute-start.54 = (s16[16,32,128]{2,1,0:T(8,128)(2,1)S(1)}, s16[16,32,128]{2,1,0:T(8,128)(2,1)S(1)}, u32[]{:S(2)}, u32[]{:S(2)}) collective-permute-start(s16[16,32,128]{2,1,0:T(8,128)(2,1)S(1)} %bitcast.39), channel_id=1, source_target_pairs={{0,6},{2,4},{4,2},{6,0},{1,7},{3,5},{5,3},{7,1},{8,14},{10,12},{12... | collective-permute-start | bytes 393224 | tf_op jit(solution)/shard_map/ppermute | solution.py:637
  160.1 8.3 %collective-permute-start.59 = (s16[64,32,128]{2,1,0:T(8,128)(2,1)S(1)}, s16[64,32,128]{2,1,0:T(8,128)(2,1)S(1)}, u32[]{:S(2)}, u32[]{:S(2)}) collective-permute-start(s16[64,32,128]{2,1,0:T(8,128)(2,1)S(1)} %bitcast.25), channel_id=1, source_target_pairs={{0,1},{1,0},{2,3},{3,2},{4,5},{5,4},{6,7},{7,6},{8,9},{9,8},{10,11... | collective-permute-start | bytes 1572872 | tf_op jit(solution)/shard_map/ppermute | solution.py:575
  165.7 6.6 %collective-permute-start.55 = (s16[64,32,128]{2,1,0:T(8,128)(2,1)S(1)}, s16[64,32,128]{2,1,0:T(8,128)(2,1)S(1)}, u32[]{:S(2)}, u32[]{:S(2)}) collective-permute-start(s16[64,32,128]{2,1,0:T(8,128)(2,1)S(1)} %bitcast.27), channel_id=1, source_target_pairs={{0,1},{1,0},{2,3},{3,2},{4,5},{5,4},{6,7},{7,6},{8,9},{9,8},{10,11... | collective-permute-start | bytes 1572872 | tf_op jit(solution)/shard_map/ppermute | solution.py:575
  (35 other events, 148.4 us)

commit v15 on v14

--- a/solution.py
+++ b/solution.py
@@ -143,14 +143,14 @@
     is_first = flag_ref[3] == 0
     channels = planes[0].shape[2]
     lane = lax.broadcasted_iota(jnp.int32, (channels, 128), 1)
+    start = pl.multiple_of(jnp.where(is_first, first_ref.shape[3] - 128, 0), 128)
     acc = jnp.zeros((channels, 128), F32)
     number = 0
     for ref in planes:
         for row in range(ref.shape[0]):
             for frame in range(ref.shape[1]):
-                last = pltpu.roll(ref[row, frame, :, -128:].astype(F32), 1, axis=1)
-                edge = jnp.where(is_first, last, ref[row, frame, :, :128].astype(F32))
-                moved = pltpu.roll(edge, number, axis=1) if number else edge
+                half = ref[row, frame, :, pl.ds(start, 128)].astype(F32)
+                moved = pltpu.roll(half, number + is_first.astype(jnp.int32), axis=1)
                 acc = jnp.where(lane == number, moved, acc)
                 number += 1
     out_ref[...] = acc.astype(BF16)

time: 177 us -> 176 us (level)
  Pallas kernels: 50.6 us -> 47.7 us
    pallas_call x30, Pallas kernels: 50.6 us -> 47.7 us  [call(): pl.pallas_call(body, out_shape=tuple(outs), in_specs=specs, out_specs=tup...]
  transfers between devices with their start and end apart: 60 -> 60, of which waited for: 19 -> 18; matrix products, arithmetic and copies ran while one was open for 0% -> 0% of each run, Pallas kernels for 21% -> 20%
where the time goes in v15:
time: 176 us; the launch traced here: 175 us
  starting transfers between devices  89.6 us (51%)
  Pallas kernels  47.7 us (27%)
  waiting for transfers between devices  31.1 us (18%)
  local copies, waits for them, and re-layouts  4.96 us (3%)
    pallas_call x30, Pallas kernels, call(): pl.pallas_call(body, out_shape=tuple(outs), in_specs=specs, out_specs=tup...  47.7 us
    ppermute x14, starting transfers between devices, all_stats(): parts = [value] + [lax.ppermute(value, axis, pairs) for pairs in exchanges]  23.7 us
    ppermute x10, starting transfers between devices, shifted(): lax.ppermute(value, axis, [(source, source + steps) for source in range(i...  20.7 us
    ppermute x11, starting transfers between devices, all_sum(): parts = [value] + [lax.ppermute(value, axis, pairs) for pairs in exchanges]  15.2 us
    ppermute x10, starting transfers between devices, swapped(): return lax.ppermute(value, 'width', [(0, 1), (1, 0)])  13 us
    ppermute x10, waiting for transfers between devices, shifted(): lax.ppermute(value, axis, [(source, source + steps) for source in range(i...  11.1 us
    ppermute x6, starting transfers between devices, gathered(): pieces = [value] + [lax.ppermute(value, axis, pairs) for pairs in exchanges]  5.36 us
    ppermute x14, waiting for transfers between devices, all_stats(): parts = [value] + [lax.ppermute(value, axis, pairs) for pairs in exchanges]  4.56 us
  transfers between devices with their start and end apart: 60, of which 18 were waited for; matrix products, arithmetic and copies ran while one was open for 0% of the time, Pallas kernels for 20%

profile of v15, /device:TPU:1, one launch (start us, length us, event | category | flops | bytes accessed | tf_op | source)
XLA Modules:
  0.0 175.2 jit_solution(5957625487133953809)
XLA Ops:
  4.3 2.6 %shard_map.112 = (bf16[4,2,128,256]{3,2,1,0:T(8,128)(2,1)S(1)}, bf16[4,2,128,256]{3,2,1,0:T(8,128)(2,1)S(1)}, bf16[2,2,128,256]{3,2,1,0:T(8,128)(2,1)S(1)}, bf16...) custom-call(bf16[128,2,4,256]{3,2,1,0:T(4,128)(2,1)S(1)} %copy-done.3, bf16[128,2,4,256]{3,2,1,0:T(4,128)(2,1)S(1)} %copy-done.4, ...), custom_call_target="tpu_custom_call" | custom-call | bytes 2626560 | tf_op jit(solution)/shard_map/pallas_call | solution.py:24
  7.0 2.2 %collective-permute-start.6 = (f32[1,2,128]{2,1,0:T(2,128)S(1)}, f32[1,2,128]{2,1,0:T(2,128)S(1)}, u32[]{:S(2)}, u32[]{:S(2)}) collective-permute-start(f32[1,2,128]{2,1,0:T(2,128)S(1)} %get-tuple-element.47), channel_id=1, source_target_pairs={{0,8},{8,0},{16,24},{24,16},{1,9},{9,1},{17,25},{25,17},{2,10},{10... | collective-permute-start | bytes 3080 | tf_op jit(solution)/shard_map/ppermute | solution.py:558
  9.2 2.3 %collective-permute-start.7 = (f32[1,2,128]{2,1,0:T(2,128)S(1)}, f32[1,2,128]{2,1,0:T(2,128)S(1)}, u32[]{:S(2)}, u32[]{:S(2)}) collective-permute-start(f32[1,2,128]{2,1,0:T(2,128)S(1)} %get-tuple-element.47), channel_id=1, source_target_pairs={{0,16},{8,24},{16,0},{24,8},{1,17},{9,25},{17,1},{25,9},{2,18},{10... | collective-permute-start | bytes 3080 | tf_op jit(solution)/shard_map/ppermute | solution.py:558
  11.5 3.1 %collective-permute-start.1 = (bf16[2,2,128,256]{3,2,1,0:T(8,128)(2,1)S(1)}, bf16[2,2,128,256]{3,2,1,0:T(8,128)(2,1)S(1)}, u32[]{:S(2)}, u32[]{:S(2)}) collective-permute-start(bf16[2,2,128,256]{3,2,1,0:T(8,128)(2,1)S(1)} %get-tuple-element.44), channel_id=1, source_target_pairs={{0,2},{2,4},{4,6},{1,3},{3,5},{5,7},{8,10},{10,12},{12,14},{9,11},... | collective-permute-start | bytes 786440 | tf_op jit(solution)/shard_map/ppermute | solution.py:513
  16.0 3.1 %collective-permute-start.10 = (f32[1,2,128]{2,1,0:T(2,128)S(1)}, f32[1,2,128]{2,1,0:T(2,128)S(1)}, u32[]{:S(2)}, u32[]{:S(2)}) collective-permute-start(f32[1,2,128]{2,1,0:T(2,128)S(1)} %pad_maximum_fusion), channel_id=1, source_target_pairs={{0,4},{2,6},{4,0},{6,2},{1,5},{3,7},{5,1},{7,3},{8,12},{10,14},{12... | collective-permute-start | bytes 3080 | tf_op jit(solution)/shard_map/ppermute | solution.py:558
  20.3 3.1 %collective-permute-start = (bf16[4,2,128,256]{3,2,1,0:T(8,128)(2,1)S(1)}, bf16[4,2,128,256]{3,2,1,0:T(8,128)(2,1)}, u32[]{:S(2)}, u32[]{:S(2)}) collective-permute-start(bf16[4,2,128,256]{3,2,1,0:T(8,128)(2,1)S(1)} %get-tuple-element.43.first_ref.own.refs_7_.latent), channel_id=1, source_target_pairs={{0,8},{8,16},{16,24},{1,9},{9,17},{17,25},{2,10},{10,18},{18,26},{... | collective-permute-start | bytes 1572872 | tf_op jit(solution)/shard_map/ppermute | solution.py:513
  27.8 3.1 %collective-permute-start.3 = (bf16[2,2,128,256]{3,2,1,0:T(8,128)(2,1)}, bf16[2,2,128,256]{3,2,1,0:T(8,128)(2,1)}, u32[]{:S(2)}, u32[]{:S(2)}) collective-permute-start(bf16[2,2,128,256]{3,2,1,0:T(8,128)(2,1)} %get-tuple-element.46.first_ref.near), channel_id=1, source_target_pairs={{0,8},{8,16},{16,24},{1,9},{9,17},{17,25},{2,10},{10,18},{18,26},{... | collective-permute-start | bytes 786440 | tf_op jit(solution)/shard_map/ppermute | solution.py:513
  30.9 3.5 %collective-permute-start.12 = (f32[1,2,128]{2,1,0:T(2,128)S(1)}, f32[1,2,128]{2,1,0:T(2,128)S(1)}, u32[]{:S(2)}, u32[]{:S(2)}) collective-permute-start(f32[1,2,128]{2,1,0:T(2,128)S(1)} %pad_maximum_fusion.1), channel_id=1, source_target_pairs={{0,1},{1,0},{2,3},{3,2},{4,5},{5,4},{6,7},{7,6},{8,9},{9,8},{10,11... | collective-permute-start | bytes 3080 | tf_op jit(solution)/shard_map/ppermute | solution.py:558
  38.5 3.1 %collective-permute-start.5 = (bf16[128,128]{1,0:T(8,128)(2,1)S(1)}, bf16[128,128]{1,0:T(8,128)(2,1)S(1)}, u32[]{:S(2)}, u32[]{:S(2)}) collective-permute-start(bf16[128,128]{1,0:T(8,128)(2,1)S(1)} %shard_map.115), channel_id=1, source_target_pairs={{0,1},{1,0},{2,3},{3,2},{4,5},{5,4},{6,7},{7,6},{8,9},{9,8},{10,11... | collective-permute-start | bytes 98312 | tf_op jit(solution)/shard_map/ppermute | solution.py:575
  43.0 2.8 %collective-permute-done.13.after.second_ref.refs_3_ = bf16[2,2,128,256]{3,2,1,0:T(8,128)(2,1)S(1)} collective-permute-done((bf16[2,2,128,256]{3,2,1,0:T(8,128)(2,1)}, bf16[2,2,128,256]{3,2,1,0:T(8,128)(2,1)S(1)}, u32[]{:S(2)}, u32[]{:S(2)}) %collective-permute-start.13) | collective-permute-done | bytes 262176 | tf_op jit(solution)/shard_map/ppermute | solution.py:513
  45.8 5.2 %shard_map.117 = (f32[4,2,128,256]{3,2,1,0:T(8,128)S(1)}, f32[1,2,128]{2,1,0:T(2,128)S(1)}, bf16[6,4,384,256]{3,2,1,0:T(8,128)(2,1)S(1)}) custom-call(s32[6]{0:T(128)S(1)} %stack.57.flag_ref, bf16[4,2,128,256]{3,2,1,0:T(8,128)(2,1)S(1)} %get-tuple-element.43.first_ref.own.refs_7_.latent, bf16[4,2,128,256]{3,2,1,0:T(8,128)(2,1)} %collective-permute-done.second_ref.past, ...), custom_call_target="tpu_custom_call" | custom-call | flops 7247757312 | bytes 10033176 | tf_op jit(solution)/shard_map/pallas_call | solution.py:24
  55.8 2.1 %collective-permute-start.18 = (f32[1,2,128]{2,1,0:T(2,128)S(1)}, f32[1,2,128]{2,1,0:T(2,128)S(1)}, u32[]{:S(2)}, u32[]{:S(2)}) collective-permute-start(f32[1,2,128]{2,1,0:T(2,128)S(1)} %get-tuple-element.51.refs_0_), channel_id=1, source_target_pairs={{0,16},{8,24},{16,0},{24,8},{1,17},{9,25},{17,1},{25,9},{2,18},{10... | collective-permute-start | bytes 3080 | tf_op jit(solution)/shard_map/ppermute | solution.py:558
  58.2 3.9 %shard_map.121 = (f32[4,2,128,256]{3,2,1,0:T(8,128)S(1)}, bf16[6,4,384,256]{3,2,1,0:T(8,128)(2,1)S(1)}) custom-call(s32[6]{0:T(128)S(1)} %stack.57.flag_ref, bf16[4,2,128,256]{3,2,1,0:T(8,128)(2,1)S(1)} %get-tuple-element.50.first_ref.refs_0_.cotangent, bf16[4,2,128,256]{3,2,1,0:T(8,128)(2,1)} %collective-permute-done.14.second_ref.refs_1_, ...), custom_call_target="tpu_custom_call" | custom-call | flops 7247757312 | bytes 9764888 | tf_op jit(solution)/shard_map/pallas_call | solution.py:24
  62.2 3.5 %collective-permute-start.20 = (f32[1,2,128]{2,1,0:T(2,128)S(1)}, f32[1,2,128]{2,1,0:T(2,128)S(1)}, u32[]{:S(2)}, u32[]{:S(2)}) collective-permute-start(f32[1,2,128]{2,1,0:T(2,128)S(1)} %shard_map.122), channel_id=1, source_target_pairs={{0,2},{2,0},{4,6},{6,4},{1,3},{3,1},{5,7},{7,5},{8,10},{10,8},{12,... | collective-permute-start | bytes 3080 | tf_op jit(solution)/shard_map/ppermute | solution.py:558
  69.0 2.8 %collective-permute-start.23 = (f32[1,2,128]{2,1,0:T(2,128)S(1)}, f32[1,2,128]{2,1,0:T(2,128)S(1)}, u32[]{:S(2)}, u32[]{:S(2)}) collective-permute-start(f32[1,2,128]{2,1,0:T(2,128)S(1)} %pad_maximum_fusion.3), channel_id=1, source_target_pairs={{0,1},{1,0},{2,3},{3,2},{4,5},{5,4},{6,7},{7,6},{8,9},{9,8},{10,11... | collective-permute-start | bytes 3080 | tf_op jit(solution)/shard_map/ppermute | solution.py:558
  77.2 4.1 %shard_map.124 = (f32[2048,128]{1,0:T(8,128)S(1)}, f32[2048,128]{1,0:T(8,128)S(1)}) custom-call(s32[6]{0:T(128)S(1)} %stack.57.flag_ref, bf16[6,4,384,256]{3,2,1,0:T(8,128)(2,1)S(1)} %get-tuple-element.55.stack_ref, bf16[4,2,128,256]{3,2,1,0:T(8,128)(2,1)S(1)} %get-tuple-element.56.act_ref), custom_call_target="tpu_custom_call" | custom-call | flops 7247757312 | bytes 7340056 | tf_op jit(solution)/shard_map/pallas_call | solution.py:24
  86.6 2.6 %collective-permute-start.30 = (f32[1,2,128]{2,1,0:T(2,128)S(1)}, f32[1,2,128]{2,1,0:T(2,128)S(1)}, u32[]{:S(2)}, u32[]{:S(2)}) collective-permute-start(f32[1,2,128]{2,1,0:T(2,128)S(1)} %add_add_fusion.1), channel_id=1, source_target_pairs={{0,1},{1,0},{2,3},{3,2},{4,5},{5,4},{6,7},{7,6},{8,9},{9,8},{10,11... | collective-permute-start | bytes 3080 | tf_op jit(solution)/shard_map/ppermute | solution.py:542
  92.0 3.6 %collective-permute-start.32 = (bf16[1,2,128,256]{3,2,1,0:T(8,128)(2,1)S(1)}, bf16[1,2,128,256]{3,2,1,0:T(8,128)(2,1)S(1)}, u32[]{:S(2)}, u32[]{:S(2)}) collective-permute-start(bf16[1,2,128,256]{3,2,1,0:T(8,128)(2,1)S(1)} %get-tuple-element.59), channel_id=1, source_target_pairs={{0,2},{2,4},{4,6},{1,3},{3,5},{5,7},{8,10},{10,12},{12,14},{9,11},... | collective-permute-start | bytes 393224 | tf_op jit(solution)/shard_map/ppermute | solution.py:513
  96.9 4.6 %shard_map.127 = (f32[2048,128]{1,0:T(8,128)S(1)}, f32[2048,128]{1,0:T(8,128)S(1)}) custom-call(s32[6]{0:T(128)S(1)} %stack.57.flag_ref, bf16[6,4,384,256]{3,2,1,0:T(8,128)(2,1)S(1)} %get-tuple-element.61.stack_ref, bf16[4,2,128,256]{3,2,1,0:T(8,128)(2,1)S(1)} %get-tuple-element.58.grad_ref.first_ref.refs_0_), custom_call_target="tpu_custom_call" | custom-call | flops 7247757312 | bytes 7340056 | tf_op jit(solution)/shard_map/pallas_call | solution.py:24
  103.0 2.8 %collective-permute-done.31.after.second_ref.refs_1_.refs_4_ = bf16[4,2,128,256]{3,2,1,0:T(8,128)(2,1)S(1)} collective-permute-done((bf16[4,2,128,256]{3,2,1,0:T(8,128)(2,1)S(1)}, bf16[4,2,128,256]{3,2,1,0:T(8,128)(2,1)S(1)}, u32[]{:S(2)}, u32[]{:S(2)}) %collective-permute-start.31) | collective-permute-done | bytes 524320 | tf_op jit(solution)/shard_map/ppermute | solution.py:513
  113.1 4.0 %collective-permute-done.34.second_ref.refs_3_ = bf16[2,2,128,256]{3,2,1,0:T(8,128)(2,1)S(1)} collective-permute-done((bf16[2,2,128,256]{3,2,1,0:T(8,128)(2,1)S(1)}, bf16[2,2,128,256]{3,2,1,0:T(8,128)(2,1)S(1)}, u32[]{:S(2)}, u32[]{:S(2)}) %collective-permute-start.34) | collective-permute-done | bytes 262176 | tf_op jit(solution)/shard_map/ppermute | solution.py:513
  120.7 3.9 %collective-permute-done.41.refs_12_ = s16[2,16,32,128]{3,2,1,0:T(8,128)(2,1)S(1)} collective-permute-done((s16[2,16,32,128]{3,2,1,0:T(8,128)(2,1)S(1)}, s16[2,16,32,128]{3,2,1,0:T(8,128)(2,1)S(1)}, u32[]{:S(2)}, u32[]{:S(2)}) %collective-permute-start.41) | collective-permute-done | bytes 262176 | tf_op jit(solution)/shard_map/ppermute | solution.py:595
  124.7 4.0 %shard_map.133 = (f32[4,2,128,256]{3,2,1,0:T(8,128)S(1)}, f32[1,2,128]{2,1,0:T(2,128)S(1)}) custom-call(s32[6]{0:T(128)S(1)} %stack.57.flag_ref, bf16[4,2,128,256]{3,2,1,0:T(8,128)(2,1)S(1)} %get-tuple-element.58.grad_ref.first_ref.refs_0_, bf16[4,2,128,256]{3,2,1,0:T(8,128)(2,1)S(1)} %collective-permute-done.31.after.second_ref.refs_1_.refs_4_, ...), custom_call_target="tpu_custom_call" | custom-call | flops 7247757312 | bytes 6363160 | tf_op jit(solution)/shard_map/pallas_call | solution.py:24
  131.6 2.2 %collective-permute-start.44 = (s16[2,4,32,128]{3,2,1,0:T(8,128)(2,1)S(1)}, s16[2,4,32,128]{3,2,1,0:T(8,128)(2,1)S(1)}, u32[]{:S(2)}, u32[]{:S(2)}) collective-permute-start(s16[2,4,32,128]{3,2,1,0:T(8,128)(2,1)S(1)} %get-tuple-element.76), channel_id=1, source_target_pairs={{0,24},{8,16},{16,8},{24,0},{1,25},{9,17},{17,9},{25,1},{2,26},{10... | collective-permute-start | bytes 196616 | tf_op jit(solution)/shard_map/ppermute | solution.py:613
  133.8 4.2 %collective-permute-done.43.refs_2_ = s16[2,4,32,128]{3,2,1,0:T(8,128)(2,1)S(1)} collective-permute-done((s16[2,4,32,128]{3,2,1,0:T(8,128)(2,1)S(1)}, s16[2,4,32,128]{3,2,1,0:T(8,128)(2,1)S(1)}, u32[]{:S(2)}, u32[]{:S(2)}) %collective-permute-start.43) | collective-permute-done | bytes 65568 | tf_op jit(solution)/shard_map/ppermute | solution.py:613
  140.8 2.4 %collective-permute-start.49 = (s16[2,4,32,128]{3,2,1,0:T(8,128)(2,1)S(1)}, s16[2,4,32,128]{3,2,1,0:T(8,128)(2,1)S(1)}, u32[]{:S(2)}, u32[]{:S(2)}) collective-permute-start(s16[2,4,32,128]{3,2,1,0:T(8,128)(2,1)S(1)} %get-tuple-element.79.refs_0_), channel_id=1, source_target_pairs={{0,8},{8,0},{16,24},{24,16},{1,9},{9,1},{17,25},{25,17},{2,10},{10... | collective-permute-start | bytes 196616 | tf_op jit(solution)/shard_map/ppermute | solution.py:626
  143.2 2.1 %collective-permute-start.51 = (s16[2,4,32,128]{3,2,1,0:T(8,128)(2,1)S(1)}, s16[2,4,32,128]{3,2,1,0:T(8,128)(2,1)S(1)}, u32[]{:S(2)}, u32[]{:S(2)}) collective-permute-start(s16[2,4,32,128]{3,2,1,0:T(8,128)(2,1)S(1)} %get-tuple-element.79.refs_0_), channel_id=1, source_target_pairs={{0,24},{8,16},{16,8},{24,0},{1,25},{9,17},{17,9},{25,1},{2,26},{10... | collective-permute-start | bytes 196616 | tf_op jit(solution)/shard_map/ppermute | solution.py:626
  145.3 3.3 %collective-permute-start.48 = (f32[1,2,128]{2,1,0:T(2,128)S(1)}, f32[1,2,128]{2,1,0:T(2,128)S(1)}, u32[]{:S(2)}, u32[]{:S(2)}) collective-permute-start(f32[1,2,128]{2,1,0:T(2,128)S(1)} %add_add_fusion), channel_id=1, source_target_pairs={{0,1},{1,0},{2,3},{3,2},{4,5},{5,4},{6,7},{7,6},{8,9},{9,8},{10,11... | collective-permute-start | bytes 3080 | tf_op jit(solution)/shard_map/ppermute | solution.py:542
  159.1 3.9 %collective-permute-start.59 = (s16[64,32,128]{2,1,0:T(8,128)(2,1)S(1)}, s16[64,32,128]{2,1,0:T(8,128)(2,1)S(1)}, u32[]{:S(2)}, u32[]{:S(2)}) collective-permute-start(s16[64,32,128]{2,1,0:T(8,128)(2,1)S(1)} %bitcast.25), channel_id=1, source_target_pairs={{0,1},{1,0},{2,3},{3,2},{4,5},{5,4},{6,7},{7,6},{8,9},{9,8},{10,11... | collective-permute-start | bytes 1572872 | tf_op jit(solution)/shard_map/ppermute | solution.py:575
  164.7 2.7 %collective-permute-start.55 = (s16[64,32,128]{2,1,0:T(8,128)(2,1)S(1)}, s16[64,32,128]{2,1,0:T(8,128)(2,1)S(1)}, u32[]{:S(2)}, u32[]{:S(2)}) collective-permute-start(s16[64,32,128]{2,1,0:T(8,128)(2,1)S(1)} %bitcast.27), channel_id=1, source_target_pairs={{0,1},{1,0},{2,3},{3,2},{4,5},{5,4},{6,7},{7,6},{8,9},{9,8},{10,11... | collective-permute-start | bytes 1572872 | tf_op jit(solution)/shard_map/ppermute | solution.py:575
  167.4 3.9 %shard_map.141 = f32[128,3456]{1,0:T(8,128)} custom-call(s32[6]{0:T(128)S(1)} %stack.57.flag_ref, s16[64,32,128]{2,1,0:T(8,128)(2,1)S(1)} %bitcast.26, s16[64,32,128]{2,1,0:T(8,128)(2,1)S(1)} %collective-permute-done.59.theirs_ref), custom_call_target="tpu_custom_call" | custom-call | bytes 2818072 | tf_op jit(solution)/shard_map/pallas_call | solution.py:24
  171.3 3.9 %shard_map.139 = f32[128,3456]{1,0:T(8,128)} custom-call(s32[6]{0:T(128)S(1)} %stack.57.flag_ref, s16[64,32,128]{2,1,0:T(8,128)(2,1)S(1)} %bitcast.28, s16[64,32,128]{2,1,0:T(8,128)(2,1)S(1)} %collective-permute-done.55.theirs_ref), custom_call_target="tpu_custom_call" | custom-call | bytes 2818072 | tf_op jit(solution)/shard_map/pallas_call | solution.py:24
  (153 shorter events, 69.5 us)
Async XLA Ops:
  7.0 8.9 %collective-permute-start.6 = (f32[1,2,128]{2,1,0:T(2,128)S(1)}, f32[1,2,128]{2,1,0:T(2,128)S(1)}, u32[]{:S(2)}, u32[]{:S(2)}) collective-permute-start(f32[1,2,128]{2,1,0:T(2,128)S(1)} %get-tuple-element.47), channel_id=1, source_target_pairs={{0,8},{8,0},{16,24},{24,16},{1,9},{9,1},{17,25},{25,17},{2,10},{10... | collective-permute-start | bytes 3080 | tf_op jit(solution)/shard_map/ppermute | solution.py:558
  9.2 6.8 %collective-permute-start.7 = (f32[1,2,128]{2,1,0:T(2,128)S(1)}, f32[1,2,128]{2,1,0:T(2,128)S(1)}, u32[]{:S(2)}, u32[]{:S(2)}) collective-permute-start(f32[1,2,128]{2,1,0:T(2,128)S(1)} %get-tuple-element.47), channel_id=1, source_target_pairs={{0,16},{8,24},{16,0},{24,8},{1,17},{9,25},{17,1},{25,9},{2,18},{10... | collective-permute-start | bytes 3080 | tf_op jit(solution)/shard_map/ppermute | solution.py:558
  11.5 14.9 %collective-permute-start.1 = (bf16[2,2,128,256]{3,2,1,0:T(8,128)(2,1)S(1)}, bf16[2,2,128,256]{3,2,1,0:T(8,128)(2,1)S(1)}, u32[]{:S(2)}, u32[]{:S(2)}) collective-permute-start(bf16[2,2,128,256]{3,2,1,0:T(8,128)(2,1)S(1)} %get-tuple-element.44), channel_id=1, source_target_pairs={{0,2},{2,4},{4,6},{1,3},{3,5},{5,7},{8,10},{10,12},{12,14},{9,11},... | collective-permute-start | bytes 786440 | tf_op jit(solution)/shard_map/ppermute | solution.py:513
  14.6 11.7 %collective-permute-start.2 = (bf16[2,2,128,256]{3,2,1,0:T(8,128)(2,1)S(1)}, bf16[2,2,128,256]{3,2,1,0:T(8,128)(2,1)S(1)}, u32[]{:S(2)}, u32[]{:S(2)}) collective-permute-start(bf16[2,2,128,256]{3,2,1,0:T(8,128)(2,1)S(1)} %get-tuple-element.45), channel_id=1, source_target_pairs={{2,0},{4,2},{6,4},{3,1},{5,3},{7,5},{10,8},{12,10},{14,12},{11,9},... | collective-permute-start | bytes 786440 | tf_op jit(solution)/shard_map/ppermute | solution.py:513
  19.3 7.0 %collective-permute-start.9 = (f32[1,2,128]{2,1,0:T(2,128)S(1)}, f32[1,2,128]{2,1,0:T(2,128)S(1)}, u32[]{:S(2)}, u32[]{:S(2)}) collective-permute-start(f32[1,2,128]{2,1,0:T(2,128)S(1)} %pad_maximum_fusion), channel_id=1, source_target_pairs={{0,2},{2,0},{4,6},{6,4},{1,3},{3,1},{5,7},{7,5},{8,10},{10,8},{12,... | collective-permute-start | bytes 3080 | tf_op jit(solution)/shard_map/ppermute | solution.py:558
  20.3 21.3 %collective-permute-start = (bf16[4,2,128,256]{3,2,1,0:T(8,128)(2,1)S(1)}, bf16[4,2,128,256]{3,2,1,0:T(8,128)(2,1)}, u32[]{:S(2)}, u32[]{:S(2)}) collective-permute-start(bf16[4,2,128,256]{3,2,1,0:T(8,128)(2,1)S(1)} %get-tuple-element.43.first_ref.own.refs_7_.latent), channel_id=1, source_target_pairs={{0,8},{8,16},{16,24},{1,9},{9,17},{17,25},{2,10},{10,18},{18,26},{... | collective-permute-start | bytes 1572872 | tf_op jit(solution)/shard_map/ppermute | solution.py:513
  23.4 29.3 %collective-permute-start.14 = (bf16[4,2,128,256]{3,2,1,0:T(8,128)(2,1)S(1)}, bf16[4,2,128,256]{3,2,1,0:T(8,128)(2,1)}, u32[]{:S(2)}, u32[]{:S(2)}) collective-permute-start(bf16[4,2,128,256]{3,2,1,0:T(8,128)(2,1)S(1)} %get-tuple-element.50.first_ref.refs_0_.cotangent), channel_id=1, source_target_pairs={{8,0},{16,8},{24,16},{9,1},{17,9},{25,17},{10,2},{18,10},{26,18},{... | collective-permute-start | bytes 1572872 | tf_op jit(solution)/shard_map/ppermute | solution.py:513
  27.8 9.5 %collective-permute-start.3 = (bf16[2,2,128,256]{3,2,1,0:T(8,128)(2,1)}, bf16[2,2,128,256]{3,2,1,0:T(8,128)(2,1)}, u32[]{:S(2)}, u32[]{:S(2)}) collective-permute-start(bf16[2,2,128,256]{3,2,1,0:T(8,128)(2,1)} %get-tuple-element.46.first_ref.near), channel_id=1, source_target_pairs={{0,8},{8,16},{16,24},{1,9},{9,17},{17,25},{2,10},{10,18},{18,26},{... | collective-permute-start | bytes 786440 | tf_op jit(solution)/shard_map/ppermute | solution.py:513
  30.9 6.4 %collective-permute-start.12 = (f32[1,2,128]{2,1,0:T(2,128)S(1)}, f32[1,2,128]{2,1,0:T(2,128)S(1)}, u32[]{:S(2)}, u32[]{:S(2)}) collective-permute-start(f32[1,2,128]{2,1,0:T(2,128)S(1)} %pad_maximum_fusion.1), channel_id=1, source_target_pairs={{0,1},{1,0},{2,3},{3,2},{4,5},{5,4},{6,7},{7,6},{8,9},{9,8},{10,11... | collective-permute-start | bytes 3080 | tf_op jit(solution)/shard_map/ppermute | solution.py:558
  35.8 10.0 %collective-permute-start.13 = (bf16[2,2,128,256]{3,2,1,0:T(8,128)(2,1)}, bf16[2,2,128,256]{3,2,1,0:T(8,128)(2,1)S(1)}, u32[]{:S(2)}, u32[]{:S(2)}) collective-permute-start(bf16[2,2,128,256]{3,2,1,0:T(8,128)(2,1)} %copy-done.5), channel_id=1, source_target_pairs={{8,0},{16,8},{24,16},{9,1},{17,9},{25,17},{10,2},{18,10},{26,18},{... | collective-permute-start | bytes 786440 | tf_op jit(solution)/shard_map/ppermute | solution.py:513
  38.5 7.3 %collective-permute-start.5 = (bf16[128,128]{1,0:T(8,128)(2,1)S(1)}, bf16[128,128]{1,0:T(8,128)(2,1)S(1)}, u32[]{:S(2)}, u32[]{:S(2)}) collective-permute-start(bf16[128,128]{1,0:T(8,128)(2,1)S(1)} %shard_map.115), channel_id=1, source_target_pairs={{0,1},{1,0},{2,3},{3,2},{4,5},{5,4},{6,7},{7,6},{8,9},{9,8},{10,11... | collective-permute-start | bytes 98312 | tf_op jit(solution)/shard_map/ppermute | solution.py:575
  51.8 6.4 %collective-permute-start.16 = (bf16[128,128]{1,0:T(8,128)(2,1)S(1)}, bf16[128,128]{1,0:T(8,128)(2,1)S(1)}, u32[]{:S(2)}, u32[]{:S(2)}) collective-permute-start(bf16[128,128]{1,0:T(8,128)(2,1)S(1)} %shard_map.119), channel_id=1, source_target_pairs={{0,1},{1,0},{2,3},{3,2},{4,5},{5,4},{6,7},{7,6},{8,9},{9,8},{10,11... | collective-permute-start | bytes 98312 | tf_op jit(solution)/shard_map/ppermute | solution.py:575
  54.4 7.7 %collective-permute-start.17 = (f32[1,2,128]{2,1,0:T(2,128)S(1)}, f32[1,2,128]{2,1,0:T(2,128)S(1)}, u32[]{:S(2)}, u32[]{:S(2)}) collective-permute-start(f32[1,2,128]{2,1,0:T(2,128)S(1)} %get-tuple-element.51.refs_0_), channel_id=1, source_target_pairs={{0,8},{8,0},{16,24},{24,16},{1,9},{9,1},{17,25},{25,17},{2,10},{10... | collective-permute-start | bytes 3080 | tf_op jit(solution)/shard_map/ppermute | solution.py:558
  73.6 7.7 %collective-permute-start.24 = (f32[1,2,128]{2,1,0:T(2,128)S(1)}, f32[1,2,128]{2,1,0:T(2,128)S(1)}, u32[]{:S(2)}, u32[]{:S(2)}) collective-permute-start(f32[1,2,128]{2,1,0:T(2,128)S(1)} %get-tuple-element.54.refs_0_), channel_id=1, source_target_pairs={{0,8},{8,0},{16,24},{24,16},{1,9},{9,1},{17,25},{25,17},{2,10},{10... | collective-permute-start | bytes 3080 | tf_op jit(solution)/shard_map/ppermute | solution.py:542
  73.7 7.7 %collective-permute-start.25 = (f32[1,2,128]{2,1,0:T(2,128)S(1)}, f32[1,2,128]{2,1,0:T(2,128)S(1)}, u32[]{:S(2)}, u32[]{:S(2)}) collective-permute-start(f32[1,2,128]{2,1,0:T(2,128)S(1)} %get-tuple-element.54.refs_0_), channel_id=1, source_target_pairs={{0,16},{8,24},{16,0},{24,8},{1,17},{9,25},{17,1},{25,9},{2,18},{10... | collective-permute-start | bytes 3080 | tf_op jit(solution)/shard_map/ppermute | solution.py:542
  89.2 19.4 %collective-permute-start.35 = (f32[64,32,128]{2,1,0:T(8,128)S(1)}, f32[64,32,128]{2,1,0:T(8,128)S(1)}, u32[]{:S(2)}, u32[]{:S(2)}) collective-permute-start(f32[64,32,128]{2,1,0:T(8,128)S(1)} %bitcast.45), channel_id=1, source_target_pairs={{0,1},{1,0},{2,3},{3,2},{4,5},{5,4},{6,7},{7,6},{8,9},{9,8},{10,11... | collective-permute-start | bytes 3145736 | tf_op jit(solution)/shard_map/ppermute | solution.py:575
  90.7 15.1 %collective-permute-start.31 = (bf16[4,2,128,256]{3,2,1,0:T(8,128)(2,1)S(1)}, bf16[4,2,128,256]{3,2,1,0:T(8,128)(2,1)S(1)}, u32[]{:S(2)}, u32[]{:S(2)}) collective-permute-start(bf16[4,2,128,256]{3,2,1,0:T(8,128)(2,1)S(1)} %get-tuple-element.58.grad_ref.first_ref.refs_0_), channel_id=1, source_target_pairs={{8,0},{16,8},{24,16},{9,1},{17,9},{25,17},{10,2},{18,10},{26,18},{... | collective-permute-start | bytes 1572872 | tf_op jit(solution)/shard_map/ppermute | solution.py:513
  92.0 9.5 %collective-permute-start.32 = (bf16[1,2,128,256]{3,2,1,0:T(8,128)(2,1)S(1)}, bf16[1,2,128,256]{3,2,1,0:T(8,128)(2,1)S(1)}, u32[]{:S(2)}, u32[]{:S(2)}) collective-permute-start(bf16[1,2,128,256]{3,2,1,0:T(8,128)(2,1)S(1)} %get-tuple-element.59), channel_id=1, source_target_pairs={{0,2},{2,4},{4,6},{1,3},{3,5},{5,7},{8,10},{10,12},{12,14},{9,11},... | collective-permute-start | bytes 393224 | tf_op jit(solution)/shard_map/ppermute | solution.py:513
  95.6 7.4 %collective-permute-start.33 = (bf16[1,2,128,256]{3,2,1,0:T(8,128)(2,1)S(1)}, bf16[1,2,128,256]{3,2,1,0:T(8,128)(2,1)S(1)}, u32[]{:S(2)}, u32[]{:S(2)}) collective-permute-start(bf16[1,2,128,256]{3,2,1,0:T(8,128)(2,1)S(1)} %get-tuple-element.60), channel_id=1, source_target_pairs={{2,0},{4,2},{6,4},{3,1},{5,3},{7,5},{10,8},{12,10},{14,12},{11,9},... | collective-permute-start | bytes 393224 | tf_op jit(solution)/shard_map/ppermute | solution.py:513
  107.3 9.8 %collective-permute-start.34 = (bf16[2,2,128,256]{3,2,1,0:T(8,128)(2,1)S(1)}, bf16[2,2,128,256]{3,2,1,0:T(8,128)(2,1)S(1)}, u32[]{:S(2)}, u32[]{:S(2)}) collective-permute-start(bf16[2,2,128,256]{3,2,1,0:T(8,128)(2,1)S(1)} %get-tuple-element.63.first_ref.refs_2_.refs_5_), channel_id=1, source_target_pairs={{8,0},{16,8},{24,16},{9,1},{17,9},{25,17},{10,2},{18,10},{26,18},{... | collective-permute-start | bytes 786440 | tf_op jit(solution)/shard_map/ppermute | solution.py:513
  110.1 10.6 %collective-permute-start.39 = (s16[2,16,32,128]{3,2,1,0:T(8,128)(2,1)S(1)}, s16[2,16,32,128]{3,2,1,0:T(8,128)(2,1)S(1)}, u32[]{:S(2)}, u32[]{:S(2)}) collective-permute-start(s16[2,16,32,128]{3,2,1,0:T(8,128)(2,1)S(1)} %get-tuple-element.67.refs_0_), channel_id=1, source_target_pairs={{0,2},{2,0},{4,6},{6,4},{1,3},{3,1},{5,7},{7,5},{8,10},{10,8},{12,... | collective-permute-start | bytes 786440 | tf_op jit(solution)/shard_map/ppermute | solution.py:595
  111.9 8.9 %collective-permute-start.40 = (s16[2,16,32,128]{3,2,1,0:T(8,128)(2,1)S(1)}, s16[2,16,32,128]{3,2,1,0:T(8,128)(2,1)S(1)}, u32[]{:S(2)}, u32[]{:S(2)}) collective-permute-start(s16[2,16,32,128]{3,2,1,0:T(8,128)(2,1)S(1)} %get-tuple-element.68), channel_id=1, source_target_pairs={{0,4},{2,6},{4,0},{6,2},{1,5},{3,7},{5,1},{7,3},{8,12},{10,14},{12... | collective-permute-start | bytes 786440 | tf_op jit(solution)/shard_map/ppermute | solution.py:595
  111.9 12.8 %collective-permute-start.41 = (s16[2,16,32,128]{3,2,1,0:T(8,128)(2,1)S(1)}, s16[2,16,32,128]{3,2,1,0:T(8,128)(2,1)S(1)}, u32[]{:S(2)}, u32[]{:S(2)}) collective-permute-start(s16[2,16,32,128]{3,2,1,0:T(8,128)(2,1)S(1)} %get-tuple-element.69), channel_id=1, source_target_pairs={{0,6},{2,4},{4,2},{6,0},{1,7},{3,5},{5,3},{7,1},{8,14},{10,12},{12... | collective-permute-start | bytes 786440 | tf_op jit(solution)/shard_map/ppermute | solution.py:595
  138.6 6.7 %collective-permute-start.46 = (f32[1,2,128]{2,1,0:T(2,128)S(1)}, f32[1,2,128]{2,1,0:T(2,128)S(1)}, u32[]{:S(2)}, u32[]{:S(2)}) collective-permute-start(f32[1,2,128]{2,1,0:T(2,128)S(1)} %get-tuple-element.77), channel_id=1, source_target_pairs={{0,4},{2,6},{4,0},{6,2},{1,5},{3,7},{5,1},{7,3},{8,12},{10,14},{12... | collective-permute-start | bytes 3080 | tf_op jit(solution)/shard_map/ppermute | solution.py:542
  140.8 10.5 %collective-permute-start.49 = (s16[2,4,32,128]{3,2,1,0:T(8,128)(2,1)S(1)}, s16[2,4,32,128]{3,2,1,0:T(8,128)(2,1)S(1)}, u32[]{:S(2)}, u32[]{:S(2)}) collective-permute-start(s16[2,4,32,128]{3,2,1,0:T(8,128)(2,1)S(1)} %get-tuple-element.79.refs_0_), channel_id=1, source_target_pairs={{0,8},{8,0},{16,24},{24,16},{1,9},{9,1},{17,25},{25,17},{2,10},{10... | collective-permute-start | bytes 196616 | tf_op jit(solution)/shard_map/ppermute | solution.py:626
  143.2 8.1 %collective-permute-start.50 = (s16[2,4,32,128]{3,2,1,0:T(8,128)(2,1)S(1)}, s16[2,4,32,128]{3,2,1,0:T(8,128)(2,1)S(1)}, u32[]{:S(2)}, u32[]{:S(2)}) collective-permute-start(s16[2,4,32,128]{3,2,1,0:T(8,128)(2,1)S(1)} %get-tuple-element.79.refs_0_), channel_id=1, source_target_pairs={{0,16},{8,24},{16,0},{24,8},{1,17},{9,25},{17,1},{25,9},{2,18},{10... | collective-permute-start | bytes 196616 | tf_op jit(solution)/shard_map/ppermute | solution.py:626
  143.2 8.1 %collective-permute-start.51 = (s16[2,4,32,128]{3,2,1,0:T(8,128)(2,1)S(1)}, s16[2,4,32,128]{3,2,1,0:T(8,128)(2,1)S(1)}, u32[]{:S(2)}, u32[]{:S(2)}) collective-permute-start(s16[2,4,32,128]{3,2,1,0:T(8,128)(2,1)S(1)} %get-tuple-element.79.refs_0_), channel_id=1, source_target_pairs={{0,24},{8,16},{16,8},{24,0},{1,25},{9,17},{17,9},{25,1},{2,26},{10... | collective-permute-start | bytes 196616 | tf_op jit(solution)/shard_map/ppermute | solution.py:626
  154.6 8.4 %collective-permute-start.52 = (s16[16,32,128]{2,1,0:T(8,128)(2,1)S(1)}, s16[16,32,128]{2,1,0:T(8,128)(2,1)S(1)}, u32[]{:S(2)}, u32[]{:S(2)}) collective-permute-start(s16[16,32,128]{2,1,0:T(8,128)(2,1)S(1)} %bitcast.37), channel_id=1, source_target_pairs={{0,2},{2,0},{4,6},{6,4},{1,3},{3,1},{5,7},{7,5},{8,10},{10,8},{12,... | collective-permute-start | bytes 393224 | tf_op jit(solution)/shard_map/ppermute | solution.py:637
  154.7 9.5 %collective-permute-start.53 = (s16[16,32,128]{2,1,0:T(8,128)(2,1)S(1)}, s16[16,32,128]{2,1,0:T(8,128)(2,1)S(1)}, u32[]{:S(2)}, u32[]{:S(2)}) collective-permute-start(s16[16,32,128]{2,1,0:T(8,128)(2,1)S(1)} %bitcast.38), channel_id=1, source_target_pairs={{0,4},{2,6},{4,0},{6,2},{1,5},{3,7},{5,1},{7,3},{8,12},{10,14},{12... | collective-permute-start | bytes 393224 | tf_op jit(solution)/shard_map/ppermute | solution.py:637
  156.0 8.2 %collective-permute-start.54 = (s16[16,32,128]{2,1,0:T(8,128)(2,1)S(1)}, s16[16,32,128]{2,1,0:T(8,128)(2,1)S(1)}, u32[]{:S(2)}, u32[]{:S(2)}) collective-permute-start(s16[16,32,128]{2,1,0:T(8,128)(2,1)S(1)} %bitcast.39), channel_id=1, source_target_pairs={{0,6},{2,4},{4,2},{6,0},{1,7},{3,5},{5,3},{7,1},{8,14},{10,12},{12... | collective-permute-start | bytes 393224 | tf_op jit(solution)/shard_map/ppermute | solution.py:637
  159.1 8.3 %collective-permute-start.59 = (s16[64,32,128]{2,1,0:T(8,128)(2,1)S(1)}, s16[64,32,128]{2,1,0:T(8,128)(2,1)S(1)}, u32[]{:S(2)}, u32[]{:S(2)}) collective-permute-start(s16[64,32,128]{2,1,0:T(8,128)(2,1)S(1)} %bitcast.25), channel_id=1, source_target_pairs={{0,1},{1,0},{2,3},{3,2},{4,5},{5,4},{6,7},{7,6},{8,9},{9,8},{10,11... | collective-permute-start | bytes 1572872 | tf_op jit(solution)/shard_map/ppermute | solution.py:575
  164.7 6.6 %collective-permute-start.55 = (s16[64,32,128]{2,1,0:T(8,128)(2,1)S(1)}, s16[64,32,128]{2,1,0:T(8,128)(2,1)S(1)}, u32[]{:S(2)}, u32[]{:S(2)}) collective-permute-start(s16[64,32,128]{2,1,0:T(8,128)(2,1)S(1)} %bitcast.27), channel_id=1, source_target_pairs={{0,1},{1,0},{2,3},{3,2},{4,5},{5,4},{6,7},{7,6},{8,9},{9,8},{10,11... | collective-permute-start | bytes 1572872 | tf_op jit(solution)/shard_map/ppermute | solution.py:575
  (35 other events, 149.3 us)

commit v16 on v15

--- a/solution.py
+++ b/solution.py
@@ -377,9 +377,9 @@
             refs[which - 2][me ^ k] = ref[which]
 
 
-def gather_kernel(flag_ref, *refs, slot):
+def gather_kernel(flag_ref, *refs, received, slot):
     me = flag_ref[slot]
-    for k, ref in enumerate(refs[:-1]):
+    for k, ref in enumerate(refs[:received]):
         refs[-1][me ^ k] = ref[...]
 
 
@@ -455,8 +455,7 @@
     put_rows(sums_ref, group_sums(first), group_sums(second))
 
 
-def decoded_grad_kernel(scaled, latent, cotangent, par_ref, st_ref, sums_ref, out_ref, token_ref, *, count):
-    token_ref[...] = jnp.zeros(token_ref.shape, F32)
+def decoded_grad_kernel(scaled, latent, cotangent, par_ref, st_ref, sums_ref, out_ref, *, count):
     rows, frames, channels, cols = latent.shape
     mean, inverse, _, _, scale = norm_columns(par_ref, st_ref, count, 1)
     means = sums_ref[0] / count
@@ -627,19 +626,20 @@
     values = call(
         functools.partial(split_kernel, received=len(pieces), slot=number),
         [shape((len(pieces), rows, SLOTS, channels), jnp.int16)] * 2,
-        [SMEM] + [VMEM] * (len(pieces) + 1),
-        (flags, *pieces, after_last),
+        [SMEM] + [VMEM] * len(pieces),
+        (flags, *pieces),
     )
     results = []
-    for value in values:
+    for which, value in enumerate(values):
+        after = (after_last,) if which else ()
         for number, (axis, _, exchanges) in back[1:]:
             value = value.reshape(-1, SLOTS, channels)
             pieces = [value] + [lax.ppermute(value, axis, pairs) for pairs in exchanges]
             (value,) = call(
-                functools.partial(gather_kernel, slot=number),
+                functools.partial(gather_kernel, received=len(pieces), slot=number),
                 [shape((len(pieces), *value.shape), jnp.int16)],
-                [SMEM] + [VMEM] * len(pieces),
-                (flags, *pieces),
+                [SMEM] + [VMEM] * (len(pieces) + len(after)),
+                (flags, *pieces, *after),
             )
         results.append(value.reshape(-1, SLOTS, channels))
     return results
@@ -807,13 +807,13 @@
     )
     total, sums_first = summed(flags, weights, sums_first, around[:2])
     sums_first = all_sum(sums_first, axes=("height", "width"))
-    decoded_grad, token = call(
+    (decoded_grad,) = call(
         functools.partial(decoded_grad_kernel, count=count),
-        [shape((channels, frames, rows, cols), F32), shape((8, 128), F32)],
+        [shape((channels, frames, rows, cols), F32)],
         [VMEM] * 6,
         (scaled, latent, cotangent, par, stats_first, sums_first),
     )
-    second, first = gathered(flags, total, token)
+    second, first = gathered(flags, total, sums_first)
     conv_second_grad = joined(flags, second, swapped(second))
     conv_first_grad = joined(flags, first, swapped(first))
     return decoded_grad, conv_first_grad, conv_second_grad

time: 176 us -> 177 us (level)
  waiting for transfers between devices: 31.1 us -> 36.5 us
  starting transfers between devices: 89.6 us -> 85.1 us
    ppermute x6, waiting for transfers between devices: 2.43 us -> 7.32 us  [gathered(): pieces = [value] + [lax.ppermute(value, axis, pairs) for pairs in exchanges]]
    ppermute x10, starting transfers between devices: 13 us -> 8.73 us  [swapped(): return lax.ppermute(value, 'width', [(0, 1), (1, 0)])]
  transfers between devices with their start and end apart: 60 -> 60, of which waited for: 18 -> 19; matrix products, arithmetic and copies ran while one was open for 0% -> 0% of each run, Pallas kernels for 20% -> 20%
where the time goes in v16:
time: 177 us; the launch traced here: 176 us
  starting transfers between devices  85.1 us (48%)
  Pallas kernels  47.8 us (27%)
  waiting for transfers between devices  36.5 us (21%)
  local copies, waits for them, and re-layouts  4.96 us (3%)
    pallas_call x30, Pallas kernels, call(): pl.pallas_call(body, out_shape=tuple(outs), in_specs=specs, out_specs=tup...  47.8 us
    ppermute x14, starting transfers between devices, all_stats(): parts = [value] + [lax.ppermute(value, axis, pairs) for pairs in exchanges]  23.7 us
    ppermute x10, starting transfers between devices, shifted(): lax.ppermute(value, axis, [(source, source + steps) for source in range(i...  20.7 us
    ppermute x11, starting transfers between devices, all_sum(): parts = [value] + [lax.ppermute(value, axis, pairs) for pairs in exchanges]  15.2 us
    ppermute x10, waiting for transfers between devices, shifted(): lax.ppermute(value, axis, [(source, source + steps) for source in range(i...  11.1 us
    ppermute x10, starting transfers between devices, swapped(): return lax.ppermute(value, 'width', [(0, 1), (1, 0)])  8.73 us
    ppermute x6, waiting for transfers between devices, gathered(): pieces = [value] + [lax.ppermute(value, axis, pairs) for pairs in exchanges]  7.32 us
    ppermute x6, starting transfers between devices, gathered(): pieces = [value] + [lax.ppermute(value, axis, pairs) for pairs in exchanges]  4.9 us
  transfers between devices with their start and end apart: 60, of which 19 were waited for; matrix products, arithmetic and copies ran while one was open for 0% of the time, Pallas kernels for 20%

profile of v16, /device:TPU:1, one launch (start us, length us, event | category | flops | bytes accessed | tf_op | source)
XLA Modules:
  0.0 176.2 jit_solution(14830258773447230082)
XLA Ops:
  4.3 2.6 %shard_map.112 = (bf16[4,2,128,256]{3,2,1,0:T(8,128)(2,1)S(1)}, bf16[4,2,128,256]{3,2,1,0:T(8,128)(2,1)S(1)}, bf16[2,2,128,256]{3,2,1,0:T(8,128)(2,1)S(1)}, bf16...) custom-call(bf16[128,2,4,256]{3,2,1,0:T(4,128)(2,1)S(1)} %copy-done.3, bf16[128,2,4,256]{3,2,1,0:T(4,128)(2,1)S(1)} %copy-done.4, ...), custom_call_target="tpu_custom_call" | custom-call | bytes 2626560 | tf_op jit(solution)/shard_map/pallas_call | solution.py:24
  7.0 2.2 %collective-permute-start.6 = (f32[1,2,128]{2,1,0:T(2,128)S(1)}, f32[1,2,128]{2,1,0:T(2,128)S(1)}, u32[]{:S(2)}, u32[]{:S(2)}) collective-permute-start(f32[1,2,128]{2,1,0:T(2,128)S(1)} %get-tuple-element.45), channel_id=1, source_target_pairs={{0,8},{8,0},{16,24},{24,16},{1,9},{9,1},{17,25},{25,17},{2,10},{10... | collective-permute-start | bytes 3080 | tf_op jit(solution)/shard_map/ppermute | solution.py:557
  9.2 2.3 %collective-permute-start.7 = (f32[1,2,128]{2,1,0:T(2,128)S(1)}, f32[1,2,128]{2,1,0:T(2,128)S(1)}, u32[]{:S(2)}, u32[]{:S(2)}) collective-permute-start(f32[1,2,128]{2,1,0:T(2,128)S(1)} %get-tuple-element.45), channel_id=1, source_target_pairs={{0,16},{8,24},{16,0},{24,8},{1,17},{9,25},{17,1},{25,9},{2,18},{10... | collective-permute-start | bytes 3080 | tf_op jit(solution)/shard_map/ppermute | solution.py:557
  11.5 3.1 %collective-permute-start.1 = (bf16[2,2,128,256]{3,2,1,0:T(8,128)(2,1)S(1)}, bf16[2,2,128,256]{3,2,1,0:T(8,128)(2,1)S(1)}, u32[]{:S(2)}, u32[]{:S(2)}) collective-permute-start(bf16[2,2,128,256]{3,2,1,0:T(8,128)(2,1)S(1)} %get-tuple-element.42), channel_id=1, source_target_pairs={{0,2},{2,4},{4,6},{1,3},{3,5},{5,7},{8,10},{10,12},{12,14},{9,11},... | collective-permute-start | bytes 786440 | tf_op jit(solution)/shard_map/ppermute | solution.py:512
  16.0 3.1 %collective-permute-start.10 = (f32[1,2,128]{2,1,0:T(2,128)S(1)}, f32[1,2,128]{2,1,0:T(2,128)S(1)}, u32[]{:S(2)}, u32[]{:S(2)}) collective-permute-start(f32[1,2,128]{2,1,0:T(2,128)S(1)} %pad_maximum_fusion), channel_id=1, source_target_pairs={{0,4},{2,6},{4,0},{6,2},{1,5},{3,7},{5,1},{7,3},{8,12},{10,14},{12... | collective-permute-start | bytes 3080 | tf_op jit(solution)/shard_map/ppermute | solution.py:557
  20.3 3.1 %collective-permute-start = (bf16[4,2,128,256]{3,2,1,0:T(8,128)(2,1)S(1)}, bf16[4,2,128,256]{3,2,1,0:T(8,128)(2,1)}, u32[]{:S(2)}, u32[]{:S(2)}) collective-permute-start(bf16[4,2,128,256]{3,2,1,0:T(8,128)(2,1)S(1)} %get-tuple-element.41.first_ref.own.refs_7_.latent), channel_id=1, source_target_pairs={{0,8},{8,16},{16,24},{1,9},{9,17},{17,25},{2,10},{10,18},{18,26},{... | collective-permute-start | bytes 1572872 | tf_op jit(solution)/shard_map/ppermute | solution.py:512
  27.8 3.0 %collective-permute-start.3 = (bf16[2,2,128,256]{3,2,1,0:T(8,128)(2,1)}, bf16[2,2,128,256]{3,2,1,0:T(8,128)(2,1)}, u32[]{:S(2)}, u32[]{:S(2)}) collective-permute-start(bf16[2,2,128,256]{3,2,1,0:T(8,128)(2,1)} %get-tuple-element.44.first_ref.near), channel_id=1, source_target_pairs={{0,8},{8,16},{16,24},{1,9},{9,17},{17,25},{2,10},{10,18},{18,26},{... | collective-permute-start | bytes 786440 | tf_op jit(solution)/shard_map/ppermute | solution.py:512
  30.8 3.5 %collective-permute-start.12 = (f32[1,2,128]{2,1,0:T(2,128)S(1)}, f32[1,2,128]{2,1,0:T(2,128)S(1)}, u32[]{:S(2)}, u32[]{:S(2)}) collective-permute-start(f32[1,2,128]{2,1,0:T(2,128)S(1)} %pad_maximum_fusion.1), channel_id=1, source_target_pairs={{0,1},{1,0},{2,3},{3,2},{4,5},{5,4},{6,7},{7,6},{8,9},{9,8},{10,11... | collective-permute-start | bytes 3080 | tf_op jit(solution)/shard_map/ppermute | solution.py:557
  38.5 3.1 %collective-permute-start.5 = (bf16[128,128]{1,0:T(8,128)(2,1)S(1)}, bf16[128,128]{1,0:T(8,128)(2,1)S(1)}, u32[]{:S(2)}, u32[]{:S(2)}) collective-permute-start(bf16[128,128]{1,0:T(8,128)(2,1)S(1)} %shard_map.115), channel_id=1, source_target_pairs={{0,1},{1,0},{2,3},{3,2},{4,5},{5,4},{6,7},{7,6},{8,9},{9,8},{10,11... | collective-permute-start | bytes 98312 | tf_op jit(solution)/shard_map/ppermute | solution.py:574
  43.0 2.8 %collective-permute-done.13.after.second_ref.refs_3_ = bf16[2,2,128,256]{3,2,1,0:T(8,128)(2,1)S(1)} collective-permute-done((bf16[2,2,128,256]{3,2,1,0:T(8,128)(2,1)}, bf16[2,2,128,256]{3,2,1,0:T(8,128)(2,1)S(1)}, u32[]{:S(2)}, u32[]{:S(2)}) %collective-permute-start.13) | collective-permute-done | bytes 262176 | tf_op jit(solution)/shard_map/ppermute | solution.py:512
  45.8 5.3 %shard_map.117 = (f32[4,2,128,256]{3,2,1,0:T(8,128)S(1)}, f32[1,2,128]{2,1,0:T(2,128)S(1)}, bf16[6,4,384,256]{3,2,1,0:T(8,128)(2,1)S(1)}) custom-call(s32[6]{0:T(128)S(1)} %stack.57.flag_ref, bf16[4,2,128,256]{3,2,1,0:T(8,128)(2,1)S(1)} %get-tuple-element.41.first_ref.own.refs_7_.latent, bf16[4,2,128,256]{3,2,1,0:T(8,128)(2,1)} %collective-permute-done.second_ref.past, ...), custom_call_target="tpu_custom_call" | custom-call | flops 7247757312 | bytes 10033176 | tf_op jit(solution)/shard_map/pallas_call | solution.py:24
  55.9 2.1 %collective-permute-start.18 = (f32[1,2,128]{2,1,0:T(2,128)S(1)}, f32[1,2,128]{2,1,0:T(2,128)S(1)}, u32[]{:S(2)}, u32[]{:S(2)}) collective-permute-start(f32[1,2,128]{2,1,0:T(2,128)S(1)} %get-tuple-element.49.refs_0_), channel_id=1, source_target_pairs={{0,16},{8,24},{16,0},{24,8},{1,17},{9,25},{17,1},{25,9},{2,18},{10... | collective-permute-start | bytes 3080 | tf_op jit(solution)/shard_map/ppermute | solution.py:557
  58.2 3.9 %shard_map.121 = (f32[4,2,128,256]{3,2,1,0:T(8,128)S(1)}, bf16[6,4,384,256]{3,2,1,0:T(8,128)(2,1)S(1)}) custom-call(s32[6]{0:T(128)S(1)} %stack.57.flag_ref, bf16[4,2,128,256]{3,2,1,0:T(8,128)(2,1)S(1)} %get-tuple-element.48.first_ref.refs_0_.cotangent, bf16[4,2,128,256]{3,2,1,0:T(8,128)(2,1)} %collective-permute-done.14.second_ref.refs_1_, ...), custom_call_target="tpu_custom_call" | custom-call | flops 7247757312 | bytes 9764888 | tf_op jit(solution)/shard_map/pallas_call | solution.py:24
  62.2 3.5 %collective-permute-start.20 = (f32[1,2,128]{2,1,0:T(2,128)S(1)}, f32[1,2,128]{2,1,0:T(2,128)S(1)}, u32[]{:S(2)}, u32[]{:S(2)}) collective-permute-start(f32[1,2,128]{2,1,0:T(2,128)S(1)} %shard_map.122), channel_id=1, source_target_pairs={{0,2},{2,0},{4,6},{6,4},{1,3},{3,1},{5,7},{7,5},{8,10},{10,8},{12,... | collective-permute-start | bytes 3080 | tf_op jit(solution)/shard_map/ppermute | solution.py:557
  69.1 2.8 %collective-permute-start.23 = (f32[1,2,128]{2,1,0:T(2,128)S(1)}, f32[1,2,128]{2,1,0:T(2,128)S(1)}, u32[]{:S(2)}, u32[]{:S(2)}) collective-permute-start(f32[1,2,128]{2,1,0:T(2,128)S(1)} %pad_maximum_fusion.3), channel_id=1, source_target_pairs={{0,1},{1,0},{2,3},{3,2},{4,5},{5,4},{6,7},{7,6},{8,9},{9,8},{10,11... | collective-permute-start | bytes 3080 | tf_op jit(solution)/shard_map/ppermute | solution.py:557
  77.3 4.1 %shard_map.124 = (f32[2048,128]{1,0:T(8,128)S(1)}, f32[2048,128]{1,0:T(8,128)S(1)}) custom-call(s32[6]{0:T(128)S(1)} %stack.57.flag_ref, bf16[6,4,384,256]{3,2,1,0:T(8,128)(2,1)S(1)} %get-tuple-element.53.stack_ref, bf16[4,2,128,256]{3,2,1,0:T(8,128)(2,1)S(1)} %get-tuple-element.54.act_ref), custom_call_target="tpu_custom_call" | custom-call | flops 7247757312 | bytes 7340056 | tf_op jit(solution)/shard_map/pallas_call | solution.py:24
  86.7 2.6 %collective-permute-start.30 = (f32[1,2,128]{2,1,0:T(2,128)S(1)}, f32[1,2,128]{2,1,0:T(2,128)S(1)}, u32[]{:S(2)}, u32[]{:S(2)}) collective-permute-start(f32[1,2,128]{2,1,0:T(2,128)S(1)} %add_add_fusion.1), channel_id=1, source_target_pairs={{0,1},{1,0},{2,3},{3,2},{4,5},{5,4},{6,7},{7,6},{8,9},{9,8},{10,11... | collective-permute-start | bytes 3080 | tf_op jit(solution)/shard_map/ppermute | solution.py:541
  92.1 3.6 %collective-permute-start.32 = (bf16[1,2,128,256]{3,2,1,0:T(8,128)(2,1)S(1)}, bf16[1,2,128,256]{3,2,1,0:T(8,128)(2,1)S(1)}, u32[]{:S(2)}, u32[]{:S(2)}) collective-permute-start(bf16[1,2,128,256]{3,2,1,0:T(8,128)(2,1)S(1)} %get-tuple-element.57), channel_id=1, source_target_pairs={{0,2},{2,4},{4,6},{1,3},{3,5},{5,7},{8,10},{10,12},{12,14},{9,11},... | collective-permute-start | bytes 393224 | tf_op jit(solution)/shard_map/ppermute | solution.py:512
  97.0 4.6 %shard_map.127 = (f32[2048,128]{1,0:T(8,128)S(1)}, f32[2048,128]{1,0:T(8,128)S(1)}) custom-call(s32[6]{0:T(128)S(1)} %stack.57.flag_ref, bf16[6,4,384,256]{3,2,1,0:T(8,128)(2,1)S(1)} %get-tuple-element.59.stack_ref, bf16[4,2,128,256]{3,2,1,0:T(8,128)(2,1)S(1)} %get-tuple-element.56.grad_ref.first_ref.refs_0_), custom_call_target="tpu_custom_call" | custom-call | flops 7247757312 | bytes 7340056 | tf_op jit(solution)/shard_map/pallas_call | solution.py:24
  103.1 2.8 %collective-permute-done.31.after.second_ref.refs_1_.refs_4_ = bf16[4,2,128,256]{3,2,1,0:T(8,128)(2,1)S(1)} collective-permute-done((bf16[4,2,128,256]{3,2,1,0:T(8,128)(2,1)S(1)}, bf16[4,2,128,256]{3,2,1,0:T(8,128)(2,1)S(1)}, u32[]{:S(2)}, u32[]{:S(2)}) %collective-permute-start.31) | collective-permute-done | bytes 524320 | tf_op jit(solution)/shard_map/ppermute | solution.py:512
  113.2 4.0 %collective-permute-done.34.second_ref.refs_3_ = bf16[2,2,128,256]{3,2,1,0:T(8,128)(2,1)S(1)} collective-permute-done((bf16[2,2,128,256]{3,2,1,0:T(8,128)(2,1)S(1)}, bf16[2,2,128,256]{3,2,1,0:T(8,128)(2,1)S(1)}, u32[]{:S(2)}, u32[]{:S(2)}) %collective-permute-start.34) | collective-permute-done | bytes 262176 | tf_op jit(solution)/shard_map/ppermute | solution.py:512
  120.8 4.0 %collective-permute-done.41.refs_12_ = s16[2,16,32,128]{3,2,1,0:T(8,128)(2,1)S(1)} collective-permute-done((s16[2,16,32,128]{3,2,1,0:T(8,128)(2,1)S(1)}, s16[2,16,32,128]{3,2,1,0:T(8,128)(2,1)S(1)}, u32[]{:S(2)}, u32[]{:S(2)}) %collective-permute-start.41) | collective-permute-done | bytes 262176 | tf_op jit(solution)/shard_map/ppermute | solution.py:594
  124.8 4.0 %shard_map.133 = (f32[4,2,128,256]{3,2,1,0:T(8,128)S(1)}, f32[1,2,128]{2,1,0:T(2,128)S(1)}) custom-call(s32[6]{0:T(128)S(1)} %stack.57.flag_ref, bf16[4,2,128,256]{3,2,1,0:T(8,128)(2,1)S(1)} %get-tuple-element.56.grad_ref.first_ref.refs_0_, bf16[4,2,128,256]{3,2,1,0:T(8,128)(2,1)S(1)} %collective-permute-done.31.after.second_ref.refs_1_.refs_4_, ...), custom_call_target="tpu_custom_call" | custom-call | flops 7247757312 | bytes 6363160 | tf_op jit(solution)/shard_map/pallas_call | solution.py:24
  131.7 2.2 %collective-permute-start.44 = (s16[2,4,32,128]{3,2,1,0:T(8,128)(2,1)S(1)}, s16[2,4,32,128]{3,2,1,0:T(8,128)(2,1)S(1)}, u32[]{:S(2)}, u32[]{:S(2)}) collective-permute-start(s16[2,4,32,128]{3,2,1,0:T(8,128)(2,1)S(1)} %get-tuple-element.74), channel_id=1, source_target_pairs={{0,24},{8,16},{16,8},{24,0},{1,25},{9,17},{17,9},{25,1},{2,26},{10... | collective-permute-start | bytes 196616 | tf_op jit(solution)/shard_map/ppermute | solution.py:612
  133.9 4.2 %collective-permute-done.43.refs_2_ = s16[2,4,32,128]{3,2,1,0:T(8,128)(2,1)S(1)} collective-permute-done((s16[2,4,32,128]{3,2,1,0:T(8,128)(2,1)S(1)}, s16[2,4,32,128]{3,2,1,0:T(8,128)(2,1)S(1)}, u32[]{:S(2)}, u32[]{:S(2)}) %collective-permute-start.43) | collective-permute-done | bytes 65568 | tf_op jit(solution)/shard_map/ppermute | solution.py:612
  138.2 2.5 %collective-permute-start.49 = (s16[2,4,32,128]{3,2,1,0:T(8,128)(2,1)S(1)}, s16[2,4,32,128]{3,2,1,0:T(8,128)(2,1)S(1)}, u32[]{:S(2)}, u32[]{:S(2)}) collective-permute-start(s16[2,4,32,128]{3,2,1,0:T(8,128)(2,1)S(1)} %get-tuple-element.76.refs_0_), channel_id=1, source_target_pairs={{0,8},{8,0},{16,24},{24,16},{1,9},{9,1},{17,25},{25,17},{2,10},{10... | collective-permute-start | bytes 196616 | tf_op jit(solution)/shard_map/ppermute | solution.py:625
  140.7 2.2 %collective-permute-start.51 = (s16[2,4,32,128]{3,2,1,0:T(8,128)(2,1)S(1)}, s16[2,4,32,128]{3,2,1,0:T(8,128)(2,1)S(1)}, u32[]{:S(2)}, u32[]{:S(2)}) collective-permute-start(s16[2,4,32,128]{3,2,1,0:T(8,128)(2,1)S(1)} %get-tuple-element.76.refs_0_), channel_id=1, source_target_pairs={{0,24},{8,16},{16,8},{24,0},{1,25},{9,17},{17,9},{25,1},{2,26},{10... | collective-permute-start | bytes 196616 | tf_op jit(solution)/shard_map/ppermute | solution.py:625
  148.1 3.4 %collective-permute-start.48 = (f32[1,2,128]{2,1,0:T(2,128)S(1)}, f32[1,2,128]{2,1,0:T(2,128)S(1)}, u32[]{:S(2)}, u32[]{:S(2)}) collective-permute-start(f32[1,2,128]{2,1,0:T(2,128)S(1)} %add_add_fusion), channel_id=1, source_target_pairs={{0,1},{1,0},{2,3},{3,2},{4,5},{5,4},{6,7},{7,6},{8,9},{9,8},{10,11... | collective-permute-start | bytes 3080 | tf_op jit(solution)/shard_map/ppermute | solution.py:541
  155.7 3.7 %collective-permute-done.57.refs_2_ = s16[16,32,128]{2,1,0:T(8,128)(2,1)S(1)} collective-permute-done((s16[16,32,128]{2,1,0:T(8,128)(2,1)S(1)}, s16[16,32,128]{2,1,0:T(8,128)(2,1)S(1)}, u32[]{:S(2)}, u32[]{:S(2)}) %collective-permute-start.57) | collective-permute-done | bytes 131104 | tf_op jit(solution)/shard_map/ppermute | solution.py:637
  161.4 3.6 %collective-permute-done.53.refs_2_ = s16[16,32,128]{2,1,0:T(8,128)(2,1)S(1)} collective-permute-done((s16[16,32,128]{2,1,0:T(8,128)(2,1)S(1)}, s16[16,32,128]{2,1,0:T(8,128)(2,1)S(1)}, u32[]{:S(2)}, u32[]{:S(2)}) %collective-permute-start.53) | collective-permute-done | bytes 131104 | tf_op jit(solution)/shard_map/ppermute | solution.py:637
  168.4 3.9 %shard_map.141 = f32[128,3456]{1,0:T(8,128)} custom-call(s32[6]{0:T(128)S(1)} %stack.57.flag_ref, s16[64,32,128]{2,1,0:T(8,128)(2,1)S(1)} %bitcast.28, s16[64,32,128]{2,1,0:T(8,128)(2,1)S(1)} %collective-permute-done.59.theirs_ref), custom_call_target="tpu_custom_call" | custom-call | bytes 2818072 | tf_op jit(solution)/shard_map/pallas_call | solution.py:24
  172.3 3.9 %shard_map.139 = f32[128,3456]{1,0:T(8,128)} custom-call(s32[6]{0:T(128)S(1)} %stack.57.flag_ref, s16[64,32,128]{2,1,0:T(8,128)(2,1)S(1)} %bitcast.26, s16[64,32,128]{2,1,0:T(8,128)(2,1)S(1)} %collective-permute-done.55.theirs_ref), custom_call_target="tpu_custom_call" | custom-call | bytes 2818072 | tf_op jit(solution)/shard_map/pallas_call | solution.py:24
  (153 shorter events, 69.4 us)
Async XLA Ops:
  7.0 8.9 %collective-permute-start.6 = (f32[1,2,128]{2,1,0:T(2,128)S(1)}, f32[1,2,128]{2,1,0:T(2,128)S(1)}, u32[]{:S(2)}, u32[]{:S(2)}) collective-permute-start(f32[1,2,128]{2,1,0:T(2,128)S(1)} %get-tuple-element.45), channel_id=1, source_target_pairs={{0,8},{8,0},{16,24},{24,16},{1,9},{9,1},{17,25},{25,17},{2,10},{10... | collective-permute-start | bytes 3080 | tf_op jit(solution)/shard_map/ppermute | solution.py:557
  9.2 6.8 %collective-permute-start.7 = (f32[1,2,128]{2,1,0:T(2,128)S(1)}, f32[1,2,128]{2,1,0:T(2,128)S(1)}, u32[]{:S(2)}, u32[]{:S(2)}) collective-permute-start(f32[1,2,128]{2,1,0:T(2,128)S(1)} %get-tuple-element.45), channel_id=1, source_target_pairs={{0,16},{8,24},{16,0},{24,8},{1,17},{9,25},{17,1},{25,9},{2,18},{10... | collective-permute-start | bytes 3080 | tf_op jit(solution)/shard_map/ppermute | solution.py:557
  11.5 14.9 %collective-permute-start.1 = (bf16[2,2,128,256]{3,2,1,0:T(8,128)(2,1)S(1)}, bf16[2,2,128,256]{3,2,1,0:T(8,128)(2,1)S(1)}, u32[]{:S(2)}, u32[]{:S(2)}) collective-permute-start(bf16[2,2,128,256]{3,2,1,0:T(8,128)(2,1)S(1)} %get-tuple-element.42), channel_id=1, source_target_pairs={{0,2},{2,4},{4,6},{1,3},{3,5},{5,7},{8,10},{10,12},{12,14},{9,11},... | collective-permute-start | bytes 786440 | tf_op jit(solution)/shard_map/ppermute | solution.py:512
  14.6 11.7 %collective-permute-start.2 = (bf16[2,2,128,256]{3,2,1,0:T(8,128)(2,1)S(1)}, bf16[2,2,128,256]{3,2,1,0:T(8,128)(2,1)S(1)}, u32[]{:S(2)}, u32[]{:S(2)}) collective-permute-start(bf16[2,2,128,256]{3,2,1,0:T(8,128)(2,1)S(1)} %get-tuple-element.43), channel_id=1, source_target_pairs={{2,0},{4,2},{6,4},{3,1},{5,3},{7,5},{10,8},{12,10},{14,12},{11,9},... | collective-permute-start | bytes 786440 | tf_op jit(solution)/shard_map/ppermute | solution.py:512
  19.3 7.0 %collective-permute-start.9 = (f32[1,2,128]{2,1,0:T(2,128)S(1)}, f32[1,2,128]{2,1,0:T(2,128)S(1)}, u32[]{:S(2)}, u32[]{:S(2)}) collective-permute-start(f32[1,2,128]{2,1,0:T(2,128)S(1)} %pad_maximum_fusion), channel_id=1, source_target_pairs={{0,2},{2,0},{4,6},{6,4},{1,3},{3,1},{5,7},{7,5},{8,10},{10,8},{12,... | collective-permute-start | bytes 3080 | tf_op jit(solution)/shard_map/ppermute | solution.py:557
  20.3 21.3 %collective-permute-start = (bf16[4,2,128,256]{3,2,1,0:T(8,128)(2,1)S(1)}, bf16[4,2,128,256]{3,2,1,0:T(8,128)(2,1)}, u32[]{:S(2)}, u32[]{:S(2)}) collective-permute-start(bf16[4,2,128,256]{3,2,1,0:T(8,128)(2,1)S(1)} %get-tuple-element.41.first_ref.own.refs_7_.latent), channel_id=1, source_target_pairs={{0,8},{8,16},{16,24},{1,9},{9,17},{17,25},{2,10},{10,18},{18,26},{... | collective-permute-start | bytes 1572872 | tf_op jit(solution)/shard_map/ppermute | solution.py:512
  23.4 29.3 %collective-permute-start.14 = (bf16[4,2,128,256]{3,2,1,0:T(8,128)(2,1)S(1)}, bf16[4,2,128,256]{3,2,1,0:T(8,128)(2,1)}, u32[]{:S(2)}, u32[]{:S(2)}) collective-permute-start(bf16[4,2,128,256]{3,2,1,0:T(8,128)(2,1)S(1)} %get-tuple-element.48.first_ref.refs_0_.cotangent), channel_id=1, source_target_pairs={{8,0},{16,8},{24,16},{9,1},{17,9},{25,17},{10,2},{18,10},{26,18},{... | collective-permute-start | bytes 1572872 | tf_op jit(solution)/shard_map/ppermute | solution.py:512
  27.8 9.5 %collective-permute-start.3 = (bf16[2,2,128,256]{3,2,1,0:T(8,128)(2,1)}, bf16[2,2,128,256]{3,2,1,0:T(8,128)(2,1)}, u32[]{:S(2)}, u32[]{:S(2)}) collective-permute-start(bf16[2,2,128,256]{3,2,1,0:T(8,128)(2,1)} %get-tuple-element.44.first_ref.near), channel_id=1, source_target_pairs={{0,8},{8,16},{16,24},{1,9},{9,17},{17,25},{2,10},{10,18},{18,26},{... | collective-permute-start | bytes 786440 | tf_op jit(solution)/shard_map/ppermute | solution.py:512
  30.8 6.4 %collective-permute-start.12 = (f32[1,2,128]{2,1,0:T(2,128)S(1)}, f32[1,2,128]{2,1,0:T(2,128)S(1)}, u32[]{:S(2)}, u32[]{:S(2)}) collective-permute-start(f32[1,2,128]{2,1,0:T(2,128)S(1)} %pad_maximum_fusion.1), channel_id=1, source_target_pairs={{0,1},{1,0},{2,3},{3,2},{4,5},{5,4},{6,7},{7,6},{8,9},{9,8},{10,11... | collective-permute-start | bytes 3080 | tf_op jit(solution)/shard_map/ppermute | solution.py:557
  35.8 10.0 %collective-permute-start.13 = (bf16[2,2,128,256]{3,2,1,0:T(8,128)(2,1)}, bf16[2,2,128,256]{3,2,1,0:T(8,128)(2,1)S(1)}, u32[]{:S(2)}, u32[]{:S(2)}) collective-permute-start(bf16[2,2,128,256]{3,2,1,0:T(8,128)(2,1)} %copy-done.5), channel_id=1, source_target_pairs={{8,0},{16,8},{24,16},{9,1},{17,9},{25,17},{10,2},{18,10},{26,18},{... | collective-permute-start | bytes 786440 | tf_op jit(solution)/shard_map/ppermute | solution.py:512
  38.5 7.3 %collective-permute-start.5 = (bf16[128,128]{1,0:T(8,128)(2,1)S(1)}, bf16[128,128]{1,0:T(8,128)(2,1)S(1)}, u32[]{:S(2)}, u32[]{:S(2)}) collective-permute-start(bf16[128,128]{1,0:T(8,128)(2,1)S(1)} %shard_map.115), channel_id=1, source_target_pairs={{0,1},{1,0},{2,3},{3,2},{4,5},{5,4},{6,7},{7,6},{8,9},{9,8},{10,11... | collective-permute-start | bytes 98312 | tf_op jit(solution)/shard_map/ppermute | solution.py:574
  51.8 6.4 %collective-permute-start.16 = (bf16[128,128]{1,0:T(8,128)(2,1)S(1)}, bf16[128,128]{1,0:T(8,128)(2,1)S(1)}, u32[]{:S(2)}, u32[]{:S(2)}) collective-permute-start(bf16[128,128]{1,0:T(8,128)(2,1)S(1)} %shard_map.119), channel_id=1, source_target_pairs={{0,1},{1,0},{2,3},{3,2},{4,5},{5,4},{6,7},{7,6},{8,9},{9,8},{10,11... | collective-permute-start | bytes 98312 | tf_op jit(solution)/shard_map/ppermute | solution.py:574
  54.4 7.8 %collective-permute-start.17 = (f32[1,2,128]{2,1,0:T(2,128)S(1)}, f32[1,2,128]{2,1,0:T(2,128)S(1)}, u32[]{:S(2)}, u32[]{:S(2)}) collective-permute-start(f32[1,2,128]{2,1,0:T(2,128)S(1)} %get-tuple-element.49.refs_0_), channel_id=1, source_target_pairs={{0,8},{8,0},{16,24},{24,16},{1,9},{9,1},{17,25},{25,17},{2,10},{10... | collective-permute-start | bytes 3080 | tf_op jit(solution)/shard_map/ppermute | solution.py:557
  73.7 7.7 %collective-permute-start.24 = (f32[1,2,128]{2,1,0:T(2,128)S(1)}, f32[1,2,128]{2,1,0:T(2,128)S(1)}, u32[]{:S(2)}, u32[]{:S(2)}) collective-permute-start(f32[1,2,128]{2,1,0:T(2,128)S(1)} %get-tuple-element.52.refs_0_), channel_id=1, source_target_pairs={{0,8},{8,0},{16,24},{24,16},{1,9},{9,1},{17,25},{25,17},{2,10},{10... | collective-permute-start | bytes 3080 | tf_op jit(solution)/shard_map/ppermute | solution.py:541
  73.7 7.7 %collective-permute-start.25 = (f32[1,2,128]{2,1,0:T(2,128)S(1)}, f32[1,2,128]{2,1,0:T(2,128)S(1)}, u32[]{:S(2)}, u32[]{:S(2)}) collective-permute-start(f32[1,2,128]{2,1,0:T(2,128)S(1)} %get-tuple-element.52.refs_0_), channel_id=1, source_target_pairs={{0,16},{8,24},{16,0},{24,8},{1,17},{9,25},{17,1},{25,9},{2,18},{10... | collective-permute-start | bytes 3080 | tf_op jit(solution)/shard_map/ppermute | solution.py:541
  89.3 19.4 %collective-permute-start.35 = (f32[64,32,128]{2,1,0:T(8,128)S(1)}, f32[64,32,128]{2,1,0:T(8,128)S(1)}, u32[]{:S(2)}, u32[]{:S(2)}) collective-permute-start(f32[64,32,128]{2,1,0:T(8,128)S(1)} %bitcast.45), channel_id=1, source_target_pairs={{0,1},{1,0},{2,3},{3,2},{4,5},{5,4},{6,7},{7,6},{8,9},{9,8},{10,11... | collective-permute-start | bytes 3145736 | tf_op jit(solution)/shard_map/ppermute | solution.py:574
  90.8 15.1 %collective-permute-start.31 = (bf16[4,2,128,256]{3,2,1,0:T(8,128)(2,1)S(1)}, bf16[4,2,128,256]{3,2,1,0:T(8,128)(2,1)S(1)}, u32[]{:S(2)}, u32[]{:S(2)}) collective-permute-start(bf16[4,2,128,256]{3,2,1,0:T(8,128)(2,1)S(1)} %get-tuple-element.56.grad_ref.first_ref.refs_0_), channel_id=1, source_target_pairs={{8,0},{16,8},{24,16},{9,1},{17,9},{25,17},{10,2},{18,10},{26,18},{... | collective-permute-start | bytes 1572872 | tf_op jit(solution)/shard_map/ppermute | solution.py:512
  92.1 9.5 %collective-permute-start.32 = (bf16[1,2,128,256]{3,2,1,0:T(8,128)(2,1)S(1)}, bf16[1,2,128,256]{3,2,1,0:T(8,128)(2,1)S(1)}, u32[]{:S(2)}, u32[]{:S(2)}) collective-permute-start(bf16[1,2,128,256]{3,2,1,0:T(8,128)(2,1)S(1)} %get-tuple-element.57), channel_id=1, source_target_pairs={{0,2},{2,4},{4,6},{1,3},{3,5},{5,7},{8,10},{10,12},{12,14},{9,11},... | collective-permute-start | bytes 393224 | tf_op jit(solution)/shard_map/ppermute | solution.py:512
  95.7 7.4 %collective-permute-start.33 = (bf16[1,2,128,256]{3,2,1,0:T(8,128)(2,1)S(1)}, bf16[1,2,128,256]{3,2,1,0:T(8,128)(2,1)S(1)}, u32[]{:S(2)}, u32[]{:S(2)}) collective-permute-start(bf16[1,2,128,256]{3,2,1,0:T(8,128)(2,1)S(1)} %get-tuple-element.58), channel_id=1, source_target_pairs={{2,0},{4,2},{6,4},{3,1},{5,3},{7,5},{10,8},{12,10},{14,12},{11,9},... | collective-permute-start | bytes 393224 | tf_op jit(solution)/shard_map/ppermute | solution.py:512
  107.4 9.8 %collective-permute-start.34 = (bf16[2,2,128,256]{3,2,1,0:T(8,128)(2,1)S(1)}, bf16[2,2,128,256]{3,2,1,0:T(8,128)(2,1)S(1)}, u32[]{:S(2)}, u32[]{:S(2)}) collective-permute-start(bf16[2,2,128,256]{3,2,1,0:T(8,128)(2,1)S(1)} %get-tuple-element.61.first_ref.refs_2_.refs_5_), channel_id=1, source_target_pairs={{8,0},{16,8},{24,16},{9,1},{17,9},{25,17},{10,2},{18,10},{26,18},{... | collective-permute-start | bytes 786440 | tf_op jit(solution)/shard_map/ppermute | solution.py:512
  110.2 10.6 %collective-permute-start.39 = (s16[2,16,32,128]{3,2,1,0:T(8,128)(2,1)S(1)}, s16[2,16,32,128]{3,2,1,0:T(8,128)(2,1)S(1)}, u32[]{:S(2)}, u32[]{:S(2)}) collective-permute-start(s16[2,16,32,128]{3,2,1,0:T(8,128)(2,1)S(1)} %get-tuple-element.65.refs_0_), channel_id=1, source_target_pairs={{0,2},{2,0},{4,6},{6,4},{1,3},{3,1},{5,7},{7,5},{8,10},{10,8},{12,... | collective-permute-start | bytes 786440 | tf_op jit(solution)/shard_map/ppermute | solution.py:594
  111.9 8.9 %collective-permute-start.40 = (s16[2,16,32,128]{3,2,1,0:T(8,128)(2,1)S(1)}, s16[2,16,32,128]{3,2,1,0:T(8,128)(2,1)S(1)}, u32[]{:S(2)}, u32[]{:S(2)}) collective-permute-start(s16[2,16,32,128]{3,2,1,0:T(8,128)(2,1)S(1)} %get-tuple-element.66), channel_id=1, source_target_pairs={{0,4},{2,6},{4,0},{6,2},{1,5},{3,7},{5,1},{7,3},{8,12},{10,14},{12... | collective-permute-start | bytes 786440 | tf_op jit(solution)/shard_map/ppermute | solution.py:594
  111.9 12.8 %collective-permute-start.41 = (s16[2,16,32,128]{3,2,1,0:T(8,128)(2,1)S(1)}, s16[2,16,32,128]{3,2,1,0:T(8,128)(2,1)S(1)}, u32[]{:S(2)}, u32[]{:S(2)}) collective-permute-start(s16[2,16,32,128]{3,2,1,0:T(8,128)(2,1)S(1)} %get-tuple-element.67), channel_id=1, source_target_pairs={{0,6},{2,4},{4,2},{6,0},{1,7},{3,5},{5,3},{7,1},{8,14},{10,12},{12... | collective-permute-start | bytes 786440 | tf_op jit(solution)/shard_map/ppermute | solution.py:594
  131.7 6.3 %collective-permute-start.43 = (s16[2,4,32,128]{3,2,1,0:T(8,128)(2,1)S(1)}, s16[2,4,32,128]{3,2,1,0:T(8,128)(2,1)S(1)}, u32[]{:S(2)}, u32[]{:S(2)}) collective-permute-start(s16[2,4,32,128]{3,2,1,0:T(8,128)(2,1)S(1)} %get-tuple-element.73), channel_id=1, source_target_pairs={{0,16},{8,24},{16,0},{24,8},{1,17},{9,25},{17,1},{25,9},{2,18},{10... | collective-permute-start | bytes 196616 | tf_op jit(solution)/shard_map/ppermute | solution.py:612
  146.5 8.3 %collective-permute-start.56 = (s16[16,32,128]{2,1,0:T(8,128)(2,1)S(1)}, s16[16,32,128]{2,1,0:T(8,128)(2,1)S(1)}, u32[]{:S(2)}, u32[]{:S(2)}) collective-permute-start(s16[16,32,128]{2,1,0:T(8,128)(2,1)S(1)} %bitcast.41), channel_id=1, source_target_pairs={{0,2},{2,0},{4,6},{6,4},{1,3},{3,1},{5,7},{7,5},{8,10},{10,8},{12,... | collective-permute-start | bytes 393224 | tf_op jit(solution)/shard_map/ppermute | solution.py:637
  151.5 7.9 %collective-permute-start.57 = (s16[16,32,128]{2,1,0:T(8,128)(2,1)S(1)}, s16[16,32,128]{2,1,0:T(8,128)(2,1)S(1)}, u32[]{:S(2)}, u32[]{:S(2)}) collective-permute-start(s16[16,32,128]{2,1,0:T(8,128)(2,1)S(1)} %bitcast.42), channel_id=1, source_target_pairs={{0,4},{2,6},{4,0},{6,2},{1,5},{3,7},{5,1},{7,3},{8,12},{10,14},{12... | collective-permute-start | bytes 393224 | tf_op jit(solution)/shard_map/ppermute | solution.py:637
  152.1 7.3 %collective-permute-start.58 = (s16[16,32,128]{2,1,0:T(8,128)(2,1)S(1)}, s16[16,32,128]{2,1,0:T(8,128)(2,1)S(1)}, u32[]{:S(2)}, u32[]{:S(2)}) collective-permute-start(s16[16,32,128]{2,1,0:T(8,128)(2,1)S(1)} %bitcast.43), channel_id=1, source_target_pairs={{0,6},{2,4},{4,2},{6,0},{1,7},{3,5},{5,3},{7,1},{8,14},{10,12},{12... | collective-permute-start | bytes 393224 | tf_op jit(solution)/shard_map/ppermute | solution.py:637
  153.1 8.3 %collective-permute-start.52 = (s16[16,32,128]{2,1,0:T(8,128)(2,1)S(1)}, s16[16,32,128]{2,1,0:T(8,128)(2,1)S(1)}, u32[]{:S(2)}, u32[]{:S(2)}) collective-permute-start(s16[16,32,128]{2,1,0:T(8,128)(2,1)S(1)} %bitcast.37), channel_id=1, source_target_pairs={{0,2},{2,0},{4,6},{6,4},{1,3},{3,1},{5,7},{7,5},{8,10},{10,8},{12,... | collective-permute-start | bytes 393224 | tf_op jit(solution)/shard_map/ppermute | solution.py:637
  154.2 10.8 %collective-permute-start.53 = (s16[16,32,128]{2,1,0:T(8,128)(2,1)S(1)}, s16[16,32,128]{2,1,0:T(8,128)(2,1)S(1)}, u32[]{:S(2)}, u32[]{:S(2)}) collective-permute-start(s16[16,32,128]{2,1,0:T(8,128)(2,1)S(1)} %bitcast.38), channel_id=1, source_target_pairs={{0,4},{2,6},{4,0},{6,2},{1,5},{3,7},{5,1},{7,3},{8,12},{10,14},{12... | collective-permute-start | bytes 393224 | tf_op jit(solution)/shard_map/ppermute | solution.py:637
  154.7 10.3 %collective-permute-start.54 = (s16[16,32,128]{2,1,0:T(8,128)(2,1)S(1)}, s16[16,32,128]{2,1,0:T(8,128)(2,1)S(1)}, u32[]{:S(2)}, u32[]{:S(2)}) collective-permute-start(s16[16,32,128]{2,1,0:T(8,128)(2,1)S(1)} %bitcast.39), channel_id=1, source_target_pairs={{0,6},{2,4},{4,2},{6,0},{1,7},{3,5},{5,3},{7,1},{8,14},{10,12},{12... | collective-permute-start | bytes 393224 | tf_op jit(solution)/shard_map/ppermute | solution.py:637
  160.0 8.4 %collective-permute-start.59 = (s16[64,32,128]{2,1,0:T(8,128)(2,1)S(1)}, s16[64,32,128]{2,1,0:T(8,128)(2,1)S(1)}, u32[]{:S(2)}, u32[]{:S(2)}) collective-permute-start(s16[64,32,128]{2,1,0:T(8,128)(2,1)S(1)} %bitcast.27), channel_id=1, source_target_pairs={{0,1},{1,0},{2,3},{3,2},{4,5},{5,4},{6,7},{7,6},{8,9},{9,8},{10,11... | collective-permute-start | bytes 1572872 | tf_op jit(solution)/shard_map/ppermute | solution.py:574
  165.6 6.7 %collective-permute-start.55 = (s16[64,32,128]{2,1,0:T(8,128)(2,1)S(1)}, s16[64,32,128]{2,1,0:T(8,128)(2,1)S(1)}, u32[]{:S(2)}, u32[]{:S(2)}) collective-permute-start(s16[64,32,128]{2,1,0:T(8,128)(2,1)S(1)} %bitcast.25), channel_id=1, source_target_pairs={{0,1},{1,0},{2,3},{3,2},{4,5},{5,4},{6,7},{7,6},{8,9},{9,8},{10,11... | collective-permute-start | bytes 1572872 | tf_op jit(solution)/shard_map/ppermute | solution.py:574
  (35 other events, 148.4 us)
